TPU v7x, 32 devices: a whole 2x2x4 slice. The times are simulated.
32 devices in a mesh: clus: 4 (over y, x), rep: 8 (over z, core).
Axes of the slice: x: 2, y: 2, z: 4, core: 2. Of those that a mesh axis runs over, the one named last changes fastest.
Arguments:
- descriptors: bfloat16 [8, 4, 512, 2048], P('rep', 'clus')
- request: int32 [8, 4, 4, 32], P('rep', 'clus'), may hold values from 0 to 1535
- pick: int32 [8, 4, 512, 10], P('rep', 'clus'), may hold values from 0 to 127, as said below
Outputs:
- augmented: bfloat16 [8, 4, 512, 2048], P('rep', 'clus')
Inputs may be any that keep to these rules, and one draw needn't show every extreme that they name: `pick`: the 10 slots of one descriptor are distinct.
All inputs are finite; a program needn't handle non-finite values.
Results may differ from a plain program's by a relative error of at most 0.0075.
Values may be sent and summed in bfloat16 or wider, within the bound.
No kernel may reach another device: no remote copies, remote signals or barrier semaphores. Data moves between devices by JAX's collectives and lax.ppermute only.
A program may use at most 64 MiB of HBM per device.

v0:
```python
import jax
import jax.numpy as jnp
from jax import lax
from jax.sharding import PartitionSpec as P

ROUNDS = 2


def with_halo(block, sides, width):
    for axis, dim in sides:
        count = lax.axis_size(axis)
        forward = [(i, i + 1) for i in range(count - 1)]
        forward.append((count - 1, 0))
        backward = [(target, source) for source, target in forward]
        low = lax.ppermute(
            lax.slice_in_dim(block, block.shape[dim] - width, None, axis=dim), axis, forward
        )
        high = lax.ppermute(lax.slice_in_dim(block, 0, width, axis=dim), axis, backward)
        block = jnp.concatenate([low, block, high], axis=dim)
    return block


def normalize(value):
    return value * lax.rsqrt(jnp.mean(value * value, axis=-1, keepdims=True) + 1e-06)


def local(descriptors, request, pick):
    rows_dev = descriptors.shape[2]
    width = descriptors.shape[3]
    wanted = request[0, 0]
    slots = pick[0, 0]
    servers = wanted.shape[0]
    slot_cap = wanted.shape[1]
    total = servers * slot_cap
    current = normalize(descriptors[0, 0].astype(jnp.float32)).astype(jnp.bfloat16)
    chosen = jnp.any(slots[:, :, None] == jnp.arange(total, dtype=jnp.int32)[None, None, :], axis=1)
    incoming = lax.all_to_all(wanted, "clus", split_axis=0, concat_axis=0, tiled=True).reshape(
        total
    )
    for step in range(ROUNDS):
        window_rows = with_halo(current, (("rep", 0),), rows_dev)
        served = window_rows[incoming]
        buffer = lax.all_to_all(
            served.reshape(servers, slot_cap, width),
            "clus",
            split_axis=0,
            concat_axis=0,
            tiled=True,
        )
        buffer = buffer.reshape(total, width)
        sims = (
            lax.dot_general(
                current, buffer, (((1,), (1,)), ((), ())), preferred_element_type=jnp.float32
            )
            / width
        )
        positive = jnp.maximum(sims, 0.0)
        weights = jnp.where(chosen, positive * positive * positive, 0.0).astype(jnp.bfloat16)
        mixed = current.astype(jnp.float32) + jnp.dot(
            weights, buffer, preferred_element_type=jnp.float32
        )
        current = normalize(mixed).astype(jnp.bfloat16)
    return current[None, None]


def solution(mesh):
    return jax.shard_map(
        local,
        mesh=mesh,
        in_specs=(
            P("rep", "clus", None, None),
            P("rep", "clus", None, None),
            P("rep", "clus", None, None),
        ),
        out_specs=P("rep", "clus", None, None),
        check_vma=False,
    )
```

profile of v0, /device:TPU:0, one launch (start us, length us, event | category | flops | bytes accessed | tf_op | source)
XLA Modules:
  0.0 168.0 jit_solution(10594940032802784645)
XLA Ops:
  0.0 0.0 copy-start.2
  0.0 2.1 %fusion.2 = f32[512]{0:T(512)S(1)} fusion(bf16[1,1,512,2048]{3,2,1,0:T(8,128)(2,1)} %param.3), kind=kLoop, calls=%fused_computation.8 | loop fusion | flops 3145216 | bytes 2099200 | tf_op jit(solution)/shard_map/reduce_sum | solution.py:24
  2.1 2.0 %fusion.3 = bf16[512,2048]{1,0:T(8,128)(2,1)S(1)} fusion(bf16[1,1,512,2048]{3,2,1,0:T(8,128)(2,1)} %param.3, f32[512]{0:T(512)S(1)} %add_rsqrt_fusion.2), kind=kLoop, calls=%fused_computation.9 | loop fusion | flops 3145728 | bytes 4196352 | tf_op jit(solution)/shard_map/convert_element_type | solution.py:35
  4.1 0.5 collective-permute-start
  4.6 4.1 %collective-permute-start.1 = (bf16[512,2048]{1,0:T(8,128)(2,1)S(1)}, bf16[512,2048]{1,0:T(8,128)(2,1)}, u32[]{:S(2)}, u32[]{:S(2)}) collective-permute-start(bf16[512,2048]{1,0:T(8,128)(2,1)S(1)} %fusion.3), channel_id=1, source_target_pairs={{1,0},{2,1},{3,2},{4,3},{5,4},{6,5},{7,6},{0,7},{9,8},{10,9},{11,1... | collective-permute-start | bytes 6291464 | tf_op jit(solution)/shard_map/ppermute | solution.py:18
  8.7 0.0 copy-done.2
  8.7 8.6 %all_to_all.19 = s32[4,1,32]{2,1,0:T(1,128)S(1)} all-to-all(s32[4,1,32]{2,1,0:T(1,128)S(1)} %bitcast.52), channel_id=1, replica_groups=mesh['clus'=4,'rep'=8] {'clus'}, dimensions={0} | all-to-all | bytes 1024 | tf_op jit(solution)/shard_map/all_to_all | solution.py:37
  17.3 0.5 broadcast.109
  17.8 0.7 reduce.3
  18.5 0.1 reshape.82
  18.6 33.7 %collective-permute-done = bf16[512,2048]{1,0:T(8,128)(2,1)} collective-permute-done((bf16[512,2048]{1,0:T(8,128)(2,1)S(1)}, bf16[512,2048]{1,0:T(8,128)(2,1)}, u32[]{:S(2)}, u32[]{:S(2)}) %collective-permute-start) | collective-permute-done | bytes 2097184 | tf_op jit(solution)/shard_map/ppermute | solution.py:15
  52.3 0.4 collective-permute-done.1
  52.7 5.4 %pad_maximum_fusion = bf16[1536,2048]{1,0:T(8,128)(2,1)} fusion(bf16[512,2048]{1,0:T(8,128)(2,1)} %collective-permute-done.1, bf16[512,2048]{1,0:T(8,128)(2,1)S(1)} %fusion.3, bf16[512,2048]{1,0:T(8,128)(2,1)} %collective-permute-done), kind=kLoop, calls=%fused_computation.2 | loop fusion | flops 18874368 | bytes 12582912 | tf_op jit(solution)/shard_map/concatenate | solution.py:19
  58.1 0.0 copy-start.1
  58.1 0.0 copy-start
  58.1 6.0 %gather_fusion = bf16[128,2048]{1,0:T(8,128)(2,1)} fusion(bf16[1536,2048]{1,0:T(8,128)(2,1)} %pad_maximum_fusion, s32[1024]{0:T(1024)S(1)} %pad_clamp_fusion), kind=kCustom, calls=%fused_computation | custom fusion | bytes 1049088 | tf_op jit(solution)/shard_map/gather | solution.py:42
  64.1 4.3 %all-to-all-start.1 = ((bf16[4,32,2048]{2,1,0:T(8,128)(2,1)}), bf16[4,32,2048]{2,1,0:T(8,128)(2,1)S(1)}, u32[]{:S(2)}, u32[]{:S(2)}) async-start(bf16[4,32,2048]{2,1,0:T(8,128)(2,1)} %bitcast.5), calls=%async_computation.1 | async-start | bytes 1048576 | tf_op jit(solution)/shard_map/all_to_all | solution.py:43
  68.4 0.0 copy-done.1
  68.4 1.0 fusion.5
  69.4 7.7 %all-to-all-done.1 = bf16[4,32,2048]{2,1,0:T(8,128)(2,1)S(1)} async-done(((bf16[4,32,2048]{2,1,0:T(8,128)(2,1)}), bf16[4,32,2048]{2,1,0:T(8,128)(2,1)S(1)}, u32[]{:S(2)}, u32[]{:S(2)}) %all-to-all-start.1) | async-done | bytes 524320 | tf_op jit(solution)/shard_map/all_to_all | solution.py:43
  77.1 0.0 copy-done
  77.1 4.3 %multiply_reduce_fusion.1 = (f32[512]{0:T(512)S(1)}, f32[512,2048]{1,0:T(8,128)}) fusion(bf16[128,2048]{1,0:T(8,128)(2,1)S(1)} %bitcast.50, pred[512,128]{1,0:T(8,128)(4,1)S(1)} %fusion.5, bf16[1,1,512,2048]{3,2,1,0:T(8,128)(2,1)S(1)} %copy-done, f32[512]{0:T(512)S(1)} %add_rsqrt_fusion.2), kind=kOutput, calls=%fused_computation.15 | convolution fusion | flops 547749376 | bytes 6885376 | tf_op jit(solution)/shard_map/dot_general | solution.py:59
  81.4 2.5 %multiply_convert_fusion.1 = bf16[512,2048]{1,0:T(8,128)(2,1)S(1)} fusion(f32[512,2048]{1,0:T(8,128)} %get-tuple-element.6, f32[512]{0:T(512)S(1)} %add_rsqrt_fusion.1), kind=kLoop, calls=%fused_computation.14 | loop fusion | flops 2097152 | bytes 6293504 | tf_op jit(solution)/shard_map/convert_element_type | solution.py:62
  83.9 0.6 collective-permute-start.2
  84.5 3.0 %collective-permute-start.3 = (bf16[512,2048]{1,0:T(8,128)(2,1)S(1)}, bf16[512,2048]{1,0:T(8,128)(2,1)S(1)}, u32[]{:S(2)}, u32[]{:S(2)}) collective-permute-start(bf16[512,2048]{1,0:T(8,128)(2,1)S(1)} %multiply_convert_fusion.1), channel_id=1, source_target_pairs={{1,0},{2,1},{3,2},{4,3},{5,4},{6,5},{7,6},{0,7},{9,8},{10,9},{11,1... | collective-permute-start | bytes 6291464 | tf_op jit(solution)/shard_map/ppermute | solution.py:18
  87.5 44.4 %collective-permute-done.2 = bf16[512,2048]{1,0:T(8,128)(2,1)S(1)} collective-permute-done((bf16[512,2048]{1,0:T(8,128)(2,1)S(1)}, bf16[512,2048]{1,0:T(8,128)(2,1)S(1)}, u32[]{:S(2)}, u32[]{:S(2)}) %collective-permute-start.2) | collective-permute-done | bytes 2097184 | tf_op jit(solution)/shard_map/ppermute | solution.py:15
  131.9 0.0 collective-permute-done.3
  131.9 11.3 %pad_maximum_fusion.1 = bf16[1536,2048]{1,0:T(8,128)(2,1)} fusion(bf16[512,2048]{1,0:T(8,128)(2,1)S(1)} %collective-permute-done.3, bf16[512,2048]{1,0:T(8,128)(2,1)S(1)} %multiply_convert_fusion.1, bf16[512,2048]{1,0:T(8,128)(2,1)S(1)} %collective-permute-done.2), kind=kLoop, calls=%fused_computation.3 | loop fusion | flops 18874368 | bytes 12582912 | tf_op jit(solution)/shard_map/concatenate | solution.py:19
  143.2 5.0 %gather_fusion.1 = bf16[128,2048]{1,0:T(8,128)(2,1)S(1)} fusion(bf16[1536,2048]{1,0:T(8,128)(2,1)} %pad_maximum_fusion.1, s32[1024]{0:T(1024)S(1)} %pad_clamp_fusion), kind=kCustom, calls=%fused_computation.1 | custom fusion | bytes 1049088 | tf_op jit(solution)/shard_map/gather | solution.py:42
  148.2 11.7 %all_to_all.20 = bf16[4,32,2048]{2,1,0:T(8,128)(2,1)S(1)} all-to-all(bf16[4,32,2048]{2,1,0:T(8,128)(2,1)S(1)} %bitcast.49), channel_id=1, replica_groups=mesh['clus'=4,'rep'=8] {'clus'}, dimensions={0} | all-to-all | bytes 1048576 | tf_op jit(solution)/shard_map/all_to_all | solution.py:43
  160.0 4.2 %multiply_reduce_fusion = (f32[512]{0:T(512)S(1)}, f32[512,2048]{1,0:T(8,128)}) fusion(bf16[128,2048]{1,0:T(8,128)(2,1)S(1)} %bitcast.48, pred[512,128]{1,0:T(8,128)(4,1)S(1)} %fusion.5, bf16[512,2048]{1,0:T(8,128)(2,1)S(1)} %multiply_convert_fusion.1), kind=kOutput, calls=%fused_computation.12 | convolution fusion | flops 541457920 | bytes 6883328 | tf_op jit(solution)/shard_map/dot_general | solution.py:59
  164.2 3.8 %fusion.6 = bf16[1,1,512,2048]{3,2,1,0:T(8,128)(2,1)} fusion(f32[512,2048]{1,0:T(8,128)} %get-tuple-element.8, f32[512]{0:T(512)S(1)} %add_rsqrt_fusion), kind=kLoop, calls=%fused_computation.19 | loop fusion | flops 2097152 | bytes 6293504 | tf_op jit(solution)/shard_map/broadcast_in_dim | solution.py:63
  (6 shorter events, 0.0 us)
Async XLA Ops:
  0.0 8.7 %copy-start.2 = (s32[1,1,4,32]{3,2,1,0:T(4,128)S(1)}, s32[1,1,4,32]{3,2,1,0:T(4,128)}, u32[]{:S(2)}) copy-start(s32[1,1,4,32]{3,2,1,0:T(4,128)} %param.4) | copy-start | bytes 1540
  4.1 48.2 %collective-permute-start = (bf16[512,2048]{1,0:T(8,128)(2,1)S(1)}, bf16[512,2048]{1,0:T(8,128)(2,1)}, u32[]{:S(2)}, u32[]{:S(2)}) collective-permute-start(bf16[512,2048]{1,0:T(8,128)(2,1)S(1)} %fusion.3), channel_id=1, source_target_pairs={{0,1},{1,2},{2,3},{3,4},{4,5},{5,6},{6,7},{7,0},{8,9},{9,10},{10,1... | collective-permute-start | bytes 6291464 | tf_op jit(solution)/shard_map/ppermute | solution.py:15
  4.6 48.1 %collective-permute-start.1 = (bf16[512,2048]{1,0:T(8,128)(2,1)S(1)}, bf16[512,2048]{1,0:T(8,128)(2,1)}, u32[]{:S(2)}, u32[]{:S(2)}) collective-permute-start(bf16[512,2048]{1,0:T(8,128)(2,1)S(1)} %fusion.3), channel_id=1, source_target_pairs={{1,0},{2,1},{3,2},{4,3},{5,4},{6,5},{7,6},{0,7},{9,8},{10,9},{11,1... | collective-permute-start | bytes 6291464 | tf_op jit(solution)/shard_map/ppermute | solution.py:18
  58.1 10.3 %copy-start.1 = (s32[1,1,512,10]{2,1,3,0:T(1,128)S(1)}, s32[1,1,512,10]{2,1,3,0:T(1,128)}, u32[]{:S(2)}) copy-start(s32[1,1,512,10]{2,1,3,0:T(1,128)} %param.5) | copy-start | bytes 61444
  58.1 19.0 %copy-start = (bf16[1,1,512,2048]{3,2,1,0:T(8,128)(2,1)S(1)}, bf16[1,1,512,2048]{3,2,1,0:T(8,128)(2,1)}, u32[]{:S(2)}) copy-start(bf16[1,1,512,2048]{3,2,1,0:T(8,128)(2,1)} %param.3) | copy-start | bytes 6291460
  64.1 13.0 %all-to-all-start.1 = ((bf16[4,32,2048]{2,1,0:T(8,128)(2,1)}), bf16[4,32,2048]{2,1,0:T(8,128)(2,1)S(1)}, u32[]{:S(2)}, u32[]{:S(2)}) async-start(bf16[4,32,2048]{2,1,0:T(8,128)(2,1)} %bitcast.5), calls=%async_computation.1 | async-start | bytes 1048576 | tf_op jit(solution)/shard_map/all_to_all | solution.py:43
  83.9 48.0 %collective-permute-start.2 = (bf16[512,2048]{1,0:T(8,128)(2,1)S(1)}, bf16[512,2048]{1,0:T(8,128)(2,1)S(1)}, u32[]{:S(2)}, u32[]{:S(2)}) collective-permute-start(bf16[512,2048]{1,0:T(8,128)(2,1)S(1)} %multiply_convert_fusion.1), channel_id=1, source_target_pairs={{0,1},{1,2},{2,3},{3,4},{4,5},{5,6},{6,7},{7,0},{8,9},{9,10},{10,1... | collective-permute-start | bytes 6291464 | tf_op jit(solution)/shard_map/ppermute | solution.py:15
  84.5 47.5 %collective-permute-start.3 = (bf16[512,2048]{1,0:T(8,128)(2,1)S(1)}, bf16[512,2048]{1,0:T(8,128)(2,1)S(1)}, u32[]{:S(2)}, u32[]{:S(2)}) collective-permute-start(bf16[512,2048]{1,0:T(8,128)(2,1)S(1)} %multiply_convert_fusion.1), channel_id=1, source_target_pairs={{1,0},{2,1},{3,2},{4,3},{5,4},{6,5},{7,6},{0,7},{9,8},{10,9},{11,1... | collective-permute-start | bytes 6291464 | tf_op jit(solution)/shard_map/ppermute | solution.py:18
where the time goes:
time: 169 us; the launch traced here: 168 us
  waiting for transfers between devices  86.2 us (51%)
  other arithmetic  28.8 us (17%)
  blocking collectives  20.3 us (12%)
  starting transfers between devices  12.5 us (7%)
  local copies, waits for them, and re-layouts  11.6 us (7%)
  matrix products  8.51 us (5%)
    ppermute x2, waiting for transfers between devices, with_halo(): lax.ppermute(lax.slice_in_dim(block, block.shape[dim] - width, None, axis...  78.1 us
    concatenate x2, other arithmetic, with_halo(): block = jnp.concatenate([low, block, high], axis=dim)  16.7 us
    all_to_all x1, blocking collectives, local(): lax.all_to_all(served.reshape(servers, slot_cap, width), 'clus', split_ax...  11.7 us
    gather x2, local copies, waits for them, and re-layouts, local(): served = window_rows[incoming]  11 us
    all_to_all x1, blocking collectives, local(): lax.all_to_all(wanted, 'clus', split_axis=0, concat_axis=0, tiled=True)  8.59 us
    dot_general x2, matrix products, local(): jnp.dot(weights, buffer, preferred_element_type=jnp.float32)  8.51 us
    all_to_all x1, waiting for transfers between devices, local(): lax.all_to_all(served.reshape(servers, slot_cap, width), 'clus', split_ax...  7.7 us
    ppermute x2, starting transfers between devices, with_halo(): lax.ppermute(lax.slice_in_dim(block, 0, width, axis=dim), axis, backward)  7.13 us
  transfers between devices with their start and end apart: 5, of which 4 were waited for; matrix products, arithmetic and copies ran while one was open for 1% of the time, Pallas kernels for 0%

commit v1 on v0

v1 whole, which is shorter than its diff:
```python
import functools

import jax
import jax.numpy as jnp
from jax import lax
from jax.experimental import pallas as pl
from jax.experimental.pallas import tpu as pltpu
from jax.sharding import PartitionSpec as P

ROUNDS = 2
LANES = 128
BLOCK = 128


def params():
    return pltpu.CompilerParams(vmem_limit_bytes=32 * 1024 * 1024)


def normalize(value):
    return value * lax.rsqrt(jnp.mean(value * value, axis=-1, keepdims=True) + 1e-06)


def normalize_kernel(slot_cap, x_ref, pick_ref, out_ref, mask_ref):
    out_ref[...] = normalize(x_ref[...].astype(jnp.float32)).astype(jnp.bfloat16)
    rows, total = x_ref.shape[0], mask_ref.shape[1] // 2
    slot = lax.broadcasted_iota(jnp.int32, (rows, 2 * total), 1)
    turned = lax.axis_index("clus") * slot_cap
    slot = jnp.where(slot < total, slot, (slot - total) ^ turned)
    chosen = jnp.zeros((rows, 2 * total), jnp.float32)
    for k in range(pick_ref.shape[1]):
        chosen = jnp.where(pick_ref[:, k : k + 1] == slot, 1.0, chosen)
    mask_ref[...] = chosen.astype(jnp.bfloat16)


def normalize_call(descriptors, slots, total, slot_cap):
    rows, width = descriptors.shape
    return pl.pallas_call(
        functools.partial(normalize_kernel, slot_cap),
        grid=(rows // BLOCK,),
        in_specs=[
            pl.BlockSpec((BLOCK, width), lambda i: (i, 0)),
            pl.BlockSpec((BLOCK, slots.shape[1]), lambda i: (i, 0)),
        ],
        out_specs=[
            pl.BlockSpec((BLOCK, width), lambda i: (i, 0)),
            pl.BlockSpec((BLOCK, 2 * total), lambda i: (i, 0)),
        ],
        out_shape=[
            jax.ShapeDtypeStruct((rows, width), jnp.bfloat16),
            jax.ShapeDtypeStruct((rows, 2 * total), jnp.bfloat16),
        ],
        compiler_params=params(),
        cost_estimate=pl.CostEstimate(
            flops=6 * rows * width, bytes_accessed=4 * rows * width, transcendentals=rows
        ),
        name="normalize",
    )(descriptors, slots)


def serve(x, select, out_core, out_own, out_across):
    total = out_own.shape[0]
    cap = out_across[0].shape[0]
    fetched = jnp.dot(select, x, preferred_element_type=jnp.float32).astype(jnp.bfloat16)
    out_core[...] = fetched[:total]
    out_own[...] = fetched[total : 2 * total]
    for d, out in enumerate(out_across):
        out[...] = fetched[2 * total + d * cap : 2 * total + (d + 1) * cap]


def serve_kernel(x_ref, asked_ref, select_ref, core_ref, own_ref, *across_refs):
    rows = x_ref.shape[0]
    total = asked_ref.shape[2]
    asked = jnp.sum(asked_ref[...].astype(jnp.float32), axis=0)
    odd = lax.axis_index("rep") % 2
    thirds = (2 * odd, 1, 2 - 2 * odd)
    for q in range(3):
        column = jnp.broadcast_to(asked[q : q + 1], (LANES, total)).T
        column = column.astype(jnp.int32) - thirds[q] * rows
        for t in range(rows // LANES):
            lane = lax.broadcasted_iota(jnp.int32, (total, LANES), 1) + t * LANES
            select_ref[q * total : (q + 1) * total, t * LANES : (t + 1) * LANES] = jnp.where(
                column == lane, 1.0, 0.0
            ).astype(jnp.bfloat16)
    serve(x_ref[...], select_ref[...], core_ref, own_ref, across_refs)


def served_shapes(servers, cap, width):
    total = servers * cap
    return [jax.ShapeDtypeStruct((total, width), jnp.bfloat16)] * 2 + [
        jax.ShapeDtypeStruct((cap, width), jnp.bfloat16)
    ] * servers


def serve_call(x, asked, servers, cap):
    rows, width = x.shape
    total = servers * cap
    out = pl.pallas_call(
        serve_kernel,
        out_shape=[jax.ShapeDtypeStruct((3 * total, rows), jnp.bfloat16)]
        + served_shapes(servers, cap, width),
        compiler_params=params(),
        cost_estimate=pl.CostEstimate(
            flops=6 * total * rows * width, bytes_accessed=4 * rows * width, transcendentals=0
        ),
        name="serve",
    )(x, asked)
    return out[0], out[1:]


def mix(x_ref, mask_ref, buffer):
    width = x_ref.shape[1]
    x = x_ref[...]
    sims = lax.dot_general(
        x, buffer[...], (((1,), (1,)), ((), ())), preferred_element_type=jnp.float32
    )
    positive = jnp.maximum(sims * (1.0 / width), 0.0)
    cubed = (positive * positive * positive).astype(jnp.bfloat16)
    weights = cubed * mask_ref[...]
    mixed = x.astype(jnp.float32) + jnp.dot(
        weights, buffer[...], preferred_element_type=jnp.float32
    )
    return normalize(mixed).astype(jnp.bfloat16)


def fill(buffer, near_ref, across):
    total = near_ref.shape[0]
    cap = across[0].shape[0]
    buffer[:total] = near_ref[...]
    for d, ref in enumerate(across):
        buffer[total + d * cap : total + (d + 1) * cap] = ref[...]


def last_kernel(servers, x_ref, mask_ref, near_ref, *rest):
    across, out_ref, buffer = rest[:servers], rest[servers], rest[servers + 1]

    @pl.when(pl.program_id(0) == 0)
    def _():
        fill(buffer, near_ref, across)

    out_ref[...] = mix(x_ref, mask_ref, buffer)


def round_kernel(servers, x_ref, mask_ref, near_ref, *rest):
    across, rest = rest[:servers], rest[servers:]
    select_ref, out_ref, core_ref, own_ref = rest[:4]
    served, (buffer, whole) = rest[4 : 4 + servers], rest[4 + servers :]
    step = pl.program_id(0)

    @pl.when(step == 0)
    def _():
        fill(buffer, near_ref, across)

    block = mix(x_ref, mask_ref, buffer)
    out_ref[...] = block
    whole[pl.ds(pl.multiple_of(step * BLOCK, BLOCK), BLOCK), :] = block

    @pl.when(step == pl.num_programs(0) - 1)
    def _():
        serve(whole[...], select_ref[...], core_ref, own_ref, served)


def mix_call(x, mask, near, across, select):
    rows, width = x.shape
    total = near.shape[0]
    cap = across[0].shape[0]
    servers = len(across)
    again = select is not None

    def whole(shape):
        return pl.BlockSpec(shape, lambda i: (0, 0))

    in_specs = [
        pl.BlockSpec((BLOCK, width), lambda i: (i, 0)),
        pl.BlockSpec((BLOCK, 2 * total), lambda i: (i, 0)),
        whole(near.shape),
    ] + [whole((cap, width))] * servers
    out_specs = [pl.BlockSpec((BLOCK, width), lambda i: (i, 0))]
    out_shape = [jax.ShapeDtypeStruct((rows, width), jnp.bfloat16)]
    scratch = [pltpu.VMEM((2 * total, width), jnp.bfloat16)]
    args = [x, mask, near, *across]
    if again:
        in_specs.append(whole(select.shape))
        args.append(select)
        shapes = served_shapes(servers, cap, width)
        out_shape += shapes
        out_specs += [whole(s.shape) for s in shapes]
        scratch.append(pltpu.VMEM((rows, width), jnp.bfloat16))
    out = pl.pallas_call(
        functools.partial(round_kernel if again else last_kernel, servers),
        grid=(rows // BLOCK,),
        in_specs=in_specs,
        out_specs=out_specs,
        out_shape=out_shape,
        scratch_shapes=scratch,
        compiler_params=params(),
        cost_estimate=pl.CostEstimate(
            flops=8 * total * rows * width, bytes_accessed=6 * rows * width, transcendentals=rows
        ),
        name="mix_and_serve" if again else "mix",
    )(*args)
    return out[0], out[1:]


def local(descriptors, request, pick):
    width = descriptors.shape[3]
    wanted = request[0, 0]
    servers, cap = wanted.shape
    total = servers * cap
    groups = lax.axis_size("rep")
    column = lax.axis_index("clus")
    within = [g ^ 1 for g in range(groups)]
    beyond = [(g + 1) % groups if g % 2 else (g - 1) % groups for g in range(groups)]

    def swap(value, partner):
        return lax.ppermute(value, "rep", list(enumerate(partner)))

    def across(value, turn):
        pairs = [
            (c * groups + g, (c ^ turn) * groups + beyond[g])
            for g in range(groups)
            for c in range(servers)
        ]
        return lax.ppermute(value, ("clus", "rep"), pairs)

    core_wanted = swap(wanted, within)
    far_wanted = swap(wanted, beyond)
    x, mask = normalize_call(descriptors[0, 0], pick[0, 0], total, cap)

    place = lax.broadcasted_iota(jnp.int32, (servers, total), 1) // cap
    server = lax.broadcasted_iota(jnp.int32, (servers, total), 0)

    def placed(value, where):
        return jnp.where(place == where, jnp.tile(value, (1, servers)), 0)

    payload = jnp.stack(
        [
            placed(core_wanted, column),
            placed(wanted, column),
            placed(far_wanted, server ^ column),
        ],
        axis=1,
    )
    asked = lax.all_to_all(payload, "clus", split_axis=0, concat_axis=0, tiled=True)
    select, served = serve_call(x, asked, servers, cap)
    for step in range(ROUNDS):
        core, own, *far = served
        core = swap(core, within)
        far = [across(value, d) for d, value in enumerate(far)]
        near = lax.all_to_all(
            (core + own).reshape(servers, cap, width),
            "clus",
            split_axis=0,
            concat_axis=0,
            tiled=True,
        ).reshape(total, width)
        x, served = mix_call(x, mask, near, far, select if step < ROUNDS - 1 else None)
    return x[None, None]


def solution(mesh):
    return jax.shard_map(
        local,
        mesh=mesh,
        in_specs=(
            P("rep", "clus", None, None),
            P("rep", "clus", None, None),
            P("rep", "clus", None, None),
        ),
        out_specs=P("rep", "clus", None, None),
        check_vma=False,
    )
```

time: 169 us -> 80.2 us (0.47)
  waiting for transfers between devices: 86.2 us -> 22 us
  other arithmetic: 28.8 us -> 2.56 us
  starting transfers between devices: 12.5 us -> 33.6 us
  blocking collectives: 20.3 us -> 0 us
  Pallas kernels: 0 us -> 13.9 us
  matrix products: 8.51 us -> 0 us
  local copies, waits for them, and re-layouts: 11.6 us -> 7.58 us
    ppermute x4 -> x12, waiting for transfers between devices: 78.5 us -> 21.4 us  [the longest x8 16.9 us: across(): return lax.ppermute(value, ('clus', 'rep'), pairs)]
    all_to_all x2 -> x0, blocking collectives: 20.3 us -> none  [the longest x1 11.7 us: local(): lax.all_to_all(served.reshape(servers, slot_cap, width), 'clus', split_ax...]
    concatenate x2 -> x0, other arithmetic: 16.7 us -> none  [with_halo(): block = jnp.concatenate([low, block, high], axis=dim)]
    ppermute x4 -> x12, starting transfers between devices: 8.2 us -> 22.4 us  [the longest x8 17.8 us: across(): return lax.ppermute(value, ('clus', 'rep'), pairs)]
    pallas_call x0 -> x4, Pallas kernels: none -> 13.9 us  [the longest x2 11.2 us: mix_call(): pl.pallas_call(functools.partial(round_kernel if again else last_kernel,...]
    gather x2 -> x0, local copies, waits for them, and re-layouts: 11 us -> none  [local(): served = window_rows[incoming]]
    dot_general x2 -> x0, matrix products: 8.51 us -> none  [local(): jnp.dot(weights, buffer, preferred_element_type=jnp.float32)]
    all_to_all x1 -> x3, waiting for transfers between devices: 7.7 us -> 0.62 us  [the longest x1 0.62 us: local(): lax.all_to_all(payload, 'clus', split_axis=0, concat_axis=0, tiled=True)]
  transfers between devices with their start and end apart: 5 -> 15, of which waited for: 4 -> 10; matrix products, arithmetic and copies ran while one was open for 1% -> 2% of each run, Pallas kernels for 0% -> 2%
where the time goes in v1:
time: 80.2 us; the launch traced here: 79.8 us
  starting transfers between devices  33.6 us (42%)
  waiting for transfers between devices  22 us (27%)
  Pallas kernels  13.9 us (17%)
  local copies, waits for them, and re-layouts  7.58 us (9%)
  other arithmetic  2.56 us (3%)
    ppermute x8, starting transfers between devices, across(): return lax.ppermute(value, ('clus', 'rep'), pairs)  17.8 us
    ppermute x8, waiting for transfers between devices, across(): return lax.ppermute(value, ('clus', 'rep'), pairs)  16.9 us
    pallas_call x2, Pallas kernels, mix_call(): pl.pallas_call(functools.partial(round_kernel if again else last_kernel,...  11.2 us
    all_to_all x2, starting transfers between devices, local(): lax.all_to_all((core + own).reshape(servers, cap, width), 'clus', split_a...  7.06 us
    unnamed x15, local copies, waits for them, and re-layouts  6.6 us
    ppermute x4, starting transfers between devices, swap(): return lax.ppermute(value, 'rep', list(enumerate(partner)))  4.56 us
    ppermute x4, waiting for transfers between devices, swap(): return lax.ppermute(value, 'rep', list(enumerate(partner)))  4.48 us
    all_to_all x1, starting transfers between devices, local(): lax.all_to_all(payload, 'clus', split_axis=0, concat_axis=0, tiled=True)  4.17 us
  transfers between devices with their start and end apart: 15, of which 10 were waited for; matrix products, arithmetic and copies ran while one was open for 2% of the time, Pallas kernels for 2%

profile of v1, /device:TPU:0, one launch (start us, length us, event | category | flops | bytes accessed | tf_op | source)
XLA Modules:
  0.0 79.8 jit_solution(11015878397060257961)
XLA Ops:
  0.0 4.5 %collective-permute-start.1 = (s32[4,32]{1,0:T(4,128)}, s32[4,32]{1,0:T(4,128)S(1)}, u32[]{:S(2)}, u32[]{:S(2)}) collective-permute-start(s32[4,32]{1,0:T(4,128)} %bitcast.12), channel_id=1, source_target_pairs={{0,7},{1,2},{2,1},{3,4},{4,3},{5,6},{6,5},{7,0},{8,15},{9,10},{10,... | collective-permute-start | bytes 1544 | tf_op jit(solution)/shard_map/ppermute | solution.py:215
  4.5 0.0 collective-permute-start
  4.5 0.7 tile.28
  5.2 0.1 tile.29
  5.3 0.7 collective-permute-done.1
  6.0 0.1 tile.31
  6.1 0.0 collective-permute-done
  6.1 0.1 tile.13
  6.2 0.1 compare_select_fusion.2
  6.3 0.6 pad_add_fusion
  6.9 4.2 %all-to-all-start = ((s32[4,3,128]{2,1,0:T(4,128)}), s32[4,3,128]{2,1,0:T(4,128)S(1)}, u32[]{:S(2)}, u32[]{:S(2)}) async-start(s32[4,3,128]{2,1,0:T(4,128)} %pad_add_fusion), calls=%async_computation | async-start | bytes 16384 | tf_op jit(solution)/shard_map/all_to_all | solution.py:243
  11.1 0.9 %copy.4 = s32[1,1,512,10]{3,2,1,0:T(8,128)S(1)} copy(s32[1,1,512,10]{2,1,3,0:T(1,128)} %param.5) | data formatting | bytes 40960 | tf_op args[2]
  11.9 0.0 copy-start
  11.9 1.6 %copy-done = bf16[1,1,512,2048]{3,2,1,0:T(8,128)(2,1)S(1)} copy-done((bf16[1,1,512,2048]{3,2,1,0:T(8,128)(2,1)S(1)}, bf16[1,1,512,2048]{3,2,1,0:T(8,128)(2,1)}, u32[]{:S(2)}) %copy-start) | copy-done | bytes 2097176
  13.5 1.6 %normalize.1 = (bf16[512,2048]{1,0:T(8,128)(2,1)S(1)}, bf16[512,256]{1,0:T(8,128)(2,1)S(1)}) custom-call(bf16[512,2048]{1,0:T(8,128)(2,1)S(1)} %bitcast.8, s32[512,10]{1,0:T(8,128)S(1)} %bitcast.10), custom_call_target="tpu_custom_call" | custom-call | flops 6291456 | bytes 4194304 | tf_op jit(solution)/shard_map/normalize/pallas_call | solution.py:37
  15.1 0.0 copy-start.1
  15.1 0.6 all-to-all-done.asked_ref
  15.7 1.1 %serve.1 = (bf16[384,512]{1,0:T(8,128)(2,1)S(1)}, bf16[128,2048]{1,0:T(8,128)(2,1)S(1)}, bf16[128,2048]{1,0:T(8,128)(2,1)S(1)}, bf16[32,2048]{1,0:T(8,128)(2,1)S...) custom-call(bf16[512,2048]{1,0:T(8,128)(2,1)S(1)} %get-tuple-element.21.x_ref, ...), custom_call_target="tpu_custom_call" | custom-call | flops 805306368 | bytes 4194304 | tf_op jit(solution)/shard_map/serve/pallas_call | solution.py:97
  16.8 0.1 collective-permute-start.2
  16.9 1.9 %collective-permute-done.2 = bf16[128,2048]{1,0:T(8,128)(2,1)S(1)} collective-permute-done((bf16[128,2048]{1,0:T(8,128)(2,1)S(1)}, bf16[128,2048]{1,0:T(8,128)(2,1)S(1)}, u32[]{:S(2)}, u32[]{:S(2)}) %collective-permute-start.2) | collective-permute-done | bytes 524320 | tf_op jit(solution)/shard_map/ppermute | solution.py:215
  18.8 0.9 %add.8 = bf16[128,2048]{1,0:T(8,128)(2,1)} add(bf16[128,2048]{1,0:T(8,128)(2,1)S(1)} %collective-permute-done.2, bf16[128,2048]{1,0:T(8,128)(2,1)S(1)} %get-tuple-element.24) | non-fusion elementwise | flops 262144 | bytes 1572864 | tf_op jit(solution)/shard_map/add | solution.py:250
  19.7 3.6 %all-to-all-start.1 = ((bf16[4,32,2048]{2,1,0:T(8,128)(2,1)}), bf16[4,32,2048]{2,1,0:T(8,128)(2,1)S(1)}, u32[]{:S(2)}, u32[]{:S(2)}) async-start(bf16[4,32,2048]{2,1,0:T(8,128)(2,1)} %bitcast.3), calls=%async_computation.1 | async-start | bytes 1048576 | tf_op jit(solution)/shard_map/all_to_all | solution.py:249
  23.3 2.2 %collective-permute-start.3 = (bf16[32,2048]{1,0:T(8,128)(2,1)S(1)}, bf16[32,2048]{1,0:T(8,128)(2,1)S(1)}, u32[]{:S(2)}, u32[]{:S(2)}) collective-permute-start(bf16[32,2048]{1,0:T(8,128)(2,1)S(1)} %get-tuple-element.25), channel_id=1, source_target_pairs={{0,7},{8,15},{16,23},{24,31},{1,2},{9,10},{17,18},{25,26},{2,1},{1... | collective-permute-start | bytes 393224 | tf_op jit(solution)/shard_map/ppermute | solution.py:223
  25.5 2.8 %collective-permute-start.4 = (bf16[32,2048]{1,0:T(8,128)(2,1)S(1)}, bf16[32,2048]{1,0:T(8,128)(2,1)S(1)}, u32[]{:S(2)}, u32[]{:S(2)}) collective-permute-start(bf16[32,2048]{1,0:T(8,128)(2,1)S(1)} %get-tuple-element.26), channel_id=1, source_target_pairs={{0,15},{8,7},{16,31},{24,23},{1,10},{9,2},{17,26},{25,18},{2,9},{1... | collective-permute-start | bytes 393224 | tf_op jit(solution)/shard_map/ppermute | solution.py:223
  28.3 2.8 %collective-permute-start.5 = (bf16[32,2048]{1,0:T(8,128)(2,1)S(1)}, bf16[32,2048]{1,0:T(8,128)(2,1)S(1)}, u32[]{:S(2)}, u32[]{:S(2)}) collective-permute-start(bf16[32,2048]{1,0:T(8,128)(2,1)S(1)} %get-tuple-element.27), channel_id=1, source_target_pairs={{0,23},{8,31},{16,7},{24,15},{1,18},{9,26},{17,2},{25,10},{2,17},{... | collective-permute-start | bytes 393224 | tf_op jit(solution)/shard_map/ppermute | solution.py:223
  31.2 1.1 %collective-permute-start.6 = (bf16[32,2048]{1,0:T(8,128)(2,1)S(1)}, bf16[32,2048]{1,0:T(8,128)(2,1)S(1)}, u32[]{:S(2)}, u32[]{:S(2)}) collective-permute-start(bf16[32,2048]{1,0:T(8,128)(2,1)S(1)} %get-tuple-element.28), channel_id=1, source_target_pairs={{0,31},{8,23},{16,15},{24,7},{1,26},{9,18},{17,10},{25,2},{2,25},{... | collective-permute-start | bytes 393224 | tf_op jit(solution)/shard_map/ppermute | solution.py:223
  32.2 0.0 collective-permute-done.3.rest_0_
  32.2 2.9 %collective-permute-done.4.rest_1_ = bf16[32,2048]{1,0:T(8,128)(2,1)S(1)} collective-permute-done((bf16[32,2048]{1,0:T(8,128)(2,1)S(1)}, bf16[32,2048]{1,0:T(8,128)(2,1)S(1)}, u32[]{:S(2)}, u32[]{:S(2)}) %collective-permute-start.4) | collective-permute-done | bytes 131104 | tf_op jit(solution)/shard_map/ppermute | solution.py:223
  35.2 2.8 %collective-permute-done.5.rest_2_ = bf16[32,2048]{1,0:T(8,128)(2,1)S(1)} collective-permute-done((bf16[32,2048]{1,0:T(8,128)(2,1)S(1)}, bf16[32,2048]{1,0:T(8,128)(2,1)S(1)}, u32[]{:S(2)}, u32[]{:S(2)}) %collective-permute-start.5) | collective-permute-done | bytes 131104 | tf_op jit(solution)/shard_map/ppermute | solution.py:223
  38.0 3.0 %collective-permute-done.6.rest_3_ = bf16[32,2048]{1,0:T(8,128)(2,1)S(1)} collective-permute-done((bf16[32,2048]{1,0:T(8,128)(2,1)S(1)}, bf16[32,2048]{1,0:T(8,128)(2,1)S(1)}, u32[]{:S(2)}, u32[]{:S(2)}) %collective-permute-start.6) | collective-permute-done | bytes 131104 | tf_op jit(solution)/shard_map/ppermute | solution.py:223
  41.0 0.6 copy-done.3
  41.6 1.6 %copy-done.2 = bf16[512,2048]{1,0:T(8,128)(2,1)S(1)} copy-done((bf16[512,2048]{1,0:T(8,128)(2,1)S(1)}, bf16[512,2048]{1,0:T(8,128)(2,1)}, u32[]{:S(2)}) %copy-start.2) | copy-done | bytes 2097176
  43.2 0.9 %copy-done.4 = bf16[32,2048]{1,0:T(8,128)(2,1)S(1)} copy-done((bf16[32,2048]{1,0:T(8,128)(2,1)S(1)}, bf16[32,2048]{1,0:T(8,128)(2,1)}, u32[]{:S(2)}) %copy-start.4) | copy-done | bytes 131096
  44.1 1.0 %copy-done.6 = bf16[384,512]{1,0:T(8,128)(2,1)S(1)} copy-done((bf16[384,512]{1,0:T(8,128)(2,1)S(1)}, bf16[384,512]{1,0:T(8,128)(2,1)}, u32[]{:S(2)}) %copy-start.6) | copy-done | bytes 393240
  45.1 6.1 %mix_and_serve.1 = (bf16[512,2048]{1,0:T(8,128)(2,1)S(1)}, bf16[128,2048]{1,0:T(8,128)(2,1)S(1)}, bf16[128,2048]{1,0:T(8,128)(2,1)S(1)}, bf16[32,2048]{1,0:T(8,1...) custom-call(bf16[512,2048]{1,0:T(8,128)(2,1)S(1)} %copy-done.2, ...), custom_call_target="tpu_custom_call" | custom-call | flops 1073741824 | bytes 6291456 | tf_op jit(solution)/shard_map/mix_and_serve/pallas_call | solution.py:188
  51.2 0.0 collective-permute-start.7
  51.2 1.9 %collective-permute-done.7 = bf16[128,2048]{1,0:T(8,128)(2,1)S(1)} collective-permute-done((bf16[128,2048]{1,0:T(8,128)(2,1)S(1)}, bf16[128,2048]{1,0:T(8,128)(2,1)S(1)}, u32[]{:S(2)}, u32[]{:S(2)}) %collective-permute-start.7) | collective-permute-done | bytes 524320 | tf_op jit(solution)/shard_map/ppermute | solution.py:215
  53.1 0.9 %add.9 = bf16[128,2048]{1,0:T(8,128)(2,1)} add(bf16[128,2048]{1,0:T(8,128)(2,1)S(1)} %collective-permute-done.7, bf16[128,2048]{1,0:T(8,128)(2,1)S(1)} %get-tuple-element.32) | non-fusion elementwise | flops 262144 | bytes 1572864 | tf_op jit(solution)/shard_map/add | solution.py:250
  54.1 3.5 %all-to-all-start.2 = ((bf16[4,32,2048]{2,1,0:T(8,128)(2,1)}), bf16[4,32,2048]{2,1,0:T(8,128)(2,1)S(1)}, u32[]{:S(2)}, u32[]{:S(2)}) async-start(bf16[4,32,2048]{2,1,0:T(8,128)(2,1)} %bitcast.5), calls=%async_computation.2 | async-start | bytes 1048576 | tf_op jit(solution)/shard_map/all_to_all | solution.py:249
  57.5 1.3 %collective-permute-start.8 = (bf16[32,2048]{1,0:T(8,128)(2,1)}, bf16[32,2048]{1,0:T(8,128)(2,1)S(1)}, u32[]{:S(2)}, u32[]{:S(2)}) collective-permute-start(bf16[32,2048]{1,0:T(8,128)(2,1)} %get-tuple-element.33), channel_id=1, source_target_pairs={{0,7},{8,15},{16,23},{24,31},{1,2},{9,10},{17,18},{25,26},{2,1},{1... | collective-permute-start | bytes 393224 | tf_op jit(solution)/shard_map/ppermute | solution.py:223
  58.8 3.7 %collective-permute-start.9 = (bf16[32,2048]{1,0:T(8,128)(2,1)}, bf16[32,2048]{1,0:T(8,128)(2,1)S(1)}, u32[]{:S(2)}, u32[]{:S(2)}) collective-permute-start(bf16[32,2048]{1,0:T(8,128)(2,1)} %get-tuple-element.34), channel_id=1, source_target_pairs={{0,15},{8,7},{16,31},{24,23},{1,10},{9,2},{17,26},{25,18},{2,9},{1... | collective-permute-start | bytes 393224 | tf_op jit(solution)/shard_map/ppermute | solution.py:223
  62.5 1.8 %collective-permute-start.10 = (bf16[32,2048]{1,0:T(8,128)(2,1)}, bf16[32,2048]{1,0:T(8,128)(2,1)S(1)}, u32[]{:S(2)}, u32[]{:S(2)}) collective-permute-start(bf16[32,2048]{1,0:T(8,128)(2,1)} %get-tuple-element.35), channel_id=1, source_target_pairs={{0,23},{8,31},{16,7},{24,15},{1,18},{9,26},{17,2},{25,10},{2,17},{... | collective-permute-start | bytes 393224 | tf_op jit(solution)/shard_map/ppermute | solution.py:223
  64.3 2.2 %collective-permute-start.11 = (bf16[32,2048]{1,0:T(8,128)(2,1)S(1)}, bf16[32,2048]{1,0:T(8,128)(2,1)S(1)}, u32[]{:S(2)}, u32[]{:S(2)}) collective-permute-start(bf16[32,2048]{1,0:T(8,128)(2,1)S(1)} %get-tuple-element.36), channel_id=1, source_target_pairs={{0,31},{8,23},{16,15},{24,7},{1,26},{9,18},{17,10},{25,2},{2,25},{... | collective-permute-start | bytes 393224 | tf_op jit(solution)/shard_map/ppermute | solution.py:223
  66.5 3.1 %collective-permute-done.9.rest_1_ = bf16[32,2048]{1,0:T(8,128)(2,1)S(1)} collective-permute-done((bf16[32,2048]{1,0:T(8,128)(2,1)}, bf16[32,2048]{1,0:T(8,128)(2,1)S(1)}, u32[]{:S(2)}, u32[]{:S(2)}) %collective-permute-start.9) | collective-permute-done | bytes 131104 | tf_op jit(solution)/shard_map/ppermute | solution.py:223
  69.6 1.9 %collective-permute-done.10.rest_2_ = bf16[32,2048]{1,0:T(8,128)(2,1)S(1)} collective-permute-done((bf16[32,2048]{1,0:T(8,128)(2,1)}, bf16[32,2048]{1,0:T(8,128)(2,1)S(1)}, u32[]{:S(2)}, u32[]{:S(2)}) %collective-permute-start.10) | collective-permute-done | bytes 131104 | tf_op jit(solution)/shard_map/ppermute | solution.py:223
  71.6 3.1 %collective-permute-done.11.rest_3_ = bf16[32,2048]{1,0:T(8,128)(2,1)S(1)} collective-permute-done((bf16[32,2048]{1,0:T(8,128)(2,1)S(1)}, bf16[32,2048]{1,0:T(8,128)(2,1)S(1)}, u32[]{:S(2)}, u32[]{:S(2)}) %collective-permute-start.11) | collective-permute-done | bytes 131104 | tf_op jit(solution)/shard_map/ppermute | solution.py:223
  74.6 0.0 all-to-all-done.2
  74.6 5.1 %mix.1 = bf16[512,2048]{1,0:T(8,128)(2,1)} custom-call(bf16[512,2048]{1,0:T(8,128)(2,1)S(1)} %get-tuple-element.30.x_ref, bf16[512,256]{1,0:T(8,128)(2,1)S(1)} %get-tuple-element.22.mask_ref, bf16[128,2048]{1,0:T(8,128)(2,1)S(1)} %bitcast.9, bf16[32,2048]{1,0:T(8,128)(2,1)S(1)} %collective-permute-done.8.rest_0_, ...), custom_call_target="tpu_custom_call" | custom-call | flops 1073741824 | bytes 6291456 | tf_op jit(solution)/shard_map/mix/pallas_call | solution.py:188
  (14 shorter events, 0.0 us)
Async XLA Ops:
  0.0 6.0 %collective-permute-start.1 = (s32[4,32]{1,0:T(4,128)}, s32[4,32]{1,0:T(4,128)S(1)}, u32[]{:S(2)}, u32[]{:S(2)}) collective-permute-start(s32[4,32]{1,0:T(4,128)} %bitcast.12), channel_id=1, source_target_pairs={{0,7},{1,2},{2,1},{3,4},{4,3},{5,6},{6,5},{7,0},{8,15},{9,10},{10,... | collective-permute-start | bytes 1544 | tf_op jit(solution)/shard_map/ppermute | solution.py:215
  4.5 1.6 %collective-permute-start = (s32[4,32]{1,0:T(4,128)}, s32[4,32]{1,0:T(4,128)S(1)}, u32[]{:S(2)}, u32[]{:S(2)}) collective-permute-start(s32[4,32]{1,0:T(4,128)} %bitcast.13), channel_id=1, source_target_pairs={{0,1},{1,0},{2,3},{3,2},{4,5},{5,4},{6,7},{7,6},{8,9},{9,8},{10,11... | collective-permute-start | bytes 1544 | tf_op jit(solution)/shard_map/ppermute | solution.py:215
  6.9 8.9 %all-to-all-start = ((s32[4,3,128]{2,1,0:T(4,128)}), s32[4,3,128]{2,1,0:T(4,128)S(1)}, u32[]{:S(2)}, u32[]{:S(2)}) async-start(s32[4,3,128]{2,1,0:T(4,128)} %pad_add_fusion), calls=%async_computation | async-start | bytes 16384 | tf_op jit(solution)/shard_map/all_to_all | solution.py:243
  11.9 1.6 %copy-start = (bf16[1,1,512,2048]{3,2,1,0:T(8,128)(2,1)S(1)}, bf16[1,1,512,2048]{3,2,1,0:T(8,128)(2,1)}, u32[]{:S(2)}) copy-start(bf16[1,1,512,2048]{3,2,1,0:T(8,128)(2,1)} %param.3) | copy-start | bytes 6291460
  15.1 4.6 %copy-start.1 = (bf16[512,2048]{1,0:T(8,128)(2,1)}, bf16[512,2048]{1,0:T(8,128)(2,1)S(1)}, u32[]{:S(2)}) copy-start(bf16[512,2048]{1,0:T(8,128)(2,1)S(1)} %get-tuple-element.21.x_ref) | copy-start | bytes 6291460
  16.8 2.9 %copy-start.5 = (bf16[384,512]{1,0:T(8,128)(2,1)}, bf16[384,512]{1,0:T(8,128)(2,1)S(1)}, u32[]{:S(2)}) copy-start(bf16[384,512]{1,0:T(8,128)(2,1)S(1)} %get-tuple-element.29.rest_4_) | copy-start | bytes 1179652
  16.8 2.0 %collective-permute-start.2 = (bf16[128,2048]{1,0:T(8,128)(2,1)S(1)}, bf16[128,2048]{1,0:T(8,128)(2,1)S(1)}, u32[]{:S(2)}, u32[]{:S(2)}) collective-permute-start(bf16[128,2048]{1,0:T(8,128)(2,1)S(1)} %get-tuple-element.23), channel_id=1, source_target_pairs={{0,1},{1,0},{2,3},{3,2},{4,5},{5,4},{6,7},{7,6},{8,9},{9,8},{10,11... | collective-permute-start | bytes 1572872 | tf_op jit(solution)/shard_map/ppermute | solution.py:215
  19.7 21.9 %all-to-all-start.1 = ((bf16[4,32,2048]{2,1,0:T(8,128)(2,1)}), bf16[4,32,2048]{2,1,0:T(8,128)(2,1)S(1)}, u32[]{:S(2)}, u32[]{:S(2)}) async-start(bf16[4,32,2048]{2,1,0:T(8,128)(2,1)} %bitcast.3), calls=%async_computation.1 | async-start | bytes 1048576 | tf_op jit(solution)/shard_map/all_to_all | solution.py:249
  23.3 8.9 %collective-permute-start.3 = (bf16[32,2048]{1,0:T(8,128)(2,1)S(1)}, bf16[32,2048]{1,0:T(8,128)(2,1)S(1)}, u32[]{:S(2)}, u32[]{:S(2)}) collective-permute-start(bf16[32,2048]{1,0:T(8,128)(2,1)S(1)} %get-tuple-element.25), channel_id=1, source_target_pairs={{0,7},{8,15},{16,23},{24,31},{1,2},{9,10},{17,18},{25,26},{2,1},{1... | collective-permute-start | bytes 393224 | tf_op jit(solution)/shard_map/ppermute | solution.py:223
  25.5 9.6 %collective-permute-start.4 = (bf16[32,2048]{1,0:T(8,128)(2,1)S(1)}, bf16[32,2048]{1,0:T(8,128)(2,1)S(1)}, u32[]{:S(2)}, u32[]{:S(2)}) collective-permute-start(bf16[32,2048]{1,0:T(8,128)(2,1)S(1)} %get-tuple-element.26), channel_id=1, source_target_pairs={{0,15},{8,7},{16,31},{24,23},{1,10},{9,2},{17,26},{25,18},{2,9},{1... | collective-permute-start | bytes 393224 | tf_op jit(solution)/shard_map/ppermute | solution.py:223
  28.3 9.7 %collective-permute-start.5 = (bf16[32,2048]{1,0:T(8,128)(2,1)S(1)}, bf16[32,2048]{1,0:T(8,128)(2,1)S(1)}, u32[]{:S(2)}, u32[]{:S(2)}) collective-permute-start(bf16[32,2048]{1,0:T(8,128)(2,1)S(1)} %get-tuple-element.27), channel_id=1, source_target_pairs={{0,23},{8,31},{16,7},{24,15},{1,18},{9,26},{17,2},{25,10},{2,17},{... | collective-permute-start | bytes 393224 | tf_op jit(solution)/shard_map/ppermute | solution.py:223
  31.2 9.8 %collective-permute-start.6 = (bf16[32,2048]{1,0:T(8,128)(2,1)S(1)}, bf16[32,2048]{1,0:T(8,128)(2,1)S(1)}, u32[]{:S(2)}, u32[]{:S(2)}) collective-permute-start(bf16[32,2048]{1,0:T(8,128)(2,1)S(1)} %get-tuple-element.28), channel_id=1, source_target_pairs={{0,31},{8,23},{16,15},{24,7},{1,26},{9,18},{17,10},{25,2},{2,25},{... | collective-permute-start | bytes 393224 | tf_op jit(solution)/shard_map/ppermute | solution.py:223
  41.0 0.7 copy-start.3
  41.6 1.6 %copy-start.2 = (bf16[512,2048]{1,0:T(8,128)(2,1)S(1)}, bf16[512,2048]{1,0:T(8,128)(2,1)}, u32[]{:S(2)}) copy-start(bf16[512,2048]{1,0:T(8,128)(2,1)} %copy-done.1) | copy-start | bytes 6291460
  43.2 0.9 %copy-start.4 = (bf16[32,2048]{1,0:T(8,128)(2,1)S(1)}, bf16[32,2048]{1,0:T(8,128)(2,1)}, u32[]{:S(2)}) copy-start(bf16[32,2048]{1,0:T(8,128)(2,1)} %copy-done.3) | copy-start | bytes 393220
  44.1 1.0 %copy-start.6 = (bf16[384,512]{1,0:T(8,128)(2,1)S(1)}, bf16[384,512]{1,0:T(8,128)(2,1)}, u32[]{:S(2)}) copy-start(bf16[384,512]{1,0:T(8,128)(2,1)} %copy-done.5) | copy-start | bytes 1179652
  51.2 1.9 %collective-permute-start.7 = (bf16[128,2048]{1,0:T(8,128)(2,1)S(1)}, bf16[128,2048]{1,0:T(8,128)(2,1)S(1)}, u32[]{:S(2)}, u32[]{:S(2)}) collective-permute-start(bf16[128,2048]{1,0:T(8,128)(2,1)S(1)} %get-tuple-element.31), channel_id=1, source_target_pairs={{0,1},{1,0},{2,3},{3,2},{4,5},{5,4},{6,7},{7,6},{8,9},{9,8},{10,11... | collective-permute-start | bytes 1572872 | tf_op jit(solution)/shard_map/ppermute | solution.py:215
  54.1 20.6 %all-to-all-start.2 = ((bf16[4,32,2048]{2,1,0:T(8,128)(2,1)}), bf16[4,32,2048]{2,1,0:T(8,128)(2,1)S(1)}, u32[]{:S(2)}, u32[]{:S(2)}) async-start(bf16[4,32,2048]{2,1,0:T(8,128)(2,1)} %bitcast.5), calls=%async_computation.2 | async-start | bytes 1048576 | tf_op jit(solution)/shard_map/all_to_all | solution.py:249
  57.5 9.0 %collective-permute-start.8 = (bf16[32,2048]{1,0:T(8,128)(2,1)}, bf16[32,2048]{1,0:T(8,128)(2,1)S(1)}, u32[]{:S(2)}, u32[]{:S(2)}) collective-permute-start(bf16[32,2048]{1,0:T(8,128)(2,1)} %get-tuple-element.33), channel_id=1, source_target_pairs={{0,7},{8,15},{16,23},{24,31},{1,2},{9,10},{17,18},{25,26},{2,1},{1... | collective-permute-start | bytes 393224 | tf_op jit(solution)/shard_map/ppermute | solution.py:223
  58.8 10.8 %collective-permute-start.9 = (bf16[32,2048]{1,0:T(8,128)(2,1)}, bf16[32,2048]{1,0:T(8,128)(2,1)S(1)}, u32[]{:S(2)}, u32[]{:S(2)}) collective-permute-start(bf16[32,2048]{1,0:T(8,128)(2,1)} %get-tuple-element.34), channel_id=1, source_target_pairs={{0,15},{8,7},{16,31},{24,23},{1,10},{9,2},{17,26},{25,18},{2,9},{1... | collective-permute-start | bytes 393224 | tf_op jit(solution)/shard_map/ppermute | solution.py:223
  62.5 9.1 %collective-permute-start.10 = (bf16[32,2048]{1,0:T(8,128)(2,1)}, bf16[32,2048]{1,0:T(8,128)(2,1)S(1)}, u32[]{:S(2)}, u32[]{:S(2)}) collective-permute-start(bf16[32,2048]{1,0:T(8,128)(2,1)} %get-tuple-element.35), channel_id=1, source_target_pairs={{0,23},{8,31},{16,7},{24,15},{1,18},{9,26},{17,2},{25,10},{2,17},{... | collective-permute-start | bytes 393224 | tf_op jit(solution)/shard_map/ppermute | solution.py:223
  64.3 10.3 %collective-permute-start.11 = (bf16[32,2048]{1,0:T(8,128)(2,1)S(1)}, bf16[32,2048]{1,0:T(8,128)(2,1)S(1)}, u32[]{:S(2)}, u32[]{:S(2)}) collective-permute-start(bf16[32,2048]{1,0:T(8,128)(2,1)S(1)} %get-tuple-element.36), channel_id=1, source_target_pairs={{0,31},{8,23},{16,15},{24,7},{1,26},{9,18},{17,10},{25,2},{2,25},{... | collective-permute-start | bytes 393224 | tf_op jit(solution)/shard_map/ppermute | solution.py:223

commit v2 on v0

v2 whole, which is shorter than its diff:
```python
import functools

import jax
import jax.numpy as jnp
from jax import lax
from jax.experimental import pallas as pl
from jax.experimental.pallas import tpu as pltpu
from jax.sharding import PartitionSpec as P

ROUNDS = 2
LANES = 128
BLOCK = 128


def params():
    return pltpu.CompilerParams(vmem_limit_bytes=32 * 1024 * 1024)


def bf16(*shape):
    return jax.ShapeDtypeStruct(shape, jnp.bfloat16)


def normalize(value):
    return value * lax.rsqrt(jnp.mean(value * value, axis=-1, keepdims=True) + 1e-06)


def normalize_kernel(slot_cap, x_ref, pick_ref, out_ref, mask_ref):
    out_ref[...] = normalize(x_ref[...].astype(jnp.float32)).astype(jnp.bfloat16)
    slot = lax.broadcasted_iota(jnp.int32, mask_ref.shape, 1)
    slot = slot ^ (lax.axis_index("clus") * slot_cap)
    chosen = jnp.zeros(mask_ref.shape, jnp.float32)
    for k in range(pick_ref.shape[1]):
        chosen = jnp.where(pick_ref[:, k : k + 1] == slot, 1.0, chosen)
    mask_ref[...] = chosen.astype(jnp.bfloat16)


def normalize_call(descriptors, slots, total, slot_cap):
    rows, width = descriptors.shape
    return pl.pallas_call(
        functools.partial(normalize_kernel, slot_cap),
        grid=(rows // BLOCK,),
        in_specs=[
            pl.BlockSpec((BLOCK, width), lambda i: (i, 0)),
            pl.BlockSpec((BLOCK, slots.shape[1]), lambda i: (i, 0)),
        ],
        out_specs=[
            pl.BlockSpec((BLOCK, width), lambda i: (i, 0)),
            pl.BlockSpec((BLOCK, total), lambda i: (i, 0)),
        ],
        out_shape=[bf16(rows, width), bf16(rows, total)],
        compiler_params=params(),
        cost_estimate=pl.CostEstimate(
            flops=6 * rows * width, bytes_accessed=4 * rows * width, transcendentals=rows
        ),
        name="normalize",
    )(descriptors, slots)


def serve(x, select_ref, core_ref, own_ref, far_ref):
    total, sent = own_ref.shape[0], far_ref.shape[0]
    fetched = jnp.dot(
        select_ref[: 2 * total + sent], x, preferred_element_type=jnp.float32
    ).astype(jnp.bfloat16)
    core_ref[...] = fetched[:total]
    own_ref[...] = fetched[total : 2 * total]
    far_ref[...] = fetched[2 * total :]


def one_hot(asked, third, rows):
    total = asked.shape[1]
    column = jnp.broadcast_to(asked, (LANES, total)).T - third * rows
    tiles = []
    for t in range(rows // LANES):
        lane = lax.broadcasted_iota(jnp.int32, (total, LANES), 1) + t * LANES
        tiles.append(jnp.where(column == lane, 1.0, 0.0))
    return jnp.concatenate(tiles, axis=1)


def index_kernel(groups, x_ref, asked_ref, select_ref, expand_ref, core_ref, own_ref, far_ref):
    rows = x_ref.shape[0]
    servers, cap = asked_ref.shape[1:]
    total = servers * cap
    group, column = lax.axis_index("rep"), lax.axis_index("clus")
    odd = group % 2
    beyond = (group + 2 * odd - 1 + groups) % groups

    def asked(requester):
        parts = [
            asked_ref[(column ^ d) * groups + requester, pl.ds(column, 1), :]
            for d in range(servers)
        ]
        return jnp.concatenate(parts, axis=1)

    own = asked(group)
    from_own = one_hot(own, 1, rows)
    from_core = one_hot(asked(group ^ 1), 2 * odd, rows)
    to_far = one_hot(asked(beyond), 2 - 2 * odd, rows)
    from_far = one_hot(own, 2 * odd, rows)
    needed = jnp.concatenate(
        [
            jnp.broadcast_to(jnp.max(to_far, axis=0, keepdims=True), (8, rows)),
            jnp.broadcast_to(jnp.max(from_far, axis=0, keepdims=True), (8, rows)),
        ],
        axis=0,
    )
    before = lax.broadcasted_iota(jnp.int32, (rows, rows), 0) < lax.broadcasted_iota(
        jnp.int32, (rows, rows), 1
    )
    rank = jnp.dot(
        needed.astype(jnp.bfloat16),
        jnp.where(before, 1.0, 0.0).astype(jnp.bfloat16),
        preferred_element_type=jnp.float32,
    )
    rank = jnp.where(needed > 0, rank, -1.0).astype(jnp.int32)
    place = lax.broadcasted_iota(jnp.int32, (total, rows), 0)
    pack = jnp.where(place == rank[0:1], 1.0, 0.0).astype(jnp.bfloat16)
    packed = jnp.where(place == rank[8:9], 1.0, 0.0).astype(jnp.bfloat16)
    expand_ref[...] = lax.dot_general(
        from_far.astype(jnp.bfloat16),
        packed,
        (((1,), (1,)), ((), ())),
        preferred_element_type=jnp.float32,
    ).astype(jnp.bfloat16)
    select_ref[:total] = from_core.astype(jnp.bfloat16)
    select_ref[total : 2 * total] = from_own.astype(jnp.bfloat16)
    select_ref[2 * total :] = pack
    serve(x_ref[...], select_ref, core_ref, own_ref, far_ref)


def index_call(x, asked, groups):
    rows, width = x.shape
    total = asked.shape[1] * asked.shape[2]
    return pl.pallas_call(
        functools.partial(index_kernel, groups),
        out_shape=[
            bf16(3 * total, rows),
            bf16(total, total),
            bf16(total, width),
            bf16(total, width),
            bf16(total, width),
        ],
        compiler_params=params(),
        cost_estimate=pl.CostEstimate(
            flops=6 * total * rows * width, bytes_accessed=4 * rows * width, transcendentals=0
        ),
        name="index_and_serve",
    )(x, asked)


def combine_kernel(expand_ref, far_ref, own_ref, core_ref, *out_refs):
    cap, sent = out_refs[0].shape[0], far_ref.shape[0]
    far = jnp.dot(expand_ref[:, :sent], far_ref[...], preferred_element_type=jnp.float32)
    rows = (far + own_ref[...].astype(jnp.float32) + core_ref[...].astype(jnp.float32)).astype(
        jnp.bfloat16
    )
    for d, out in enumerate(out_refs):
        out[...] = rows[d * cap : (d + 1) * cap]


def combine_call(expand, far, own, core, servers):
    total, width = own.shape
    return pl.pallas_call(
        combine_kernel,
        out_shape=[bf16(total // servers, width)] * servers,
        compiler_params=params(),
        cost_estimate=pl.CostEstimate(
            flops=2 * total * far.shape[0] * width,
            bytes_accessed=8 * total * width,
            transcendentals=0,
        ),
        name="combine",
    )(expand, far, own, core)


def fill(buffer, parts):
    cap = parts[0].shape[0]
    for d, ref in enumerate(parts):
        buffer[d * cap : (d + 1) * cap] = ref[...]


def weigh(x, buffer, mask):
    sims = lax.dot_general(x, buffer, (((1,), (1,)), ((), ())), preferred_element_type=jnp.float32)
    positive = jnp.maximum(sims * (1.0 / x.shape[1]), 0.0)
    return (positive * positive * positive).astype(jnp.bfloat16) * mask


def add_up(x, weights, buffer):
    mixed = x.astype(jnp.float32) + jnp.dot(weights, buffer, preferred_element_type=jnp.float32)
    return normalize(mixed).astype(jnp.bfloat16)


def last_kernel(servers, x_ref, mask_ref, *rest):
    parts, out_ref, buffer = rest[:servers], rest[servers], rest[servers + 1]

    @pl.when(pl.program_id(0) == 0)
    def _():
        fill(buffer, parts)

    x = x_ref[...]
    out_ref[...] = add_up(x, weigh(x, buffer[...], mask_ref[...]), buffer[...])


def last_call(x, mask, parts):
    rows, width = x.shape
    total, servers = mask.shape[1], len(parts)
    return pl.pallas_call(
        functools.partial(last_kernel, servers),
        grid=(rows // BLOCK,),
        in_specs=[
            pl.BlockSpec((BLOCK, width), lambda i: (i, 0)),
            pl.BlockSpec((BLOCK, total), lambda i: (i, 0)),
        ]
        + [pl.BlockSpec(part.shape, lambda i: (0, 0)) for part in parts],
        out_specs=pl.BlockSpec((BLOCK, width), lambda i: (i, 0)),
        out_shape=bf16(rows, width),
        scratch_shapes=[pltpu.VMEM((total, width), jnp.bfloat16)],
        compiler_params=params(),
        cost_estimate=pl.CostEstimate(
            flops=4 * total * rows * width, bytes_accessed=4 * rows * width, transcendentals=rows
        ),
        name="mix",
    )(x, mask, *parts)


def round_kernel(servers, x_ref, mask_ref, select_ref, *rest):
    parts, rest = rest[:servers], rest[servers:]
    out_ref, core_ref, own_ref, far_ref, buffer, weights = rest
    fill(buffer, parts)
    weights[...] = weigh(x_ref[...], buffer[...], mask_ref[...])
    for start in range(0, x_ref.shape[0], BLOCK):
        stop = start + BLOCK
        out_ref[start:stop] = add_up(x_ref[start:stop], weights[start:stop], buffer[...])
    serve(out_ref[...], select_ref, core_ref, own_ref, far_ref)


def round_call(x, mask, select, parts, sent):
    rows, width = x.shape
    total, servers = mask.shape[1], len(parts)
    return pl.pallas_call(
        functools.partial(round_kernel, servers),
        out_shape=[bf16(rows, width), bf16(total, width), bf16(total, width), bf16(sent, width)],
        scratch_shapes=[
            pltpu.VMEM((total, width), jnp.bfloat16),
            pltpu.VMEM((rows, total), jnp.bfloat16),
        ],
        compiler_params=params(),
        cost_estimate=pl.CostEstimate(
            flops=10 * total * rows * width, bytes_accessed=6 * rows * width, transcendentals=rows
        ),
        name="mix_and_serve",
    )(x, mask, select, *parts)


def local(descriptors, request, pick):
    wanted = request[0, 0]
    servers, cap = wanted.shape
    total = servers * cap
    groups = lax.axis_size("rep")
    within = [(g, g ^ 1) for g in range(groups)]
    beyond = [(g, (g + 2 * (g % 2) - 1 + groups) % groups) for g in range(groups)]

    everyone = servers * groups
    asked = lax.all_to_all(
        jnp.broadcast_to(wanted[None], (everyone, servers, cap)),
        ("clus", "rep"),
        split_axis=0,
        concat_axis=0,
        tiled=True,
    )
    x, mask = normalize_call(descriptors[0, 0], pick[0, 0], total, cap)
    select, expand, core, own, far = index_call(x, asked, groups)
    for step in range(ROUNDS):
        far = lax.ppermute(far, "rep", beyond)
        core = lax.ppermute(core, "rep", within)
        parts = combine_call(expand, far, own, core, servers)
        parts = [parts[0]] + [
            lax.ppermute(parts[d], "clus", [(c, c ^ d) for c in range(servers)])
            for d in range(1, servers)
        ]
        if step < ROUNDS - 1:
            x, core, own, far = round_call(x, mask, select, parts, far.shape[0])
        else:
            x = last_call(x, mask, parts)
    return x[None, None]


def solution(mesh):
    return jax.shard_map(
        local,
        mesh=mesh,
        in_specs=(
            P("rep", "clus", None, None),
            P("rep", "clus", None, None),
            P("rep", "clus", None, None),
        ),
        out_specs=P("rep", "clus", None, None),
        check_vma=False,
    )
```

time: 169 us -> 72.1 us (0.43)
  waiting for transfers between devices: 86.2 us -> 39.3 us
  other arithmetic: 28.8 us -> 0.68 us
  blocking collectives: 20.3 us -> 0 us
  Pallas kernels: 0 us -> 11.7 us
  matrix products: 8.51 us -> 0 us
  local copies, waits for them, and re-layouts: 11.6 us -> 4.46 us
  starting transfers between devices: 12.5 us -> 15.6 us
    ppermute x4 -> x10, waiting for transfers between devices: 78.5 us -> 36.3 us  [the longest x2 27.3 us: local(): far = lax.ppermute(far, 'rep', beyond)]
    all_to_all x2 -> x0, blocking collectives: 20.3 us -> none  [the longest x1 11.7 us: local(): lax.all_to_all(served.reshape(servers, slot_cap, width), 'clus', split_ax...]
    concatenate x2 -> x0, other arithmetic: 16.7 us -> none  [with_halo(): block = jnp.concatenate([low, block, high], axis=dim)]
    pallas_call x0 -> x6, Pallas kernels: none -> 11.7 us  [the longest x1 4.51 us: last_call(): pl.pallas_call(functools.partial(last_kernel, servers), grid=(rows // BLO...]
    gather x2 -> x0, local copies, waits for them, and re-layouts: 11 us -> none  [local(): served = window_rows[incoming]]
    dot_general x2 -> x0, matrix products: 8.51 us -> none  [local(): jnp.dot(weights, buffer, preferred_element_type=jnp.float32)]
    all_to_all x1, waiting for transfers between devices: 7.7 us -> 3.01 us  [local(): lax.all_to_all(jnp.broadcast_to(wanted[None], (everyone, servers, cap)),...]
    convert_element_type x2 -> x0, other arithmetic: 4.47 us -> none  [the longest x1 2.47 us: local(): current = normalize(mixed).astype(jnp.bfloat16)]
  transfers between devices with their start and end apart: 5 -> 11, of which waited for: 4 -> 9; matrix products, arithmetic and copies ran while one was open for 1% -> 1% of each run, Pallas kernels for 0% -> 2%
where the time goes in v2:
time: 72.1 us; the launch traced here: 71.8 us
  waiting for transfers between devices  39.3 us (55%)
  starting transfers between devices  15.6 us (22%)
  Pallas kernels  11.7 us (16%)
  local copies, waits for them, and re-layouts  4.46 us (6%)
    ppermute x2, waiting for transfers between devices, local(): far = lax.ppermute(far, 'rep', beyond)  27.3 us
    ppermute x6, waiting for transfers between devices, local(): lax.ppermute(parts[d], 'clus', [(c, c ^ d) for c in range(servers)])  9.02 us
    all_to_all x1, starting transfers between devices, local(): lax.all_to_all(jnp.broadcast_to(wanted[None], (everyone, servers, cap)),...  7.3 us
    ppermute x6, starting transfers between devices, local(): lax.ppermute(parts[d], 'clus', [(c, c ^ d) for c in range(servers)])  7.11 us
    pallas_call x1, Pallas kernels, last_call(): pl.pallas_call(functools.partial(last_kernel, servers), grid=(rows // BLO...  4.51 us
    pallas_call x1, Pallas kernels, round_call(): pl.pallas_call(functools.partial(round_kernel, servers), out_shape=[bf16(...  3.47 us
    unnamed x5, local copies, waits for them, and re-layouts  3.26 us
    all_to_all x1, waiting for transfers between devices, local(): lax.all_to_all(jnp.broadcast_to(wanted[None], (everyone, servers, cap)),...  3.01 us
  transfers between devices with their start and end apart: 11, of which 9 were waited for; matrix products, arithmetic and copies ran while one was open for 1% of the time, Pallas kernels for 2%

profile of v2, /device:TPU:0, one launch (start us, length us, event | category | flops | bytes accessed | tf_op | source)
XLA Modules:
  0.0 71.8 jit_solution(16841389170684915291)
XLA Ops:
  0.0 0.7 broadcast_in_dim.11
  0.7 0.7 reshape.1
  1.4 7.3 %all-to-all-start = ((s32[32,1,128]{2,1,0:T(1,128)}), s32[32,1,128]{2,1,0:T(1,128)S(1)}, u32[]{:S(2)}, u32[]{:S(2)}) async-start(s32[32,1,128]{2,1,0:T(1,128)} %reshape.1), calls=%async_computation | async-start | bytes 32768 | tf_op jit(solution)/shard_map/all_to_all | solution.py:263
  8.7 0.9 %copy.4 = s32[1,1,512,10]{3,2,1,0:T(8,128)S(1)} copy(s32[1,1,512,10]{2,1,3,0:T(1,128)} %param.5) | data formatting | bytes 40960 | tf_op args[2]
  9.6 0.0 copy-start
  9.6 1.6 %copy-done = bf16[1,1,512,2048]{3,2,1,0:T(8,128)(2,1)S(1)} copy-done((bf16[1,1,512,2048]{3,2,1,0:T(8,128)(2,1)S(1)}, bf16[1,1,512,2048]{3,2,1,0:T(8,128)(2,1)}, u32[]{:S(2)}) %copy-start) | copy-done | bytes 2097176
  11.2 1.6 %normalize.1 = (bf16[512,2048]{1,0:T(8,128)(2,1)S(1)}, bf16[512,128]{1,0:T(8,128)(2,1)S(1)}) custom-call(bf16[512,2048]{1,0:T(8,128)(2,1)S(1)} %bitcast.4, s32[512,10]{1,0:T(8,128)S(1)} %bitcast.5), custom_call_target="tpu_custom_call" | custom-call | flops 6291456 | bytes 4194304 | tf_op jit(solution)/shard_map/normalize/pallas_call | solution.py:39
  12.8 3.0 %all-to-all-done = s32[32,1,128]{2,1,0:T(1,128)S(1)} async-done(((s32[32,1,128]{2,1,0:T(1,128)}), s32[32,1,128]{2,1,0:T(1,128)S(1)}, u32[]{:S(2)}, u32[]{:S(2)}) %all-to-all-start) | async-done | bytes 16416 | tf_op jit(solution)/shard_map/all_to_all | solution.py:263
  15.8 0.5 broadcast
  16.3 0.7 reduce
  17.0 0.1 reshape.2.asked_ref
  17.1 1.5 %index_and_serve.1 = (bf16[384,512]{1,0:T(8,128)(2,1)S(1)}, bf16[128,128]{1,0:T(8,128)(2,1)S(1)}, bf16[128,2048]{1,0:T(8,128)(2,1)S(1)}, bf16[128,2048]{1,0:T(8,128)(2,1)S(1)}, bf16[128,2048]{1,0:T(8,128)(2,1)S(1)}) custom-call(bf16[512,2048]{1,0:T(8,128)(2,1)S(1)} %get-tuple-element.24.x_ref, s32[32,4,32]{2,1,0:T(4,128)S(1)} %reshape.2.asked_ref), custom_call_target="tpu_custom_call" | custom-call | flops 805306368 | bytes 4194304 | tf_op jit(solution)/shard_map/index_and_serve/pallas_call | solution.py:133
  18.6 0.4 collective-permute-start
  19.0 0.3 collective-permute-start.1
  19.3 13.6 %collective-permute-done.far_ref = bf16[128,2048]{1,0:T(8,128)(2,1)S(1)} collective-permute-done((bf16[128,2048]{1,0:T(8,128)(2,1)S(1)}, bf16[128,2048]{1,0:T(8,128)(2,1)S(1)}, u32[]{:S(2)}, u32[]{:S(2)}) %collective-permute-start) | collective-permute-done | bytes 524320 | tf_op jit(solution)/shard_map/ppermute | solution.py:273
  32.9 0.0 collective-permute-done.1.core_ref
  32.9 0.3 combine.2
  33.2 0.9 %collective-permute-start.2 = (bf16[32,2048]{1,0:T(8,128)(2,1)S(1)}, bf16[32,2048]{1,0:T(8,128)(2,1)S(1)}, u32[]{:S(2)}, u32[]{:S(2)}) collective-permute-start(bf16[32,2048]{1,0:T(8,128)(2,1)S(1)} %get-tuple-element.32), channel_id=1, source_target_pairs={{0,8},{8,0},{16,24},{24,16},{1,9},{9,1},{17,25},{25,17},{2,10},{10... | collective-permute-start | bytes 393224 | tf_op jit(solution)/shard_map/ppermute | solution.py:277
  34.1 1.5 %collective-permute-start.3 = (bf16[32,2048]{1,0:T(8,128)(2,1)S(1)}, bf16[32,2048]{1,0:T(8,128)(2,1)S(1)}, u32[]{:S(2)}, u32[]{:S(2)}) collective-permute-start(bf16[32,2048]{1,0:T(8,128)(2,1)S(1)} %get-tuple-element.33), channel_id=1, source_target_pairs={{0,16},{8,24},{16,0},{24,8},{1,17},{9,25},{17,1},{25,9},{2,18},{10... | collective-permute-start | bytes 393224 | tf_op jit(solution)/shard_map/ppermute | solution.py:277
  35.6 1.1 %collective-permute-start.4 = (bf16[32,2048]{1,0:T(8,128)(2,1)S(1)}, bf16[32,2048]{1,0:T(8,128)(2,1)S(1)}, u32[]{:S(2)}, u32[]{:S(2)}) collective-permute-start(bf16[32,2048]{1,0:T(8,128)(2,1)S(1)} %get-tuple-element.34), channel_id=1, source_target_pairs={{0,24},{8,16},{16,8},{24,0},{1,25},{9,17},{17,9},{25,1},{2,26},{10... | collective-permute-start | bytes 393224 | tf_op jit(solution)/shard_map/ppermute | solution.py:277
  36.8 1.6 %collective-permute-done.2.rest_1_ = bf16[32,2048]{1,0:T(8,128)(2,1)S(1)} collective-permute-done((bf16[32,2048]{1,0:T(8,128)(2,1)S(1)}, bf16[32,2048]{1,0:T(8,128)(2,1)S(1)}, u32[]{:S(2)}, u32[]{:S(2)}) %collective-permute-start.2) | collective-permute-done | bytes 131104 | tf_op jit(solution)/shard_map/ppermute | solution.py:277
  38.4 0.7 %collective-permute-done.3.rest_2_ = bf16[32,2048]{1,0:T(8,128)(2,1)S(1)} collective-permute-done((bf16[32,2048]{1,0:T(8,128)(2,1)S(1)}, bf16[32,2048]{1,0:T(8,128)(2,1)S(1)}, u32[]{:S(2)}, u32[]{:S(2)}) %collective-permute-start.3) | collective-permute-done | bytes 131104 | tf_op jit(solution)/shard_map/ppermute | solution.py:277
  39.1 2.4 %collective-permute-done.4.rest_3_ = bf16[32,2048]{1,0:T(8,128)(2,1)S(1)} collective-permute-done((bf16[32,2048]{1,0:T(8,128)(2,1)S(1)}, bf16[32,2048]{1,0:T(8,128)(2,1)S(1)}, u32[]{:S(2)}, u32[]{:S(2)}) %collective-permute-start.4) | collective-permute-done | bytes 131104 | tf_op jit(solution)/shard_map/ppermute | solution.py:277
  41.5 3.5 %mix_and_serve.1 = (bf16[512,2048]{1,0:T(8,128)(2,1)S(1)}, bf16[128,2048]{1,0:T(8,128)(2,1)S(1)}, bf16[128,2048]{1,0:T(8,128)(2,1)S(1)}, bf16[128,2048]{1,0:T(8,128)(2,1)S(1)}) custom-call(bf16[512,2048]{1,0:T(8,128)(2,1)S(1)} %get-tuple-element.24.x_ref, bf16[512,128]{1,0:T(8,128)(2,1)S(1)} %get-tuple-element.25.mask_ref, ...), custom_call_target="tpu_custom_call" | custom-call | flops 1342177280 | bytes 6291456 | tf_op jit(solution)/shard_map/mix_and_serve/pallas_call | solution.py:239
  45.0 0.5 collective-permute-start.5
  45.5 0.0 collective-permute-start.6
  45.5 13.7 %collective-permute-done.5.far_ref = bf16[128,2048]{1,0:T(8,128)(2,1)S(1)} collective-permute-done((bf16[128,2048]{1,0:T(8,128)(2,1)S(1)}, bf16[128,2048]{1,0:T(8,128)(2,1)S(1)}, u32[]{:S(2)}, u32[]{:S(2)}) %collective-permute-start.5) | collective-permute-done | bytes 524320 | tf_op jit(solution)/shard_map/ppermute | solution.py:273
  59.2 0.0 collective-permute-done.6.core_ref
  59.2 0.3 combine.3
  59.5 0.4 collective-permute-start.7
  59.9 1.6 %collective-permute-start.8 = (bf16[32,2048]{1,0:T(8,128)(2,1)S(1)}, bf16[32,2048]{1,0:T(8,128)(2,1)S(1)}, u32[]{:S(2)}, u32[]{:S(2)}) collective-permute-start(bf16[32,2048]{1,0:T(8,128)(2,1)S(1)} %get-tuple-element.41), channel_id=1, source_target_pairs={{0,16},{8,24},{16,0},{24,8},{1,17},{9,25},{17,1},{25,9},{2,18},{10... | collective-permute-start | bytes 393224 | tf_op jit(solution)/shard_map/ppermute | solution.py:277
  61.5 1.6 %collective-permute-start.9 = (bf16[32,2048]{1,0:T(8,128)(2,1)S(1)}, bf16[32,2048]{1,0:T(8,128)(2,1)S(1)}, u32[]{:S(2)}, u32[]{:S(2)}) collective-permute-start(bf16[32,2048]{1,0:T(8,128)(2,1)S(1)} %get-tuple-element.42), channel_id=1, source_target_pairs={{0,24},{8,16},{16,8},{24,0},{1,25},{9,17},{17,9},{25,1},{2,26},{10... | collective-permute-start | bytes 393224 | tf_op jit(solution)/shard_map/ppermute | solution.py:277
  63.0 1.5 %collective-permute-done.7.rest_1_ = bf16[32,2048]{1,0:T(8,128)(2,1)S(1)} collective-permute-done((bf16[32,2048]{1,0:T(8,128)(2,1)S(1)}, bf16[32,2048]{1,0:T(8,128)(2,1)S(1)}, u32[]{:S(2)}, u32[]{:S(2)}) %collective-permute-start.7) | collective-permute-done | bytes 131104 | tf_op jit(solution)/shard_map/ppermute | solution.py:277
  64.5 0.3 collective-permute-done.8.rest_2_
  64.8 2.5 %collective-permute-done.9.rest_3_ = bf16[32,2048]{1,0:T(8,128)(2,1)S(1)} collective-permute-done((bf16[32,2048]{1,0:T(8,128)(2,1)S(1)}, bf16[32,2048]{1,0:T(8,128)(2,1)S(1)}, u32[]{:S(2)}, u32[]{:S(2)}) %collective-permute-start.9) | collective-permute-done | bytes 131104 | tf_op jit(solution)/shard_map/ppermute | solution.py:277
  67.3 4.5 %mix.1 = bf16[512,2048]{1,0:T(8,128)(2,1)} custom-call(bf16[512,2048]{1,0:T(8,128)(2,1)S(1)} %get-tuple-element.35.x_ref, bf16[512,128]{1,0:T(8,128)(2,1)S(1)} %get-tuple-element.25.mask_ref, bf16[32,2048]{1,0:T(8,128)(2,1)S(1)} %get-tuple-element.39.rest_0_, bf16[32,2048]{1,0:T(8,128)(2,1)S(1)} %collective-permute-done.7.rest_1_, ...), custom_call_target="tpu_custom_call" | custom-call | flops 536870912 | bytes 4194304 | tf_op jit(solution)/shard_map/mix/pallas_call | solution.py:206
Async XLA Ops:
  1.4 14.4 %all-to-all-start = ((s32[32,1,128]{2,1,0:T(1,128)}), s32[32,1,128]{2,1,0:T(1,128)S(1)}, u32[]{:S(2)}, u32[]{:S(2)}) async-start(s32[32,1,128]{2,1,0:T(1,128)} %reshape.1), calls=%async_computation | async-start | bytes 32768 | tf_op jit(solution)/shard_map/all_to_all | solution.py:263
  9.6 1.6 %copy-start = (bf16[1,1,512,2048]{3,2,1,0:T(8,128)(2,1)S(1)}, bf16[1,1,512,2048]{3,2,1,0:T(8,128)(2,1)}, u32[]{:S(2)}) copy-start(bf16[1,1,512,2048]{3,2,1,0:T(8,128)(2,1)} %param.3) | copy-start | bytes 6291460
  18.6 14.3 %collective-permute-start = (bf16[128,2048]{1,0:T(8,128)(2,1)S(1)}, bf16[128,2048]{1,0:T(8,128)(2,1)S(1)}, u32[]{:S(2)}, u32[]{:S(2)}) collective-permute-start(bf16[128,2048]{1,0:T(8,128)(2,1)S(1)} %get-tuple-element.28), channel_id=1, source_target_pairs={{0,7},{1,2},{2,1},{3,4},{4,3},{5,6},{6,5},{7,0},{8,15},{9,10},{10,... | collective-permute-start | bytes 1572872 | tf_op jit(solution)/shard_map/ppermute | solution.py:273
  19.0 13.9 %collective-permute-start.1 = (bf16[128,2048]{1,0:T(8,128)(2,1)S(1)}, bf16[128,2048]{1,0:T(8,128)(2,1)S(1)}, u32[]{:S(2)}, u32[]{:S(2)}) collective-permute-start(bf16[128,2048]{1,0:T(8,128)(2,1)S(1)} %get-tuple-element.30), channel_id=1, source_target_pairs={{0,1},{1,0},{2,3},{3,2},{4,5},{5,4},{6,7},{7,6},{8,9},{9,8},{10,11... | collective-permute-start | bytes 1572872 | tf_op jit(solution)/shard_map/ppermute | solution.py:274
  33.2 5.1 %collective-permute-start.2 = (bf16[32,2048]{1,0:T(8,128)(2,1)S(1)}, bf16[32,2048]{1,0:T(8,128)(2,1)S(1)}, u32[]{:S(2)}, u32[]{:S(2)}) collective-permute-start(bf16[32,2048]{1,0:T(8,128)(2,1)S(1)} %get-tuple-element.32), channel_id=1, source_target_pairs={{0,8},{8,0},{16,24},{24,16},{1,9},{9,1},{17,25},{25,17},{2,10},{10... | collective-permute-start | bytes 393224 | tf_op jit(solution)/shard_map/ppermute | solution.py:277
  34.1 5.0 %collective-permute-start.3 = (bf16[32,2048]{1,0:T(8,128)(2,1)S(1)}, bf16[32,2048]{1,0:T(8,128)(2,1)S(1)}, u32[]{:S(2)}, u32[]{:S(2)}) collective-permute-start(bf16[32,2048]{1,0:T(8,128)(2,1)S(1)} %get-tuple-element.33), channel_id=1, source_target_pairs={{0,16},{8,24},{16,0},{24,8},{1,17},{9,25},{17,1},{25,9},{2,18},{10... | collective-permute-start | bytes 393224 | tf_op jit(solution)/shard_map/ppermute | solution.py:277
  35.6 5.9 %collective-permute-start.4 = (bf16[32,2048]{1,0:T(8,128)(2,1)S(1)}, bf16[32,2048]{1,0:T(8,128)(2,1)S(1)}, u32[]{:S(2)}, u32[]{:S(2)}) collective-permute-start(bf16[32,2048]{1,0:T(8,128)(2,1)S(1)} %get-tuple-element.34), channel_id=1, source_target_pairs={{0,24},{8,16},{16,8},{24,0},{1,25},{9,17},{17,9},{25,1},{2,26},{10... | collective-permute-start | bytes 393224 | tf_op jit(solution)/shard_map/ppermute | solution.py:277
  45.0 14.2 %collective-permute-start.5 = (bf16[128,2048]{1,0:T(8,128)(2,1)S(1)}, bf16[128,2048]{1,0:T(8,128)(2,1)S(1)}, u32[]{:S(2)}, u32[]{:S(2)}) collective-permute-start(bf16[128,2048]{1,0:T(8,128)(2,1)S(1)} %get-tuple-element.36), channel_id=1, source_target_pairs={{0,7},{1,2},{2,1},{3,4},{4,3},{5,6},{6,5},{7,0},{8,15},{9,10},{10,... | collective-permute-start | bytes 1572872 | tf_op jit(solution)/shard_map/ppermute | solution.py:273
  45.5 13.7 %collective-permute-start.6 = (bf16[128,2048]{1,0:T(8,128)(2,1)S(1)}, bf16[128,2048]{1,0:T(8,128)(2,1)S(1)}, u32[]{:S(2)}, u32[]{:S(2)}) collective-permute-start(bf16[128,2048]{1,0:T(8,128)(2,1)S(1)} %get-tuple-element.38), channel_id=1, source_target_pairs={{0,1},{1,0},{2,3},{3,2},{4,5},{5,4},{6,7},{7,6},{8,9},{9,8},{10,11... | collective-permute-start | bytes 1572872 | tf_op jit(solution)/shard_map/ppermute | solution.py:274
  59.5 5.0 %collective-permute-start.7 = (bf16[32,2048]{1,0:T(8,128)(2,1)S(1)}, bf16[32,2048]{1,0:T(8,128)(2,1)S(1)}, u32[]{:S(2)}, u32[]{:S(2)}) collective-permute-start(bf16[32,2048]{1,0:T(8,128)(2,1)S(1)} %get-tuple-element.40), channel_id=1, source_target_pairs={{0,8},{8,0},{16,24},{24,16},{1,9},{9,1},{17,25},{25,17},{2,10},{10... | collective-permute-start | bytes 393224 | tf_op jit(solution)/shard_map/ppermute | solution.py:277
  59.9 5.0 %collective-permute-start.8 = (bf16[32,2048]{1,0:T(8,128)(2,1)S(1)}, bf16[32,2048]{1,0:T(8,128)(2,1)S(1)}, u32[]{:S(2)}, u32[]{:S(2)}) collective-permute-start(bf16[32,2048]{1,0:T(8,128)(2,1)S(1)} %get-tuple-element.41), channel_id=1, source_target_pairs={{0,16},{8,24},{16,0},{24,8},{1,17},{9,25},{17,1},{25,9},{2,18},{10... | collective-permute-start | bytes 393224 | tf_op jit(solution)/shard_map/ppermute | solution.py:277
  61.5 5.9 %collective-permute-start.9 = (bf16[32,2048]{1,0:T(8,128)(2,1)S(1)}, bf16[32,2048]{1,0:T(8,128)(2,1)S(1)}, u32[]{:S(2)}, u32[]{:S(2)}) collective-permute-start(bf16[32,2048]{1,0:T(8,128)(2,1)S(1)} %get-tuple-element.42), channel_id=1, source_target_pairs={{0,24},{8,16},{16,8},{24,0},{1,25},{9,17},{17,9},{25,1},{2,26},{10... | collective-permute-start | bytes 393224 | tf_op jit(solution)/shard_map/ppermute | solution.py:277

commit v3 on v2

--- a/solution.py
+++ b/solution.py
@@ -190,14 +190,18 @@
 
 
 def last_kernel(servers, x_ref, mask_ref, *rest):
-    parts, out_ref, buffer = rest[:servers], rest[servers], rest[servers + 1]
-
-    @pl.when(pl.program_id(0) == 0)
-    def _():
-        fill(buffer, parts)
-
-    x = x_ref[...]
-    out_ref[...] = add_up(x, weigh(x, buffer[...], mask_ref[...]), buffer[...])
+    parts, rest = rest[:servers], rest[servers:]
+    out_ref, buffer, weights, whole, sems = rest
+    fill(buffer, parts)
+    weights[...] = weigh(x_ref[...], buffer[...], mask_ref[...])
+    copies = []
+    for i, start in enumerate(range(0, x_ref.shape[0], BLOCK)):
+        here = pl.ds(start, BLOCK)
+        whole[here] = add_up(x_ref[here], weights[here], buffer[...])
+        copies.append(pltpu.make_async_copy(whole.at[here], out_ref.at[here], sems.at[i]))
+        copies[-1].start()
+    for copy in copies:
+        copy.wait()
 
 
 def last_call(x, mask, parts):
@@ -205,15 +209,14 @@
     total, servers = mask.shape[1], len(parts)
     return pl.pallas_call(
         functools.partial(last_kernel, servers),
-        grid=(rows // BLOCK,),
-        in_specs=[
-            pl.BlockSpec((BLOCK, width), lambda i: (i, 0)),
-            pl.BlockSpec((BLOCK, total), lambda i: (i, 0)),
-        ]
-        + [pl.BlockSpec(part.shape, lambda i: (0, 0)) for part in parts],
-        out_specs=pl.BlockSpec((BLOCK, width), lambda i: (i, 0)),
+        out_specs=pl.BlockSpec(memory_space=pl.ANY),
         out_shape=bf16(rows, width),
-        scratch_shapes=[pltpu.VMEM((total, width), jnp.bfloat16)],
+        scratch_shapes=[
+            pltpu.VMEM((total, width), jnp.bfloat16),
+            pltpu.VMEM((rows, total), jnp.bfloat16),
+            pltpu.VMEM((rows, width), jnp.bfloat16),
+            pltpu.SemaphoreType.DMA((rows // BLOCK,)),
+        ],
         compiler_params=params(),
         cost_estimate=pl.CostEstimate(
             flops=4 * total * rows * width, bytes_accessed=4 * rows * width, transcendentals=rows
@@ -259,14 +262,7 @@
     within = [(g, g ^ 1) for g in range(groups)]
     beyond = [(g, (g + 2 * (g % 2) - 1 + groups) % groups) for g in range(groups)]
 
-    everyone = servers * groups
-    asked = lax.all_to_all(
-        jnp.broadcast_to(wanted[None], (everyone, servers, cap)),
-        ("clus", "rep"),
-        split_axis=0,
-        concat_axis=0,
-        tiled=True,
-    )
+    asked = lax.all_gather(wanted, ("clus", "rep"), axis=0, tiled=False)
     x, mask = normalize_call(descriptors[0, 0], pick[0, 0], total, cap)
     select, expand, core, own, far = index_call(x, asked, groups)
     for step in range(ROUNDS):

time: 72.1 us -> 101 us (1.40)
  blocking collectives: 0 us -> 43.7 us
  starting transfers between devices: 15.6 us -> 9.41 us
  waiting for transfers between devices: 39.3 us -> 34.2 us
  local copies, waits for them, and re-layouts: 4.46 us -> 2.45 us
  Pallas kernels: 11.7 us -> 10.5 us
    all_gather x0 -> x1, blocking collectives: none -> 43.7 us  [local(): asked = lax.all_gather(wanted, ('clus', 'rep'), axis=0, tiled=False)]
    all_to_all x1 -> x0, starting transfers between devices: 7.3 us -> none  [local(): lax.all_to_all(jnp.broadcast_to(wanted[None], (everyone, servers, cap)),...]
    ppermute x2, waiting for transfers between devices: 27.3 us -> 24.3 us  [local(): far = lax.ppermute(far, 'rep', beyond)]
    all_to_all x1 -> x0, waiting for transfers between devices: 3.01 us -> none  [local(): lax.all_to_all(jnp.broadcast_to(wanted[None], (everyone, servers, cap)),...]
    pallas_call x1, Pallas kernels: 4.51 us -> 3.33 us  [last_call(): pl.pallas_call(functools.partial(last_kernel, servers), out_specs=pl.Bloc...]
    unnamed x5 -> x3, local copies, waits for them, and re-layouts: 3.26 us -> 2.45 us
  transfers between devices with their start and end apart: 11 -> 10, of which waited for: 9 -> 7; matrix products, arithmetic and copies ran while one was open for 1% -> 0% of each run, Pallas kernels for 2% -> 0%
where the time goes in v3:
time: 101 us; the launch traced here: 100 us
  blocking collectives  43.7 us (43%)
  waiting for transfers between devices  34.2 us (34%)
  Pallas kernels  10.5 us (10%)
  starting transfers between devices  9.41 us (9%)
  local copies, waits for them, and re-layouts  2.45 us (2%)
    all_gather x1, blocking collectives, local(): asked = lax.all_gather(wanted, ('clus', 'rep'), axis=0, tiled=False)  43.7 us
    ppermute x2, waiting for transfers between devices, local(): far = lax.ppermute(far, 'rep', beyond)  24.3 us
    ppermute x6, waiting for transfers between devices, local(): lax.ppermute(parts[d], 'clus', [(c, c ^ d) for c in range(servers)])  9.96 us
    ppermute x6, starting transfers between devices, local(): lax.ppermute(parts[d], 'clus', [(c, c ^ d) for c in range(servers)])  7.1 us
    pallas_call x1, Pallas kernels, round_call(): pl.pallas_call(functools.partial(round_kernel, servers), out_shape=[bf16(...  3.47 us
    pallas_call x1, Pallas kernels, last_call(): pl.pallas_call(functools.partial(last_kernel, servers), out_specs=pl.Bloc...  3.33 us
    unnamed x3, local copies, waits for them, and re-layouts  2.45 us
  transfers between devices with their start and end apart: 10, of which 7 were waited for; matrix products, arithmetic and copies ran while one was open for 0% of the time, Pallas kernels for 0%

profile of v3, /device:TPU:0, one launch (start us, length us, event | category | flops | bytes accessed | tf_op | source)
XLA Modules:
  0.0 100.3 jit_solution(3145653654127685880)
XLA Ops:
  0.0 43.7 %all-gather = s32[32,1,4,32]{3,2,1,0:T(4,128)S(1)} all-gather(s32[1,1,4,32]{3,2,1,0:T(4,128)} %param.4), channel_id=2, replica_groups=mesh['clus'=4,'rep'=8] {'clus','rep'}, dimensions={0}, use_global_device_ids=true | all-gather | bytes 16896 | tf_op jit(solution)/shard_map/all_gather | solution.py:265
  43.7 0.9 copy.6
  44.5 0.0 copy-start
  44.6 1.6 %copy-done = bf16[1,1,512,2048]{3,2,1,0:T(8,128)(2,1)S(1)} copy-done((bf16[1,1,512,2048]{3,2,1,0:T(8,128)(2,1)S(1)}, bf16[1,1,512,2048]{3,2,1,0:T(8,128)(2,1)}, u32[]{:S(2)}) %copy-start) | copy-done | bytes 2097176
  46.1 1.6 %normalize.1 = (bf16[512,2048]{1,0:T(8,128)(2,1)S(1)}, bf16[512,128]{1,0:T(8,128)(2,1)S(1)}) custom-call(bf16[512,2048]{1,0:T(8,128)(2,1)S(1)} %bitcast.4, s32[512,10]{1,0:T(8,128)S(1)} %bitcast.5), custom_call_target="tpu_custom_call" | custom-call | flops 6291456 | bytes 4194304 | tf_op jit(solution)/shard_map/normalize/pallas_call | solution.py:39
  47.7 1.5 %index_and_serve.1 = (bf16[384,512]{1,0:T(8,128)(2,1)S(1)}, bf16[128,128]{1,0:T(8,128)(2,1)S(1)}, bf16[128,2048]{1,0:T(8,128)(2,1)S(1)}, bf16[128,2048]{1,0:T(8,128)(2,1)S(1)}, bf16[128,2048]{1,0:T(8,128)(2,1)S(1)}) custom-call(bf16[512,2048]{1,0:T(8,128)(2,1)S(1)} %get-tuple-element.24.x_ref, s32[32,4,32]{2,1,0:T(4,128)S(1)} %bitcast.6), custom_call_target="tpu_custom_call" | custom-call | flops 805306368 | bytes 4194304 | tf_op jit(solution)/shard_map/index_and_serve/pallas_call | solution.py:133
  49.2 0.1 collective-permute-start
  49.3 0.4 collective-permute-start.1
  49.7 11.7 %collective-permute-done.far_ref = bf16[128,2048]{1,0:T(8,128)(2,1)S(1)} collective-permute-done((bf16[128,2048]{1,0:T(8,128)(2,1)S(1)}, bf16[128,2048]{1,0:T(8,128)(2,1)S(1)}, u32[]{:S(2)}, u32[]{:S(2)}) %collective-permute-start) | collective-permute-done | bytes 524320 | tf_op jit(solution)/shard_map/ppermute | solution.py:269
  61.4 0.0 collective-permute-done.1.core_ref
  61.4 0.3 combine.2
  61.7 0.1 collective-permute-start.2
  61.8 1.2 %collective-permute-start.3 = (bf16[32,2048]{1,0:T(8,128)(2,1)S(1)}, bf16[32,2048]{1,0:T(8,128)(2,1)S(1)}, u32[]{:S(2)}, u32[]{:S(2)}) collective-permute-start(bf16[32,2048]{1,0:T(8,128)(2,1)S(1)} %get-tuple-element.33), channel_id=1, source_target_pairs={{0,16},{8,24},{16,0},{24,8},{1,17},{9,25},{17,1},{25,9},{2,18},{10... | collective-permute-start | bytes 393224 | tf_op jit(solution)/shard_map/ppermute | solution.py:273
  63.0 2.3 %collective-permute-start.4 = (bf16[32,2048]{1,0:T(8,128)(2,1)S(1)}, bf16[32,2048]{1,0:T(8,128)(2,1)S(1)}, u32[]{:S(2)}, u32[]{:S(2)}) collective-permute-start(bf16[32,2048]{1,0:T(8,128)(2,1)S(1)} %get-tuple-element.34), channel_id=1, source_target_pairs={{0,24},{8,16},{16,8},{24,0},{1,25},{9,17},{17,9},{25,1},{2,26},{10... | collective-permute-start | bytes 393224 | tf_op jit(solution)/shard_map/ppermute | solution.py:273
  65.3 1.5 %collective-permute-done.2.rest_1_ = bf16[32,2048]{1,0:T(8,128)(2,1)S(1)} collective-permute-done((bf16[32,2048]{1,0:T(8,128)(2,1)S(1)}, bf16[32,2048]{1,0:T(8,128)(2,1)S(1)}, u32[]{:S(2)}, u32[]{:S(2)}) %collective-permute-start.2) | collective-permute-done | bytes 131104 | tf_op jit(solution)/shard_map/ppermute | solution.py:273
  66.8 0.1 collective-permute-done.3.rest_2_
  66.8 3.4 %collective-permute-done.4.rest_3_ = bf16[32,2048]{1,0:T(8,128)(2,1)S(1)} collective-permute-done((bf16[32,2048]{1,0:T(8,128)(2,1)S(1)}, bf16[32,2048]{1,0:T(8,128)(2,1)S(1)}, u32[]{:S(2)}, u32[]{:S(2)}) %collective-permute-start.4) | collective-permute-done | bytes 131104 | tf_op jit(solution)/shard_map/ppermute | solution.py:273
  70.3 3.5 %mix_and_serve.1 = (bf16[512,2048]{1,0:T(8,128)(2,1)S(1)}, bf16[128,2048]{1,0:T(8,128)(2,1)S(1)}, bf16[128,2048]{1,0:T(8,128)(2,1)S(1)}, bf16[128,2048]{1,0:T(8,128)(2,1)S(1)}) custom-call(bf16[512,2048]{1,0:T(8,128)(2,1)S(1)} %get-tuple-element.24.x_ref, bf16[512,128]{1,0:T(8,128)(2,1)S(1)} %get-tuple-element.25.mask_ref, ...), custom_call_target="tpu_custom_call" | custom-call | flops 1342177280 | bytes 6291456 | tf_op jit(solution)/shard_map/mix_and_serve/pallas_call | solution.py:242
  73.8 1.8 %collective-permute-start.5 = (bf16[128,2048]{1,0:T(8,128)(2,1)S(1)}, bf16[128,2048]{1,0:T(8,128)(2,1)S(1)}, u32[]{:S(2)}, u32[]{:S(2)}) collective-permute-start(bf16[128,2048]{1,0:T(8,128)(2,1)S(1)} %get-tuple-element.36), channel_id=1, source_target_pairs={{0,7},{1,2},{2,1},{3,4},{4,3},{5,6},{6,5},{7,0},{8,15},{9,10},{10,... | collective-permute-start | bytes 1572872 | tf_op jit(solution)/shard_map/ppermute | solution.py:269
  75.6 0.0 collective-permute-start.6
  75.6 12.5 %collective-permute-done.5.far_ref = bf16[128,2048]{1,0:T(8,128)(2,1)S(1)} collective-permute-done((bf16[128,2048]{1,0:T(8,128)(2,1)S(1)}, bf16[128,2048]{1,0:T(8,128)(2,1)S(1)}, u32[]{:S(2)}, u32[]{:S(2)}) %collective-permute-start.5) | collective-permute-done | bytes 524320 | tf_op jit(solution)/shard_map/ppermute | solution.py:269
  88.1 0.0 collective-permute-done.6.core_ref
  88.1 0.3 combine.3
  88.5 0.4 collective-permute-start.7
  88.9 0.7 collective-permute-start.8
  89.6 2.5 %collective-permute-start.9 = (bf16[32,2048]{1,0:T(8,128)(2,1)S(1)}, bf16[32,2048]{1,0:T(8,128)(2,1)S(1)}, u32[]{:S(2)}, u32[]{:S(2)}) collective-permute-start(bf16[32,2048]{1,0:T(8,128)(2,1)S(1)} %get-tuple-element.42), channel_id=1, source_target_pairs={{0,24},{8,16},{16,8},{24,0},{1,25},{9,17},{17,9},{25,1},{2,26},{10... | collective-permute-start | bytes 393224 | tf_op jit(solution)/shard_map/ppermute | solution.py:273
  92.0 2.7 %collective-permute-done.7.rest_1_ = bf16[32,2048]{1,0:T(8,128)(2,1)S(1)} collective-permute-done((bf16[32,2048]{1,0:T(8,128)(2,1)S(1)}, bf16[32,2048]{1,0:T(8,128)(2,1)S(1)}, u32[]{:S(2)}, u32[]{:S(2)}) %collective-permute-start.7) | collective-permute-done | bytes 131104 | tf_op jit(solution)/shard_map/ppermute | solution.py:273
  94.8 0.0 collective-permute-done.8.rest_2_
  94.8 2.2 %collective-permute-done.9.rest_3_ = bf16[32,2048]{1,0:T(8,128)(2,1)S(1)} collective-permute-done((bf16[32,2048]{1,0:T(8,128)(2,1)S(1)}, bf16[32,2048]{1,0:T(8,128)(2,1)S(1)}, u32[]{:S(2)}, u32[]{:S(2)}) %collective-permute-start.9) | collective-permute-done | bytes 131104 | tf_op jit(solution)/shard_map/ppermute | solution.py:273
  97.0 3.3 %mix.1 = bf16[512,2048]{1,0:T(8,128)(2,1)} custom-call(bf16[512,2048]{1,0:T(8,128)(2,1)S(1)} %get-tuple-element.35.x_ref, bf16[512,128]{1,0:T(8,128)(2,1)S(1)} %get-tuple-element.25.mask_ref, bf16[32,2048]{1,0:T(8,128)(2,1)S(1)} %get-tuple-element.39.rest_0_, bf16[32,2048]{1,0:T(8,128)(2,1)S(1)} %collective-permute-done.7.rest_1_, ...), custom_call_target="tpu_custom_call" | custom-call | flops 536870912 | bytes 4194304 | tf_op jit(solution)/shard_map/mix/pallas_call | solution.py:210
Async XLA Ops:
  44.5 1.6 %copy-start = (bf16[1,1,512,2048]{3,2,1,0:T(8,128)(2,1)S(1)}, bf16[1,1,512,2048]{3,2,1,0:T(8,128)(2,1)}, u32[]{:S(2)}) copy-start(bf16[1,1,512,2048]{3,2,1,0:T(8,128)(2,1)} %param.3) | copy-start | bytes 6291460
  49.2 12.2 %collective-permute-start = (bf16[128,2048]{1,0:T(8,128)(2,1)S(1)}, bf16[128,2048]{1,0:T(8,128)(2,1)S(1)}, u32[]{:S(2)}, u32[]{:S(2)}) collective-permute-start(bf16[128,2048]{1,0:T(8,128)(2,1)S(1)} %get-tuple-element.28), channel_id=1, source_target_pairs={{0,7},{1,2},{2,1},{3,4},{4,3},{5,6},{6,5},{7,0},{8,15},{9,10},{10,... | collective-permute-start | bytes 1572872 | tf_op jit(solution)/shard_map/ppermute | solution.py:269
  49.3 12.1 %collective-permute-start.1 = (bf16[128,2048]{1,0:T(8,128)(2,1)S(1)}, bf16[128,2048]{1,0:T(8,128)(2,1)S(1)}, u32[]{:S(2)}, u32[]{:S(2)}) collective-permute-start(bf16[128,2048]{1,0:T(8,128)(2,1)S(1)} %get-tuple-element.30), channel_id=1, source_target_pairs={{0,1},{1,0},{2,3},{3,2},{4,5},{5,4},{6,7},{7,6},{8,9},{9,8},{10,11... | collective-permute-start | bytes 1572872 | tf_op jit(solution)/shard_map/ppermute | solution.py:270
  61.7 5.0 %collective-permute-start.2 = (bf16[32,2048]{1,0:T(8,128)(2,1)S(1)}, bf16[32,2048]{1,0:T(8,128)(2,1)S(1)}, u32[]{:S(2)}, u32[]{:S(2)}) collective-permute-start(bf16[32,2048]{1,0:T(8,128)(2,1)S(1)} %get-tuple-element.32), channel_id=1, source_target_pairs={{0,8},{8,0},{16,24},{24,16},{1,9},{9,1},{17,25},{25,17},{2,10},{10... | collective-permute-start | bytes 393224 | tf_op jit(solution)/shard_map/ppermute | solution.py:273
  61.8 5.0 %collective-permute-start.3 = (bf16[32,2048]{1,0:T(8,128)(2,1)S(1)}, bf16[32,2048]{1,0:T(8,128)(2,1)S(1)}, u32[]{:S(2)}, u32[]{:S(2)}) collective-permute-start(bf16[32,2048]{1,0:T(8,128)(2,1)S(1)} %get-tuple-element.33), channel_id=1, source_target_pairs={{0,16},{8,24},{16,0},{24,8},{1,17},{9,25},{17,1},{25,9},{2,18},{10... | collective-permute-start | bytes 393224 | tf_op jit(solution)/shard_map/ppermute | solution.py:273
  63.0 7.3 %collective-permute-start.4 = (bf16[32,2048]{1,0:T(8,128)(2,1)S(1)}, bf16[32,2048]{1,0:T(8,128)(2,1)S(1)}, u32[]{:S(2)}, u32[]{:S(2)}) collective-permute-start(bf16[32,2048]{1,0:T(8,128)(2,1)S(1)} %get-tuple-element.34), channel_id=1, source_target_pairs={{0,24},{8,16},{16,8},{24,0},{1,25},{9,17},{17,9},{25,1},{2,26},{10... | collective-permute-start | bytes 393224 | tf_op jit(solution)/shard_map/ppermute | solution.py:273
  73.8 14.4 %collective-permute-start.5 = (bf16[128,2048]{1,0:T(8,128)(2,1)S(1)}, bf16[128,2048]{1,0:T(8,128)(2,1)S(1)}, u32[]{:S(2)}, u32[]{:S(2)}) collective-permute-start(bf16[128,2048]{1,0:T(8,128)(2,1)S(1)} %get-tuple-element.36), channel_id=1, source_target_pairs={{0,7},{1,2},{2,1},{3,4},{4,3},{5,6},{6,5},{7,0},{8,15},{9,10},{10,... | collective-permute-start | bytes 1572872 | tf_op jit(solution)/shard_map/ppermute | solution.py:269
  75.6 12.5 %collective-permute-start.6 = (bf16[128,2048]{1,0:T(8,128)(2,1)S(1)}, bf16[128,2048]{1,0:T(8,128)(2,1)S(1)}, u32[]{:S(2)}, u32[]{:S(2)}) collective-permute-start(bf16[128,2048]{1,0:T(8,128)(2,1)S(1)} %get-tuple-element.38), channel_id=1, source_target_pairs={{0,1},{1,0},{2,3},{3,2},{4,5},{5,4},{6,7},{7,6},{8,9},{9,8},{10,11... | collective-permute-start | bytes 1572872 | tf_op jit(solution)/shard_map/ppermute | solution.py:270
  88.5 6.3 %collective-permute-start.7 = (bf16[32,2048]{1,0:T(8,128)(2,1)S(1)}, bf16[32,2048]{1,0:T(8,128)(2,1)S(1)}, u32[]{:S(2)}, u32[]{:S(2)}) collective-permute-start(bf16[32,2048]{1,0:T(8,128)(2,1)S(1)} %get-tuple-element.40), channel_id=1, source_target_pairs={{0,8},{8,0},{16,24},{24,16},{1,9},{9,1},{17,25},{25,17},{2,10},{10... | collective-permute-start | bytes 393224 | tf_op jit(solution)/shard_map/ppermute | solution.py:273
  88.9 5.9 %collective-permute-start.8 = (bf16[32,2048]{1,0:T(8,128)(2,1)S(1)}, bf16[32,2048]{1,0:T(8,128)(2,1)S(1)}, u32[]{:S(2)}, u32[]{:S(2)}) collective-permute-start(bf16[32,2048]{1,0:T(8,128)(2,1)S(1)} %get-tuple-element.41), channel_id=1, source_target_pairs={{0,16},{8,24},{16,0},{24,8},{1,17},{9,25},{17,1},{25,9},{2,18},{10... | collective-permute-start | bytes 393224 | tf_op jit(solution)/shard_map/ppermute | solution.py:273
  89.6 7.4 %collective-permute-start.9 = (bf16[32,2048]{1,0:T(8,128)(2,1)S(1)}, bf16[32,2048]{1,0:T(8,128)(2,1)S(1)}, u32[]{:S(2)}, u32[]{:S(2)}) collective-permute-start(bf16[32,2048]{1,0:T(8,128)(2,1)S(1)} %get-tuple-element.42), channel_id=1, source_target_pairs={{0,24},{8,16},{16,8},{24,0},{1,25},{9,17},{17,9},{25,1},{2,26},{10... | collective-permute-start | bytes 393224 | tf_op jit(solution)/shard_map/ppermute | solution.py:273

commit v4 on v3

--- a/solution.py
+++ b/solution.py
@@ -12,8 +12,11 @@
 BLOCK = 128
 
 
-def params():
-    return pltpu.CompilerParams(vmem_limit_bytes=32 * 1024 * 1024)
+FAR_SHARE = 3, 8
+
+
+def params(mib=32):
+    return pltpu.CompilerParams(vmem_limit_bytes=mib * 1024 * 1024)
 
 
 def bf16(*shape):
@@ -26,29 +29,31 @@
 
 def normalize_kernel(slot_cap, x_ref, pick_ref, out_ref, mask_ref):
     out_ref[...] = normalize(x_ref[...].astype(jnp.float32)).astype(jnp.bfloat16)
-    slot = lax.broadcasted_iota(jnp.int32, mask_ref.shape, 1)
+    shape = mask_ref.shape[1], mask_ref.shape[0]
+    slot = lax.broadcasted_iota(jnp.int32, shape, 0)
     slot = slot ^ (lax.axis_index("clus") * slot_cap)
-    chosen = jnp.zeros(mask_ref.shape, jnp.float32)
-    for k in range(pick_ref.shape[1]):
-        chosen = jnp.where(pick_ref[:, k : k + 1] == slot, 1.0, chosen)
-    mask_ref[...] = chosen.astype(jnp.bfloat16)
+    chosen = jnp.zeros(shape, jnp.float32)
+    for k in range(pick_ref.shape[0]):
+        chosen = jnp.where(pick_ref[k] == slot, 1.0, chosen)
+    mask_ref[...] = chosen.T.astype(jnp.bfloat16)
 
 
 def normalize_call(descriptors, slots, total, slot_cap):
     rows, width = descriptors.shape
+    count = slots.shape[0]
     return pl.pallas_call(
         functools.partial(normalize_kernel, slot_cap),
         grid=(rows // BLOCK,),
         in_specs=[
             pl.BlockSpec((BLOCK, width), lambda i: (i, 0)),
-            pl.BlockSpec((BLOCK, slots.shape[1]), lambda i: (i, 0)),
+            pl.BlockSpec((count, 1, BLOCK), lambda i: (0, 0, i)),
         ],
         out_specs=[
             pl.BlockSpec((BLOCK, width), lambda i: (i, 0)),
             pl.BlockSpec((BLOCK, total), lambda i: (i, 0)),
         ],
         out_shape=[bf16(rows, width), bf16(rows, total)],
-        compiler_params=params(),
+        compiler_params=params(56),
         cost_estimate=pl.CostEstimate(
             flops=6 * rows * width, bytes_accessed=4 * rows * width, transcendentals=rows
         ),
@@ -56,14 +61,53 @@
     )(descriptors, slots)
 
 
-def serve(x, select_ref, core_ref, own_ref, far_ref):
-    total, sent = own_ref.shape[0], far_ref.shape[0]
-    fetched = jnp.dot(
-        select_ref[: 2 * total + sent], x, preferred_element_type=jnp.float32
-    ).astype(jnp.bfloat16)
-    core_ref[...] = fetched[:total]
-    own_ref[...] = fetched[total : 2 * total]
-    far_ref[...] = fetched[2 * total :]
+def list_kernel(rows, *refs):
+    parts, out_ref = refs[:-1], refs[-1]
+    column = lax.axis_index("clus")
+    third = lax.axis_index("rep") % 2 * 2
+    total = out_ref.shape[1]
+    mine = jnp.concatenate([ref[pl.ds(column, 1), :] for ref in parts], axis=1)
+    most = jnp.zeros((1, 1), jnp.float32)
+    lane = lax.broadcasted_iota(jnp.int32, (1, total), 1)
+    earlier = lax.broadcasted_iota(jnp.int32, (total, total), 0) < lax.broadcasted_iota(
+        jnp.int32, (total, total), 1
+    )
+    for server in range(len(parts)):
+        asked = jnp.concatenate([ref[server : server + 1, :] for ref in parts], axis=1)
+        far = (asked >= third * rows) & (asked < (third + 1) * rows)
+        key = jnp.where(far, asked, -1 - lane).astype(jnp.float32)
+        column_key = jnp.broadcast_to(key, (total, total)).T
+        again = jnp.where((column_key == key) & earlier, 1.0, 0.0)
+        again = jnp.max(again, axis=0, keepdims=True)
+        first = jnp.where(far, 1.0 - again, 0.0)
+        most = jnp.maximum(most, jnp.sum(first, axis=1, keepdims=True))
+    place = lax.broadcasted_iota(jnp.int32, out_ref.shape, 0)
+    out_ref[...] = jnp.where(
+        place == 1, jnp.broadcast_to(most.astype(jnp.int32), out_ref.shape), mine
+    )
+
+
+def list_call(parts, rows):
+    total = parts[0].size
+    return pl.pallas_call(
+        functools.partial(list_kernel, rows),
+        out_shape=jax.ShapeDtypeStruct((8, total), jnp.int32),
+        compiler_params=params(),
+        cost_estimate=pl.CostEstimate(
+            flops=6 * total * total, bytes_accessed=8 * total, transcendentals=0
+        ),
+        name="list",
+    )(*parts)
+
+
+def serve(x, select_ref, *out_refs):
+    count = sum(out.shape[0] for out in out_refs)
+    fetched = jnp.dot(select_ref[:count], x, preferred_element_type=jnp.float32)
+    start = 0
+    for out in out_refs:
+        stop = start + out.shape[0]
+        out[...] = fetched[start:stop].astype(jnp.bfloat16)
+        start = stop
 
 
 def one_hot(asked, third, rows):
@@ -76,25 +120,16 @@
     return jnp.concatenate(tiles, axis=1)
 
 
-def index_kernel(groups, x_ref, asked_ref, select_ref, expand_ref, core_ref, own_ref, far_ref):
-    rows = x_ref.shape[0]
-    servers, cap = asked_ref.shape[1:]
-    total = servers * cap
-    group, column = lax.axis_index("rep"), lax.axis_index("clus")
-    odd = group % 2
-    beyond = (group + 2 * odd - 1 + groups) % groups
-
-    def asked(requester):
-        parts = [
-            asked_ref[(column ^ d) * groups + requester, pl.ds(column, 1), :]
-            for d in range(servers)
-        ]
-        return jnp.concatenate(parts, axis=1)
-
-    own = asked(group)
+def index_kernel(x_ref, mine_ref, within_ref, beyond_ref, *out_refs):
+    select_ref, expand_ref, most_ref, core_ref, own_ref, far_ref, rest_ref = out_refs
+    rows, total = x_ref.shape[0], mine_ref.shape[1]
+    odd = lax.axis_index("rep") % 2
+    most = jnp.maximum(mine_ref[...], jnp.maximum(within_ref[...], beyond_ref[...]))
+    most_ref[...] = jnp.broadcast_to(most[1:2, :LANES], most_ref.shape)
+    own = mine_ref[0:1]
     from_own = one_hot(own, 1, rows)
-    from_core = one_hot(asked(group ^ 1), 2 * odd, rows)
-    to_far = one_hot(asked(beyond), 2 - 2 * odd, rows)
+    from_core = one_hot(within_ref[0:1], 2 * odd, rows)
+    to_far = one_hot(beyond_ref[0:1], 2 - 2 * odd, rows)
     from_far = one_hot(own, 2 * odd, rows)
     needed = jnp.concatenate(
         [
@@ -124,27 +159,29 @@
     select_ref[:total] = from_core.astype(jnp.bfloat16)
     select_ref[total : 2 * total] = from_own.astype(jnp.bfloat16)
     select_ref[2 * total :] = pack
-    serve(x_ref[...], select_ref, core_ref, own_ref, far_ref)
-
-
-def index_call(x, asked, groups):
+    serve(x_ref[...], select_ref, core_ref, own_ref, far_ref, rest_ref)
+
+
+def index_call(x, mine, within, beyond, sent):
     rows, width = x.shape
-    total = asked.shape[1] * asked.shape[2]
-    return pl.pallas_call(
-        functools.partial(index_kernel, groups),
+    total = mine.shape[1]
+    return pl.pallas_call(
+        index_kernel,
         out_shape=[
             bf16(3 * total, rows),
             bf16(total, total),
+            jax.ShapeDtypeStruct((8, LANES), jnp.int32),
             bf16(total, width),
             bf16(total, width),
-            bf16(total, width),
+            bf16(sent, width),
+            bf16(total - sent, width),
         ],
         compiler_params=params(),
         cost_estimate=pl.CostEstimate(
             flops=6 * total * rows * width, bytes_accessed=4 * rows * width, transcendentals=0
         ),
         name="index_and_serve",
-    )(x, asked)
+    )(x, mine, within, beyond)
 
 
 def combine_kernel(expand_ref, far_ref, own_ref, core_ref, *out_refs):
@@ -256,27 +293,58 @@
 
 def local(descriptors, request, pick):
     wanted = request[0, 0]
+    rows = descriptors.shape[2]
     servers, cap = wanted.shape
     total = servers * cap
     groups = lax.axis_size("rep")
+    sent = total * FAR_SHARE[0] // FAR_SHARE[1]
     within = [(g, g ^ 1) for g in range(groups)]
     beyond = [(g, (g + 2 * (g % 2) - 1 + groups) % groups) for g in range(groups)]
 
-    asked = lax.all_gather(wanted, ("clus", "rep"), axis=0, tiled=False)
-    x, mask = normalize_call(descriptors[0, 0], pick[0, 0], total, cap)
-    select, expand, core, own, far = index_call(x, asked, groups)
-    for step in range(ROUNDS):
-        far = lax.ppermute(far, "rep", beyond)
-        core = lax.ppermute(core, "rep", within)
+    def turn(value, d):
+        return lax.ppermute(value, "clus", [(c, c ^ d) for c in range(servers)])
+
+    def shift(value, by):
+        return lax.ppermute(value, "rep", [(g, (g + by) % groups) for g in range(groups)])
+
+    def across(value):
+        return lax.ppermute(value, "rep", beyond)
+
+    def exchange(expand, far, own, core):
         parts = combine_call(expand, far, own, core, servers)
-        parts = [parts[0]] + [
-            lax.ppermute(parts[d], "clus", [(c, c ^ d) for c in range(servers)])
-            for d in range(1, servers)
-        ]
-        if step < ROUNDS - 1:
-            x, core, own, far = round_call(x, mask, select, parts, far.shape[0])
-        else:
-            x = last_call(x, mask, parts)
+        return [parts[0]] + [turn(parts[d], d) for d in range(1, servers)]
+
+    def rounds(x, mask, select, expand, far, own, core):
+        for step in range(ROUNDS):
+            if step:
+                far, core = across(far), lax.ppermute(core, "rep", within)
+            parts = exchange(expand, far, own, core)
+            if step < ROUNDS - 1:
+                x, core, own, far = round_call(x, mask, select, parts, far.shape[0])
+        return last_call(x, mask, parts)
+
+    def in_full(x, mask, select, expand, far, rest, own, core):
+        far = jnp.concatenate([far, across(rest)], axis=0)
+        return rounds(x, mask, select, expand, far, own, core)
+
+    def as_sent(x, mask, select, expand, far, rest, own, core):
+        return rounds(x, mask, select, expand, far, own, core)
+
+    asked = [wanted] + [turn(wanted, d) for d in range(1, servers)]
+    x, mask = normalize_call(descriptors[0, 0], pick.transpose(0, 3, 1, 2)[0], total, cap)
+    mine = list_call(asked, rows)
+    select, expand, most, core, own, far, rest = index_call(
+        x, mine, lax.ppermute(mine, "rep", within), across(mine), sent
+    )
+    far, core = across(far), lax.ppermute(core, "rep", within)
+    reach = 1
+    while 2 * reach + 1 < groups:
+        by = 2 * reach + 1
+        most = jnp.maximum(most, jnp.maximum(shift(most, by), shift(most, -by)))
+        reach += by
+    x = lax.cond(
+        most[0, 0] > sent, in_full, as_sent, x, mask, select, expand, far, rest, own, core
+    )
     return x[None, None]
 
 

time: 101 us -> 61.4 us (0.61)
  blocking collectives: 43.7 us -> 0 us
  starting transfers between devices: 9.41 us -> 19.8 us
  waiting for transfers between devices: 34.2 us -> 26 us
  Pallas kernels: 10.5 us -> 12 us
    all_gather x1 -> x0, blocking collectives: 43.7 us -> none  [local(): asked = lax.all_gather(wanted, ('clus', 'rep'), axis=0, tiled=False)]
    ppermute x10 -> x17, starting transfers between devices: 9.41 us -> 19.8 us  [the longest x9 11.6 us: turn(): return lax.ppermute(value, 'clus', [(c, c ^ d) for c in range(servers)])]
    ppermute x10 -> x17, waiting for transfers between devices: 34.2 us -> 26 us  [the longest x9 14.1 us: turn(): return lax.ppermute(value, 'clus', [(c, c ^ d) for c in range(servers)])]
    pallas_call x1, Pallas kernels: 1.59 us -> 2.86 us  [normalize_call(): pl.pallas_call(functools.partial(normalize_kernel, slot_cap), grid=(rows...]
    unnamed x3 -> x4, local copies, waits for them, and re-layouts: 2.45 us -> 2 us
  transfers between devices with their start and end apart: 10 -> 17, of which waited for: 7 -> 13; matrix products, arithmetic and copies ran while one was open for 0% -> 1% of each run, Pallas kernels for 0% -> 5%
where the time goes in v4:
time: 61.4 us; the launch traced here: 61.2 us
  waiting for transfers between devices  26 us (42%)
  starting transfers between devices  19.8 us (32%)
  Pallas kernels  12 us (20%)
  local copies, waits for them, and re-layouts  2.51 us (4%)
  between operations  0.71 us (1%)
    ppermute x9, waiting for transfers between devices, turn(): return lax.ppermute(value, 'clus', [(c, c ^ d) for c in range(servers)])  14.1 us
    ppermute x9, starting transfers between devices, turn(): return lax.ppermute(value, 'clus', [(c, c ^ d) for c in range(servers)])  11.6 us
    ppermute x3, waiting for transfers between devices, across(): return lax.ppermute(value, 'rep', beyond)  10.2 us
    ppermute x3, starting transfers between devices, across(): return lax.ppermute(value, 'rep', beyond)  5.29 us
    pallas_call x1, Pallas kernels, round_call(): pl.pallas_call(functools.partial(round_kernel, servers), out_shape=[bf16(...  3.41 us
    pallas_call x1, Pallas kernels, last_call(): pl.pallas_call(functools.partial(last_kernel, servers), out_specs=pl.Bloc...  3.41 us
    pallas_call x1, Pallas kernels, normalize_call(): pl.pallas_call(functools.partial(normalize_kernel, slot_cap), grid=(rows...  2.86 us
    ppermute x2, starting transfers between devices, shift(): lax.ppermute(value, 'rep', [(g, (g + by) % groups) for g in range(groups)])  2.44 us
  transfers between devices with their start and end apart: 17, of which 13 were waited for; matrix products, arithmetic and copies ran while one was open for 1% of the time, Pallas kernels for 5%

profile of v4, /device:TPU:0, one launch (start us, length us, event | category | flops | bytes accessed | tf_op | source)
XLA Modules:
  0.0 61.2 jit_solution(9000229580707557717)
XLA Ops:
  0.0 3.9 %collective-permute-start.19 = (s32[4,32]{1,0:T(4,128)}, s32[4,32]{1,0:T(4,128)S(1)}, u32[]{:S(2)}, u32[]{:S(2)}) collective-permute-start(s32[4,32]{1,0:T(4,128)} %bitcast.8), channel_id=1, source_target_pairs={{0,24},{8,16},{16,8},{24,0},{1,25},{9,17},{17,9},{25,1},{2,26},{10... | collective-permute-start | bytes 1544 | tf_op jit(solution)/shard_map/ppermute | solution.py:305
  3.9 0.5 collective-permute-start.18
  4.4 0.1 collective-permute-start.17
  4.5 1.2 %collective-permute-done.19.refs_3_ = s32[4,32]{1,0:T(4,128)S(1)} collective-permute-done((s32[4,32]{1,0:T(4,128)}, s32[4,32]{1,0:T(4,128)S(1)}, u32[]{:S(2)}, u32[]{:S(2)}) %collective-permute-start.19) | collective-permute-done | bytes 544 | tf_op jit(solution)/shard_map/ppermute | solution.py:305
  5.7 2.0 %collective-permute-done.18.refs_2_ = s32[4,32]{1,0:T(4,128)S(1)} collective-permute-done((s32[4,32]{1,0:T(4,128)}, s32[4,32]{1,0:T(4,128)S(1)}, u32[]{:S(2)}, u32[]{:S(2)}) %collective-permute-start.18) | collective-permute-done | bytes 544 | tf_op jit(solution)/shard_map/ppermute | solution.py:305
  7.7 0.5 collective-permute-done.17.refs_1_
  8.2 0.0 copy-start
  8.2 0.7 %copy-done = s32[1,1,4,32]{3,2,1,0:T(4,128)S(1)} copy-done((s32[1,1,4,32]{3,2,1,0:T(4,128)S(1)}, s32[1,1,4,32]{3,2,1,0:T(4,128)}, u32[]{:S(2)}) %copy-start) | copy-done | bytes 536
  8.9 0.3 list.1.mine_ref
  9.2 1.3 %collective-permute-start.21 = (s32[8,128]{1,0:T(8,128)S(1)}, s32[8,128]{1,0:T(8,128)S(1)}, u32[]{:S(2)}, u32[]{:S(2)}) collective-permute-start(s32[8,128]{1,0:T(8,128)S(1)} %list.1.mine_ref), channel_id=1, source_target_pairs={{0,7},{1,2},{2,1},{3,4},{4,3},{5,6},{6,5},{7,0},{8,15},{9,10},{10,... | collective-permute-start | bytes 12296 | tf_op jit(solution)/shard_map/ppermute | solution.py:311
  10.5 0.4 collective-permute-start.20
  10.9 2.9 %normalize.1 = (bf16[512,2048]{1,0:T(8,128)(2,1)S(1)}, bf16[512,128]{1,0:T(8,128)(2,1)S(1)}) custom-call(bf16[512,2048]{1,0:T(8,128)(2,1)} %bitcast.14, s32[10,1,512]{2,1,0:T(1,128)} %bitcast.15), custom_call_target="tpu_custom_call" | custom-call | flops 6291456 | bytes 4194304 | tf_op jit(solution)/shard_map/normalize/pallas_call | solution.py:44
  13.8 0.3 collective-permute-done.21.beyond_ref
  14.0 0.0 collective-permute-done.20.within_ref
  14.1 1.4 %index_and_serve.1 = (bf16[384,512]{1,0:T(8,128)(2,1)S(1)}, bf16[128,128]{1,0:T(8,128)(2,1)S(1)}, s32[8,128]{1,0:T(8,128)S(1)}, bf16[128,2048]{1,0:T(8,128)(2,1)...) custom-call(bf16[512,2048]{1,0:T(8,128)(2,1)S(1)} %get-tuple-element.87.x_ref, ...), custom_call_target="tpu_custom_call" | custom-call | flops 805306368 | bytes 4194304 | tf_op jit(solution)/shard_map/index_and_serve/pallas_call | solution.py:168
  15.4 0.1 collective-permute-start.25
  15.5 2.4 %collective-permute-start.23 = (s32[8,128]{1,0:T(8,128)S(1)}, s32[8,128]{1,0:T(8,128)S(1)}, u32[]{:S(2)}, u32[]{:S(2)}) collective-permute-start(s32[8,128]{1,0:T(8,128)S(1)} %get-tuple-element.88), channel_id=1, source_target_pairs={{0,5},{1,6},{2,7},{3,0},{4,1},{5,2},{6,3},{7,4},{8,13},{9,14},{10,... | collective-permute-start | bytes 12296 | tf_op jit(solution)/shard_map/ppermute | solution.py:308
  18.0 0.0 collective-permute-start.22
  18.0 2.3 %collective-permute-start.24 = (bf16[48,2048]{1,0:T(8,128)(2,1)S(1)}, bf16[48,2048]{1,0:T(8,128)(2,1)S(1)}, u32[]{:S(2)}, u32[]{:S(2)}) collective-permute-start(bf16[48,2048]{1,0:T(8,128)(2,1)S(1)} %get-tuple-element.90), channel_id=1, source_target_pairs={{0,7},{1,2},{2,1},{3,4},{4,3},{5,6},{6,5},{7,0},{8,15},{9,10},{10,... | collective-permute-start | bytes 589832 | tf_op jit(solution)/shard_map/ppermute | solution.py:311
  20.3 0.0 collective-permute-done.23
  20.3 1.7 %collective-permute-done.22 = s32[8,128]{1,0:T(8,128)S(1)} collective-permute-done((s32[8,128]{1,0:T(8,128)S(1)}, s32[8,128]{1,0:T(8,128)S(1)}, u32[]{:S(2)}, u32[]{:S(2)}) %collective-permute-start.22) | collective-permute-done | bytes 4128 | tf_op jit(solution)/shard_map/ppermute | solution.py:308
  22.0 0.5 slice.3
  23.2 3.1 %collective-permute-done.24 = bf16[48,2048]{1,0:T(8,128)(2,1)S(1)} collective-permute-done((bf16[48,2048]{1,0:T(8,128)(2,1)S(1)}, bf16[48,2048]{1,0:T(8,128)(2,1)S(1)}, u32[]{:S(2)}, u32[]{:S(2)}) %collective-permute-start.24) | collective-permute-done | bytes 196640 | tf_op jit(solution)/shard_map/ppermute | solution.py:311
  26.2 0.0 collective-permute-done.25
  26.2 33.7 %conditional.1 = (bf16[1,1,512,2048]{3,2,1,0:T(8,128)(2,1)S(1)}) conditional(s32[]{:T(128)} %bitcast.6, (bf16[128,128]{1,0:T(8,128)(2,1)S(1)}, bf16[48,2048]{1,0:T(8,128)(2,1)S(1)}, bf16[128,2048]{1,0:T(8,128)(2,1)S(1)}, bf16[128,2048]{1,0:T(8,128)(2,1)S(1)}, bf16[512,2048]{1,0:T(8,128)(2,1)S(1)}, /*index=5*/bf16[512,128]{1,0:T(8,128)(2,1)S(1)}, ...), branch_computations={%region_0.0_spmd, %region_1.0_spmd} | conditional | flops 2014314496 | bytes 24379760 | solution.py:345
  26.2 0.3 combine.4
  26.5 0.6 collective-permute-start
  27.1 1.5 %collective-permute-start.1 = (bf16[32,2048]{1,0:T(8,128)(2,1)S(1)}, bf16[32,2048]{1,0:T(8,128)(2,1)S(1)}, u32[]{:S(2)}, u32[]{:S(2)}) collective-permute-start(bf16[32,2048]{1,0:T(8,128)(2,1)S(1)} %get-tuple-element.48), channel_id=1, source_target_pairs={{0,16},{8,24},{16,0},{24,8},{1,17},{9,25},{17,1},{25,9},{2,18},{10... | collective-permute-start | bytes 393224 | tf_op jit(solution)/shard_map/cond/branch_0_fun/ppermute | solution.py:305
  28.7 1.4 %collective-permute-start.2 = (bf16[32,2048]{1,0:T(8,128)(2,1)S(1)}, bf16[32,2048]{1,0:T(8,128)(2,1)S(1)}, u32[]{:S(2)}, u32[]{:S(2)}) collective-permute-start(bf16[32,2048]{1,0:T(8,128)(2,1)S(1)} %get-tuple-element.49), channel_id=1, source_target_pairs={{0,24},{8,16},{16,8},{24,0},{1,25},{9,17},{17,9},{25,1},{2,26},{10... | collective-permute-start | bytes 393224 | tf_op jit(solution)/shard_map/cond/branch_0_fun/ppermute | solution.py:305
  30.1 2.9 %collective-permute-done.rest_1_ = bf16[32,2048]{1,0:T(8,128)(2,1)S(1)} collective-permute-done((bf16[32,2048]{1,0:T(8,128)(2,1)S(1)}, bf16[32,2048]{1,0:T(8,128)(2,1)S(1)}, u32[]{:S(2)}, u32[]{:S(2)}) %collective-permute-start) | collective-permute-done | bytes 131104 | tf_op jit(solution)/shard_map/cond/branch_0_fun/ppermute | solution.py:305
  33.0 1.1 %collective-permute-done.1.rest_2_ = bf16[32,2048]{1,0:T(8,128)(2,1)S(1)} collective-permute-done((bf16[32,2048]{1,0:T(8,128)(2,1)S(1)}, bf16[32,2048]{1,0:T(8,128)(2,1)S(1)}, u32[]{:S(2)}, u32[]{:S(2)}) %collective-permute-start.1) | collective-permute-done | bytes 131104 | tf_op jit(solution)/shard_map/cond/branch_0_fun/ppermute | solution.py:305
  34.1 1.6 %collective-permute-done.2.rest_3_ = bf16[32,2048]{1,0:T(8,128)(2,1)S(1)} collective-permute-done((bf16[32,2048]{1,0:T(8,128)(2,1)S(1)}, bf16[32,2048]{1,0:T(8,128)(2,1)S(1)}, u32[]{:S(2)}, u32[]{:S(2)}) %collective-permute-start.2) | collective-permute-done | bytes 131104 | tf_op jit(solution)/shard_map/cond/branch_0_fun/ppermute | solution.py:305
  35.7 3.4 %mix_and_serve.2 = (bf16[512,2048]{1,0:T(8,128)(2,1)S(1)}, bf16[128,2048]{1,0:T(8,128)(2,1)S(1)}, bf16[128,2048]{1,0:T(8,128)(2,1)S(1)}, bf16[48,2048]{1,0:T(8,128)(2,1)S(1)}) custom-call(bf16[512,2048]{1,0:T(8,128)(2,1)S(1)} %get-tuple-element.39.x_ref, bf16[512,128]{1,0:T(8,128)(2,1)S(1)} %get-tuple-element.40.mask_ref, ...), custom_call_target="tpu_custom_call" | custom-call | flops 1342177280 | bytes 6291456 | tf_op jit(solution)/shard_map/cond/branch_0_fun/mix_and_serve/pallas_call | solution.py:279
  39.1 0.1 collective-permute-start.4
  39.2 1.6 %collective-permute-start.3 = (bf16[48,2048]{1,0:T(8,128)(2,1)S(1)}, bf16[48,2048]{1,0:T(8,128)(2,1)S(1)}, u32[]{:S(2)}, u32[]{:S(2)}) collective-permute-start(bf16[48,2048]{1,0:T(8,128)(2,1)S(1)} %get-tuple-element.51), channel_id=1, source_target_pairs={{0,7},{1,2},{2,1},{3,4},{4,3},{5,6},{6,5},{7,0},{8,15},{9,10},{10,... | collective-permute-start | bytes 589832 | tf_op jit(solution)/shard_map/cond/branch_0_fun/ppermute | solution.py:311
  40.8 6.8 %collective-permute-done.3.far_ref = bf16[48,2048]{1,0:T(8,128)(2,1)S(1)} collective-permute-done((bf16[48,2048]{1,0:T(8,128)(2,1)S(1)}, bf16[48,2048]{1,0:T(8,128)(2,1)S(1)}, u32[]{:S(2)}, u32[]{:S(2)}) %collective-permute-start.3) | collective-permute-done | bytes 196640 | tf_op jit(solution)/shard_map/cond/branch_0_fun/ppermute | solution.py:311
  47.7 0.0 collective-permute-done.4.core_ref
  47.7 0.3 combine.5
  48.0 0.9 %collective-permute-start.5 = (bf16[32,2048]{1,0:T(8,128)(2,1)S(1)}, bf16[32,2048]{1,0:T(8,128)(2,1)S(1)}, u32[]{:S(2)}, u32[]{:S(2)}) collective-permute-start(bf16[32,2048]{1,0:T(8,128)(2,1)S(1)} %get-tuple-element.55), channel_id=1, source_target_pairs={{0,8},{8,0},{16,24},{24,16},{1,9},{9,1},{17,25},{25,17},{2,10},{10... | collective-permute-start | bytes 393224 | tf_op jit(solution)/shard_map/cond/branch_0_fun/ppermute | solution.py:305
  48.9 1.5 %collective-permute-start.6 = (bf16[32,2048]{1,0:T(8,128)(2,1)S(1)}, bf16[32,2048]{1,0:T(8,128)(2,1)S(1)}, u32[]{:S(2)}, u32[]{:S(2)}) collective-permute-start(bf16[32,2048]{1,0:T(8,128)(2,1)S(1)} %get-tuple-element.56), channel_id=1, source_target_pairs={{0,16},{8,24},{16,0},{24,8},{1,17},{9,25},{17,1},{25,9},{2,18},{10... | collective-permute-start | bytes 393224 | tf_op jit(solution)/shard_map/cond/branch_0_fun/ppermute | solution.py:305
  50.4 1.1 %collective-permute-start.7 = (bf16[32,2048]{1,0:T(8,128)(2,1)S(1)}, bf16[32,2048]{1,0:T(8,128)(2,1)S(1)}, u32[]{:S(2)}, u32[]{:S(2)}) collective-permute-start(bf16[32,2048]{1,0:T(8,128)(2,1)S(1)} %get-tuple-element.57), channel_id=1, source_target_pairs={{0,24},{8,16},{16,8},{24,0},{1,25},{9,17},{17,9},{25,1},{2,26},{10... | collective-permute-start | bytes 393224 | tf_op jit(solution)/shard_map/cond/branch_0_fun/ppermute | solution.py:305
  51.6 2.0 %collective-permute-done.5.rest_1_ = bf16[32,2048]{1,0:T(8,128)(2,1)S(1)} collective-permute-done((bf16[32,2048]{1,0:T(8,128)(2,1)S(1)}, bf16[32,2048]{1,0:T(8,128)(2,1)S(1)}, u32[]{:S(2)}, u32[]{:S(2)}) %collective-permute-start.5) | collective-permute-done | bytes 131104 | tf_op jit(solution)/shard_map/cond/branch_0_fun/ppermute | solution.py:305
  53.5 1.2 %collective-permute-done.6.rest_2_ = bf16[32,2048]{1,0:T(8,128)(2,1)S(1)} collective-permute-done((bf16[32,2048]{1,0:T(8,128)(2,1)S(1)}, bf16[32,2048]{1,0:T(8,128)(2,1)S(1)}, u32[]{:S(2)}, u32[]{:S(2)}) %collective-permute-start.6) | collective-permute-done | bytes 131104 | tf_op jit(solution)/shard_map/cond/branch_0_fun/ppermute | solution.py:305
  54.8 1.5 %collective-permute-done.7.rest_3_ = bf16[32,2048]{1,0:T(8,128)(2,1)S(1)} collective-permute-done((bf16[32,2048]{1,0:T(8,128)(2,1)S(1)}, bf16[32,2048]{1,0:T(8,128)(2,1)S(1)}, u32[]{:S(2)}, u32[]{:S(2)}) %collective-permute-start.7) | collective-permute-done | bytes 131104 | tf_op jit(solution)/shard_map/cond/branch_0_fun/ppermute | solution.py:305
  56.3 3.4 %mix.2 = bf16[512,2048]{1,0:T(8,128)(2,1)S(1)} custom-call(bf16[512,2048]{1,0:T(8,128)(2,1)S(1)} %get-tuple-element.50.x_ref, bf16[512,128]{1,0:T(8,128)(2,1)S(1)} %get-tuple-element.40.mask_ref, bf16[32,2048]{1,0:T(8,128)(2,1)S(1)} %get-tuple-element.54.rest_0_, bf16[32,2048]{1,0:T(8,128)(2,1)S(1)} %collective-permute-done.5.rest_1_, ...), custom_call_target="tpu_custom_call" | custom-call | flops 536870912 | bytes 4194304 | tf_op jit(solution)/shard_map/cond/branch_0_fun/mix/pallas_call | solution.py:247
  59.9 0.0 copy-start.1
  59.9 1.3 %copy-done.1 = bf16[1,1,512,2048]{3,2,1,0:T(8,128)(2,1)} copy-done((bf16[1,1,512,2048]{3,2,1,0:T(8,128)(2,1)}, bf16[1,1,512,2048]{3,2,1,0:T(8,128)(2,1)S(1)}, u32[]{:S(2)}) %copy-start.1) | copy-done | bytes 2097176
  (1 shorter events, 0.0 us)
Async XLA Ops:
  0.0 5.7 %collective-permute-start.19 = (s32[4,32]{1,0:T(4,128)}, s32[4,32]{1,0:T(4,128)S(1)}, u32[]{:S(2)}, u32[]{:S(2)}) collective-permute-start(s32[4,32]{1,0:T(4,128)} %bitcast.8), channel_id=1, source_target_pairs={{0,24},{8,16},{16,8},{24,0},{1,25},{9,17},{17,9},{25,1},{2,26},{10... | collective-permute-start | bytes 1544 | tf_op jit(solution)/shard_map/ppermute | solution.py:305
  3.9 3.8 %collective-permute-start.18 = (s32[4,32]{1,0:T(4,128)}, s32[4,32]{1,0:T(4,128)S(1)}, u32[]{:S(2)}, u32[]{:S(2)}) collective-permute-start(s32[4,32]{1,0:T(4,128)} %bitcast.9), channel_id=1, source_target_pairs={{0,16},{8,24},{16,0},{24,8},{1,17},{9,25},{17,1},{25,9},{2,18},{10... | collective-permute-start | bytes 1544 | tf_op jit(solution)/shard_map/ppermute | solution.py:305
  4.4 3.8 %collective-permute-start.17 = (s32[4,32]{1,0:T(4,128)}, s32[4,32]{1,0:T(4,128)S(1)}, u32[]{:S(2)}, u32[]{:S(2)}) collective-permute-start(s32[4,32]{1,0:T(4,128)} %bitcast.10), channel_id=1, source_target_pairs={{0,8},{8,0},{16,24},{24,16},{1,9},{9,1},{17,25},{25,17},{2,10},{10... | collective-permute-start | bytes 1544 | tf_op jit(solution)/shard_map/ppermute | solution.py:305
  8.2 0.7 %copy-start = (s32[1,1,4,32]{3,2,1,0:T(4,128)S(1)}, s32[1,1,4,32]{3,2,1,0:T(4,128)}, u32[]{:S(2)}) copy-start(s32[1,1,4,32]{3,2,1,0:T(4,128)} %param.6) | copy-start | bytes 1540
  9.2 4.8 %collective-permute-start.21 = (s32[8,128]{1,0:T(8,128)S(1)}, s32[8,128]{1,0:T(8,128)S(1)}, u32[]{:S(2)}, u32[]{:S(2)}) collective-permute-start(s32[8,128]{1,0:T(8,128)S(1)} %list.1.mine_ref), channel_id=1, source_target_pairs={{0,7},{1,2},{2,1},{3,4},{4,3},{5,6},{6,5},{7,0},{8,15},{9,10},{10,... | collective-permute-start | bytes 12296 | tf_op jit(solution)/shard_map/ppermute | solution.py:311
  10.5 3.5 %collective-permute-start.20 = (s32[8,128]{1,0:T(8,128)S(1)}, s32[8,128]{1,0:T(8,128)S(1)}, u32[]{:S(2)}, u32[]{:S(2)}) collective-permute-start(s32[8,128]{1,0:T(8,128)S(1)} %list.1.mine_ref), channel_id=1, source_target_pairs={{0,1},{1,0},{2,3},{3,2},{4,5},{5,4},{6,7},{7,6},{8,9},{9,8},{10,11... | collective-permute-start | bytes 12296 | tf_op jit(solution)/shard_map/ppermute | solution.py:337
  15.4 10.8 %collective-permute-start.25 = (bf16[128,2048]{1,0:T(8,128)(2,1)S(1)}, bf16[128,2048]{1,0:T(8,128)(2,1)S(1)}, u32[]{:S(2)}, u32[]{:S(2)}) collective-permute-start(bf16[128,2048]{1,0:T(8,128)(2,1)S(1)} %get-tuple-element.92), channel_id=1, source_target_pairs={{0,1},{1,0},{2,3},{3,2},{4,5},{5,4},{6,7},{7,6},{8,9},{9,8},{10,11... | collective-permute-start | bytes 1572872 | tf_op jit(solution)/shard_map/ppermute | solution.py:339
  15.5 4.7 %collective-permute-start.23 = (s32[8,128]{1,0:T(8,128)S(1)}, s32[8,128]{1,0:T(8,128)S(1)}, u32[]{:S(2)}, u32[]{:S(2)}) collective-permute-start(s32[8,128]{1,0:T(8,128)S(1)} %get-tuple-element.88), channel_id=1, source_target_pairs={{0,5},{1,6},{2,7},{3,0},{4,1},{5,2},{6,3},{7,4},{8,13},{9,14},{10,... | collective-permute-start | bytes 12296 | tf_op jit(solution)/shard_map/ppermute | solution.py:308
  18.0 4.0 %collective-permute-start.22 = (s32[8,128]{1,0:T(8,128)S(1)}, s32[8,128]{1,0:T(8,128)S(1)}, u32[]{:S(2)}, u32[]{:S(2)}) collective-permute-start(s32[8,128]{1,0:T(8,128)S(1)} %get-tuple-element.88), channel_id=1, source_target_pairs={{0,3},{1,4},{2,5},{3,6},{4,7},{5,0},{6,1},{7,2},{8,11},{9,12},{10,... | collective-permute-start | bytes 12296 | tf_op jit(solution)/shard_map/ppermute | solution.py:308
  18.0 8.3 %collective-permute-start.24 = (bf16[48,2048]{1,0:T(8,128)(2,1)S(1)}, bf16[48,2048]{1,0:T(8,128)(2,1)S(1)}, u32[]{:S(2)}, u32[]{:S(2)}) collective-permute-start(bf16[48,2048]{1,0:T(8,128)(2,1)S(1)} %get-tuple-element.90), channel_id=1, source_target_pairs={{0,7},{1,2},{2,1},{3,4},{4,3},{5,6},{6,5},{7,0},{8,15},{9,10},{10,... | collective-permute-start | bytes 589832 | tf_op jit(solution)/shard_map/ppermute | solution.py:311
  26.5 6.4 %collective-permute-start = (bf16[32,2048]{1,0:T(8,128)(2,1)S(1)}, bf16[32,2048]{1,0:T(8,128)(2,1)S(1)}, u32[]{:S(2)}, u32[]{:S(2)}) collective-permute-start(bf16[32,2048]{1,0:T(8,128)(2,1)S(1)} %get-tuple-element.47), channel_id=1, source_target_pairs={{0,8},{8,0},{16,24},{24,16},{1,9},{9,1},{17,25},{25,17},{2,10},{10... | collective-permute-start | bytes 393224 | tf_op jit(solution)/shard_map/cond/branch_0_fun/ppermute | solution.py:305
  27.1 6.9 %collective-permute-start.1 = (bf16[32,2048]{1,0:T(8,128)(2,1)S(1)}, bf16[32,2048]{1,0:T(8,128)(2,1)S(1)}, u32[]{:S(2)}, u32[]{:S(2)}) collective-permute-start(bf16[32,2048]{1,0:T(8,128)(2,1)S(1)} %get-tuple-element.48), channel_id=1, source_target_pairs={{0,16},{8,24},{16,0},{24,8},{1,17},{9,25},{17,1},{25,9},{2,18},{10... | collective-permute-start | bytes 393224 | tf_op jit(solution)/shard_map/cond/branch_0_fun/ppermute | solution.py:305
  28.7 7.0 %collective-permute-start.2 = (bf16[32,2048]{1,0:T(8,128)(2,1)S(1)}, bf16[32,2048]{1,0:T(8,128)(2,1)S(1)}, u32[]{:S(2)}, u32[]{:S(2)}) collective-permute-start(bf16[32,2048]{1,0:T(8,128)(2,1)S(1)} %get-tuple-element.49), channel_id=1, source_target_pairs={{0,24},{8,16},{16,8},{24,0},{1,25},{9,17},{17,9},{25,1},{2,26},{10... | collective-permute-start | bytes 393224 | tf_op jit(solution)/shard_map/cond/branch_0_fun/ppermute | solution.py:305
  39.1 8.6 %collective-permute-start.4 = (bf16[128,2048]{1,0:T(8,128)(2,1)S(1)}, bf16[128,2048]{1,0:T(8,128)(2,1)S(1)}, u32[]{:S(2)}, u32[]{:S(2)}) collective-permute-start(bf16[128,2048]{1,0:T(8,128)(2,1)S(1)} %get-tuple-element.53), channel_id=1, source_target_pairs={{0,1},{1,0},{2,3},{3,2},{4,5},{5,4},{6,7},{7,6},{8,9},{9,8},{10,11... | collective-permute-start | bytes 1572872 | tf_op jit(solution)/shard_map/cond/branch_0_fun/ppermute | solution.py:320
  39.2 8.5 %collective-permute-start.3 = (bf16[48,2048]{1,0:T(8,128)(2,1)S(1)}, bf16[48,2048]{1,0:T(8,128)(2,1)S(1)}, u32[]{:S(2)}, u32[]{:S(2)}) collective-permute-start(bf16[48,2048]{1,0:T(8,128)(2,1)S(1)} %get-tuple-element.51), channel_id=1, source_target_pairs={{0,7},{1,2},{2,1},{3,4},{4,3},{5,6},{6,5},{7,0},{8,15},{9,10},{10,... | collective-permute-start | bytes 589832 | tf_op jit(solution)/shard_map/cond/branch_0_fun/ppermute | solution.py:311
  48.0 5.5 %collective-permute-start.5 = (bf16[32,2048]{1,0:T(8,128)(2,1)S(1)}, bf16[32,2048]{1,0:T(8,128)(2,1)S(1)}, u32[]{:S(2)}, u32[]{:S(2)}) collective-permute-start(bf16[32,2048]{1,0:T(8,128)(2,1)S(1)} %get-tuple-element.55), channel_id=1, source_target_pairs={{0,8},{8,0},{16,24},{24,16},{1,9},{9,1},{17,25},{25,17},{2,10},{10... | collective-permute-start | bytes 393224 | tf_op jit(solution)/shard_map/cond/branch_0_fun/ppermute | solution.py:305
  48.9 5.8 %collective-permute-start.6 = (bf16[32,2048]{1,0:T(8,128)(2,1)S(1)}, bf16[32,2048]{1,0:T(8,128)(2,1)S(1)}, u32[]{:S(2)}, u32[]{:S(2)}) collective-permute-start(bf16[32,2048]{1,0:T(8,128)(2,1)S(1)} %get-tuple-element.56), channel_id=1, source_target_pairs={{0,16},{8,24},{16,0},{24,8},{1,17},{9,25},{17,1},{25,9},{2,18},{10... | collective-permute-start | bytes 393224 | tf_op jit(solution)/shard_map/cond/branch_0_fun/ppermute | solution.py:305
  50.4 5.9 %collective-permute-start.7 = (bf16[32,2048]{1,0:T(8,128)(2,1)S(1)}, bf16[32,2048]{1,0:T(8,128)(2,1)S(1)}, u32[]{:S(2)}, u32[]{:S(2)}) collective-permute-start(bf16[32,2048]{1,0:T(8,128)(2,1)S(1)} %get-tuple-element.57), channel_id=1, source_target_pairs={{0,24},{8,16},{16,8},{24,0},{1,25},{9,17},{17,9},{25,1},{2,26},{10... | collective-permute-start | bytes 393224 | tf_op jit(solution)/shard_map/cond/branch_0_fun/ppermute | solution.py:305
  59.9 1.3 %copy-start.1 = (bf16[1,1,512,2048]{3,2,1,0:T(8,128)(2,1)}, bf16[1,1,512,2048]{3,2,1,0:T(8,128)(2,1)S(1)}, u32[]{:S(2)}) copy-start(bf16[1,1,512,2048]{3,2,1,0:T(8,128)(2,1)S(1)} %get-tuple-element.145) | copy-start | bytes 6291460

commit v5 on v4

--- a/solution.py
+++ b/solution.py
@@ -27,8 +27,40 @@
     return value * lax.rsqrt(jnp.mean(value * value, axis=-1, keepdims=True) + 1e-06)
 
 
-def normalize_kernel(slot_cap, x_ref, pick_ref, out_ref, mask_ref):
-    out_ref[...] = normalize(x_ref[...].astype(jnp.float32)).astype(jnp.bfloat16)
+def normalize_kernel(x_hbm, wanted_hbm, out_ref, wanted_ref, raw, sems):
+    copies = [pltpu.make_async_copy(wanted_hbm, wanted_ref, sems.at[0])]
+    starts = range(0, raw.shape[0], BLOCK)
+    for i, start in enumerate(starts):
+        here = pl.ds(start, BLOCK)
+        copies.append(pltpu.make_async_copy(x_hbm.at[here], raw.at[here], sems.at[i + 1]))
+    for copy in copies:
+        copy.start()
+    for copy, start in zip(copies[1:], starts):
+        copy.wait()
+        here = pl.ds(start, BLOCK)
+        out_ref[here] = normalize(raw[here].astype(jnp.float32)).astype(jnp.bfloat16)
+    copies[0].wait()
+
+
+def normalize_call(descriptors, wanted):
+    rows, width = descriptors.shape
+    return pl.pallas_call(
+        normalize_kernel,
+        in_specs=[pl.BlockSpec(memory_space=pl.ANY)] * 2,
+        out_shape=[bf16(rows, width), jax.ShapeDtypeStruct(wanted.shape, jnp.int32)],
+        scratch_shapes=[
+            pltpu.VMEM((rows, width), jnp.bfloat16),
+            pltpu.SemaphoreType.DMA((rows // BLOCK + 1,)),
+        ],
+        compiler_params=params(56),
+        cost_estimate=pl.CostEstimate(
+            flops=6 * rows * width, bytes_accessed=4 * rows * width, transcendentals=rows
+        ),
+        name="normalize",
+    )(descriptors, wanted)
+
+
+def mask_kernel(slot_cap, pick_ref, mask_ref):
     shape = mask_ref.shape[1], mask_ref.shape[0]
     slot = lax.broadcasted_iota(jnp.int32, shape, 0)
     slot = slot ^ (lax.axis_index("clus") * slot_cap)
@@ -38,27 +70,17 @@
     mask_ref[...] = chosen.T.astype(jnp.bfloat16)
 
 
-def normalize_call(descriptors, slots, total, slot_cap):
-    rows, width = descriptors.shape
-    count = slots.shape[0]
-    return pl.pallas_call(
-        functools.partial(normalize_kernel, slot_cap),
-        grid=(rows // BLOCK,),
-        in_specs=[
-            pl.BlockSpec((BLOCK, width), lambda i: (i, 0)),
-            pl.BlockSpec((count, 1, BLOCK), lambda i: (0, 0, i)),
-        ],
-        out_specs=[
-            pl.BlockSpec((BLOCK, width), lambda i: (i, 0)),
-            pl.BlockSpec((BLOCK, total), lambda i: (i, 0)),
-        ],
-        out_shape=[bf16(rows, width), bf16(rows, total)],
-        compiler_params=params(56),
-        cost_estimate=pl.CostEstimate(
-            flops=6 * rows * width, bytes_accessed=4 * rows * width, transcendentals=rows
-        ),
-        name="normalize",
-    )(descriptors, slots)
+def mask_call(slots, total, slot_cap):
+    count, _, rows = slots.shape
+    return pl.pallas_call(
+        functools.partial(mask_kernel, slot_cap),
+        out_shape=bf16(rows, total),
+        compiler_params=params(),
+        cost_estimate=pl.CostEstimate(
+            flops=2 * count * rows * total, bytes_accessed=2 * rows * total, transcendentals=0
+        ),
+        name="mask",
+    )(slots)
 
 
 def list_kernel(rows, *refs):
@@ -120,24 +142,9 @@
     return jnp.concatenate(tiles, axis=1)
 
 
-def index_kernel(x_ref, mine_ref, within_ref, beyond_ref, *out_refs):
-    select_ref, expand_ref, most_ref, core_ref, own_ref, far_ref, rest_ref = out_refs
-    rows, total = x_ref.shape[0], mine_ref.shape[1]
-    odd = lax.axis_index("rep") % 2
-    most = jnp.maximum(mine_ref[...], jnp.maximum(within_ref[...], beyond_ref[...]))
-    most_ref[...] = jnp.broadcast_to(most[1:2, :LANES], most_ref.shape)
-    own = mine_ref[0:1]
-    from_own = one_hot(own, 1, rows)
-    from_core = one_hot(within_ref[0:1], 2 * odd, rows)
-    to_far = one_hot(beyond_ref[0:1], 2 - 2 * odd, rows)
-    from_far = one_hot(own, 2 * odd, rows)
-    needed = jnp.concatenate(
-        [
-            jnp.broadcast_to(jnp.max(to_far, axis=0, keepdims=True), (8, rows)),
-            jnp.broadcast_to(jnp.max(from_far, axis=0, keepdims=True), (8, rows)),
-        ],
-        axis=0,
-    )
+def packing(selected, rows):
+    total = selected.shape[0]
+    needed = jnp.broadcast_to(jnp.max(selected, axis=0, keepdims=True), (8, rows))
     before = lax.broadcasted_iota(jnp.int32, (rows, rows), 0) < lax.broadcasted_iota(
         jnp.int32, (rows, rows), 1
     )
@@ -148,40 +155,89 @@
     )
     rank = jnp.where(needed > 0, rank, -1.0).astype(jnp.int32)
     place = lax.broadcasted_iota(jnp.int32, (total, rows), 0)
-    pack = jnp.where(place == rank[0:1], 1.0, 0.0).astype(jnp.bfloat16)
-    packed = jnp.where(place == rank[8:9], 1.0, 0.0).astype(jnp.bfloat16)
+    return jnp.where(place == rank[0:1], 1.0, 0.0).astype(jnp.bfloat16)
+
+
+def far_kernel(x_ref, beyond_ref, pack_ref, far_ref):
+    rows = x_ref.shape[0]
+    third = 2 - lax.axis_index("rep") % 2 * 2
+    pack_ref[...] = packing(one_hot(beyond_ref[0:1], third, rows), rows)
+    serve(x_ref[...], pack_ref, far_ref)
+
+
+def far_call(x, beyond, sent):
+    rows, width = x.shape
+    total = beyond.shape[1]
+    return pl.pallas_call(
+        far_kernel,
+        out_shape=[bf16(total, rows), bf16(sent, width)],
+        compiler_params=params(),
+        cost_estimate=pl.CostEstimate(
+            flops=2 * rows * rows * LANES, bytes_accessed=2 * rows * width, transcendentals=0
+        ),
+        name="pack_far",
+    )(x, beyond)
+
+
+def near_kernel(x_ref, pack_ref, mine_ref, within_ref, beyond_ref, *out_refs):
+    select_ref, expand_ref, most_ref, core_ref, own_ref, rest_ref = out_refs
+    rows, total = x_ref.shape[0], mine_ref.shape[1]
+    third = lax.axis_index("rep") % 2 * 2
+    most = jnp.maximum(mine_ref[...], jnp.maximum(within_ref[...], beyond_ref[...]))
+    most_ref[...] = jnp.broadcast_to(most[1:2, :LANES], most_ref.shape)
+    own = mine_ref[0:1]
+    select_ref[:total] = one_hot(within_ref[0:1], third, rows).astype(jnp.bfloat16)
+    select_ref[total:] = one_hot(own, 1, rows).astype(jnp.bfloat16)
+    x = x_ref[...]
+    serve(x, select_ref, core_ref, own_ref)
+    rest = total - rest_ref.shape[0]
+    serve(x, pack_ref.at[rest:], rest_ref)
+    from_far = one_hot(own, third, rows)
     expand_ref[...] = lax.dot_general(
         from_far.astype(jnp.bfloat16),
-        packed,
+        packing(from_far, rows),
         (((1,), (1,)), ((), ())),
         preferred_element_type=jnp.float32,
     ).astype(jnp.bfloat16)
-    select_ref[:total] = from_core.astype(jnp.bfloat16)
-    select_ref[total : 2 * total] = from_own.astype(jnp.bfloat16)
-    select_ref[2 * total :] = pack
-    serve(x_ref[...], select_ref, core_ref, own_ref, far_ref, rest_ref)
-
-
-def index_call(x, mine, within, beyond, sent):
+
+
+def near_call(x, pack, mine, within, beyond, sent):
     rows, width = x.shape
     total = mine.shape[1]
     return pl.pallas_call(
-        index_kernel,
+        near_kernel,
         out_shape=[
-            bf16(3 * total, rows),
+            bf16(2 * total, rows),
             bf16(total, total),
             jax.ShapeDtypeStruct((8, LANES), jnp.int32),
             bf16(total, width),
             bf16(total, width),
-            bf16(sent, width),
             bf16(total - sent, width),
         ],
         compiler_params=params(),
         cost_estimate=pl.CostEstimate(
             flops=6 * total * rows * width, bytes_accessed=4 * rows * width, transcendentals=0
         ),
-        name="index_and_serve",
-    )(x, mine, within, beyond)
+        name="serve_near",
+    )(x, pack, mine, within, beyond)
+
+
+def again_kernel(x_ref, select_ref, core_ref, own_ref):
+    serve(x_ref[...], select_ref, core_ref, own_ref)
+
+
+def again_call(x, select):
+    rows, width = x.shape
+    total = select.shape[0] // 2
+    return pl.pallas_call(
+        again_kernel,
+        out_shape=[bf16(total, width)] * 2,
+        compiler_params=params(),
+        cost_estimate=pl.CostEstimate(
+            flops=4 * total * rows * width, bytes_accessed=4 * rows * width, transcendentals=0
+        ),
+        name="serve_again",
+    )(x, select)
 
 
 def combine_kernel(expand_ref, far_ref, own_ref, core_ref, *out_refs):
@@ -262,33 +318,33 @@
     )(x, mask, *parts)
 
 
-def round_kernel(servers, x_ref, mask_ref, select_ref, *rest):
+def round_kernel(servers, x_ref, mask_ref, pack_ref, *rest):
     parts, rest = rest[:servers], rest[servers:]
-    out_ref, core_ref, own_ref, far_ref, buffer, weights = rest
+    out_ref, far_ref, buffer, weights = rest
     fill(buffer, parts)
     weights[...] = weigh(x_ref[...], buffer[...], mask_ref[...])
     for start in range(0, x_ref.shape[0], BLOCK):
         stop = start + BLOCK
         out_ref[start:stop] = add_up(x_ref[start:stop], weights[start:stop], buffer[...])
-    serve(out_ref[...], select_ref, core_ref, own_ref, far_ref)
-
-
-def round_call(x, mask, select, parts, sent):
+    serve(out_ref[...], pack_ref, far_ref)
+
+
+def round_call(x, mask, pack, parts, sent):
     rows, width = x.shape
     total, servers = mask.shape[1], len(parts)
     return pl.pallas_call(
         functools.partial(round_kernel, servers),
-        out_shape=[bf16(rows, width), bf16(total, width), bf16(total, width), bf16(sent, width)],
+        out_shape=[bf16(rows, width), bf16(sent, width)],
         scratch_shapes=[
             pltpu.VMEM((total, width), jnp.bfloat16),
             pltpu.VMEM((rows, total), jnp.bfloat16),
         ],
         compiler_params=params(),
         cost_estimate=pl.CostEstimate(
-            flops=10 * total * rows * width, bytes_accessed=6 * rows * width, transcendentals=rows
-        ),
-        name="mix_and_serve",
-    )(x, mask, select, *parts)
+            flops=5 * total * rows * width, bytes_accessed=6 * rows * width, transcendentals=rows
+        ),
+        name="mix_and_pack",
+    )(x, mask, pack, *parts)
 
 
 def local(descriptors, request, pick):
@@ -310,42 +366,50 @@
     def across(value):
         return lax.ppermute(value, "rep", beyond)
 
+    def inside(value):
+        return lax.ppermute(value, "rep", within)
+
     def exchange(expand, far, own, core):
         parts = combine_call(expand, far, own, core, servers)
-        return [parts[0]] + [turn(parts[d], d) for d in range(1, servers)]
-
-    def rounds(x, mask, select, expand, far, own, core):
-        for step in range(ROUNDS):
-            if step:
-                far, core = across(far), lax.ppermute(core, "rep", within)
-            parts = exchange(expand, far, own, core)
-            if step < ROUNDS - 1:
-                x, core, own, far = round_call(x, mask, select, parts, far.shape[0])
-        return last_call(x, mask, parts)
-
-    def in_full(x, mask, select, expand, far, rest, own, core):
+        got = {d: turn(parts[d], d) for d in reversed(range(1, servers))}
+        return [parts[0]] + [got[d] for d in range(1, servers)]
+
+    def rounds(x, mask, pack, select, expand, far, own, core):
+        parts = exchange(expand, far, own, core)
+        for _ in range(ROUNDS - 1):
+            x, far = round_call(x, mask, pack, parts, far.shape[0])
+            far = across(far)
+            core, own = again_call(x, select)
+            parts = exchange(expand, far, own, inside(core))
+        return x, *parts
+
+    def in_full(x, mask, pack, select, expand, far, rest, own, core):
         far = jnp.concatenate([far, across(rest)], axis=0)
-        return rounds(x, mask, select, expand, far, own, core)
-
-    def as_sent(x, mask, select, expand, far, rest, own, core):
-        return rounds(x, mask, select, expand, far, own, core)
-
-    asked = [wanted] + [turn(wanted, d) for d in range(1, servers)]
-    x, mask = normalize_call(descriptors[0, 0], pick.transpose(0, 3, 1, 2)[0], total, cap)
-    mine = list_call(asked, rows)
-    select, expand, most, core, own, far, rest = index_call(
-        x, mine, lax.ppermute(mine, "rep", within), across(mine), sent
-    )
-    far, core = across(far), lax.ppermute(core, "rep", within)
+        return rounds(x, mask, pack, select, expand, far, own, core)
+
+    def as_sent(x, mask, pack, select, expand, far, rest, own, core):
+        return rounds(x, mask, pack, select, expand, far, own, core)
+
+    asked = {d: turn(wanted, d) for d in reversed(range(1, servers))}
+    x, held = normalize_call(descriptors[0, 0], wanted)
+    mine = list_call([held] + [asked[d] for d in range(1, servers)], rows)
+    beyond_list, within_list = across(mine), inside(mine)
+    pack, far = far_call(x, beyond_list, sent)
+    far = across(far)
+    select, expand, most, core, own, rest = near_call(
+        x, pack, mine, within_list, beyond_list, sent
+    )
+    core = inside(core)
+    mask = mask_call(pick.transpose(0, 3, 1, 2)[0], total, cap)
     reach = 1
     while 2 * reach + 1 < groups:
         by = 2 * reach + 1
         most = jnp.maximum(most, jnp.maximum(shift(most, by), shift(most, -by)))
         reach += by
-    x = lax.cond(
-        most[0, 0] > sent, in_full, as_sent, x, mask, select, expand, far, rest, own, core
-    )
-    return x[None, None]
+    x, *parts = lax.cond(
+        most[0, 0] > sent, in_full, as_sent, x, mask, pack, select, expand, far, rest, own, core
+    )
+    return last_call(x, mask, parts)[None, None]
 
 
 def solution(mesh):

time: 61.4 us -> 65.4 us (1.065)
  Pallas kernels: 12 us -> 17.2 us
  local copies, waits for them, and re-layouts: 2.51 us -> 1.2 us
    ppermute x3, waiting for transfers between devices: 10.2 us -> 13.7 us  [across(): return lax.ppermute(value, 'rep', beyond)]
    pallas_call x2 -> x5, Pallas kernels: 4.24 us -> 7.19 us  [the longest x1 2.47 us: normalize_call(): pl.pallas_call(normalize_kernel, in_specs=[pl.BlockSpec(memory_space=pl.A...]
    ppermute x9, waiting for transfers between devices: 14.1 us -> 12.3 us  [turn(): return lax.ppermute(value, 'clus', [(c, c ^ d) for c in range(servers)])]
    ppermute x2, waiting for transfers between devices: 1.73 us -> 0.01 us  [shift(): lax.ppermute(value, 'rep', [(g, (g + by) % groups) for g in range(groups)])]
    pallas_call x1, Pallas kernels: 3.41 us -> 5 us  [last_call(): pl.pallas_call(functools.partial(last_kernel, servers), out_specs=pl.Bloc...]
    unnamed x4, local copies, waits for them, and re-layouts: 2 us -> 0.69 us
    ppermute x3, starting transfers between devices: 5.29 us -> 6.3 us  [across(): return lax.ppermute(value, 'rep', beyond)]
  transfers between devices with their start and end apart: 17 -> 17, of which waited for: 13 -> 10; matrix products, arithmetic and copies ran while one was open for 1% -> 1% of each run, Pallas kernels for 5% -> 5%
where the time goes in v5:
time: 65.4 us; the launch traced here: 65.2 us
  waiting for transfers between devices  26 us (40%)
  starting transfers between devices  20 us (31%)
  Pallas kernels  17.2 us (26%)
  local copies, waits for them, and re-layouts  1.2 us (2%)
  between operations  0.7 us (1%)
    ppermute x3, waiting for transfers between devices, across(): return lax.ppermute(value, 'rep', beyond)  13.7 us
    ppermute x9, waiting for transfers between devices, turn(): return lax.ppermute(value, 'clus', [(c, c ^ d) for c in range(servers)])  12.3 us
    ppermute x9, starting transfers between devices, turn(): return lax.ppermute(value, 'clus', [(c, c ^ d) for c in range(servers)])  11.6 us
    ppermute x3, starting transfers between devices, across(): return lax.ppermute(value, 'rep', beyond)  6.3 us
    pallas_call x1, Pallas kernels, last_call(): pl.pallas_call(functools.partial(last_kernel, servers), out_specs=pl.Bloc...  5 us
    pallas_call x1, Pallas kernels, round_call(): pl.pallas_call(functools.partial(round_kernel, servers), out_shape=[bf16(...  4.03 us
    pallas_call x1, Pallas kernels, normalize_call(): pl.pallas_call(normalize_kernel, in_specs=[pl.BlockSpec(memory_space=pl.A...  2.47 us
    pallas_call x1, Pallas kernels, again_call(): pl.pallas_call(again_kernel, out_shape=[bf16(total, width)] * 2, compiler...  2.3 us
  transfers between devices with their start and end apart: 17, of which 10 were waited for; matrix products, arithmetic and copies ran while one was open for 1% of the time, Pallas kernels for 5%

profile of v5, /device:TPU:0, one launch (start us, length us, event | category | flops | bytes accessed | tf_op | source)
XLA Modules:
  0.0 65.2 jit_solution(16477980686934292482)
XLA Ops:
  0.0 3.9 %collective-permute-start.19 = (s32[4,32]{1,0:T(4,128)}, s32[4,32]{1,0:T(4,128)S(1)}, u32[]{:S(2)}, u32[]{:S(2)}) collective-permute-start(s32[4,32]{1,0:T(4,128)} %bitcast.9), channel_id=1, source_target_pairs={{0,24},{8,16},{16,8},{24,0},{1,25},{9,17},{17,9},{25,1},{2,26},{10... | collective-permute-start | bytes 1544 | tf_op jit(solution)/shard_map/ppermute | solution.py:361
  3.9 0.5 collective-permute-start.18
  4.4 0.1 collective-permute-start.17
  4.5 2.5 %normalize.1 = (bf16[512,2048]{1,0:T(8,128)(2,1)S(1)}, s32[4,32]{1,0:T(4,128)}) custom-call(bf16[512,2048]{1,0:T(8,128)(2,1)} %bitcast.8, s32[4,32]{1,0:T(4,128)} %bitcast.12), custom_call_target="tpu_custom_call" | custom-call | flops 6291456 | bytes 4194304 | tf_op jit(solution)/shard_map/normalize/pallas_call | solution.py:47
  6.9 0.0 collective-permute-done.19.refs_3_
  6.9 0.7 %collective-permute-done.18.refs_2_ = s32[4,32]{1,0:T(4,128)S(1)} collective-permute-done((s32[4,32]{1,0:T(4,128)}, s32[4,32]{1,0:T(4,128)S(1)}, u32[]{:S(2)}, u32[]{:S(2)}) %collective-permute-start.18) | collective-permute-done | bytes 544 | tf_op jit(solution)/shard_map/ppermute | solution.py:361
  7.7 0.5 collective-permute-done.17.refs_1_
  8.2 0.7 %copy-done.1 = s32[4,32]{1,0:T(4,128)S(1)} copy-done((s32[4,32]{1,0:T(4,128)S(1)}, s32[4,32]{1,0:T(4,128)}, u32[]{:S(2)}) %copy-start.1) | copy-done | bytes 536
  8.9 0.3 list.1.mine_ref
  9.2 1.5 %collective-permute-start.20 = (s32[8,128]{1,0:T(8,128)S(1)}, s32[8,128]{1,0:T(8,128)S(1)}, u32[]{:S(2)}, u32[]{:S(2)}) collective-permute-start(s32[8,128]{1,0:T(8,128)S(1)} %list.1.mine_ref), channel_id=1, source_target_pairs={{0,7},{1,2},{2,1},{3,4},{4,3},{5,6},{6,5},{7,0},{8,15},{9,10},{10,... | collective-permute-start | bytes 12296 | tf_op jit(solution)/shard_map/ppermute | solution.py:367
  10.7 0.2 collective-permute-start.21
  10.9 3.1 %collective-permute-done.20.beyond_ref = s32[8,128]{1,0:T(8,128)S(1)} collective-permute-done((s32[8,128]{1,0:T(8,128)S(1)}, s32[8,128]{1,0:T(8,128)S(1)}, u32[]{:S(2)}, u32[]{:S(2)}) %collective-permute-start.20) | collective-permute-done | bytes 4128 | tf_op jit(solution)/shard_map/ppermute | solution.py:367
  14.0 0.7 %pack_far.1 = (bf16[128,512]{1,0:T(8,128)(2,1)S(1)}, bf16[48,2048]{1,0:T(8,128)(2,1)S(1)}) custom-call(bf16[512,2048]{1,0:T(8,128)(2,1)S(1)} %get-tuple-element.95.x_ref, s32[8,128]{1,0:T(8,128)S(1)} %collective-permute-done.20.beyond_ref), custom_call_target="tpu_custom_call" | custom-call | flops 67108864 | bytes 2097152 | tf_op jit(solution)/shard_map/pack_far/pallas_call | solution.py:171
  14.8 0.0 collective-permute-done.21.within_ref
  14.8 1.4 %serve_near.1 = (bf16[256,512]{1,0:T(8,128)(2,1)S(1)}, bf16[128,128]{1,0:T(8,128)(2,1)S(1)}, s32[8,128]{1,0:T(8,128)S(1)}, bf16[128,2048]{1,0:T(8,128)(2,1)S(1)}...) custom-call(bf16[512,2048]{1,0:T(8,128)(2,1)S(1)} %get-tuple-element.95.x_ref, ...), custom_call_target="tpu_custom_call" | custom-call | flops 805306368 | bytes 4194304 | tf_op jit(solution)/shard_map/serve_near/pallas_call | solution.py:207
  16.2 0.1 collective-permute-start.25
  16.3 0.9 %collective-permute-start.23 = (s32[8,128]{1,0:T(8,128)S(1)}, s32[8,128]{1,0:T(8,128)S(1)}, u32[]{:S(2)}, u32[]{:S(2)}) collective-permute-start(s32[8,128]{1,0:T(8,128)S(1)} %get-tuple-element.98), channel_id=1, source_target_pairs={{0,5},{1,6},{2,7},{3,0},{4,1},{5,2},{6,3},{7,4},{8,13},{9,14},{10,... | collective-permute-start | bytes 12296 | tf_op jit(solution)/shard_map/ppermute | solution.py:364
  17.2 0.9 %collective-permute-start.22 = (s32[8,128]{1,0:T(8,128)S(1)}, s32[8,128]{1,0:T(8,128)S(1)}, u32[]{:S(2)}, u32[]{:S(2)}) collective-permute-start(s32[8,128]{1,0:T(8,128)S(1)} %get-tuple-element.98), channel_id=1, source_target_pairs={{0,3},{1,4},{2,5},{3,6},{4,7},{5,0},{6,1},{7,2},{8,11},{9,12},{10,... | collective-permute-start | bytes 12296 | tf_op jit(solution)/shard_map/ppermute | solution.py:364
  18.1 0.0 copy-done
  18.1 0.3 mask.1.mask_ref
  18.4 2.8 %collective-permute-start.24 = (bf16[48,2048]{1,0:T(8,128)(2,1)S(1)}, bf16[48,2048]{1,0:T(8,128)(2,1)S(1)}, u32[]{:S(2)}, u32[]{:S(2)}) collective-permute-start(bf16[48,2048]{1,0:T(8,128)(2,1)S(1)} %get-tuple-element.100), channel_id=1, source_target_pairs={{0,7},{1,2},{2,1},{3,4},{4,3},{5,6},{6,5},{7,0},{8,15},{9,10},{10,... | collective-permute-start | bytes 589832 | tf_op jit(solution)/shard_map/ppermute | solution.py:367
  21.2 0.0 collective-permute-done.23
  21.2 0.0 collective-permute-done.22
  21.2 0.5 slice.3
  22.4 4.8 %collective-permute-done.24 = bf16[48,2048]{1,0:T(8,128)(2,1)S(1)} collective-permute-done((bf16[48,2048]{1,0:T(8,128)(2,1)S(1)}, bf16[48,2048]{1,0:T(8,128)(2,1)S(1)}, u32[]{:S(2)}, u32[]{:S(2)}) %collective-permute-start.24) | collective-permute-done | bytes 196640 | tf_op jit(solution)/shard_map/ppermute | solution.py:367
  27.2 0.0 collective-permute-done.25
  27.2 33.0 %conditional.1 = (bf16[512,2048]{1,0:T(8,128)(2,1)}, bf16[32,2048]{1,0:T(8,128)(2,1)S(1)}, bf16[32,2048]{1,0:T(8,128)(2,1)}, bf16[32,2048]{1,0:T(8,128)(2,1)}, bf16[32,2048]{1,0:T(8,128)(2,1)}) conditional(s32[]{:T(128)} %bitcast.2, (bf16[128,128]{1,0:T(8,128)(2,1)S(1)}, bf16[48,2048]{1,0:T(8,128)(2,1)S(1)}, bf16[128,2048]{1,0:T(8,128)(2,1)S(1)}, ...), branch_computations={%region_0.0_spmd, %region_1.0_spmd} | conditional | flops 1343225856 | bytes 24379792 | solution.py:409
  27.2 0.3 combine.4
  27.5 0.2 collective-permute-start
  27.7 1.5 %collective-permute-start.1 = (bf16[32,2048]{1,0:T(8,128)(2,1)S(1)}, bf16[32,2048]{1,0:T(8,128)(2,1)S(1)}, u32[]{:S(2)}, u32[]{:S(2)}) collective-permute-start(bf16[32,2048]{1,0:T(8,128)(2,1)S(1)} %get-tuple-element.48), channel_id=1, source_target_pairs={{0,16},{8,24},{16,0},{24,8},{1,17},{9,25},{17,1},{25,9},{2,18},{10... | collective-permute-start | bytes 393224 | tf_op jit(solution)/shard_map/cond/branch_0_fun/ppermute | solution.py:361
  29.2 1.8 %collective-permute-start.2 = (bf16[32,2048]{1,0:T(8,128)(2,1)S(1)}, bf16[32,2048]{1,0:T(8,128)(2,1)S(1)}, u32[]{:S(2)}, u32[]{:S(2)}) collective-permute-start(bf16[32,2048]{1,0:T(8,128)(2,1)S(1)} %get-tuple-element.49), channel_id=1, source_target_pairs={{0,24},{8,16},{16,8},{24,0},{1,25},{9,17},{17,9},{25,1},{2,26},{10... | collective-permute-start | bytes 393224 | tf_op jit(solution)/shard_map/cond/branch_0_fun/ppermute | solution.py:361
  31.0 2.9 %collective-permute-done.rest_1_ = bf16[32,2048]{1,0:T(8,128)(2,1)S(1)} collective-permute-done((bf16[32,2048]{1,0:T(8,128)(2,1)S(1)}, bf16[32,2048]{1,0:T(8,128)(2,1)S(1)}, u32[]{:S(2)}, u32[]{:S(2)}) %collective-permute-start) | collective-permute-done | bytes 131104 | tf_op jit(solution)/shard_map/cond/branch_0_fun/ppermute | solution.py:361
  33.9 1.3 %collective-permute-done.1.rest_2_ = bf16[32,2048]{1,0:T(8,128)(2,1)S(1)} collective-permute-done((bf16[32,2048]{1,0:T(8,128)(2,1)S(1)}, bf16[32,2048]{1,0:T(8,128)(2,1)S(1)}, u32[]{:S(2)}, u32[]{:S(2)}) %collective-permute-start.1) | collective-permute-done | bytes 131104 | tf_op jit(solution)/shard_map/cond/branch_0_fun/ppermute | solution.py:361
  35.1 1.7 %collective-permute-done.2.rest_3_ = bf16[32,2048]{1,0:T(8,128)(2,1)S(1)} collective-permute-done((bf16[32,2048]{1,0:T(8,128)(2,1)S(1)}, bf16[32,2048]{1,0:T(8,128)(2,1)S(1)}, u32[]{:S(2)}, u32[]{:S(2)}) %collective-permute-start.2) | collective-permute-done | bytes 131104 | tf_op jit(solution)/shard_map/cond/branch_0_fun/ppermute | solution.py:361
  36.8 4.0 %mix_and_pack.2 = (bf16[512,2048]{1,0:T(8,128)(2,1)}, bf16[48,2048]{1,0:T(8,128)(2,1)S(1)}) custom-call(bf16[512,2048]{1,0:T(8,128)(2,1)S(1)} %get-tuple-element.39.x_ref, bf16[512,128]{1,0:T(8,128)(2,1)S(1)} %get-tuple-element.40.mask_ref, bf16[128,512]{1,0:T(8,128)(2,1)S(1)} %get-tuple-element.41.pack_ref, bf16[32,2048]{1,0:T(8,128)(2,1)S(1)} %get-tuple-element.46.rest_0_, ...), custom_call_target="tpu_custom_call" | custom-call | flops 671088640 | bytes 6291456 | tf_op jit(solution)/shard_map/cond/branch_0_fun/mix_and_pack/pallas_call | solution.py:335
  40.9 2.3 %serve_again.2 = (bf16[128,2048]{1,0:T(8,128)(2,1)S(1)}, bf16[128,2048]{1,0:T(8,128)(2,1)S(1)}) custom-call(bf16[512,2048]{1,0:T(8,128)(2,1)} %get-tuple-element.110.x_ref, bf16[256,512]{1,0:T(8,128)(2,1)S(1)} %get-tuple-element.52.select_ref), custom_call_target="tpu_custom_call" | custom-call | flops 536870912 | bytes 4194304 | tf_op jit(solution)/shard_map/cond/branch_0_fun/serve_again/pallas_call | solution.py:232
  43.2 0.1 collective-permute-start.4
  43.2 2.0 %collective-permute-start.3 = (bf16[48,2048]{1,0:T(8,128)(2,1)S(1)}, bf16[48,2048]{1,0:T(8,128)(2,1)S(1)}, u32[]{:S(2)}, u32[]{:S(2)}) collective-permute-start(bf16[48,2048]{1,0:T(8,128)(2,1)S(1)} %get-tuple-element.51), channel_id=1, source_target_pairs={{0,7},{1,2},{2,1},{3,4},{4,3},{5,6},{6,5},{7,0},{8,15},{9,10},{10,... | collective-permute-start | bytes 589832 | tf_op jit(solution)/shard_map/cond/branch_0_fun/ppermute | solution.py:367
  45.3 5.8 %collective-permute-done.3.far_ref = bf16[48,2048]{1,0:T(8,128)(2,1)S(1)} collective-permute-done((bf16[48,2048]{1,0:T(8,128)(2,1)S(1)}, bf16[48,2048]{1,0:T(8,128)(2,1)S(1)}, u32[]{:S(2)}, u32[]{:S(2)}) %collective-permute-start.3) | collective-permute-done | bytes 196640 | tf_op jit(solution)/shard_map/cond/branch_0_fun/ppermute | solution.py:367
  51.1 0.0 collective-permute-done.4.core_ref
  51.1 0.3 combine.5
  51.4 0.9 %collective-permute-start.5 = (bf16[32,2048]{1,0:T(8,128)(2,1)S(1)}, bf16[32,2048]{1,0:T(8,128)(2,1)}, u32[]{:S(2)}, u32[]{:S(2)}) collective-permute-start(bf16[32,2048]{1,0:T(8,128)(2,1)S(1)} %get-tuple-element.56), channel_id=1, source_target_pairs={{0,8},{8,0},{16,24},{24,16},{1,9},{9,1},{17,25},{25,17},{2,10},{10... | collective-permute-start | bytes 393224 | tf_op jit(solution)/shard_map/cond/branch_0_fun/ppermute | solution.py:361
  52.3 0.9 %collective-permute-start.6 = (bf16[32,2048]{1,0:T(8,128)(2,1)S(1)}, bf16[32,2048]{1,0:T(8,128)(2,1)}, u32[]{:S(2)}, u32[]{:S(2)}) collective-permute-start(bf16[32,2048]{1,0:T(8,128)(2,1)S(1)} %get-tuple-element.57), channel_id=1, source_target_pairs={{0,16},{8,24},{16,0},{24,8},{1,17},{9,25},{17,1},{25,9},{2,18},{10... | collective-permute-start | bytes 393224 | tf_op jit(solution)/shard_map/cond/branch_0_fun/ppermute | solution.py:361
  53.2 1.8 %collective-permute-start.7 = (bf16[32,2048]{1,0:T(8,128)(2,1)S(1)}, bf16[32,2048]{1,0:T(8,128)(2,1)}, u32[]{:S(2)}, u32[]{:S(2)}) collective-permute-start(bf16[32,2048]{1,0:T(8,128)(2,1)S(1)} %get-tuple-element.58), channel_id=1, source_target_pairs={{0,24},{8,16},{16,8},{24,0},{1,25},{9,17},{17,9},{25,1},{2,26},{10... | collective-permute-start | bytes 393224 | tf_op jit(solution)/shard_map/cond/branch_0_fun/ppermute | solution.py:361
  55.0 3.0 %collective-permute-done.5 = bf16[32,2048]{1,0:T(8,128)(2,1)} collective-permute-done((bf16[32,2048]{1,0:T(8,128)(2,1)S(1)}, bf16[32,2048]{1,0:T(8,128)(2,1)}, u32[]{:S(2)}, u32[]{:S(2)}) %collective-permute-start.5) | collective-permute-done | bytes 131104 | tf_op jit(solution)/shard_map/cond/branch_0_fun/ppermute | solution.py:361
  57.9 2.2 %collective-permute-done.6 = bf16[32,2048]{1,0:T(8,128)(2,1)} collective-permute-done((bf16[32,2048]{1,0:T(8,128)(2,1)S(1)}, bf16[32,2048]{1,0:T(8,128)(2,1)}, u32[]{:S(2)}, u32[]{:S(2)}) %collective-permute-start.6) | collective-permute-done | bytes 131104 | tf_op jit(solution)/shard_map/cond/branch_0_fun/ppermute | solution.py:361
  60.2 0.0 collective-permute-done.7
  60.2 5.0 %mix.1 = bf16[512,2048]{1,0:T(8,128)(2,1)} custom-call(bf16[512,2048]{1,0:T(8,128)(2,1)} %get-tuple-element.105.x_ref, bf16[512,128]{1,0:T(8,128)(2,1)S(1)} %mask.1.mask_ref, bf16[32,2048]{1,0:T(8,128)(2,1)S(1)} %get-tuple-element.106.rest_0_, bf16[32,2048]{1,0:T(8,128)(2,1)} %get-tuple-element.107.rest_1_, bf16[32,2048]{1,0:T(8,128)(2,1)} %get-tuple-element.108.rest_2_, ...), custom_call_target="tpu_custom_call" | custom-call | flops 536870912 | bytes 4194304 | tf_op jit(solution)/shard_map/mix/pallas_call | solution.py:303
  (3 shorter events, 0.0 us)
Async XLA Ops:
  0.0 6.9 %collective-permute-start.19 = (s32[4,32]{1,0:T(4,128)}, s32[4,32]{1,0:T(4,128)S(1)}, u32[]{:S(2)}, u32[]{:S(2)}) collective-permute-start(s32[4,32]{1,0:T(4,128)} %bitcast.9), channel_id=1, source_target_pairs={{0,24},{8,16},{16,8},{24,0},{1,25},{9,17},{17,9},{25,1},{2,26},{10... | collective-permute-start | bytes 1544 | tf_op jit(solution)/shard_map/ppermute | solution.py:361
  3.9 3.8 %collective-permute-start.18 = (s32[4,32]{1,0:T(4,128)}, s32[4,32]{1,0:T(4,128)S(1)}, u32[]{:S(2)}, u32[]{:S(2)}) collective-permute-start(s32[4,32]{1,0:T(4,128)} %bitcast.10), channel_id=1, source_target_pairs={{0,16},{8,24},{16,0},{24,8},{1,17},{9,25},{17,1},{25,9},{2,18},{10... | collective-permute-start | bytes 1544 | tf_op jit(solution)/shard_map/ppermute | solution.py:361
  4.4 3.8 %collective-permute-start.17 = (s32[4,32]{1,0:T(4,128)}, s32[4,32]{1,0:T(4,128)S(1)}, u32[]{:S(2)}, u32[]{:S(2)}) collective-permute-start(s32[4,32]{1,0:T(4,128)} %bitcast.11), channel_id=1, source_target_pairs={{0,8},{8,0},{16,24},{24,16},{1,9},{9,1},{17,25},{25,17},{2,10},{10... | collective-permute-start | bytes 1544 | tf_op jit(solution)/shard_map/ppermute | solution.py:361
  8.2 0.7 %copy-start.1 = (s32[4,32]{1,0:T(4,128)S(1)}, s32[4,32]{1,0:T(4,128)}, u32[]{:S(2)}) copy-start(s32[4,32]{1,0:T(4,128)} %get-tuple-element.96.refs_0_) | copy-start | bytes 1540
  9.2 4.8 %collective-permute-start.20 = (s32[8,128]{1,0:T(8,128)S(1)}, s32[8,128]{1,0:T(8,128)S(1)}, u32[]{:S(2)}, u32[]{:S(2)}) collective-permute-start(s32[8,128]{1,0:T(8,128)S(1)} %list.1.mine_ref), channel_id=1, source_target_pairs={{0,7},{1,2},{2,1},{3,4},{4,3},{5,6},{6,5},{7,0},{8,15},{9,10},{10,... | collective-permute-start | bytes 12296 | tf_op jit(solution)/shard_map/ppermute | solution.py:367
  10.7 4.1 %collective-permute-start.21 = (s32[8,128]{1,0:T(8,128)S(1)}, s32[8,128]{1,0:T(8,128)S(1)}, u32[]{:S(2)}, u32[]{:S(2)}) collective-permute-start(s32[8,128]{1,0:T(8,128)S(1)} %list.1.mine_ref), channel_id=1, source_target_pairs={{0,1},{1,0},{2,3},{3,2},{4,5},{5,4},{6,7},{7,6},{8,9},{9,8},{10,11... | collective-permute-start | bytes 12296 | tf_op jit(solution)/shard_map/ppermute | solution.py:370
  14.0 4.1 %copy-start = (s32[1,1,512,10]{2,1,3,0:T(1,128)S(1)}, s32[1,1,512,10]{2,1,3,0:T(1,128)}, u32[]{:S(2)}) copy-start(s32[1,1,512,10]{2,1,3,0:T(1,128)} %param.7) | copy-start | bytes 61444
  16.2 10.9 %collective-permute-start.25 = (bf16[128,2048]{1,0:T(8,128)(2,1)S(1)}, bf16[128,2048]{1,0:T(8,128)(2,1)S(1)}, u32[]{:S(2)}, u32[]{:S(2)}) collective-permute-start(bf16[128,2048]{1,0:T(8,128)(2,1)S(1)} %get-tuple-element.102), channel_id=1, source_target_pairs={{0,1},{1,0},{2,3},{3,2},{4,5},{5,4},{6,7},{7,6},{8,9},{9,8},{10,11... | collective-permute-start | bytes 1572872 | tf_op jit(solution)/shard_map/ppermute | solution.py:370
  16.3 4.9 %collective-permute-start.23 = (s32[8,128]{1,0:T(8,128)S(1)}, s32[8,128]{1,0:T(8,128)S(1)}, u32[]{:S(2)}, u32[]{:S(2)}) collective-permute-start(s32[8,128]{1,0:T(8,128)S(1)} %get-tuple-element.98), channel_id=1, source_target_pairs={{0,5},{1,6},{2,7},{3,0},{4,1},{5,2},{6,3},{7,4},{8,13},{9,14},{10,... | collective-permute-start | bytes 12296 | tf_op jit(solution)/shard_map/ppermute | solution.py:364
  17.2 4.0 %collective-permute-start.22 = (s32[8,128]{1,0:T(8,128)S(1)}, s32[8,128]{1,0:T(8,128)S(1)}, u32[]{:S(2)}, u32[]{:S(2)}) collective-permute-start(s32[8,128]{1,0:T(8,128)S(1)} %get-tuple-element.98), channel_id=1, source_target_pairs={{0,3},{1,4},{2,5},{3,6},{4,7},{5,0},{6,1},{7,2},{8,11},{9,12},{10,... | collective-permute-start | bytes 12296 | tf_op jit(solution)/shard_map/ppermute | solution.py:364
  18.4 8.8 %collective-permute-start.24 = (bf16[48,2048]{1,0:T(8,128)(2,1)S(1)}, bf16[48,2048]{1,0:T(8,128)(2,1)S(1)}, u32[]{:S(2)}, u32[]{:S(2)}) collective-permute-start(bf16[48,2048]{1,0:T(8,128)(2,1)S(1)} %get-tuple-element.100), channel_id=1, source_target_pairs={{0,7},{1,2},{2,1},{3,4},{4,3},{5,6},{6,5},{7,0},{8,15},{9,10},{10,... | collective-permute-start | bytes 589832 | tf_op jit(solution)/shard_map/ppermute | solution.py:367
  27.5 6.4 %collective-permute-start = (bf16[32,2048]{1,0:T(8,128)(2,1)S(1)}, bf16[32,2048]{1,0:T(8,128)(2,1)S(1)}, u32[]{:S(2)}, u32[]{:S(2)}) collective-permute-start(bf16[32,2048]{1,0:T(8,128)(2,1)S(1)} %get-tuple-element.47), channel_id=1, source_target_pairs={{0,8},{8,0},{16,24},{24,16},{1,9},{9,1},{17,25},{25,17},{2,10},{10... | collective-permute-start | bytes 393224 | tf_op jit(solution)/shard_map/cond/branch_0_fun/ppermute | solution.py:361
  27.7 7.5 %collective-permute-start.1 = (bf16[32,2048]{1,0:T(8,128)(2,1)S(1)}, bf16[32,2048]{1,0:T(8,128)(2,1)S(1)}, u32[]{:S(2)}, u32[]{:S(2)}) collective-permute-start(bf16[32,2048]{1,0:T(8,128)(2,1)S(1)} %get-tuple-element.48), channel_id=1, source_target_pairs={{0,16},{8,24},{16,0},{24,8},{1,17},{9,25},{17,1},{25,9},{2,18},{10... | collective-permute-start | bytes 393224 | tf_op jit(solution)/shard_map/cond/branch_0_fun/ppermute | solution.py:361
  29.2 7.7 %collective-permute-start.2 = (bf16[32,2048]{1,0:T(8,128)(2,1)S(1)}, bf16[32,2048]{1,0:T(8,128)(2,1)S(1)}, u32[]{:S(2)}, u32[]{:S(2)}) collective-permute-start(bf16[32,2048]{1,0:T(8,128)(2,1)S(1)} %get-tuple-element.49), channel_id=1, source_target_pairs={{0,24},{8,16},{16,8},{24,0},{1,25},{9,17},{17,9},{25,1},{2,26},{10... | collective-permute-start | bytes 393224 | tf_op jit(solution)/shard_map/cond/branch_0_fun/ppermute | solution.py:361
  43.2 7.9 %collective-permute-start.4 = (bf16[128,2048]{1,0:T(8,128)(2,1)S(1)}, bf16[128,2048]{1,0:T(8,128)(2,1)S(1)}, u32[]{:S(2)}, u32[]{:S(2)}) collective-permute-start(bf16[128,2048]{1,0:T(8,128)(2,1)S(1)} %get-tuple-element.54), channel_id=1, source_target_pairs={{0,1},{1,0},{2,3},{3,2},{4,5},{5,4},{6,7},{7,6},{8,9},{9,8},{10,11... | collective-permute-start | bytes 1572872 | tf_op jit(solution)/shard_map/cond/branch_0_fun/ppermute | solution.py:370
  43.2 7.8 %collective-permute-start.3 = (bf16[48,2048]{1,0:T(8,128)(2,1)S(1)}, bf16[48,2048]{1,0:T(8,128)(2,1)S(1)}, u32[]{:S(2)}, u32[]{:S(2)}) collective-permute-start(bf16[48,2048]{1,0:T(8,128)(2,1)S(1)} %get-tuple-element.51), channel_id=1, source_target_pairs={{0,7},{1,2},{2,1},{3,4},{4,3},{5,6},{6,5},{7,0},{8,15},{9,10},{10,... | collective-permute-start | bytes 589832 | tf_op jit(solution)/shard_map/cond/branch_0_fun/ppermute | solution.py:367
  51.4 6.5 %collective-permute-start.5 = (bf16[32,2048]{1,0:T(8,128)(2,1)S(1)}, bf16[32,2048]{1,0:T(8,128)(2,1)}, u32[]{:S(2)}, u32[]{:S(2)}) collective-permute-start(bf16[32,2048]{1,0:T(8,128)(2,1)S(1)} %get-tuple-element.56), channel_id=1, source_target_pairs={{0,8},{8,0},{16,24},{24,16},{1,9},{9,1},{17,25},{25,17},{2,10},{10... | collective-permute-start | bytes 393224 | tf_op jit(solution)/shard_map/cond/branch_0_fun/ppermute | solution.py:361
  52.3 7.9 %collective-permute-start.6 = (bf16[32,2048]{1,0:T(8,128)(2,1)S(1)}, bf16[32,2048]{1,0:T(8,128)(2,1)}, u32[]{:S(2)}, u32[]{:S(2)}) collective-permute-start(bf16[32,2048]{1,0:T(8,128)(2,1)S(1)} %get-tuple-element.57), channel_id=1, source_target_pairs={{0,16},{8,24},{16,0},{24,8},{1,17},{9,25},{17,1},{25,9},{2,18},{10... | collective-permute-start | bytes 393224 | tf_op jit(solution)/shard_map/cond/branch_0_fun/ppermute | solution.py:361
  53.2 7.0 %collective-permute-start.7 = (bf16[32,2048]{1,0:T(8,128)(2,1)S(1)}, bf16[32,2048]{1,0:T(8,128)(2,1)}, u32[]{:S(2)}, u32[]{:S(2)}) collective-permute-start(bf16[32,2048]{1,0:T(8,128)(2,1)S(1)} %get-tuple-element.58), channel_id=1, source_target_pairs={{0,24},{8,16},{16,8},{24,0},{1,25},{9,17},{17,9},{25,1},{2,26},{10... | collective-permute-start | bytes 393224 | tf_op jit(solution)/shard_map/cond/branch_0_fun/ppermute | solution.py:361

commit v6 on v5

--- a/solution.py
+++ b/solution.py
@@ -47,7 +47,7 @@
     return pl.pallas_call(
         normalize_kernel,
         in_specs=[pl.BlockSpec(memory_space=pl.ANY)] * 2,
-        out_shape=[bf16(rows, width), jax.ShapeDtypeStruct(wanted.shape, jnp.int32)],
+        out_shape=[bf16(rows, width), pltpu.VMEM(wanted.shape, jnp.int32)],
         scratch_shapes=[
             pltpu.VMEM((rows, width), jnp.bfloat16),
             pltpu.SemaphoreType.DMA((rows // BLOCK + 1,)),
@@ -240,29 +240,42 @@
     )(x, select)
 
 
-def combine_kernel(expand_ref, far_ref, own_ref, core_ref, *out_refs):
-    cap, sent = out_refs[0].shape[0], far_ref.shape[0]
-    far = jnp.dot(expand_ref[:, :sent], far_ref[...], preferred_element_type=jnp.float32)
-    rows = (far + own_ref[...].astype(jnp.float32) + core_ref[...].astype(jnp.float32)).astype(
-        jnp.bfloat16
-    )
+def unpack_kernel(first, expand_ref, far_ref, base_ref, out_ref):
+    sent = far_ref.shape[0]
+    far = jnp.dot(
+        expand_ref[:, first : first + sent], far_ref[...], preferred_element_type=jnp.float32
+    )
+    out_ref[...] = (far + base_ref[...].astype(jnp.float32)).astype(jnp.bfloat16)
+
+
+def unpack_call(expand, far, base, first=0):
+    return pl.pallas_call(
+        functools.partial(unpack_kernel, first),
+        out_shape=bf16(*base.shape),
+        compiler_params=params(),
+        cost_estimate=pl.CostEstimate(flops=2**34, bytes_accessed=2**25, transcendentals=0),
+        name="unpack",
+    )(expand, far, base)
+
+
+def combine_kernel(base_ref, core_ref, *out_refs):
+    cap = out_refs[0].shape[0]
     for d, out in enumerate(out_refs):
-        out[...] = rows[d * cap : (d + 1) * cap]
-
-
-def combine_call(expand, far, own, core, servers):
-    total, width = own.shape
+        here = slice(d * cap, (d + 1) * cap)
+        out[...] = base_ref[here] + core_ref[here]
+
+
+def combine_call(base, core, servers):
+    total, width = base.shape
     return pl.pallas_call(
         combine_kernel,
         out_shape=[bf16(total // servers, width)] * servers,
         compiler_params=params(),
         cost_estimate=pl.CostEstimate(
-            flops=2 * total * far.shape[0] * width,
-            bytes_accessed=8 * total * width,
-            transcendentals=0,
+            flops=total * width, bytes_accessed=6 * total * width, transcendentals=0
         ),
         name="combine",
-    )(expand, far, own, core)
+    )(base, core)
 
 
 def fill(buffer, parts):
@@ -302,8 +315,8 @@
     total, servers = mask.shape[1], len(parts)
     return pl.pallas_call(
         functools.partial(last_kernel, servers),
-        out_specs=pl.BlockSpec(memory_space=pl.ANY),
-        out_shape=bf16(rows, width),
+        out_specs=pl.BlockSpec(memory_space=pltpu.HBM),
+        out_shape=pltpu.HBM((rows, width), jnp.bfloat16),
         scratch_shapes=[
             pltpu.VMEM((total, width), jnp.bfloat16),
             pltpu.VMEM((rows, total), jnp.bfloat16),
@@ -369,26 +382,27 @@
     def inside(value):
         return lax.ppermute(value, "rep", within)
 
-    def exchange(expand, far, own, core):
-        parts = combine_call(expand, far, own, core, servers)
+    def exchange(base, core):
+        parts = combine_call(base, core, servers)
         got = {d: turn(parts[d], d) for d in reversed(range(1, servers))}
         return [parts[0]] + [got[d] for d in range(1, servers)]
 
-    def rounds(x, mask, pack, select, expand, far, own, core):
-        parts = exchange(expand, far, own, core)
+    def rounds(x, mask, pack, select, expand, count, base, core):
+        parts = exchange(base, core)
         for _ in range(ROUNDS - 1):
-            x, far = round_call(x, mask, pack, parts, far.shape[0])
+            x, far = round_call(x, mask, pack, parts, count)
             far = across(far)
             core, own = again_call(x, select)
-            parts = exchange(expand, far, own, inside(core))
-        return x, *parts
-
-    def in_full(x, mask, pack, select, expand, far, rest, own, core):
-        far = jnp.concatenate([far, across(rest)], axis=0)
-        return rounds(x, mask, pack, select, expand, far, own, core)
-
-    def as_sent(x, mask, pack, select, expand, far, rest, own, core):
-        return rounds(x, mask, pack, select, expand, far, own, core)
+            core = inside(core)
+            parts = exchange(unpack_call(expand, far, own), core)
+        return last_call(x, mask, parts)
+
+    def in_full(x, mask, pack, select, expand, rest, base, core):
+        base = unpack_call(expand, across(rest), base, sent)
+        return rounds(x, mask, pack, select, expand, total, base, core)
+
+    def as_sent(x, mask, pack, select, expand, rest, base, core):
+        return rounds(x, mask, pack, select, expand, sent, base, core)
 
     asked = {d: turn(wanted, d) for d in reversed(range(1, servers))}
     x, held = normalize_call(descriptors[0, 0], wanted)
@@ -400,16 +414,17 @@
         x, pack, mine, within_list, beyond_list, sent
     )
     core = inside(core)
+    base = unpack_call(expand, far, own)
     mask = mask_call(pick.transpose(0, 3, 1, 2)[0], total, cap)
     reach = 1
     while 2 * reach + 1 < groups:
         by = 2 * reach + 1
         most = jnp.maximum(most, jnp.maximum(shift(most, by), shift(most, -by)))
         reach += by
-    x, *parts = lax.cond(
-        most[0, 0] > sent, in_full, as_sent, x, mask, pack, select, expand, far, rest, own, core
-    )
-    return last_call(x, mask, parts)[None, None]
+    out = lax.cond(
+        most[0, 0] > sent, in_full, as_sent, x, mask, pack, select, expand, rest, base, core
+    )
+    return out[None, None]
 
 
 def solution(mesh):

time: 65.4 us -> 58.5 us (0.89)
  Pallas kernels: 17.2 us -> 12.3 us
  starting transfers between devices: 20 us -> 18 us
  local copies, waits for them, and re-layouts: 1.2 us -> 0.52 us
    ppermute x3, starting transfers between devices: 6.3 us -> 4.17 us  [across(): return lax.ppermute(value, 'rep', beyond)]
    ppermute x3, waiting for transfers between devices: 13.7 us -> 15.5 us  [across(): return lax.ppermute(value, 'rep', beyond)]
    pallas_call x1, Pallas kernels: 5 us -> 3.33 us  [last_call(): pl.pallas_call(functools.partial(last_kernel, servers), out_specs=pl.Bloc...]
    pallas_call x1, Pallas kernels: 2.3 us -> 0.71 us  [again_call(): pl.pallas_call(again_kernel, out_shape=[bf16(total, width)] * 2, compiler...]
    ppermute x9, waiting for transfers between devices: 12.3 us -> 10.8 us  [turn(): return lax.ppermute(value, 'clus', [(c, c ^ d) for c in range(servers)])]
    pallas_call x1, Pallas kernels: 4.03 us -> 3.01 us  [round_call(): pl.pallas_call(functools.partial(round_kernel, servers), out_shape=[bf16(...]
    unnamed x4 -> x2, local copies, waits for them, and re-layouts: 0.69 us -> 0.01 us
  transfers between devices with their start and end apart: 17 -> 17, of which waited for: 10 -> 12; matrix products, arithmetic and copies ran while one was open for 1% -> 1% of each run, Pallas kernels for 5% -> 7%
where the time goes in v6:
time: 58.5 us; the launch traced here: 58.4 us
  waiting for transfers between devices  26.4 us (45%)
  starting transfers between devices  18 us (31%)
  Pallas kernels  12.3 us (21%)
  between operations  0.86 us (1%)
    ppermute x3, waiting for transfers between devices, across(): return lax.ppermute(value, 'rep', beyond)  15.5 us
    ppermute x9, starting transfers between devices, turn(): return lax.ppermute(value, 'clus', [(c, c ^ d) for c in range(servers)])  11.6 us
    ppermute x9, waiting for transfers between devices, turn(): return lax.ppermute(value, 'clus', [(c, c ^ d) for c in range(servers)])  10.8 us
    ppermute x3, starting transfers between devices, across(): return lax.ppermute(value, 'rep', beyond)  4.17 us
    pallas_call x1, Pallas kernels, last_call(): pl.pallas_call(functools.partial(last_kernel, servers), out_specs=pl.Bloc...  3.33 us
    pallas_call x1, Pallas kernels, round_call(): pl.pallas_call(functools.partial(round_kernel, servers), out_shape=[bf16(...  3.01 us
    pallas_call x1, Pallas kernels, normalize_call(): pl.pallas_call(normalize_kernel, in_specs=[pl.BlockSpec(memory_space=pl.A...  1.89 us
    ppermute x2, starting transfers between devices, shift(): lax.ppermute(value, 'rep', [(g, (g + by) % groups) for g in range(groups)])  1.8 us
  transfers between devices with their start and end apart: 17, of which 12 were waited for; matrix products, arithmetic and copies ran while one was open for 1% of the time, Pallas kernels for 7%

profile of v6, /device:TPU:0, one launch (start us, length us, event | category | flops | bytes accessed | tf_op | source)
XLA Modules:
  0.0 58.4 jit_solution(6374517862179627829)
XLA Ops:
  0.0 3.9 %collective-permute-start.19 = (s32[4,32]{1,0:T(4,128)}, s32[4,32]{1,0:T(4,128)S(1)}, u32[]{:S(2)}, u32[]{:S(2)}) collective-permute-start(s32[4,32]{1,0:T(4,128)} %bitcast.12), channel_id=1, source_target_pairs={{0,24},{8,16},{16,8},{24,0},{1,25},{9,17},{17,9},{25,1},{2,26},{10... | collective-permute-start | bytes 1544 | tf_op jit(solution)/shard_map/ppermute | solution.py:374
  3.9 0.5 collective-permute-start.18
  4.4 0.1 collective-permute-start.17
  4.5 1.9 %normalize.1 = (bf16[512,2048]{1,0:T(8,128)(2,1)S(1)}, s32[4,32]{1,0:T(4,128)S(1)}) custom-call(bf16[512,2048]{1,0:T(8,128)(2,1)} %bitcast.11, s32[4,32]{1,0:T(4,128)} %bitcast.15), custom_call_target="tpu_custom_call" | custom-call | flops 6291456 | bytes 4194304 | tf_op jit(solution)/shard_map/normalize/pallas_call | solution.py:47
  6.4 0.0 collective-permute-done.19.refs_3_
  6.4 1.3 %collective-permute-done.18.refs_2_ = s32[4,32]{1,0:T(4,128)S(1)} collective-permute-done((s32[4,32]{1,0:T(4,128)}, s32[4,32]{1,0:T(4,128)S(1)}, u32[]{:S(2)}, u32[]{:S(2)}) %collective-permute-start.18) | collective-permute-done | bytes 544 | tf_op jit(solution)/shard_map/ppermute | solution.py:374
  7.7 0.5 collective-permute-done.17.refs_1_
  8.2 0.3 list.1.mine_ref
  8.5 1.3 %collective-permute-start.20 = (s32[8,128]{1,0:T(8,128)S(1)}, s32[8,128]{1,0:T(8,128)S(1)}, u32[]{:S(2)}, u32[]{:S(2)}) collective-permute-start(s32[8,128]{1,0:T(8,128)S(1)} %list.1.mine_ref), channel_id=1, source_target_pairs={{0,7},{1,2},{2,1},{3,4},{4,3},{5,6},{6,5},{7,0},{8,15},{9,10},{10,... | collective-permute-start | bytes 12296 | tf_op jit(solution)/shard_map/ppermute | solution.py:380
  9.9 0.4 collective-permute-start.21
  10.2 3.1 %collective-permute-done.20.beyond_ref = s32[8,128]{1,0:T(8,128)S(1)} collective-permute-done((s32[8,128]{1,0:T(8,128)S(1)}, s32[8,128]{1,0:T(8,128)S(1)}, u32[]{:S(2)}, u32[]{:S(2)}) %collective-permute-start.20) | collective-permute-done | bytes 4128 | tf_op jit(solution)/shard_map/ppermute | solution.py:380
  13.4 0.7 %pack_far.1 = (bf16[128,512]{1,0:T(8,128)(2,1)S(1)}, bf16[48,2048]{1,0:T(8,128)(2,1)S(1)}) custom-call(bf16[512,2048]{1,0:T(8,128)(2,1)S(1)} %get-tuple-element.88.x_ref, s32[8,128]{1,0:T(8,128)S(1)} %collective-permute-done.20.beyond_ref), custom_call_target="tpu_custom_call" | custom-call | flops 67108864 | bytes 2097152 | tf_op jit(solution)/shard_map/pack_far/pallas_call | solution.py:171
  14.1 0.0 collective-permute-done.21.within_ref
  14.1 1.5 %serve_near.1 = (bf16[256,512]{1,0:T(8,128)(2,1)S(1)}, bf16[128,128]{1,0:T(8,128)(2,1)S(1)}, s32[8,128]{1,0:T(8,128)S(1)}, bf16[128,2048]{1,0:T(8,128)(2,1)S(1)}...) custom-call(bf16[512,2048]{1,0:T(8,128)(2,1)S(1)} %get-tuple-element.88.x_ref, ...), custom_call_target="tpu_custom_call" | custom-call | flops 805306368 | bytes 4194304 | tf_op jit(solution)/shard_map/serve_near/pallas_call | solution.py:207
  15.6 0.6 collective-permute-start.23
  16.1 1.2 %collective-permute-start.22 = (s32[8,128]{1,0:T(8,128)S(1)}, s32[8,128]{1,0:T(8,128)S(1)}, u32[]{:S(2)}, u32[]{:S(2)}) collective-permute-start(s32[8,128]{1,0:T(8,128)S(1)} %get-tuple-element.91), channel_id=1, source_target_pairs={{0,3},{1,4},{2,5},{3,6},{4,7},{5,0},{6,1},{7,2},{8,11},{9,12},{10,... | collective-permute-start | bytes 12296 | tf_op jit(solution)/shard_map/ppermute | solution.py:377
  17.4 0.3 mask.1
  17.6 2.3 %collective-permute-start.24 = (bf16[48,2048]{1,0:T(8,128)(2,1)S(1)}, bf16[48,2048]{1,0:T(8,128)(2,1)S(1)}, u32[]{:S(2)}, u32[]{:S(2)}) collective-permute-start(bf16[48,2048]{1,0:T(8,128)(2,1)S(1)} %get-tuple-element.93), channel_id=1, source_target_pairs={{0,7},{1,2},{2,1},{3,4},{4,3},{5,6},{6,5},{7,0},{8,15},{9,10},{10,... | collective-permute-start | bytes 589832 | tf_op jit(solution)/shard_map/ppermute | solution.py:380
  19.9 0.0 collective-permute-start.25
  19.9 0.0 collective-permute-done.23
  19.9 0.1 collective-permute-done.22
  20.0 0.5 slice.3
  21.2 5.2 %collective-permute-done.24.far_ref = bf16[48,2048]{1,0:T(8,128)(2,1)S(1)} collective-permute-done((bf16[48,2048]{1,0:T(8,128)(2,1)S(1)}, bf16[48,2048]{1,0:T(8,128)(2,1)S(1)}, u32[]{:S(2)}, u32[]{:S(2)}) %collective-permute-start.24) | collective-permute-done | bytes 196640 | tf_op jit(solution)/shard_map/ppermute | solution.py:380
  26.4 0.3 unpack.7
  26.7 0.0 collective-permute-done.25
  26.7 31.5 %conditional.1 = (bf16[1,1,512,2048]{3,2,1,0:T(8,128)(2,1)}) conditional(s32[]{:T(128)} %bitcast.4, (bf16[128,2048]{1,0:T(8,128)(2,1)S(1)}, bf16[128,2048]{1,0:T(8,128)(2,1)S(1)}, bf16[512,2048]{1,0:T(8,128)(2,1)S(1)}, bf16[512,128]{1,0:T(8,128)(2,1)S(1)}, bf16[128,512]{1,0:T(8,128)(2,1)S(1)}, /*index=5*/bf16[256,512]{1,0:T(8,128)(2,1)S(1)}, ...), branch_computations={%region_0.0_spmd, %region_1.0_spmd} | conditional | flops 36105093120 | bytes 93585776 | solution.py:424
  26.7 0.1 combine.4
  26.8 0.1 collective-permute-start
  26.9 2.0 %collective-permute-start.1 = (bf16[32,2048]{1,0:T(8,128)(2,1)S(1)}, bf16[32,2048]{1,0:T(8,128)(2,1)S(1)}, u32[]{:S(2)}, u32[]{:S(2)}) collective-permute-start(bf16[32,2048]{1,0:T(8,128)(2,1)S(1)} %get-tuple-element.46), channel_id=1, source_target_pairs={{0,16},{8,24},{16,0},{24,8},{1,17},{9,25},{17,1},{25,9},{2,18},{10... | collective-permute-start | bytes 393224 | tf_op jit(solution)/shard_map/cond/branch_0_fun/ppermute | solution.py:374
  28.9 1.4 %collective-permute-start.2 = (bf16[32,2048]{1,0:T(8,128)(2,1)S(1)}, bf16[32,2048]{1,0:T(8,128)(2,1)S(1)}, u32[]{:S(2)}, u32[]{:S(2)}) collective-permute-start(bf16[32,2048]{1,0:T(8,128)(2,1)S(1)} %get-tuple-element.47), channel_id=1, source_target_pairs={{0,24},{8,16},{16,8},{24,0},{1,25},{9,17},{17,9},{25,1},{2,26},{10... | collective-permute-start | bytes 393224 | tf_op jit(solution)/shard_map/cond/branch_0_fun/ppermute | solution.py:374
  30.3 1.9 %collective-permute-done.rest_1_ = bf16[32,2048]{1,0:T(8,128)(2,1)S(1)} collective-permute-done((bf16[32,2048]{1,0:T(8,128)(2,1)S(1)}, bf16[32,2048]{1,0:T(8,128)(2,1)S(1)}, u32[]{:S(2)}, u32[]{:S(2)}) %collective-permute-start) | collective-permute-done | bytes 131104 | tf_op jit(solution)/shard_map/cond/branch_0_fun/ppermute | solution.py:374
  32.3 0.7 %collective-permute-done.1.rest_2_ = bf16[32,2048]{1,0:T(8,128)(2,1)S(1)} collective-permute-done((bf16[32,2048]{1,0:T(8,128)(2,1)S(1)}, bf16[32,2048]{1,0:T(8,128)(2,1)S(1)}, u32[]{:S(2)}, u32[]{:S(2)}) %collective-permute-start.1) | collective-permute-done | bytes 131104 | tf_op jit(solution)/shard_map/cond/branch_0_fun/ppermute | solution.py:374
  33.0 1.8 %collective-permute-done.2.rest_3_ = bf16[32,2048]{1,0:T(8,128)(2,1)S(1)} collective-permute-done((bf16[32,2048]{1,0:T(8,128)(2,1)S(1)}, bf16[32,2048]{1,0:T(8,128)(2,1)S(1)}, u32[]{:S(2)}, u32[]{:S(2)}) %collective-permute-start.2) | collective-permute-done | bytes 131104 | tf_op jit(solution)/shard_map/cond/branch_0_fun/ppermute | solution.py:374
  34.8 3.0 %mix_and_pack.2 = (bf16[512,2048]{1,0:T(8,128)(2,1)S(1)}, bf16[48,2048]{1,0:T(8,128)(2,1)S(1)}) custom-call(bf16[512,2048]{1,0:T(8,128)(2,1)S(1)} %get-tuple-element.39.x_ref, bf16[512,128]{1,0:T(8,128)(2,1)S(1)} %get-tuple-element.40.mask_ref, bf16[128,512]{1,0:T(8,128)(2,1)S(1)} %get-tuple-element.41.pack_ref, ...), custom_call_target="tpu_custom_call" | custom-call | flops 671088640 | bytes 6291456 | tf_op jit(solution)/shard_map/cond/branch_0_fun/mix_and_pack/pallas_call | solution.py:348
  37.8 0.6 collective-permute-start.3
  38.3 0.7 %serve_again.2 = (bf16[128,2048]{1,0:T(8,128)(2,1)S(1)}, bf16[128,2048]{1,0:T(8,128)(2,1)S(1)}) custom-call(bf16[512,2048]{1,0:T(8,128)(2,1)S(1)} %get-tuple-element.48.x_ref, bf16[256,512]{1,0:T(8,128)(2,1)S(1)} %get-tuple-element.51.select_ref), custom_call_target="tpu_custom_call" | custom-call | flops 536870912 | bytes 4194304 | tf_op jit(solution)/shard_map/cond/branch_0_fun/serve_again/pallas_call | solution.py:232
  39.0 0.1 collective-permute-start.4
  39.1 7.1 %collective-permute-done.3.far_ref = bf16[48,2048]{1,0:T(8,128)(2,1)S(1)} collective-permute-done((bf16[48,2048]{1,0:T(8,128)(2,1)S(1)}, bf16[48,2048]{1,0:T(8,128)(2,1)S(1)}, u32[]{:S(2)}, u32[]{:S(2)}) %collective-permute-start.3) | collective-permute-done | bytes 196640 | tf_op jit(solution)/shard_map/cond/branch_0_fun/ppermute | solution.py:380
  46.3 0.3 unpack.4.base_ref
  46.5 0.0 collective-permute-done.4.core_ref
  46.5 0.1 combine.5
  46.6 1.2 %collective-permute-start.5 = (bf16[32,2048]{1,0:T(8,128)(2,1)S(1)}, bf16[32,2048]{1,0:T(8,128)(2,1)S(1)}, u32[]{:S(2)}, u32[]{:S(2)}) collective-permute-start(bf16[32,2048]{1,0:T(8,128)(2,1)S(1)} %get-tuple-element.55), channel_id=1, source_target_pairs={{0,8},{8,0},{16,24},{24,16},{1,9},{9,1},{17,25},{25,17},{2,10},{10... | collective-permute-start | bytes 393224 | tf_op jit(solution)/shard_map/cond/branch_0_fun/ppermute | solution.py:374
  47.8 1.0 %collective-permute-start.6 = (bf16[32,2048]{1,0:T(8,128)(2,1)S(1)}, bf16[32,2048]{1,0:T(8,128)(2,1)S(1)}, u32[]{:S(2)}, u32[]{:S(2)}) collective-permute-start(bf16[32,2048]{1,0:T(8,128)(2,1)S(1)} %get-tuple-element.56), channel_id=1, source_target_pairs={{0,16},{8,24},{16,0},{24,8},{1,17},{9,25},{17,1},{25,9},{2,18},{10... | collective-permute-start | bytes 393224 | tf_op jit(solution)/shard_map/cond/branch_0_fun/ppermute | solution.py:374
  48.8 1.3 %collective-permute-start.7 = (bf16[32,2048]{1,0:T(8,128)(2,1)S(1)}, bf16[32,2048]{1,0:T(8,128)(2,1)S(1)}, u32[]{:S(2)}, u32[]{:S(2)}) collective-permute-start(bf16[32,2048]{1,0:T(8,128)(2,1)S(1)} %get-tuple-element.57), channel_id=1, source_target_pairs={{0,24},{8,16},{16,8},{24,0},{1,25},{9,17},{17,9},{25,1},{2,26},{10... | collective-permute-start | bytes 393224 | tf_op jit(solution)/shard_map/cond/branch_0_fun/ppermute | solution.py:374
  50.2 1.5 %collective-permute-done.5.rest_1_ = bf16[32,2048]{1,0:T(8,128)(2,1)S(1)} collective-permute-done((bf16[32,2048]{1,0:T(8,128)(2,1)S(1)}, bf16[32,2048]{1,0:T(8,128)(2,1)S(1)}, u32[]{:S(2)}, u32[]{:S(2)}) %collective-permute-start.5) | collective-permute-done | bytes 131104 | tf_op jit(solution)/shard_map/cond/branch_0_fun/ppermute | solution.py:374
  51.6 1.1 %collective-permute-done.6.rest_2_ = bf16[32,2048]{1,0:T(8,128)(2,1)S(1)} collective-permute-done((bf16[32,2048]{1,0:T(8,128)(2,1)S(1)}, bf16[32,2048]{1,0:T(8,128)(2,1)S(1)}, u32[]{:S(2)}, u32[]{:S(2)}) %collective-permute-start.6) | collective-permute-done | bytes 131104 | tf_op jit(solution)/shard_map/cond/branch_0_fun/ppermute | solution.py:374
  52.8 1.9 %collective-permute-done.7.rest_3_ = bf16[32,2048]{1,0:T(8,128)(2,1)S(1)} collective-permute-done((bf16[32,2048]{1,0:T(8,128)(2,1)S(1)}, bf16[32,2048]{1,0:T(8,128)(2,1)S(1)}, u32[]{:S(2)}, u32[]{:S(2)}) %collective-permute-start.7) | collective-permute-done | bytes 131104 | tf_op jit(solution)/shard_map/cond/branch_0_fun/ppermute | solution.py:374
  54.7 3.3 %mix.2 = bf16[512,2048]{1,0:T(8,128)(2,1)} custom-call(bf16[512,2048]{1,0:T(8,128)(2,1)S(1)} %get-tuple-element.48.x_ref, bf16[512,128]{1,0:T(8,128)(2,1)S(1)} %get-tuple-element.40.mask_ref, bf16[32,2048]{1,0:T(8,128)(2,1)S(1)} %get-tuple-element.54.rest_0_, bf16[32,2048]{1,0:T(8,128)(2,1)S(1)} %collective-permute-done.5.rest_1_, ...), custom_call_target="tpu_custom_call" | custom-call | flops 536870912 | bytes 4194304 | tf_op jit(solution)/shard_map/cond/branch_0_fun/mix/pallas_call | solution.py:316
  (3 shorter events, 0.0 us)
Async XLA Ops:
  0.0 6.4 %collective-permute-start.19 = (s32[4,32]{1,0:T(4,128)}, s32[4,32]{1,0:T(4,128)S(1)}, u32[]{:S(2)}, u32[]{:S(2)}) collective-permute-start(s32[4,32]{1,0:T(4,128)} %bitcast.12), channel_id=1, source_target_pairs={{0,24},{8,16},{16,8},{24,0},{1,25},{9,17},{17,9},{25,1},{2,26},{10... | collective-permute-start | bytes 1544 | tf_op jit(solution)/shard_map/ppermute | solution.py:374
  3.9 3.8 %collective-permute-start.18 = (s32[4,32]{1,0:T(4,128)}, s32[4,32]{1,0:T(4,128)S(1)}, u32[]{:S(2)}, u32[]{:S(2)}) collective-permute-start(s32[4,32]{1,0:T(4,128)} %bitcast.13), channel_id=1, source_target_pairs={{0,16},{8,24},{16,0},{24,8},{1,17},{9,25},{17,1},{25,9},{2,18},{10... | collective-permute-start | bytes 1544 | tf_op jit(solution)/shard_map/ppermute | solution.py:374
  4.4 3.8 %collective-permute-start.17 = (s32[4,32]{1,0:T(4,128)}, s32[4,32]{1,0:T(4,128)S(1)}, u32[]{:S(2)}, u32[]{:S(2)}) collective-permute-start(s32[4,32]{1,0:T(4,128)} %bitcast.14), channel_id=1, source_target_pairs={{0,8},{8,0},{16,24},{24,16},{1,9},{9,1},{17,25},{25,17},{2,10},{10... | collective-permute-start | bytes 1544 | tf_op jit(solution)/shard_map/ppermute | solution.py:374
  8.5 4.8 %collective-permute-start.20 = (s32[8,128]{1,0:T(8,128)S(1)}, s32[8,128]{1,0:T(8,128)S(1)}, u32[]{:S(2)}, u32[]{:S(2)}) collective-permute-start(s32[8,128]{1,0:T(8,128)S(1)} %list.1.mine_ref), channel_id=1, source_target_pairs={{0,7},{1,2},{2,1},{3,4},{4,3},{5,6},{6,5},{7,0},{8,15},{9,10},{10,... | collective-permute-start | bytes 12296 | tf_op jit(solution)/shard_map/ppermute | solution.py:380
  9.9 4.2 %collective-permute-start.21 = (s32[8,128]{1,0:T(8,128)S(1)}, s32[8,128]{1,0:T(8,128)S(1)}, u32[]{:S(2)}, u32[]{:S(2)}) collective-permute-start(s32[8,128]{1,0:T(8,128)S(1)} %list.1.mine_ref), channel_id=1, source_target_pairs={{0,1},{1,0},{2,3},{3,2},{4,5},{5,4},{6,7},{7,6},{8,9},{9,8},{10,11... | collective-permute-start | bytes 12296 | tf_op jit(solution)/shard_map/ppermute | solution.py:383
  13.4 4.0 %copy-start = (s32[1,1,512,10]{2,1,3,0:T(1,128)S(1)}, s32[1,1,512,10]{2,1,3,0:T(1,128)}, u32[]{:S(2)}) copy-start(s32[1,1,512,10]{2,1,3,0:T(1,128)} %param.7) | copy-start | bytes 61444
  15.6 4.3 %collective-permute-start.23 = (s32[8,128]{1,0:T(8,128)S(1)}, s32[8,128]{1,0:T(8,128)S(1)}, u32[]{:S(2)}, u32[]{:S(2)}) collective-permute-start(s32[8,128]{1,0:T(8,128)S(1)} %get-tuple-element.91), channel_id=1, source_target_pairs={{0,5},{1,6},{2,7},{3,0},{4,1},{5,2},{6,3},{7,4},{8,13},{9,14},{10,... | collective-permute-start | bytes 12296 | tf_op jit(solution)/shard_map/ppermute | solution.py:377
  16.1 3.9 %collective-permute-start.22 = (s32[8,128]{1,0:T(8,128)S(1)}, s32[8,128]{1,0:T(8,128)S(1)}, u32[]{:S(2)}, u32[]{:S(2)}) collective-permute-start(s32[8,128]{1,0:T(8,128)S(1)} %get-tuple-element.91), channel_id=1, source_target_pairs={{0,3},{1,4},{2,5},{3,6},{4,7},{5,0},{6,1},{7,2},{8,11},{9,12},{10,... | collective-permute-start | bytes 12296 | tf_op jit(solution)/shard_map/ppermute | solution.py:377
  17.6 8.8 %collective-permute-start.24 = (bf16[48,2048]{1,0:T(8,128)(2,1)S(1)}, bf16[48,2048]{1,0:T(8,128)(2,1)S(1)}, u32[]{:S(2)}, u32[]{:S(2)}) collective-permute-start(bf16[48,2048]{1,0:T(8,128)(2,1)S(1)} %get-tuple-element.93), channel_id=1, source_target_pairs={{0,7},{1,2},{2,1},{3,4},{4,3},{5,6},{6,5},{7,0},{8,15},{9,10},{10,... | collective-permute-start | bytes 589832 | tf_op jit(solution)/shard_map/ppermute | solution.py:380
  19.9 6.8 %collective-permute-start.25 = (bf16[128,2048]{1,0:T(8,128)(2,1)S(1)}, bf16[128,2048]{1,0:T(8,128)(2,1)S(1)}, u32[]{:S(2)}, u32[]{:S(2)}) collective-permute-start(bf16[128,2048]{1,0:T(8,128)(2,1)S(1)} %get-tuple-element.95), channel_id=1, source_target_pairs={{0,1},{1,0},{2,3},{3,2},{4,5},{5,4},{6,7},{7,6},{8,9},{9,8},{10,11... | collective-permute-start | bytes 1572872 | tf_op jit(solution)/shard_map/ppermute | solution.py:383
  26.8 5.5 %collective-permute-start = (bf16[32,2048]{1,0:T(8,128)(2,1)S(1)}, bf16[32,2048]{1,0:T(8,128)(2,1)S(1)}, u32[]{:S(2)}, u32[]{:S(2)}) collective-permute-start(bf16[32,2048]{1,0:T(8,128)(2,1)S(1)} %get-tuple-element.45), channel_id=1, source_target_pairs={{0,8},{8,0},{16,24},{24,16},{1,9},{9,1},{17,25},{25,17},{2,10},{10... | collective-permute-start | bytes 393224 | tf_op jit(solution)/shard_map/cond/branch_0_fun/ppermute | solution.py:374
  26.9 6.1 %collective-permute-start.1 = (bf16[32,2048]{1,0:T(8,128)(2,1)S(1)}, bf16[32,2048]{1,0:T(8,128)(2,1)S(1)}, u32[]{:S(2)}, u32[]{:S(2)}) collective-permute-start(bf16[32,2048]{1,0:T(8,128)(2,1)S(1)} %get-tuple-element.46), channel_id=1, source_target_pairs={{0,16},{8,24},{16,0},{24,8},{1,17},{9,25},{17,1},{25,9},{2,18},{10... | collective-permute-start | bytes 393224 | tf_op jit(solution)/shard_map/cond/branch_0_fun/ppermute | solution.py:374
  28.9 5.9 %collective-permute-start.2 = (bf16[32,2048]{1,0:T(8,128)(2,1)S(1)}, bf16[32,2048]{1,0:T(8,128)(2,1)S(1)}, u32[]{:S(2)}, u32[]{:S(2)}) collective-permute-start(bf16[32,2048]{1,0:T(8,128)(2,1)S(1)} %get-tuple-element.47), channel_id=1, source_target_pairs={{0,24},{8,16},{16,8},{24,0},{1,25},{9,17},{17,9},{25,1},{2,26},{10... | collective-permute-start | bytes 393224 | tf_op jit(solution)/shard_map/cond/branch_0_fun/ppermute | solution.py:374
  37.8 8.5 %collective-permute-start.3 = (bf16[48,2048]{1,0:T(8,128)(2,1)S(1)}, bf16[48,2048]{1,0:T(8,128)(2,1)S(1)}, u32[]{:S(2)}, u32[]{:S(2)}) collective-permute-start(bf16[48,2048]{1,0:T(8,128)(2,1)S(1)} %get-tuple-element.50), channel_id=1, source_target_pairs={{0,7},{1,2},{2,1},{3,4},{4,3},{5,6},{6,5},{7,0},{8,15},{9,10},{10,... | collective-permute-start | bytes 589832 | tf_op jit(solution)/shard_map/cond/branch_0_fun/ppermute | solution.py:380
  39.0 7.5 %collective-permute-start.4 = (bf16[128,2048]{1,0:T(8,128)(2,1)S(1)}, bf16[128,2048]{1,0:T(8,128)(2,1)S(1)}, u32[]{:S(2)}, u32[]{:S(2)}) collective-permute-start(bf16[128,2048]{1,0:T(8,128)(2,1)S(1)} %get-tuple-element.53), channel_id=1, source_target_pairs={{0,1},{1,0},{2,3},{3,2},{4,5},{5,4},{6,7},{7,6},{8,9},{9,8},{10,11... | collective-permute-start | bytes 1572872 | tf_op jit(solution)/shard_map/cond/branch_0_fun/ppermute | solution.py:383
  46.6 5.0 %collective-permute-start.5 = (bf16[32,2048]{1,0:T(8,128)(2,1)S(1)}, bf16[32,2048]{1,0:T(8,128)(2,1)S(1)}, u32[]{:S(2)}, u32[]{:S(2)}) collective-permute-start(bf16[32,2048]{1,0:T(8,128)(2,1)S(1)} %get-tuple-element.55), channel_id=1, source_target_pairs={{0,8},{8,0},{16,24},{24,16},{1,9},{9,1},{17,25},{25,17},{2,10},{10... | collective-permute-start | bytes 393224 | tf_op jit(solution)/shard_map/cond/branch_0_fun/ppermute | solution.py:374
  47.8 5.0 %collective-permute-start.6 = (bf16[32,2048]{1,0:T(8,128)(2,1)S(1)}, bf16[32,2048]{1,0:T(8,128)(2,1)S(1)}, u32[]{:S(2)}, u32[]{:S(2)}) collective-permute-start(bf16[32,2048]{1,0:T(8,128)(2,1)S(1)} %get-tuple-element.56), channel_id=1, source_target_pairs={{0,16},{8,24},{16,0},{24,8},{1,17},{9,25},{17,1},{25,9},{2,18},{10... | collective-permute-start | bytes 393224 | tf_op jit(solution)/shard_map/cond/branch_0_fun/ppermute | solution.py:374
  48.8 5.9 %collective-permute-start.7 = (bf16[32,2048]{1,0:T(8,128)(2,1)S(1)}, bf16[32,2048]{1,0:T(8,128)(2,1)S(1)}, u32[]{:S(2)}, u32[]{:S(2)}) collective-permute-start(bf16[32,2048]{1,0:T(8,128)(2,1)S(1)} %get-tuple-element.57), channel_id=1, source_target_pairs={{0,24},{8,16},{16,8},{24,0},{1,25},{9,17},{17,9},{25,1},{2,26},{10... | collective-permute-start | bytes 393224 | tf_op jit(solution)/shard_map/cond/branch_0_fun/ppermute | solution.py:374

commit v7 on v6

--- a/solution.py
+++ b/solution.py
@@ -27,60 +27,69 @@
     return value * lax.rsqrt(jnp.mean(value * value, axis=-1, keepdims=True) + 1e-06)
 
 
-def normalize_kernel(x_hbm, wanted_hbm, out_ref, wanted_ref, raw, sems):
-    copies = [pltpu.make_async_copy(wanted_hbm, wanted_ref, sems.at[0])]
+def normalize_kernel(x_hbm, out_ref, raw, sems):
+    copies = []
     starts = range(0, raw.shape[0], BLOCK)
     for i, start in enumerate(starts):
         here = pl.ds(start, BLOCK)
-        copies.append(pltpu.make_async_copy(x_hbm.at[here], raw.at[here], sems.at[i + 1]))
-    for copy in copies:
-        copy.start()
-    for copy, start in zip(copies[1:], starts):
+        copies.append(pltpu.make_async_copy(x_hbm.at[here], raw.at[here], sems.at[i]))
+        copies[-1].start()
+    for copy, start in zip(copies, starts):
         copy.wait()
         here = pl.ds(start, BLOCK)
         out_ref[here] = normalize(raw[here].astype(jnp.float32)).astype(jnp.bfloat16)
-    copies[0].wait()
-
-
-def normalize_call(descriptors, wanted):
+
+
+def normalize_call(descriptors):
     rows, width = descriptors.shape
     return pl.pallas_call(
         normalize_kernel,
-        in_specs=[pl.BlockSpec(memory_space=pl.ANY)] * 2,
-        out_shape=[bf16(rows, width), pltpu.VMEM(wanted.shape, jnp.int32)],
+        in_specs=[pl.BlockSpec(memory_space=pl.ANY)],
+        out_shape=bf16(rows, width),
         scratch_shapes=[
             pltpu.VMEM((rows, width), jnp.bfloat16),
-            pltpu.SemaphoreType.DMA((rows // BLOCK + 1,)),
+            pltpu.SemaphoreType.DMA((rows // BLOCK,)),
         ],
         compiler_params=params(56),
         cost_estimate=pl.CostEstimate(
             flops=6 * rows * width, bytes_accessed=4 * rows * width, transcendentals=rows
         ),
         name="normalize",
-    )(descriptors, wanted)
-
-
-def mask_kernel(slot_cap, pick_ref, mask_ref):
+    )(descriptors)
+
+
+def mask_kernel(slot_cap, pick_hbm, wanted_hbm, mask_ref, wanted_ref, pick, sems):
+    copies = [
+        pltpu.make_async_copy(pick_hbm, pick, sems.at[0]),
+        pltpu.make_async_copy(wanted_hbm, wanted_ref, sems.at[1]),
+    ]
+    for copy in copies:
+        copy.start()
     shape = mask_ref.shape[1], mask_ref.shape[0]
     slot = lax.broadcasted_iota(jnp.int32, shape, 0)
     slot = slot ^ (lax.axis_index("clus") * slot_cap)
     chosen = jnp.zeros(shape, jnp.float32)
-    for k in range(pick_ref.shape[0]):
-        chosen = jnp.where(pick_ref[k] == slot, 1.0, chosen)
+    copies[0].wait()
+    for k in range(pick.shape[0]):
+        chosen = jnp.where(pick[k] == slot, 1.0, chosen)
     mask_ref[...] = chosen.T.astype(jnp.bfloat16)
-
-
-def mask_call(slots, total, slot_cap):
+    copies[1].wait()
+
+
+def mask_call(slots, wanted):
     count, _, rows = slots.shape
-    return pl.pallas_call(
-        functools.partial(mask_kernel, slot_cap),
-        out_shape=bf16(rows, total),
-        compiler_params=params(),
+    total = wanted.size
+    return pl.pallas_call(
+        functools.partial(mask_kernel, wanted.shape[1]),
+        in_specs=[pl.BlockSpec(memory_space=pl.ANY)] * 2,
+        out_shape=[bf16(rows, total), pltpu.VMEM(wanted.shape, jnp.int32)],
+        scratch_shapes=[pltpu.VMEM(slots.shape, jnp.int32), pltpu.SemaphoreType.DMA((2,))],
+        compiler_params=params(56),
         cost_estimate=pl.CostEstimate(
             flops=2 * count * rows * total, bytes_accessed=2 * rows * total, transcendentals=0
         ),
         name="mask",
-    )(slots)
+    )(slots, wanted)
 
 
 def list_kernel(rows, *refs):
@@ -158,33 +167,37 @@
     return jnp.where(place == rank[0:1], 1.0, 0.0).astype(jnp.bfloat16)
 
 
-def far_kernel(x_ref, beyond_ref, pack_ref, far_ref):
+def far_kernel(x_ref, mine_ref, within_ref, beyond_ref, pack_ref, most_ref, far_ref):
     rows = x_ref.shape[0]
+    most = jnp.maximum(mine_ref[...], jnp.maximum(within_ref[...], beyond_ref[...]))
+    most_ref[...] = jnp.broadcast_to(most[1:2, :LANES], most_ref.shape)
     third = 2 - lax.axis_index("rep") % 2 * 2
     pack_ref[...] = packing(one_hot(beyond_ref[0:1], third, rows), rows)
     serve(x_ref[...], pack_ref, far_ref)
 
 
-def far_call(x, beyond, sent):
+def far_call(x, mine, within, beyond, sent):
     rows, width = x.shape
-    total = beyond.shape[1]
+    total = mine.shape[1]
     return pl.pallas_call(
         far_kernel,
-        out_shape=[bf16(total, rows), bf16(sent, width)],
+        out_shape=[
+            bf16(total, rows),
+            jax.ShapeDtypeStruct((8, LANES), jnp.int32),
+            bf16(sent, width),
+        ],
         compiler_params=params(),
         cost_estimate=pl.CostEstimate(
             flops=2 * rows * rows * LANES, bytes_accessed=2 * rows * width, transcendentals=0
         ),
         name="pack_far",
-    )(x, beyond)
-
-
-def near_kernel(x_ref, pack_ref, mine_ref, within_ref, beyond_ref, *out_refs):
-    select_ref, expand_ref, most_ref, core_ref, own_ref, rest_ref = out_refs
+    )(x, mine, within, beyond)
+
+
+def near_kernel(x_ref, pack_ref, mine_ref, within_ref, *out_refs):
+    select_ref, expand_ref, core_ref, own_ref, rest_ref = out_refs
     rows, total = x_ref.shape[0], mine_ref.shape[1]
     third = lax.axis_index("rep") % 2 * 2
-    most = jnp.maximum(mine_ref[...], jnp.maximum(within_ref[...], beyond_ref[...]))
-    most_ref[...] = jnp.broadcast_to(most[1:2, :LANES], most_ref.shape)
     own = mine_ref[0:1]
     select_ref[:total] = one_hot(within_ref[0:1], third, rows).astype(jnp.bfloat16)
     select_ref[total:] = one_hot(own, 1, rows).astype(jnp.bfloat16)
@@ -201,7 +214,7 @@
     ).astype(jnp.bfloat16)
 
 
-def near_call(x, pack, mine, within, beyond, sent):
+def near_call(x, pack, mine, within, sent):
     rows, width = x.shape
     total = mine.shape[1]
     return pl.pallas_call(
@@ -209,7 +222,6 @@
         out_shape=[
             bf16(2 * total, rows),
             bf16(total, total),
-            jax.ShapeDtypeStruct((8, LANES), jnp.int32),
             bf16(total, width),
             bf16(total, width),
             bf16(total - sent, width),
@@ -219,7 +231,7 @@
             flops=6 * total * rows * width, bytes_accessed=4 * rows * width, transcendentals=0
         ),
         name="serve_near",
-    )(x, pack, mine, within, beyond)
+    )(x, pack, mine, within)
 
 
 def again_kernel(x_ref, select_ref, core_ref, own_ref):
@@ -240,47 +252,52 @@
     )(x, select)
 
 
-def unpack_kernel(first, expand_ref, far_ref, base_ref, out_ref):
-    sent = far_ref.shape[0]
-    far = jnp.dot(
+def unpack_kernel(first, expand_ref, far_ref, *refs):
+    out_ref, sent = refs[-1], far_ref.shape[0]
+    rows = jnp.dot(
         expand_ref[:, first : first + sent], far_ref[...], preferred_element_type=jnp.float32
     )
-    out_ref[...] = (far + base_ref[...].astype(jnp.float32)).astype(jnp.bfloat16)
-
-
-def unpack_call(expand, far, base, first=0):
+    for base_ref in refs[:-1]:
+        rows += base_ref[...].astype(jnp.float32)
+    out_ref[...] = rows.astype(jnp.bfloat16)
+
+
+def unpack_call(expand, far, *base, first=0):
     return pl.pallas_call(
         functools.partial(unpack_kernel, first),
-        out_shape=bf16(*base.shape),
+        out_shape=bf16(expand.shape[0], far.shape[1]),
         compiler_params=params(),
         cost_estimate=pl.CostEstimate(flops=2**34, bytes_accessed=2**25, transcendentals=0),
         name="unpack",
-    )(expand, far, base)
-
-
-def combine_kernel(base_ref, core_ref, *out_refs):
+    )(expand, far, *base)
+
+
+def combine_kernel(base_ref, core_ref, most_ref, out_most_ref, *out_refs):
     cap = out_refs[0].shape[0]
+    out_most_ref[...] = most_ref[...]
     for d, out in enumerate(out_refs):
         here = slice(d * cap, (d + 1) * cap)
         out[...] = base_ref[here] + core_ref[here]
 
 
-def combine_call(base, core, servers):
+def combine_call(base, core, most, servers):
     total, width = base.shape
-    return pl.pallas_call(
+    most, *parts = pl.pallas_call(
         combine_kernel,
-        out_shape=[bf16(total // servers, width)] * servers,
+        out_shape=[jax.ShapeDtypeStruct(most.shape, most.dtype)]
+        + [bf16(total // servers, width)] * servers,
         compiler_params=params(),
         cost_estimate=pl.CostEstimate(
             flops=total * width, bytes_accessed=6 * total * width, transcendentals=0
         ),
         name="combine",
-    )(base, core)
+    )(base, core, most)
+    return most, parts
 
 
 def fill(buffer, parts):
     cap = parts[0].shape[0]
-    for d, ref in enumerate(parts):
+    for d, ref in enumerate(reversed(parts)):
         buffer[d * cap : (d + 1) * cap] = ref[...]
 
 
@@ -328,12 +345,13 @@
             flops=4 * total * rows * width, bytes_accessed=4 * rows * width, transcendentals=rows
         ),
         name="mix",
-    )(x, mask, *parts)
+    )(x, mask, *reversed(parts))
 
 
 def round_kernel(servers, x_ref, mask_ref, pack_ref, *rest):
     parts, rest = rest[:servers], rest[servers:]
-    out_ref, far_ref, buffer, weights = rest
+    *most_refs, out_ref, far_ref, most_ref, buffer, weights = rest
+    most_ref[...] = functools.reduce(jnp.maximum, [ref[...] for ref in most_refs])
     fill(buffer, parts)
     weights[...] = weigh(x_ref[...], buffer[...], mask_ref[...])
     for start in range(0, x_ref.shape[0], BLOCK):
@@ -342,12 +360,16 @@
     serve(out_ref[...], pack_ref, far_ref)
 
 
-def round_call(x, mask, pack, parts, sent):
+def round_call(x, mask, pack, parts, mosts, sent):
     rows, width = x.shape
     total, servers = mask.shape[1], len(parts)
     return pl.pallas_call(
         functools.partial(round_kernel, servers),
-        out_shape=[bf16(rows, width), bf16(sent, width)],
+        out_shape=[
+            bf16(rows, width),
+            bf16(sent, width),
+            jax.ShapeDtypeStruct((8, LANES), jnp.int32),
+        ],
         scratch_shapes=[
             pltpu.VMEM((total, width), jnp.bfloat16),
             pltpu.VMEM((rows, total), jnp.bfloat16),
@@ -357,7 +379,7 @@
             flops=5 * total * rows * width, bytes_accessed=6 * rows * width, transcendentals=rows
         ),
         name="mix_and_pack",
-    )(x, mask, pack, *parts)
+    )(x, mask, pack, *reversed(parts), *mosts)
 
 
 def local(descriptors, request, pick):
@@ -382,49 +404,56 @@
     def inside(value):
         return lax.ppermute(value, "rep", within)
 
-    def exchange(base, core):
-        parts = combine_call(base, core, servers)
+    def exchange(base, core, most):
+        most, parts = combine_call(base, core, most, servers)
+        return most, turned(parts)
+
+    def turned(parts):
         got = {d: turn(parts[d], d) for d in reversed(range(1, servers))}
         return [parts[0]] + [got[d] for d in range(1, servers)]
 
-    def rounds(x, mask, pack, select, expand, count, base, core):
-        parts = exchange(base, core)
+    def next_parts(x, far, select, expand, most):
+        far = across(far)
+        core, own = again_call(x, select)
+        core = inside(core)
+        return exchange(unpack_call(expand, far, own), core, most)
+
+    def in_full(raw, x, rest, mask, pack, select, expand, most, first, last):
+        late = unpack_call(expand, across(rest), first=sent).reshape(servers, cap, -1)
+        parts = [a + b for a, b in zip(first, turned(list(late)))]
+        x = raw
         for _ in range(ROUNDS - 1):
-            x, far = round_call(x, mask, pack, parts, count)
-            far = across(far)
-            core, own = again_call(x, select)
-            core = inside(core)
-            parts = exchange(unpack_call(expand, far, own), core)
+            x, far, most = round_call(x, mask, pack, parts, [most], total)
+            most, parts = next_parts(x, far, select, expand, most)
         return last_call(x, mask, parts)
 
-    def in_full(x, mask, pack, select, expand, rest, base, core):
-        base = unpack_call(expand, across(rest), base, sent)
-        return rounds(x, mask, pack, select, expand, total, base, core)
-
-    def as_sent(x, mask, pack, select, expand, rest, base, core):
-        return rounds(x, mask, pack, select, expand, sent, base, core)
+    def as_sent(raw, x, rest, mask, pack, select, expand, most, first, last):
+        return last_call(x, mask, last)
 
     asked = {d: turn(wanted, d) for d in reversed(range(1, servers))}
-    x, held = normalize_call(descriptors[0, 0], wanted)
+    mask, held = mask_call(pick.transpose(0, 3, 1, 2)[0], wanted)
     mine = list_call([held] + [asked[d] for d in range(1, servers)], rows)
     beyond_list, within_list = across(mine), inside(mine)
-    pack, far = far_call(x, beyond_list, sent)
+    x = normalize_call(descriptors[0, 0])
+    pack, most, far = far_call(x, mine, within_list, beyond_list, sent)
     far = across(far)
-    select, expand, most, core, own, rest = near_call(
-        x, pack, mine, within_list, beyond_list, sent
-    )
+    select, expand, core, own, rest = near_call(x, pack, mine, within_list, sent)
     core = inside(core)
-    base = unpack_call(expand, far, own)
-    mask = mask_call(pick.transpose(0, 3, 1, 2)[0], total, cap)
+    most, first = exchange(unpack_call(expand, far, own), core, most)
+    mosts = [most]
     reach = 1
     while 2 * reach + 1 < groups:
         by = 2 * reach + 1
-        most = jnp.maximum(most, jnp.maximum(shift(most, by), shift(most, -by)))
+        most = functools.reduce(jnp.maximum, mosts)
+        mosts = [most, shift(most, by), shift(most, -by)]
         reach += by
-    out = lax.cond(
-        most[0, 0] > sent, in_full, as_sent, x, mask, pack, select, expand, rest, base, core
-    )
-    return out[None, None]
+    mixed, parts = x, first
+    for _ in range(ROUNDS - 1):
+        mixed, far, most = round_call(mixed, mask, pack, parts, mosts, sent)
+        most, parts = next_parts(mixed, far, select, expand, most)
+        mosts = [most]
+    state = x, mixed, rest, mask, pack, select, expand, most, first, parts
+    return lax.cond(most[0, 0] > sent, in_full, as_sent, *state)[None, None]
 
 
 def solution(mesh):

time: 58.5 us -> 53.2 us (0.909)
  waiting for transfers between devices: 26.4 us -> 20.5 us
  Pallas kernels: 12.3 us -> 13.1 us
    ppermute x9, waiting for transfers between devices: 10.8 us -> 5.69 us  [turn(): return lax.ppermute(value, 'clus', [(c, c ^ d) for c in range(servers)])]
    ppermute x3, waiting for transfers between devices: 15.5 us -> 12.6 us  [across(): return lax.ppermute(value, 'rep', beyond)]
    ppermute x2, waiting for transfers between devices: 0.14 us -> 2.19 us  [shift(): lax.ppermute(value, 'rep', [(g, (g + by) % groups) for g in range(groups)])]
    pallas_call x6, Pallas kernels: 1.63 us -> 2.38 us  [the longest x1 0.99 us: mask_call(): pl.pallas_call(functools.partial(mask_kernel, wanted.shape[1]), in_specs=...]
  transfers between devices with their start and end apart: 17 -> 17, of which waited for: 12 -> 11; matrix products, arithmetic and copies ran while one was open for 1% -> 1% of each run, Pallas kernels for 7% -> 11%
where the time goes in v7:
time: 53.2 us; the launch traced here: 53 us
  waiting for transfers between devices  20.5 us (39%)
  starting transfers between devices  17.8 us (33%)
  Pallas kernels  13.1 us (25%)
  between operations  0.93 us (2%)
    ppermute x3, waiting for transfers between devices, across(): return lax.ppermute(value, 'rep', beyond)  12.6 us
    ppermute x9, starting transfers between devices, turn(): return lax.ppermute(value, 'clus', [(c, c ^ d) for c in range(servers)])  11.6 us
    ppermute x9, waiting for transfers between devices, turn(): return lax.ppermute(value, 'clus', [(c, c ^ d) for c in range(servers)])  5.69 us
    ppermute x3, starting transfers between devices, across(): return lax.ppermute(value, 'rep', beyond)  3.95 us
    pallas_call x1, Pallas kernels, last_call(): pl.pallas_call(functools.partial(last_kernel, servers), out_specs=pl.Bloc...  3.37 us
    pallas_call x1, Pallas kernels, round_call(): pl.pallas_call(functools.partial(round_kernel, servers), out_shape=[bf16(...  3.01 us
    ppermute x2, waiting for transfers between devices, shift(): lax.ppermute(value, 'rep', [(g, (g + by) % groups) for g in range(groups)])  2.19 us
    pallas_call x1, Pallas kernels, normalize_call(): pl.pallas_call(normalize_kernel, in_specs=[pl.BlockSpec(memory_space=pl.A...  1.87 us
  transfers between devices with their start and end apart: 17, of which 11 were waited for; matrix products, arithmetic and copies ran while one was open for 1% of the time, Pallas kernels for 11%

profile of v7, /device:TPU:0, one launch (start us, length us, event | category | flops | bytes accessed | tf_op | source)
XLA Modules:
  0.0 53.0 jit_solution(8162271861809902730)
XLA Ops:
  0.0 3.9 %collective-permute-start.11 = (s32[4,32]{1,0:T(4,128)}, s32[4,32]{1,0:T(4,128)S(1)}, u32[]{:S(2)}, u32[]{:S(2)}) collective-permute-start(s32[4,32]{1,0:T(4,128)} %bitcast.12), channel_id=1, source_target_pairs={{0,24},{8,16},{16,8},{24,0},{1,25},{9,17},{17,9},{25,1},{2,26},{10... | collective-permute-start | bytes 1544 | tf_op jit(solution)/shard_map/ppermute | solution.py:396
  3.9 0.5 collective-permute-start.10
  4.4 0.1 collective-permute-start.9
  4.5 1.0 %mask.1 = (bf16[512,128]{1,0:T(8,128)(2,1)S(1)}, s32[4,32]{1,0:T(4,128)S(1)}) custom-call(s32[10,1,512]{2,1,0:T(1,128)} %bitcast.11, s32[4,32]{1,0:T(4,128)} %bitcast.15), custom_call_target="tpu_custom_call" | custom-call | flops 1310720 | bytes 131072 | tf_op jit(solution)/shard_map/mask/pallas_call | solution.py:82
  5.5 0.2 collective-permute-done.11.refs_3_
  5.7 2.0 %collective-permute-done.10.refs_2_ = s32[4,32]{1,0:T(4,128)S(1)} collective-permute-done((s32[4,32]{1,0:T(4,128)}, s32[4,32]{1,0:T(4,128)S(1)}, u32[]{:S(2)}, u32[]{:S(2)}) %collective-permute-start.10) | collective-permute-done | bytes 544 | tf_op jit(solution)/shard_map/ppermute | solution.py:396
  7.7 0.5 collective-permute-done.9.refs_1_
  8.2 0.3 list.1.mine_ref
  8.5 1.3 %collective-permute-start.13 = (s32[8,128]{1,0:T(8,128)S(1)}, s32[8,128]{1,0:T(8,128)S(1)}, u32[]{:S(2)}, u32[]{:S(2)}) collective-permute-start(s32[8,128]{1,0:T(8,128)S(1)} %list.1.mine_ref), channel_id=1, source_target_pairs={{0,7},{1,2},{2,1},{3,4},{4,3},{5,6},{6,5},{7,0},{8,15},{9,10},{10,... | collective-permute-start | bytes 12296 | tf_op jit(solution)/shard_map/ppermute | solution.py:402
  9.9 0.4 collective-permute-start.12
  10.2 1.9 %normalize.1.x_ref = bf16[512,2048]{1,0:T(8,128)(2,1)S(1)} custom-call(bf16[512,2048]{1,0:T(8,128)(2,1)} %bitcast.10), custom_call_target="tpu_custom_call" | custom-call | flops 6291456 | bytes 4194304 | tf_op jit(solution)/shard_map/normalize/pallas_call | solution.py:45
  12.1 1.3 %collective-permute-done.13.beyond_ref = s32[8,128]{1,0:T(8,128)S(1)} collective-permute-done((s32[8,128]{1,0:T(8,128)S(1)}, s32[8,128]{1,0:T(8,128)S(1)}, u32[]{:S(2)}, u32[]{:S(2)}) %collective-permute-start.13) | collective-permute-done | bytes 4128 | tf_op jit(solution)/shard_map/ppermute | solution.py:402
  13.4 0.0 collective-permute-done.12.within_ref
  13.4 0.7 %pack_far.1 = (bf16[128,512]{1,0:T(8,128)(2,1)S(1)}, s32[8,128]{1,0:T(8,128)S(1)}, bf16[48,2048]{1,0:T(8,128)(2,1)S(1)}) custom-call(bf16[512,2048]{1,0:T(8,128)(2,1)S(1)} %normalize.1.x_ref, s32[8,128]{1,0:T(8,128)S(1)} %list.1.mine_ref, s32[8,128]{1,0:T(8,128)S(1)} %collective-permute-done.12.within_ref, s32[8,128]{1,0:T(8,128)S(1)} %collective-permute-done.13.beyond_ref), custom_call_target="tpu_custom_call" | custom-call | flops 67108864 | bytes 2097152 | tf_op jit(solution)/shard_map/pack_far/pallas_call | solution.py:182
  14.1 1.4 %collective-permute-start.14 = (bf16[48,2048]{1,0:T(8,128)(2,1)S(1)}, bf16[48,2048]{1,0:T(8,128)(2,1)S(1)}, u32[]{:S(2)}, u32[]{:S(2)}) collective-permute-start(bf16[48,2048]{1,0:T(8,128)(2,1)S(1)} %get-tuple-element.98), channel_id=1, source_target_pairs={{0,7},{1,2},{2,1},{3,4},{4,3},{5,6},{6,5},{7,0},{8,15},{9,10},{10,... | collective-permute-start | bytes 589832 | tf_op jit(solution)/shard_map/ppermute | solution.py:402
  15.5 1.4 %serve_near.1 = (bf16[256,512]{1,0:T(8,128)(2,1)S(1)}, bf16[128,128]{1,0:T(8,128)(2,1)S(1)}, bf16[128,2048]{1,0:T(8,128)(2,1)S(1)}, bf16[128,2048]{1,0:T(8,128)(2,1)S(1)}, bf16[80,2048]{1,0:T(8,128)(2,1)S(1)}) custom-call(bf16[512,2048]{1,0:T(8,128)(2,1)S(1)} %normalize.1.x_ref, bf16[128,512]{1,0:T(8,128)(2,1)S(1)} %get-tuple-element.95.pack_ref, ...), custom_call_target="tpu_custom_call" | custom-call | flops 805306368 | bytes 4194304 | tf_op jit(solution)/shard_map/serve_near/pallas_call | solution.py:220
  16.9 0.1 collective-permute-start.15
  17.0 5.3 %collective-permute-done.14.far_ref = bf16[48,2048]{1,0:T(8,128)(2,1)S(1)} collective-permute-done((bf16[48,2048]{1,0:T(8,128)(2,1)S(1)}, bf16[48,2048]{1,0:T(8,128)(2,1)S(1)}, u32[]{:S(2)}, u32[]{:S(2)}) %collective-permute-start.14) | collective-permute-done | bytes 196640 | tf_op jit(solution)/shard_map/ppermute | solution.py:402
  22.3 0.3 unpack.6.base_ref
  22.6 0.0 collective-permute-done.15.core_ref
  22.6 0.1 combine.4
  22.7 1.6 %collective-permute-start.16 = (bf16[32,2048]{1,0:T(8,128)(2,1)S(1)}, bf16[32,2048]{1,0:T(8,128)(2,1)S(1)}, u32[]{:S(2)}, u32[]{:S(2)}) collective-permute-start(bf16[32,2048]{1,0:T(8,128)(2,1)S(1)} %get-tuple-element.102), channel_id=1, source_target_pairs={{0,24},{8,16},{16,8},{24,0},{1,25},{9,17},{17,9},{25,1},{2,26},{10... | collective-permute-start | bytes 393224 | tf_op jit(solution)/shard_map/ppermute | solution.py:396
  24.2 0.5 collective-permute-start.17
  24.7 1.5 %collective-permute-start.18 = (bf16[32,2048]{1,0:T(8,128)(2,1)S(1)}, bf16[32,2048]{1,0:T(8,128)(2,1)S(1)}, u32[]{:S(2)}, u32[]{:S(2)}) collective-permute-start(bf16[32,2048]{1,0:T(8,128)(2,1)S(1)} %get-tuple-element.104), channel_id=1, source_target_pairs={{0,8},{8,0},{16,24},{24,16},{1,9},{9,1},{17,25},{25,17},{2,10},{10... | collective-permute-start | bytes 393224 | tf_op jit(solution)/shard_map/ppermute | solution.py:396
  26.2 0.0 collective-permute-start.20
  26.2 1.7 %collective-permute-start.19 = (s32[8,128]{1,0:T(8,128)S(1)}, s32[8,128]{1,0:T(8,128)S(1)}, u32[]{:S(2)}, u32[]{:S(2)}) collective-permute-start(s32[8,128]{1,0:T(8,128)S(1)} %get-tuple-element.106.rest_4_), channel_id=1, source_target_pairs={{0,3},{1,4},{2,5},{3,6},{4,7},{5,0},{6,1},{7,2},{8,11},{9,12},{10,... | collective-permute-start | bytes 12296 | tf_op jit(solution)/shard_map/ppermute | solution.py:399
  28.0 1.3 %collective-permute-done.20.rest_6_ = s32[8,128]{1,0:T(8,128)S(1)} collective-permute-done((s32[8,128]{1,0:T(8,128)S(1)}, s32[8,128]{1,0:T(8,128)S(1)}, u32[]{:S(2)}, u32[]{:S(2)}) %collective-permute-start.20) | collective-permute-done | bytes 4128 | tf_op jit(solution)/shard_map/ppermute | solution.py:399
  29.2 0.9 %collective-permute-done.19.rest_5_ = s32[8,128]{1,0:T(8,128)S(1)} collective-permute-done((s32[8,128]{1,0:T(8,128)S(1)}, s32[8,128]{1,0:T(8,128)S(1)}, u32[]{:S(2)}, u32[]{:S(2)}) %collective-permute-start.19) | collective-permute-done | bytes 4128 | tf_op jit(solution)/shard_map/ppermute | solution.py:399
  30.1 0.0 collective-permute-done.16.rest_0_
  30.1 0.0 collective-permute-done.17.rest_1_
  30.2 0.0 collective-permute-done.18.rest_2_
  30.2 3.0 %mix_and_pack.3 = (bf16[512,2048]{1,0:T(8,128)(2,1)S(1)}, bf16[48,2048]{1,0:T(8,128)(2,1)S(1)}, s32[8,128]{1,0:T(8,128)S(1)}) custom-call(bf16[512,2048]{1,0:T(8,128)(2,1)S(1)} %normalize.1.x_ref, bf16[512,128]{1,0:T(8,128)(2,1)S(1)} %get-tuple-element.97.mask_ref, bf16[128,512]{1,0:T(8,128)(2,1)S(1)} %get-tuple-element.95.pack_ref, ...), custom_call_target="tpu_custom_call" | custom-call | flops 671088640 | bytes 6291456 | tf_op jit(solution)/shard_map/mix_and_pack/pallas_call | solution.py:366
  33.2 1.2 %collective-permute-start.21 = (bf16[48,2048]{1,0:T(8,128)(2,1)S(1)}, bf16[48,2048]{1,0:T(8,128)(2,1)S(1)}, u32[]{:S(2)}, u32[]{:S(2)}) collective-permute-start(bf16[48,2048]{1,0:T(8,128)(2,1)S(1)} %get-tuple-element.107), channel_id=1, source_target_pairs={{0,7},{1,2},{2,1},{3,4},{4,3},{5,6},{6,5},{7,0},{8,15},{9,10},{10,... | collective-permute-start | bytes 589832 | tf_op jit(solution)/shard_map/ppermute | solution.py:402
  34.4 0.7 %serve_again.3 = (bf16[128,2048]{1,0:T(8,128)(2,1)S(1)}, bf16[128,2048]{1,0:T(8,128)(2,1)S(1)}) custom-call(bf16[512,2048]{1,0:T(8,128)(2,1)S(1)} %get-tuple-element.108.x_ref, bf16[256,512]{1,0:T(8,128)(2,1)S(1)} %get-tuple-element.109.select_ref), custom_call_target="tpu_custom_call" | custom-call | flops 536870912 | bytes 4194304 | tf_op jit(solution)/shard_map/serve_again/pallas_call | solution.py:244
  35.2 0.1 collective-permute-start.22
  35.2 6.1 %collective-permute-done.21.far_ref = bf16[48,2048]{1,0:T(8,128)(2,1)S(1)} collective-permute-done((bf16[48,2048]{1,0:T(8,128)(2,1)S(1)}, bf16[48,2048]{1,0:T(8,128)(2,1)S(1)}, u32[]{:S(2)}, u32[]{:S(2)}) %collective-permute-start.21) | collective-permute-done | bytes 196640 | tf_op jit(solution)/shard_map/ppermute | solution.py:402
  41.3 0.3 unpack.7.base_ref
  41.6 0.0 collective-permute-done.22.core_ref
  41.6 0.1 combine.5
  41.7 1.5 %collective-permute-start.23 = (bf16[32,2048]{1,0:T(8,128)(2,1)S(1)}, bf16[32,2048]{1,0:T(8,128)(2,1)S(1)}, u32[]{:S(2)}, u32[]{:S(2)}) collective-permute-start(bf16[32,2048]{1,0:T(8,128)(2,1)S(1)} %get-tuple-element.114), channel_id=1, source_target_pairs={{0,24},{8,16},{16,8},{24,0},{1,25},{9,17},{17,9},{25,1},{2,26},{10... | collective-permute-start | bytes 393224 | tf_op jit(solution)/shard_map/ppermute | solution.py:396
  43.2 1.1 %collective-permute-start.24 = (bf16[32,2048]{1,0:T(8,128)(2,1)S(1)}, bf16[32,2048]{1,0:T(8,128)(2,1)S(1)}, u32[]{:S(2)}, u32[]{:S(2)}) collective-permute-start(bf16[32,2048]{1,0:T(8,128)(2,1)S(1)} %get-tuple-element.115), channel_id=1, source_target_pairs={{0,16},{8,24},{16,0},{24,8},{1,17},{9,25},{17,1},{25,9},{2,18},{10... | collective-permute-start | bytes 393224 | tf_op jit(solution)/shard_map/ppermute | solution.py:396
  44.4 0.9 %collective-permute-start.25 = (bf16[32,2048]{1,0:T(8,128)(2,1)S(1)}, bf16[32,2048]{1,0:T(8,128)(2,1)S(1)}, u32[]{:S(2)}, u32[]{:S(2)}) collective-permute-start(bf16[32,2048]{1,0:T(8,128)(2,1)S(1)} %get-tuple-element.116), channel_id=1, source_target_pairs={{0,8},{8,0},{16,24},{24,16},{1,9},{9,1},{17,25},{25,17},{2,10},{10... | collective-permute-start | bytes 393224 | tf_op jit(solution)/shard_map/ppermute | solution.py:396
  45.2 0.5 slice.7
  46.4 1.3 %collective-permute-done.23 = bf16[32,2048]{1,0:T(8,128)(2,1)S(1)} collective-permute-done((bf16[32,2048]{1,0:T(8,128)(2,1)S(1)}, bf16[32,2048]{1,0:T(8,128)(2,1)S(1)}, u32[]{:S(2)}, u32[]{:S(2)}) %collective-permute-start.23) | collective-permute-done | bytes 131104 | tf_op jit(solution)/shard_map/ppermute | solution.py:396
  47.7 1.3 %collective-permute-done.24 = bf16[32,2048]{1,0:T(8,128)(2,1)S(1)} collective-permute-done((bf16[32,2048]{1,0:T(8,128)(2,1)S(1)}, bf16[32,2048]{1,0:T(8,128)(2,1)S(1)}, u32[]{:S(2)}, u32[]{:S(2)}) %collective-permute-start.24) | collective-permute-done | bytes 131104 | tf_op jit(solution)/shard_map/ppermute | solution.py:396
  49.0 0.3 collective-permute-done.25
  49.3 3.6 %conditional.1 = (bf16[1,1,512,2048]{3,2,1,0:T(8,128)(2,1)}) conditional(s32[]{:T(128)} %bitcast.6, (bf16[512,2048]{1,0:T(8,128)(2,1)S(1)}, bf16[512,128]{1,0:T(8,128)(2,1)S(1)}, bf16[32,2048]{1,0:T(8,128)(2,1)S(1)}, bf16[32,2048]{1,0:T(8,128)(2,1)S(1)}, bf16[32,2048]{1,0:T(8,128)(2,1)S(1)}, /*index=5*/bf16[32,2048]{1,0:T(8,128)(2,1)S(1)}) %tuple.13, ...), branch_computations={%region_0.0_spmd, %region_1.0_spmd} | conditional | flops 36105093120 | bytes 94372208 | solution.py:456
  49.3 3.4 %mix.2 = bf16[512,2048]{1,0:T(8,128)(2,1)} custom-call(bf16[512,2048]{1,0:T(8,128)(2,1)S(1)} %get-tuple-element.43.x_ref, bf16[512,128]{1,0:T(8,128)(2,1)S(1)} %get-tuple-element.44.mask_ref, bf16[32,2048]{1,0:T(8,128)(2,1)S(1)} %get-tuple-element.45.rest_0_, bf16[32,2048]{1,0:T(8,128)(2,1)S(1)} %get-tuple-element.46.rest_1_, ...), custom_call_target="tpu_custom_call" | custom-call | flops 536870912 | bytes 4194304 | tf_op jit(solution)/shard_map/cond/branch_0_fun/mix/pallas_call | solution.py:333
Async XLA Ops:
  0.0 5.7 %collective-permute-start.11 = (s32[4,32]{1,0:T(4,128)}, s32[4,32]{1,0:T(4,128)S(1)}, u32[]{:S(2)}, u32[]{:S(2)}) collective-permute-start(s32[4,32]{1,0:T(4,128)} %bitcast.12), channel_id=1, source_target_pairs={{0,24},{8,16},{16,8},{24,0},{1,25},{9,17},{17,9},{25,1},{2,26},{10... | collective-permute-start | bytes 1544 | tf_op jit(solution)/shard_map/ppermute | solution.py:396
  3.9 3.8 %collective-permute-start.10 = (s32[4,32]{1,0:T(4,128)}, s32[4,32]{1,0:T(4,128)S(1)}, u32[]{:S(2)}, u32[]{:S(2)}) collective-permute-start(s32[4,32]{1,0:T(4,128)} %bitcast.13), channel_id=1, source_target_pairs={{0,16},{8,24},{16,0},{24,8},{1,17},{9,25},{17,1},{25,9},{2,18},{10... | collective-permute-start | bytes 1544 | tf_op jit(solution)/shard_map/ppermute | solution.py:396
  4.4 3.8 %collective-permute-start.9 = (s32[4,32]{1,0:T(4,128)}, s32[4,32]{1,0:T(4,128)S(1)}, u32[]{:S(2)}, u32[]{:S(2)}) collective-permute-start(s32[4,32]{1,0:T(4,128)} %bitcast.14), channel_id=1, source_target_pairs={{0,8},{8,0},{16,24},{24,16},{1,9},{9,1},{17,25},{25,17},{2,10},{10... | collective-permute-start | bytes 1544 | tf_op jit(solution)/shard_map/ppermute | solution.py:396
  8.5 4.8 %collective-permute-start.13 = (s32[8,128]{1,0:T(8,128)S(1)}, s32[8,128]{1,0:T(8,128)S(1)}, u32[]{:S(2)}, u32[]{:S(2)}) collective-permute-start(s32[8,128]{1,0:T(8,128)S(1)} %list.1.mine_ref), channel_id=1, source_target_pairs={{0,7},{1,2},{2,1},{3,4},{4,3},{5,6},{6,5},{7,0},{8,15},{9,10},{10,... | collective-permute-start | bytes 12296 | tf_op jit(solution)/shard_map/ppermute | solution.py:402
  9.9 3.5 %collective-permute-start.12 = (s32[8,128]{1,0:T(8,128)S(1)}, s32[8,128]{1,0:T(8,128)S(1)}, u32[]{:S(2)}, u32[]{:S(2)}) collective-permute-start(s32[8,128]{1,0:T(8,128)S(1)} %list.1.mine_ref), channel_id=1, source_target_pairs={{0,1},{1,0},{2,3},{3,2},{4,5},{5,4},{6,7},{7,6},{8,9},{9,8},{10,11... | collective-permute-start | bytes 12296 | tf_op jit(solution)/shard_map/ppermute | solution.py:405
  14.1 8.2 %collective-permute-start.14 = (bf16[48,2048]{1,0:T(8,128)(2,1)S(1)}, bf16[48,2048]{1,0:T(8,128)(2,1)S(1)}, u32[]{:S(2)}, u32[]{:S(2)}) collective-permute-start(bf16[48,2048]{1,0:T(8,128)(2,1)S(1)} %get-tuple-element.98), channel_id=1, source_target_pairs={{0,7},{1,2},{2,1},{3,4},{4,3},{5,6},{6,5},{7,0},{8,15},{9,10},{10,... | collective-permute-start | bytes 589832 | tf_op jit(solution)/shard_map/ppermute | solution.py:402
  16.9 5.7 %collective-permute-start.15 = (bf16[128,2048]{1,0:T(8,128)(2,1)S(1)}, bf16[128,2048]{1,0:T(8,128)(2,1)S(1)}, u32[]{:S(2)}, u32[]{:S(2)}) collective-permute-start(bf16[128,2048]{1,0:T(8,128)(2,1)S(1)} %get-tuple-element.100), channel_id=1, source_target_pairs={{0,1},{1,0},{2,3},{3,2},{4,5},{5,4},{6,7},{7,6},{8,9},{9,8},{10,11... | collective-permute-start | bytes 1572872 | tf_op jit(solution)/shard_map/ppermute | solution.py:405
  22.7 7.5 %collective-permute-start.16 = (bf16[32,2048]{1,0:T(8,128)(2,1)S(1)}, bf16[32,2048]{1,0:T(8,128)(2,1)S(1)}, u32[]{:S(2)}, u32[]{:S(2)}) collective-permute-start(bf16[32,2048]{1,0:T(8,128)(2,1)S(1)} %get-tuple-element.102), channel_id=1, source_target_pairs={{0,24},{8,16},{16,8},{24,0},{1,25},{9,17},{17,9},{25,1},{2,26},{10... | collective-permute-start | bytes 393224 | tf_op jit(solution)/shard_map/ppermute | solution.py:396
  24.2 5.9 %collective-permute-start.17 = (bf16[32,2048]{1,0:T(8,128)(2,1)S(1)}, bf16[32,2048]{1,0:T(8,128)(2,1)S(1)}, u32[]{:S(2)}, u32[]{:S(2)}) collective-permute-start(bf16[32,2048]{1,0:T(8,128)(2,1)S(1)} %get-tuple-element.103), channel_id=1, source_target_pairs={{0,16},{8,24},{16,0},{24,8},{1,17},{9,25},{17,1},{25,9},{2,18},{10... | collective-permute-start | bytes 393224 | tf_op jit(solution)/shard_map/ppermute | solution.py:396
  24.7 5.4 %collective-permute-start.18 = (bf16[32,2048]{1,0:T(8,128)(2,1)S(1)}, bf16[32,2048]{1,0:T(8,128)(2,1)S(1)}, u32[]{:S(2)}, u32[]{:S(2)}) collective-permute-start(bf16[32,2048]{1,0:T(8,128)(2,1)S(1)} %get-tuple-element.104), channel_id=1, source_target_pairs={{0,8},{8,0},{16,24},{24,16},{1,9},{9,1},{17,25},{25,17},{2,10},{10... | collective-permute-start | bytes 393224 | tf_op jit(solution)/shard_map/ppermute | solution.py:396
  26.2 3.0 %collective-permute-start.20 = (s32[8,128]{1,0:T(8,128)S(1)}, s32[8,128]{1,0:T(8,128)S(1)}, u32[]{:S(2)}, u32[]{:S(2)}) collective-permute-start(s32[8,128]{1,0:T(8,128)S(1)} %get-tuple-element.106.rest_4_), channel_id=1, source_target_pairs={{0,5},{1,6},{2,7},{3,0},{4,1},{5,2},{6,3},{7,4},{8,13},{9,14},{10,... | collective-permute-start | bytes 12296 | tf_op jit(solution)/shard_map/ppermute | solution.py:399
  26.2 3.9 %collective-permute-start.19 = (s32[8,128]{1,0:T(8,128)S(1)}, s32[8,128]{1,0:T(8,128)S(1)}, u32[]{:S(2)}, u32[]{:S(2)}) collective-permute-start(s32[8,128]{1,0:T(8,128)S(1)} %get-tuple-element.106.rest_4_), channel_id=1, source_target_pairs={{0,3},{1,4},{2,5},{3,6},{4,7},{5,0},{6,1},{7,2},{8,11},{9,12},{10,... | collective-permute-start | bytes 12296 | tf_op jit(solution)/shard_map/ppermute | solution.py:399
  33.2 8.1 %collective-permute-start.21 = (bf16[48,2048]{1,0:T(8,128)(2,1)S(1)}, bf16[48,2048]{1,0:T(8,128)(2,1)S(1)}, u32[]{:S(2)}, u32[]{:S(2)}) collective-permute-start(bf16[48,2048]{1,0:T(8,128)(2,1)S(1)} %get-tuple-element.107), channel_id=1, source_target_pairs={{0,7},{1,2},{2,1},{3,4},{4,3},{5,6},{6,5},{7,0},{8,15},{9,10},{10,... | collective-permute-start | bytes 589832 | tf_op jit(solution)/shard_map/ppermute | solution.py:402
  35.2 6.4 %collective-permute-start.22 = (bf16[128,2048]{1,0:T(8,128)(2,1)S(1)}, bf16[128,2048]{1,0:T(8,128)(2,1)S(1)}, u32[]{:S(2)}, u32[]{:S(2)}) collective-permute-start(bf16[128,2048]{1,0:T(8,128)(2,1)S(1)} %get-tuple-element.111), channel_id=1, source_target_pairs={{0,1},{1,0},{2,3},{3,2},{4,5},{5,4},{6,7},{7,6},{8,9},{9,8},{10,11... | collective-permute-start | bytes 1572872 | tf_op jit(solution)/shard_map/ppermute | solution.py:405
  41.7 6.0 %collective-permute-start.23 = (bf16[32,2048]{1,0:T(8,128)(2,1)S(1)}, bf16[32,2048]{1,0:T(8,128)(2,1)S(1)}, u32[]{:S(2)}, u32[]{:S(2)}) collective-permute-start(bf16[32,2048]{1,0:T(8,128)(2,1)S(1)} %get-tuple-element.114), channel_id=1, source_target_pairs={{0,24},{8,16},{16,8},{24,0},{1,25},{9,17},{17,9},{25,1},{2,26},{10... | collective-permute-start | bytes 393224 | tf_op jit(solution)/shard_map/ppermute | solution.py:396
  43.2 5.8 %collective-permute-start.24 = (bf16[32,2048]{1,0:T(8,128)(2,1)S(1)}, bf16[32,2048]{1,0:T(8,128)(2,1)S(1)}, u32[]{:S(2)}, u32[]{:S(2)}) collective-permute-start(bf16[32,2048]{1,0:T(8,128)(2,1)S(1)} %get-tuple-element.115), channel_id=1, source_target_pairs={{0,16},{8,24},{16,0},{24,8},{1,17},{9,25},{17,1},{25,9},{2,18},{10... | collective-permute-start | bytes 393224 | tf_op jit(solution)/shard_map/ppermute | solution.py:396
  44.4 5.0 %collective-permute-start.25 = (bf16[32,2048]{1,0:T(8,128)(2,1)S(1)}, bf16[32,2048]{1,0:T(8,128)(2,1)S(1)}, u32[]{:S(2)}, u32[]{:S(2)}) collective-permute-start(bf16[32,2048]{1,0:T(8,128)(2,1)S(1)} %get-tuple-element.116), channel_id=1, source_target_pairs={{0,8},{8,0},{16,24},{24,16},{1,9},{9,1},{17,25},{25,17},{2,10},{10... | collective-permute-start | bytes 393224 | tf_op jit(solution)/shard_map/ppermute | solution.py:396

commit v8 on v7

--- a/solution.py
+++ b/solution.py
@@ -10,6 +10,7 @@
 ROUNDS = 2
 LANES = 128
 BLOCK = 128
+TILE = 256
 
 
 FAR_SHARE = 3, 8
@@ -301,27 +302,45 @@
         buffer[d * cap : (d + 1) * cap] = ref[...]
 
 
-def weigh(x, buffer, mask):
-    sims = lax.dot_general(x, buffer, (((1,), (1,)), ((), ())), preferred_element_type=jnp.float32)
-    positive = jnp.maximum(sims * (1.0 / x.shape[1]), 0.0)
-    return (positive * positive * positive).astype(jnp.bfloat16) * mask
-
-
-def add_up(x, weights, buffer):
+def weigh(x_ref, buffer, mask):
+    rows, width = x_ref.shape
+    across = (((1,), (1,)), ((), ()))
+    gram = lax.dot_general(buffer, buffer, across, preferred_element_type=jnp.float32)
+    high = gram.astype(jnp.bfloat16)
+    low = (gram - high.astype(jnp.float32)).astype(jnp.bfloat16)
+    dots = lax.dot_general(x_ref[...], buffer, across, preferred_element_type=jnp.float32)
+    positive = jnp.maximum(dots * (1.0 / width), 0.0)
+    weights = (positive * positive * positive).astype(jnp.bfloat16) * mask
+    crossed = jnp.dot(weights, high, preferred_element_type=jnp.float32)
+    crossed += jnp.dot(weights, low, preferred_element_type=jnp.float32)
+    squares = weights.astype(jnp.float32) * (2.0 * dots + crossed)
+    own = jnp.zeros((rows, LANES), jnp.float32)
+    for start in range(0, width, LANES):
+        tile = x_ref[:, start : start + LANES].astype(jnp.float32)
+        own += tile * tile
+    if squares.shape[1] == LANES:
+        total = jnp.sum(own + squares, axis=1, keepdims=True)
+    else:
+        total = jnp.sum(own, axis=1, keepdims=True) + jnp.sum(squares, axis=1, keepdims=True)
+    return weights, lax.rsqrt(total * (1.0 / width) + 1e-06)
+
+
+def add_up(x, weights, scale, buffer):
     mixed = x.astype(jnp.float32) + jnp.dot(weights, buffer, preferred_element_type=jnp.float32)
-    return normalize(mixed).astype(jnp.bfloat16)
+    return (mixed * scale).astype(jnp.bfloat16)
 
 
 def last_kernel(servers, x_ref, mask_ref, *rest):
     parts, rest = rest[:servers], rest[servers:]
-    out_ref, buffer, weights, whole, sems = rest
+    out_ref, buffer, whole, sems = rest
     fill(buffer, parts)
-    weights[...] = weigh(x_ref[...], buffer[...], mask_ref[...])
+    weights, scale = weigh(x_ref, buffer[...], mask_ref[...])
     copies = []
-    for i, start in enumerate(range(0, x_ref.shape[0], BLOCK)):
-        here = pl.ds(start, BLOCK)
-        whole[here] = add_up(x_ref[here], weights[here], buffer[...])
-        copies.append(pltpu.make_async_copy(whole.at[here], out_ref.at[here], sems.at[i]))
+    for i, start in enumerate(range(0, x_ref.shape[1], TILE)):
+        here = slice(start, start + TILE)
+        whole[:, here] = add_up(x_ref[:, here], weights, scale, buffer[:, here])
+        tile = pl.ds(start, TILE)
+        copies.append(pltpu.make_async_copy(whole.at[:, tile], out_ref.at[:, tile], sems.at[i]))
         copies[-1].start()
     for copy in copies:
         copy.wait()
@@ -336,9 +355,8 @@
         out_shape=pltpu.HBM((rows, width), jnp.bfloat16),
         scratch_shapes=[
             pltpu.VMEM((total, width), jnp.bfloat16),
-            pltpu.VMEM((rows, total), jnp.bfloat16),
             pltpu.VMEM((rows, width), jnp.bfloat16),
-            pltpu.SemaphoreType.DMA((rows // BLOCK,)),
+            pltpu.SemaphoreType.DMA((width // TILE,)),
         ],
         compiler_params=params(),
         cost_estimate=pl.CostEstimate(
@@ -350,14 +368,18 @@
 
 def round_kernel(servers, x_ref, mask_ref, pack_ref, *rest):
     parts, rest = rest[:servers], rest[servers:]
-    *most_refs, out_ref, far_ref, most_ref, buffer, weights = rest
+    *most_refs, out_ref, far_ref, most_ref, buffer = rest
     most_ref[...] = functools.reduce(jnp.maximum, [ref[...] for ref in most_refs])
     fill(buffer, parts)
-    weights[...] = weigh(x_ref[...], buffer[...], mask_ref[...])
-    for start in range(0, x_ref.shape[0], BLOCK):
-        stop = start + BLOCK
-        out_ref[start:stop] = add_up(x_ref[start:stop], weights[start:stop], buffer[...])
-    serve(out_ref[...], pack_ref, far_ref)
+    weights, scale = weigh(x_ref, buffer[...], mask_ref[...])
+    pack = pack_ref[: far_ref.shape[0]]
+    for start in range(0, x_ref.shape[1], TILE):
+        here = slice(start, start + TILE)
+        tile = add_up(x_ref[:, here], weights, scale, buffer[:, here])
+        out_ref[:, here] = tile
+        far_ref[:, here] = jnp.dot(pack, tile, preferred_element_type=jnp.float32).astype(
+            jnp.bfloat16
+        )
 
 
 def round_call(x, mask, pack, parts, mosts, sent):
@@ -370,10 +392,7 @@
             bf16(sent, width),
             jax.ShapeDtypeStruct((8, LANES), jnp.int32),
         ],
-        scratch_shapes=[
-            pltpu.VMEM((total, width), jnp.bfloat16),
-            pltpu.VMEM((rows, total), jnp.bfloat16),
-        ],
+        scratch_shapes=[pltpu.VMEM((total, width), jnp.bfloat16)],
         compiler_params=params(),
         cost_estimate=pl.CostEstimate(
             flops=5 * total * rows * width, bytes_accessed=6 * rows * width, transcendentals=rows

time: 53.2 us -> 53.9 us (1.013)
  Pallas kernels: 13.1 us -> 13.8 us
    pallas_call x1, Pallas kernels: 3.01 us -> 3.75 us  [round_call(): pl.pallas_call(functools.partial(round_kernel, servers), out_shape=[bf16(...]
  transfers between devices with their start and end apart: 17 -> 17, of which waited for: 11 -> 11; matrix products, arithmetic and copies ran while one was open for 1% -> 1% of each run, Pallas kernels for 11% -> 10%
where the time goes in v8:
time: 53.9 us; the launch traced here: 53.7 us
  waiting for transfers between devices  20.5 us (38%)
  starting transfers between devices  17.8 us (33%)
  Pallas kernels  13.8 us (26%)
  between operations  0.93 us (2%)
    ppermute x3, waiting for transfers between devices, across(): return lax.ppermute(value, 'rep', beyond)  12.6 us
    ppermute x9, starting transfers between devices, turn(): return lax.ppermute(value, 'clus', [(c, c ^ d) for c in range(servers)])  11.6 us
    ppermute x9, waiting for transfers between devices, turn(): return lax.ppermute(value, 'clus', [(c, c ^ d) for c in range(servers)])  5.7 us
    ppermute x3, starting transfers between devices, across(): return lax.ppermute(value, 'rep', beyond)  3.95 us
    pallas_call x1, Pallas kernels, round_call(): pl.pallas_call(functools.partial(round_kernel, servers), out_shape=[bf16(...  3.75 us
    pallas_call x1, Pallas kernels, last_call(): pl.pallas_call(functools.partial(last_kernel, servers), out_specs=pl.Bloc...  3.3 us
    ppermute x2, waiting for transfers between devices, shift(): lax.ppermute(value, 'rep', [(g, (g + by) % groups) for g in range(groups)])  2.19 us
    pallas_call x1, Pallas kernels, normalize_call(): pl.pallas_call(normalize_kernel, in_specs=[pl.BlockSpec(memory_space=pl.A...  1.87 us
  transfers between devices with their start and end apart: 17, of which 11 were waited for; matrix products, arithmetic and copies ran while one was open for 1% of the time, Pallas kernels for 10%

profile of v8, /device:TPU:0, one launch (start us, length us, event | category | flops | bytes accessed | tf_op | source)
XLA Modules:
  0.0 53.7 jit_solution(1007770724774554276)
XLA Ops:
  0.0 3.9 %collective-permute-start.11 = (s32[4,32]{1,0:T(4,128)}, s32[4,32]{1,0:T(4,128)S(1)}, u32[]{:S(2)}, u32[]{:S(2)}) collective-permute-start(s32[4,32]{1,0:T(4,128)} %bitcast.12), channel_id=1, source_target_pairs={{0,24},{8,16},{16,8},{24,0},{1,25},{9,17},{17,9},{25,1},{2,26},{10... | collective-permute-start | bytes 1544 | tf_op jit(solution)/shard_map/ppermute | solution.py:415
  3.9 0.5 collective-permute-start.10
  4.4 0.1 collective-permute-start.9
  4.5 1.0 %mask.1 = (bf16[512,128]{1,0:T(8,128)(2,1)S(1)}, s32[4,32]{1,0:T(4,128)S(1)}) custom-call(s32[10,1,512]{2,1,0:T(1,128)} %bitcast.11, s32[4,32]{1,0:T(4,128)} %bitcast.15), custom_call_target="tpu_custom_call" | custom-call | flops 1310720 | bytes 131072 | tf_op jit(solution)/shard_map/mask/pallas_call | solution.py:83
  5.5 0.2 collective-permute-done.11.refs_3_
  5.7 2.0 %collective-permute-done.10.refs_2_ = s32[4,32]{1,0:T(4,128)S(1)} collective-permute-done((s32[4,32]{1,0:T(4,128)}, s32[4,32]{1,0:T(4,128)S(1)}, u32[]{:S(2)}, u32[]{:S(2)}) %collective-permute-start.10) | collective-permute-done | bytes 544 | tf_op jit(solution)/shard_map/ppermute | solution.py:415
  7.7 0.5 collective-permute-done.9.refs_1_
  8.2 0.3 list.1.mine_ref
  8.5 1.3 %collective-permute-start.13 = (s32[8,128]{1,0:T(8,128)S(1)}, s32[8,128]{1,0:T(8,128)S(1)}, u32[]{:S(2)}, u32[]{:S(2)}) collective-permute-start(s32[8,128]{1,0:T(8,128)S(1)} %list.1.mine_ref), channel_id=1, source_target_pairs={{0,7},{1,2},{2,1},{3,4},{4,3},{5,6},{6,5},{7,0},{8,15},{9,10},{10,... | collective-permute-start | bytes 12296 | tf_op jit(solution)/shard_map/ppermute | solution.py:421
  9.9 0.4 collective-permute-start.12
  10.2 1.9 %normalize.1.x_ref = bf16[512,2048]{1,0:T(8,128)(2,1)S(1)} custom-call(bf16[512,2048]{1,0:T(8,128)(2,1)} %bitcast.10), custom_call_target="tpu_custom_call" | custom-call | flops 6291456 | bytes 4194304 | tf_op jit(solution)/shard_map/normalize/pallas_call | solution.py:46
  12.1 1.3 %collective-permute-done.13.beyond_ref = s32[8,128]{1,0:T(8,128)S(1)} collective-permute-done((s32[8,128]{1,0:T(8,128)S(1)}, s32[8,128]{1,0:T(8,128)S(1)}, u32[]{:S(2)}, u32[]{:S(2)}) %collective-permute-start.13) | collective-permute-done | bytes 4128 | tf_op jit(solution)/shard_map/ppermute | solution.py:421
  13.4 0.0 collective-permute-done.12.within_ref
  13.4 0.7 %pack_far.1 = (bf16[128,512]{1,0:T(8,128)(2,1)S(1)}, s32[8,128]{1,0:T(8,128)S(1)}, bf16[48,2048]{1,0:T(8,128)(2,1)S(1)}) custom-call(bf16[512,2048]{1,0:T(8,128)(2,1)S(1)} %normalize.1.x_ref, s32[8,128]{1,0:T(8,128)S(1)} %list.1.mine_ref, s32[8,128]{1,0:T(8,128)S(1)} %collective-permute-done.12.within_ref, s32[8,128]{1,0:T(8,128)S(1)} %collective-permute-done.13.beyond_ref), custom_call_target="tpu_custom_call" | custom-call | flops 67108864 | bytes 2097152 | tf_op jit(solution)/shard_map/pack_far/pallas_call | solution.py:183
  14.1 1.4 %collective-permute-start.14 = (bf16[48,2048]{1,0:T(8,128)(2,1)S(1)}, bf16[48,2048]{1,0:T(8,128)(2,1)S(1)}, u32[]{:S(2)}, u32[]{:S(2)}) collective-permute-start(bf16[48,2048]{1,0:T(8,128)(2,1)S(1)} %get-tuple-element.98), channel_id=1, source_target_pairs={{0,7},{1,2},{2,1},{3,4},{4,3},{5,6},{6,5},{7,0},{8,15},{9,10},{10,... | collective-permute-start | bytes 589832 | tf_op jit(solution)/shard_map/ppermute | solution.py:421
  15.5 1.4 %serve_near.1 = (bf16[256,512]{1,0:T(8,128)(2,1)S(1)}, bf16[128,128]{1,0:T(8,128)(2,1)S(1)}, bf16[128,2048]{1,0:T(8,128)(2,1)S(1)}, bf16[128,2048]{1,0:T(8,128)(2,1)S(1)}, bf16[80,2048]{1,0:T(8,128)(2,1)S(1)}) custom-call(bf16[512,2048]{1,0:T(8,128)(2,1)S(1)} %normalize.1.x_ref, bf16[128,512]{1,0:T(8,128)(2,1)S(1)} %get-tuple-element.95.pack_ref, ...), custom_call_target="tpu_custom_call" | custom-call | flops 805306368 | bytes 4194304 | tf_op jit(solution)/shard_map/serve_near/pallas_call | solution.py:221
  16.9 0.1 collective-permute-start.15
  17.0 5.3 %collective-permute-done.14.far_ref = bf16[48,2048]{1,0:T(8,128)(2,1)S(1)} collective-permute-done((bf16[48,2048]{1,0:T(8,128)(2,1)S(1)}, bf16[48,2048]{1,0:T(8,128)(2,1)S(1)}, u32[]{:S(2)}, u32[]{:S(2)}) %collective-permute-start.14) | collective-permute-done | bytes 196640 | tf_op jit(solution)/shard_map/ppermute | solution.py:421
  22.3 0.3 unpack.6.base_ref
  22.6 0.0 collective-permute-done.15.core_ref
  22.6 0.1 combine.4
  22.7 1.6 %collective-permute-start.16 = (bf16[32,2048]{1,0:T(8,128)(2,1)S(1)}, bf16[32,2048]{1,0:T(8,128)(2,1)S(1)}, u32[]{:S(2)}, u32[]{:S(2)}) collective-permute-start(bf16[32,2048]{1,0:T(8,128)(2,1)S(1)} %get-tuple-element.102), channel_id=1, source_target_pairs={{0,24},{8,16},{16,8},{24,0},{1,25},{9,17},{17,9},{25,1},{2,26},{10... | collective-permute-start | bytes 393224 | tf_op jit(solution)/shard_map/ppermute | solution.py:415
  24.2 0.5 collective-permute-start.17
  24.7 1.5 %collective-permute-start.18 = (bf16[32,2048]{1,0:T(8,128)(2,1)S(1)}, bf16[32,2048]{1,0:T(8,128)(2,1)S(1)}, u32[]{:S(2)}, u32[]{:S(2)}) collective-permute-start(bf16[32,2048]{1,0:T(8,128)(2,1)S(1)} %get-tuple-element.104), channel_id=1, source_target_pairs={{0,8},{8,0},{16,24},{24,16},{1,9},{9,1},{17,25},{25,17},{2,10},{10... | collective-permute-start | bytes 393224 | tf_op jit(solution)/shard_map/ppermute | solution.py:415
  26.2 0.0 collective-permute-start.20
  26.2 1.7 %collective-permute-start.19 = (s32[8,128]{1,0:T(8,128)S(1)}, s32[8,128]{1,0:T(8,128)S(1)}, u32[]{:S(2)}, u32[]{:S(2)}) collective-permute-start(s32[8,128]{1,0:T(8,128)S(1)} %get-tuple-element.106.rest_4_), channel_id=1, source_target_pairs={{0,3},{1,4},{2,5},{3,6},{4,7},{5,0},{6,1},{7,2},{8,11},{9,12},{10,... | collective-permute-start | bytes 12296 | tf_op jit(solution)/shard_map/ppermute | solution.py:418
  28.0 1.3 %collective-permute-done.20.rest_6_ = s32[8,128]{1,0:T(8,128)S(1)} collective-permute-done((s32[8,128]{1,0:T(8,128)S(1)}, s32[8,128]{1,0:T(8,128)S(1)}, u32[]{:S(2)}, u32[]{:S(2)}) %collective-permute-start.20) | collective-permute-done | bytes 4128 | tf_op jit(solution)/shard_map/ppermute | solution.py:418
  29.2 0.9 %collective-permute-done.19.rest_5_ = s32[8,128]{1,0:T(8,128)S(1)} collective-permute-done((s32[8,128]{1,0:T(8,128)S(1)}, s32[8,128]{1,0:T(8,128)S(1)}, u32[]{:S(2)}, u32[]{:S(2)}) %collective-permute-start.19) | collective-permute-done | bytes 4128 | tf_op jit(solution)/shard_map/ppermute | solution.py:418
  30.1 0.0 collective-permute-done.16.rest_0_
  30.1 0.0 collective-permute-done.17.rest_1_
  30.2 0.0 collective-permute-done.18.rest_2_
  30.2 3.8 %mix_and_pack.3 = (bf16[512,2048]{1,0:T(8,128)(2,1)S(1)}, bf16[48,2048]{1,0:T(8,128)(2,1)S(1)}, s32[8,128]{1,0:T(8,128)S(1)}) custom-call(bf16[512,2048]{1,0:T(8,128)(2,1)S(1)} %normalize.1.x_ref, bf16[512,128]{1,0:T(8,128)(2,1)S(1)} %get-tuple-element.97.mask_ref, bf16[128,512]{1,0:T(8,128)(2,1)S(1)} %get-tuple-element.95.pack_ref, ...), custom_call_target="tpu_custom_call" | custom-call | flops 671088640 | bytes 6291456 | tf_op jit(solution)/shard_map/mix_and_pack/pallas_call | solution.py:388
  33.9 1.2 %collective-permute-start.21 = (bf16[48,2048]{1,0:T(8,128)(2,1)S(1)}, bf16[48,2048]{1,0:T(8,128)(2,1)S(1)}, u32[]{:S(2)}, u32[]{:S(2)}) collective-permute-start(bf16[48,2048]{1,0:T(8,128)(2,1)S(1)} %get-tuple-element.107), channel_id=1, source_target_pairs={{0,7},{1,2},{2,1},{3,4},{4,3},{5,6},{6,5},{7,0},{8,15},{9,10},{10,... | collective-permute-start | bytes 589832 | tf_op jit(solution)/shard_map/ppermute | solution.py:421
  35.2 0.7 %serve_again.3 = (bf16[128,2048]{1,0:T(8,128)(2,1)S(1)}, bf16[128,2048]{1,0:T(8,128)(2,1)S(1)}) custom-call(bf16[512,2048]{1,0:T(8,128)(2,1)S(1)} %get-tuple-element.108.x_ref, bf16[256,512]{1,0:T(8,128)(2,1)S(1)} %get-tuple-element.109.select_ref), custom_call_target="tpu_custom_call" | custom-call | flops 536870912 | bytes 4194304 | tf_op jit(solution)/shard_map/serve_again/pallas_call | solution.py:245
  35.9 0.1 collective-permute-start.22
  36.0 6.1 %collective-permute-done.21.far_ref = bf16[48,2048]{1,0:T(8,128)(2,1)S(1)} collective-permute-done((bf16[48,2048]{1,0:T(8,128)(2,1)S(1)}, bf16[48,2048]{1,0:T(8,128)(2,1)S(1)}, u32[]{:S(2)}, u32[]{:S(2)}) %collective-permute-start.21) | collective-permute-done | bytes 196640 | tf_op jit(solution)/shard_map/ppermute | solution.py:421
  42.0 0.3 unpack.7.base_ref
  42.3 0.0 collective-permute-done.22.core_ref
  42.3 0.1 combine.5
  42.4 1.5 %collective-permute-start.23 = (bf16[32,2048]{1,0:T(8,128)(2,1)S(1)}, bf16[32,2048]{1,0:T(8,128)(2,1)S(1)}, u32[]{:S(2)}, u32[]{:S(2)}) collective-permute-start(bf16[32,2048]{1,0:T(8,128)(2,1)S(1)} %get-tuple-element.114), channel_id=1, source_target_pairs={{0,24},{8,16},{16,8},{24,0},{1,25},{9,17},{17,9},{25,1},{2,26},{10... | collective-permute-start | bytes 393224 | tf_op jit(solution)/shard_map/ppermute | solution.py:415
  43.9 1.2 %collective-permute-start.24 = (bf16[32,2048]{1,0:T(8,128)(2,1)S(1)}, bf16[32,2048]{1,0:T(8,128)(2,1)S(1)}, u32[]{:S(2)}, u32[]{:S(2)}) collective-permute-start(bf16[32,2048]{1,0:T(8,128)(2,1)S(1)} %get-tuple-element.115), channel_id=1, source_target_pairs={{0,16},{8,24},{16,0},{24,8},{1,17},{9,25},{17,1},{25,9},{2,18},{10... | collective-permute-start | bytes 393224 | tf_op jit(solution)/shard_map/ppermute | solution.py:415
  45.1 0.8 %collective-permute-start.25 = (bf16[32,2048]{1,0:T(8,128)(2,1)S(1)}, bf16[32,2048]{1,0:T(8,128)(2,1)S(1)}, u32[]{:S(2)}, u32[]{:S(2)}) collective-permute-start(bf16[32,2048]{1,0:T(8,128)(2,1)S(1)} %get-tuple-element.116), channel_id=1, source_target_pairs={{0,8},{8,0},{16,24},{24,16},{1,9},{9,1},{17,25},{25,17},{2,10},{10... | collective-permute-start | bytes 393224 | tf_op jit(solution)/shard_map/ppermute | solution.py:415
  46.0 0.5 slice.7
  47.1 1.3 %collective-permute-done.23 = bf16[32,2048]{1,0:T(8,128)(2,1)S(1)} collective-permute-done((bf16[32,2048]{1,0:T(8,128)(2,1)S(1)}, bf16[32,2048]{1,0:T(8,128)(2,1)S(1)}, u32[]{:S(2)}, u32[]{:S(2)}) %collective-permute-start.23) | collective-permute-done | bytes 131104 | tf_op jit(solution)/shard_map/ppermute | solution.py:415
  48.4 1.3 %collective-permute-done.24 = bf16[32,2048]{1,0:T(8,128)(2,1)S(1)} collective-permute-done((bf16[32,2048]{1,0:T(8,128)(2,1)S(1)}, bf16[32,2048]{1,0:T(8,128)(2,1)S(1)}, u32[]{:S(2)}, u32[]{:S(2)}) %collective-permute-start.24) | collective-permute-done | bytes 131104 | tf_op jit(solution)/shard_map/ppermute | solution.py:415
  49.7 0.3 collective-permute-done.25
  50.1 3.5 %conditional.1 = (bf16[1,1,512,2048]{3,2,1,0:T(8,128)(2,1)}) conditional(s32[]{:T(128)} %bitcast.6, (bf16[512,2048]{1,0:T(8,128)(2,1)S(1)}, bf16[512,128]{1,0:T(8,128)(2,1)S(1)}, bf16[32,2048]{1,0:T(8,128)(2,1)S(1)}, bf16[32,2048]{1,0:T(8,128)(2,1)S(1)}, bf16[32,2048]{1,0:T(8,128)(2,1)S(1)}, /*index=5*/bf16[32,2048]{1,0:T(8,128)(2,1)S(1)}) %tuple.13, ...), branch_computations={%region_0.0_spmd, %region_1.0_spmd} | conditional | flops 36105093120 | bytes 94372208 | solution.py:475
  50.1 3.3 %mix.2 = bf16[512,2048]{1,0:T(8,128)(2,1)} custom-call(bf16[512,2048]{1,0:T(8,128)(2,1)S(1)} %get-tuple-element.43.x_ref, bf16[512,128]{1,0:T(8,128)(2,1)S(1)} %get-tuple-element.44.mask_ref, bf16[32,2048]{1,0:T(8,128)(2,1)S(1)} %get-tuple-element.45.rest_0_, bf16[32,2048]{1,0:T(8,128)(2,1)S(1)} %get-tuple-element.46.rest_1_, ...), custom_call_target="tpu_custom_call" | custom-call | flops 536870912 | bytes 4194304 | tf_op jit(solution)/shard_map/cond/branch_0_fun/mix/pallas_call | solution.py:352
Async XLA Ops:
  0.0 5.7 %collective-permute-start.11 = (s32[4,32]{1,0:T(4,128)}, s32[4,32]{1,0:T(4,128)S(1)}, u32[]{:S(2)}, u32[]{:S(2)}) collective-permute-start(s32[4,32]{1,0:T(4,128)} %bitcast.12), channel_id=1, source_target_pairs={{0,24},{8,16},{16,8},{24,0},{1,25},{9,17},{17,9},{25,1},{2,26},{10... | collective-permute-start | bytes 1544 | tf_op jit(solution)/shard_map/ppermute | solution.py:415
  3.9 3.8 %collective-permute-start.10 = (s32[4,32]{1,0:T(4,128)}, s32[4,32]{1,0:T(4,128)S(1)}, u32[]{:S(2)}, u32[]{:S(2)}) collective-permute-start(s32[4,32]{1,0:T(4,128)} %bitcast.13), channel_id=1, source_target_pairs={{0,16},{8,24},{16,0},{24,8},{1,17},{9,25},{17,1},{25,9},{2,18},{10... | collective-permute-start | bytes 1544 | tf_op jit(solution)/shard_map/ppermute | solution.py:415
  4.4 3.8 %collective-permute-start.9 = (s32[4,32]{1,0:T(4,128)}, s32[4,32]{1,0:T(4,128)S(1)}, u32[]{:S(2)}, u32[]{:S(2)}) collective-permute-start(s32[4,32]{1,0:T(4,128)} %bitcast.14), channel_id=1, source_target_pairs={{0,8},{8,0},{16,24},{24,16},{1,9},{9,1},{17,25},{25,17},{2,10},{10... | collective-permute-start | bytes 1544 | tf_op jit(solution)/shard_map/ppermute | solution.py:415
  8.5 4.8 %collective-permute-start.13 = (s32[8,128]{1,0:T(8,128)S(1)}, s32[8,128]{1,0:T(8,128)S(1)}, u32[]{:S(2)}, u32[]{:S(2)}) collective-permute-start(s32[8,128]{1,0:T(8,128)S(1)} %list.1.mine_ref), channel_id=1, source_target_pairs={{0,7},{1,2},{2,1},{3,4},{4,3},{5,6},{6,5},{7,0},{8,15},{9,10},{10,... | collective-permute-start | bytes 12296 | tf_op jit(solution)/shard_map/ppermute | solution.py:421
  9.9 3.5 %collective-permute-start.12 = (s32[8,128]{1,0:T(8,128)S(1)}, s32[8,128]{1,0:T(8,128)S(1)}, u32[]{:S(2)}, u32[]{:S(2)}) collective-permute-start(s32[8,128]{1,0:T(8,128)S(1)} %list.1.mine_ref), channel_id=1, source_target_pairs={{0,1},{1,0},{2,3},{3,2},{4,5},{5,4},{6,7},{7,6},{8,9},{9,8},{10,11... | collective-permute-start | bytes 12296 | tf_op jit(solution)/shard_map/ppermute | solution.py:424
  14.1 8.2 %collective-permute-start.14 = (bf16[48,2048]{1,0:T(8,128)(2,1)S(1)}, bf16[48,2048]{1,0:T(8,128)(2,1)S(1)}, u32[]{:S(2)}, u32[]{:S(2)}) collective-permute-start(bf16[48,2048]{1,0:T(8,128)(2,1)S(1)} %get-tuple-element.98), channel_id=1, source_target_pairs={{0,7},{1,2},{2,1},{3,4},{4,3},{5,6},{6,5},{7,0},{8,15},{9,10},{10,... | collective-permute-start | bytes 589832 | tf_op jit(solution)/shard_map/ppermute | solution.py:421
  16.9 5.7 %collective-permute-start.15 = (bf16[128,2048]{1,0:T(8,128)(2,1)S(1)}, bf16[128,2048]{1,0:T(8,128)(2,1)S(1)}, u32[]{:S(2)}, u32[]{:S(2)}) collective-permute-start(bf16[128,2048]{1,0:T(8,128)(2,1)S(1)} %get-tuple-element.100), channel_id=1, source_target_pairs={{0,1},{1,0},{2,3},{3,2},{4,5},{5,4},{6,7},{7,6},{8,9},{9,8},{10,11... | collective-permute-start | bytes 1572872 | tf_op jit(solution)/shard_map/ppermute | solution.py:424
  22.7 7.5 %collective-permute-start.16 = (bf16[32,2048]{1,0:T(8,128)(2,1)S(1)}, bf16[32,2048]{1,0:T(8,128)(2,1)S(1)}, u32[]{:S(2)}, u32[]{:S(2)}) collective-permute-start(bf16[32,2048]{1,0:T(8,128)(2,1)S(1)} %get-tuple-element.102), channel_id=1, source_target_pairs={{0,24},{8,16},{16,8},{24,0},{1,25},{9,17},{17,9},{25,1},{2,26},{10... | collective-permute-start | bytes 393224 | tf_op jit(solution)/shard_map/ppermute | solution.py:415
  24.2 5.9 %collective-permute-start.17 = (bf16[32,2048]{1,0:T(8,128)(2,1)S(1)}, bf16[32,2048]{1,0:T(8,128)(2,1)S(1)}, u32[]{:S(2)}, u32[]{:S(2)}) collective-permute-start(bf16[32,2048]{1,0:T(8,128)(2,1)S(1)} %get-tuple-element.103), channel_id=1, source_target_pairs={{0,16},{8,24},{16,0},{24,8},{1,17},{9,25},{17,1},{25,9},{2,18},{10... | collective-permute-start | bytes 393224 | tf_op jit(solution)/shard_map/ppermute | solution.py:415
  24.7 5.4 %collective-permute-start.18 = (bf16[32,2048]{1,0:T(8,128)(2,1)S(1)}, bf16[32,2048]{1,0:T(8,128)(2,1)S(1)}, u32[]{:S(2)}, u32[]{:S(2)}) collective-permute-start(bf16[32,2048]{1,0:T(8,128)(2,1)S(1)} %get-tuple-element.104), channel_id=1, source_target_pairs={{0,8},{8,0},{16,24},{24,16},{1,9},{9,1},{17,25},{25,17},{2,10},{10... | collective-permute-start | bytes 393224 | tf_op jit(solution)/shard_map/ppermute | solution.py:415
  26.2 3.0 %collective-permute-start.20 = (s32[8,128]{1,0:T(8,128)S(1)}, s32[8,128]{1,0:T(8,128)S(1)}, u32[]{:S(2)}, u32[]{:S(2)}) collective-permute-start(s32[8,128]{1,0:T(8,128)S(1)} %get-tuple-element.106.rest_4_), channel_id=1, source_target_pairs={{0,5},{1,6},{2,7},{3,0},{4,1},{5,2},{6,3},{7,4},{8,13},{9,14},{10,... | collective-permute-start | bytes 12296 | tf_op jit(solution)/shard_map/ppermute | solution.py:418
  26.2 3.9 %collective-permute-start.19 = (s32[8,128]{1,0:T(8,128)S(1)}, s32[8,128]{1,0:T(8,128)S(1)}, u32[]{:S(2)}, u32[]{:S(2)}) collective-permute-start(s32[8,128]{1,0:T(8,128)S(1)} %get-tuple-element.106.rest_4_), channel_id=1, source_target_pairs={{0,3},{1,4},{2,5},{3,6},{4,7},{5,0},{6,1},{7,2},{8,11},{9,12},{10,... | collective-permute-start | bytes 12296 | tf_op jit(solution)/shard_map/ppermute | solution.py:418
  33.9 8.1 %collective-permute-start.21 = (bf16[48,2048]{1,0:T(8,128)(2,1)S(1)}, bf16[48,2048]{1,0:T(8,128)(2,1)S(1)}, u32[]{:S(2)}, u32[]{:S(2)}) collective-permute-start(bf16[48,2048]{1,0:T(8,128)(2,1)S(1)} %get-tuple-element.107), channel_id=1, source_target_pairs={{0,7},{1,2},{2,1},{3,4},{4,3},{5,6},{6,5},{7,0},{8,15},{9,10},{10,... | collective-permute-start | bytes 589832 | tf_op jit(solution)/shard_map/ppermute | solution.py:421
  35.9 6.4 %collective-permute-start.22 = (bf16[128,2048]{1,0:T(8,128)(2,1)S(1)}, bf16[128,2048]{1,0:T(8,128)(2,1)S(1)}, u32[]{:S(2)}, u32[]{:S(2)}) collective-permute-start(bf16[128,2048]{1,0:T(8,128)(2,1)S(1)} %get-tuple-element.111), channel_id=1, source_target_pairs={{0,1},{1,0},{2,3},{3,2},{4,5},{5,4},{6,7},{7,6},{8,9},{9,8},{10,11... | collective-permute-start | bytes 1572872 | tf_op jit(solution)/shard_map/ppermute | solution.py:424
  42.4 6.0 %collective-permute-start.23 = (bf16[32,2048]{1,0:T(8,128)(2,1)S(1)}, bf16[32,2048]{1,0:T(8,128)(2,1)S(1)}, u32[]{:S(2)}, u32[]{:S(2)}) collective-permute-start(bf16[32,2048]{1,0:T(8,128)(2,1)S(1)} %get-tuple-element.114), channel_id=1, source_target_pairs={{0,24},{8,16},{16,8},{24,0},{1,25},{9,17},{17,9},{25,1},{2,26},{10... | collective-permute-start | bytes 393224 | tf_op jit(solution)/shard_map/ppermute | solution.py:415
  43.9 5.8 %collective-permute-start.24 = (bf16[32,2048]{1,0:T(8,128)(2,1)S(1)}, bf16[32,2048]{1,0:T(8,128)(2,1)S(1)}, u32[]{:S(2)}, u32[]{:S(2)}) collective-permute-start(bf16[32,2048]{1,0:T(8,128)(2,1)S(1)} %get-tuple-element.115), channel_id=1, source_target_pairs={{0,16},{8,24},{16,0},{24,8},{1,17},{9,25},{17,1},{25,9},{2,18},{10... | collective-permute-start | bytes 393224 | tf_op jit(solution)/shard_map/ppermute | solution.py:415
  45.1 5.0 %collective-permute-start.25 = (bf16[32,2048]{1,0:T(8,128)(2,1)S(1)}, bf16[32,2048]{1,0:T(8,128)(2,1)S(1)}, u32[]{:S(2)}, u32[]{:S(2)}) collective-permute-start(bf16[32,2048]{1,0:T(8,128)(2,1)S(1)} %get-tuple-element.116), channel_id=1, source_target_pairs={{0,8},{8,0},{16,24},{24,16},{1,9},{9,1},{17,25},{25,17},{2,10},{10... | collective-permute-start | bytes 393224 | tf_op jit(solution)/shard_map/ppermute | solution.py:415

commit v9 on v8

--- a/solution.py
+++ b/solution.py
@@ -11,6 +11,7 @@
 LANES = 128
 BLOCK = 128
 TILE = 256
+CHUNK = 32
 
 
 FAR_SHARE = 3, 8
@@ -195,8 +196,9 @@
     )(x, mine, within, beyond)
 
 
-def near_kernel(x_ref, pack_ref, mine_ref, within_ref, *out_refs):
-    select_ref, expand_ref, core_ref, own_ref, rest_ref = out_refs
+def near_kernel(x_ref, pack_ref, mine_ref, within_ref, far_ref, *out_refs):
+    select_ref, expand_ref, core_ref, own_ref, rest_ref, held_ref = out_refs
+    held_ref[...] = far_ref[...]
     rows, total = x_ref.shape[0], mine_ref.shape[1]
     third = lax.axis_index("rep") % 2 * 2
     own = mine_ref[0:1]
@@ -215,9 +217,9 @@
     ).astype(jnp.bfloat16)
 
 
-def near_call(x, pack, mine, within, sent):
+def near_call(x, pack, mine, within, far):
     rows, width = x.shape
-    total = mine.shape[1]
+    total, sent = mine.shape[1], far.shape[0]
     return pl.pallas_call(
         near_kernel,
         out_shape=[
@@ -226,51 +228,54 @@
             bf16(total, width),
             bf16(total, width),
             bf16(total - sent, width),
+            bf16(sent, width),
         ],
         compiler_params=params(),
         cost_estimate=pl.CostEstimate(
             flops=6 * total * rows * width, bytes_accessed=4 * rows * width, transcendentals=0
         ),
         name="serve_near",
-    )(x, pack, mine, within)
-
-
-def again_kernel(x_ref, select_ref, core_ref, own_ref):
+    )(x, pack, mine, within, far)
+
+
+def again_kernel(x_ref, select_ref, far_ref, core_ref, own_ref, held_ref):
+    held_ref[...] = far_ref[...]
     serve(x_ref[...], select_ref, core_ref, own_ref)
 
 
-def again_call(x, select):
+def again_call(x, select, far):
     rows, width = x.shape
     total = select.shape[0] // 2
     return pl.pallas_call(
         again_kernel,
-        out_shape=[bf16(total, width)] * 2,
+        out_shape=[bf16(total, width)] * 2 + [bf16(*far.shape)],
         compiler_params=params(),
         cost_estimate=pl.CostEstimate(
             flops=4 * total * rows * width, bytes_accessed=4 * rows * width, transcendentals=0
         ),
         name="serve_again",
-    )(x, select)
-
-
-def unpack_kernel(first, expand_ref, far_ref, *refs):
-    out_ref, sent = refs[-1], far_ref.shape[0]
+    )(x, select, far)
+
+
+def unpack_kernel(first, expand_ref, around_ref, beside_ref, *refs):
+    out_ref, sent = refs[-1], around_ref.shape[0]
+    far = around_ref[...] + beside_ref[...]
     rows = jnp.dot(
-        expand_ref[:, first : first + sent], far_ref[...], preferred_element_type=jnp.float32
+        expand_ref[:, first : first + sent], far, preferred_element_type=jnp.float32
     )
     for base_ref in refs[:-1]:
         rows += base_ref[...].astype(jnp.float32)
     out_ref[...] = rows.astype(jnp.bfloat16)
 
 
-def unpack_call(expand, far, *base, first=0):
+def unpack_call(expand, around, beside, *base, first=0):
     return pl.pallas_call(
         functools.partial(unpack_kernel, first),
-        out_shape=bf16(expand.shape[0], far.shape[1]),
+        out_shape=bf16(expand.shape[0], around.shape[1]),
         compiler_params=params(),
         cost_estimate=pl.CostEstimate(flops=2**34, bytes_accessed=2**25, transcendentals=0),
         name="unpack",
-    )(expand, far, *base)
+    )(expand, around, beside, *base)
 
 
 def combine_kernel(base_ref, core_ref, most_ref, out_most_ref, *out_refs):
@@ -314,14 +319,14 @@
     crossed = jnp.dot(weights, high, preferred_element_type=jnp.float32)
     crossed += jnp.dot(weights, low, preferred_element_type=jnp.float32)
     squares = weights.astype(jnp.float32) * (2.0 * dots + crossed)
-    own = jnp.zeros((rows, LANES), jnp.float32)
-    for start in range(0, width, LANES):
-        tile = x_ref[:, start : start + LANES].astype(jnp.float32)
-        own += tile * tile
-    if squares.shape[1] == LANES:
-        total = jnp.sum(own + squares, axis=1, keepdims=True)
-    else:
-        total = jnp.sum(own, axis=1, keepdims=True) + jnp.sum(squares, axis=1, keepdims=True)
+    own = []
+    for first in range(0, rows, CHUNK):
+        chunk = jnp.zeros((CHUNK, LANES), jnp.float32)
+        for start in range(0, width, LANES):
+            tile = x_ref[first : first + CHUNK, start : start + LANES].astype(jnp.float32)
+            chunk += tile * tile
+        own.append(jnp.sum(chunk, axis=1, keepdims=True))
+    total = jnp.concatenate(own, axis=0) + jnp.sum(squares, axis=1, keepdims=True)
     return weights, lax.rsqrt(total * (1.0 / width) + 1e-06)
 
 
@@ -372,14 +377,10 @@
     most_ref[...] = functools.reduce(jnp.maximum, [ref[...] for ref in most_refs])
     fill(buffer, parts)
     weights, scale = weigh(x_ref, buffer[...], mask_ref[...])
-    pack = pack_ref[: far_ref.shape[0]]
     for start in range(0, x_ref.shape[1], TILE):
         here = slice(start, start + TILE)
-        tile = add_up(x_ref[:, here], weights, scale, buffer[:, here])
-        out_ref[:, here] = tile
-        far_ref[:, here] = jnp.dot(pack, tile, preferred_element_type=jnp.float32).astype(
-            jnp.bfloat16
-        )
+        out_ref[:, here] = add_up(x_ref[:, here], weights, scale, buffer[:, here])
+    serve(out_ref[...], pack_ref, far_ref)
 
 
 def round_call(x, mask, pack, parts, mosts, sent):
@@ -410,6 +411,8 @@
     sent = total * FAR_SHARE[0] // FAR_SHARE[1]
     within = [(g, g ^ 1) for g in range(groups)]
     beyond = [(g, (g + 2 * (g % 2) - 1 + groups) % groups) for g in range(groups)]
+    ends = [(g, to) for g, to in beyond if abs(g - to) > 1]
+    beside = [(g, to) for g, to in beyond if abs(g - to) == 1]
 
     def turn(value, d):
         return lax.ppermute(value, "clus", [(c, c ^ d) for c in range(servers)])
@@ -419,6 +422,12 @@
 
     def across(value):
         return lax.ppermute(value, "rep", beyond)
+
+    def around_ends(value):
+        return lax.ppermute(value, "rep", ends)
+
+    def to_side(value):
+        return lax.ppermute(value, "rep", beside)
 
     def inside(value):
         return lax.ppermute(value, "rep", within)
@@ -432,13 +441,13 @@
         return [parts[0]] + [got[d] for d in range(1, servers)]
 
     def next_parts(x, far, select, expand, most):
-        far = across(far)
-        core, own = again_call(x, select)
-        core = inside(core)
-        return exchange(unpack_call(expand, far, own), core, most)
+        around = around_ends(far)
+        core, own, far = again_call(x, select, far)
+        base = unpack_call(expand, around, to_side(far), own)
+        return exchange(base, inside(core), most)
 
     def in_full(raw, x, rest, mask, pack, select, expand, most, first, last):
-        late = unpack_call(expand, across(rest), first=sent).reshape(servers, cap, -1)
+        late = unpack_call(expand, around_ends(rest), to_side(rest), first=sent).reshape(servers, cap, -1)
         parts = [a + b for a, b in zip(first, turned(list(late)))]
         x = raw
         for _ in range(ROUNDS - 1):
@@ -455,10 +464,10 @@
     beyond_list, within_list = across(mine), inside(mine)
     x = normalize_call(descriptors[0, 0])
     pack, most, far = far_call(x, mine, within_list, beyond_list, sent)
-    far = across(far)
-    select, expand, core, own, rest = near_call(x, pack, mine, within_list, sent)
-    core = inside(core)
-    most, first = exchange(unpack_call(expand, far, own), core, most)
+    around = around_ends(far)
+    select, expand, core, own, rest, far = near_call(x, pack, mine, within_list, far)
+    base = unpack_call(expand, around, to_side(far), own)
+    most, first = exchange(base, inside(core), most)
     mosts = [most]
     reach = 1
     while 2 * reach + 1 < groups:

time: 53.9 us -> 61.7 us (1.14)
  starting transfers between devices: 17.8 us -> 23.6 us
  waiting for transfers between devices: 20.5 us -> 23.2 us
  Pallas kernels: 13.8 us -> 13 us
    ppermute x3 -> x1, waiting for transfers between devices: 12.6 us -> 1.26 us  [across(): return lax.ppermute(value, 'rep', beyond)]
    ppermute x0 -> x4, waiting for transfers between devices: none -> 9.34 us  [the longest x2 9.34 us: around_ends(): return lax.ppermute(value, 'rep', ends)]
    ppermute x0 -> x4, starting transfers between devices: none -> 7.49 us  [the longest x2 6.14 us: around_ends(): return lax.ppermute(value, 'rep', ends)]
    ppermute x9, waiting for transfers between devices: 5.7 us -> 9.63 us  [turn(): return lax.ppermute(value, 'clus', [(c, c ^ d) for c in range(servers)])]
    ppermute x3 -> x1, starting transfers between devices: 3.95 us -> 1.34 us  [across(): return lax.ppermute(value, 'rep', beyond)]
    pallas_call x1, Pallas kernels: 3.75 us -> 2.69 us  [round_call(): pl.pallas_call(functools.partial(round_kernel, servers), out_shape=[bf16(...]
    ppermute x3, starting transfers between devices: 0.5 us -> 1.41 us  [inside(): return lax.ppermute(value, 'rep', within)]
    ppermute x2, waiting for transfers between devices: 2.19 us -> 2.96 us  [shift(): lax.ppermute(value, 'rep', [(g, (g + by) % groups) for g in range(groups)])]
  transfers between devices with their start and end apart: 17 -> 19, of which waited for: 11 -> 12; matrix products, arithmetic and copies ran while one was open for 1% -> 1% of each run, Pallas kernels for 10% -> 9%
where the time goes in v9:
time: 61.7 us; the launch traced here: 61.5 us
  starting transfers between devices  23.6 us (38%)
  waiting for transfers between devices  23.2 us (38%)
  Pallas kernels  13 us (21%)
  between operations  0.97 us (2%)
    ppermute x9, starting transfers between devices, turn(): return lax.ppermute(value, 'clus', [(c, c ^ d) for c in range(servers)])  11.6 us
    ppermute x9, waiting for transfers between devices, turn(): return lax.ppermute(value, 'clus', [(c, c ^ d) for c in range(servers)])  9.63 us
    ppermute x2, waiting for transfers between devices, around_ends(): return lax.ppermute(value, 'rep', ends)  9.34 us
    ppermute x2, starting transfers between devices, around_ends(): return lax.ppermute(value, 'rep', ends)  6.14 us
    pallas_call x1, Pallas kernels, last_call(): pl.pallas_call(functools.partial(last_kernel, servers), out_specs=pl.Bloc...  3.58 us
    ppermute x2, waiting for transfers between devices, shift(): lax.ppermute(value, 'rep', [(g, (g + by) % groups) for g in range(groups)])  2.96 us
    pallas_call x1, Pallas kernels, round_call(): pl.pallas_call(functools.partial(round_kernel, servers), out_shape=[bf16(...  2.69 us
    pallas_call x1, Pallas kernels, normalize_call(): pl.pallas_call(normalize_kernel, in_specs=[pl.BlockSpec(memory_space=pl.A...  1.87 us
  transfers between devices with their start and end apart: 19, of which 12 were waited for; matrix products, arithmetic and copies ran while one was open for 1% of the time, Pallas kernels for 9%

profile of v9, /device:TPU:0, one launch (start us, length us, event | category | flops | bytes accessed | tf_op | source)
XLA Modules:
  0.0 61.5 jit_solution(13140333058247953099)
XLA Ops:
  0.0 3.9 %collective-permute-start.13 = (s32[4,32]{1,0:T(4,128)}, s32[4,32]{1,0:T(4,128)S(1)}, u32[]{:S(2)}, u32[]{:S(2)}) collective-permute-start(s32[4,32]{1,0:T(4,128)} %bitcast.12), channel_id=1, source_target_pairs={{0,24},{8,16},{16,8},{24,0},{1,25},{9,17},{17,9},{25,1},{2,26},{10... | collective-permute-start | bytes 1544 | tf_op jit(solution)/shard_map/ppermute | solution.py:418
  3.9 0.5 collective-permute-start.12
  4.4 0.1 collective-permute-start.11
  4.5 1.0 %mask.1 = (bf16[512,128]{1,0:T(8,128)(2,1)S(1)}, s32[4,32]{1,0:T(4,128)S(1)}) custom-call(s32[10,1,512]{2,1,0:T(1,128)} %bitcast.11, s32[4,32]{1,0:T(4,128)} %bitcast.15), custom_call_target="tpu_custom_call" | custom-call | flops 1310720 | bytes 131072 | tf_op jit(solution)/shard_map/mask/pallas_call | solution.py:84
  5.5 0.2 collective-permute-done.13.refs_3_
  5.7 2.0 %collective-permute-done.12.refs_2_ = s32[4,32]{1,0:T(4,128)S(1)} collective-permute-done((s32[4,32]{1,0:T(4,128)}, s32[4,32]{1,0:T(4,128)S(1)}, u32[]{:S(2)}, u32[]{:S(2)}) %collective-permute-start.12) | collective-permute-done | bytes 544 | tf_op jit(solution)/shard_map/ppermute | solution.py:418
  7.7 0.5 collective-permute-done.11.refs_1_
  8.2 0.3 list.1.mine_ref
  8.5 1.3 %collective-permute-start.15 = (s32[8,128]{1,0:T(8,128)S(1)}, s32[8,128]{1,0:T(8,128)S(1)}, u32[]{:S(2)}, u32[]{:S(2)}) collective-permute-start(s32[8,128]{1,0:T(8,128)S(1)} %list.1.mine_ref), channel_id=1, source_target_pairs={{0,7},{1,2},{2,1},{3,4},{4,3},{5,6},{6,5},{7,0},{8,15},{9,10},{10,... | collective-permute-start | bytes 12296 | tf_op jit(solution)/shard_map/ppermute | solution.py:424
  9.9 0.4 collective-permute-start.14
  10.2 1.9 %normalize.1.x_ref = bf16[512,2048]{1,0:T(8,128)(2,1)S(1)} custom-call(bf16[512,2048]{1,0:T(8,128)(2,1)} %bitcast.10), custom_call_target="tpu_custom_call" | custom-call | flops 6291456 | bytes 4194304 | tf_op jit(solution)/shard_map/normalize/pallas_call | solution.py:47
  12.1 1.3 %collective-permute-done.15.beyond_ref = s32[8,128]{1,0:T(8,128)S(1)} collective-permute-done((s32[8,128]{1,0:T(8,128)S(1)}, s32[8,128]{1,0:T(8,128)S(1)}, u32[]{:S(2)}, u32[]{:S(2)}) %collective-permute-start.15) | collective-permute-done | bytes 4128 | tf_op jit(solution)/shard_map/ppermute | solution.py:424
  13.4 0.7 %pack_far.1 = (bf16[128,512]{1,0:T(8,128)(2,1)S(1)}, s32[8,128]{1,0:T(8,128)S(1)}, bf16[48,2048]{1,0:T(8,128)(2,1)S(1)}) custom-call(bf16[512,2048]{1,0:T(8,128)(2,1)S(1)} %normalize.1.x_ref, s32[8,128]{1,0:T(8,128)S(1)} %list.1.mine_ref, s32[8,128]{1,0:T(8,128)S(1)} %collective-permute-done.14.within_ref, s32[8,128]{1,0:T(8,128)S(1)} %collective-permute-done.15.beyond_ref), custom_call_target="tpu_custom_call" | custom-call | flops 67108864 | bytes 2097152 | tf_op jit(solution)/shard_map/pack_far/pallas_call | solution.py:184
  14.1 3.2 %collective-permute-start.16 = (bf16[48,2048]{1,0:T(8,128)(2,1)S(1)}, bf16[48,2048]{1,0:T(8,128)(2,1)S(1)}, u32[]{:S(2)}, u32[]{:S(2)}) collective-permute-start(bf16[48,2048]{1,0:T(8,128)(2,1)S(1)} %get-tuple-element.99.far_ref), channel_id=1, source_target_pairs={{0,7},{7,0},{8,15},{15,8},{16,23},{23,16},{24,31},{31,24}} | collective-permute-start | bytes 589832 | tf_op jit(solution)/shard_map/ppermute | solution.py:427
  17.3 1.4 %serve_near.1 = (bf16[256,512]{1,0:T(8,128)(2,1)S(1)}, bf16[128,128]{1,0:T(8,128)(2,1)S(1)}, bf16[128,2048]{1,0:T(8,128)(2,1)S(1)}, bf16[128,2048]{1,0:T(8,128)(...) custom-call(bf16[512,2048]{1,0:T(8,128)(2,1)S(1)} %normalize.1.x_ref, ...), custom_call_target="tpu_custom_call" | custom-call | flops 805306368 | bytes 4194304 | tf_op jit(solution)/shard_map/serve_near/pallas_call | solution.py:223
  18.8 0.7 %collective-permute-start.17 = (bf16[48,2048]{1,0:T(8,128)(2,1)S(1)}, bf16[48,2048]{1,0:T(8,128)(2,1)S(1)}, u32[]{:S(2)}, u32[]{:S(2)}) collective-permute-start(bf16[48,2048]{1,0:T(8,128)(2,1)S(1)} %get-tuple-element.102), channel_id=1, source_target_pairs={{1,2},{2,1},{3,4},{4,3},{5,6},{6,5},{9,10},{10,9},{11,12},{12,11},... | collective-permute-start | bytes 589832 | tf_op jit(solution)/shard_map/ppermute | solution.py:430
  19.5 0.1 collective-permute-start.18
  19.5 4.1 %collective-permute-done.16.around_ref = bf16[48,2048]{1,0:T(8,128)(2,1)S(1)} collective-permute-done((bf16[48,2048]{1,0:T(8,128)(2,1)S(1)}, bf16[48,2048]{1,0:T(8,128)(2,1)S(1)}, u32[]{:S(2)}, u32[]{:S(2)}) %collective-permute-start.16) | collective-permute-done | bytes 196640 | tf_op jit(solution)/shard_map/ppermute | solution.py:427
  23.7 0.0 collective-permute-done.17.beside_ref
  23.7 0.3 unpack.6.base_ref
  23.9 0.1 combine.4
  24.0 1.6 %collective-permute-start.19 = (bf16[32,2048]{1,0:T(8,128)(2,1)S(1)}, bf16[32,2048]{1,0:T(8,128)(2,1)S(1)}, u32[]{:S(2)}, u32[]{:S(2)}) collective-permute-start(bf16[32,2048]{1,0:T(8,128)(2,1)S(1)} %get-tuple-element.106), channel_id=1, source_target_pairs={{0,24},{8,16},{16,8},{24,0},{1,25},{9,17},{17,9},{25,1},{2,26},{10... | collective-permute-start | bytes 393224 | tf_op jit(solution)/shard_map/ppermute | solution.py:418
  25.6 0.1 collective-permute-start.20
  25.7 1.9 %collective-permute-start.21 = (bf16[32,2048]{1,0:T(8,128)(2,1)S(1)}, bf16[32,2048]{1,0:T(8,128)(2,1)S(1)}, u32[]{:S(2)}, u32[]{:S(2)}) collective-permute-start(bf16[32,2048]{1,0:T(8,128)(2,1)S(1)} %get-tuple-element.108), channel_id=1, source_target_pairs={{0,8},{8,0},{16,24},{24,16},{1,9},{9,1},{17,25},{25,17},{2,10},{10... | collective-permute-start | bytes 393224 | tf_op jit(solution)/shard_map/ppermute | solution.py:418
  27.6 0.8 %collective-permute-start.23 = (s32[8,128]{1,0:T(8,128)S(1)}, s32[8,128]{1,0:T(8,128)S(1)}, u32[]{:S(2)}, u32[]{:S(2)}) collective-permute-start(s32[8,128]{1,0:T(8,128)S(1)} %get-tuple-element.110.rest_4_), channel_id=1, source_target_pairs={{0,5},{1,6},{2,7},{3,0},{4,1},{5,2},{6,3},{7,4},{8,13},{9,14},{10,... | collective-permute-start | bytes 12296 | tf_op jit(solution)/shard_map/ppermute | solution.py:421
  28.3 1.0 %collective-permute-start.22 = (s32[8,128]{1,0:T(8,128)S(1)}, s32[8,128]{1,0:T(8,128)S(1)}, u32[]{:S(2)}, u32[]{:S(2)}) collective-permute-start(s32[8,128]{1,0:T(8,128)S(1)} %get-tuple-element.110.rest_4_), channel_id=1, source_target_pairs={{0,3},{1,4},{2,5},{3,6},{4,7},{5,0},{6,1},{7,2},{8,11},{9,12},{10,... | collective-permute-start | bytes 12296 | tf_op jit(solution)/shard_map/ppermute | solution.py:421
  29.3 1.3 %collective-permute-done.23.rest_6_ = s32[8,128]{1,0:T(8,128)S(1)} collective-permute-done((s32[8,128]{1,0:T(8,128)S(1)}, s32[8,128]{1,0:T(8,128)S(1)}, u32[]{:S(2)}, u32[]{:S(2)}) %collective-permute-start.23) | collective-permute-done | bytes 4128 | tf_op jit(solution)/shard_map/ppermute | solution.py:421
  30.6 1.7 %collective-permute-done.22.rest_5_ = s32[8,128]{1,0:T(8,128)S(1)} collective-permute-done((s32[8,128]{1,0:T(8,128)S(1)}, s32[8,128]{1,0:T(8,128)S(1)}, u32[]{:S(2)}, u32[]{:S(2)}) %collective-permute-start.22) | collective-permute-done | bytes 4128 | tf_op jit(solution)/shard_map/ppermute | solution.py:421
  32.3 0.0 collective-permute-done.19.rest_0_
  32.3 1.5 %collective-permute-done.20.rest_1_ = bf16[32,2048]{1,0:T(8,128)(2,1)S(1)} collective-permute-done((bf16[32,2048]{1,0:T(8,128)(2,1)S(1)}, bf16[32,2048]{1,0:T(8,128)(2,1)S(1)}, u32[]{:S(2)}, u32[]{:S(2)}) %collective-permute-start.20) | collective-permute-done | bytes 131104 | tf_op jit(solution)/shard_map/ppermute | solution.py:418
  33.8 0.1 collective-permute-done.21.rest_2_
  33.9 2.7 %mix_and_pack.3 = (bf16[512,2048]{1,0:T(8,128)(2,1)S(1)}, bf16[48,2048]{1,0:T(8,128)(2,1)S(1)}, s32[8,128]{1,0:T(8,128)S(1)}) custom-call(bf16[512,2048]{1,0:T(8,128)(2,1)S(1)} %normalize.1.x_ref, bf16[512,128]{1,0:T(8,128)(2,1)S(1)} %get-tuple-element.101.mask_ref, bf16[128,512]{1,0:T(8,128)(2,1)S(1)} %get-tuple-element.98.pack_ref, ...), custom_call_target="tpu_custom_call" | custom-call | flops 671088640 | bytes 6291456 | tf_op jit(solution)/shard_map/mix_and_pack/pallas_call | solution.py:389
  36.6 2.9 %collective-permute-start.24 = (bf16[48,2048]{1,0:T(8,128)(2,1)S(1)}, bf16[48,2048]{1,0:T(8,128)(2,1)S(1)}, u32[]{:S(2)}, u32[]{:S(2)}) collective-permute-start(bf16[48,2048]{1,0:T(8,128)(2,1)S(1)} %get-tuple-element.111.far_ref), channel_id=1, source_target_pairs={{0,7},{7,0},{8,15},{15,8},{16,23},{23,16},{24,31},{31,24}} | collective-permute-start | bytes 589832 | tf_op jit(solution)/shard_map/ppermute | solution.py:427
  39.5 0.7 %serve_again.3 = (bf16[128,2048]{1,0:T(8,128)(2,1)S(1)}, bf16[128,2048]{1,0:T(8,128)(2,1)S(1)}, bf16[48,2048]{1,0:T(8,128)(2,1)S(1)}) custom-call(bf16[512,2048]{1,0:T(8,128)(2,1)S(1)} %get-tuple-element.112.x_ref, bf16[256,512]{1,0:T(8,128)(2,1)S(1)} %get-tuple-element.113.select_ref, bf16[48,2048]{1,0:T(8,128)(2,1)S(1)} %get-tuple-element.111.far_ref), custom_call_target="tpu_custom_call" | custom-call | flops 536870912 | bytes 4194304 | tf_op jit(solution)/shard_map/serve_again/pallas_call | solution.py:249
  40.2 0.7 %collective-permute-start.25 = (bf16[48,2048]{1,0:T(8,128)(2,1)S(1)}, bf16[48,2048]{1,0:T(8,128)(2,1)S(1)}, u32[]{:S(2)}, u32[]{:S(2)}) collective-permute-start(bf16[48,2048]{1,0:T(8,128)(2,1)S(1)} %get-tuple-element.114), channel_id=1, source_target_pairs={{1,2},{2,1},{3,4},{4,3},{5,6},{6,5},{9,10},{10,9},{11,12},{12,11},... | collective-permute-start | bytes 589832 | tf_op jit(solution)/shard_map/ppermute | solution.py:430
  40.9 1.0 %collective-permute-start.26 = (bf16[128,2048]{1,0:T(8,128)(2,1)S(1)}, bf16[128,2048]{1,0:T(8,128)(2,1)S(1)}, u32[]{:S(2)}, u32[]{:S(2)}) collective-permute-start(bf16[128,2048]{1,0:T(8,128)(2,1)S(1)} %get-tuple-element.116), channel_id=1, source_target_pairs={{0,1},{1,0},{2,3},{3,2},{4,5},{5,4},{6,7},{7,6},{8,9},{9,8},{10,11... | collective-permute-start | bytes 1572872 | tf_op jit(solution)/shard_map/ppermute | solution.py:433
  41.9 5.2 %collective-permute-done.24.around_ref = bf16[48,2048]{1,0:T(8,128)(2,1)S(1)} collective-permute-done((bf16[48,2048]{1,0:T(8,128)(2,1)S(1)}, bf16[48,2048]{1,0:T(8,128)(2,1)S(1)}, u32[]{:S(2)}, u32[]{:S(2)}) %collective-permute-start.24) | collective-permute-done | bytes 196640 | tf_op jit(solution)/shard_map/ppermute | solution.py:427
  47.1 0.0 collective-permute-done.25.beside_ref
  47.1 0.3 unpack.7.base_ref
  47.4 0.1 combine.5
  47.4 1.3 %collective-permute-start.27 = (bf16[32,2048]{1,0:T(8,128)(2,1)S(1)}, bf16[32,2048]{1,0:T(8,128)(2,1)S(1)}, u32[]{:S(2)}, u32[]{:S(2)}) collective-permute-start(bf16[32,2048]{1,0:T(8,128)(2,1)S(1)} %get-tuple-element.119), channel_id=1, source_target_pairs={{0,24},{8,16},{16,8},{24,0},{1,25},{9,17},{17,9},{25,1},{2,26},{10... | collective-permute-start | bytes 393224 | tf_op jit(solution)/shard_map/ppermute | solution.py:418
  48.8 0.9 %collective-permute-start.28 = (bf16[32,2048]{1,0:T(8,128)(2,1)S(1)}, bf16[32,2048]{1,0:T(8,128)(2,1)S(1)}, u32[]{:S(2)}, u32[]{:S(2)}) collective-permute-start(bf16[32,2048]{1,0:T(8,128)(2,1)S(1)} %get-tuple-element.120), channel_id=1, source_target_pairs={{0,16},{8,24},{16,0},{24,8},{1,17},{9,25},{17,1},{25,9},{2,18},{10... | collective-permute-start | bytes 393224 | tf_op jit(solution)/shard_map/ppermute | solution.py:418
  49.7 1.3 %collective-permute-start.29 = (bf16[32,2048]{1,0:T(8,128)(2,1)S(1)}, bf16[32,2048]{1,0:T(8,128)(2,1)S(1)}, u32[]{:S(2)}, u32[]{:S(2)}) collective-permute-start(bf16[32,2048]{1,0:T(8,128)(2,1)S(1)} %get-tuple-element.121), channel_id=1, source_target_pairs={{0,8},{8,0},{16,24},{24,16},{1,9},{9,1},{17,25},{25,17},{2,10},{10... | collective-permute-start | bytes 393224 | tf_op jit(solution)/shard_map/ppermute | solution.py:418
  51.0 0.5 slice.7
  52.2 2.7 %collective-permute-done.27 = bf16[32,2048]{1,0:T(8,128)(2,1)S(1)} collective-permute-done((bf16[32,2048]{1,0:T(8,128)(2,1)S(1)}, bf16[32,2048]{1,0:T(8,128)(2,1)S(1)}, u32[]{:S(2)}, u32[]{:S(2)}) %collective-permute-start.27) | collective-permute-done | bytes 131104 | tf_op jit(solution)/shard_map/ppermute | solution.py:418
  54.8 2.6 %collective-permute-done.28 = bf16[32,2048]{1,0:T(8,128)(2,1)S(1)} collective-permute-done((bf16[32,2048]{1,0:T(8,128)(2,1)S(1)}, bf16[32,2048]{1,0:T(8,128)(2,1)S(1)}, u32[]{:S(2)}, u32[]{:S(2)}) %collective-permute-start.28) | collective-permute-done | bytes 131104 | tf_op jit(solution)/shard_map/ppermute | solution.py:418
  57.5 3.8 %conditional.1 = (bf16[1,1,512,2048]{3,2,1,0:T(8,128)(2,1)}) conditional(s32[]{:T(128)} %bitcast.6, (bf16[512,2048]{1,0:T(8,128)(2,1)S(1)}, bf16[512,128]{1,0:T(8,128)(2,1)S(1)}, bf16[32,2048]{1,0:T(8,128)(2,1)S(1)}, bf16[32,2048]{1,0:T(8,128)(2,1)S(1)}, bf16[32,2048]{1,0:T(8,128)(2,1)S(1)}, /*index=5*/bf16[32,2048]{1,0:T(8,128)(2,1)S(1)}) %tuple.13, ...), branch_computations={%region_0.0_spmd, %region_1.0_spmd} | conditional | flops 36105093120 | bytes 97780160 | solution.py:484
  57.5 3.6 %mix.2 = bf16[512,2048]{1,0:T(8,128)(2,1)} custom-call(bf16[512,2048]{1,0:T(8,128)(2,1)S(1)} %get-tuple-element.43.x_ref, bf16[512,128]{1,0:T(8,128)(2,1)S(1)} %get-tuple-element.44.mask_ref, bf16[32,2048]{1,0:T(8,128)(2,1)S(1)} %get-tuple-element.45.rest_0_, bf16[32,2048]{1,0:T(8,128)(2,1)S(1)} %get-tuple-element.46.rest_1_, ...), custom_call_target="tpu_custom_call" | custom-call | flops 536870912 | bytes 4194304 | tf_op jit(solution)/shard_map/cond/branch_0_fun/mix/pallas_call | solution.py:357
  (4 shorter events, 0.0 us)
Async XLA Ops:
  0.0 5.7 %collective-permute-start.13 = (s32[4,32]{1,0:T(4,128)}, s32[4,32]{1,0:T(4,128)S(1)}, u32[]{:S(2)}, u32[]{:S(2)}) collective-permute-start(s32[4,32]{1,0:T(4,128)} %bitcast.12), channel_id=1, source_target_pairs={{0,24},{8,16},{16,8},{24,0},{1,25},{9,17},{17,9},{25,1},{2,26},{10... | collective-permute-start | bytes 1544 | tf_op jit(solution)/shard_map/ppermute | solution.py:418
  3.9 3.8 %collective-permute-start.12 = (s32[4,32]{1,0:T(4,128)}, s32[4,32]{1,0:T(4,128)S(1)}, u32[]{:S(2)}, u32[]{:S(2)}) collective-permute-start(s32[4,32]{1,0:T(4,128)} %bitcast.13), channel_id=1, source_target_pairs={{0,16},{8,24},{16,0},{24,8},{1,17},{9,25},{17,1},{25,9},{2,18},{10... | collective-permute-start | bytes 1544 | tf_op jit(solution)/shard_map/ppermute | solution.py:418
  4.4 3.8 %collective-permute-start.11 = (s32[4,32]{1,0:T(4,128)}, s32[4,32]{1,0:T(4,128)S(1)}, u32[]{:S(2)}, u32[]{:S(2)}) collective-permute-start(s32[4,32]{1,0:T(4,128)} %bitcast.14), channel_id=1, source_target_pairs={{0,8},{8,0},{16,24},{24,16},{1,9},{9,1},{17,25},{25,17},{2,10},{10... | collective-permute-start | bytes 1544 | tf_op jit(solution)/shard_map/ppermute | solution.py:418
  8.5 4.8 %collective-permute-start.15 = (s32[8,128]{1,0:T(8,128)S(1)}, s32[8,128]{1,0:T(8,128)S(1)}, u32[]{:S(2)}, u32[]{:S(2)}) collective-permute-start(s32[8,128]{1,0:T(8,128)S(1)} %list.1.mine_ref), channel_id=1, source_target_pairs={{0,7},{1,2},{2,1},{3,4},{4,3},{5,6},{6,5},{7,0},{8,15},{9,10},{10,... | collective-permute-start | bytes 12296 | tf_op jit(solution)/shard_map/ppermute | solution.py:424
  9.9 3.5 %collective-permute-start.14 = (s32[8,128]{1,0:T(8,128)S(1)}, s32[8,128]{1,0:T(8,128)S(1)}, u32[]{:S(2)}, u32[]{:S(2)}) collective-permute-start(s32[8,128]{1,0:T(8,128)S(1)} %list.1.mine_ref), channel_id=1, source_target_pairs={{0,1},{1,0},{2,3},{3,2},{4,5},{5,4},{6,7},{7,6},{8,9},{9,8},{10,11... | collective-permute-start | bytes 12296 | tf_op jit(solution)/shard_map/ppermute | solution.py:433
  14.1 9.6 %collective-permute-start.16 = (bf16[48,2048]{1,0:T(8,128)(2,1)S(1)}, bf16[48,2048]{1,0:T(8,128)(2,1)S(1)}, u32[]{:S(2)}, u32[]{:S(2)}) collective-permute-start(bf16[48,2048]{1,0:T(8,128)(2,1)S(1)} %get-tuple-element.99.far_ref), channel_id=1, source_target_pairs={{0,7},{7,0},{8,15},{15,8},{16,23},{23,16},{24,31},{31,24}} | collective-permute-start | bytes 589832 | tf_op jit(solution)/shard_map/ppermute | solution.py:427
  18.8 4.9 %collective-permute-start.17 = (bf16[48,2048]{1,0:T(8,128)(2,1)S(1)}, bf16[48,2048]{1,0:T(8,128)(2,1)S(1)}, u32[]{:S(2)}, u32[]{:S(2)}) collective-permute-start(bf16[48,2048]{1,0:T(8,128)(2,1)S(1)} %get-tuple-element.102), channel_id=1, source_target_pairs={{1,2},{2,1},{3,4},{4,3},{5,6},{6,5},{9,10},{10,9},{11,12},{12,11},... | collective-permute-start | bytes 589832 | tf_op jit(solution)/shard_map/ppermute | solution.py:430
  19.5 4.5 %collective-permute-start.18 = (bf16[128,2048]{1,0:T(8,128)(2,1)S(1)}, bf16[128,2048]{1,0:T(8,128)(2,1)S(1)}, u32[]{:S(2)}, u32[]{:S(2)}) collective-permute-start(bf16[128,2048]{1,0:T(8,128)(2,1)S(1)} %get-tuple-element.104), channel_id=1, source_target_pairs={{0,1},{1,0},{2,3},{3,2},{4,5},{5,4},{6,7},{7,6},{8,9},{9,8},{10,11... | collective-permute-start | bytes 1572872 | tf_op jit(solution)/shard_map/ppermute | solution.py:433
  24.0 8.3 %collective-permute-start.19 = (bf16[32,2048]{1,0:T(8,128)(2,1)S(1)}, bf16[32,2048]{1,0:T(8,128)(2,1)S(1)}, u32[]{:S(2)}, u32[]{:S(2)}) collective-permute-start(bf16[32,2048]{1,0:T(8,128)(2,1)S(1)} %get-tuple-element.106), channel_id=1, source_target_pairs={{0,24},{8,16},{16,8},{24,0},{1,25},{9,17},{17,9},{25,1},{2,26},{10... | collective-permute-start | bytes 393224 | tf_op jit(solution)/shard_map/ppermute | solution.py:418
  25.6 8.2 %collective-permute-start.20 = (bf16[32,2048]{1,0:T(8,128)(2,1)S(1)}, bf16[32,2048]{1,0:T(8,128)(2,1)S(1)}, u32[]{:S(2)}, u32[]{:S(2)}) collective-permute-start(bf16[32,2048]{1,0:T(8,128)(2,1)S(1)} %get-tuple-element.107), channel_id=1, source_target_pairs={{0,16},{8,24},{16,0},{24,8},{1,17},{9,25},{17,1},{25,9},{2,18},{10... | collective-permute-start | bytes 393224 | tf_op jit(solution)/shard_map/ppermute | solution.py:418
  25.7 8.2 %collective-permute-start.21 = (bf16[32,2048]{1,0:T(8,128)(2,1)S(1)}, bf16[32,2048]{1,0:T(8,128)(2,1)S(1)}, u32[]{:S(2)}, u32[]{:S(2)}) collective-permute-start(bf16[32,2048]{1,0:T(8,128)(2,1)S(1)} %get-tuple-element.108), channel_id=1, source_target_pairs={{0,8},{8,0},{16,24},{24,16},{1,9},{9,1},{17,25},{25,17},{2,10},{10... | collective-permute-start | bytes 393224 | tf_op jit(solution)/shard_map/ppermute | solution.py:418
  27.6 3.0 %collective-permute-start.23 = (s32[8,128]{1,0:T(8,128)S(1)}, s32[8,128]{1,0:T(8,128)S(1)}, u32[]{:S(2)}, u32[]{:S(2)}) collective-permute-start(s32[8,128]{1,0:T(8,128)S(1)} %get-tuple-element.110.rest_4_), channel_id=1, source_target_pairs={{0,5},{1,6},{2,7},{3,0},{4,1},{5,2},{6,3},{7,4},{8,13},{9,14},{10,... | collective-permute-start | bytes 12296 | tf_op jit(solution)/shard_map/ppermute | solution.py:421
  28.3 3.9 %collective-permute-start.22 = (s32[8,128]{1,0:T(8,128)S(1)}, s32[8,128]{1,0:T(8,128)S(1)}, u32[]{:S(2)}, u32[]{:S(2)}) collective-permute-start(s32[8,128]{1,0:T(8,128)S(1)} %get-tuple-element.110.rest_4_), channel_id=1, source_target_pairs={{0,3},{1,4},{2,5},{3,6},{4,7},{5,0},{6,1},{7,2},{8,11},{9,12},{10,... | collective-permute-start | bytes 12296 | tf_op jit(solution)/shard_map/ppermute | solution.py:421
  36.6 10.5 %collective-permute-start.24 = (bf16[48,2048]{1,0:T(8,128)(2,1)S(1)}, bf16[48,2048]{1,0:T(8,128)(2,1)S(1)}, u32[]{:S(2)}, u32[]{:S(2)}) collective-permute-start(bf16[48,2048]{1,0:T(8,128)(2,1)S(1)} %get-tuple-element.111.far_ref), channel_id=1, source_target_pairs={{0,7},{7,0},{8,15},{15,8},{16,23},{23,16},{24,31},{31,24}} | collective-permute-start | bytes 589832 | tf_op jit(solution)/shard_map/ppermute | solution.py:427
  40.2 6.9 %collective-permute-start.25 = (bf16[48,2048]{1,0:T(8,128)(2,1)S(1)}, bf16[48,2048]{1,0:T(8,128)(2,1)S(1)}, u32[]{:S(2)}, u32[]{:S(2)}) collective-permute-start(bf16[48,2048]{1,0:T(8,128)(2,1)S(1)} %get-tuple-element.114), channel_id=1, source_target_pairs={{1,2},{2,1},{3,4},{4,3},{5,6},{6,5},{9,10},{10,9},{11,12},{12,11},... | collective-permute-start | bytes 589832 | tf_op jit(solution)/shard_map/ppermute | solution.py:430
  40.9 6.5 %collective-permute-start.26 = (bf16[128,2048]{1,0:T(8,128)(2,1)S(1)}, bf16[128,2048]{1,0:T(8,128)(2,1)S(1)}, u32[]{:S(2)}, u32[]{:S(2)}) collective-permute-start(bf16[128,2048]{1,0:T(8,128)(2,1)S(1)} %get-tuple-element.116), channel_id=1, source_target_pairs={{0,1},{1,0},{2,3},{3,2},{4,5},{5,4},{6,7},{7,6},{8,9},{9,8},{10,11... | collective-permute-start | bytes 1572872 | tf_op jit(solution)/shard_map/ppermute | solution.py:433
  47.4 7.4 %collective-permute-start.27 = (bf16[32,2048]{1,0:T(8,128)(2,1)S(1)}, bf16[32,2048]{1,0:T(8,128)(2,1)S(1)}, u32[]{:S(2)}, u32[]{:S(2)}) collective-permute-start(bf16[32,2048]{1,0:T(8,128)(2,1)S(1)} %get-tuple-element.119), channel_id=1, source_target_pairs={{0,24},{8,16},{16,8},{24,0},{1,25},{9,17},{17,9},{25,1},{2,26},{10... | collective-permute-start | bytes 393224 | tf_op jit(solution)/shard_map/ppermute | solution.py:418
  48.8 8.7 %collective-permute-start.28 = (bf16[32,2048]{1,0:T(8,128)(2,1)S(1)}, bf16[32,2048]{1,0:T(8,128)(2,1)S(1)}, u32[]{:S(2)}, u32[]{:S(2)}) collective-permute-start(bf16[32,2048]{1,0:T(8,128)(2,1)S(1)} %get-tuple-element.120), channel_id=1, source_target_pairs={{0,16},{8,24},{16,0},{24,8},{1,17},{9,25},{17,1},{25,9},{2,18},{10... | collective-permute-start | bytes 393224 | tf_op jit(solution)/shard_map/ppermute | solution.py:418
  49.7 7.8 %collective-permute-start.29 = (bf16[32,2048]{1,0:T(8,128)(2,1)S(1)}, bf16[32,2048]{1,0:T(8,128)(2,1)S(1)}, u32[]{:S(2)}, u32[]{:S(2)}) collective-permute-start(bf16[32,2048]{1,0:T(8,128)(2,1)S(1)} %get-tuple-element.121), channel_id=1, source_target_pairs={{0,8},{8,0},{16,24},{24,16},{1,9},{9,1},{17,25},{25,17},{2,10},{10... | collective-permute-start | bytes 393224 | tf_op jit(solution)/shard_map/ppermute | solution.py:418

commit v10 on v7

--- a/solution.py
+++ b/solution.py
@@ -7,9 +7,11 @@
 from jax.experimental.pallas import tpu as pltpu
 from jax.sharding import PartitionSpec as P
 
-ROUNDS = 2
 LANES = 128
 BLOCK = 128
+LAST_BLOCK = 256
+CHUNK = 32
+BOTH_LAST = (((1,), (1,)), ((), ()))
 
 
 FAR_SHARE = 3, 8
@@ -194,8 +196,8 @@
     )(x, mine, within, beyond)
 
 
-def near_kernel(x_ref, pack_ref, mine_ref, within_ref, *out_refs):
-    select_ref, expand_ref, core_ref, own_ref, rest_ref = out_refs
+def near_kernel(x_ref, pack_ref, mask_ref, mine_ref, within_ref, *out_refs):
+    expand_ref, core_ref, own_ref, rest_ref, near_mask_ref, far_mask_ref, select_ref = out_refs
     rows, total = x_ref.shape[0], mine_ref.shape[1]
     third = lax.axis_index("rep") % 2 * 2
     own = mine_ref[0:1]
@@ -206,6 +208,9 @@
     rest = total - rest_ref.shape[0]
     serve(x, pack_ref.at[rest:], rest_ref)
     from_far = one_hot(own, third, rows)
+    mask = mask_ref[...]
+    serve(mask, select_ref, near_mask_ref)
+    serve(mask, pack_ref, far_mask_ref)
     expand_ref[...] = lax.dot_general(
         from_far.astype(jnp.bfloat16),
         packing(from_far, rows),
@@ -214,42 +219,26 @@
     ).astype(jnp.bfloat16)
 
 
-def near_call(x, pack, mine, within, sent):
+def near_call(x, pack, mask, mine, within, sent):
     rows, width = x.shape
     total = mine.shape[1]
     return pl.pallas_call(
         near_kernel,
         out_shape=[
-            bf16(2 * total, rows),
             bf16(total, total),
             bf16(total, width),
             bf16(total, width),
             bf16(total - sent, width),
+            bf16(2 * total, total),
+            bf16(total, total),
         ],
+        scratch_shapes=[pltpu.VMEM((2 * total, rows), jnp.bfloat16)],
         compiler_params=params(),
         cost_estimate=pl.CostEstimate(
             flops=6 * total * rows * width, bytes_accessed=4 * rows * width, transcendentals=0
         ),
         name="serve_near",
-    )(x, pack, mine, within)
-
-
-def again_kernel(x_ref, select_ref, core_ref, own_ref):
-    serve(x_ref[...], select_ref, core_ref, own_ref)
-
-
-def again_call(x, select):
-    rows, width = x.shape
-    total = select.shape[0] // 2
-    return pl.pallas_call(
-        again_kernel,
-        out_shape=[bf16(total, width)] * 2,
-        compiler_params=params(),
-        cost_estimate=pl.CostEstimate(
-            flops=4 * total * rows * width, bytes_accessed=4 * rows * width, transcendentals=0
-        ),
-        name="serve_again",
-    )(x, select)
+    )(x, pack, mask, mine, within)
 
 
 def unpack_kernel(first, expand_ref, far_ref, *refs):
@@ -284,7 +273,7 @@
     total, width = base.shape
     most, *parts = pl.pallas_call(
         combine_kernel,
-        out_shape=[jax.ShapeDtypeStruct(most.shape, most.dtype)]
+        out_shape=[jax.ShapeDtypeStruct(most.shape, jnp.int32)]
         + [bf16(total // servers, width)] * servers,
         compiler_params=params(),
         cost_estimate=pl.CostEstimate(
@@ -302,32 +291,129 @@
 
 
 def weigh(x, buffer, mask):
-    sims = lax.dot_general(x, buffer, (((1,), (1,)), ((), ())), preferred_element_type=jnp.float32)
-    positive = jnp.maximum(sims * (1.0 / x.shape[1]), 0.0)
-    return (positive * positive * positive).astype(jnp.bfloat16) * mask
-
-
-def add_up(x, weights, buffer):
+    dots = lax.dot_general(x, buffer, BOTH_LAST, preferred_element_type=jnp.float32)
+    positive = jnp.maximum(dots * (1.0 / x.shape[1]), 0.0)
+    return (positive * positive * positive).astype(jnp.bfloat16) * mask, dots
+
+
+def mix(x, weights, buffer):
     mixed = x.astype(jnp.float32) + jnp.dot(weights, buffer, preferred_element_type=jnp.float32)
     return normalize(mixed).astype(jnp.bfloat16)
 
 
-def last_kernel(servers, x_ref, mask_ref, *rest):
+def far_mix_kernel(servers, x_ref, mask_ref, *rest):
     parts, rest = rest[:servers], rest[servers:]
-    out_ref, buffer, weights, whole, sems = rest
+    *most_refs, out_ref, most_ref, buffer = rest
+    most_ref[...] = functools.reduce(jnp.maximum, [ref[...] for ref in most_refs])
     fill(buffer, parts)
-    weights[...] = weigh(x_ref[...], buffer[...], mask_ref[...])
+    weights, _ = weigh(x_ref[...], buffer[...], mask_ref[: x_ref.shape[0]])
+    out_ref[...] = mix(x_ref[...], weights, buffer[...])
+
+
+def far_mix_call(x, mask, parts, mosts):
+    rows, width = x.shape
+    total, servers = mask.shape[1], len(parts)
+    return pl.pallas_call(
+        functools.partial(far_mix_kernel, servers),
+        out_shape=[bf16(rows, width), jax.ShapeDtypeStruct(mosts[0].shape, jnp.int32)],
+        scratch_shapes=[pltpu.VMEM((total, width), jnp.bfloat16)],
+        compiler_params=params(),
+        cost_estimate=pl.CostEstimate(
+            flops=4 * total * rows * width, bytes_accessed=4 * rows * width, transcendentals=rows
+        ),
+        name="mix_far",
+    )(x, mask, *reversed(parts), *mosts)
+
+
+def near_mix_kernel(servers, core_ref, own_ref, mask_ref, *rest):
+    parts, (new_core_ref, new_own_ref, buffer) = rest[:servers], rest[servers:]
+    fill(buffer, parts)
+    total = core_ref.shape[0]
+    for i, (x_ref, out_ref) in enumerate([(core_ref, new_core_ref), (own_ref, new_own_ref)]):
+        mask = mask_ref[i * total : (i + 1) * total]
+        weights, _ = weigh(x_ref[...], buffer[...], mask)
+        out_ref[...] = mix(x_ref[...], weights, buffer[...])
+
+
+def near_mix_call(core, own, mask, parts):
+    total, width = core.shape
+    servers = len(parts)
+    return pl.pallas_call(
+        functools.partial(near_mix_kernel, servers),
+        out_shape=[bf16(total, width)] * 2,
+        scratch_shapes=[pltpu.VMEM((total, width), jnp.bfloat16)],
+        compiler_params=params(),
+        cost_estimate=pl.CostEstimate(
+            flops=8 * total * total * width, bytes_accessed=8 * total * width, transcendentals=0
+        ),
+        name="mix_near",
+    )(core, own, mask, *reversed(parts))
+
+
+def squared(x):
+    x = x.astype(jnp.float32)
+    return sum(x[:, i : i + LANES] * x[:, i : i + LANES] for i in range(0, x.shape[1], LANES))
+
+
+def whole_kernel(servers, x_ref, mask_ref, *rest):
+    parts, (out_ref, squares_ref, buffer, weights) = rest[:servers], rest[servers:]
+    fill(buffer, parts)
+    weights[...], _ = weigh(x_ref[...], buffer[...], mask_ref[...])
+    for start in range(0, x_ref.shape[0], BLOCK):
+        here = slice(start, start + BLOCK)
+        out_ref[here] = mix(x_ref[here], weights[here], buffer[...])
+    for start in range(0, x_ref.shape[0], CHUNK):
+        here = slice(start, start + CHUNK)
+        squares_ref[here] = squared(out_ref[here])
+
+
+def whole_call(x, mask, parts):
+    rows, width = x.shape
+    total, servers = mask.shape[1], len(parts)
+    return pl.pallas_call(
+        functools.partial(whole_kernel, servers),
+        out_shape=[bf16(rows, width), jax.ShapeDtypeStruct((rows, LANES), jnp.float32)],
+        scratch_shapes=[
+            pltpu.VMEM((total, width), jnp.bfloat16),
+            pltpu.VMEM((rows, total), jnp.bfloat16),
+        ],
+        compiler_params=params(),
+        cost_estimate=pl.CostEstimate(
+            flops=4 * total * rows * width, bytes_accessed=4 * rows * width, transcendentals=rows
+        ),
+        name="mix_whole",
+    )(x, mask, *reversed(parts))
+
+
+def last_kernel(servers, x_ref, mask_ref, squares_ref, *rest):
+    parts, rest = rest[:servers], rest[servers:]
+    out_ref, buffer, whole, sems = rest
+    rows, width = x_ref.shape
+    fill(buffer, parts)
+    b = buffer[...]
+    gram = lax.dot_general(b, b, BOTH_LAST, preferred_element_type=jnp.float32)
+    high = gram.astype(jnp.bfloat16)
+    low = (gram - high.astype(jnp.float32)).astype(jnp.bfloat16)
+    weights, dots = weigh(x_ref[...], b, mask_ref[...])
+    crossed = jnp.dot(weights, high, preferred_element_type=jnp.float32)
+    crossed += jnp.dot(weights, low, preferred_element_type=jnp.float32)
+    added = jnp.sum(weights.astype(jnp.float32) * (2.0 * dots + crossed), axis=1, keepdims=True)
+    square = jnp.sum(squares_ref[...], axis=1, keepdims=True) + added
+    scale = lax.rsqrt(square * (1.0 / width) + 1e-06)
     copies = []
-    for i, start in enumerate(range(0, x_ref.shape[0], BLOCK)):
-        here = pl.ds(start, BLOCK)
-        whole[here] = add_up(x_ref[here], weights[here], buffer[...])
-        copies.append(pltpu.make_async_copy(whole.at[here], out_ref.at[here], sems.at[i]))
+    for i, start in enumerate(range(0, rows, LAST_BLOCK)):
+        here = slice(start, start + LAST_BLOCK)
+        mixed = jnp.dot(weights[here], b, preferred_element_type=jnp.float32)
+        mixed += x_ref[here].astype(jnp.float32)
+        whole[here] = (mixed * scale[here]).astype(jnp.bfloat16)
+        block = pl.ds(start, LAST_BLOCK)
+        copies.append(pltpu.make_async_copy(whole.at[block], out_ref.at[block], sems.at[i]))
         copies[-1].start()
     for copy in copies:
         copy.wait()
 
 
-def last_call(x, mask, parts):
+def last_call(x, mask, squares, parts):
     rows, width = x.shape
     total, servers = mask.shape[1], len(parts)
     return pl.pallas_call(
@@ -336,50 +422,15 @@
         out_shape=pltpu.HBM((rows, width), jnp.bfloat16),
         scratch_shapes=[
             pltpu.VMEM((total, width), jnp.bfloat16),
-            pltpu.VMEM((rows, total), jnp.bfloat16),
             pltpu.VMEM((rows, width), jnp.bfloat16),
-            pltpu.SemaphoreType.DMA((rows // BLOCK,)),
+            pltpu.SemaphoreType.DMA((rows // LAST_BLOCK,)),
         ],
         compiler_params=params(),
         cost_estimate=pl.CostEstimate(
             flops=4 * total * rows * width, bytes_accessed=4 * rows * width, transcendentals=rows
         ),
         name="mix",
-    )(x, mask, *reversed(parts))
-
-
-def round_kernel(servers, x_ref, mask_ref, pack_ref, *rest):
-    parts, rest = rest[:servers], rest[servers:]
-    *most_refs, out_ref, far_ref, most_ref, buffer, weights = rest
-    most_ref[...] = functools.reduce(jnp.maximum, [ref[...] for ref in most_refs])
-    fill(buffer, parts)
-    weights[...] = weigh(x_ref[...], buffer[...], mask_ref[...])
-    for start in range(0, x_ref.shape[0], BLOCK):
-        stop = start + BLOCK
-        out_ref[start:stop] = add_up(x_ref[start:stop], weights[start:stop], buffer[...])
-    serve(out_ref[...], pack_ref, far_ref)
-
-
-def round_call(x, mask, pack, parts, mosts, sent):
-    rows, width = x.shape
-    total, servers = mask.shape[1], len(parts)
-    return pl.pallas_call(
-        functools.partial(round_kernel, servers),
-        out_shape=[
-            bf16(rows, width),
-            bf16(sent, width),
-            jax.ShapeDtypeStruct((8, LANES), jnp.int32),
-        ],
-        scratch_shapes=[
-            pltpu.VMEM((total, width), jnp.bfloat16),
-            pltpu.VMEM((rows, total), jnp.bfloat16),
-        ],
-        compiler_params=params(),
-        cost_estimate=pl.CostEstimate(
-            flops=5 * total * rows * width, bytes_accessed=6 * rows * width, transcendentals=rows
-        ),
-        name="mix_and_pack",
-    )(x, mask, pack, *reversed(parts), *mosts)
+    )(x, mask, squares, *reversed(parts))
 
 
 def local(descriptors, request, pick):
@@ -404,31 +455,31 @@
     def inside(value):
         return lax.ppermute(value, "rep", within)
 
-    def exchange(base, core, most):
-        most, parts = combine_call(base, core, most, servers)
-        return most, turned(parts)
-
     def turned(parts):
         got = {d: turn(parts[d], d) for d in reversed(range(1, servers))}
         return [parts[0]] + [got[d] for d in range(1, servers)]
 
-    def next_parts(x, far, select, expand, most):
-        far = across(far)
-        core, own = again_call(x, select)
-        core = inside(core)
-        return exchange(unpack_call(expand, far, own), core, most)
-
-    def in_full(raw, x, rest, mask, pack, select, expand, most, first, last):
+    def exchange(expand, far, core, own, most):
+        base = unpack_call(expand, across(far), own)
+        most, parts = combine_call(base, inside(core), most, servers)
+        return most, turned(parts)
+
+    def next_parts(served, masks, expand, parts, mosts):
+        far, core, own = served
+        far, most = far_mix_call(far, masks[1], parts, mosts)
+        core, own = near_mix_call(core, own, masks[2], parts)
+        return exchange(expand, far, core, own, most)
+
+    def in_full(x, y, squares, masks, served, rest, expand, most, first, last):
         late = unpack_call(expand, across(rest), first=sent).reshape(servers, cap, -1)
-        parts = [a + b for a, b in zip(first, turned(list(late)))]
-        x = raw
-        for _ in range(ROUNDS - 1):
-            x, far, most = round_call(x, mask, pack, parts, [most], total)
-            most, parts = next_parts(x, far, select, expand, most)
-        return last_call(x, mask, parts)
-
-    def as_sent(raw, x, rest, mask, pack, select, expand, most, first, last):
-        return last_call(x, mask, last)
+        first = [a + b for a, b in zip(first, turned(list(late)))]
+        served = jnp.concatenate([served[0], rest], axis=0), *served[1:]
+        _, last = next_parts(served, masks, expand, first, [most])
+        y, squares = whole_call(x, masks[0], first)
+        return last_call(y, masks[0], squares, last)
+
+    def as_sent(x, y, squares, masks, served, rest, expand, most, first, last):
+        return last_call(y, masks[0], squares, last)
 
     asked = {d: turn(wanted, d) for d in reversed(range(1, servers))}
     mask, held = mask_call(pick.transpose(0, 3, 1, 2)[0], wanted)
@@ -436,10 +487,10 @@
     beyond_list, within_list = across(mine), inside(mine)
     x = normalize_call(descriptors[0, 0])
     pack, most, far = far_call(x, mine, within_list, beyond_list, sent)
-    far = across(far)
-    select, expand, core, own, rest = near_call(x, pack, mine, within_list, sent)
-    core = inside(core)
-    most, first = exchange(unpack_call(expand, far, own), core, most)
+    expand, core, own, rest, near_mask, far_mask = near_call(
+        x, pack, mask, mine, within_list, sent
+    )
+    most, first = exchange(expand, far, core, own, most)
     mosts = [most]
     reach = 1
     while 2 * reach + 1 < groups:
@@ -447,12 +498,10 @@
         most = functools.reduce(jnp.maximum, mosts)
         mosts = [most, shift(most, by), shift(most, -by)]
         reach += by
-    mixed, parts = x, first
-    for _ in range(ROUNDS - 1):
-        mixed, far, most = round_call(mixed, mask, pack, parts, mosts, sent)
-        most, parts = next_parts(mixed, far, select, expand, most)
-        mosts = [most]
-    state = x, mixed, rest, mask, pack, select, expand, most, first, parts
+    masks, served = (mask, far_mask, near_mask), (far, core, own)
+    most, last = next_parts(served, masks, expand, first, mosts)
+    y, squares = whole_call(x, mask, first)
+    state = x, y, squares, masks, served, rest, expand, most, first, last
     return lax.cond(most[0, 0] > sent, in_full, as_sent, *state)[None, None]
 
 

time: 53.2 us -> 52.1 us (0.979)
  waiting for transfers between devices: 20.5 us -> 13.4 us
  starting transfers between devices: 17.8 us -> 22.4 us
  Pallas kernels: 13.1 us -> 14.5 us
    ppermute x3, starting transfers between devices: 3.95 us -> 8 us  [across(): return lax.ppermute(value, 'rep', beyond)]
    ppermute x3, waiting for transfers between devices: 12.6 us -> 8.77 us  [across(): return lax.ppermute(value, 'rep', beyond)]
    ppermute x9, waiting for transfers between devices: 5.69 us -> 3.28 us  [turn(): return lax.ppermute(value, 'clus', [(c, c ^ d) for c in range(servers)])]
    pallas_call x3 -> x4, Pallas kernels: 5.19 us -> 6.47 us  [the longest x1 2.75 us: whole_call(): pl.pallas_call(functools.partial(whole_kernel, servers), out_shape=[bf16(...]
    ppermute x2, starting transfers between devices: 1.75 us -> 2.64 us  [shift(): lax.ppermute(value, 'rep', [(g, (g + by) % groups) for g in range(groups)])]
    ppermute x2, waiting for transfers between devices: 2.19 us -> 1.33 us  [shift(): lax.ppermute(value, 'rep', [(g, (g + by) % groups) for g in range(groups)])]
  transfers between devices with their start and end apart: 17 -> 17, of which waited for: 11 -> 7; matrix products, arithmetic and copies ran while one was open for 1% -> 1% of each run, Pallas kernels for 11% -> 18%
where the time goes in v10:
time: 52.1 us; the launch traced here: 51.9 us
  starting transfers between devices  22.4 us (43%)
  Pallas kernels  14.5 us (28%)
  waiting for transfers between devices  13.4 us (26%)
  between operations  0.98 us (2%)
    ppermute x9, starting transfers between devices, turn(): return lax.ppermute(value, 'clus', [(c, c ^ d) for c in range(servers)])  11.6 us
    ppermute x3, waiting for transfers between devices, across(): return lax.ppermute(value, 'rep', beyond)  8.77 us
    ppermute x3, starting transfers between devices, across(): return lax.ppermute(value, 'rep', beyond)  8 us
    pallas_call x1, Pallas kernels, last_call(): pl.pallas_call(functools.partial(last_kernel, servers), out_specs=pl.Bloc...  3.43 us
    ppermute x9, waiting for transfers between devices, turn(): return lax.ppermute(value, 'clus', [(c, c ^ d) for c in range(servers)])  3.28 us
    pallas_call x1, Pallas kernels, whole_call(): pl.pallas_call(functools.partial(whole_kernel, servers), out_shape=[bf16(...  2.75 us
    ppermute x2, starting transfers between devices, shift(): lax.ppermute(value, 'rep', [(g, (g + by) % groups) for g in range(groups)])  2.64 us
    pallas_call x1, Pallas kernels, normalize_call(): pl.pallas_call(normalize_kernel, in_specs=[pl.BlockSpec(memory_space=pl.A...  1.87 us
  transfers between devices with their start and end apart: 17, of which 7 were waited for; matrix products, arithmetic and copies ran while one was open for 1% of the time, Pallas kernels for 18%

profile of v10, /device:TPU:0, one launch (start us, length us, event | category | flops | bytes accessed | tf_op | source)
XLA Modules:
  0.0 51.9 jit_solution(7756129068448536337)
XLA Ops:
  0.0 3.0 %collective-permute-start.10 = (s32[4,32]{1,0:T(4,128)}, s32[4,32]{1,0:T(4,128)S(1)}, u32[]{:S(2)}, u32[]{:S(2)}) collective-permute-start(s32[4,32]{1,0:T(4,128)} %bitcast.12), channel_id=1, source_target_pairs={{0,16},{8,24},{16,0},{24,8},{1,17},{9,25},{17,1},{25,9},{2,18},{10... | collective-permute-start | bytes 1544 | tf_op jit(solution)/shard_map/ppermute | solution.py:447
  3.0 1.4 %collective-permute-start.11 = (s32[4,32]{1,0:T(4,128)}, s32[4,32]{1,0:T(4,128)S(1)}, u32[]{:S(2)}, u32[]{:S(2)}) collective-permute-start(s32[4,32]{1,0:T(4,128)} %bitcast.13), channel_id=1, source_target_pairs={{0,24},{8,16},{16,8},{24,0},{1,25},{9,17},{17,9},{25,1},{2,26},{10... | collective-permute-start | bytes 1544 | tf_op jit(solution)/shard_map/ppermute | solution.py:447
  4.4 0.1 collective-permute-start.9
  4.5 1.0 %mask.1 = (bf16[512,128]{1,0:T(8,128)(2,1)S(1)}, s32[4,32]{1,0:T(4,128)S(1)}) custom-call(s32[10,1,512]{2,1,0:T(1,128)} %bitcast.11, s32[4,32]{1,0:T(4,128)} %bitcast.15), custom_call_target="tpu_custom_call" | custom-call | flops 1310720 | bytes 131072 | tf_op jit(solution)/shard_map/mask/pallas_call | solution.py:84
  5.5 0.0 collective-permute-done.10.refs_2_
  5.5 2.2 %collective-permute-done.11.refs_3_ = s32[4,32]{1,0:T(4,128)S(1)} collective-permute-done((s32[4,32]{1,0:T(4,128)}, s32[4,32]{1,0:T(4,128)S(1)}, u32[]{:S(2)}, u32[]{:S(2)}) %collective-permute-start.11) | collective-permute-done | bytes 544 | tf_op jit(solution)/shard_map/ppermute | solution.py:447
  7.7 0.5 %collective-permute-done.9.refs_1_ = s32[4,32]{1,0:T(4,128)S(1)} collective-permute-done((s32[4,32]{1,0:T(4,128)}, s32[4,32]{1,0:T(4,128)S(1)}, u32[]{:S(2)}, u32[]{:S(2)}) %collective-permute-start.9) | collective-permute-done | bytes 544 | tf_op jit(solution)/shard_map/ppermute | solution.py:447
  8.2 0.3 list.1.mine_ref
  8.5 0.0 collective-permute-start.12
  8.5 3.7 %collective-permute-start.13 = (s32[8,128]{1,0:T(8,128)S(1)}, s32[8,128]{1,0:T(8,128)S(1)}, u32[]{:S(2)}, u32[]{:S(2)}) collective-permute-start(s32[8,128]{1,0:T(8,128)S(1)} %list.1.mine_ref), channel_id=1, source_target_pairs={{0,7},{1,2},{2,1},{3,4},{4,3},{5,6},{6,5},{7,0},{8,15},{9,10},{10,... | collective-permute-start | bytes 12296 | tf_op jit(solution)/shard_map/ppermute | solution.py:453
  12.3 1.9 %normalize.1.x_ref = bf16[512,2048]{1,0:T(8,128)(2,1)S(1)} custom-call(bf16[512,2048]{1,0:T(8,128)(2,1)} %bitcast.8), custom_call_target="tpu_custom_call" | custom-call | flops 6291456 | bytes 4194304 | tf_op jit(solution)/shard_map/normalize/pallas_call | solution.py:47
  14.1 0.0 collective-permute-done.12.within_ref
  14.1 0.0 collective-permute-done.13.beyond_ref
  14.1 0.7 %pack_far.1 = (bf16[128,512]{1,0:T(8,128)(2,1)S(1)}, s32[8,128]{1,0:T(8,128)S(1)}, bf16[48,2048]{1,0:T(8,128)(2,1)S(1)}) custom-call(bf16[512,2048]{1,0:T(8,128)(2,1)S(1)} %normalize.1.x_ref, s32[8,128]{1,0:T(8,128)S(1)} %list.1.mine_ref, s32[8,128]{1,0:T(8,128)S(1)} %collective-permute-done.12.within_ref, s32[8,128]{1,0:T(8,128)S(1)} %collective-permute-done.13.beyond_ref), custom_call_target="tpu_custom_call" | custom-call | flops 67108864 | bytes 2097152 | tf_op jit(solution)/shard_map/pack_far/pallas_call | solution.py:184
  14.9 3.0 %collective-permute-start.14 = (bf16[48,2048]{1,0:T(8,128)(2,1)S(1)}, bf16[48,2048]{1,0:T(8,128)(2,1)S(1)}, u32[]{:S(2)}, u32[]{:S(2)}) collective-permute-start(bf16[48,2048]{1,0:T(8,128)(2,1)S(1)} %get-tuple-element.113.x_ref), channel_id=1, source_target_pairs={{0,7},{1,2},{2,1},{3,4},{4,3},{5,6},{6,5},{7,0},{8,15},{9,10},{10,... | collective-permute-start | bytes 589832 | tf_op jit(solution)/shard_map/ppermute | solution.py:453
  17.8 1.5 %serve_near.1 = (bf16[128,128]{1,0:T(8,128)(2,1)S(1)}, bf16[128,2048]{1,0:T(8,128)(2,1)S(1)}, bf16[128,2048]{1,0:T(8,128)(2,1)S(1)}, bf16[80,2048]{1,0:T(8,128)(...) custom-call(bf16[512,2048]{1,0:T(8,128)(2,1)S(1)} %normalize.1.x_ref, ...), custom_call_target="tpu_custom_call" | custom-call | flops 805306368 | bytes 4194304 | tf_op jit(solution)/shard_map/serve_near/pallas_call | solution.py:225
  19.3 0.1 collective-permute-start.15
  19.4 2.9 %collective-permute-done.14.far_ref = bf16[48,2048]{1,0:T(8,128)(2,1)S(1)} collective-permute-done((bf16[48,2048]{1,0:T(8,128)(2,1)S(1)}, bf16[48,2048]{1,0:T(8,128)(2,1)S(1)}, u32[]{:S(2)}, u32[]{:S(2)}) %collective-permute-start.14) | collective-permute-done | bytes 196640 | tf_op jit(solution)/shard_map/ppermute | solution.py:453
  22.4 0.3 unpack.6.base_ref
  22.6 0.0 collective-permute-done.15.core_ref
  22.7 0.1 combine.4
  22.7 1.6 %collective-permute-start.16 = (bf16[32,2048]{1,0:T(8,128)(2,1)S(1)}, bf16[32,2048]{1,0:T(8,128)(2,1)S(1)}, u32[]{:S(2)}, u32[]{:S(2)}) collective-permute-start(bf16[32,2048]{1,0:T(8,128)(2,1)S(1)} %get-tuple-element.118), channel_id=1, source_target_pairs={{0,24},{8,16},{16,8},{24,0},{1,25},{9,17},{17,9},{25,1},{2,26},{10... | collective-permute-start | bytes 393224 | tf_op jit(solution)/shard_map/ppermute | solution.py:447
  24.3 0.9 %collective-permute-start.17 = (bf16[32,2048]{1,0:T(8,128)(2,1)S(1)}, bf16[32,2048]{1,0:T(8,128)(2,1)S(1)}, u32[]{:S(2)}, u32[]{:S(2)}) collective-permute-start(bf16[32,2048]{1,0:T(8,128)(2,1)S(1)} %get-tuple-element.119), channel_id=1, source_target_pairs={{0,16},{8,24},{16,0},{24,8},{1,17},{9,25},{17,1},{25,9},{2,18},{10... | collective-permute-start | bytes 393224 | tf_op jit(solution)/shard_map/ppermute | solution.py:447
  25.2 1.1 %collective-permute-start.18 = (bf16[32,2048]{1,0:T(8,128)(2,1)S(1)}, bf16[32,2048]{1,0:T(8,128)(2,1)S(1)}, u32[]{:S(2)}, u32[]{:S(2)}) collective-permute-start(bf16[32,2048]{1,0:T(8,128)(2,1)S(1)} %get-tuple-element.120), channel_id=1, source_target_pairs={{0,8},{8,0},{16,24},{24,16},{1,9},{9,1},{17,25},{25,17},{2,10},{10... | collective-permute-start | bytes 393224 | tf_op jit(solution)/shard_map/ppermute | solution.py:447
  26.3 0.0 collective-permute-start.19
  26.3 2.6 %collective-permute-start.20 = (s32[8,128]{1,0:T(8,128)S(1)}, s32[8,128]{1,0:T(8,128)S(1)}, u32[]{:S(2)}, u32[]{:S(2)}) collective-permute-start(s32[8,128]{1,0:T(8,128)S(1)} %get-tuple-element.122.rest_4_), channel_id=1, source_target_pairs={{0,5},{1,6},{2,7},{3,0},{4,1},{5,2},{6,3},{7,4},{8,13},{9,14},{10,... | collective-permute-start | bytes 12296 | tf_op jit(solution)/shard_map/ppermute | solution.py:450
  28.9 1.3 %collective-permute-done.19.rest_5_ = s32[8,128]{1,0:T(8,128)S(1)} collective-permute-done((s32[8,128]{1,0:T(8,128)S(1)}, s32[8,128]{1,0:T(8,128)S(1)}, u32[]{:S(2)}, u32[]{:S(2)}) %collective-permute-start.19) | collective-permute-done | bytes 4128 | tf_op jit(solution)/shard_map/ppermute | solution.py:450
  30.2 0.0 collective-permute-done.20.rest_6_
  30.3 0.0 collective-permute-done.16.rest_0_
  30.3 0.4 collective-permute-done.17.rest_1_
  30.7 0.1 collective-permute-done.18.rest_2_
  30.8 0.7 %mix_far.3 = (bf16[48,2048]{1,0:T(8,128)(2,1)S(1)}, s32[8,128]{1,0:T(8,128)S(1)}) custom-call(bf16[48,2048]{1,0:T(8,128)(2,1)S(1)} %get-tuple-element.113.x_ref, bf16[128,128]{1,0:T(8,128)(2,1)S(1)} %get-tuple-element.114.mask_ref, bf16[32,2048]{1,0:T(8,128)(2,1)S(1)} %collective-permute-done.16.rest_0_, ...), custom_call_target="tpu_custom_call" | custom-call | flops 50331648 | bytes 393216 | tf_op jit(solution)/shard_map/mix_far/pallas_call | solution.py:316
  31.5 1.3 %collective-permute-start.21 = (bf16[48,2048]{1,0:T(8,128)(2,1)S(1)}, bf16[48,2048]{1,0:T(8,128)(2,1)S(1)}, u32[]{:S(2)}, u32[]{:S(2)}) collective-permute-start(bf16[48,2048]{1,0:T(8,128)(2,1)S(1)} %get-tuple-element.123), channel_id=1, source_target_pairs={{0,7},{1,2},{2,1},{3,4},{4,3},{5,6},{6,5},{7,0},{8,15},{9,10},{10,... | collective-permute-start | bytes 589832 | tf_op jit(solution)/shard_map/ppermute | solution.py:453
  32.8 1.6 %mix_near.3 = (bf16[128,2048]{1,0:T(8,128)(2,1)S(1)}, bf16[128,2048]{1,0:T(8,128)(2,1)S(1)}) custom-call(bf16[128,2048]{1,0:T(8,128)(2,1)S(1)} %get-tuple-element.116.core_ref, bf16[128,2048]{1,0:T(8,128)(2,1)S(1)} %get-tuple-element.115.refs_0_.own_ref, bf16[256,128]{1,0:T(8,128)(2,1)S(1)} %get-tuple-element.124.mask_ref, ...), custom_call_target="tpu_custom_call" | custom-call | flops 268435456 | bytes 2097152 | tf_op jit(solution)/shard_map/mix_near/pallas_call | solution.py:341
  34.4 0.1 collective-permute-start.22
  34.5 5.8 %collective-permute-done.21.far_ref = bf16[48,2048]{1,0:T(8,128)(2,1)S(1)} collective-permute-done((bf16[48,2048]{1,0:T(8,128)(2,1)S(1)}, bf16[48,2048]{1,0:T(8,128)(2,1)S(1)}, u32[]{:S(2)}, u32[]{:S(2)}) %collective-permute-start.21) | collective-permute-done | bytes 196640 | tf_op jit(solution)/shard_map/ppermute | solution.py:453
  40.3 0.3 unpack.7.base_ref
  40.5 0.0 collective-permute-done.22.core_ref
  40.6 0.1 combine.5
  40.6 1.5 %collective-permute-start.23 = (bf16[32,2048]{1,0:T(8,128)(2,1)S(1)}, bf16[32,2048]{1,0:T(8,128)(2,1)S(1)}, u32[]{:S(2)}, u32[]{:S(2)}) collective-permute-start(bf16[32,2048]{1,0:T(8,128)(2,1)S(1)} %get-tuple-element.131), channel_id=1, source_target_pairs={{0,24},{8,16},{16,8},{24,0},{1,25},{9,17},{17,9},{25,1},{2,26},{10... | collective-permute-start | bytes 393224 | tf_op jit(solution)/shard_map/ppermute | solution.py:447
  42.2 0.8 %collective-permute-start.24 = (bf16[32,2048]{1,0:T(8,128)(2,1)S(1)}, bf16[32,2048]{1,0:T(8,128)(2,1)S(1)}, u32[]{:S(2)}, u32[]{:S(2)}) collective-permute-start(bf16[32,2048]{1,0:T(8,128)(2,1)S(1)} %get-tuple-element.132), channel_id=1, source_target_pairs={{0,16},{8,24},{16,0},{24,8},{1,17},{9,25},{17,1},{25,9},{2,18},{10... | collective-permute-start | bytes 393224 | tf_op jit(solution)/shard_map/ppermute | solution.py:447
  43.0 1.2 %collective-permute-start.25 = (bf16[32,2048]{1,0:T(8,128)(2,1)S(1)}, bf16[32,2048]{1,0:T(8,128)(2,1)S(1)}, u32[]{:S(2)}, u32[]{:S(2)}) collective-permute-start(bf16[32,2048]{1,0:T(8,128)(2,1)S(1)} %get-tuple-element.133), channel_id=1, source_target_pairs={{0,8},{8,0},{16,24},{24,16},{1,9},{9,1},{17,25},{25,17},{2,10},{10... | collective-permute-start | bytes 393224 | tf_op jit(solution)/shard_map/ppermute | solution.py:447
  44.2 2.8 %mix_whole.3 = (bf16[512,2048]{1,0:T(8,128)(2,1)S(1)}, f32[512,128]{1,0:T(8,128)S(1)}) custom-call(bf16[512,2048]{1,0:T(8,128)(2,1)S(1)} %normalize.1.x_ref, bf16[512,128]{1,0:T(8,128)(2,1)S(1)} %get-tuple-element.111.mask_ref, bf16[32,2048]{1,0:T(8,128)(2,1)S(1)} %collective-permute-done.16.rest_0_, bf16[32,2048]{1,0:T(8,128)(2,1)S(1)} %collective-permute-done.17.rest_1_, ...), custom_call_target="tpu_custom_call" | custom-call | flops 536870912 | bytes 4194304 | tf_op jit(solution)/shard_map/mix_whole/pallas_call | solution.py:373
  46.9 0.5 slice.7
  48.1 0.0 collective-permute-done.23
  48.1 0.0 collective-permute-done.24
  48.1 3.6 %conditional.1 = (bf16[1,1,512,2048]{3,2,1,0:T(8,128)(2,1)}) conditional(s32[]{:T(128)} %bitcast.6, (bf16[512,2048]{1,0:T(8,128)(2,1)S(1)}, bf16[512,128]{1,0:T(8,128)(2,1)S(1)}, f32[512,128]{1,0:T(8,128)S(1)}, bf16[32,2048]{1,0:T(8,128)(2,1)S(1)}, bf16[32,2048]{1,0:T(8,128)(2,1)S(1)}, /*index=5*/bf16[32,2048]{1,0:T(8,128)(2,1)S(1)}, ...), branch_computations={%region_0.0_spmd, %region_1.0_spmd} | conditional | flops 35837706240 | bytes 92275056 | solution.py:505
  48.1 3.4 %mix.2 = bf16[512,2048]{1,0:T(8,128)(2,1)} custom-call(bf16[512,2048]{1,0:T(8,128)(2,1)S(1)} %get-tuple-element.51.x_ref, bf16[512,128]{1,0:T(8,128)(2,1)S(1)} %get-tuple-element.52.mask_ref, f32[512,128]{1,0:T(8,128)S(1)} %get-tuple-element.53.squares_ref, bf16[32,2048]{1,0:T(8,128)(2,1)S(1)} %get-tuple-element.54.rest_0_, ...), custom_call_target="tpu_custom_call" | custom-call | flops 536870912 | bytes 4194304 | tf_op jit(solution)/shard_map/cond/branch_0_fun/mix/pallas_call | solution.py:419
  (1 shorter events, 0.0 us)
Async XLA Ops:
  0.0 5.5 %collective-permute-start.10 = (s32[4,32]{1,0:T(4,128)}, s32[4,32]{1,0:T(4,128)S(1)}, u32[]{:S(2)}, u32[]{:S(2)}) collective-permute-start(s32[4,32]{1,0:T(4,128)} %bitcast.12), channel_id=1, source_target_pairs={{0,16},{8,24},{16,0},{24,8},{1,17},{9,25},{17,1},{25,9},{2,18},{10... | collective-permute-start | bytes 1544 | tf_op jit(solution)/shard_map/ppermute | solution.py:447
  3.0 4.7 %collective-permute-start.11 = (s32[4,32]{1,0:T(4,128)}, s32[4,32]{1,0:T(4,128)S(1)}, u32[]{:S(2)}, u32[]{:S(2)}) collective-permute-start(s32[4,32]{1,0:T(4,128)} %bitcast.13), channel_id=1, source_target_pairs={{0,24},{8,16},{16,8},{24,0},{1,25},{9,17},{17,9},{25,1},{2,26},{10... | collective-permute-start | bytes 1544 | tf_op jit(solution)/shard_map/ppermute | solution.py:447
  4.4 3.8 %collective-permute-start.9 = (s32[4,32]{1,0:T(4,128)}, s32[4,32]{1,0:T(4,128)S(1)}, u32[]{:S(2)}, u32[]{:S(2)}) collective-permute-start(s32[4,32]{1,0:T(4,128)} %bitcast.14), channel_id=1, source_target_pairs={{0,8},{8,0},{16,24},{24,16},{1,9},{9,1},{17,25},{25,17},{2,10},{10... | collective-permute-start | bytes 1544 | tf_op jit(solution)/shard_map/ppermute | solution.py:447
  8.5 5.6 %collective-permute-start.12 = (s32[8,128]{1,0:T(8,128)S(1)}, s32[8,128]{1,0:T(8,128)S(1)}, u32[]{:S(2)}, u32[]{:S(2)}) collective-permute-start(s32[8,128]{1,0:T(8,128)S(1)} %list.1.mine_ref), channel_id=1, source_target_pairs={{0,1},{1,0},{2,3},{3,2},{4,5},{5,4},{6,7},{7,6},{8,9},{9,8},{10,11... | collective-permute-start | bytes 12296 | tf_op jit(solution)/shard_map/ppermute | solution.py:456
  8.5 5.6 %collective-permute-start.13 = (s32[8,128]{1,0:T(8,128)S(1)}, s32[8,128]{1,0:T(8,128)S(1)}, u32[]{:S(2)}, u32[]{:S(2)}) collective-permute-start(s32[8,128]{1,0:T(8,128)S(1)} %list.1.mine_ref), channel_id=1, source_target_pairs={{0,7},{1,2},{2,1},{3,4},{4,3},{5,6},{6,5},{7,0},{8,15},{9,10},{10,... | collective-permute-start | bytes 12296 | tf_op jit(solution)/shard_map/ppermute | solution.py:453
  14.9 7.5 %collective-permute-start.14 = (bf16[48,2048]{1,0:T(8,128)(2,1)S(1)}, bf16[48,2048]{1,0:T(8,128)(2,1)S(1)}, u32[]{:S(2)}, u32[]{:S(2)}) collective-permute-start(bf16[48,2048]{1,0:T(8,128)(2,1)S(1)} %get-tuple-element.113.x_ref), channel_id=1, source_target_pairs={{0,7},{1,2},{2,1},{3,4},{4,3},{5,6},{6,5},{7,0},{8,15},{9,10},{10,... | collective-permute-start | bytes 589832 | tf_op jit(solution)/shard_map/ppermute | solution.py:453
  19.3 3.3 %collective-permute-start.15 = (bf16[128,2048]{1,0:T(8,128)(2,1)S(1)}, bf16[128,2048]{1,0:T(8,128)(2,1)S(1)}, u32[]{:S(2)}, u32[]{:S(2)}) collective-permute-start(bf16[128,2048]{1,0:T(8,128)(2,1)S(1)} %get-tuple-element.116.core_ref), channel_id=1, source_target_pairs={{0,1},{1,0},{2,3},{3,2},{4,5},{5,4},{6,7},{7,6},{8,9},{9,8},{10,11... | collective-permute-start | bytes 1572872 | tf_op jit(solution)/shard_map/ppermute | solution.py:456
  22.7 7.5 %collective-permute-start.16 = (bf16[32,2048]{1,0:T(8,128)(2,1)S(1)}, bf16[32,2048]{1,0:T(8,128)(2,1)S(1)}, u32[]{:S(2)}, u32[]{:S(2)}) collective-permute-start(bf16[32,2048]{1,0:T(8,128)(2,1)S(1)} %get-tuple-element.118), channel_id=1, source_target_pairs={{0,24},{8,16},{16,8},{24,0},{1,25},{9,17},{17,9},{25,1},{2,26},{10... | collective-permute-start | bytes 393224 | tf_op jit(solution)/shard_map/ppermute | solution.py:447
  24.3 6.4 %collective-permute-start.17 = (bf16[32,2048]{1,0:T(8,128)(2,1)S(1)}, bf16[32,2048]{1,0:T(8,128)(2,1)S(1)}, u32[]{:S(2)}, u32[]{:S(2)}) collective-permute-start(bf16[32,2048]{1,0:T(8,128)(2,1)S(1)} %get-tuple-element.119), channel_id=1, source_target_pairs={{0,16},{8,24},{16,0},{24,8},{1,17},{9,25},{17,1},{25,9},{2,18},{10... | collective-permute-start | bytes 393224 | tf_op jit(solution)/shard_map/ppermute | solution.py:447
  25.2 5.6 %collective-permute-start.18 = (bf16[32,2048]{1,0:T(8,128)(2,1)S(1)}, bf16[32,2048]{1,0:T(8,128)(2,1)S(1)}, u32[]{:S(2)}, u32[]{:S(2)}) collective-permute-start(bf16[32,2048]{1,0:T(8,128)(2,1)S(1)} %get-tuple-element.120), channel_id=1, source_target_pairs={{0,8},{8,0},{16,24},{24,16},{1,9},{9,1},{17,25},{25,17},{2,10},{10... | collective-permute-start | bytes 393224 | tf_op jit(solution)/shard_map/ppermute | solution.py:447
  26.3 3.9 %collective-permute-start.19 = (s32[8,128]{1,0:T(8,128)S(1)}, s32[8,128]{1,0:T(8,128)S(1)}, u32[]{:S(2)}, u32[]{:S(2)}) collective-permute-start(s32[8,128]{1,0:T(8,128)S(1)} %get-tuple-element.122.rest_4_), channel_id=1, source_target_pairs={{0,3},{1,4},{2,5},{3,6},{4,7},{5,0},{6,1},{7,2},{8,11},{9,12},{10,... | collective-permute-start | bytes 12296 | tf_op jit(solution)/shard_map/ppermute | solution.py:450
  26.3 4.0 %collective-permute-start.20 = (s32[8,128]{1,0:T(8,128)S(1)}, s32[8,128]{1,0:T(8,128)S(1)}, u32[]{:S(2)}, u32[]{:S(2)}) collective-permute-start(s32[8,128]{1,0:T(8,128)S(1)} %get-tuple-element.122.rest_4_), channel_id=1, source_target_pairs={{0,5},{1,6},{2,7},{3,0},{4,1},{5,2},{6,3},{7,4},{8,13},{9,14},{10,... | collective-permute-start | bytes 12296 | tf_op jit(solution)/shard_map/ppermute | solution.py:450
  31.5 8.8 %collective-permute-start.21 = (bf16[48,2048]{1,0:T(8,128)(2,1)S(1)}, bf16[48,2048]{1,0:T(8,128)(2,1)S(1)}, u32[]{:S(2)}, u32[]{:S(2)}) collective-permute-start(bf16[48,2048]{1,0:T(8,128)(2,1)S(1)} %get-tuple-element.123), channel_id=1, source_target_pairs={{0,7},{1,2},{2,1},{3,4},{4,3},{5,6},{6,5},{7,0},{8,15},{9,10},{10,... | collective-permute-start | bytes 589832 | tf_op jit(solution)/shard_map/ppermute | solution.py:453
  34.4 6.2 %collective-permute-start.22 = (bf16[128,2048]{1,0:T(8,128)(2,1)S(1)}, bf16[128,2048]{1,0:T(8,128)(2,1)S(1)}, u32[]{:S(2)}, u32[]{:S(2)}) collective-permute-start(bf16[128,2048]{1,0:T(8,128)(2,1)S(1)} %get-tuple-element.126), channel_id=1, source_target_pairs={{0,1},{1,0},{2,3},{3,2},{4,5},{5,4},{6,7},{7,6},{8,9},{9,8},{10,11... | collective-permute-start | bytes 1572872 | tf_op jit(solution)/shard_map/ppermute | solution.py:456
  40.6 7.5 %collective-permute-start.23 = (bf16[32,2048]{1,0:T(8,128)(2,1)S(1)}, bf16[32,2048]{1,0:T(8,128)(2,1)S(1)}, u32[]{:S(2)}, u32[]{:S(2)}) collective-permute-start(bf16[32,2048]{1,0:T(8,128)(2,1)S(1)} %get-tuple-element.131), channel_id=1, source_target_pairs={{0,24},{8,16},{16,8},{24,0},{1,25},{9,17},{17,9},{25,1},{2,26},{10... | collective-permute-start | bytes 393224 | tf_op jit(solution)/shard_map/ppermute | solution.py:447
  42.2 6.0 %collective-permute-start.24 = (bf16[32,2048]{1,0:T(8,128)(2,1)S(1)}, bf16[32,2048]{1,0:T(8,128)(2,1)S(1)}, u32[]{:S(2)}, u32[]{:S(2)}) collective-permute-start(bf16[32,2048]{1,0:T(8,128)(2,1)S(1)} %get-tuple-element.132), channel_id=1, source_target_pairs={{0,16},{8,24},{16,0},{24,8},{1,17},{9,25},{17,1},{25,9},{2,18},{10... | collective-permute-start | bytes 393224 | tf_op jit(solution)/shard_map/ppermute | solution.py:447
  43.0 5.1 %collective-permute-start.25 = (bf16[32,2048]{1,0:T(8,128)(2,1)S(1)}, bf16[32,2048]{1,0:T(8,128)(2,1)S(1)}, u32[]{:S(2)}, u32[]{:S(2)}) collective-permute-start(bf16[32,2048]{1,0:T(8,128)(2,1)S(1)} %get-tuple-element.133), channel_id=1, source_target_pairs={{0,8},{8,0},{16,24},{24,16},{1,9},{9,1},{17,25},{25,17},{2,10},{10... | collective-permute-start | bytes 393224 | tf_op jit(solution)/shard_map/ppermute | solution.py:447

commit v11 on v0

v11 whole, which is shorter than its diff:
```python
import functools

import jax
import jax.numpy as jnp
from jax import lax
from jax.experimental import pallas as pl
from jax.experimental.pallas import tpu as pltpu
from jax.sharding import PartitionSpec as P

LANES = 128
BLOCK = 128
FIRST_SHARE = 3, 8
BOTH_LAST = (((1,), (1,)), ((), ()))


def bf16(*shape):
    return jax.ShapeDtypeStruct(shape, jnp.bfloat16)


def int32(*shape):
    return jax.ShapeDtypeStruct(shape, jnp.int32)


def kernel_call(name, kernel, outs, *args, flops, moved=0, scratch=(), mib=32, **specs):
    return pl.pallas_call(
        kernel,
        out_shape=outs,
        scratch_shapes=scratch,
        compiler_params=pltpu.CompilerParams(vmem_limit_bytes=mib * 1024 * 1024),
        cost_estimate=pl.CostEstimate(flops=flops, bytes_accessed=moved, transcendentals=0),
        name=name,
        **specs,
    )(*args)


def normalize(value):
    return value * lax.rsqrt(jnp.mean(value * value, axis=-1, keepdims=True) + 1e-06)


def normalize_kernel(x_hbm, out_ref, raw, sems):
    copies = []
    starts = range(0, raw.shape[0], BLOCK)
    for i, start in enumerate(starts):
        here = pl.ds(start, BLOCK)
        copies.append(pltpu.make_async_copy(x_hbm.at[here], raw.at[here], sems.at[i]))
        copies[-1].start()
    for copy, start in zip(copies, starts):
        copy.wait()
        here = pl.ds(start, BLOCK)
        out_ref[here] = normalize(raw[here].astype(jnp.float32)).astype(jnp.bfloat16)


def normalize_call(descriptors):
    rows, width = descriptors.shape
    return kernel_call(
        "normalize",
        normalize_kernel,
        bf16(rows, width),
        descriptors,
        flops=6 * rows * width,
        moved=4 * rows * width,
        scratch=[
            pltpu.VMEM((rows, width), jnp.bfloat16),
            pltpu.SemaphoreType.DMA((rows // BLOCK,)),
        ],
        mib=56,
        in_specs=[pl.BlockSpec(memory_space=pl.ANY)],
    )


def mask_kernel(slot_cap, pick_hbm, wanted_hbm, mask_ref, wanted_ref, pick, sems):
    copies = [
        pltpu.make_async_copy(pick_hbm, pick, sems.at[0]),
        pltpu.make_async_copy(wanted_hbm, wanted_ref, sems.at[1]),
    ]
    for copy in copies:
        copy.start()
    shape = mask_ref.shape[1], mask_ref.shape[0]
    slot = lax.broadcasted_iota(jnp.int32, shape, 0)
    slot = slot ^ (lax.axis_index("clus") * slot_cap)
    chosen = jnp.zeros(shape, jnp.float32)
    copies[0].wait()
    for k in range(pick.shape[0]):
        chosen = jnp.where(pick[k] == slot, 1.0, chosen)
    mask_ref[...] = chosen.T.astype(jnp.bfloat16)
    copies[1].wait()


def mask_call(slots, wanted):
    count, _, rows = slots.shape
    total = wanted.size
    return kernel_call(
        "mask",
        functools.partial(mask_kernel, wanted.shape[1]),
        [bf16(rows, total), pltpu.VMEM(wanted.shape, jnp.int32)],
        slots,
        wanted,
        flops=2 * count * rows * total,
        moved=2 * rows * total,
        scratch=[pltpu.VMEM(slots.shape, jnp.int32), pltpu.SemaphoreType.DMA((2,))],
        mib=56,
        in_specs=[pl.BlockSpec(memory_space=pl.ANY)] * 2,
    )


def list_kernel(rows, *refs):
    parts, refs = refs[:-5], refs[-5:]
    own_ref, far_ref, core_ref, expand_far_ref, expand_core_ref = refs
    total = own_ref.shape[1]
    lane = lax.broadcasted_iota(jnp.int32, (total, total), 1)
    sublane = lax.broadcasted_iota(jnp.int32, (total, total), 0)
    odd = lax.axis_index("rep") % 2
    lows = [(2 * odd * rows).astype(jnp.float32), ((2 - 2 * odd) * rows).astype(jnp.float32)]

    def inside(value, low):
        return (value >= low) & (value < low + rows)

    def asked(server):
        row = jnp.concatenate([ref[server, :] for ref in parts], axis=1).astype(jnp.float32)
        column = jnp.broadcast_to(row, (total, total)).T
        again = jnp.where((column == row) & (sublane < lane), 1.0, 0.0)
        return row, column, 1.0 - jnp.max(again, axis=0, keepdims=True)

    most = jnp.zeros((1, 1), jnp.float32)
    for server in range(len(parts)):
        row, _, first = asked(slice(server, server + 1))
        for low in lows:
            count = jnp.sum(jnp.where(inside(row, low), first, 0.0), axis=1, keepdims=True)
            most = jnp.maximum(most, count)
    row, column, first = asked(pl.ds(lax.axis_index("clus"), 1))
    own_ref[...] = jnp.broadcast_to(row - rows, own_ref.shape).astype(jnp.int32)
    place = lax.broadcasted_iota(jnp.int32, own_ref.shape, 0)
    for low, out_ref, expand_ref in zip(lows, (far_ref, core_ref), (expand_far_ref, expand_core_ref)):
        counted = jnp.where(inside(row, low), first, 0.0)
        rank = jnp.sum(jnp.where(row < column, counted, 0.0), axis=1, keepdims=True)
        here = inside(column, low) & (rank.astype(jnp.int32) == lane)
        expand_ref[...] = jnp.where(here, 1.0, 0.0).astype(jnp.bfloat16)
        packed = jnp.max(jnp.where(here, column - low, -1.0), axis=0, keepdims=True)
        out_ref[...] = jnp.where(place == 1, most, packed).astype(jnp.int32)


def list_call(parts, rows):
    total = parts[0].size
    return kernel_call(
        "list",
        functools.partial(list_kernel, rows),
        [int32(8, total)] * 3 + [bf16(total, total)] * 2,
        *parts,
        flops=40 * total * total,
    )


def one_hot(numbers, rows):
    total = numbers.shape[1]
    column = jnp.broadcast_to(numbers.astype(jnp.float32), (LANES, total)).T.astype(jnp.int32)
    tiles = []
    for start in range(0, rows, LANES):
        lane = lax.broadcasted_iota(jnp.int32, (total, LANES), 1) + start
        tiles.append(jnp.where(column == lane, 1.0, 0.0).astype(jnp.bfloat16))
    return jnp.concatenate(tiles, axis=1)


def take(select, x):
    return jnp.dot(select, x, preferred_element_type=jnp.float32).astype(jnp.bfloat16)


def far_kernel(x_ref, beyond_ref, pack_ref, far_ref):
    pack_ref[...] = one_hot(beyond_ref[0:1], x_ref.shape[0])
    far_ref[...] = take(pack_ref[: far_ref.shape[0]], x_ref[...])


def far_call(x, beyond, sent):
    rows, width = x.shape
    total = beyond.shape[1]
    return kernel_call(
        "pack_far",
        far_kernel,
        [bf16(total, rows), bf16(sent, width)],
        x,
        beyond,
        flops=2 * rows * sent * width,
    )


def near_kernel(x_ref, mask_ref, pack_ref, own_list_ref, *refs):
    far_list_ref, beyond_ref, within_ref, *refs = refs
    core_ref, own_ref, near_ref, rest_far_ref, rest_core_ref, *refs = refs
    far_mask_ref, core_mask_ref, near_mask_ref, most_ref, select = refs
    total, sent = own_ref.shape[0], core_ref.shape[0]
    rows = x_ref.shape[0]
    select[:total] = one_hot(within_ref[0:1], rows)
    select[total:] = one_hot(own_list_ref[0:1], rows)
    fetched = take(select[...], x_ref[...])
    core_ref[...] = fetched[:sent]
    near_ref[:sent] = fetched[:sent]
    rest_core_ref[...] = fetched[sent:total]
    own_ref[...] = fetched[total:]
    near_ref[sent:] = fetched[total:]
    rest_far_ref[...] = take(pack_ref[sent:], x_ref[...])
    masks = take(select[...], mask_ref[...])
    core_mask_ref[...] = masks[:total]
    near_mask_ref[:sent] = masks[:sent]
    near_mask_ref[sent:] = masks[total:]
    far_mask_ref[...] = take(pack_ref[...], mask_ref[...])
    most = jnp.maximum(far_list_ref[...], jnp.maximum(beyond_ref[...], within_ref[...]))
    most_ref[...] = jnp.broadcast_to(most[1:2, :LANES], most_ref.shape)


def near_call(x, mask, pack, own_list, far_list, beyond, within, sent):
    rows, width = x.shape
    total = mask.shape[1]
    return kernel_call(
        "serve_near",
        near_kernel,
        [
            bf16(sent, width),
            bf16(total, width),
            bf16(sent + total, width),
            bf16(total - sent, width),
            bf16(total - sent, width),
            bf16(total, total),
            bf16(total, total),
            bf16(sent + total, total),
            int32(8, LANES),
        ],
        x,
        mask,
        pack,
        own_list,
        far_list,
        beyond,
        within,
        flops=6 * total * rows * width,
        scratch=[pltpu.VMEM((2 * total, rows), jnp.bfloat16)],
    )


def unpack_kernel(first, bases, expand_ref, far_ref, *refs):
    out_ref, sent = refs[-1], far_ref.shape[0]
    rows = jnp.dot(
        expand_ref[:, first : first + sent], far_ref[...], preferred_element_type=jnp.float32
    )
    for base_ref in refs[:bases]:
        rows += base_ref[...].astype(jnp.float32)
    out_ref[...] = rows.astype(jnp.bfloat16)


def unpack_call(expand, far, *base, first=0, after=()):
    in_vmem = [pl.BlockSpec(memory_space=pltpu.VMEM)] * (2 + len(base))
    return kernel_call(
        "unpack",
        functools.partial(unpack_kernel, first, len(base)),
        bf16(expand.shape[0], far.shape[1]),
        expand,
        far,
        *base,
        *after,
        flops=2**34,
        moved=2**25,
        in_specs=in_vmem + [pl.BlockSpec(memory_space=pl.ANY)] * len(after),
    )


def combine_kernel(expand_ref, core_ref, base_ref, most_ref, out_most_ref, *out_refs):
    out_most_ref[...] = most_ref[...]
    cap, sent = out_refs[0].shape[0], core_ref.shape[0]
    rows = jnp.dot(expand_ref[:, :sent], core_ref[...], preferred_element_type=jnp.float32)
    rows = (rows + base_ref[...].astype(jnp.float32)).astype(jnp.bfloat16)
    for d, out in enumerate(out_refs):
        out[...] = rows[d * cap : (d + 1) * cap]


def combine_call(expand, core, base, most, servers):
    total, width = base.shape
    most, *parts = kernel_call(
        "combine",
        combine_kernel,
        [int32(*most.shape)] + [bf16(total // servers, width)] * servers,
        expand,
        core,
        base,
        most,
        flops=2 * total * core.shape[0] * width,
    )
    return most, parts


def fill(buffer, parts):
    cap = parts[0].shape[0]
    for d, ref in enumerate(reversed(parts)):
        buffer[d * cap : (d + 1) * cap] = ref[...]


def weigh(x, buffer, mask):
    dots = lax.dot_general(x, buffer, BOTH_LAST, preferred_element_type=jnp.float32)
    positive = jnp.maximum(dots * (1.0 / x.shape[1]), 0.0)
    return (positive * positive * positive).astype(jnp.bfloat16) * mask


def mix(x, weights, buffer):
    mixed = x.astype(jnp.float32) + jnp.dot(weights, buffer, preferred_element_type=jnp.float32)
    return normalize(mixed).astype(jnp.bfloat16)


def far_mix_kernel(servers, x_ref, mask_ref, *rest):
    parts, rest = rest[:servers], rest[servers:]
    *most_refs, out_ref, most_ref, buffer = rest
    most_ref[...] = functools.reduce(jnp.maximum, [ref[...] for ref in most_refs])
    fill(buffer, parts)
    weights = weigh(x_ref[...], buffer[...], mask_ref[: x_ref.shape[0]])
    out_ref[...] = mix(x_ref[...], weights, buffer[...])


def far_mix_call(x, mask, parts, mosts):
    rows, width = x.shape
    total, servers = mask.shape[1], len(parts)
    return kernel_call(
        "mix_far",
        functools.partial(far_mix_kernel, servers),
        [bf16(rows, width), int32(*mosts[0].shape)],
        x,
        mask,
        *reversed(parts),
        *mosts,
        flops=4 * total * rows * width,
        scratch=[pltpu.VMEM((total, width), jnp.bfloat16)],
    )


def near_mix_kernel(servers, x_ref, mask_ref, *rest):
    parts, (core_ref, own_ref, buffer) = rest[:servers], rest[servers:]
    fill(buffer, parts)
    weights = weigh(x_ref[...], buffer[...], mask_ref[...])
    mixed = mix(x_ref[...], weights, buffer[...])
    core_ref[...] = mixed[: core_ref.shape[0]]
    own_ref[...] = mixed[core_ref.shape[0] :]


def near_mix_call(x, mask, parts):
    rows, width = x.shape
    total, servers = mask.shape[1], len(parts)
    return kernel_call(
        "mix_near",
        functools.partial(near_mix_kernel, servers),
        [bf16(rows - total, width), bf16(total, width)],
        x,
        mask,
        *reversed(parts),
        flops=4 * total * rows * width,
        scratch=[pltpu.VMEM((total, width), jnp.bfloat16)],
    )


def whole_kernel(servers, x_ref, mask_ref, *rest):
    parts, (out_ref, buffer, weights) = rest[:servers], rest[servers:]
    fill(buffer, parts)
    weights[...] = weigh(x_ref[...], buffer[...], mask_ref[...])
    for start in range(0, x_ref.shape[0], BLOCK):
        here = pl.ds(start, BLOCK)
        out_ref[here] = mix(x_ref[here], weights[here], buffer[...])


def whole_call(x, mask, parts):
    rows, width = x.shape
    total, servers = mask.shape[1], len(parts)
    return kernel_call(
        "mix_whole",
        functools.partial(whole_kernel, servers),
        bf16(rows, width),
        x,
        mask,
        *reversed(parts),
        flops=4 * total * rows * width,
        scratch=[
            pltpu.VMEM((total, width), jnp.bfloat16),
            pltpu.VMEM((rows, total), jnp.bfloat16),
        ],
    )


def last_kernel(servers, x_ref, mask_ref, *rest):
    parts, rest = rest[:servers], rest[servers:]
    out_ref, buffer, weights, whole, sems = rest
    fill(buffer, parts)
    weights[...] = weigh(x_ref[...], buffer[...], mask_ref[...])
    copies = []
    for i, start in enumerate(range(0, x_ref.shape[0], BLOCK)):
        here = pl.ds(start, BLOCK)
        whole[here] = mix(x_ref[here], weights[here], buffer[...])
        copies.append(pltpu.make_async_copy(whole.at[here], out_ref.at[here], sems.at[i]))
        copies[-1].start()
    for copy in copies:
        copy.wait()


def last_call(x, mask, parts):
    rows, width = x.shape
    total, servers = mask.shape[1], len(parts)
    return kernel_call(
        "mix",
        functools.partial(last_kernel, servers),
        pltpu.HBM((rows, width), jnp.bfloat16),
        x,
        mask,
        *reversed(parts),
        flops=4 * total * rows * width,
        moved=4 * rows * width,
        scratch=[
            pltpu.VMEM((total, width), jnp.bfloat16),
            pltpu.VMEM((rows, total), jnp.bfloat16),
            pltpu.VMEM((rows, width), jnp.bfloat16),
            pltpu.SemaphoreType.DMA((rows // BLOCK,)),
        ],
        out_specs=pl.BlockSpec(memory_space=pltpu.HBM),
    )


def local(descriptors, request, pick):
    wanted = request[0, 0]
    rows = descriptors.shape[2]
    servers, cap = wanted.shape
    total = servers * cap
    groups = lax.axis_size("rep")
    sent = total * FIRST_SHARE[0] // FIRST_SHARE[1]
    within = [(g, g ^ 1) for g in range(groups)]
    beyond = [(g, (g + 2 * (g % 2) - 1 + groups) % groups) for g in range(groups)]

    def turn(value, d):
        return lax.ppermute(value, "clus", [(c, c ^ d) for c in range(servers)])

    def shift(value, by):
        return lax.ppermute(value, "rep", [(g, (g + by) % groups) for g in range(groups)])

    def across(value):
        return lax.ppermute(value, "rep", beyond)

    def inside(value):
        return lax.ppermute(value, "rep", within)

    def turned(parts):
        got = {d: turn(parts[d], d) for d in reversed(range(1, servers))}
        return [parts[0]] + [got[d] for d in range(1, servers)]

    def exchange(expands, far, core, own, most, after=()):
        base = unpack_call(expands[0], across(far), own, after=after)
        most, parts = combine_call(expands[1], inside(core), base, most, servers)
        return most, turned(parts)

    def next_round(x, mask, far, near, far_mask, near_mask, expands, parts, mosts):
        far, most = far_mix_call(far, far_mask, parts, mosts)
        core, own = near_mix_call(near, near_mask, parts)
        x = whole_call(x, mask, parts)
        return x, *exchange(expands, far, core, own, most, after=[x])

    def in_full(x, y, mask, far, near, rest, masks, expands, most, first, last):
        late = unpack_call(expands[1], inside(rest[1]), first=sent)
        late = unpack_call(expands[0], across(rest[0]), late, first=sent)
        late = turned(list(late.reshape(servers, cap, -1)))
        first = [a + b for a, b in zip(first, late)]
        far = jnp.concatenate([far, rest[0]], axis=0)
        near = jnp.concatenate([near[:sent], rest[1], near[sent:]], axis=0)
        near_mask = jnp.concatenate([masks[1], masks[2][sent:]], axis=0)
        y, _, last = next_round(
            x, mask, far, near, masks[0], near_mask, expands, first, [most]
        )
        return last_call(y, mask, last)

    def as_sent(x, y, mask, far, near, rest, masks, expands, most, first, last):
        return last_call(y, mask, last)

    asked = {d: turn(wanted, d) for d in reversed(range(1, servers))}
    mask, held = mask_call(pick.transpose(0, 3, 1, 2)[0], wanted)
    own_list, far_list, core_list, *expands = list_call(
        [held] + [asked[d] for d in range(1, servers)], rows
    )
    beyond_list, within_list = across(far_list), inside(core_list)
    x = normalize_call(descriptors[0, 0])
    pack, far = far_call(x, beyond_list, sent)
    core, own, near, *others, most = near_call(
        x, mask, pack, own_list, far_list, beyond_list, within_list, sent
    )
    rest, masks = others[:2], others[2:]
    most, first = exchange(expands, far, core, own, most)
    mosts = [most]
    reach = 1
    while 2 * reach + 1 < groups:
        by = 2 * reach + 1
        most = functools.reduce(jnp.maximum, mosts)
        mosts = [most, shift(most, by), shift(most, -by)]
        reach += by
    y, most, last = next_round(
        x, mask, far, near, masks[0], masks[2], expands, first, mosts
    )
    state = x, y, mask, far, near, rest, masks, expands, most, first, last
    return lax.cond(most[0, 0] > sent, in_full, as_sent, *state)[None, None]


def solution(mesh):
    return jax.shard_map(
        local,
        mesh=mesh,
        in_specs=(
            P("rep", "clus", None, None),
            P("rep", "clus", None, None),
            P("rep", "clus", None, None),
        ),
        out_specs=P("rep", "clus", None, None),
        check_vma=False,
    )
```

time: 169 us -> 52.8 us (0.31)
  waiting for transfers between devices: 86.2 us -> 19.1 us
  other arithmetic: 28.8 us -> 0 us
  blocking collectives: 20.3 us -> 0 us
  Pallas kernels: 0 us -> 13.8 us
  local copies, waits for them, and re-layouts: 11.6 us -> 0.51 us
  matrix products: 8.51 us -> 0 us
  starting transfers between devices: 12.5 us -> 18.1 us
    ppermute x4 -> x17, waiting for transfers between devices: 78.5 us -> 19.1 us  [the longest x3 9.68 us: across(): return lax.ppermute(value, 'rep', beyond)]
    all_to_all x2 -> x0, blocking collectives: 20.3 us -> none  [the longest x1 11.7 us: local(): lax.all_to_all(served.reshape(servers, slot_cap, width), 'clus', split_ax...]
    concatenate x2 -> x0, other arithmetic: 16.7 us -> none  [with_halo(): block = jnp.concatenate([low, block, high], axis=dim)]
    pallas_call x0 -> x13, Pallas kernels: none -> 13.8 us  [kernel_call(): pl.pallas_call(kernel, out_shape=outs, scratch_shapes=scratch, compiler_p...]
    gather x2 -> x0, local copies, waits for them, and re-layouts: 11 us -> none  [local(): served = window_rows[incoming]]
    ppermute x4 -> x17, starting transfers between devices: 8.2 us -> 18.1 us  [the longest x9 11.6 us: turn(): return lax.ppermute(value, 'clus', [(c, c ^ d) for c in range(servers)])]
    dot_general x2 -> x0, matrix products: 8.51 us -> none  [local(): jnp.dot(weights, buffer, preferred_element_type=jnp.float32)]
    all_to_all x1 -> x0, waiting for transfers between devices: 7.7 us -> none  [local(): lax.all_to_all(served.reshape(servers, slot_cap, width), 'clus', split_ax...]
  transfers between devices with their start and end apart: 5 -> 17, of which waited for: 4 -> 10; matrix products, arithmetic and copies ran while one was open for 1% -> 1% of each run, Pallas kernels for 0% -> 16%
where the time goes in v11:
time: 52.8 us; the launch traced here: 52.6 us
  waiting for transfers between devices  19.1 us (36%)
  starting transfers between devices  18.1 us (34%)
  Pallas kernels  13.8 us (26%)
  between operations  0.94 us (2%)
    pallas_call x13, Pallas kernels, kernel_call(): pl.pallas_call(kernel, out_shape=outs, scratch_shapes=scratch, compiler_p...  13.8 us
    ppermute x9, starting transfers between devices, turn(): return lax.ppermute(value, 'clus', [(c, c ^ d) for c in range(servers)])  11.6 us
    ppermute x3, waiting for transfers between devices, across(): return lax.ppermute(value, 'rep', beyond)  9.68 us
    ppermute x9, waiting for transfers between devices, turn(): return lax.ppermute(value, 'clus', [(c, c ^ d) for c in range(servers)])  6.94 us
    ppermute x3, starting transfers between devices, across(): return lax.ppermute(value, 'rep', beyond)  3.26 us
    ppermute x2, starting transfers between devices, shift(): lax.ppermute(value, 'rep', [(g, (g + by) % groups) for g in range(groups)])  2.64 us
    ppermute x2, waiting for transfers between devices, shift(): lax.ppermute(value, 'rep', [(g, (g + by) % groups) for g in range(groups)])  1.33 us
    ppermute x3, waiting for transfers between devices, inside(): return lax.ppermute(value, 'rep', within)  1.17 us
  transfers between devices with their start and end apart: 17, of which 10 were waited for; matrix products, arithmetic and copies ran while one was open for 1% of the time, Pallas kernels for 16%

profile of v11, /device:TPU:0, one launch (start us, length us, event | category | flops | bytes accessed | tf_op | source)
XLA Modules:
  0.0 52.6 jit_solution(14486096498806555209)
XLA Ops:
  0.0 2.9 %collective-permute-start.10 = (s32[4,32]{1,0:T(4,128)}, s32[4,32]{1,0:T(4,128)S(1)}, u32[]{:S(2)}, u32[]{:S(2)}) collective-permute-start(s32[4,32]{1,0:T(4,128)} %bitcast.12), channel_id=1, source_target_pairs={{0,8},{8,0},{16,24},{24,16},{1,9},{9,1},{17,25},{25,17},{2,10},{10... | collective-permute-start | bytes 1544 | tf_op jit(solution)/shard_map/ppermute | solution.py:429
  2.9 1.5 %collective-permute-start.11 = (s32[4,32]{1,0:T(4,128)}, s32[4,32]{1,0:T(4,128)S(1)}, u32[]{:S(2)}, u32[]{:S(2)}) collective-permute-start(s32[4,32]{1,0:T(4,128)} %bitcast.13), channel_id=1, source_target_pairs={{0,16},{8,24},{16,0},{24,8},{1,17},{9,25},{17,1},{25,9},{2,18},{10... | collective-permute-start | bytes 1544 | tf_op jit(solution)/shard_map/ppermute | solution.py:429
  4.5 0.0 collective-permute-start.12
  4.5 1.0 %mask.1 = (bf16[512,128]{1,0:T(8,128)(2,1)S(1)}, s32[4,32]{1,0:T(4,128)S(1)}) custom-call(s32[10,1,512]{2,1,0:T(1,128)} %bitcast.11, s32[4,32]{1,0:T(4,128)} %bitcast.15), custom_call_target="tpu_custom_call" | custom-call | flops 1310720 | bytes 131072 | tf_op jit(solution)/shard_map/mask/pallas_call | solution.py:25
  5.5 0.0 collective-permute-done.10.refs_1_
  5.5 1.3 %collective-permute-done.11.refs_2_ = s32[4,32]{1,0:T(4,128)S(1)} collective-permute-done((s32[4,32]{1,0:T(4,128)}, s32[4,32]{1,0:T(4,128)S(1)}, u32[]{:S(2)}, u32[]{:S(2)}) %collective-permute-start.11) | collective-permute-done | bytes 544 | tf_op jit(solution)/shard_map/ppermute | solution.py:429
  6.7 2.4 %collective-permute-done.12.refs_3_ = s32[4,32]{1,0:T(4,128)S(1)} collective-permute-done((s32[4,32]{1,0:T(4,128)}, s32[4,32]{1,0:T(4,128)S(1)}, u32[]{:S(2)}, u32[]{:S(2)}) %collective-permute-start.12) | collective-permute-done | bytes 544 | tf_op jit(solution)/shard_map/ppermute | solution.py:429
  9.2 0.5 list.1
  9.6 1.4 %collective-permute-start.13 = (s32[8,128]{1,0:T(8,128)S(1)}, s32[8,128]{1,0:T(8,128)S(1)}, u32[]{:S(2)}, u32[]{:S(2)}) collective-permute-start(s32[8,128]{1,0:T(8,128)S(1)} %get-tuple-element.118.refs_0_), channel_id=1, source_target_pairs={{0,7},{1,2},{2,1},{3,4},{4,3},{5,6},{6,5},{7,0},{8,15},{9,10},{10,... | collective-permute-start | bytes 12296 | tf_op jit(solution)/shard_map/ppermute | solution.py:435
  11.0 1.9 %normalize.1.x_ref = bf16[512,2048]{1,0:T(8,128)(2,1)S(1)} custom-call(bf16[512,2048]{1,0:T(8,128)(2,1)} %bitcast.10), custom_call_target="tpu_custom_call" | custom-call | flops 6291456 | bytes 4194304 | tf_op jit(solution)/shard_map/normalize/pallas_call | solution.py:25
  12.9 1.6 %collective-permute-done.13.beyond_ref.refs_1_ = s32[8,128]{1,0:T(8,128)S(1)} collective-permute-done((s32[8,128]{1,0:T(8,128)S(1)}, s32[8,128]{1,0:T(8,128)S(1)}, u32[]{:S(2)}, u32[]{:S(2)}) %collective-permute-start.13) | collective-permute-done | bytes 4128 | tf_op jit(solution)/shard_map/ppermute | solution.py:435
  14.5 0.5 pack_far.1
  15.0 1.4 %collective-permute-start.16 = (bf16[48,2048]{1,0:T(8,128)(2,1)S(1)}, bf16[48,2048]{1,0:T(8,128)(2,1)S(1)}, u32[]{:S(2)}, u32[]{:S(2)}) collective-permute-start(bf16[48,2048]{1,0:T(8,128)(2,1)S(1)} %get-tuple-element.126.x_ref), channel_id=1, source_target_pairs={{0,7},{1,2},{2,1},{3,4},{4,3},{5,6},{6,5},{7,0},{8,15},{9,10},{10,... | collective-permute-start | bytes 589832 | tf_op jit(solution)/shard_map/ppermute | solution.py:435
  16.4 0.0 collective-permute-start.14
  16.4 1.2 %collective-permute-done.14.refs_2_ = s32[8,128]{1,0:T(8,128)S(1)} collective-permute-done((s32[8,128]{1,0:T(8,128)S(1)}, s32[8,128]{1,0:T(8,128)S(1)}, u32[]{:S(2)}, u32[]{:S(2)}) %collective-permute-start.14) | collective-permute-done | bytes 4128 | tf_op jit(solution)/shard_map/ppermute | solution.py:438
  17.6 1.2 %serve_near.1 = (bf16[48,2048]{1,0:T(8,128)(2,1)S(1)}, bf16[128,2048]{1,0:T(8,128)(2,1)S(1)}, bf16[176,2048]{1,0:T(8,128)(2,1)S(1)}, bf16[80,2048]{1,0:T(8,128)(...) custom-call(bf16[512,2048]{1,0:T(8,128)(2,1)S(1)} %normalize.1.x_ref, ...), custom_call_target="tpu_custom_call" | custom-call | flops 805306368 | tf_op jit(solution)/shard_map/serve_near/pallas_call | solution.py:25
  18.8 0.2 collective-permute-start.15
  19.1 4.2 %collective-permute-done.16.far_ref = bf16[48,2048]{1,0:T(8,128)(2,1)S(1)} collective-permute-done((bf16[48,2048]{1,0:T(8,128)(2,1)S(1)}, bf16[48,2048]{1,0:T(8,128)(2,1)S(1)}, u32[]{:S(2)}, u32[]{:S(2)}) %collective-permute-start.16) | collective-permute-done | bytes 196640 | tf_op jit(solution)/shard_map/ppermute | solution.py:435
  23.3 0.3 unpack.8.base_ref
  23.5 0.0 collective-permute-done.15.core_ref
  23.6 0.3 combine.4
  23.8 0.5 %collective-permute-start.17 = (bf16[32,2048]{1,0:T(8,128)(2,1)S(1)}, bf16[32,2048]{1,0:T(8,128)(2,1)S(1)}, u32[]{:S(2)}, u32[]{:S(2)}) collective-permute-start(bf16[32,2048]{1,0:T(8,128)(2,1)S(1)} %get-tuple-element.129), channel_id=1, source_target_pairs={{0,24},{8,16},{16,8},{24,0},{1,25},{9,17},{17,9},{25,1},{2,26},{10... | collective-permute-start | bytes 393224 | tf_op jit(solution)/shard_map/ppermute | solution.py:429
  24.4 1.5 %collective-permute-start.18 = (bf16[32,2048]{1,0:T(8,128)(2,1)S(1)}, bf16[32,2048]{1,0:T(8,128)(2,1)S(1)}, u32[]{:S(2)}, u32[]{:S(2)}) collective-permute-start(bf16[32,2048]{1,0:T(8,128)(2,1)S(1)} %get-tuple-element.130), channel_id=1, source_target_pairs={{0,16},{8,24},{16,0},{24,8},{1,17},{9,25},{17,1},{25,9},{2,18},{10... | collective-permute-start | bytes 393224 | tf_op jit(solution)/shard_map/ppermute | solution.py:429
  25.9 1.5 %collective-permute-start.19 = (bf16[32,2048]{1,0:T(8,128)(2,1)S(1)}, bf16[32,2048]{1,0:T(8,128)(2,1)S(1)}, u32[]{:S(2)}, u32[]{:S(2)}) collective-permute-start(bf16[32,2048]{1,0:T(8,128)(2,1)S(1)} %get-tuple-element.131), channel_id=1, source_target_pairs={{0,8},{8,0},{16,24},{24,16},{1,9},{9,1},{17,25},{25,17},{2,10},{10... | collective-permute-start | bytes 393224 | tf_op jit(solution)/shard_map/ppermute | solution.py:429
  27.4 0.0 collective-permute-start.21
  27.4 2.6 %collective-permute-start.22 = (s32[8,128]{1,0:T(8,128)S(1)}, s32[8,128]{1,0:T(8,128)S(1)}, u32[]{:S(2)}, u32[]{:S(2)}) collective-permute-start(s32[8,128]{1,0:T(8,128)S(1)} %get-tuple-element.135.rest_4_), channel_id=1, source_target_pairs={{0,5},{1,6},{2,7},{3,0},{4,1},{5,2},{6,3},{7,4},{8,13},{9,14},{10,... | collective-permute-start | bytes 12296 | tf_op jit(solution)/shard_map/ppermute | solution.py:432
  30.0 1.3 %collective-permute-done.21.rest_5_ = s32[8,128]{1,0:T(8,128)S(1)} collective-permute-done((s32[8,128]{1,0:T(8,128)S(1)}, s32[8,128]{1,0:T(8,128)S(1)}, u32[]{:S(2)}, u32[]{:S(2)}) %collective-permute-start.21) | collective-permute-done | bytes 4128 | tf_op jit(solution)/shard_map/ppermute | solution.py:432
  31.3 0.0 collective-permute-done.22.rest_6_
  31.4 0.0 collective-permute-done.17.rest_0_
  31.4 0.0 collective-permute-done.18.rest_1_
  31.4 0.7 %mix_far.3 = (bf16[48,2048]{1,0:T(8,128)(2,1)S(1)}, s32[8,128]{1,0:T(8,128)S(1)}) custom-call(bf16[48,2048]{1,0:T(8,128)(2,1)S(1)} %get-tuple-element.126.x_ref, bf16[128,128]{1,0:T(8,128)(2,1)S(1)} %get-tuple-element.134.mask_ref, bf16[32,2048]{1,0:T(8,128)(2,1)S(1)} %collective-permute-done.17.rest_0_, ...), custom_call_target="tpu_custom_call" | custom-call | flops 50331648 | tf_op jit(solution)/shard_map/mix_far/pallas_call | solution.py:25
  32.1 0.5 collective-permute-start.23
  32.5 1.1 %mix_near.3 = (bf16[48,2048]{1,0:T(8,128)(2,1)S(1)}, bf16[128,2048]{1,0:T(8,128)(2,1)S(1)}) custom-call(bf16[176,2048]{1,0:T(8,128)(2,1)S(1)} %get-tuple-element.122.x_ref, bf16[176,128]{1,0:T(8,128)(2,1)S(1)} %get-tuple-element.123.mask_ref, bf16[32,2048]{1,0:T(8,128)(2,1)S(1)} %collective-permute-done.17.rest_0_, ...), custom_call_target="tpu_custom_call" | custom-call | flops 184549376 | tf_op jit(solution)/shard_map/mix_near/pallas_call | solution.py:25
  33.7 0.3 collective-permute-start.20
  34.0 2.5 %mix_whole.3.refs_1_ = bf16[512,2048]{1,0:T(8,128)(2,1)S(1)} custom-call(bf16[512,2048]{1,0:T(8,128)(2,1)S(1)} %normalize.1.x_ref, bf16[512,128]{1,0:T(8,128)(2,1)S(1)} %get-tuple-element.117.mask_ref, bf16[32,2048]{1,0:T(8,128)(2,1)S(1)} %collective-permute-done.17.rest_0_, bf16[32,2048]{1,0:T(8,128)(2,1)S(1)} %collective-permute-done.18.rest_1_, ...), custom_call_target="tpu_custom_call" | custom-call | flops 536870912 | tf_op jit(solution)/shard_map/mix_whole/pallas_call | solution.py:25
  36.5 3.9 %collective-permute-done.23.far_ref = bf16[48,2048]{1,0:T(8,128)(2,1)S(1)} collective-permute-done((bf16[48,2048]{1,0:T(8,128)(2,1)S(1)}, bf16[48,2048]{1,0:T(8,128)(2,1)S(1)}, u32[]{:S(2)}, u32[]{:S(2)}) %collective-permute-start.23) | collective-permute-done | bytes 196640 | tf_op jit(solution)/shard_map/ppermute | solution.py:435
  40.4 0.3 unpack.9.base_ref
  40.6 0.0 collective-permute-done.20.core_ref
  40.6 0.3 combine.5
  40.9 1.5 %collective-permute-start.24 = (bf16[32,2048]{1,0:T(8,128)(2,1)S(1)}, bf16[32,2048]{1,0:T(8,128)(2,1)S(1)}, u32[]{:S(2)}, u32[]{:S(2)}) collective-permute-start(bf16[32,2048]{1,0:T(8,128)(2,1)S(1)} %get-tuple-element.140), channel_id=1, source_target_pairs={{0,24},{8,16},{16,8},{24,0},{1,25},{9,17},{17,9},{25,1},{2,26},{10... | collective-permute-start | bytes 393224 | tf_op jit(solution)/shard_map/ppermute | solution.py:429
  42.4 1.5 %collective-permute-start.25 = (bf16[32,2048]{1,0:T(8,128)(2,1)S(1)}, bf16[32,2048]{1,0:T(8,128)(2,1)S(1)}, u32[]{:S(2)}, u32[]{:S(2)}) collective-permute-start(bf16[32,2048]{1,0:T(8,128)(2,1)S(1)} %get-tuple-element.141), channel_id=1, source_target_pairs={{0,16},{8,24},{16,0},{24,8},{1,17},{9,25},{17,1},{25,9},{2,18},{10... | collective-permute-start | bytes 393224 | tf_op jit(solution)/shard_map/ppermute | solution.py:429
  43.9 0.6 %collective-permute-start.26 = (bf16[32,2048]{1,0:T(8,128)(2,1)S(1)}, bf16[32,2048]{1,0:T(8,128)(2,1)S(1)}, u32[]{:S(2)}, u32[]{:S(2)}) collective-permute-start(bf16[32,2048]{1,0:T(8,128)(2,1)S(1)} %get-tuple-element.142), channel_id=1, source_target_pairs={{0,8},{8,0},{16,24},{24,16},{1,9},{9,1},{17,25},{25,17},{2,10},{10... | collective-permute-start | bytes 393224 | tf_op jit(solution)/shard_map/ppermute | solution.py:429
  44.5 0.5 slice.16
  45.6 1.3 %collective-permute-done.24 = bf16[32,2048]{1,0:T(8,128)(2,1)S(1)} collective-permute-done((bf16[32,2048]{1,0:T(8,128)(2,1)S(1)}, bf16[32,2048]{1,0:T(8,128)(2,1)S(1)}, u32[]{:S(2)}, u32[]{:S(2)}) %collective-permute-start.24) | collective-permute-done | bytes 131104 | tf_op jit(solution)/shard_map/ppermute | solution.py:429
  47.0 1.3 %collective-permute-done.25 = bf16[32,2048]{1,0:T(8,128)(2,1)S(1)} collective-permute-done((bf16[32,2048]{1,0:T(8,128)(2,1)S(1)}, bf16[32,2048]{1,0:T(8,128)(2,1)S(1)}, u32[]{:S(2)}, u32[]{:S(2)}) %collective-permute-start.25) | collective-permute-done | bytes 131104 | tf_op jit(solution)/shard_map/ppermute | solution.py:429
  48.3 0.6 %collective-permute-done.26 = bf16[32,2048]{1,0:T(8,128)(2,1)S(1)} collective-permute-done((bf16[32,2048]{1,0:T(8,128)(2,1)S(1)}, bf16[32,2048]{1,0:T(8,128)(2,1)S(1)}, u32[]{:S(2)}, u32[]{:S(2)}) %collective-permute-start.26) | collective-permute-done | bytes 131104 | tf_op jit(solution)/shard_map/ppermute | solution.py:429
  48.9 3.6 %conditional.1 = (bf16[1,1,512,2048]{3,2,1,0:T(8,128)(2,1)}) conditional(s32[]{:T(128)} %bitcast.6, (bf16[512,2048]{1,0:T(8,128)(2,1)S(1)}, bf16[512,128]{1,0:T(8,128)(2,1)S(1)}, bf16[32,2048]{1,0:T(8,128)(2,1)S(1)}, bf16[32,2048]{1,0:T(8,128)(2,1)S(1)}, bf16[32,2048]{1,0:T(8,128)(2,1)S(1)}, /*index=5*/bf16[32,2048]{1,0:T(8,128)(2,1)S(1)}) %tuple.13, ...), branch_computations={%region_0.0_spmd, %region_1.0_spmd} | conditional | flops 53087698944 | bytes 121962904 | solution.py:495
  48.9 3.4 %mix.2 = bf16[512,2048]{1,0:T(8,128)(2,1)} custom-call(bf16[512,2048]{1,0:T(8,128)(2,1)S(1)} %get-tuple-element.53.x_ref, bf16[512,128]{1,0:T(8,128)(2,1)S(1)} %get-tuple-element.54.mask_ref, bf16[32,2048]{1,0:T(8,128)(2,1)S(1)} %get-tuple-element.55.rest_0_, bf16[32,2048]{1,0:T(8,128)(2,1)S(1)} %get-tuple-element.56.rest_1_, ...), custom_call_target="tpu_custom_call" | custom-call | flops 536870912 | bytes 4194304 | tf_op jit(solution)/shard_map/cond/branch_0_fun/mix/pallas_call | solution.py:25
  (1 shorter events, 0.0 us)
Async XLA Ops:
  0.0 5.5 %collective-permute-start.10 = (s32[4,32]{1,0:T(4,128)}, s32[4,32]{1,0:T(4,128)S(1)}, u32[]{:S(2)}, u32[]{:S(2)}) collective-permute-start(s32[4,32]{1,0:T(4,128)} %bitcast.12), channel_id=1, source_target_pairs={{0,8},{8,0},{16,24},{24,16},{1,9},{9,1},{17,25},{25,17},{2,10},{10... | collective-permute-start | bytes 1544 | tf_op jit(solution)/shard_map/ppermute | solution.py:429
  2.9 3.8 %collective-permute-start.11 = (s32[4,32]{1,0:T(4,128)}, s32[4,32]{1,0:T(4,128)S(1)}, u32[]{:S(2)}, u32[]{:S(2)}) collective-permute-start(s32[4,32]{1,0:T(4,128)} %bitcast.13), channel_id=1, source_target_pairs={{0,16},{8,24},{16,0},{24,8},{1,17},{9,25},{17,1},{25,9},{2,18},{10... | collective-permute-start | bytes 1544 | tf_op jit(solution)/shard_map/ppermute | solution.py:429
  4.5 4.7 %collective-permute-start.12 = (s32[4,32]{1,0:T(4,128)}, s32[4,32]{1,0:T(4,128)S(1)}, u32[]{:S(2)}, u32[]{:S(2)}) collective-permute-start(s32[4,32]{1,0:T(4,128)} %bitcast.14), channel_id=1, source_target_pairs={{0,24},{8,16},{16,8},{24,0},{1,25},{9,17},{17,9},{25,1},{2,26},{10... | collective-permute-start | bytes 1544 | tf_op jit(solution)/shard_map/ppermute | solution.py:429
  9.6 4.9 %collective-permute-start.13 = (s32[8,128]{1,0:T(8,128)S(1)}, s32[8,128]{1,0:T(8,128)S(1)}, u32[]{:S(2)}, u32[]{:S(2)}) collective-permute-start(s32[8,128]{1,0:T(8,128)S(1)} %get-tuple-element.118.refs_0_), channel_id=1, source_target_pairs={{0,7},{1,2},{2,1},{3,4},{4,3},{5,6},{6,5},{7,0},{8,15},{9,10},{10,... | collective-permute-start | bytes 12296 | tf_op jit(solution)/shard_map/ppermute | solution.py:435
  15.0 8.2 %collective-permute-start.16 = (bf16[48,2048]{1,0:T(8,128)(2,1)S(1)}, bf16[48,2048]{1,0:T(8,128)(2,1)S(1)}, u32[]{:S(2)}, u32[]{:S(2)}) collective-permute-start(bf16[48,2048]{1,0:T(8,128)(2,1)S(1)} %get-tuple-element.126.x_ref), channel_id=1, source_target_pairs={{0,7},{1,2},{2,1},{3,4},{4,3},{5,6},{6,5},{7,0},{8,15},{9,10},{10,... | collective-permute-start | bytes 589832 | tf_op jit(solution)/shard_map/ppermute | solution.py:435
  16.4 1.2 %collective-permute-start.14 = (s32[8,128]{1,0:T(8,128)S(1)}, s32[8,128]{1,0:T(8,128)S(1)}, u32[]{:S(2)}, u32[]{:S(2)}) collective-permute-start(s32[8,128]{1,0:T(8,128)S(1)} %get-tuple-element.121), channel_id=1, source_target_pairs={{0,1},{1,0},{2,3},{3,2},{4,5},{5,4},{6,7},{7,6},{8,9},{9,8},{10,11... | collective-permute-start | bytes 12296 | tf_op jit(solution)/shard_map/ppermute | solution.py:438
  18.8 4.7 %collective-permute-start.15 = (bf16[48,2048]{1,0:T(8,128)(2,1)S(1)}, bf16[48,2048]{1,0:T(8,128)(2,1)S(1)}, u32[]{:S(2)}, u32[]{:S(2)}) collective-permute-start(bf16[48,2048]{1,0:T(8,128)(2,1)S(1)} %get-tuple-element.124), channel_id=1, source_target_pairs={{0,1},{1,0},{2,3},{3,2},{4,5},{5,4},{6,7},{7,6},{8,9},{9,8},{10,11... | collective-permute-start | bytes 589832 | tf_op jit(solution)/shard_map/ppermute | solution.py:438
  23.8 7.5 %collective-permute-start.17 = (bf16[32,2048]{1,0:T(8,128)(2,1)S(1)}, bf16[32,2048]{1,0:T(8,128)(2,1)S(1)}, u32[]{:S(2)}, u32[]{:S(2)}) collective-permute-start(bf16[32,2048]{1,0:T(8,128)(2,1)S(1)} %get-tuple-element.129), channel_id=1, source_target_pairs={{0,24},{8,16},{16,8},{24,0},{1,25},{9,17},{17,9},{25,1},{2,26},{10... | collective-permute-start | bytes 393224 | tf_op jit(solution)/shard_map/ppermute | solution.py:429
  24.4 7.0 %collective-permute-start.18 = (bf16[32,2048]{1,0:T(8,128)(2,1)S(1)}, bf16[32,2048]{1,0:T(8,128)(2,1)S(1)}, u32[]{:S(2)}, u32[]{:S(2)}) collective-permute-start(bf16[32,2048]{1,0:T(8,128)(2,1)S(1)} %get-tuple-element.130), channel_id=1, source_target_pairs={{0,16},{8,24},{16,0},{24,8},{1,17},{9,25},{17,1},{25,9},{2,18},{10... | collective-permute-start | bytes 393224 | tf_op jit(solution)/shard_map/ppermute | solution.py:429
  25.9 5.5 %collective-permute-start.19 = (bf16[32,2048]{1,0:T(8,128)(2,1)S(1)}, bf16[32,2048]{1,0:T(8,128)(2,1)S(1)}, u32[]{:S(2)}, u32[]{:S(2)}) collective-permute-start(bf16[32,2048]{1,0:T(8,128)(2,1)S(1)} %get-tuple-element.131), channel_id=1, source_target_pairs={{0,8},{8,0},{16,24},{24,16},{1,9},{9,1},{17,25},{25,17},{2,10},{10... | collective-permute-start | bytes 393224 | tf_op jit(solution)/shard_map/ppermute | solution.py:429
  27.4 3.9 %collective-permute-start.21 = (s32[8,128]{1,0:T(8,128)S(1)}, s32[8,128]{1,0:T(8,128)S(1)}, u32[]{:S(2)}, u32[]{:S(2)}) collective-permute-start(s32[8,128]{1,0:T(8,128)S(1)} %get-tuple-element.135.rest_4_), channel_id=1, source_target_pairs={{0,3},{1,4},{2,5},{3,6},{4,7},{5,0},{6,1},{7,2},{8,11},{9,12},{10,... | collective-permute-start | bytes 12296 | tf_op jit(solution)/shard_map/ppermute | solution.py:432
  27.4 4.0 %collective-permute-start.22 = (s32[8,128]{1,0:T(8,128)S(1)}, s32[8,128]{1,0:T(8,128)S(1)}, u32[]{:S(2)}, u32[]{:S(2)}) collective-permute-start(s32[8,128]{1,0:T(8,128)S(1)} %get-tuple-element.135.rest_4_), channel_id=1, source_target_pairs={{0,5},{1,6},{2,7},{3,0},{4,1},{5,2},{6,3},{7,4},{8,13},{9,14},{10,... | collective-permute-start | bytes 12296 | tf_op jit(solution)/shard_map/ppermute | solution.py:432
  32.1 8.3 %collective-permute-start.23 = (bf16[48,2048]{1,0:T(8,128)(2,1)S(1)}, bf16[48,2048]{1,0:T(8,128)(2,1)S(1)}, u32[]{:S(2)}, u32[]{:S(2)}) collective-permute-start(bf16[48,2048]{1,0:T(8,128)(2,1)S(1)} %get-tuple-element.136), channel_id=1, source_target_pairs={{0,7},{1,2},{2,1},{3,4},{4,3},{5,6},{6,5},{7,0},{8,15},{9,10},{10,... | collective-permute-start | bytes 589832 | tf_op jit(solution)/shard_map/ppermute | solution.py:435
  33.7 7.0 %collective-permute-start.20 = (bf16[48,2048]{1,0:T(8,128)(2,1)S(1)}, bf16[48,2048]{1,0:T(8,128)(2,1)S(1)}, u32[]{:S(2)}, u32[]{:S(2)}) collective-permute-start(bf16[48,2048]{1,0:T(8,128)(2,1)S(1)} %get-tuple-element.133), channel_id=1, source_target_pairs={{0,1},{1,0},{2,3},{3,2},{4,5},{5,4},{6,7},{7,6},{8,9},{9,8},{10,11... | collective-permute-start | bytes 589832 | tf_op jit(solution)/shard_map/ppermute | solution.py:438
  40.9 6.0 %collective-permute-start.24 = (bf16[32,2048]{1,0:T(8,128)(2,1)S(1)}, bf16[32,2048]{1,0:T(8,128)(2,1)S(1)}, u32[]{:S(2)}, u32[]{:S(2)}) collective-permute-start(bf16[32,2048]{1,0:T(8,128)(2,1)S(1)} %get-tuple-element.140), channel_id=1, source_target_pairs={{0,24},{8,16},{16,8},{24,0},{1,25},{9,17},{17,9},{25,1},{2,26},{10... | collective-permute-start | bytes 393224 | tf_op jit(solution)/shard_map/ppermute | solution.py:429
  42.4 5.8 %collective-permute-start.25 = (bf16[32,2048]{1,0:T(8,128)(2,1)S(1)}, bf16[32,2048]{1,0:T(8,128)(2,1)S(1)}, u32[]{:S(2)}, u32[]{:S(2)}) collective-permute-start(bf16[32,2048]{1,0:T(8,128)(2,1)S(1)} %get-tuple-element.141), channel_id=1, source_target_pairs={{0,16},{8,24},{16,0},{24,8},{1,17},{9,25},{17,1},{25,9},{2,18},{10... | collective-permute-start | bytes 393224 | tf_op jit(solution)/shard_map/ppermute | solution.py:429
  43.9 5.0 %collective-permute-start.26 = (bf16[32,2048]{1,0:T(8,128)(2,1)S(1)}, bf16[32,2048]{1,0:T(8,128)(2,1)S(1)}, u32[]{:S(2)}, u32[]{:S(2)}) collective-permute-start(bf16[32,2048]{1,0:T(8,128)(2,1)S(1)} %get-tuple-element.142), channel_id=1, source_target_pairs={{0,8},{8,0},{16,24},{24,16},{1,9},{9,1},{17,25},{25,17},{2,10},{10... | collective-permute-start | bytes 393224 | tf_op jit(solution)/shard_map/ppermute | solution.py:429

commit v12 on v11

--- a/solution.py
+++ b/solution.py
@@ -104,7 +104,7 @@
 
 
 def list_kernel(rows, *refs):
-    parts, refs = refs[:-5], refs[-5:]
+    parts, refs = refs[-6::-1], refs[-5:]
     own_ref, far_ref, core_ref, expand_far_ref, expand_core_ref = refs
     total = own_ref.shape[1]
     lane = lax.broadcasted_iota(jnp.int32, (total, total), 1)
@@ -145,7 +145,7 @@
         "list",
         functools.partial(list_kernel, rows),
         [int32(8, total)] * 3 + [bf16(total, total)] * 2,
-        *parts,
+        *reversed(parts),
         flops=40 * total * total,
     )
 
@@ -302,24 +302,47 @@
     return normalize(mixed).astype(jnp.bfloat16)
 
 
-def far_mix_kernel(servers, x_ref, mask_ref, *rest):
+def at_end(groups):
+    group = lax.axis_index("rep")
+    return (group == 0) | (group == groups - 1)
+
+
+def near_mix(x_ref, mask_ref, buffer, core_ref, own_ref):
+    weights = weigh(x_ref[...], buffer[...], mask_ref[...])
+    mixed = mix(x_ref[...], weights, buffer[...])
+    core_ref[...] = mixed[: core_ref.shape[0]]
+    own_ref[...] = mixed[core_ref.shape[0] :]
+
+
+def far_mix_kernel(groups, servers, far_ref, far_mask_ref, near_ref, near_mask_ref, *rest):
     parts, rest = rest[:servers], rest[servers:]
-    *most_refs, out_ref, most_ref, buffer = rest
+    *most_refs, out_ref, core_ref, own_ref, most_ref, buffer = rest
     most_ref[...] = functools.reduce(jnp.maximum, [ref[...] for ref in most_refs])
     fill(buffer, parts)
-    weights = weigh(x_ref[...], buffer[...], mask_ref[: x_ref.shape[0]])
-    out_ref[...] = mix(x_ref[...], weights, buffer[...])
-
-
-def far_mix_call(x, mask, parts, mosts):
-    rows, width = x.shape
-    total, servers = mask.shape[1], len(parts)
+    weights = weigh(far_ref[...], buffer[...], far_mask_ref[: far_ref.shape[0]])
+    out_ref[...] = mix(far_ref[...], weights, buffer[...])
+
+    @pl.when(jnp.logical_not(at_end(groups)))
+    def _():
+        near_mix(near_ref, near_mask_ref, buffer, core_ref, own_ref)
+
+
+def far_mix_call(groups, far, far_mask, near, near_mask, parts, mosts):
+    rows, width = far.shape
+    total, servers = far_mask.shape[1], len(parts)
     return kernel_call(
         "mix_far",
-        functools.partial(far_mix_kernel, servers),
-        [bf16(rows, width), int32(*mosts[0].shape)],
-        x,
-        mask,
+        functools.partial(far_mix_kernel, groups, servers),
+        [
+            bf16(rows, width),
+            bf16(near.shape[0] - total, width),
+            bf16(total, width),
+            int32(*mosts[0].shape),
+        ],
+        far,
+        far_mask,
+        near,
+        near_mask,
         *reversed(parts),
         *mosts,
         flops=4 * total * rows * width,
@@ -327,27 +350,30 @@
     )
 
 
-def near_mix_kernel(servers, x_ref, mask_ref, *rest):
+def end_mix_kernel(groups, servers, near_ref, mask_ref, core_in, own_in, *rest):
     parts, (core_ref, own_ref, buffer) = rest[:servers], rest[servers:]
-    fill(buffer, parts)
-    weights = weigh(x_ref[...], buffer[...], mask_ref[...])
-    mixed = mix(x_ref[...], weights, buffer[...])
-    core_ref[...] = mixed[: core_ref.shape[0]]
-    own_ref[...] = mixed[core_ref.shape[0] :]
-
-
-def near_mix_call(x, mask, parts):
-    rows, width = x.shape
+
+    @pl.when(at_end(groups))
+    def _():
+        fill(buffer, parts)
+        near_mix(near_ref, mask_ref, buffer, core_ref, own_ref)
+
+
+def end_mix_call(groups, near, mask, core, own, parts):
+    rows, width = near.shape
     total, servers = mask.shape[1], len(parts)
     return kernel_call(
-        "mix_near",
-        functools.partial(near_mix_kernel, servers),
-        [bf16(rows - total, width), bf16(total, width)],
-        x,
+        "mix_near_at_ends",
+        functools.partial(end_mix_kernel, groups, servers),
+        [bf16(*core.shape), bf16(*own.shape)],
+        near,
         mask,
+        core,
+        own,
         *reversed(parts),
         flops=4 * total * rows * width,
         scratch=[pltpu.VMEM((total, width), jnp.bfloat16)],
+        input_output_aliases={2: 0, 3: 1},
     )
 
 
@@ -447,8 +473,10 @@
         return most, turned(parts)
 
     def next_round(x, mask, far, near, far_mask, near_mask, expands, parts, mosts):
-        far, most = far_mix_call(far, far_mask, parts, mosts)
-        core, own = near_mix_call(near, near_mask, parts)
+        far, core, own, most = far_mix_call(
+            groups, far, far_mask, near, near_mask, parts, mosts
+        )
+        core, own = end_mix_call(groups, near, near_mask, core, own, parts)
         x = whole_call(x, mask, parts)
         return x, *exchange(expands, far, core, own, most, after=[x])
 

time: 52.8 us -> 52.3 us (level)
  waiting for transfers between devices: 19.1 us -> 17.3 us
  starting transfers between devices: 18.1 us -> 19.2 us
    ppermute x3, waiting for transfers between devices: 9.68 us -> 7.33 us  [across(): return lax.ppermute(value, 'rep', beyond)]
    ppermute x3, starting transfers between devices: 3.26 us -> 4.73 us  [across(): return lax.ppermute(value, 'rep', beyond)]
    ppermute x9, waiting for transfers between devices: 6.94 us -> 7.5 us  [turn(): return lax.ppermute(value, 'clus', [(c, c ^ d) for c in range(servers)])]
  transfers between devices with their start and end apart: 17 -> 17, of which waited for: 10 -> 11; matrix products, arithmetic and copies ran while one was open for 1% -> 1% of each run, Pallas kernels for 16% -> 16%
where the time goes in v12:
time: 52.3 us; the launch traced here: 52.1 us
  starting transfers between devices  19.2 us (37%)
  waiting for transfers between devices  17.3 us (33%)
  Pallas kernels  13.8 us (26%)
  between operations  0.96 us (2%)
    pallas_call x13, Pallas kernels, kernel_call(): pl.pallas_call(kernel, out_shape=outs, scratch_shapes=scratch, compiler_p...  13.8 us
    ppermute x9, starting transfers between devices, turn(): return lax.ppermute(value, 'clus', [(c, c ^ d) for c in range(servers)])  11.6 us
    ppermute x9, waiting for transfers between devices, turn(): return lax.ppermute(value, 'clus', [(c, c ^ d) for c in range(servers)])  7.5 us
    ppermute x3, waiting for transfers between devices, across(): return lax.ppermute(value, 'rep', beyond)  7.33 us
    ppermute x3, starting transfers between devices, across(): return lax.ppermute(value, 'rep', beyond)  4.73 us
    ppermute x2, starting transfers between devices, shift(): lax.ppermute(value, 'rep', [(g, (g + by) % groups) for g in range(groups)])  2.64 us
    ppermute x2, waiting for transfers between devices, shift(): lax.ppermute(value, 'rep', [(g, (g + by) % groups) for g in range(groups)])  1.33 us
    ppermute x3, waiting for transfers between devices, inside(): return lax.ppermute(value, 'rep', within)  1.17 us
  transfers between devices with their start and end apart: 17, of which 11 were waited for; matrix products, arithmetic and copies ran while one was open for 1% of the time, Pallas kernels for 16%

profile of v12, /device:TPU:0, one launch (start us, length us, event | category | flops | bytes accessed | tf_op | source)
XLA Modules:
  0.0 52.1 jit_solution(2921552563420555612)
XLA Ops:
  0.0 3.9 %collective-permute-start.10 = (s32[4,32]{1,0:T(4,128)}, s32[4,32]{1,0:T(4,128)S(1)}, u32[]{:S(2)}, u32[]{:S(2)}) collective-permute-start(s32[4,32]{1,0:T(4,128)} %bitcast.12), channel_id=1, source_target_pairs={{0,24},{8,16},{16,8},{24,0},{1,25},{9,17},{17,9},{25,1},{2,26},{10... | collective-permute-start | bytes 1544 | tf_op jit(solution)/shard_map/ppermute | solution.py:455
  3.9 0.5 collective-permute-start.11
  4.4 0.1 collective-permute-start.12
  4.5 1.0 %mask.1 = (bf16[512,128]{1,0:T(8,128)(2,1)S(1)}, s32[4,32]{1,0:T(4,128)S(1)}) custom-call(s32[10,1,512]{2,1,0:T(1,128)} %bitcast.11, s32[4,32]{1,0:T(4,128)} %bitcast.15), custom_call_target="tpu_custom_call" | custom-call | flops 1310720 | bytes 131072 | tf_op jit(solution)/shard_map/mask/pallas_call | solution.py:25
  5.5 0.2 collective-permute-done.10.refs_0_
  5.7 2.0 %collective-permute-done.11.refs_1_ = s32[4,32]{1,0:T(4,128)S(1)} collective-permute-done((s32[4,32]{1,0:T(4,128)}, s32[4,32]{1,0:T(4,128)S(1)}, u32[]{:S(2)}, u32[]{:S(2)}) %collective-permute-start.11) | collective-permute-done | bytes 544 | tf_op jit(solution)/shard_map/ppermute | solution.py:455
  7.7 0.5 collective-permute-done.12.refs_2_
  8.2 0.5 list.1
  8.7 1.4 %collective-permute-start.13 = (s32[8,128]{1,0:T(8,128)S(1)}, s32[8,128]{1,0:T(8,128)S(1)}, u32[]{:S(2)}, u32[]{:S(2)}) collective-permute-start(s32[8,128]{1,0:T(8,128)S(1)} %get-tuple-element.122.refs_0_), channel_id=1, source_target_pairs={{0,7},{1,2},{2,1},{3,4},{4,3},{5,6},{6,5},{7,0},{8,15},{9,10},{10,... | collective-permute-start | bytes 12296 | tf_op jit(solution)/shard_map/ppermute | solution.py:461
  10.1 1.9 %normalize.1.x_ref = bf16[512,2048]{1,0:T(8,128)(2,1)S(1)} custom-call(bf16[512,2048]{1,0:T(8,128)(2,1)} %bitcast.10), custom_call_target="tpu_custom_call" | custom-call | flops 6291456 | bytes 4194304 | tf_op jit(solution)/shard_map/normalize/pallas_call | solution.py:25
  11.9 1.6 %collective-permute-done.13.beyond_ref.refs_1_ = s32[8,128]{1,0:T(8,128)S(1)} collective-permute-done((s32[8,128]{1,0:T(8,128)S(1)}, s32[8,128]{1,0:T(8,128)S(1)}, u32[]{:S(2)}, u32[]{:S(2)}) %collective-permute-start.13) | collective-permute-done | bytes 4128 | tf_op jit(solution)/shard_map/ppermute | solution.py:461
  13.6 0.5 pack_far.1
  14.1 1.4 %collective-permute-start.16 = (bf16[48,2048]{1,0:T(8,128)(2,1)S(1)}, bf16[48,2048]{1,0:T(8,128)(2,1)S(1)}, u32[]{:S(2)}, u32[]{:S(2)}) collective-permute-start(bf16[48,2048]{1,0:T(8,128)(2,1)S(1)} %get-tuple-element.128.far_ref), channel_id=1, source_target_pairs={{0,7},{1,2},{2,1},{3,4},{4,3},{5,6},{6,5},{7,0},{8,15},{9,10},{10,... | collective-permute-start | bytes 589832 | tf_op jit(solution)/shard_map/ppermute | solution.py:461
  15.5 0.0 collective-permute-start.14
  15.5 1.2 %collective-permute-done.14.refs_2_ = s32[8,128]{1,0:T(8,128)S(1)} collective-permute-done((s32[8,128]{1,0:T(8,128)S(1)}, s32[8,128]{1,0:T(8,128)S(1)}, u32[]{:S(2)}, u32[]{:S(2)}) %collective-permute-start.14) | collective-permute-done | bytes 4128 | tf_op jit(solution)/shard_map/ppermute | solution.py:464
  16.7 1.2 %serve_near.1 = (bf16[48,2048]{1,0:T(8,128)(2,1)S(1)}, bf16[128,2048]{1,0:T(8,128)(2,1)S(1)}, bf16[176,2048]{1,0:T(8,128)(2,1)S(1)}, bf16[80,2048]{1,0:T(8,128)(...) custom-call(bf16[512,2048]{1,0:T(8,128)(2,1)S(1)} %normalize.1.x_ref, ...), custom_call_target="tpu_custom_call" | custom-call | flops 805306368 | tf_op jit(solution)/shard_map/serve_near/pallas_call | solution.py:25
  17.9 0.2 collective-permute-start.15
  18.1 4.2 %collective-permute-done.16.far_ref = bf16[48,2048]{1,0:T(8,128)(2,1)S(1)} collective-permute-done((bf16[48,2048]{1,0:T(8,128)(2,1)S(1)}, bf16[48,2048]{1,0:T(8,128)(2,1)S(1)}, u32[]{:S(2)}, u32[]{:S(2)}) %collective-permute-start.16) | collective-permute-done | bytes 196640 | tf_op jit(solution)/shard_map/ppermute | solution.py:461
  22.3 0.3 unpack.8.base_ref
  22.6 0.0 collective-permute-done.15.core_ref
  22.6 0.3 combine.4
  22.9 1.6 %collective-permute-start.17 = (bf16[32,2048]{1,0:T(8,128)(2,1)S(1)}, bf16[32,2048]{1,0:T(8,128)(2,1)S(1)}, u32[]{:S(2)}, u32[]{:S(2)}) collective-permute-start(bf16[32,2048]{1,0:T(8,128)(2,1)S(1)} %get-tuple-element.134), channel_id=1, source_target_pairs={{0,24},{8,16},{16,8},{24,0},{1,25},{9,17},{17,9},{25,1},{2,26},{10... | collective-permute-start | bytes 393224 | tf_op jit(solution)/shard_map/ppermute | solution.py:455
  24.4 0.5 collective-permute-start.18
  24.9 1.5 %collective-permute-start.19 = (bf16[32,2048]{1,0:T(8,128)(2,1)S(1)}, bf16[32,2048]{1,0:T(8,128)(2,1)S(1)}, u32[]{:S(2)}, u32[]{:S(2)}) collective-permute-start(bf16[32,2048]{1,0:T(8,128)(2,1)S(1)} %get-tuple-element.136), channel_id=1, source_target_pairs={{0,8},{8,0},{16,24},{24,16},{1,9},{9,1},{17,25},{25,17},{2,10},{10... | collective-permute-start | bytes 393224 | tf_op jit(solution)/shard_map/ppermute | solution.py:455
  26.4 0.0 collective-permute-start.20
  26.4 2.6 %collective-permute-start.21 = (s32[8,128]{1,0:T(8,128)S(1)}, s32[8,128]{1,0:T(8,128)S(1)}, u32[]{:S(2)}, u32[]{:S(2)}) collective-permute-start(s32[8,128]{1,0:T(8,128)S(1)} %get-tuple-element.138.rest_4_), channel_id=1, source_target_pairs={{0,5},{1,6},{2,7},{3,0},{4,1},{5,2},{6,3},{7,4},{8,13},{9,14},{10,... | collective-permute-start | bytes 12296 | tf_op jit(solution)/shard_map/ppermute | solution.py:458
  29.1 1.3 %collective-permute-done.20.rest_5_ = s32[8,128]{1,0:T(8,128)S(1)} collective-permute-done((s32[8,128]{1,0:T(8,128)S(1)}, s32[8,128]{1,0:T(8,128)S(1)}, u32[]{:S(2)}, u32[]{:S(2)}) %collective-permute-start.20) | collective-permute-done | bytes 4128 | tf_op jit(solution)/shard_map/ppermute | solution.py:458
  30.4 0.0 collective-permute-done.21.rest_6_
  30.4 0.0 collective-permute-done.17.rest_0_
  30.4 0.0 collective-permute-done.18.rest_1_
  30.4 0.7 %mix_far.3 = (bf16[48,2048]{1,0:T(8,128)(2,1)S(1)}, bf16[48,2048]{1,0:T(8,128)(2,1)S(1)}, bf16[128,2048]{1,0:T(8,128)(2,1)S(1)}, s32[8,128]{1,0:T(8,128)S(1)}) custom-call(bf16[48,2048]{1,0:T(8,128)(2,1)S(1)} %get-tuple-element.128.far_ref, bf16[128,128]{1,0:T(8,128)(2,1)S(1)} %get-tuple-element.129.far_mask_ref, ...), custom_call_target="tpu_custom_call" | custom-call | flops 50331648 | tf_op jit(solution)/shard_map/mix_far/pallas_call | solution.py:25
  31.1 1.9 %collective-permute-start.23 = (bf16[48,2048]{1,0:T(8,128)(2,1)S(1)}, bf16[48,2048]{1,0:T(8,128)(2,1)S(1)}, u32[]{:S(2)}, u32[]{:S(2)}) collective-permute-start(bf16[48,2048]{1,0:T(8,128)(2,1)S(1)} %get-tuple-element.142), channel_id=1, source_target_pairs={{0,7},{1,2},{2,1},{3,4},{4,3},{5,6},{6,5},{7,0},{8,15},{9,10},{10,... | collective-permute-start | bytes 589832 | tf_op jit(solution)/shard_map/ppermute | solution.py:461
  33.1 1.1 %mix_near_at_ends.3 = (bf16[48,2048]{1,0:T(8,128)(2,1)S(1)}, bf16[128,2048]{1,0:T(8,128)(2,1)S(1)}) custom-call(bf16[176,2048]{1,0:T(8,128)(2,1)S(1)} %get-tuple-element.126.near_ref, bf16[176,128]{1,0:T(8,128)(2,1)S(1)} %get-tuple-element.127.near_mask_ref.mask_ref, ...), custom_call_target="tpu_custom_call", output_to_operand_aliasing={{0}: (2, {}), {1}: (3, {})} | custom-call | flops 184549376 | tf_op jit(solution)/shard_map/mix_near_at_ends/pallas_call | solution.py:25
  34.2 0.1 collective-permute-start.22
  34.2 2.5 %mix_whole.3.refs_1_ = bf16[512,2048]{1,0:T(8,128)(2,1)S(1)} custom-call(bf16[512,2048]{1,0:T(8,128)(2,1)S(1)} %normalize.1.x_ref, bf16[512,128]{1,0:T(8,128)(2,1)S(1)} %get-tuple-element.121.mask_ref, bf16[32,2048]{1,0:T(8,128)(2,1)S(1)} %collective-permute-done.17.rest_0_, bf16[32,2048]{1,0:T(8,128)(2,1)S(1)} %collective-permute-done.18.rest_1_, ...), custom_call_target="tpu_custom_call" | custom-call | flops 536870912 | tf_op jit(solution)/shard_map/mix_whole/pallas_call | solution.py:25
  36.7 1.5 %collective-permute-done.23.far_ref = bf16[48,2048]{1,0:T(8,128)(2,1)S(1)} collective-permute-done((bf16[48,2048]{1,0:T(8,128)(2,1)S(1)}, bf16[48,2048]{1,0:T(8,128)(2,1)S(1)}, u32[]{:S(2)}, u32[]{:S(2)}) %collective-permute-start.23) | collective-permute-done | bytes 196640 | tf_op jit(solution)/shard_map/ppermute | solution.py:461
  38.2 0.3 unpack.9.base_ref
  38.5 0.0 collective-permute-done.22.core_ref
  38.5 0.3 combine.5
  38.8 2.5 %collective-permute-start.24 = (bf16[32,2048]{1,0:T(8,128)(2,1)S(1)}, bf16[32,2048]{1,0:T(8,128)(2,1)S(1)}, u32[]{:S(2)}, u32[]{:S(2)}) collective-permute-start(bf16[32,2048]{1,0:T(8,128)(2,1)S(1)} %get-tuple-element.146), channel_id=1, source_target_pairs={{0,24},{8,16},{16,8},{24,0},{1,25},{9,17},{17,9},{25,1},{2,26},{10... | collective-permute-start | bytes 393224 | tf_op jit(solution)/shard_map/ppermute | solution.py:455
  41.3 0.5 collective-permute-start.25
  41.8 0.6 %collective-permute-start.26 = (bf16[32,2048]{1,0:T(8,128)(2,1)S(1)}, bf16[32,2048]{1,0:T(8,128)(2,1)S(1)}, u32[]{:S(2)}, u32[]{:S(2)}) collective-permute-start(bf16[32,2048]{1,0:T(8,128)(2,1)S(1)} %get-tuple-element.148), channel_id=1, source_target_pairs={{0,8},{8,0},{16,24},{24,16},{1,9},{9,1},{17,25},{25,17},{2,10},{10... | collective-permute-start | bytes 393224 | tf_op jit(solution)/shard_map/ppermute | solution.py:455
  42.4 0.5 slice.16
  43.5 2.6 %collective-permute-done.24 = bf16[32,2048]{1,0:T(8,128)(2,1)S(1)} collective-permute-done((bf16[32,2048]{1,0:T(8,128)(2,1)S(1)}, bf16[32,2048]{1,0:T(8,128)(2,1)S(1)}, u32[]{:S(2)}, u32[]{:S(2)}) %collective-permute-start.24) | collective-permute-done | bytes 131104 | tf_op jit(solution)/shard_map/ppermute | solution.py:455
  46.1 1.2 %collective-permute-done.25 = bf16[32,2048]{1,0:T(8,128)(2,1)S(1)} collective-permute-done((bf16[32,2048]{1,0:T(8,128)(2,1)S(1)}, bf16[32,2048]{1,0:T(8,128)(2,1)S(1)}, u32[]{:S(2)}, u32[]{:S(2)}) %collective-permute-start.25) | collective-permute-done | bytes 131104 | tf_op jit(solution)/shard_map/ppermute | solution.py:455
  47.4 0.9 %collective-permute-done.26 = bf16[32,2048]{1,0:T(8,128)(2,1)S(1)} collective-permute-done((bf16[32,2048]{1,0:T(8,128)(2,1)S(1)}, bf16[32,2048]{1,0:T(8,128)(2,1)S(1)}, u32[]{:S(2)}, u32[]{:S(2)}) %collective-permute-start.26) | collective-permute-done | bytes 131104 | tf_op jit(solution)/shard_map/ppermute | solution.py:455
  48.3 3.6 %conditional.1 = (bf16[1,1,512,2048]{3,2,1,0:T(8,128)(2,1)}) conditional(s32[]{:T(128)} %bitcast.6, (bf16[512,2048]{1,0:T(8,128)(2,1)S(1)}, bf16[512,128]{1,0:T(8,128)(2,1)S(1)}, bf16[32,2048]{1,0:T(8,128)(2,1)S(1)}, bf16[32,2048]{1,0:T(8,128)(2,1)S(1)}, bf16[32,2048]{1,0:T(8,128)(2,1)S(1)}, /*index=5*/bf16[32,2048]{1,0:T(8,128)(2,1)S(1)}) %tuple.13, ...), branch_computations={%region_0.0_spmd, %region_1.0_spmd} | conditional | flops 53087698944 | bytes 121962904 | solution.py:523
  48.3 3.4 %mix.2 = bf16[512,2048]{1,0:T(8,128)(2,1)} custom-call(bf16[512,2048]{1,0:T(8,128)(2,1)S(1)} %get-tuple-element.53.x_ref, bf16[512,128]{1,0:T(8,128)(2,1)S(1)} %get-tuple-element.54.mask_ref, bf16[32,2048]{1,0:T(8,128)(2,1)S(1)} %get-tuple-element.55.rest_0_, bf16[32,2048]{1,0:T(8,128)(2,1)S(1)} %get-tuple-element.56.rest_1_, ...), custom_call_target="tpu_custom_call" | custom-call | flops 536870912 | bytes 4194304 | tf_op jit(solution)/shard_map/cond/branch_0_fun/mix/pallas_call | solution.py:25
  (1 shorter events, 0.0 us)
Async XLA Ops:
  0.0 5.7 %collective-permute-start.10 = (s32[4,32]{1,0:T(4,128)}, s32[4,32]{1,0:T(4,128)S(1)}, u32[]{:S(2)}, u32[]{:S(2)}) collective-permute-start(s32[4,32]{1,0:T(4,128)} %bitcast.12), channel_id=1, source_target_pairs={{0,24},{8,16},{16,8},{24,0},{1,25},{9,17},{17,9},{25,1},{2,26},{10... | collective-permute-start | bytes 1544 | tf_op jit(solution)/shard_map/ppermute | solution.py:455
  3.9 3.8 %collective-permute-start.11 = (s32[4,32]{1,0:T(4,128)}, s32[4,32]{1,0:T(4,128)S(1)}, u32[]{:S(2)}, u32[]{:S(2)}) collective-permute-start(s32[4,32]{1,0:T(4,128)} %bitcast.13), channel_id=1, source_target_pairs={{0,16},{8,24},{16,0},{24,8},{1,17},{9,25},{17,1},{25,9},{2,18},{10... | collective-permute-start | bytes 1544 | tf_op jit(solution)/shard_map/ppermute | solution.py:455
  4.4 3.8 %collective-permute-start.12 = (s32[4,32]{1,0:T(4,128)}, s32[4,32]{1,0:T(4,128)S(1)}, u32[]{:S(2)}, u32[]{:S(2)}) collective-permute-start(s32[4,32]{1,0:T(4,128)} %bitcast.14), channel_id=1, source_target_pairs={{0,8},{8,0},{16,24},{24,16},{1,9},{9,1},{17,25},{25,17},{2,10},{10... | collective-permute-start | bytes 1544 | tf_op jit(solution)/shard_map/ppermute | solution.py:455
  8.7 4.9 %collective-permute-start.13 = (s32[8,128]{1,0:T(8,128)S(1)}, s32[8,128]{1,0:T(8,128)S(1)}, u32[]{:S(2)}, u32[]{:S(2)}) collective-permute-start(s32[8,128]{1,0:T(8,128)S(1)} %get-tuple-element.122.refs_0_), channel_id=1, source_target_pairs={{0,7},{1,2},{2,1},{3,4},{4,3},{5,6},{6,5},{7,0},{8,15},{9,10},{10,... | collective-permute-start | bytes 12296 | tf_op jit(solution)/shard_map/ppermute | solution.py:461
  14.1 8.2 %collective-permute-start.16 = (bf16[48,2048]{1,0:T(8,128)(2,1)S(1)}, bf16[48,2048]{1,0:T(8,128)(2,1)S(1)}, u32[]{:S(2)}, u32[]{:S(2)}) collective-permute-start(bf16[48,2048]{1,0:T(8,128)(2,1)S(1)} %get-tuple-element.128.far_ref), channel_id=1, source_target_pairs={{0,7},{1,2},{2,1},{3,4},{4,3},{5,6},{6,5},{7,0},{8,15},{9,10},{10,... | collective-permute-start | bytes 589832 | tf_op jit(solution)/shard_map/ppermute | solution.py:461
  15.5 1.2 %collective-permute-start.14 = (s32[8,128]{1,0:T(8,128)S(1)}, s32[8,128]{1,0:T(8,128)S(1)}, u32[]{:S(2)}, u32[]{:S(2)}) collective-permute-start(s32[8,128]{1,0:T(8,128)S(1)} %get-tuple-element.125), channel_id=1, source_target_pairs={{0,1},{1,0},{2,3},{3,2},{4,5},{5,4},{6,7},{7,6},{8,9},{9,8},{10,11... | collective-permute-start | bytes 12296 | tf_op jit(solution)/shard_map/ppermute | solution.py:464
  17.9 4.7 %collective-permute-start.15 = (bf16[48,2048]{1,0:T(8,128)(2,1)S(1)}, bf16[48,2048]{1,0:T(8,128)(2,1)S(1)}, u32[]{:S(2)}, u32[]{:S(2)}) collective-permute-start(bf16[48,2048]{1,0:T(8,128)(2,1)S(1)} %get-tuple-element.130), channel_id=1, source_target_pairs={{0,1},{1,0},{2,3},{3,2},{4,5},{5,4},{6,7},{7,6},{8,9},{9,8},{10,11... | collective-permute-start | bytes 589832 | tf_op jit(solution)/shard_map/ppermute | solution.py:464
  22.9 7.5 %collective-permute-start.17 = (bf16[32,2048]{1,0:T(8,128)(2,1)S(1)}, bf16[32,2048]{1,0:T(8,128)(2,1)S(1)}, u32[]{:S(2)}, u32[]{:S(2)}) collective-permute-start(bf16[32,2048]{1,0:T(8,128)(2,1)S(1)} %get-tuple-element.134), channel_id=1, source_target_pairs={{0,24},{8,16},{16,8},{24,0},{1,25},{9,17},{17,9},{25,1},{2,26},{10... | collective-permute-start | bytes 393224 | tf_op jit(solution)/shard_map/ppermute | solution.py:455
  24.4 6.0 %collective-permute-start.18 = (bf16[32,2048]{1,0:T(8,128)(2,1)S(1)}, bf16[32,2048]{1,0:T(8,128)(2,1)S(1)}, u32[]{:S(2)}, u32[]{:S(2)}) collective-permute-start(bf16[32,2048]{1,0:T(8,128)(2,1)S(1)} %get-tuple-element.135), channel_id=1, source_target_pairs={{0,16},{8,24},{16,0},{24,8},{1,17},{9,25},{17,1},{25,9},{2,18},{10... | collective-permute-start | bytes 393224 | tf_op jit(solution)/shard_map/ppermute | solution.py:455
  24.9 5.5 %collective-permute-start.19 = (bf16[32,2048]{1,0:T(8,128)(2,1)S(1)}, bf16[32,2048]{1,0:T(8,128)(2,1)S(1)}, u32[]{:S(2)}, u32[]{:S(2)}) collective-permute-start(bf16[32,2048]{1,0:T(8,128)(2,1)S(1)} %get-tuple-element.136), channel_id=1, source_target_pairs={{0,8},{8,0},{16,24},{24,16},{1,9},{9,1},{17,25},{25,17},{2,10},{10... | collective-permute-start | bytes 393224 | tf_op jit(solution)/shard_map/ppermute | solution.py:455
  26.4 3.9 %collective-permute-start.20 = (s32[8,128]{1,0:T(8,128)S(1)}, s32[8,128]{1,0:T(8,128)S(1)}, u32[]{:S(2)}, u32[]{:S(2)}) collective-permute-start(s32[8,128]{1,0:T(8,128)S(1)} %get-tuple-element.138.rest_4_), channel_id=1, source_target_pairs={{0,3},{1,4},{2,5},{3,6},{4,7},{5,0},{6,1},{7,2},{8,11},{9,12},{10,... | collective-permute-start | bytes 12296 | tf_op jit(solution)/shard_map/ppermute | solution.py:458
  26.4 4.0 %collective-permute-start.21 = (s32[8,128]{1,0:T(8,128)S(1)}, s32[8,128]{1,0:T(8,128)S(1)}, u32[]{:S(2)}, u32[]{:S(2)}) collective-permute-start(s32[8,128]{1,0:T(8,128)S(1)} %get-tuple-element.138.rest_4_), channel_id=1, source_target_pairs={{0,5},{1,6},{2,7},{3,0},{4,1},{5,2},{6,3},{7,4},{8,13},{9,14},{10,... | collective-permute-start | bytes 12296 | tf_op jit(solution)/shard_map/ppermute | solution.py:458
  31.1 7.1 %collective-permute-start.23 = (bf16[48,2048]{1,0:T(8,128)(2,1)S(1)}, bf16[48,2048]{1,0:T(8,128)(2,1)S(1)}, u32[]{:S(2)}, u32[]{:S(2)}) collective-permute-start(bf16[48,2048]{1,0:T(8,128)(2,1)S(1)} %get-tuple-element.142), channel_id=1, source_target_pairs={{0,7},{1,2},{2,1},{3,4},{4,3},{5,6},{6,5},{7,0},{8,15},{9,10},{10,... | collective-permute-start | bytes 589832 | tf_op jit(solution)/shard_map/ppermute | solution.py:461
  34.2 4.3 %collective-permute-start.22 = (bf16[48,2048]{1,0:T(8,128)(2,1)S(1)}, bf16[48,2048]{1,0:T(8,128)(2,1)S(1)}, u32[]{:S(2)}, u32[]{:S(2)}) collective-permute-start(bf16[48,2048]{1,0:T(8,128)(2,1)S(1)} %get-tuple-element.141), channel_id=1, source_target_pairs={{0,1},{1,0},{2,3},{3,2},{4,5},{5,4},{6,7},{7,6},{8,9},{9,8},{10,11... | collective-permute-start | bytes 589832 | tf_op jit(solution)/shard_map/ppermute | solution.py:464
  38.8 7.3 %collective-permute-start.24 = (bf16[32,2048]{1,0:T(8,128)(2,1)S(1)}, bf16[32,2048]{1,0:T(8,128)(2,1)S(1)}, u32[]{:S(2)}, u32[]{:S(2)}) collective-permute-start(bf16[32,2048]{1,0:T(8,128)(2,1)S(1)} %get-tuple-element.146), channel_id=1, source_target_pairs={{0,24},{8,16},{16,8},{24,0},{1,25},{9,17},{17,9},{25,1},{2,26},{10... | collective-permute-start | bytes 393224 | tf_op jit(solution)/shard_map/ppermute | solution.py:455
  41.3 6.1 %collective-permute-start.25 = (bf16[32,2048]{1,0:T(8,128)(2,1)S(1)}, bf16[32,2048]{1,0:T(8,128)(2,1)S(1)}, u32[]{:S(2)}, u32[]{:S(2)}) collective-permute-start(bf16[32,2048]{1,0:T(8,128)(2,1)S(1)} %get-tuple-element.147), channel_id=1, source_target_pairs={{0,16},{8,24},{16,0},{24,8},{1,17},{9,25},{17,1},{25,9},{2,18},{10... | collective-permute-start | bytes 393224 | tf_op jit(solution)/shard_map/ppermute | solution.py:455
  41.8 6.5 %collective-permute-start.26 = (bf16[32,2048]{1,0:T(8,128)(2,1)S(1)}, bf16[32,2048]{1,0:T(8,128)(2,1)S(1)}, u32[]{:S(2)}, u32[]{:S(2)}) collective-permute-start(bf16[32,2048]{1,0:T(8,128)(2,1)S(1)} %get-tuple-element.148), channel_id=1, source_target_pairs={{0,8},{8,0},{16,24},{24,16},{1,9},{9,1},{17,25},{25,17},{2,10},{10... | collective-permute-start | bytes 393224 | tf_op jit(solution)/shard_map/ppermute | solution.py:455

commit v13 on v11

--- a/solution.py
+++ b/solution.py
@@ -104,7 +104,7 @@
 
 
 def list_kernel(rows, *refs):
-    parts, refs = refs[:-5], refs[-5:]
+    parts, refs = refs[-6::-1], refs[-5:]
     own_ref, far_ref, core_ref, expand_far_ref, expand_core_ref = refs
     total = own_ref.shape[1]
     lane = lax.broadcasted_iota(jnp.int32, (total, total), 1)
@@ -145,7 +145,7 @@
         "list",
         functools.partial(list_kernel, rows),
         [int32(8, total)] * 3 + [bf16(total, total)] * 2,
-        *parts,
+        *reversed(parts),
         flops=40 * total * total,
     )
 
@@ -351,30 +351,45 @@
     )
 
 
-def whole_kernel(servers, x_ref, mask_ref, *rest):
-    parts, (out_ref, buffer, weights) = rest[:servers], rest[servers:]
-    fill(buffer, parts)
-    weights[...] = weigh(x_ref[...], buffer[...], mask_ref[...])
-    for start in range(0, x_ref.shape[0], BLOCK):
-        here = pl.ds(start, BLOCK)
-        out_ref[here] = mix(x_ref[here], weights[here], buffer[...])
-
-
-def whole_call(x, mask, parts):
+def whole_kernel(late, servers, x_ref, mask_ref, *rest):
+    parts, (out_ref, buffer, weights, whole, sems) = rest[:servers], rest[-5:]
+
+    @pl.when(((lax.axis_index("rep") + 1) % 4 < 2) == late)
+    def _():
+        fill(buffer, parts)
+        weights[...] = weigh(x_ref[...], buffer[...], mask_ref[...])
+        copies = []
+        for i, start in enumerate(range(0, x_ref.shape[0], BLOCK)):
+            here = pl.ds(start, BLOCK)
+            whole[here] = mix(x_ref[here], weights[here], buffer[...])
+            copies.append(pltpu.make_async_copy(whole.at[here], out_ref.at[here], sems.at[i]))
+            copies[-1].start()
+        for copy in copies:
+            copy.wait()
+
+
+def whole_call(late, x, mask, parts, out=()):
     rows, width = x.shape
     total, servers = mask.shape[1], len(parts)
-    return kernel_call(
-        "mix_whole",
-        functools.partial(whole_kernel, servers),
+    in_vmem = [pl.BlockSpec(memory_space=pltpu.VMEM)] * (2 + servers)
+    return kernel_call(
+        "mix_whole_late" if late else "mix_whole_early",
+        functools.partial(whole_kernel, late, servers),
         bf16(rows, width),
         x,
         mask,
         *reversed(parts),
+        *out,
         flops=4 * total * rows * width,
         scratch=[
             pltpu.VMEM((total, width), jnp.bfloat16),
             pltpu.VMEM((rows, total), jnp.bfloat16),
+            pltpu.VMEM((rows, width), jnp.bfloat16),
+            pltpu.SemaphoreType.DMA((rows // BLOCK,)),
         ],
+        in_specs=in_vmem + [pl.BlockSpec(memory_space=pl.ANY)] * len(out),
+        out_specs=pl.BlockSpec(memory_space=pl.ANY),
+        input_output_aliases={2 + servers: 0} if out else {},
     )
 
 
@@ -449,8 +464,9 @@
     def next_round(x, mask, far, near, far_mask, near_mask, expands, parts, mosts):
         far, most = far_mix_call(far, far_mask, parts, mosts)
         core, own = near_mix_call(near, near_mask, parts)
-        x = whole_call(x, mask, parts)
-        return x, *exchange(expands, far, core, own, most, after=[x])
+        y = whole_call(True, x, mask, parts)
+        most, last = exchange(expands, far, core, own, most, after=[y])
+        return whole_call(False, x, mask, parts, out=[y]), most, last
 
     def in_full(x, y, mask, far, near, rest, masks, expands, most, first, last):
         late = unpack_call(expands[1], inside(rest[1]), first=sent)

time: 52.8 us -> 51.7 us (0.979)
  waiting for transfers between devices: 19.1 us -> 16 us
  starting transfers between devices: 18.1 us -> 19.2 us
  Pallas kernels: 13.8 us -> 14.8 us
    ppermute x3, waiting for transfers between devices: 9.68 us -> 7.57 us  [across(): return lax.ppermute(value, 'rep', beyond)]
    ppermute x3, starting transfers between devices: 3.26 us -> 4.72 us  [across(): return lax.ppermute(value, 'rep', beyond)]
    ppermute x9, waiting for transfers between devices: 6.94 us -> 5.92 us  [turn(): return lax.ppermute(value, 'clus', [(c, c ^ d) for c in range(servers)])]
    pallas_call x13 -> x14, Pallas kernels: 13.8 us -> 14.8 us  [kernel_call(): pl.pallas_call(kernel, out_shape=outs, scratch_shapes=scratch, compiler_p...]
  transfers between devices with their start and end apart: 17 -> 17, of which waited for: 10 -> 11; matrix products, arithmetic and copies ran while one was open for 1% -> 1% of each run, Pallas kernels for 16% -> 18%
where the time goes in v13:
time: 51.7 us; the launch traced here: 51.5 us
  starting transfers between devices  19.2 us (37%)
  waiting for transfers between devices  16 us (31%)
  Pallas kernels  14.8 us (29%)
  between operations  0.95 us (2%)
    pallas_call x14, Pallas kernels, kernel_call(): pl.pallas_call(kernel, out_shape=outs, scratch_shapes=scratch, compiler_p...  14.8 us
    ppermute x9, starting transfers between devices, turn(): return lax.ppermute(value, 'clus', [(c, c ^ d) for c in range(servers)])  11.6 us
    ppermute x3, waiting for transfers between devices, across(): return lax.ppermute(value, 'rep', beyond)  7.57 us
    ppermute x9, waiting for transfers between devices, turn(): return lax.ppermute(value, 'clus', [(c, c ^ d) for c in range(servers)])  5.92 us
    ppermute x3, starting transfers between devices, across(): return lax.ppermute(value, 'rep', beyond)  4.72 us
    ppermute x2, starting transfers between devices, shift(): lax.ppermute(value, 'rep', [(g, (g + by) % groups) for g in range(groups)])  2.64 us
    ppermute x2, waiting for transfers between devices, shift(): lax.ppermute(value, 'rep', [(g, (g + by) % groups) for g in range(groups)])  1.33 us
    ppermute x3, waiting for transfers between devices, inside(): return lax.ppermute(value, 'rep', within)  1.17 us
  transfers between devices with their start and end apart: 17, of which 11 were waited for; matrix products, arithmetic and copies ran while one was open for 1% of the time, Pallas kernels for 18%

profile of v13, /device:TPU:0, one launch (start us, length us, event | category | flops | bytes accessed | tf_op | source)
XLA Modules:
  0.0 51.5 jit_solution(14380529222702147119)
XLA Ops:
  0.0 3.9 %collective-permute-start.10 = (s32[4,32]{1,0:T(4,128)}, s32[4,32]{1,0:T(4,128)S(1)}, u32[]{:S(2)}, u32[]{:S(2)}) collective-permute-start(s32[4,32]{1,0:T(4,128)} %bitcast.12), channel_id=1, source_target_pairs={{0,24},{8,16},{16,8},{24,0},{1,25},{9,17},{17,9},{25,1},{2,26},{10... | collective-permute-start | bytes 1544 | tf_op jit(solution)/shard_map/ppermute | solution.py:444
  3.9 0.5 collective-permute-start.11
  4.4 0.1 collective-permute-start.12
  4.5 1.0 %mask.1 = (bf16[512,128]{1,0:T(8,128)(2,1)S(1)}, s32[4,32]{1,0:T(4,128)S(1)}) custom-call(s32[10,1,512]{2,1,0:T(1,128)} %bitcast.11, s32[4,32]{1,0:T(4,128)} %bitcast.15), custom_call_target="tpu_custom_call" | custom-call | flops 1310720 | bytes 131072 | tf_op jit(solution)/shard_map/mask/pallas_call | solution.py:25
  5.5 0.2 collective-permute-done.10.refs_0_
  5.7 2.0 %collective-permute-done.11.refs_1_ = s32[4,32]{1,0:T(4,128)S(1)} collective-permute-done((s32[4,32]{1,0:T(4,128)}, s32[4,32]{1,0:T(4,128)S(1)}, u32[]{:S(2)}, u32[]{:S(2)}) %collective-permute-start.11) | collective-permute-done | bytes 544 | tf_op jit(solution)/shard_map/ppermute | solution.py:444
  7.7 0.5 collective-permute-done.12.refs_2_
  8.2 0.5 list.1
  8.7 1.4 %collective-permute-start.13 = (s32[8,128]{1,0:T(8,128)S(1)}, s32[8,128]{1,0:T(8,128)S(1)}, u32[]{:S(2)}, u32[]{:S(2)}) collective-permute-start(s32[8,128]{1,0:T(8,128)S(1)} %get-tuple-element.118.refs_0_), channel_id=1, source_target_pairs={{0,7},{1,2},{2,1},{3,4},{4,3},{5,6},{6,5},{7,0},{8,15},{9,10},{10,... | collective-permute-start | bytes 12296 | tf_op jit(solution)/shard_map/ppermute | solution.py:450
  10.1 1.9 %normalize.1.x_ref = bf16[512,2048]{1,0:T(8,128)(2,1)S(1)} custom-call(bf16[512,2048]{1,0:T(8,128)(2,1)} %bitcast.10), custom_call_target="tpu_custom_call" | custom-call | flops 6291456 | bytes 4194304 | tf_op jit(solution)/shard_map/normalize/pallas_call | solution.py:25
  11.9 1.6 %collective-permute-done.13.beyond_ref.refs_1_ = s32[8,128]{1,0:T(8,128)S(1)} collective-permute-done((s32[8,128]{1,0:T(8,128)S(1)}, s32[8,128]{1,0:T(8,128)S(1)}, u32[]{:S(2)}, u32[]{:S(2)}) %collective-permute-start.13) | collective-permute-done | bytes 4128 | tf_op jit(solution)/shard_map/ppermute | solution.py:450
  13.6 0.5 %pack_far.1 = (bf16[128,512]{1,0:T(8,128)(2,1)S(1)}, bf16[48,2048]{1,0:T(8,128)(2,1)S(1)}) custom-call(bf16[512,2048]{1,0:T(8,128)(2,1)S(1)} %normalize.1.x_ref, s32[8,128]{1,0:T(8,128)S(1)} %collective-permute-done.13.beyond_ref.refs_1_), custom_call_target="tpu_custom_call" | custom-call | flops 100663296 | tf_op jit(solution)/shard_map/pack_far/pallas_call | solution.py:25
  14.1 1.4 %collective-permute-start.16 = (bf16[48,2048]{1,0:T(8,128)(2,1)S(1)}, bf16[48,2048]{1,0:T(8,128)(2,1)S(1)}, u32[]{:S(2)}, u32[]{:S(2)}) collective-permute-start(bf16[48,2048]{1,0:T(8,128)(2,1)S(1)} %get-tuple-element.126.x_ref), channel_id=1, source_target_pairs={{0,7},{1,2},{2,1},{3,4},{4,3},{5,6},{6,5},{7,0},{8,15},{9,10},{10,... | collective-permute-start | bytes 589832 | tf_op jit(solution)/shard_map/ppermute | solution.py:450
  15.5 0.0 collective-permute-start.14
  15.5 1.2 %collective-permute-done.14.refs_2_ = s32[8,128]{1,0:T(8,128)S(1)} collective-permute-done((s32[8,128]{1,0:T(8,128)S(1)}, s32[8,128]{1,0:T(8,128)S(1)}, u32[]{:S(2)}, u32[]{:S(2)}) %collective-permute-start.14) | collective-permute-done | bytes 4128 | tf_op jit(solution)/shard_map/ppermute | solution.py:453
  16.7 1.2 %serve_near.1 = (bf16[48,2048]{1,0:T(8,128)(2,1)S(1)}, bf16[128,2048]{1,0:T(8,128)(2,1)S(1)}, bf16[176,2048]{1,0:T(8,128)(2,1)S(1)}, bf16[80,2048]{1,0:T(8,128)(...) custom-call(bf16[512,2048]{1,0:T(8,128)(2,1)S(1)} %normalize.1.x_ref, ...), custom_call_target="tpu_custom_call" | custom-call | flops 805306368 | tf_op jit(solution)/shard_map/serve_near/pallas_call | solution.py:25
  17.9 0.2 collective-permute-start.15
  18.1 4.2 %collective-permute-done.16.far_ref = bf16[48,2048]{1,0:T(8,128)(2,1)S(1)} collective-permute-done((bf16[48,2048]{1,0:T(8,128)(2,1)S(1)}, bf16[48,2048]{1,0:T(8,128)(2,1)S(1)}, u32[]{:S(2)}, u32[]{:S(2)}) %collective-permute-start.16) | collective-permute-done | bytes 196640 | tf_op jit(solution)/shard_map/ppermute | solution.py:450
  22.3 0.3 unpack.8.base_ref
  22.6 0.3 combine.4
  22.9 1.5 %collective-permute-start.17 = (bf16[32,2048]{1,0:T(8,128)(2,1)S(1)}, bf16[32,2048]{1,0:T(8,128)(2,1)S(1)}, u32[]{:S(2)}, u32[]{:S(2)}) collective-permute-start(bf16[32,2048]{1,0:T(8,128)(2,1)S(1)} %get-tuple-element.129), channel_id=1, source_target_pairs={{0,24},{8,16},{16,8},{24,0},{1,25},{9,17},{17,9},{25,1},{2,26},{10... | collective-permute-start | bytes 393224 | tf_op jit(solution)/shard_map/ppermute | solution.py:444
  24.4 0.5 %collective-permute-start.18 = (bf16[32,2048]{1,0:T(8,128)(2,1)S(1)}, bf16[32,2048]{1,0:T(8,128)(2,1)S(1)}, u32[]{:S(2)}, u32[]{:S(2)}) collective-permute-start(bf16[32,2048]{1,0:T(8,128)(2,1)S(1)} %get-tuple-element.130), channel_id=1, source_target_pairs={{0,16},{8,24},{16,0},{24,8},{1,17},{9,25},{17,1},{25,9},{2,18},{10... | collective-permute-start | bytes 393224 | tf_op jit(solution)/shard_map/ppermute | solution.py:444
  25.0 1.5 %collective-permute-start.19 = (bf16[32,2048]{1,0:T(8,128)(2,1)S(1)}, bf16[32,2048]{1,0:T(8,128)(2,1)S(1)}, u32[]{:S(2)}, u32[]{:S(2)}) collective-permute-start(bf16[32,2048]{1,0:T(8,128)(2,1)S(1)} %get-tuple-element.131), channel_id=1, source_target_pairs={{0,8},{8,0},{16,24},{24,16},{1,9},{9,1},{17,25},{25,17},{2,10},{10... | collective-permute-start | bytes 393224 | tf_op jit(solution)/shard_map/ppermute | solution.py:444
  26.4 0.0 collective-permute-start.21
  26.4 2.6 %collective-permute-start.22 = (s32[8,128]{1,0:T(8,128)S(1)}, s32[8,128]{1,0:T(8,128)S(1)}, u32[]{:S(2)}, u32[]{:S(2)}) collective-permute-start(s32[8,128]{1,0:T(8,128)S(1)} %get-tuple-element.135.rest_4_), channel_id=1, source_target_pairs={{0,5},{1,6},{2,7},{3,0},{4,1},{5,2},{6,3},{7,4},{8,13},{9,14},{10,... | collective-permute-start | bytes 12296 | tf_op jit(solution)/shard_map/ppermute | solution.py:447
  29.1 1.3 %collective-permute-done.21.rest_5_ = s32[8,128]{1,0:T(8,128)S(1)} collective-permute-done((s32[8,128]{1,0:T(8,128)S(1)}, s32[8,128]{1,0:T(8,128)S(1)}, u32[]{:S(2)}, u32[]{:S(2)}) %collective-permute-start.21) | collective-permute-done | bytes 4128 | tf_op jit(solution)/shard_map/ppermute | solution.py:447
  30.4 0.0 collective-permute-done.22.rest_6_
  30.4 0.0 collective-permute-done.17.rest_0_
  30.4 0.0 collective-permute-done.18.rest_1_
  30.4 0.7 %mix_far.3 = (bf16[48,2048]{1,0:T(8,128)(2,1)S(1)}, s32[8,128]{1,0:T(8,128)S(1)}) custom-call(bf16[48,2048]{1,0:T(8,128)(2,1)S(1)} %get-tuple-element.126.x_ref, bf16[128,128]{1,0:T(8,128)(2,1)S(1)} %get-tuple-element.134.mask_ref, bf16[32,2048]{1,0:T(8,128)(2,1)S(1)} %collective-permute-done.17.rest_0_, ...), custom_call_target="tpu_custom_call" | custom-call | flops 50331648 | tf_op jit(solution)/shard_map/mix_far/pallas_call | solution.py:25
  31.1 1.9 %collective-permute-start.23 = (bf16[48,2048]{1,0:T(8,128)(2,1)S(1)}, bf16[48,2048]{1,0:T(8,128)(2,1)S(1)}, u32[]{:S(2)}, u32[]{:S(2)}) collective-permute-start(bf16[48,2048]{1,0:T(8,128)(2,1)S(1)} %get-tuple-element.136), channel_id=1, source_target_pairs={{0,7},{1,2},{2,1},{3,4},{4,3},{5,6},{6,5},{7,0},{8,15},{9,10},{10,... | collective-permute-start | bytes 589832 | tf_op jit(solution)/shard_map/ppermute | solution.py:450
  33.0 1.1 %mix_near.3 = (bf16[48,2048]{1,0:T(8,128)(2,1)S(1)}, bf16[128,2048]{1,0:T(8,128)(2,1)S(1)}) custom-call(bf16[176,2048]{1,0:T(8,128)(2,1)S(1)} %get-tuple-element.122.x_ref, bf16[176,128]{1,0:T(8,128)(2,1)S(1)} %get-tuple-element.123.mask_ref, bf16[32,2048]{1,0:T(8,128)(2,1)S(1)} %collective-permute-done.17.rest_0_, ...), custom_call_target="tpu_custom_call" | custom-call | flops 184549376 | tf_op jit(solution)/shard_map/mix_near/pallas_call | solution.py:25
  34.2 0.1 collective-permute-start.20
  34.2 3.4 %mix_whole_late.3.refs_1_.rest_4_ = bf16[512,2048]{1,0:T(8,128)(2,1)S(1)} custom-call(bf16[512,2048]{1,0:T(8,128)(2,1)S(1)} %normalize.1.x_ref, bf16[512,128]{1,0:T(8,128)(2,1)S(1)} %get-tuple-element.117.mask_ref, bf16[32,2048]{1,0:T(8,128)(2,1)S(1)} %collective-permute-done.17.rest_0_, bf16[32,2048]{1,0:T(8,128)(2,1)S(1)} %collective-permute-done.18.rest_1_, ...), custom_call_target="tpu_custom_call" | custom-call | flops 536870912 | tf_op jit(solution)/shard_map/mix_whole_late/pallas_call | solution.py:25
  37.7 1.7 %collective-permute-done.23.far_ref = bf16[48,2048]{1,0:T(8,128)(2,1)S(1)} collective-permute-done((bf16[48,2048]{1,0:T(8,128)(2,1)S(1)}, bf16[48,2048]{1,0:T(8,128)(2,1)S(1)}, u32[]{:S(2)}, u32[]{:S(2)}) %collective-permute-start.23) | collective-permute-done | bytes 196640 | tf_op jit(solution)/shard_map/ppermute | solution.py:450
  39.4 0.3 unpack.9.base_ref
  39.7 0.0 collective-permute-done.20.core_ref
  39.7 0.3 combine.5
  40.0 2.5 %collective-permute-start.24 = (bf16[32,2048]{1,0:T(8,128)(2,1)S(1)}, bf16[32,2048]{1,0:T(8,128)(2,1)S(1)}, u32[]{:S(2)}, u32[]{:S(2)}) collective-permute-start(bf16[32,2048]{1,0:T(8,128)(2,1)S(1)} %get-tuple-element.140), channel_id=1, source_target_pairs={{0,24},{8,16},{16,8},{24,0},{1,25},{9,17},{17,9},{25,1},{2,26},{10... | collective-permute-start | bytes 393224 | tf_op jit(solution)/shard_map/ppermute | solution.py:444
  42.5 0.5 collective-permute-start.25
  43.0 0.6 %collective-permute-start.26 = (bf16[32,2048]{1,0:T(8,128)(2,1)S(1)}, bf16[32,2048]{1,0:T(8,128)(2,1)S(1)}, u32[]{:S(2)}, u32[]{:S(2)}) collective-permute-start(bf16[32,2048]{1,0:T(8,128)(2,1)S(1)} %get-tuple-element.142), channel_id=1, source_target_pairs={{0,8},{8,0},{16,24},{24,16},{1,9},{9,1},{17,25},{25,17},{2,10},{10... | collective-permute-start | bytes 393224 | tf_op jit(solution)/shard_map/ppermute | solution.py:444
  43.5 0.5 slice.16
  44.7 0.1 mix_whole_early.3
  44.7 1.1 %collective-permute-done.24 = bf16[32,2048]{1,0:T(8,128)(2,1)S(1)} collective-permute-done((bf16[32,2048]{1,0:T(8,128)(2,1)S(1)}, bf16[32,2048]{1,0:T(8,128)(2,1)S(1)}, u32[]{:S(2)}, u32[]{:S(2)}) %collective-permute-start.24) | collective-permute-done | bytes 131104 | tf_op jit(solution)/shard_map/ppermute | solution.py:444
  45.9 1.5 %collective-permute-done.25 = bf16[32,2048]{1,0:T(8,128)(2,1)S(1)} collective-permute-done((bf16[32,2048]{1,0:T(8,128)(2,1)S(1)}, bf16[32,2048]{1,0:T(8,128)(2,1)S(1)}, u32[]{:S(2)}, u32[]{:S(2)}) %collective-permute-start.25) | collective-permute-done | bytes 131104 | tf_op jit(solution)/shard_map/ppermute | solution.py:444
  47.4 0.5 collective-permute-done.26
  47.9 3.4 %conditional.1 = (bf16[1,1,512,2048]{3,2,1,0:T(8,128)(2,1)}) conditional(s32[]{:T(128)} %bitcast.6, (bf16[512,2048]{1,0:T(8,128)(2,1)S(1)}, bf16[512,128]{1,0:T(8,128)(2,1)S(1)}, bf16[32,2048]{1,0:T(8,128)(2,1)S(1)}, bf16[32,2048]{1,0:T(8,128)(2,1)S(1)}, bf16[32,2048]{1,0:T(8,128)(2,1)S(1)}, /*index=5*/bf16[32,2048]{1,0:T(8,128)(2,1)S(1)}) %tuple.13, ...), branch_computations={%region_0.0_spmd, %region_1.0_spmd} | conditional | flops 53624569856 | bytes 121962904 | solution.py:511
  47.9 3.4 %mix.2 = bf16[512,2048]{1,0:T(8,128)(2,1)} custom-call(bf16[512,2048]{1,0:T(8,128)(2,1)S(1)} %get-tuple-element.53.x_ref, bf16[512,128]{1,0:T(8,128)(2,1)S(1)} %get-tuple-element.54.mask_ref, bf16[32,2048]{1,0:T(8,128)(2,1)S(1)} %get-tuple-element.55.rest_0_, bf16[32,2048]{1,0:T(8,128)(2,1)S(1)} %get-tuple-element.56.rest_1_, ...), custom_call_target="tpu_custom_call" | custom-call | flops 536870912 | bytes 4194304 | tf_op jit(solution)/shard_map/cond/branch_0_fun/mix/pallas_call | solution.py:25
  (2 shorter events, 0.0 us)
Async XLA Ops:
  0.0 5.7 %collective-permute-start.10 = (s32[4,32]{1,0:T(4,128)}, s32[4,32]{1,0:T(4,128)S(1)}, u32[]{:S(2)}, u32[]{:S(2)}) collective-permute-start(s32[4,32]{1,0:T(4,128)} %bitcast.12), channel_id=1, source_target_pairs={{0,24},{8,16},{16,8},{24,0},{1,25},{9,17},{17,9},{25,1},{2,26},{10... | collective-permute-start | bytes 1544 | tf_op jit(solution)/shard_map/ppermute | solution.py:444
  3.9 3.8 %collective-permute-start.11 = (s32[4,32]{1,0:T(4,128)}, s32[4,32]{1,0:T(4,128)S(1)}, u32[]{:S(2)}, u32[]{:S(2)}) collective-permute-start(s32[4,32]{1,0:T(4,128)} %bitcast.13), channel_id=1, source_target_pairs={{0,16},{8,24},{16,0},{24,8},{1,17},{9,25},{17,1},{25,9},{2,18},{10... | collective-permute-start | bytes 1544 | tf_op jit(solution)/shard_map/ppermute | solution.py:444
  4.4 3.8 %collective-permute-start.12 = (s32[4,32]{1,0:T(4,128)}, s32[4,32]{1,0:T(4,128)S(1)}, u32[]{:S(2)}, u32[]{:S(2)}) collective-permute-start(s32[4,32]{1,0:T(4,128)} %bitcast.14), channel_id=1, source_target_pairs={{0,8},{8,0},{16,24},{24,16},{1,9},{9,1},{17,25},{25,17},{2,10},{10... | collective-permute-start | bytes 1544 | tf_op jit(solution)/shard_map/ppermute | solution.py:444
  8.7 4.9 %collective-permute-start.13 = (s32[8,128]{1,0:T(8,128)S(1)}, s32[8,128]{1,0:T(8,128)S(1)}, u32[]{:S(2)}, u32[]{:S(2)}) collective-permute-start(s32[8,128]{1,0:T(8,128)S(1)} %get-tuple-element.118.refs_0_), channel_id=1, source_target_pairs={{0,7},{1,2},{2,1},{3,4},{4,3},{5,6},{6,5},{7,0},{8,15},{9,10},{10,... | collective-permute-start | bytes 12296 | tf_op jit(solution)/shard_map/ppermute | solution.py:450
  14.1 8.2 %collective-permute-start.16 = (bf16[48,2048]{1,0:T(8,128)(2,1)S(1)}, bf16[48,2048]{1,0:T(8,128)(2,1)S(1)}, u32[]{:S(2)}, u32[]{:S(2)}) collective-permute-start(bf16[48,2048]{1,0:T(8,128)(2,1)S(1)} %get-tuple-element.126.x_ref), channel_id=1, source_target_pairs={{0,7},{1,2},{2,1},{3,4},{4,3},{5,6},{6,5},{7,0},{8,15},{9,10},{10,... | collective-permute-start | bytes 589832 | tf_op jit(solution)/shard_map/ppermute | solution.py:450
  15.5 1.2 %collective-permute-start.14 = (s32[8,128]{1,0:T(8,128)S(1)}, s32[8,128]{1,0:T(8,128)S(1)}, u32[]{:S(2)}, u32[]{:S(2)}) collective-permute-start(s32[8,128]{1,0:T(8,128)S(1)} %get-tuple-element.121), channel_id=1, source_target_pairs={{0,1},{1,0},{2,3},{3,2},{4,5},{5,4},{6,7},{7,6},{8,9},{9,8},{10,11... | collective-permute-start | bytes 12296 | tf_op jit(solution)/shard_map/ppermute | solution.py:453
  17.9 4.7 %collective-permute-start.15 = (bf16[48,2048]{1,0:T(8,128)(2,1)S(1)}, bf16[48,2048]{1,0:T(8,128)(2,1)S(1)}, u32[]{:S(2)}, u32[]{:S(2)}) collective-permute-start(bf16[48,2048]{1,0:T(8,128)(2,1)S(1)} %get-tuple-element.124), channel_id=1, source_target_pairs={{0,1},{1,0},{2,3},{3,2},{4,5},{5,4},{6,7},{7,6},{8,9},{9,8},{10,11... | collective-permute-start | bytes 589832 | tf_op jit(solution)/shard_map/ppermute | solution.py:453
  22.9 7.5 %collective-permute-start.17 = (bf16[32,2048]{1,0:T(8,128)(2,1)S(1)}, bf16[32,2048]{1,0:T(8,128)(2,1)S(1)}, u32[]{:S(2)}, u32[]{:S(2)}) collective-permute-start(bf16[32,2048]{1,0:T(8,128)(2,1)S(1)} %get-tuple-element.129), channel_id=1, source_target_pairs={{0,24},{8,16},{16,8},{24,0},{1,25},{9,17},{17,9},{25,1},{2,26},{10... | collective-permute-start | bytes 393224 | tf_op jit(solution)/shard_map/ppermute | solution.py:444
  24.4 6.0 %collective-permute-start.18 = (bf16[32,2048]{1,0:T(8,128)(2,1)S(1)}, bf16[32,2048]{1,0:T(8,128)(2,1)S(1)}, u32[]{:S(2)}, u32[]{:S(2)}) collective-permute-start(bf16[32,2048]{1,0:T(8,128)(2,1)S(1)} %get-tuple-element.130), channel_id=1, source_target_pairs={{0,16},{8,24},{16,0},{24,8},{1,17},{9,25},{17,1},{25,9},{2,18},{10... | collective-permute-start | bytes 393224 | tf_op jit(solution)/shard_map/ppermute | solution.py:444
  25.0 5.5 %collective-permute-start.19 = (bf16[32,2048]{1,0:T(8,128)(2,1)S(1)}, bf16[32,2048]{1,0:T(8,128)(2,1)S(1)}, u32[]{:S(2)}, u32[]{:S(2)}) collective-permute-start(bf16[32,2048]{1,0:T(8,128)(2,1)S(1)} %get-tuple-element.131), channel_id=1, source_target_pairs={{0,8},{8,0},{16,24},{24,16},{1,9},{9,1},{17,25},{25,17},{2,10},{10... | collective-permute-start | bytes 393224 | tf_op jit(solution)/shard_map/ppermute | solution.py:444
  26.4 3.9 %collective-permute-start.21 = (s32[8,128]{1,0:T(8,128)S(1)}, s32[8,128]{1,0:T(8,128)S(1)}, u32[]{:S(2)}, u32[]{:S(2)}) collective-permute-start(s32[8,128]{1,0:T(8,128)S(1)} %get-tuple-element.135.rest_4_), channel_id=1, source_target_pairs={{0,3},{1,4},{2,5},{3,6},{4,7},{5,0},{6,1},{7,2},{8,11},{9,12},{10,... | collective-permute-start | bytes 12296 | tf_op jit(solution)/shard_map/ppermute | solution.py:447
  26.4 4.0 %collective-permute-start.22 = (s32[8,128]{1,0:T(8,128)S(1)}, s32[8,128]{1,0:T(8,128)S(1)}, u32[]{:S(2)}, u32[]{:S(2)}) collective-permute-start(s32[8,128]{1,0:T(8,128)S(1)} %get-tuple-element.135.rest_4_), channel_id=1, source_target_pairs={{0,5},{1,6},{2,7},{3,0},{4,1},{5,2},{6,3},{7,4},{8,13},{9,14},{10,... | collective-permute-start | bytes 12296 | tf_op jit(solution)/shard_map/ppermute | solution.py:447
  31.1 8.3 %collective-permute-start.23 = (bf16[48,2048]{1,0:T(8,128)(2,1)S(1)}, bf16[48,2048]{1,0:T(8,128)(2,1)S(1)}, u32[]{:S(2)}, u32[]{:S(2)}) collective-permute-start(bf16[48,2048]{1,0:T(8,128)(2,1)S(1)} %get-tuple-element.136), channel_id=1, source_target_pairs={{0,7},{1,2},{2,1},{3,4},{4,3},{5,6},{6,5},{7,0},{8,15},{9,10},{10,... | collective-permute-start | bytes 589832 | tf_op jit(solution)/shard_map/ppermute | solution.py:450
  34.2 5.5 %collective-permute-start.20 = (bf16[48,2048]{1,0:T(8,128)(2,1)S(1)}, bf16[48,2048]{1,0:T(8,128)(2,1)S(1)}, u32[]{:S(2)}, u32[]{:S(2)}) collective-permute-start(bf16[48,2048]{1,0:T(8,128)(2,1)S(1)} %get-tuple-element.133), channel_id=1, source_target_pairs={{0,1},{1,0},{2,3},{3,2},{4,5},{5,4},{6,7},{7,6},{8,9},{9,8},{10,11... | collective-permute-start | bytes 589832 | tf_op jit(solution)/shard_map/ppermute | solution.py:453
  40.0 5.9 %collective-permute-start.24 = (bf16[32,2048]{1,0:T(8,128)(2,1)S(1)}, bf16[32,2048]{1,0:T(8,128)(2,1)S(1)}, u32[]{:S(2)}, u32[]{:S(2)}) collective-permute-start(bf16[32,2048]{1,0:T(8,128)(2,1)S(1)} %get-tuple-element.140), channel_id=1, source_target_pairs={{0,24},{8,16},{16,8},{24,0},{1,25},{9,17},{17,9},{25,1},{2,26},{10... | collective-permute-start | bytes 393224 | tf_op jit(solution)/shard_map/ppermute | solution.py:444
  42.5 5.0 %collective-permute-start.25 = (bf16[32,2048]{1,0:T(8,128)(2,1)S(1)}, bf16[32,2048]{1,0:T(8,128)(2,1)S(1)}, u32[]{:S(2)}, u32[]{:S(2)}) collective-permute-start(bf16[32,2048]{1,0:T(8,128)(2,1)S(1)} %get-tuple-element.141), channel_id=1, source_target_pairs={{0,16},{8,24},{16,0},{24,8},{1,17},{9,25},{17,1},{25,9},{2,18},{10... | collective-permute-start | bytes 393224 | tf_op jit(solution)/shard_map/ppermute | solution.py:444
  43.0 5.0 %collective-permute-start.26 = (bf16[32,2048]{1,0:T(8,128)(2,1)S(1)}, bf16[32,2048]{1,0:T(8,128)(2,1)S(1)}, u32[]{:S(2)}, u32[]{:S(2)}) collective-permute-start(bf16[32,2048]{1,0:T(8,128)(2,1)S(1)} %get-tuple-element.142), channel_id=1, source_target_pairs={{0,8},{8,0},{16,24},{24,16},{1,9},{9,1},{17,25},{25,17},{2,10},{10... | collective-permute-start | bytes 393224 | tf_op jit(solution)/shard_map/ppermute | solution.py:444

commit v14 on v13

--- a/solution.py
+++ b/solution.py
@@ -235,54 +235,74 @@
     )
 
 
-def unpack_kernel(first, bases, expand_ref, far_ref, *refs):
+def unpack_kernel(first, expand_ref, far_ref, own_ref, *refs):
     out_ref, sent = refs[-1], far_ref.shape[0]
     rows = jnp.dot(
         expand_ref[:, first : first + sent], far_ref[...], preferred_element_type=jnp.float32
     )
-    for base_ref in refs[:bases]:
-        rows += base_ref[...].astype(jnp.float32)
-    out_ref[...] = rows.astype(jnp.bfloat16)
-
-
-def unpack_call(expand, far, *base, first=0, after=()):
-    in_vmem = [pl.BlockSpec(memory_space=pltpu.VMEM)] * (2 + len(base))
+    out_ref[...] = (rows + own_ref[...].astype(jnp.float32)).astype(jnp.bfloat16)
+
+
+def unpack_call(expand, far, own, first=0, after=()):
     return kernel_call(
         "unpack",
-        functools.partial(unpack_kernel, first, len(base)),
-        bf16(expand.shape[0], far.shape[1]),
+        functools.partial(unpack_kernel, first),
+        bf16(*own.shape),
         expand,
         far,
-        *base,
+        own,
         *after,
         flops=2**34,
         moved=2**25,
-        in_specs=in_vmem + [pl.BlockSpec(memory_space=pl.ANY)] * len(after),
-    )
-
-
-def combine_kernel(expand_ref, core_ref, base_ref, most_ref, out_most_ref, *out_refs):
-    out_most_ref[...] = most_ref[...]
+        in_specs=[pl.BlockSpec(memory_space=pltpu.VMEM)] * 3
+        + [pl.BlockSpec(memory_space=pl.ANY)] * len(after),
+    )
+
+
+def combine_kernel(first, expand_ref, core_ref, base_ref, *out_refs):
     cap, sent = out_refs[0].shape[0], core_ref.shape[0]
-    rows = jnp.dot(expand_ref[:, :sent], core_ref[...], preferred_element_type=jnp.float32)
+    rows = jnp.dot(
+        expand_ref[:, first : first + sent], core_ref[...], preferred_element_type=jnp.float32
+    )
     rows = (rows + base_ref[...].astype(jnp.float32)).astype(jnp.bfloat16)
     for d, out in enumerate(out_refs):
         out[...] = rows[d * cap : (d + 1) * cap]
 
 
-def combine_call(expand, core, base, most, servers):
+def combine_call(expand, core, base, servers, first=0):
     total, width = base.shape
-    most, *parts = kernel_call(
+    return kernel_call(
         "combine",
-        combine_kernel,
-        [int32(*most.shape)] + [bf16(total // servers, width)] * servers,
+        functools.partial(combine_kernel, first),
+        [bf16(total // servers, width)] * servers,
         expand,
         core,
         base,
-        most,
         flops=2 * total * core.shape[0] * width,
     )
-    return most, parts
+
+
+def gather_kernel(sent, servers, *refs):
+    parts, most_refs, (buffer_ref, over_ref) = refs[:servers], refs[servers:-2], refs[-2:]
+    fill(buffer_ref, parts)
+    most = functools.reduce(jnp.maximum, [ref[...] for ref in most_refs])
+    over_ref[0, 0] = (jnp.max(most) > sent).astype(jnp.int32)
+
+
+def gather_call(parts, mosts, sent):
+    cap, width = parts[0].shape
+    return kernel_call(
+        "gather",
+        functools.partial(gather_kernel, sent, len(parts)),
+        [bf16(cap * len(parts), width), int32(1, 1)],
+        *reversed(parts),
+        *mosts,
+        flops=cap * width,
+        out_specs=[
+            pl.BlockSpec(memory_space=pltpu.VMEM),
+            pl.BlockSpec(memory_space=pltpu.SMEM),
+        ],
+    )
 
 
 def fill(buffer, parts):
@@ -303,25 +323,22 @@
 
 
 def far_mix_kernel(servers, x_ref, mask_ref, *rest):
-    parts, rest = rest[:servers], rest[servers:]
-    *most_refs, out_ref, most_ref, buffer = rest
-    most_ref[...] = functools.reduce(jnp.maximum, [ref[...] for ref in most_refs])
+    parts, (out_ref, buffer) = rest[:servers], rest[servers:]
     fill(buffer, parts)
     weights = weigh(x_ref[...], buffer[...], mask_ref[: x_ref.shape[0]])
     out_ref[...] = mix(x_ref[...], weights, buffer[...])
 
 
-def far_mix_call(x, mask, parts, mosts):
+def far_mix_call(x, mask, parts):
     rows, width = x.shape
     total, servers = mask.shape[1], len(parts)
     return kernel_call(
         "mix_far",
         functools.partial(far_mix_kernel, servers),
-        [bf16(rows, width), int32(*mosts[0].shape)],
+        bf16(rows, width),
         x,
         mask,
         *reversed(parts),
-        *mosts,
         flops=4 * total * rows * width,
         scratch=[pltpu.VMEM((total, width), jnp.bfloat16)],
     )
@@ -393,10 +410,7 @@
     )
 
 
-def last_kernel(servers, x_ref, mask_ref, *rest):
-    parts, rest = rest[:servers], rest[servers:]
-    out_ref, buffer, weights, whole, sems = rest
-    fill(buffer, parts)
+def last_kernel(x_ref, mask_ref, buffer, out_ref, weights, whole, sems):
     weights[...] = weigh(x_ref[...], buffer[...], mask_ref[...])
     copies = []
     for i, start in enumerate(range(0, x_ref.shape[0], BLOCK)):
@@ -408,20 +422,19 @@
         copy.wait()
 
 
-def last_call(x, mask, parts):
+def last_call(x, mask, buffer):
     rows, width = x.shape
-    total, servers = mask.shape[1], len(parts)
+    total = mask.shape[1]
     return kernel_call(
         "mix",
-        functools.partial(last_kernel, servers),
+        last_kernel,
         pltpu.HBM((rows, width), jnp.bfloat16),
         x,
         mask,
-        *reversed(parts),
+        buffer,
         flops=4 * total * rows * width,
         moved=4 * rows * width,
         scratch=[
-            pltpu.VMEM((total, width), jnp.bfloat16),
             pltpu.VMEM((rows, total), jnp.bfloat16),
             pltpu.VMEM((rows, width), jnp.bfloat16),
             pltpu.SemaphoreType.DMA((rows // BLOCK,)),
@@ -456,33 +469,28 @@
         got = {d: turn(parts[d], d) for d in reversed(range(1, servers))}
         return [parts[0]] + [got[d] for d in range(1, servers)]
 
-    def exchange(expands, far, core, own, most, after=()):
-        base = unpack_call(expands[0], across(far), own, after=after)
-        most, parts = combine_call(expands[1], inside(core), base, most, servers)
-        return most, turned(parts)
-
-    def next_round(x, mask, far, near, far_mask, near_mask, expands, parts, mosts):
-        far, most = far_mix_call(far, far_mask, parts, mosts)
+    def exchange(expands, far, core, own, first=0, after=()):
+        base = unpack_call(expands[0], across(far), own, first=first, after=after)
+        return turned(combine_call(expands[1], inside(core), base, servers, first=first))
+
+    def next_round(x, mask, far, near, far_mask, near_mask, expands, parts):
+        far = far_mix_call(far, far_mask, parts)
         core, own = near_mix_call(near, near_mask, parts)
         y = whole_call(True, x, mask, parts)
-        most, last = exchange(expands, far, core, own, most, after=[y])
-        return whole_call(False, x, mask, parts, out=[y]), most, last
-
-    def in_full(x, y, mask, far, near, rest, masks, expands, most, first, last):
-        late = unpack_call(expands[1], inside(rest[1]), first=sent)
-        late = unpack_call(expands[0], across(rest[0]), late, first=sent)
-        late = turned(list(late.reshape(servers, cap, -1)))
+        last = exchange(expands, far, core, own, after=[y])
+        return whole_call(False, x, mask, parts, out=[y]), last
+
+    def in_full(x, y, mask, far, near, rest, masks, expands, most, first, buffer):
+        late = exchange(expands, *rest, jnp.zeros((total, x.shape[1]), x.dtype), first=sent)
         first = [a + b for a, b in zip(first, late)]
         far = jnp.concatenate([far, rest[0]], axis=0)
         near = jnp.concatenate([near[:sent], rest[1], near[sent:]], axis=0)
         near_mask = jnp.concatenate([masks[1], masks[2][sent:]], axis=0)
-        y, _, last = next_round(
-            x, mask, far, near, masks[0], near_mask, expands, first, [most]
-        )
-        return last_call(y, mask, last)
-
-    def as_sent(x, y, mask, far, near, rest, masks, expands, most, first, last):
-        return last_call(y, mask, last)
+        y, last = next_round(x, mask, far, near, masks[0], near_mask, expands, first)
+        return last_call(y, mask, gather_call(last, [most], sent)[0])
+
+    def as_sent(x, y, mask, far, near, rest, masks, expands, most, first, buffer):
+        return last_call(y, mask, buffer)
 
     asked = {d: turn(wanted, d) for d in reversed(range(1, servers))}
     mask, held = mask_call(pick.transpose(0, 3, 1, 2)[0], wanted)
@@ -496,7 +504,8 @@
         x, mask, pack, own_list, far_list, beyond_list, within_list, sent
     )
     rest, masks = others[:2], others[2:]
-    most, first = exchange(expands, far, core, own, most)
+    first = exchange(expands, far, core, own)
+    y, last = next_round(x, mask, far, near, masks[0], masks[2], expands, first)
     mosts = [most]
     reach = 1
     while 2 * reach + 1 < groups:
@@ -504,11 +513,9 @@
         most = functools.reduce(jnp.maximum, mosts)
         mosts = [most, shift(most, by), shift(most, -by)]
         reach += by
-    y, most, last = next_round(
-        x, mask, far, near, masks[0], masks[2], expands, first, mosts
-    )
-    state = x, y, mask, far, near, rest, masks, expands, most, first, last
-    return lax.cond(most[0, 0] > sent, in_full, as_sent, *state)[None, None]
+    buffer, over = gather_call(last, mosts, sent)
+    state = x, y, mask, far, near, rest, masks, expands, most, first, buffer
+    return lax.switch(over[0, 0], [as_sent, in_full], *state)[None, None]
 
 
 def solution(mesh):

time: 51.7 us -> 53.4 us (1.033); the launches traced: 51.5 us -> 52.6 us
  Pallas kernels: 14.8 us -> 15.6 us
    pallas_call x14 -> x15, Pallas kernels: 14.8 us -> 15.6 us  [kernel_call(): pl.pallas_call(kernel, out_shape=outs, scratch_shapes=scratch, compiler_p...]
    ppermute x9, waiting for transfers between devices: 5.92 us -> 6.62 us  [turn(): return lax.ppermute(value, 'clus', [(c, c ^ d) for c in range(servers)])]
  transfers between devices with their start and end apart: 17 -> 17, of which waited for: 11 -> 11; matrix products, arithmetic and copies ran while one was open for 1% -> 0% of each run, Pallas kernels for 18% -> 17%
where the time goes in v14:
time: 53.4 us; the launch traced here: 52.6 us
  starting transfers between devices  19.4 us (36%)
  waiting for transfers between devices  16.5 us (31%)
  Pallas kernels  15.6 us (29%)
  between operations  0.95 us (2%)
    pallas_call x15, Pallas kernels, kernel_call(): pl.pallas_call(kernel, out_shape=outs, scratch_shapes=scratch, compiler_p...  15.6 us
    ppermute x9, starting transfers between devices, turn(): return lax.ppermute(value, 'clus', [(c, c ^ d) for c in range(servers)])  11.6 us
    ppermute x3, waiting for transfers between devices, across(): return lax.ppermute(value, 'rep', beyond)  7.45 us
    ppermute x9, waiting for transfers between devices, turn(): return lax.ppermute(value, 'clus', [(c, c ^ d) for c in range(servers)])  6.62 us
    ppermute x3, starting transfers between devices, across(): return lax.ppermute(value, 'rep', beyond)  4.84 us
    ppermute x2, starting transfers between devices, shift(): lax.ppermute(value, 'rep', [(g, (g + by) % groups) for g in range(groups)])  2.64 us
    ppermute x2, waiting for transfers between devices, shift(): lax.ppermute(value, 'rep', [(g, (g + by) % groups) for g in range(groups)])  1.28 us
    ppermute x3, waiting for transfers between devices, inside(): return lax.ppermute(value, 'rep', within)  1.17 us
  transfers between devices with their start and end apart: 17, of which 11 were waited for; matrix products, arithmetic and copies ran while one was open for 0% of the time, Pallas kernels for 17%

profile of v14, /device:TPU:0, one launch (start us, length us, event | category | flops | bytes accessed | tf_op | source)
XLA Modules:
  0.0 52.6 jit_solution(15356041588155012616)
XLA Ops:
  0.0 3.9 %collective-permute-start.10 = (s32[4,32]{1,0:T(4,128)}, s32[4,32]{1,0:T(4,128)S(1)}, u32[]{:S(2)}, u32[]{:S(2)}) collective-permute-start(s32[4,32]{1,0:T(4,128)} %bitcast.12), channel_id=1, source_target_pairs={{0,24},{8,16},{16,8},{24,0},{1,25},{9,17},{17,9},{25,1},{2,26},{10... | collective-permute-start | bytes 1544 | tf_op jit(solution)/shard_map/ppermute | solution.py:457
  3.9 0.5 collective-permute-start.11
  4.4 0.1 collective-permute-start.12
  4.5 1.0 %mask.1 = (bf16[512,128]{1,0:T(8,128)(2,1)S(1)}, s32[4,32]{1,0:T(4,128)S(1)}) custom-call(s32[10,1,512]{2,1,0:T(1,128)} %bitcast.11, s32[4,32]{1,0:T(4,128)} %bitcast.15), custom_call_target="tpu_custom_call" | custom-call | flops 1310720 | bytes 131072 | tf_op jit(solution)/shard_map/mask/pallas_call | solution.py:25
  5.5 0.2 collective-permute-done.10.refs_0_
  5.7 2.0 %collective-permute-done.11.refs_1_ = s32[4,32]{1,0:T(4,128)S(1)} collective-permute-done((s32[4,32]{1,0:T(4,128)}, s32[4,32]{1,0:T(4,128)S(1)}, u32[]{:S(2)}, u32[]{:S(2)}) %collective-permute-start.11) | collective-permute-done | bytes 544 | tf_op jit(solution)/shard_map/ppermute | solution.py:457
  7.7 0.5 collective-permute-done.12.refs_2_
  8.2 0.5 list.1
  8.7 1.4 %collective-permute-start.13 = (s32[8,128]{1,0:T(8,128)S(1)}, s32[8,128]{1,0:T(8,128)S(1)}, u32[]{:S(2)}, u32[]{:S(2)}) collective-permute-start(s32[8,128]{1,0:T(8,128)S(1)} %get-tuple-element.110.refs_0_), channel_id=1, source_target_pairs={{0,7},{1,2},{2,1},{3,4},{4,3},{5,6},{6,5},{7,0},{8,15},{9,10},{10,... | collective-permute-start | bytes 12296 | tf_op jit(solution)/shard_map/ppermute | solution.py:463
  10.1 1.9 %normalize.1.x_ref = bf16[512,2048]{1,0:T(8,128)(2,1)S(1)} custom-call(bf16[512,2048]{1,0:T(8,128)(2,1)} %bitcast.10), custom_call_target="tpu_custom_call" | custom-call | flops 6291456 | bytes 4194304 | tf_op jit(solution)/shard_map/normalize/pallas_call | solution.py:25
  11.9 1.6 %collective-permute-done.13.beyond_ref.refs_1_ = s32[8,128]{1,0:T(8,128)S(1)} collective-permute-done((s32[8,128]{1,0:T(8,128)S(1)}, s32[8,128]{1,0:T(8,128)S(1)}, u32[]{:S(2)}, u32[]{:S(2)}) %collective-permute-start.13) | collective-permute-done | bytes 4128 | tf_op jit(solution)/shard_map/ppermute | solution.py:463
  13.6 0.5 pack_far.1
  14.1 1.4 %collective-permute-start.16 = (bf16[48,2048]{1,0:T(8,128)(2,1)S(1)}, bf16[48,2048]{1,0:T(8,128)(2,1)S(1)}, u32[]{:S(2)}, u32[]{:S(2)}) collective-permute-start(bf16[48,2048]{1,0:T(8,128)(2,1)S(1)} %get-tuple-element.118.x_ref), channel_id=1, source_target_pairs={{0,7},{1,2},{2,1},{3,4},{4,3},{5,6},{6,5},{7,0},{8,15},{9,10},{10,... | collective-permute-start | bytes 589832 | tf_op jit(solution)/shard_map/ppermute | solution.py:463
  15.5 0.0 collective-permute-start.14
  15.5 1.2 %collective-permute-done.14.refs_2_ = s32[8,128]{1,0:T(8,128)S(1)} collective-permute-done((s32[8,128]{1,0:T(8,128)S(1)}, s32[8,128]{1,0:T(8,128)S(1)}, u32[]{:S(2)}, u32[]{:S(2)}) %collective-permute-start.14) | collective-permute-done | bytes 4128 | tf_op jit(solution)/shard_map/ppermute | solution.py:466
  16.7 1.2 %serve_near.1 = (bf16[48,2048]{1,0:T(8,128)(2,1)S(1)}, bf16[128,2048]{1,0:T(8,128)(2,1)S(1)}, bf16[176,2048]{1,0:T(8,128)(2,1)S(1)}, bf16[80,2048]{1,0:T(8,128)(...) custom-call(bf16[512,2048]{1,0:T(8,128)(2,1)S(1)} %normalize.1.x_ref, ...), custom_call_target="tpu_custom_call" | custom-call | flops 805306368 | tf_op jit(solution)/shard_map/serve_near/pallas_call | solution.py:25
  17.9 0.2 collective-permute-start.15
  18.1 4.2 %collective-permute-done.16.far_ref = bf16[48,2048]{1,0:T(8,128)(2,1)S(1)} collective-permute-done((bf16[48,2048]{1,0:T(8,128)(2,1)S(1)}, bf16[48,2048]{1,0:T(8,128)(2,1)S(1)}, u32[]{:S(2)}, u32[]{:S(2)}) %collective-permute-start.16) | collective-permute-done | bytes 196640 | tf_op jit(solution)/shard_map/ppermute | solution.py:463
  22.3 0.3 unpack.6.base_ref
  22.6 0.0 collective-permute-done.15.core_ref
  22.6 0.3 combine.6
  22.9 1.6 %collective-permute-start.17 = (bf16[32,2048]{1,0:T(8,128)(2,1)S(1)}, bf16[32,2048]{1,0:T(8,128)(2,1)S(1)}, u32[]{:S(2)}, u32[]{:S(2)}) collective-permute-start(bf16[32,2048]{1,0:T(8,128)(2,1)S(1)} %get-tuple-element.120), channel_id=1, source_target_pairs={{0,24},{8,16},{16,8},{24,0},{1,25},{9,17},{17,9},{25,1},{2,26},{10... | collective-permute-start | bytes 393224 | tf_op jit(solution)/shard_map/ppermute | solution.py:457
  24.4 0.5 collective-permute-start.18
  24.9 1.5 %collective-permute-start.19 = (bf16[32,2048]{1,0:T(8,128)(2,1)S(1)}, bf16[32,2048]{1,0:T(8,128)(2,1)S(1)}, u32[]{:S(2)}, u32[]{:S(2)}) collective-permute-start(bf16[32,2048]{1,0:T(8,128)(2,1)S(1)} %get-tuple-element.122), channel_id=1, source_target_pairs={{0,8},{8,0},{16,24},{24,16},{1,9},{9,1},{17,25},{25,17},{2,10},{10... | collective-permute-start | bytes 393224 | tf_op jit(solution)/shard_map/ppermute | solution.py:457
  26.4 2.5 %collective-permute-done.17.rest_0_ = bf16[32,2048]{1,0:T(8,128)(2,1)S(1)} collective-permute-done((bf16[32,2048]{1,0:T(8,128)(2,1)S(1)}, bf16[32,2048]{1,0:T(8,128)(2,1)S(1)}, u32[]{:S(2)}, u32[]{:S(2)}) %collective-permute-start.17) | collective-permute-done | bytes 131104 | tf_op jit(solution)/shard_map/ppermute | solution.py:457
  28.9 1.3 %collective-permute-done.18.rest_1_ = bf16[32,2048]{1,0:T(8,128)(2,1)S(1)} collective-permute-done((bf16[32,2048]{1,0:T(8,128)(2,1)S(1)}, bf16[32,2048]{1,0:T(8,128)(2,1)S(1)}, u32[]{:S(2)}, u32[]{:S(2)}) %collective-permute-start.18) | collective-permute-done | bytes 131104 | tf_op jit(solution)/shard_map/ppermute | solution.py:457
  30.2 0.1 collective-permute-done.19.rest_2_
  30.3 0.7 %mix_far.3 = bf16[48,2048]{1,0:T(8,128)(2,1)S(1)} custom-call(bf16[48,2048]{1,0:T(8,128)(2,1)S(1)} %get-tuple-element.118.x_ref, bf16[128,128]{1,0:T(8,128)(2,1)S(1)} %get-tuple-element.125.mask_ref, bf16[32,2048]{1,0:T(8,128)(2,1)S(1)} %collective-permute-done.17.rest_0_, bf16[32,2048]{1,0:T(8,128)(2,1)S(1)} %collective-permute-done.18.rest_1_, ...), custom_call_target="tpu_custom_call" | custom-call | flops 50331648 | tf_op jit(solution)/shard_map/mix_far/pallas_call | solution.py:25
  31.0 2.0 %collective-permute-start.21 = (bf16[48,2048]{1,0:T(8,128)(2,1)S(1)}, bf16[48,2048]{1,0:T(8,128)(2,1)S(1)}, u32[]{:S(2)}, u32[]{:S(2)}) collective-permute-start(bf16[48,2048]{1,0:T(8,128)(2,1)S(1)} %mix_far.3), channel_id=1, source_target_pairs={{0,7},{1,2},{2,1},{3,4},{4,3},{5,6},{6,5},{7,0},{8,15},{9,10},{10,... | collective-permute-start | bytes 589832 | tf_op jit(solution)/shard_map/ppermute | solution.py:463
  33.0 1.1 %mix_near.3 = (bf16[48,2048]{1,0:T(8,128)(2,1)S(1)}, bf16[128,2048]{1,0:T(8,128)(2,1)S(1)}) custom-call(bf16[176,2048]{1,0:T(8,128)(2,1)S(1)} %get-tuple-element.114.x_ref, bf16[176,128]{1,0:T(8,128)(2,1)S(1)} %get-tuple-element.115.mask_ref, bf16[32,2048]{1,0:T(8,128)(2,1)S(1)} %collective-permute-done.17.rest_0_, ...), custom_call_target="tpu_custom_call" | custom-call | flops 184549376 | tf_op jit(solution)/shard_map/mix_near/pallas_call | solution.py:25
  34.2 0.1 collective-permute-start.20
  34.2 3.4 %mix_whole_late.3.refs_0_.rest_4_ = bf16[512,2048]{1,0:T(8,128)(2,1)S(1)} custom-call(bf16[512,2048]{1,0:T(8,128)(2,1)S(1)} %normalize.1.x_ref, bf16[512,128]{1,0:T(8,128)(2,1)S(1)} %get-tuple-element.109.mask_ref, bf16[32,2048]{1,0:T(8,128)(2,1)S(1)} %collective-permute-done.17.rest_0_, bf16[32,2048]{1,0:T(8,128)(2,1)S(1)} %collective-permute-done.18.rest_1_, ...), custom_call_target="tpu_custom_call" | custom-call | flops 536870912 | tf_op jit(solution)/shard_map/mix_whole_late/pallas_call | solution.py:25
  37.7 1.6 %collective-permute-done.21.far_ref = bf16[48,2048]{1,0:T(8,128)(2,1)S(1)} collective-permute-done((bf16[48,2048]{1,0:T(8,128)(2,1)S(1)}, bf16[48,2048]{1,0:T(8,128)(2,1)S(1)}, u32[]{:S(2)}, u32[]{:S(2)}) %collective-permute-start.21) | collective-permute-done | bytes 196640 | tf_op jit(solution)/shard_map/ppermute | solution.py:463
  39.3 0.3 unpack.7.base_ref
  39.5 0.0 collective-permute-done.20.core_ref
  39.6 0.3 combine.7
  39.8 1.5 %collective-permute-start.22 = (bf16[32,2048]{1,0:T(8,128)(2,1)S(1)}, bf16[32,2048]{1,0:T(8,128)(2,1)S(1)}, u32[]{:S(2)}, u32[]{:S(2)}) collective-permute-start(bf16[32,2048]{1,0:T(8,128)(2,1)S(1)} %get-tuple-element.127), channel_id=1, source_target_pairs={{0,24},{8,16},{16,8},{24,0},{1,25},{9,17},{17,9},{25,1},{2,26},{10... | collective-permute-start | bytes 393224 | tf_op jit(solution)/shard_map/ppermute | solution.py:457
  41.3 0.6 %collective-permute-start.23 = (bf16[32,2048]{1,0:T(8,128)(2,1)S(1)}, bf16[32,2048]{1,0:T(8,128)(2,1)S(1)}, u32[]{:S(2)}, u32[]{:S(2)}) collective-permute-start(bf16[32,2048]{1,0:T(8,128)(2,1)S(1)} %get-tuple-element.128), channel_id=1, source_target_pairs={{0,16},{8,24},{16,0},{24,8},{1,17},{9,25},{17,1},{25,9},{2,18},{10... | collective-permute-start | bytes 393224 | tf_op jit(solution)/shard_map/ppermute | solution.py:457
  41.9 1.5 %collective-permute-start.24 = (bf16[32,2048]{1,0:T(8,128)(2,1)S(1)}, bf16[32,2048]{1,0:T(8,128)(2,1)S(1)}, u32[]{:S(2)}, u32[]{:S(2)}) collective-permute-start(bf16[32,2048]{1,0:T(8,128)(2,1)S(1)} %get-tuple-element.129), channel_id=1, source_target_pairs={{0,8},{8,0},{16,24},{24,16},{1,9},{9,1},{17,25},{25,17},{2,10},{10... | collective-permute-start | bytes 393224 | tf_op jit(solution)/shard_map/ppermute | solution.py:457
  43.4 0.0 collective-permute-start.25
  43.4 2.6 %collective-permute-start.26 = (s32[8,128]{1,0:T(8,128)S(1)}, s32[8,128]{1,0:T(8,128)S(1)}, u32[]{:S(2)}, u32[]{:S(2)}) collective-permute-start(s32[8,128]{1,0:T(8,128)S(1)} %get-tuple-element.131.refs_4_), channel_id=1, source_target_pairs={{0,5},{1,6},{2,7},{3,0},{4,1},{5,2},{6,3},{7,4},{8,13},{9,14},{10,... | collective-permute-start | bytes 12296 | tf_op jit(solution)/shard_map/ppermute | solution.py:460
  46.1 1.2 %collective-permute-done.25.refs_5_ = s32[8,128]{1,0:T(8,128)S(1)} collective-permute-done((s32[8,128]{1,0:T(8,128)S(1)}, s32[8,128]{1,0:T(8,128)S(1)}, u32[]{:S(2)}, u32[]{:S(2)}) %collective-permute-start.25) | collective-permute-done | bytes 4128 | tf_op jit(solution)/shard_map/ppermute | solution.py:460
  47.3 0.0 collective-permute-done.26.refs_6_
  47.4 0.0 collective-permute-done.22.refs_0_
  47.4 0.0 collective-permute-done.23.refs_1_
  47.4 0.7 %gather.3 = (bf16[128,2048]{1,0:T(8,128)(2,1)S(1)}, s32[1,1]{1,0:T(1,128)}) custom-call(bf16[32,2048]{1,0:T(8,128)(2,1)S(1)} %collective-permute-done.22.refs_0_, bf16[32,2048]{1,0:T(8,128)(2,1)S(1)} %collective-permute-done.23.refs_1_, bf16[32,2048]{1,0:T(8,128)(2,1)S(1)} %collective-permute-done.24.refs_2_, ...), custom_call_target="tpu_custom_call" | custom-call | flops 65536 | tf_op jit(solution)/shard_map/gather/pallas_call | solution.py:25
  48.8 3.7 %conditional.1 = (bf16[1,1,512,2048]{3,2,1,0:T(8,128)(2,1)}) conditional(s32[]{:T(128)} %bitcast.6, (bf16[512,2048]{1,0:T(8,128)(2,1)S(1)}, bf16[512,128]{1,0:T(8,128)(2,1)S(1)}, bf16[128,2048]{1,0:T(8,128)(2,1)S(1)}) %tuple.13, (bf16[80,2048]{1,0:T(8,128)(2,1)S(1)}, bf16[80,2048]{1,0:T(8,128)(2,1)S(1)}, bf16[128,128]{1,0:T(8,128)(2,1)S(1)}, ...), branch_computations={%region_0.0_spmd, %region_1.0_spmd} | conditional | flops 36486709248 | bytes 88146328 | solution.py:518
  49.0 3.5 %mix.2 = bf16[512,2048]{1,0:T(8,128)(2,1)} custom-call(bf16[512,2048]{1,0:T(8,128)(2,1)S(1)} %get-tuple-element.47.x_ref, bf16[512,128]{1,0:T(8,128)(2,1)S(1)} %get-tuple-element.48.mask_ref, bf16[128,2048]{1,0:T(8,128)(2,1)S(1)} %get-tuple-element.49.buffer), custom_call_target="tpu_custom_call" | custom-call | flops 536870912 | bytes 4194304 | tf_op jit(solution)/shard_map/cond/branch_0_fun/mix/pallas_call | solution.py:25
  (2 shorter events, 0.0 us)
Async XLA Ops:
  0.0 5.7 %collective-permute-start.10 = (s32[4,32]{1,0:T(4,128)}, s32[4,32]{1,0:T(4,128)S(1)}, u32[]{:S(2)}, u32[]{:S(2)}) collective-permute-start(s32[4,32]{1,0:T(4,128)} %bitcast.12), channel_id=1, source_target_pairs={{0,24},{8,16},{16,8},{24,0},{1,25},{9,17},{17,9},{25,1},{2,26},{10... | collective-permute-start | bytes 1544 | tf_op jit(solution)/shard_map/ppermute | solution.py:457
  3.9 3.8 %collective-permute-start.11 = (s32[4,32]{1,0:T(4,128)}, s32[4,32]{1,0:T(4,128)S(1)}, u32[]{:S(2)}, u32[]{:S(2)}) collective-permute-start(s32[4,32]{1,0:T(4,128)} %bitcast.13), channel_id=1, source_target_pairs={{0,16},{8,24},{16,0},{24,8},{1,17},{9,25},{17,1},{25,9},{2,18},{10... | collective-permute-start | bytes 1544 | tf_op jit(solution)/shard_map/ppermute | solution.py:457
  4.4 3.8 %collective-permute-start.12 = (s32[4,32]{1,0:T(4,128)}, s32[4,32]{1,0:T(4,128)S(1)}, u32[]{:S(2)}, u32[]{:S(2)}) collective-permute-start(s32[4,32]{1,0:T(4,128)} %bitcast.14), channel_id=1, source_target_pairs={{0,8},{8,0},{16,24},{24,16},{1,9},{9,1},{17,25},{25,17},{2,10},{10... | collective-permute-start | bytes 1544 | tf_op jit(solution)/shard_map/ppermute | solution.py:457
  8.7 4.9 %collective-permute-start.13 = (s32[8,128]{1,0:T(8,128)S(1)}, s32[8,128]{1,0:T(8,128)S(1)}, u32[]{:S(2)}, u32[]{:S(2)}) collective-permute-start(s32[8,128]{1,0:T(8,128)S(1)} %get-tuple-element.110.refs_0_), channel_id=1, source_target_pairs={{0,7},{1,2},{2,1},{3,4},{4,3},{5,6},{6,5},{7,0},{8,15},{9,10},{10,... | collective-permute-start | bytes 12296 | tf_op jit(solution)/shard_map/ppermute | solution.py:463
  14.1 8.2 %collective-permute-start.16 = (bf16[48,2048]{1,0:T(8,128)(2,1)S(1)}, bf16[48,2048]{1,0:T(8,128)(2,1)S(1)}, u32[]{:S(2)}, u32[]{:S(2)}) collective-permute-start(bf16[48,2048]{1,0:T(8,128)(2,1)S(1)} %get-tuple-element.118.x_ref), channel_id=1, source_target_pairs={{0,7},{1,2},{2,1},{3,4},{4,3},{5,6},{6,5},{7,0},{8,15},{9,10},{10,... | collective-permute-start | bytes 589832 | tf_op jit(solution)/shard_map/ppermute | solution.py:463
  15.5 1.2 %collective-permute-start.14 = (s32[8,128]{1,0:T(8,128)S(1)}, s32[8,128]{1,0:T(8,128)S(1)}, u32[]{:S(2)}, u32[]{:S(2)}) collective-permute-start(s32[8,128]{1,0:T(8,128)S(1)} %get-tuple-element.113), channel_id=1, source_target_pairs={{0,1},{1,0},{2,3},{3,2},{4,5},{5,4},{6,7},{7,6},{8,9},{9,8},{10,11... | collective-permute-start | bytes 12296 | tf_op jit(solution)/shard_map/ppermute | solution.py:466
  17.9 4.7 %collective-permute-start.15 = (bf16[48,2048]{1,0:T(8,128)(2,1)S(1)}, bf16[48,2048]{1,0:T(8,128)(2,1)S(1)}, u32[]{:S(2)}, u32[]{:S(2)}) collective-permute-start(bf16[48,2048]{1,0:T(8,128)(2,1)S(1)} %get-tuple-element.116), channel_id=1, source_target_pairs={{0,1},{1,0},{2,3},{3,2},{4,5},{5,4},{6,7},{7,6},{8,9},{9,8},{10,11... | collective-permute-start | bytes 589832 | tf_op jit(solution)/shard_map/ppermute | solution.py:466
  22.9 6.0 %collective-permute-start.17 = (bf16[32,2048]{1,0:T(8,128)(2,1)S(1)}, bf16[32,2048]{1,0:T(8,128)(2,1)S(1)}, u32[]{:S(2)}, u32[]{:S(2)}) collective-permute-start(bf16[32,2048]{1,0:T(8,128)(2,1)S(1)} %get-tuple-element.120), channel_id=1, source_target_pairs={{0,24},{8,16},{16,8},{24,0},{1,25},{9,17},{17,9},{25,1},{2,26},{10... | collective-permute-start | bytes 393224 | tf_op jit(solution)/shard_map/ppermute | solution.py:457
  24.4 5.8 %collective-permute-start.18 = (bf16[32,2048]{1,0:T(8,128)(2,1)S(1)}, bf16[32,2048]{1,0:T(8,128)(2,1)S(1)}, u32[]{:S(2)}, u32[]{:S(2)}) collective-permute-start(bf16[32,2048]{1,0:T(8,128)(2,1)S(1)} %get-tuple-element.121), channel_id=1, source_target_pairs={{0,16},{8,24},{16,0},{24,8},{1,17},{9,25},{17,1},{25,9},{2,18},{10... | collective-permute-start | bytes 393224 | tf_op jit(solution)/shard_map/ppermute | solution.py:457
  24.9 5.4 %collective-permute-start.19 = (bf16[32,2048]{1,0:T(8,128)(2,1)S(1)}, bf16[32,2048]{1,0:T(8,128)(2,1)S(1)}, u32[]{:S(2)}, u32[]{:S(2)}) collective-permute-start(bf16[32,2048]{1,0:T(8,128)(2,1)S(1)} %get-tuple-element.122), channel_id=1, source_target_pairs={{0,8},{8,0},{16,24},{24,16},{1,9},{9,1},{17,25},{25,17},{2,10},{10... | collective-permute-start | bytes 393224 | tf_op jit(solution)/shard_map/ppermute | solution.py:457
  31.0 8.3 %collective-permute-start.21 = (bf16[48,2048]{1,0:T(8,128)(2,1)S(1)}, bf16[48,2048]{1,0:T(8,128)(2,1)S(1)}, u32[]{:S(2)}, u32[]{:S(2)}) collective-permute-start(bf16[48,2048]{1,0:T(8,128)(2,1)S(1)} %mix_far.3), channel_id=1, source_target_pairs={{0,7},{1,2},{2,1},{3,4},{4,3},{5,6},{6,5},{7,0},{8,15},{9,10},{10,... | collective-permute-start | bytes 589832 | tf_op jit(solution)/shard_map/ppermute | solution.py:463
  34.2 5.4 %collective-permute-start.20 = (bf16[48,2048]{1,0:T(8,128)(2,1)S(1)}, bf16[48,2048]{1,0:T(8,128)(2,1)S(1)}, u32[]{:S(2)}, u32[]{:S(2)}) collective-permute-start(bf16[48,2048]{1,0:T(8,128)(2,1)S(1)} %get-tuple-element.124), channel_id=1, source_target_pairs={{0,1},{1,0},{2,3},{3,2},{4,5},{5,4},{6,7},{7,6},{8,9},{9,8},{10,11... | collective-permute-start | bytes 589832 | tf_op jit(solution)/shard_map/ppermute | solution.py:466
  39.8 7.5 %collective-permute-start.22 = (bf16[32,2048]{1,0:T(8,128)(2,1)S(1)}, bf16[32,2048]{1,0:T(8,128)(2,1)S(1)}, u32[]{:S(2)}, u32[]{:S(2)}) collective-permute-start(bf16[32,2048]{1,0:T(8,128)(2,1)S(1)} %get-tuple-element.127), channel_id=1, source_target_pairs={{0,24},{8,16},{16,8},{24,0},{1,25},{9,17},{17,9},{25,1},{2,26},{10... | collective-permute-start | bytes 393224 | tf_op jit(solution)/shard_map/ppermute | solution.py:457
  41.3 6.1 %collective-permute-start.23 = (bf16[32,2048]{1,0:T(8,128)(2,1)S(1)}, bf16[32,2048]{1,0:T(8,128)(2,1)S(1)}, u32[]{:S(2)}, u32[]{:S(2)}) collective-permute-start(bf16[32,2048]{1,0:T(8,128)(2,1)S(1)} %get-tuple-element.128), channel_id=1, source_target_pairs={{0,16},{8,24},{16,0},{24,8},{1,17},{9,25},{17,1},{25,9},{2,18},{10... | collective-permute-start | bytes 393224 | tf_op jit(solution)/shard_map/ppermute | solution.py:457
  41.9 5.5 %collective-permute-start.24 = (bf16[32,2048]{1,0:T(8,128)(2,1)S(1)}, bf16[32,2048]{1,0:T(8,128)(2,1)S(1)}, u32[]{:S(2)}, u32[]{:S(2)}) collective-permute-start(bf16[32,2048]{1,0:T(8,128)(2,1)S(1)} %get-tuple-element.129), channel_id=1, source_target_pairs={{0,8},{8,0},{16,24},{24,16},{1,9},{9,1},{17,25},{25,17},{2,10},{10... | collective-permute-start | bytes 393224 | tf_op jit(solution)/shard_map/ppermute | solution.py:457
  43.4 3.9 %collective-permute-start.25 = (s32[8,128]{1,0:T(8,128)S(1)}, s32[8,128]{1,0:T(8,128)S(1)}, u32[]{:S(2)}, u32[]{:S(2)}) collective-permute-start(s32[8,128]{1,0:T(8,128)S(1)} %get-tuple-element.131.refs_4_), channel_id=1, source_target_pairs={{0,3},{1,4},{2,5},{3,6},{4,7},{5,0},{6,1},{7,2},{8,11},{9,12},{10,... | collective-permute-start | bytes 12296 | tf_op jit(solution)/shard_map/ppermute | solution.py:460
  43.4 4.0 %collective-permute-start.26 = (s32[8,128]{1,0:T(8,128)S(1)}, s32[8,128]{1,0:T(8,128)S(1)}, u32[]{:S(2)}, u32[]{:S(2)}) collective-permute-start(s32[8,128]{1,0:T(8,128)S(1)} %get-tuple-element.131.refs_4_), channel_id=1, source_target_pairs={{0,5},{1,6},{2,7},{3,0},{4,1},{5,2},{6,3},{7,4},{8,13},{9,14},{10,... | collective-permute-start | bytes 12296 | tf_op jit(solution)/shard_map/ppermute | solution.py:460

commit v15 on v13

--- a/solution.py
+++ b/solution.py
@@ -351,35 +351,80 @@
     )
 
 
-def whole_kernel(late, servers, x_ref, mask_ref, *rest):
-    parts, (out_ref, buffer, weights, whole, sems) = rest[:servers], rest[-5:]
-
-    @pl.when(((lax.axis_index("rep") + 1) % 4 < 2) == late)
+def is_late():
+    return (lax.axis_index("rep") + 1) % 4 < 2
+
+
+def late_kernel(servers, x_ref, mask_ref, *rest):
+    parts, (out_ref, buffer, weights) = rest[:servers], rest[servers:]
+
+    @pl.when(is_late())
     def _():
         fill(buffer, parts)
         weights[...] = weigh(x_ref[...], buffer[...], mask_ref[...])
-        copies = []
-        for i, start in enumerate(range(0, x_ref.shape[0], BLOCK)):
+        for start in range(0, x_ref.shape[0], BLOCK):
             here = pl.ds(start, BLOCK)
-            whole[here] = mix(x_ref[here], weights[here], buffer[...])
-            copies.append(pltpu.make_async_copy(whole.at[here], out_ref.at[here], sems.at[i]))
-            copies[-1].start()
-        for copy in copies:
-            copy.wait()
-
-
-def whole_call(late, x, mask, parts, out=()):
+            out_ref[here] = mix(x_ref[here], weights[here], buffer[...])
+
+
+def late_call(x, mask, parts):
     rows, width = x.shape
     total, servers = mask.shape[1], len(parts)
-    in_vmem = [pl.BlockSpec(memory_space=pltpu.VMEM)] * (2 + servers)
-    return kernel_call(
-        "mix_whole_late" if late else "mix_whole_early",
-        functools.partial(whole_kernel, late, servers),
+    return kernel_call(
+        "mix_whole_late",
+        functools.partial(late_kernel, servers),
         bf16(rows, width),
         x,
         mask,
         *reversed(parts),
-        *out,
+        flops=4 * total * rows * width,
+        scratch=[
+            pltpu.VMEM((total, width), jnp.bfloat16),
+            pltpu.VMEM((rows, total), jnp.bfloat16),
+        ],
+    )
+
+
+def mix_blocks(x_ref, mask_ref, buffer, weights, whole, out_ref, sems):
+    weights[...] = weigh(x_ref[...], buffer[...], mask_ref[...])
+    blocks = [pl.ds(start, BLOCK) for start in range(0, x_ref.shape[0], BLOCK)]
+    copies, added = [], None
+    for i in range(len(blocks) + 1):
+        before = added
+        if i < len(blocks):
+            added = jnp.dot(
+                weights[blocks[i]], buffer[...], preferred_element_type=jnp.float32
+            )
+        if i:
+            here = blocks[i - 1]
+            mixed = x_ref[here].astype(jnp.float32) + before
+            whole[here] = normalize(mixed).astype(jnp.bfloat16)
+            copies.append(pltpu.make_async_copy(whole.at[here], out_ref.at[here], sems.at[i - 1]))
+            copies[-1].start()
+    for copy in copies:
+        copy.wait()
+
+
+def early_kernel(servers, x_ref, mask_ref, *rest):
+    parts, (_, out_ref, buffer, weights, whole, sems) = rest[:servers], rest[servers:]
+
+    @pl.when(jnp.logical_not(is_late()))
+    def _():
+        fill(buffer, parts)
+        mix_blocks(x_ref, mask_ref, buffer, weights, whole, out_ref, sems)
+
+
+def early_call(x, mask, parts, out):
+    rows, width = x.shape
+    total, servers = mask.shape[1], len(parts)
+    return kernel_call(
+        "mix_whole_early",
+        functools.partial(early_kernel, servers),
+        bf16(rows, width),
+        x,
+        mask,
+        *reversed(parts),
+        out,
         flops=4 * total * rows * width,
         scratch=[
             pltpu.VMEM((total, width), jnp.bfloat16),
@@ -387,25 +432,17 @@
             pltpu.VMEM((rows, width), jnp.bfloat16),
             pltpu.SemaphoreType.DMA((rows // BLOCK,)),
         ],
-        in_specs=in_vmem + [pl.BlockSpec(memory_space=pl.ANY)] * len(out),
+        in_specs=[pl.BlockSpec(memory_space=pltpu.VMEM)] * (2 + servers)
+        + [pl.BlockSpec(memory_space=pl.ANY)],
         out_specs=pl.BlockSpec(memory_space=pl.ANY),
-        input_output_aliases={2 + servers: 0} if out else {},
+        input_output_aliases={2 + servers: 0},
     )
 
 
 def last_kernel(servers, x_ref, mask_ref, *rest):
-    parts, rest = rest[:servers], rest[servers:]
-    out_ref, buffer, weights, whole, sems = rest
+    parts, (out_ref, buffer, weights, whole, sems) = rest[:servers], rest[servers:]
     fill(buffer, parts)
-    weights[...] = weigh(x_ref[...], buffer[...], mask_ref[...])
-    copies = []
-    for i, start in enumerate(range(0, x_ref.shape[0], BLOCK)):
-        here = pl.ds(start, BLOCK)
-        whole[here] = mix(x_ref[here], weights[here], buffer[...])
-        copies.append(pltpu.make_async_copy(whole.at[here], out_ref.at[here], sems.at[i]))
-        copies[-1].start()
-    for copy in copies:
-        copy.wait()
+    mix_blocks(x_ref, mask_ref, buffer, weights, whole, out_ref, sems)
 
 
 def last_call(x, mask, parts):
@@ -464,9 +501,9 @@
     def next_round(x, mask, far, near, far_mask, near_mask, expands, parts, mosts):
         far, most = far_mix_call(far, far_mask, parts, mosts)
         core, own = near_mix_call(near, near_mask, parts)
-        y = whole_call(True, x, mask, parts)
+        y = late_call(x, mask, parts)
         most, last = exchange(expands, far, core, own, most, after=[y])
-        return whole_call(False, x, mask, parts, out=[y]), most, last
+        return early_call(x, mask, parts, y), most, last
 
     def in_full(x, y, mask, far, near, rest, masks, expands, most, first, last):
         late = unpack_call(expands[1], inside(rest[1]), first=sent)

time: 51.7 us -> 51.9 us (level)
  Pallas kernels: 14.8 us -> 13.9 us
  waiting for transfers between devices: 16 us -> 16.9 us
    pallas_call x14, Pallas kernels: 14.8 us -> 13.9 us  [kernel_call(): pl.pallas_call(kernel, out_shape=outs, scratch_shapes=scratch, compiler_p...]
    ppermute x3, waiting for transfers between devices: 7.57 us -> 8.47 us  [across(): return lax.ppermute(value, 'rep', beyond)]
  transfers between devices with their start and end apart: 17 -> 17, of which waited for: 11 -> 11; matrix products, arithmetic and copies ran while one was open for 1% -> 1% of each run, Pallas kernels for 18% -> 16%
where the time goes in v15:
time: 51.9 us; the launch traced here: 51.7 us
  starting transfers between devices  19.2 us (37%)
  waiting for transfers between devices  16.9 us (33%)
  Pallas kernels  13.9 us (27%)
  between operations  0.97 us (2%)
    pallas_call x14, Pallas kernels, kernel_call(): pl.pallas_call(kernel, out_shape=outs, scratch_shapes=scratch, compiler_p...  13.9 us
    ppermute x9, starting transfers between devices, turn(): return lax.ppermute(value, 'clus', [(c, c ^ d) for c in range(servers)])  11.6 us
    ppermute x3, waiting for transfers between devices, across(): return lax.ppermute(value, 'rep', beyond)  8.47 us
    ppermute x9, waiting for transfers between devices, turn(): return lax.ppermute(value, 'clus', [(c, c ^ d) for c in range(servers)])  5.92 us
    ppermute x3, starting transfers between devices, across(): return lax.ppermute(value, 'rep', beyond)  4.72 us
    ppermute x2, starting transfers between devices, shift(): lax.ppermute(value, 'rep', [(g, (g + by) % groups) for g in range(groups)])  2.64 us
    ppermute x2, waiting for transfers between devices, shift(): lax.ppermute(value, 'rep', [(g, (g + by) % groups) for g in range(groups)])  1.33 us
    ppermute x3, waiting for transfers between devices, inside(): return lax.ppermute(value, 'rep', within)  1.17 us
  transfers between devices with their start and end apart: 17, of which 11 were waited for; matrix products, arithmetic and copies ran while one was open for 1% of the time, Pallas kernels for 16%

profile of v15, /device:TPU:0, one launch (start us, length us, event | category | flops | bytes accessed | tf_op | source)
XLA Modules:
  0.0 51.7 jit_solution(2987664175088774745)
XLA Ops:
  0.0 3.9 %collective-permute-start.10 = (s32[4,32]{1,0:T(4,128)}, s32[4,32]{1,0:T(4,128)S(1)}, u32[]{:S(2)}, u32[]{:S(2)}) collective-permute-start(s32[4,32]{1,0:T(4,128)} %bitcast.12), channel_id=1, source_target_pairs={{0,24},{8,16},{16,8},{24,0},{1,25},{9,17},{17,9},{25,1},{2,26},{10... | collective-permute-start | bytes 1544 | tf_op jit(solution)/shard_map/ppermute | solution.py:481
  3.9 0.5 collective-permute-start.11
  4.4 0.1 collective-permute-start.12
  4.5 1.0 %mask.1 = (bf16[512,128]{1,0:T(8,128)(2,1)S(1)}, s32[4,32]{1,0:T(4,128)S(1)}) custom-call(s32[10,1,512]{2,1,0:T(1,128)} %bitcast.11, s32[4,32]{1,0:T(4,128)} %bitcast.15), custom_call_target="tpu_custom_call" | custom-call | flops 1310720 | bytes 131072 | tf_op jit(solution)/shard_map/mask/pallas_call | solution.py:25
  5.5 0.2 collective-permute-done.10.refs_0_
  5.7 2.0 %collective-permute-done.11.refs_1_ = s32[4,32]{1,0:T(4,128)S(1)} collective-permute-done((s32[4,32]{1,0:T(4,128)}, s32[4,32]{1,0:T(4,128)S(1)}, u32[]{:S(2)}, u32[]{:S(2)}) %collective-permute-start.11) | collective-permute-done | bytes 544 | tf_op jit(solution)/shard_map/ppermute | solution.py:481
  7.7 0.5 collective-permute-done.12.refs_2_
  8.2 0.5 list.1
  8.7 1.4 %collective-permute-start.13 = (s32[8,128]{1,0:T(8,128)S(1)}, s32[8,128]{1,0:T(8,128)S(1)}, u32[]{:S(2)}, u32[]{:S(2)}) collective-permute-start(s32[8,128]{1,0:T(8,128)S(1)} %get-tuple-element.118.refs_0_), channel_id=1, source_target_pairs={{0,7},{1,2},{2,1},{3,4},{4,3},{5,6},{6,5},{7,0},{8,15},{9,10},{10,... | collective-permute-start | bytes 12296 | tf_op jit(solution)/shard_map/ppermute | solution.py:487
  10.1 1.9 %normalize.1.x_ref = bf16[512,2048]{1,0:T(8,128)(2,1)S(1)} custom-call(bf16[512,2048]{1,0:T(8,128)(2,1)} %bitcast.10), custom_call_target="tpu_custom_call" | custom-call | flops 6291456 | bytes 4194304 | tf_op jit(solution)/shard_map/normalize/pallas_call | solution.py:25
  11.9 1.6 %collective-permute-done.13.beyond_ref.refs_1_ = s32[8,128]{1,0:T(8,128)S(1)} collective-permute-done((s32[8,128]{1,0:T(8,128)S(1)}, s32[8,128]{1,0:T(8,128)S(1)}, u32[]{:S(2)}, u32[]{:S(2)}) %collective-permute-start.13) | collective-permute-done | bytes 4128 | tf_op jit(solution)/shard_map/ppermute | solution.py:487
  13.6 0.5 %pack_far.1 = (bf16[128,512]{1,0:T(8,128)(2,1)S(1)}, bf16[48,2048]{1,0:T(8,128)(2,1)S(1)}) custom-call(bf16[512,2048]{1,0:T(8,128)(2,1)S(1)} %normalize.1.x_ref, s32[8,128]{1,0:T(8,128)S(1)} %collective-permute-done.13.beyond_ref.refs_1_), custom_call_target="tpu_custom_call" | custom-call | flops 100663296 | tf_op jit(solution)/shard_map/pack_far/pallas_call | solution.py:25
  14.1 1.4 %collective-permute-start.16 = (bf16[48,2048]{1,0:T(8,128)(2,1)S(1)}, bf16[48,2048]{1,0:T(8,128)(2,1)S(1)}, u32[]{:S(2)}, u32[]{:S(2)}) collective-permute-start(bf16[48,2048]{1,0:T(8,128)(2,1)S(1)} %get-tuple-element.126.x_ref), channel_id=1, source_target_pairs={{0,7},{1,2},{2,1},{3,4},{4,3},{5,6},{6,5},{7,0},{8,15},{9,10},{10,... | collective-permute-start | bytes 589832 | tf_op jit(solution)/shard_map/ppermute | solution.py:487
  15.5 0.0 collective-permute-start.14
  15.5 1.2 %collective-permute-done.14.refs_2_ = s32[8,128]{1,0:T(8,128)S(1)} collective-permute-done((s32[8,128]{1,0:T(8,128)S(1)}, s32[8,128]{1,0:T(8,128)S(1)}, u32[]{:S(2)}, u32[]{:S(2)}) %collective-permute-start.14) | collective-permute-done | bytes 4128 | tf_op jit(solution)/shard_map/ppermute | solution.py:490
  16.7 1.2 %serve_near.1 = (bf16[48,2048]{1,0:T(8,128)(2,1)S(1)}, bf16[128,2048]{1,0:T(8,128)(2,1)S(1)}, bf16[176,2048]{1,0:T(8,128)(2,1)S(1)}, bf16[80,2048]{1,0:T(8,128)(...) custom-call(bf16[512,2048]{1,0:T(8,128)(2,1)S(1)} %normalize.1.x_ref, ...), custom_call_target="tpu_custom_call" | custom-call | flops 805306368 | tf_op jit(solution)/shard_map/serve_near/pallas_call | solution.py:25
  17.9 0.2 collective-permute-start.15
  18.1 4.2 %collective-permute-done.16.far_ref = bf16[48,2048]{1,0:T(8,128)(2,1)S(1)} collective-permute-done((bf16[48,2048]{1,0:T(8,128)(2,1)S(1)}, bf16[48,2048]{1,0:T(8,128)(2,1)S(1)}, u32[]{:S(2)}, u32[]{:S(2)}) %collective-permute-start.16) | collective-permute-done | bytes 196640 | tf_op jit(solution)/shard_map/ppermute | solution.py:487
  22.3 0.3 unpack.8.base_ref
  22.6 0.3 combine.4
  22.9 1.5 %collective-permute-start.17 = (bf16[32,2048]{1,0:T(8,128)(2,1)S(1)}, bf16[32,2048]{1,0:T(8,128)(2,1)S(1)}, u32[]{:S(2)}, u32[]{:S(2)}) collective-permute-start(bf16[32,2048]{1,0:T(8,128)(2,1)S(1)} %get-tuple-element.129), channel_id=1, source_target_pairs={{0,24},{8,16},{16,8},{24,0},{1,25},{9,17},{17,9},{25,1},{2,26},{10... | collective-permute-start | bytes 393224 | tf_op jit(solution)/shard_map/ppermute | solution.py:481
  24.4 0.5 %collective-permute-start.18 = (bf16[32,2048]{1,0:T(8,128)(2,1)S(1)}, bf16[32,2048]{1,0:T(8,128)(2,1)S(1)}, u32[]{:S(2)}, u32[]{:S(2)}) collective-permute-start(bf16[32,2048]{1,0:T(8,128)(2,1)S(1)} %get-tuple-element.130), channel_id=1, source_target_pairs={{0,16},{8,24},{16,0},{24,8},{1,17},{9,25},{17,1},{25,9},{2,18},{10... | collective-permute-start | bytes 393224 | tf_op jit(solution)/shard_map/ppermute | solution.py:481
  25.0 1.5 %collective-permute-start.19 = (bf16[32,2048]{1,0:T(8,128)(2,1)S(1)}, bf16[32,2048]{1,0:T(8,128)(2,1)S(1)}, u32[]{:S(2)}, u32[]{:S(2)}) collective-permute-start(bf16[32,2048]{1,0:T(8,128)(2,1)S(1)} %get-tuple-element.131), channel_id=1, source_target_pairs={{0,8},{8,0},{16,24},{24,16},{1,9},{9,1},{17,25},{25,17},{2,10},{10... | collective-permute-start | bytes 393224 | tf_op jit(solution)/shard_map/ppermute | solution.py:481
  26.4 0.0 collective-permute-start.21
  26.4 2.6 %collective-permute-start.22 = (s32[8,128]{1,0:T(8,128)S(1)}, s32[8,128]{1,0:T(8,128)S(1)}, u32[]{:S(2)}, u32[]{:S(2)}) collective-permute-start(s32[8,128]{1,0:T(8,128)S(1)} %get-tuple-element.135.rest_4_), channel_id=1, source_target_pairs={{0,5},{1,6},{2,7},{3,0},{4,1},{5,2},{6,3},{7,4},{8,13},{9,14},{10,... | collective-permute-start | bytes 12296 | tf_op jit(solution)/shard_map/ppermute | solution.py:484
  29.1 1.3 %collective-permute-done.21.rest_5_ = s32[8,128]{1,0:T(8,128)S(1)} collective-permute-done((s32[8,128]{1,0:T(8,128)S(1)}, s32[8,128]{1,0:T(8,128)S(1)}, u32[]{:S(2)}, u32[]{:S(2)}) %collective-permute-start.21) | collective-permute-done | bytes 4128 | tf_op jit(solution)/shard_map/ppermute | solution.py:484
  30.4 0.0 collective-permute-done.22.rest_6_
  30.4 0.0 collective-permute-done.17.rest_0_
  30.4 0.0 collective-permute-done.18.rest_1_
  30.4 0.7 %mix_far.3 = (bf16[48,2048]{1,0:T(8,128)(2,1)S(1)}, s32[8,128]{1,0:T(8,128)S(1)}) custom-call(bf16[48,2048]{1,0:T(8,128)(2,1)S(1)} %get-tuple-element.126.x_ref, bf16[128,128]{1,0:T(8,128)(2,1)S(1)} %get-tuple-element.134.mask_ref, bf16[32,2048]{1,0:T(8,128)(2,1)S(1)} %collective-permute-done.17.rest_0_, ...), custom_call_target="tpu_custom_call" | custom-call | flops 50331648 | tf_op jit(solution)/shard_map/mix_far/pallas_call | solution.py:25
  31.1 1.9 %collective-permute-start.23 = (bf16[48,2048]{1,0:T(8,128)(2,1)S(1)}, bf16[48,2048]{1,0:T(8,128)(2,1)S(1)}, u32[]{:S(2)}, u32[]{:S(2)}) collective-permute-start(bf16[48,2048]{1,0:T(8,128)(2,1)S(1)} %get-tuple-element.136), channel_id=1, source_target_pairs={{0,7},{1,2},{2,1},{3,4},{4,3},{5,6},{6,5},{7,0},{8,15},{9,10},{10,... | collective-permute-start | bytes 589832 | tf_op jit(solution)/shard_map/ppermute | solution.py:487
  33.0 1.1 %mix_near.3 = (bf16[48,2048]{1,0:T(8,128)(2,1)S(1)}, bf16[128,2048]{1,0:T(8,128)(2,1)S(1)}) custom-call(bf16[176,2048]{1,0:T(8,128)(2,1)S(1)} %get-tuple-element.122.x_ref, bf16[176,128]{1,0:T(8,128)(2,1)S(1)} %get-tuple-element.123.mask_ref, bf16[32,2048]{1,0:T(8,128)(2,1)S(1)} %collective-permute-done.17.rest_0_, ...), custom_call_target="tpu_custom_call" | custom-call | flops 184549376 | tf_op jit(solution)/shard_map/mix_near/pallas_call | solution.py:25
  34.2 0.1 collective-permute-start.20
  34.2 2.5 %mix_whole_late.3.refs_1_.rest_4_ = bf16[512,2048]{1,0:T(8,128)(2,1)S(1)} custom-call(bf16[512,2048]{1,0:T(8,128)(2,1)S(1)} %normalize.1.x_ref, bf16[512,128]{1,0:T(8,128)(2,1)S(1)} %get-tuple-element.117.mask_ref, bf16[32,2048]{1,0:T(8,128)(2,1)S(1)} %collective-permute-done.17.rest_0_, bf16[32,2048]{1,0:T(8,128)(2,1)S(1)} %collective-permute-done.18.rest_1_, ...), custom_call_target="tpu_custom_call" | custom-call | flops 536870912 | tf_op jit(solution)/shard_map/mix_whole_late/pallas_call | solution.py:25
  36.8 2.6 %collective-permute-done.23.far_ref = bf16[48,2048]{1,0:T(8,128)(2,1)S(1)} collective-permute-done((bf16[48,2048]{1,0:T(8,128)(2,1)S(1)}, bf16[48,2048]{1,0:T(8,128)(2,1)S(1)}, u32[]{:S(2)}, u32[]{:S(2)}) %collective-permute-start.23) | collective-permute-done | bytes 196640 | tf_op jit(solution)/shard_map/ppermute | solution.py:487
  39.4 0.3 unpack.9.base_ref
  39.7 0.0 collective-permute-done.20.core_ref
  39.7 0.3 combine.5
  40.0 2.5 %collective-permute-start.24 = (bf16[32,2048]{1,0:T(8,128)(2,1)S(1)}, bf16[32,2048]{1,0:T(8,128)(2,1)S(1)}, u32[]{:S(2)}, u32[]{:S(2)}) collective-permute-start(bf16[32,2048]{1,0:T(8,128)(2,1)S(1)} %get-tuple-element.140), channel_id=1, source_target_pairs={{0,24},{8,16},{16,8},{24,0},{1,25},{9,17},{17,9},{25,1},{2,26},{10... | collective-permute-start | bytes 393224 | tf_op jit(solution)/shard_map/ppermute | solution.py:481
  42.5 0.5 collective-permute-start.25
  43.0 0.6 %collective-permute-start.26 = (bf16[32,2048]{1,0:T(8,128)(2,1)S(1)}, bf16[32,2048]{1,0:T(8,128)(2,1)S(1)}, u32[]{:S(2)}, u32[]{:S(2)}) collective-permute-start(bf16[32,2048]{1,0:T(8,128)(2,1)S(1)} %get-tuple-element.142), channel_id=1, source_target_pairs={{0,8},{8,0},{16,24},{24,16},{1,9},{9,1},{17,25},{25,17},{2,10},{10... | collective-permute-start | bytes 393224 | tf_op jit(solution)/shard_map/ppermute | solution.py:481
  43.5 0.5 slice.16
  44.7 0.1 mix_whole_early.3
  44.7 1.1 %collective-permute-done.24 = bf16[32,2048]{1,0:T(8,128)(2,1)S(1)} collective-permute-done((bf16[32,2048]{1,0:T(8,128)(2,1)S(1)}, bf16[32,2048]{1,0:T(8,128)(2,1)S(1)}, u32[]{:S(2)}, u32[]{:S(2)}) %collective-permute-start.24) | collective-permute-done | bytes 131104 | tf_op jit(solution)/shard_map/ppermute | solution.py:481
  45.9 1.5 %collective-permute-done.25 = bf16[32,2048]{1,0:T(8,128)(2,1)S(1)} collective-permute-done((bf16[32,2048]{1,0:T(8,128)(2,1)S(1)}, bf16[32,2048]{1,0:T(8,128)(2,1)S(1)}, u32[]{:S(2)}, u32[]{:S(2)}) %collective-permute-start.25) | collective-permute-done | bytes 131104 | tf_op jit(solution)/shard_map/ppermute | solution.py:481
  47.4 0.5 collective-permute-done.26
  47.9 3.6 %conditional.1 = (bf16[1,1,512,2048]{3,2,1,0:T(8,128)(2,1)}) conditional(s32[]{:T(128)} %bitcast.6, (bf16[512,2048]{1,0:T(8,128)(2,1)S(1)}, bf16[512,128]{1,0:T(8,128)(2,1)S(1)}, bf16[32,2048]{1,0:T(8,128)(2,1)S(1)}, bf16[32,2048]{1,0:T(8,128)(2,1)S(1)}, bf16[32,2048]{1,0:T(8,128)(2,1)S(1)}, /*index=5*/bf16[32,2048]{1,0:T(8,128)(2,1)S(1)}) %tuple.13, ...), branch_computations={%region_0.0_spmd, %region_1.0_spmd} | conditional | flops 53624569856 | bytes 121962904 | solution.py:548
  47.9 3.4 %mix.2 = bf16[512,2048]{1,0:T(8,128)(2,1)} custom-call(bf16[512,2048]{1,0:T(8,128)(2,1)S(1)} %get-tuple-element.53.x_ref, bf16[512,128]{1,0:T(8,128)(2,1)S(1)} %get-tuple-element.54.mask_ref, bf16[32,2048]{1,0:T(8,128)(2,1)S(1)} %get-tuple-element.55.rest_0_, bf16[32,2048]{1,0:T(8,128)(2,1)S(1)} %get-tuple-element.56.rest_1_, ...), custom_call_target="tpu_custom_call" | custom-call | flops 536870912 | bytes 4194304 | tf_op jit(solution)/shard_map/cond/branch_0_fun/mix/pallas_call | solution.py:25
  (2 shorter events, 0.0 us)
Async XLA Ops:
  0.0 5.7 %collective-permute-start.10 = (s32[4,32]{1,0:T(4,128)}, s32[4,32]{1,0:T(4,128)S(1)}, u32[]{:S(2)}, u32[]{:S(2)}) collective-permute-start(s32[4,32]{1,0:T(4,128)} %bitcast.12), channel_id=1, source_target_pairs={{0,24},{8,16},{16,8},{24,0},{1,25},{9,17},{17,9},{25,1},{2,26},{10... | collective-permute-start | bytes 1544 | tf_op jit(solution)/shard_map/ppermute | solution.py:481
  3.9 3.8 %collective-permute-start.11 = (s32[4,32]{1,0:T(4,128)}, s32[4,32]{1,0:T(4,128)S(1)}, u32[]{:S(2)}, u32[]{:S(2)}) collective-permute-start(s32[4,32]{1,0:T(4,128)} %bitcast.13), channel_id=1, source_target_pairs={{0,16},{8,24},{16,0},{24,8},{1,17},{9,25},{17,1},{25,9},{2,18},{10... | collective-permute-start | bytes 1544 | tf_op jit(solution)/shard_map/ppermute | solution.py:481
  4.4 3.8 %collective-permute-start.12 = (s32[4,32]{1,0:T(4,128)}, s32[4,32]{1,0:T(4,128)S(1)}, u32[]{:S(2)}, u32[]{:S(2)}) collective-permute-start(s32[4,32]{1,0:T(4,128)} %bitcast.14), channel_id=1, source_target_pairs={{0,8},{8,0},{16,24},{24,16},{1,9},{9,1},{17,25},{25,17},{2,10},{10... | collective-permute-start | bytes 1544 | tf_op jit(solution)/shard_map/ppermute | solution.py:481
  8.7 4.9 %collective-permute-start.13 = (s32[8,128]{1,0:T(8,128)S(1)}, s32[8,128]{1,0:T(8,128)S(1)}, u32[]{:S(2)}, u32[]{:S(2)}) collective-permute-start(s32[8,128]{1,0:T(8,128)S(1)} %get-tuple-element.118.refs_0_), channel_id=1, source_target_pairs={{0,7},{1,2},{2,1},{3,4},{4,3},{5,6},{6,5},{7,0},{8,15},{9,10},{10,... | collective-permute-start | bytes 12296 | tf_op jit(solution)/shard_map/ppermute | solution.py:487
  14.1 8.2 %collective-permute-start.16 = (bf16[48,2048]{1,0:T(8,128)(2,1)S(1)}, bf16[48,2048]{1,0:T(8,128)(2,1)S(1)}, u32[]{:S(2)}, u32[]{:S(2)}) collective-permute-start(bf16[48,2048]{1,0:T(8,128)(2,1)S(1)} %get-tuple-element.126.x_ref), channel_id=1, source_target_pairs={{0,7},{1,2},{2,1},{3,4},{4,3},{5,6},{6,5},{7,0},{8,15},{9,10},{10,... | collective-permute-start | bytes 589832 | tf_op jit(solution)/shard_map/ppermute | solution.py:487
  15.5 1.2 %collective-permute-start.14 = (s32[8,128]{1,0:T(8,128)S(1)}, s32[8,128]{1,0:T(8,128)S(1)}, u32[]{:S(2)}, u32[]{:S(2)}) collective-permute-start(s32[8,128]{1,0:T(8,128)S(1)} %get-tuple-element.121), channel_id=1, source_target_pairs={{0,1},{1,0},{2,3},{3,2},{4,5},{5,4},{6,7},{7,6},{8,9},{9,8},{10,11... | collective-permute-start | bytes 12296 | tf_op jit(solution)/shard_map/ppermute | solution.py:490
  17.9 4.7 %collective-permute-start.15 = (bf16[48,2048]{1,0:T(8,128)(2,1)S(1)}, bf16[48,2048]{1,0:T(8,128)(2,1)S(1)}, u32[]{:S(2)}, u32[]{:S(2)}) collective-permute-start(bf16[48,2048]{1,0:T(8,128)(2,1)S(1)} %get-tuple-element.124), channel_id=1, source_target_pairs={{0,1},{1,0},{2,3},{3,2},{4,5},{5,4},{6,7},{7,6},{8,9},{9,8},{10,11... | collective-permute-start | bytes 589832 | tf_op jit(solution)/shard_map/ppermute | solution.py:490
  22.9 7.5 %collective-permute-start.17 = (bf16[32,2048]{1,0:T(8,128)(2,1)S(1)}, bf16[32,2048]{1,0:T(8,128)(2,1)S(1)}, u32[]{:S(2)}, u32[]{:S(2)}) collective-permute-start(bf16[32,2048]{1,0:T(8,128)(2,1)S(1)} %get-tuple-element.129), channel_id=1, source_target_pairs={{0,24},{8,16},{16,8},{24,0},{1,25},{9,17},{17,9},{25,1},{2,26},{10... | collective-permute-start | bytes 393224 | tf_op jit(solution)/shard_map/ppermute | solution.py:481
  24.4 6.0 %collective-permute-start.18 = (bf16[32,2048]{1,0:T(8,128)(2,1)S(1)}, bf16[32,2048]{1,0:T(8,128)(2,1)S(1)}, u32[]{:S(2)}, u32[]{:S(2)}) collective-permute-start(bf16[32,2048]{1,0:T(8,128)(2,1)S(1)} %get-tuple-element.130), channel_id=1, source_target_pairs={{0,16},{8,24},{16,0},{24,8},{1,17},{9,25},{17,1},{25,9},{2,18},{10... | collective-permute-start | bytes 393224 | tf_op jit(solution)/shard_map/ppermute | solution.py:481
  25.0 5.5 %collective-permute-start.19 = (bf16[32,2048]{1,0:T(8,128)(2,1)S(1)}, bf16[32,2048]{1,0:T(8,128)(2,1)S(1)}, u32[]{:S(2)}, u32[]{:S(2)}) collective-permute-start(bf16[32,2048]{1,0:T(8,128)(2,1)S(1)} %get-tuple-element.131), channel_id=1, source_target_pairs={{0,8},{8,0},{16,24},{24,16},{1,9},{9,1},{17,25},{25,17},{2,10},{10... | collective-permute-start | bytes 393224 | tf_op jit(solution)/shard_map/ppermute | solution.py:481
  26.4 3.9 %collective-permute-start.21 = (s32[8,128]{1,0:T(8,128)S(1)}, s32[8,128]{1,0:T(8,128)S(1)}, u32[]{:S(2)}, u32[]{:S(2)}) collective-permute-start(s32[8,128]{1,0:T(8,128)S(1)} %get-tuple-element.135.rest_4_), channel_id=1, source_target_pairs={{0,3},{1,4},{2,5},{3,6},{4,7},{5,0},{6,1},{7,2},{8,11},{9,12},{10,... | collective-permute-start | bytes 12296 | tf_op jit(solution)/shard_map/ppermute | solution.py:484
  26.4 4.0 %collective-permute-start.22 = (s32[8,128]{1,0:T(8,128)S(1)}, s32[8,128]{1,0:T(8,128)S(1)}, u32[]{:S(2)}, u32[]{:S(2)}) collective-permute-start(s32[8,128]{1,0:T(8,128)S(1)} %get-tuple-element.135.rest_4_), channel_id=1, source_target_pairs={{0,5},{1,6},{2,7},{3,0},{4,1},{5,2},{6,3},{7,4},{8,13},{9,14},{10,... | collective-permute-start | bytes 12296 | tf_op jit(solution)/shard_map/ppermute | solution.py:484
  31.1 8.3 %collective-permute-start.23 = (bf16[48,2048]{1,0:T(8,128)(2,1)S(1)}, bf16[48,2048]{1,0:T(8,128)(2,1)S(1)}, u32[]{:S(2)}, u32[]{:S(2)}) collective-permute-start(bf16[48,2048]{1,0:T(8,128)(2,1)S(1)} %get-tuple-element.136), channel_id=1, source_target_pairs={{0,7},{1,2},{2,1},{3,4},{4,3},{5,6},{6,5},{7,0},{8,15},{9,10},{10,... | collective-permute-start | bytes 589832 | tf_op jit(solution)/shard_map/ppermute | solution.py:487
  34.2 5.5 %collective-permute-start.20 = (bf16[48,2048]{1,0:T(8,128)(2,1)S(1)}, bf16[48,2048]{1,0:T(8,128)(2,1)S(1)}, u32[]{:S(2)}, u32[]{:S(2)}) collective-permute-start(bf16[48,2048]{1,0:T(8,128)(2,1)S(1)} %get-tuple-element.133), channel_id=1, source_target_pairs={{0,1},{1,0},{2,3},{3,2},{4,5},{5,4},{6,7},{7,6},{8,9},{9,8},{10,11... | collective-permute-start | bytes 589832 | tf_op jit(solution)/shard_map/ppermute | solution.py:490
  40.0 5.9 %collective-permute-start.24 = (bf16[32,2048]{1,0:T(8,128)(2,1)S(1)}, bf16[32,2048]{1,0:T(8,128)(2,1)S(1)}, u32[]{:S(2)}, u32[]{:S(2)}) collective-permute-start(bf16[32,2048]{1,0:T(8,128)(2,1)S(1)} %get-tuple-element.140), channel_id=1, source_target_pairs={{0,24},{8,16},{16,8},{24,0},{1,25},{9,17},{17,9},{25,1},{2,26},{10... | collective-permute-start | bytes 393224 | tf_op jit(solution)/shard_map/ppermute | solution.py:481
  42.5 5.0 %collective-permute-start.25 = (bf16[32,2048]{1,0:T(8,128)(2,1)S(1)}, bf16[32,2048]{1,0:T(8,128)(2,1)S(1)}, u32[]{:S(2)}, u32[]{:S(2)}) collective-permute-start(bf16[32,2048]{1,0:T(8,128)(2,1)S(1)} %get-tuple-element.141), channel_id=1, source_target_pairs={{0,16},{8,24},{16,0},{24,8},{1,17},{9,25},{17,1},{25,9},{2,18},{10... | collective-permute-start | bytes 393224 | tf_op jit(solution)/shard_map/ppermute | solution.py:481
  43.0 5.0 %collective-permute-start.26 = (bf16[32,2048]{1,0:T(8,128)(2,1)S(1)}, bf16[32,2048]{1,0:T(8,128)(2,1)S(1)}, u32[]{:S(2)}, u32[]{:S(2)}) collective-permute-start(bf16[32,2048]{1,0:T(8,128)(2,1)S(1)} %get-tuple-element.142), channel_id=1, source_target_pairs={{0,8},{8,0},{16,24},{24,16},{1,9},{9,1},{17,25},{25,17},{2,10},{10... | collective-permute-start | bytes 393224 | tf_op jit(solution)/shard_map/ppermute | solution.py:481

commit v16 on v15

--- a/solution.py
+++ b/solution.py
@@ -9,6 +9,7 @@
 
 LANES = 128
 BLOCK = 128
+COPY = 64
 FIRST_SHARE = 3, 8
 BOTH_LAST = (((1,), (1,)), ((), ()))
 
@@ -285,6 +286,33 @@
     return most, parts
 
 
+def unpack_both_kernel(far_expand, core_expand, own_ref, core_ref, far_ref, *refs):
+    out_refs = refs[1:]
+    cap, sent = out_refs[0].shape[0], far_ref.shape[0]
+    rows = jnp.dot(core_expand[:, :sent], core_ref[...], preferred_element_type=jnp.float32)
+    rows += jnp.dot(far_expand[:, :sent], far_ref[...], preferred_element_type=jnp.float32)
+    rows = (rows + own_ref[...].astype(jnp.float32)).astype(jnp.bfloat16)
+    for d, out in enumerate(out_refs):
+        out[...] = rows[d * cap : (d + 1) * cap]
+
+
+def unpack_both_call(expands, far, core, own, after, servers):
+    total, width = own.shape
+    return kernel_call(
+        "unpack_both",
+        unpack_both_kernel,
+        [bf16(total // servers, width)] * servers,
+        *expands,
+        own,
+        core,
+        far,
+        after,
+        flops=4 * total * far.shape[0] * width,
+        in_specs=[pl.BlockSpec(memory_space=pltpu.VMEM)] * 5
+        + [pl.BlockSpec(memory_space=pl.ANY)],
+    )
+
+
 def fill(buffer, parts):
     cap = parts[0].shape[0]
     for d, ref in enumerate(reversed(parts)):
@@ -385,33 +413,30 @@
     )
 
 
-def mix_blocks(x_ref, mask_ref, buffer, weights, whole, out_ref, sems):
-    weights[...] = weigh(x_ref[...], buffer[...], mask_ref[...])
-    blocks = [pl.ds(start, BLOCK) for start in range(0, x_ref.shape[0], BLOCK)]
-    copies, added = [], None
-    for i in range(len(blocks) + 1):
-        before = added
-        if i < len(blocks):
-            added = jnp.dot(
-                weights[blocks[i]], buffer[...], preferred_element_type=jnp.float32
+def mix_blocks(x_ref, mask_ref, buffer, whole, out_ref, sems):
+    copies = []
+    for start in range(0, x_ref.shape[0], BLOCK):
+        here = pl.ds(start, BLOCK)
+        weights = weigh(x_ref[here], buffer[...], mask_ref[here])
+        whole[here] = mix(x_ref[here], weights, buffer[...])
+        for half in range(start, start + BLOCK, COPY):
+            rows = pl.ds(half, COPY)
+            copy = pltpu.make_async_copy(
+                whole.at[rows], out_ref.at[rows], sems.at[half // COPY]
             )
-        if i:
-            here = blocks[i - 1]
-            mixed = x_ref[here].astype(jnp.float32) + before
-            whole[here] = normalize(mixed).astype(jnp.bfloat16)
-            copies.append(pltpu.make_async_copy(whole.at[here], out_ref.at[here], sems.at[i - 1]))
-            copies[-1].start()
+            copy.start()
+            copies.append(copy)
     for copy in copies:
         copy.wait()
 
 
 def early_kernel(servers, x_ref, mask_ref, *rest):
-    parts, (_, out_ref, buffer, weights, whole, sems) = rest[:servers], rest[servers:]
+    parts, (_, out_ref, buffer, whole, sems) = rest[:servers], rest[servers:]
 
     @pl.when(jnp.logical_not(is_late()))
     def _():
         fill(buffer, parts)
-        mix_blocks(x_ref, mask_ref, buffer, weights, whole, out_ref, sems)
+        mix_blocks(x_ref, mask_ref, buffer, whole, out_ref, sems)
 
 
 def early_call(x, mask, parts, out):
@@ -428,9 +453,8 @@
         flops=4 * total * rows * width,
         scratch=[
             pltpu.VMEM((total, width), jnp.bfloat16),
-            pltpu.VMEM((rows, total), jnp.bfloat16),
             pltpu.VMEM((rows, width), jnp.bfloat16),
-            pltpu.SemaphoreType.DMA((rows // BLOCK,)),
+            pltpu.SemaphoreType.DMA((rows // COPY,)),
         ],
         in_specs=[pl.BlockSpec(memory_space=pltpu.VMEM)] * (2 + servers)
         + [pl.BlockSpec(memory_space=pl.ANY)],
@@ -440,9 +464,9 @@
 
 
 def last_kernel(servers, x_ref, mask_ref, *rest):
-    parts, (out_ref, buffer, weights, whole, sems) = rest[:servers], rest[servers:]
+    parts, (out_ref, buffer, whole, sems) = rest[:servers], rest[servers:]
     fill(buffer, parts)
-    mix_blocks(x_ref, mask_ref, buffer, weights, whole, out_ref, sems)
+    mix_blocks(x_ref, mask_ref, buffer, whole, out_ref, sems)
 
 
 def last_call(x, mask, parts):
@@ -459,9 +483,8 @@
         moved=4 * rows * width,
         scratch=[
             pltpu.VMEM((total, width), jnp.bfloat16),
-            pltpu.VMEM((rows, total), jnp.bfloat16),
             pltpu.VMEM((rows, width), jnp.bfloat16),
-            pltpu.SemaphoreType.DMA((rows // BLOCK,)),
+            pltpu.SemaphoreType.DMA((rows // COPY,)),
         ],
         out_specs=pl.BlockSpec(memory_space=pltpu.HBM),
     )
@@ -493,8 +516,8 @@
         got = {d: turn(parts[d], d) for d in reversed(range(1, servers))}
         return [parts[0]] + [got[d] for d in range(1, servers)]
 
-    def exchange(expands, far, core, own, most, after=()):
-        base = unpack_call(expands[0], across(far), own, after=after)
+    def exchange(expands, far, core, own, most):
+        base = unpack_call(expands[0], across(far), own)
         most, parts = combine_call(expands[1], inside(core), base, most, servers)
         return most, turned(parts)
 
@@ -502,8 +525,8 @@
         far, most = far_mix_call(far, far_mask, parts, mosts)
         core, own = near_mix_call(near, near_mask, parts)
         y = late_call(x, mask, parts)
-        most, last = exchange(expands, far, core, own, most, after=[y])
-        return early_call(x, mask, parts, y), most, last
+        last = unpack_both_call(expands, across(far), inside(core), own, y, servers)
+        return early_call(x, mask, parts, y), most, turned(last)
 
     def in_full(x, y, mask, far, near, rest, masks, expands, most, first, last):
         late = unpack_call(expands[1], inside(rest[1]), first=sent)

time: 51.9 us -> 53.4 us (1.029)
  waiting for transfers between devices: 16.9 us -> 20 us
  starting transfers between devices: 19.2 us -> 18.4 us
    ppermute x9, waiting for transfers between devices: 5.92 us -> 8.68 us  [turn(): return lax.ppermute(value, 'clus', [(c, c ^ d) for c in range(servers)])]
    ppermute x3, starting transfers between devices: 0.3 us -> 1.74 us  [inside(): return lax.ppermute(value, 'rep', within)]
    ppermute x3, starting transfers between devices: 4.72 us -> 3.3 us  [across(): return lax.ppermute(value, 'rep', beyond)]
    ppermute x2, starting transfers between devices: 2.64 us -> 1.75 us  [shift(): lax.ppermute(value, 'rep', [(g, (g + by) % groups) for g in range(groups)])]
    ppermute x2, waiting for transfers between devices: 1.33 us -> 2.19 us  [shift(): lax.ppermute(value, 'rep', [(g, (g + by) % groups) for g in range(groups)])]
    pallas_call x14 -> x13, Pallas kernels: 13.9 us -> 13.4 us  [kernel_call(): pl.pallas_call(kernel, out_shape=outs, scratch_shapes=scratch, compiler_p...]
  transfers between devices with their start and end apart: 17 -> 17, of which waited for: 11 -> 10; matrix products, arithmetic and copies ran while one was open for 1% -> 1% of each run, Pallas kernels for 16% -> 15%
where the time goes in v16:
time: 53.4 us; the launch traced here: 53.2 us
  waiting for transfers between devices  20 us (37%)
  starting transfers between devices  18.4 us (34%)
  Pallas kernels  13.4 us (25%)
  between operations  0.94 us (2%)
    pallas_call x13, Pallas kernels, kernel_call(): pl.pallas_call(kernel, out_shape=outs, scratch_shapes=scratch, compiler_p...  13.4 us
    ppermute x9, starting transfers between devices, turn(): return lax.ppermute(value, 'clus', [(c, c ^ d) for c in range(servers)])  11.6 us
    ppermute x9, waiting for transfers between devices, turn(): return lax.ppermute(value, 'clus', [(c, c ^ d) for c in range(servers)])  8.68 us
    ppermute x3, waiting for transfers between devices, across(): return lax.ppermute(value, 'rep', beyond)  7.97 us
    ppermute x3, starting transfers between devices, across(): return lax.ppermute(value, 'rep', beyond)  3.3 us
    ppermute x2, waiting for transfers between devices, shift(): lax.ppermute(value, 'rep', [(g, (g + by) % groups) for g in range(groups)])  2.19 us
    ppermute x2, starting transfers between devices, shift(): lax.ppermute(value, 'rep', [(g, (g + by) % groups) for g in range(groups)])  1.75 us
    ppermute x3, starting transfers between devices, inside(): return lax.ppermute(value, 'rep', within)  1.74 us
  transfers between devices with their start and end apart: 17, of which 10 were waited for; matrix products, arithmetic and copies ran while one was open for 1% of the time, Pallas kernels for 15%

profile of v16, /device:TPU:0, one launch (start us, length us, event | category | flops | bytes accessed | tf_op | source)
XLA Modules:
  0.0 53.2 jit_solution(11365587162729981340)
XLA Ops:
  0.0 2.9 %collective-permute-start.12 = (s32[4,32]{1,0:T(4,128)}, s32[4,32]{1,0:T(4,128)S(1)}, u32[]{:S(2)}, u32[]{:S(2)}) collective-permute-start(s32[4,32]{1,0:T(4,128)} %bitcast.12), channel_id=1, source_target_pairs={{0,8},{8,0},{16,24},{24,16},{1,9},{9,1},{17,25},{25,17},{2,10},{10... | collective-permute-start | bytes 1544 | tf_op jit(solution)/shard_map/ppermute | solution.py:504
  2.9 1.5 %collective-permute-start.11 = (s32[4,32]{1,0:T(4,128)}, s32[4,32]{1,0:T(4,128)S(1)}, u32[]{:S(2)}, u32[]{:S(2)}) collective-permute-start(s32[4,32]{1,0:T(4,128)} %bitcast.13), channel_id=1, source_target_pairs={{0,16},{8,24},{16,0},{24,8},{1,17},{9,25},{17,1},{25,9},{2,18},{10... | collective-permute-start | bytes 1544 | tf_op jit(solution)/shard_map/ppermute | solution.py:504
  4.5 0.0 collective-permute-start.10
  4.5 1.0 %mask.1 = (bf16[512,128]{1,0:T(8,128)(2,1)S(1)}, s32[4,32]{1,0:T(4,128)S(1)}) custom-call(s32[10,1,512]{2,1,0:T(1,128)} %bitcast.11, s32[4,32]{1,0:T(4,128)} %bitcast.15), custom_call_target="tpu_custom_call" | custom-call | flops 1310720 | bytes 131072 | tf_op jit(solution)/shard_map/mask/pallas_call | solution.py:26
  5.5 0.0 collective-permute-done.12.refs_2_
  5.5 1.3 %collective-permute-done.11.refs_1_ = s32[4,32]{1,0:T(4,128)S(1)} collective-permute-done((s32[4,32]{1,0:T(4,128)}, s32[4,32]{1,0:T(4,128)S(1)}, u32[]{:S(2)}, u32[]{:S(2)}) %collective-permute-start.11) | collective-permute-done | bytes 544 | tf_op jit(solution)/shard_map/ppermute | solution.py:504
  6.7 2.4 %collective-permute-done.10.refs_0_ = s32[4,32]{1,0:T(4,128)S(1)} collective-permute-done((s32[4,32]{1,0:T(4,128)}, s32[4,32]{1,0:T(4,128)S(1)}, u32[]{:S(2)}, u32[]{:S(2)}) %collective-permute-start.10) | collective-permute-done | bytes 544 | tf_op jit(solution)/shard_map/ppermute | solution.py:504
  9.2 0.5 list.1
  9.6 1.4 %collective-permute-start.13 = (s32[8,128]{1,0:T(8,128)S(1)}, s32[8,128]{1,0:T(8,128)S(1)}, u32[]{:S(2)}, u32[]{:S(2)}) collective-permute-start(s32[8,128]{1,0:T(8,128)S(1)} %get-tuple-element.114.refs_0_), channel_id=1, source_target_pairs={{0,7},{1,2},{2,1},{3,4},{4,3},{5,6},{6,5},{7,0},{8,15},{9,10},{10,... | collective-permute-start | bytes 12296 | tf_op jit(solution)/shard_map/ppermute | solution.py:510
  11.0 1.9 %normalize.1.x_ref = bf16[512,2048]{1,0:T(8,128)(2,1)S(1)} custom-call(bf16[512,2048]{1,0:T(8,128)(2,1)} %bitcast.10), custom_call_target="tpu_custom_call" | custom-call | flops 6291456 | bytes 4194304 | tf_op jit(solution)/shard_map/normalize/pallas_call | solution.py:26
  12.9 1.6 %collective-permute-done.13.beyond_ref.refs_1_ = s32[8,128]{1,0:T(8,128)S(1)} collective-permute-done((s32[8,128]{1,0:T(8,128)S(1)}, s32[8,128]{1,0:T(8,128)S(1)}, u32[]{:S(2)}, u32[]{:S(2)}) %collective-permute-start.13) | collective-permute-done | bytes 4128 | tf_op jit(solution)/shard_map/ppermute | solution.py:510
  14.5 0.5 pack_far.1
  15.0 1.4 %collective-permute-start.16 = (bf16[48,2048]{1,0:T(8,128)(2,1)S(1)}, bf16[48,2048]{1,0:T(8,128)(2,1)S(1)}, u32[]{:S(2)}, u32[]{:S(2)}) collective-permute-start(bf16[48,2048]{1,0:T(8,128)(2,1)S(1)} %get-tuple-element.115.x_ref), channel_id=1, source_target_pairs={{0,7},{1,2},{2,1},{3,4},{4,3},{5,6},{6,5},{7,0},{8,15},{9,10},{10,... | collective-permute-start | bytes 589832 | tf_op jit(solution)/shard_map/ppermute | solution.py:510
  16.4 0.0 collective-permute-start.14
  16.4 1.2 %collective-permute-done.14.refs_2_ = s32[8,128]{1,0:T(8,128)S(1)} collective-permute-done((s32[8,128]{1,0:T(8,128)S(1)}, s32[8,128]{1,0:T(8,128)S(1)}, u32[]{:S(2)}, u32[]{:S(2)}) %collective-permute-start.14) | collective-permute-done | bytes 4128 | tf_op jit(solution)/shard_map/ppermute | solution.py:513
  17.6 1.2 %serve_near.1 = (bf16[48,2048]{1,0:T(8,128)(2,1)S(1)}, bf16[128,2048]{1,0:T(8,128)(2,1)S(1)}, bf16[176,2048]{1,0:T(8,128)(2,1)S(1)}, bf16[80,2048]{1,0:T(8,128)(...) custom-call(bf16[512,2048]{1,0:T(8,128)(2,1)S(1)} %normalize.1.x_ref, ...), custom_call_target="tpu_custom_call" | custom-call | flops 805306368 | tf_op jit(solution)/shard_map/serve_near/pallas_call | solution.py:26
  18.8 0.2 collective-permute-start.15
  19.1 4.2 %collective-permute-done.16.far_ref = bf16[48,2048]{1,0:T(8,128)(2,1)S(1)} collective-permute-done((bf16[48,2048]{1,0:T(8,128)(2,1)S(1)}, bf16[48,2048]{1,0:T(8,128)(2,1)S(1)}, u32[]{:S(2)}, u32[]{:S(2)}) %collective-permute-start.16) | collective-permute-done | bytes 196640 | tf_op jit(solution)/shard_map/ppermute | solution.py:510
  23.3 0.3 unpack.5.base_ref
  23.5 0.0 collective-permute-done.15.core_ref
  23.6 0.3 combine.1
  23.8 0.5 %collective-permute-start.17 = (bf16[32,2048]{1,0:T(8,128)(2,1)S(1)}, bf16[32,2048]{1,0:T(8,128)(2,1)S(1)}, u32[]{:S(2)}, u32[]{:S(2)}) collective-permute-start(bf16[32,2048]{1,0:T(8,128)(2,1)S(1)} %get-tuple-element.126), channel_id=1, source_target_pairs={{0,24},{8,16},{16,8},{24,0},{1,25},{9,17},{17,9},{25,1},{2,26},{10... | collective-permute-start | bytes 393224 | tf_op jit(solution)/shard_map/ppermute | solution.py:504
  24.4 1.5 %collective-permute-start.18 = (bf16[32,2048]{1,0:T(8,128)(2,1)S(1)}, bf16[32,2048]{1,0:T(8,128)(2,1)S(1)}, u32[]{:S(2)}, u32[]{:S(2)}) collective-permute-start(bf16[32,2048]{1,0:T(8,128)(2,1)S(1)} %get-tuple-element.127), channel_id=1, source_target_pairs={{0,16},{8,24},{16,0},{24,8},{1,17},{9,25},{17,1},{25,9},{2,18},{10... | collective-permute-start | bytes 393224 | tf_op jit(solution)/shard_map/ppermute | solution.py:504
  25.9 1.5 %collective-permute-start.19 = (bf16[32,2048]{1,0:T(8,128)(2,1)S(1)}, bf16[32,2048]{1,0:T(8,128)(2,1)S(1)}, u32[]{:S(2)}, u32[]{:S(2)}) collective-permute-start(bf16[32,2048]{1,0:T(8,128)(2,1)S(1)} %get-tuple-element.128), channel_id=1, source_target_pairs={{0,8},{8,0},{16,24},{24,16},{1,9},{9,1},{17,25},{25,17},{2,10},{10... | collective-permute-start | bytes 393224 | tf_op jit(solution)/shard_map/ppermute | solution.py:504
  27.4 0.0 collective-permute-start.21
  27.4 1.7 %collective-permute-start.20 = (s32[8,128]{1,0:T(8,128)S(1)}, s32[8,128]{1,0:T(8,128)S(1)}, u32[]{:S(2)}, u32[]{:S(2)}) collective-permute-start(s32[8,128]{1,0:T(8,128)S(1)} %get-tuple-element.130.rest_4_), channel_id=1, source_target_pairs={{0,3},{1,4},{2,5},{3,6},{4,7},{5,0},{6,1},{7,2},{8,11},{9,12},{10,... | collective-permute-start | bytes 12296 | tf_op jit(solution)/shard_map/ppermute | solution.py:507
  29.1 1.3 %collective-permute-done.21.rest_6_ = s32[8,128]{1,0:T(8,128)S(1)} collective-permute-done((s32[8,128]{1,0:T(8,128)S(1)}, s32[8,128]{1,0:T(8,128)S(1)}, u32[]{:S(2)}, u32[]{:S(2)}) %collective-permute-start.21) | collective-permute-done | bytes 4128 | tf_op jit(solution)/shard_map/ppermute | solution.py:507
  30.4 0.9 %collective-permute-done.20.rest_5_ = s32[8,128]{1,0:T(8,128)S(1)} collective-permute-done((s32[8,128]{1,0:T(8,128)S(1)}, s32[8,128]{1,0:T(8,128)S(1)}, u32[]{:S(2)}, u32[]{:S(2)}) %collective-permute-start.20) | collective-permute-done | bytes 4128 | tf_op jit(solution)/shard_map/ppermute | solution.py:507
  31.3 0.0 collective-permute-done.17.rest_0_
  31.3 0.0 collective-permute-done.18.rest_1_
  31.3 0.7 %mix_far.3 = (bf16[48,2048]{1,0:T(8,128)(2,1)S(1)}, s32[8,128]{1,0:T(8,128)S(1)}) custom-call(bf16[48,2048]{1,0:T(8,128)(2,1)S(1)} %get-tuple-element.115.x_ref, bf16[128,128]{1,0:T(8,128)(2,1)S(1)} %get-tuple-element.120.mask_ref, bf16[32,2048]{1,0:T(8,128)(2,1)S(1)} %collective-permute-done.17.rest_0_, ...), custom_call_target="tpu_custom_call" | custom-call | flops 50331648 | tf_op jit(solution)/shard_map/mix_far/pallas_call | solution.py:26
  32.0 0.5 collective-permute-start.23
  32.5 1.1 %mix_near.3 = (bf16[48,2048]{1,0:T(8,128)(2,1)S(1)}, bf16[128,2048]{1,0:T(8,128)(2,1)S(1)}) custom-call(bf16[176,2048]{1,0:T(8,128)(2,1)S(1)} %get-tuple-element.132.x_ref, bf16[176,128]{1,0:T(8,128)(2,1)S(1)} %get-tuple-element.133.mask_ref, bf16[32,2048]{1,0:T(8,128)(2,1)S(1)} %collective-permute-done.17.rest_0_, ...), custom_call_target="tpu_custom_call" | custom-call | flops 184549376 | tf_op jit(solution)/shard_map/mix_near/pallas_call | solution.py:26
  33.7 1.5 %collective-permute-start.22 = (bf16[48,2048]{1,0:T(8,128)(2,1)S(1)}, bf16[48,2048]{1,0:T(8,128)(2,1)S(1)}, u32[]{:S(2)}, u32[]{:S(2)}) collective-permute-start(bf16[48,2048]{1,0:T(8,128)(2,1)S(1)} %get-tuple-element.135), channel_id=1, source_target_pairs={{0,1},{1,0},{2,3},{3,2},{4,5},{5,4},{6,7},{7,6},{8,9},{9,8},{10,11... | collective-permute-start | bytes 589832 | tf_op jit(solution)/shard_map/ppermute | solution.py:513
  35.2 2.5 %mix_whole_late.3.rest_4_.refs_0_ = bf16[512,2048]{1,0:T(8,128)(2,1)S(1)} custom-call(bf16[512,2048]{1,0:T(8,128)(2,1)S(1)} %normalize.1.x_ref, bf16[512,128]{1,0:T(8,128)(2,1)S(1)} %get-tuple-element.116.mask_ref, bf16[32,2048]{1,0:T(8,128)(2,1)S(1)} %collective-permute-done.17.rest_0_, bf16[32,2048]{1,0:T(8,128)(2,1)S(1)} %collective-permute-done.18.rest_1_, ...), custom_call_target="tpu_custom_call" | custom-call | flops 536870912 | tf_op jit(solution)/shard_map/mix_whole_late/pallas_call | solution.py:26
  37.7 2.2 %collective-permute-done.23.far_ref = bf16[48,2048]{1,0:T(8,128)(2,1)S(1)} collective-permute-done((bf16[48,2048]{1,0:T(8,128)(2,1)S(1)}, bf16[48,2048]{1,0:T(8,128)(2,1)S(1)}, u32[]{:S(2)}, u32[]{:S(2)}) %collective-permute-start.23) | collective-permute-done | bytes 196640 | tf_op jit(solution)/shard_map/ppermute | solution.py:510
  39.8 0.0 collective-permute-done.22.core_ref
  39.8 0.4 unpack_both.3
  40.2 1.0 %collective-permute-start.24 = (bf16[32,2048]{1,0:T(8,128)(2,1)S(1)}, bf16[32,2048]{1,0:T(8,128)(2,1)S(1)}, u32[]{:S(2)}, u32[]{:S(2)}) collective-permute-start(bf16[32,2048]{1,0:T(8,128)(2,1)S(1)} %get-tuple-element.137), channel_id=1, source_target_pairs={{0,24},{8,16},{16,8},{24,0},{1,25},{9,17},{17,9},{25,1},{2,26},{10... | collective-permute-start | bytes 393224 | tf_op jit(solution)/shard_map/ppermute | solution.py:504
  41.2 1.5 %collective-permute-start.25 = (bf16[32,2048]{1,0:T(8,128)(2,1)S(1)}, bf16[32,2048]{1,0:T(8,128)(2,1)S(1)}, u32[]{:S(2)}, u32[]{:S(2)}) collective-permute-start(bf16[32,2048]{1,0:T(8,128)(2,1)S(1)} %get-tuple-element.138), channel_id=1, source_target_pairs={{0,16},{8,24},{16,0},{24,8},{1,17},{9,25},{17,1},{25,9},{2,18},{10... | collective-permute-start | bytes 393224 | tf_op jit(solution)/shard_map/ppermute | solution.py:504
  42.7 1.1 %collective-permute-start.26 = (bf16[32,2048]{1,0:T(8,128)(2,1)S(1)}, bf16[32,2048]{1,0:T(8,128)(2,1)S(1)}, u32[]{:S(2)}, u32[]{:S(2)}) collective-permute-start(bf16[32,2048]{1,0:T(8,128)(2,1)S(1)} %get-tuple-element.139), channel_id=1, source_target_pairs={{0,8},{8,0},{16,24},{24,16},{1,9},{9,1},{17,25},{25,17},{2,10},{10... | collective-permute-start | bytes 393224 | tf_op jit(solution)/shard_map/ppermute | solution.py:504
  43.8 0.5 slice.16
  45.0 0.1 mix_whole_early.3
  45.0 2.3 %collective-permute-done.24 = bf16[32,2048]{1,0:T(8,128)(2,1)S(1)} collective-permute-done((bf16[32,2048]{1,0:T(8,128)(2,1)S(1)}, bf16[32,2048]{1,0:T(8,128)(2,1)S(1)}, u32[]{:S(2)}, u32[]{:S(2)}) %collective-permute-start.24) | collective-permute-done | bytes 131104 | tf_op jit(solution)/shard_map/ppermute | solution.py:504
  47.4 2.7 %collective-permute-done.25 = bf16[32,2048]{1,0:T(8,128)(2,1)S(1)} collective-permute-done((bf16[32,2048]{1,0:T(8,128)(2,1)S(1)}, bf16[32,2048]{1,0:T(8,128)(2,1)S(1)}, u32[]{:S(2)}, u32[]{:S(2)}) %collective-permute-start.25) | collective-permute-done | bytes 131104 | tf_op jit(solution)/shard_map/ppermute | solution.py:504
  50.0 0.0 collective-permute-done.26
  50.0 3.0 %conditional.1 = (bf16[1,1,512,2048]{3,2,1,0:T(8,128)(2,1)}) conditional(s32[]{:T(128)} %bitcast.6, (bf16[512,2048]{1,0:T(8,128)(2,1)S(1)}, bf16[512,128]{1,0:T(8,128)(2,1)S(1)}, bf16[32,2048]{1,0:T(8,128)(2,1)S(1)}, bf16[32,2048]{1,0:T(8,128)(2,1)S(1)}, bf16[32,2048]{1,0:T(8,128)(2,1)S(1)}, /*index=5*/bf16[32,2048]{1,0:T(8,128)(2,1)S(1)}) %tuple.13, ...), branch_computations={%region_0.0_spmd, %region_1.0_spmd} | conditional | flops 36511809536 | bytes 88408472 | solution.py:571
  50.0 3.0 %mix.2 = bf16[512,2048]{1,0:T(8,128)(2,1)} custom-call(bf16[512,2048]{1,0:T(8,128)(2,1)S(1)} %get-tuple-element.53.x_ref, bf16[512,128]{1,0:T(8,128)(2,1)S(1)} %get-tuple-element.54.mask_ref, bf16[32,2048]{1,0:T(8,128)(2,1)S(1)} %get-tuple-element.55.rest_0_, bf16[32,2048]{1,0:T(8,128)(2,1)S(1)} %get-tuple-element.56.rest_1_, ...), custom_call_target="tpu_custom_call" | custom-call | flops 536870912 | bytes 4194304 | tf_op jit(solution)/shard_map/cond/branch_0_fun/mix/pallas_call | solution.py:26
  (1 shorter events, 0.0 us)
Async XLA Ops:
  0.0 5.5 %collective-permute-start.12 = (s32[4,32]{1,0:T(4,128)}, s32[4,32]{1,0:T(4,128)S(1)}, u32[]{:S(2)}, u32[]{:S(2)}) collective-permute-start(s32[4,32]{1,0:T(4,128)} %bitcast.12), channel_id=1, source_target_pairs={{0,8},{8,0},{16,24},{24,16},{1,9},{9,1},{17,25},{25,17},{2,10},{10... | collective-permute-start | bytes 1544 | tf_op jit(solution)/shard_map/ppermute | solution.py:504
  2.9 3.8 %collective-permute-start.11 = (s32[4,32]{1,0:T(4,128)}, s32[4,32]{1,0:T(4,128)S(1)}, u32[]{:S(2)}, u32[]{:S(2)}) collective-permute-start(s32[4,32]{1,0:T(4,128)} %bitcast.13), channel_id=1, source_target_pairs={{0,16},{8,24},{16,0},{24,8},{1,17},{9,25},{17,1},{25,9},{2,18},{10... | collective-permute-start | bytes 1544 | tf_op jit(solution)/shard_map/ppermute | solution.py:504
  4.5 4.7 %collective-permute-start.10 = (s32[4,32]{1,0:T(4,128)}, s32[4,32]{1,0:T(4,128)S(1)}, u32[]{:S(2)}, u32[]{:S(2)}) collective-permute-start(s32[4,32]{1,0:T(4,128)} %bitcast.14), channel_id=1, source_target_pairs={{0,24},{8,16},{16,8},{24,0},{1,25},{9,17},{17,9},{25,1},{2,26},{10... | collective-permute-start | bytes 1544 | tf_op jit(solution)/shard_map/ppermute | solution.py:504
  9.6 4.9 %collective-permute-start.13 = (s32[8,128]{1,0:T(8,128)S(1)}, s32[8,128]{1,0:T(8,128)S(1)}, u32[]{:S(2)}, u32[]{:S(2)}) collective-permute-start(s32[8,128]{1,0:T(8,128)S(1)} %get-tuple-element.114.refs_0_), channel_id=1, source_target_pairs={{0,7},{1,2},{2,1},{3,4},{4,3},{5,6},{6,5},{7,0},{8,15},{9,10},{10,... | collective-permute-start | bytes 12296 | tf_op jit(solution)/shard_map/ppermute | solution.py:510
  15.0 8.2 %collective-permute-start.16 = (bf16[48,2048]{1,0:T(8,128)(2,1)S(1)}, bf16[48,2048]{1,0:T(8,128)(2,1)S(1)}, u32[]{:S(2)}, u32[]{:S(2)}) collective-permute-start(bf16[48,2048]{1,0:T(8,128)(2,1)S(1)} %get-tuple-element.115.x_ref), channel_id=1, source_target_pairs={{0,7},{1,2},{2,1},{3,4},{4,3},{5,6},{6,5},{7,0},{8,15},{9,10},{10,... | collective-permute-start | bytes 589832 | tf_op jit(solution)/shard_map/ppermute | solution.py:510
  16.4 1.2 %collective-permute-start.14 = (s32[8,128]{1,0:T(8,128)S(1)}, s32[8,128]{1,0:T(8,128)S(1)}, u32[]{:S(2)}, u32[]{:S(2)}) collective-permute-start(s32[8,128]{1,0:T(8,128)S(1)} %get-tuple-element.119), channel_id=1, source_target_pairs={{0,1},{1,0},{2,3},{3,2},{4,5},{5,4},{6,7},{7,6},{8,9},{9,8},{10,11... | collective-permute-start | bytes 12296 | tf_op jit(solution)/shard_map/ppermute | solution.py:513
  18.8 4.7 %collective-permute-start.15 = (bf16[48,2048]{1,0:T(8,128)(2,1)S(1)}, bf16[48,2048]{1,0:T(8,128)(2,1)S(1)}, u32[]{:S(2)}, u32[]{:S(2)}) collective-permute-start(bf16[48,2048]{1,0:T(8,128)(2,1)S(1)} %get-tuple-element.122), channel_id=1, source_target_pairs={{0,1},{1,0},{2,3},{3,2},{4,5},{5,4},{6,7},{7,6},{8,9},{9,8},{10,11... | collective-permute-start | bytes 589832 | tf_op jit(solution)/shard_map/ppermute | solution.py:513
  23.8 7.5 %collective-permute-start.17 = (bf16[32,2048]{1,0:T(8,128)(2,1)S(1)}, bf16[32,2048]{1,0:T(8,128)(2,1)S(1)}, u32[]{:S(2)}, u32[]{:S(2)}) collective-permute-start(bf16[32,2048]{1,0:T(8,128)(2,1)S(1)} %get-tuple-element.126), channel_id=1, source_target_pairs={{0,24},{8,16},{16,8},{24,0},{1,25},{9,17},{17,9},{25,1},{2,26},{10... | collective-permute-start | bytes 393224 | tf_op jit(solution)/shard_map/ppermute | solution.py:504
  24.4 7.0 %collective-permute-start.18 = (bf16[32,2048]{1,0:T(8,128)(2,1)S(1)}, bf16[32,2048]{1,0:T(8,128)(2,1)S(1)}, u32[]{:S(2)}, u32[]{:S(2)}) collective-permute-start(bf16[32,2048]{1,0:T(8,128)(2,1)S(1)} %get-tuple-element.127), channel_id=1, source_target_pairs={{0,16},{8,24},{16,0},{24,8},{1,17},{9,25},{17,1},{25,9},{2,18},{10... | collective-permute-start | bytes 393224 | tf_op jit(solution)/shard_map/ppermute | solution.py:504
  25.9 5.4 %collective-permute-start.19 = (bf16[32,2048]{1,0:T(8,128)(2,1)S(1)}, bf16[32,2048]{1,0:T(8,128)(2,1)S(1)}, u32[]{:S(2)}, u32[]{:S(2)}) collective-permute-start(bf16[32,2048]{1,0:T(8,128)(2,1)S(1)} %get-tuple-element.128), channel_id=1, source_target_pairs={{0,8},{8,0},{16,24},{24,16},{1,9},{9,1},{17,25},{25,17},{2,10},{10... | collective-permute-start | bytes 393224 | tf_op jit(solution)/shard_map/ppermute | solution.py:504
  27.4 3.0 %collective-permute-start.21 = (s32[8,128]{1,0:T(8,128)S(1)}, s32[8,128]{1,0:T(8,128)S(1)}, u32[]{:S(2)}, u32[]{:S(2)}) collective-permute-start(s32[8,128]{1,0:T(8,128)S(1)} %get-tuple-element.130.rest_4_), channel_id=1, source_target_pairs={{0,5},{1,6},{2,7},{3,0},{4,1},{5,2},{6,3},{7,4},{8,13},{9,14},{10,... | collective-permute-start | bytes 12296 | tf_op jit(solution)/shard_map/ppermute | solution.py:507
  27.4 3.9 %collective-permute-start.20 = (s32[8,128]{1,0:T(8,128)S(1)}, s32[8,128]{1,0:T(8,128)S(1)}, u32[]{:S(2)}, u32[]{:S(2)}) collective-permute-start(s32[8,128]{1,0:T(8,128)S(1)} %get-tuple-element.130.rest_4_), channel_id=1, source_target_pairs={{0,3},{1,4},{2,5},{3,6},{4,7},{5,0},{6,1},{7,2},{8,11},{9,12},{10,... | collective-permute-start | bytes 12296 | tf_op jit(solution)/shard_map/ppermute | solution.py:507
  32.0 7.8 %collective-permute-start.23 = (bf16[48,2048]{1,0:T(8,128)(2,1)S(1)}, bf16[48,2048]{1,0:T(8,128)(2,1)S(1)}, u32[]{:S(2)}, u32[]{:S(2)}) collective-permute-start(bf16[48,2048]{1,0:T(8,128)(2,1)S(1)} %get-tuple-element.136), channel_id=1, source_target_pairs={{0,7},{1,2},{2,1},{3,4},{4,3},{5,6},{6,5},{7,0},{8,15},{9,10},{10,... | collective-permute-start | bytes 589832 | tf_op jit(solution)/shard_map/ppermute | solution.py:510
  33.7 6.2 %collective-permute-start.22 = (bf16[48,2048]{1,0:T(8,128)(2,1)S(1)}, bf16[48,2048]{1,0:T(8,128)(2,1)S(1)}, u32[]{:S(2)}, u32[]{:S(2)}) collective-permute-start(bf16[48,2048]{1,0:T(8,128)(2,1)S(1)} %get-tuple-element.135), channel_id=1, source_target_pairs={{0,1},{1,0},{2,3},{3,2},{4,5},{5,4},{6,7},{7,6},{8,9},{9,8},{10,11... | collective-permute-start | bytes 589832 | tf_op jit(solution)/shard_map/ppermute | solution.py:513
  40.2 7.2 %collective-permute-start.24 = (bf16[32,2048]{1,0:T(8,128)(2,1)S(1)}, bf16[32,2048]{1,0:T(8,128)(2,1)S(1)}, u32[]{:S(2)}, u32[]{:S(2)}) collective-permute-start(bf16[32,2048]{1,0:T(8,128)(2,1)S(1)} %get-tuple-element.137), channel_id=1, source_target_pairs={{0,24},{8,16},{16,8},{24,0},{1,25},{9,17},{17,9},{25,1},{2,26},{10... | collective-permute-start | bytes 393224 | tf_op jit(solution)/shard_map/ppermute | solution.py:504
  41.2 8.8 %collective-permute-start.25 = (bf16[32,2048]{1,0:T(8,128)(2,1)S(1)}, bf16[32,2048]{1,0:T(8,128)(2,1)S(1)}, u32[]{:S(2)}, u32[]{:S(2)}) collective-permute-start(bf16[32,2048]{1,0:T(8,128)(2,1)S(1)} %get-tuple-element.138), channel_id=1, source_target_pairs={{0,16},{8,24},{16,0},{24,8},{1,17},{9,25},{17,1},{25,9},{2,18},{10... | collective-permute-start | bytes 393224 | tf_op jit(solution)/shard_map/ppermute | solution.py:504
  42.7 7.3 %collective-permute-start.26 = (bf16[32,2048]{1,0:T(8,128)(2,1)S(1)}, bf16[32,2048]{1,0:T(8,128)(2,1)S(1)}, u32[]{:S(2)}, u32[]{:S(2)}) collective-permute-start(bf16[32,2048]{1,0:T(8,128)(2,1)S(1)} %get-tuple-element.139), channel_id=1, source_target_pairs={{0,8},{8,0},{16,24},{24,16},{1,9},{9,1},{17,25},{25,17},{2,10},{10... | collective-permute-start | bytes 393224 | tf_op jit(solution)/shard_map/ppermute | solution.py:504

commit v17 on v16

--- a/solution.py
+++ b/solution.py
@@ -562,7 +562,7 @@
     while 2 * reach + 1 < groups:
         by = 2 * reach + 1
         most = functools.reduce(jnp.maximum, mosts)
-        mosts = [most, shift(most, by), shift(most, -by)]
+        mosts = [most, shift(most, -by), shift(most, by)]
         reach += by
     y, most, last = next_round(
         x, mask, far, near, masks[0], masks[2], expands, first, mosts

time: 53.4 us -> 52.1 us (0.976)
  waiting for transfers between devices: 20 us -> 19 us
    ppermute x9, waiting for transfers between devices: 8.68 us -> 6.85 us  [turn(): return lax.ppermute(value, 'clus', [(c, c ^ d) for c in range(servers)])]
    ppermute x3, waiting for transfers between devices: 7.97 us -> 9.67 us  [across(): return lax.ppermute(value, 'rep', beyond)]
    ppermute x3, starting transfers between devices: 1.74 us -> 0.58 us  [inside(): return lax.ppermute(value, 'rep', within)]
    ppermute x2, starting transfers between devices: 1.75 us -> 2.64 us  [shift(): lax.ppermute(value, 'rep', [(g, (g + by) % groups) for g in range(groups)])]
    ppermute x2, waiting for transfers between devices: 2.19 us -> 1.33 us  [shift(): lax.ppermute(value, 'rep', [(g, (g + by) % groups) for g in range(groups)])]
where the time goes in v17:
time: 52.1 us; the launch traced here: 51.9 us
  waiting for transfers between devices  19 us (36%)
  starting transfers between devices  18.1 us (35%)
  Pallas kernels  13.4 us (26%)
  between operations  0.94 us (2%)
    pallas_call x13, Pallas kernels, kernel_call(): pl.pallas_call(kernel, out_shape=outs, scratch_shapes=scratch, compiler_p...  13.4 us
    ppermute x9, starting transfers between devices, turn(): return lax.ppermute(value, 'clus', [(c, c ^ d) for c in range(servers)])  11.6 us
    ppermute x3, waiting for transfers between devices, across(): return lax.ppermute(value, 'rep', beyond)  9.67 us
    ppermute x9, waiting for transfers between devices, turn(): return lax.ppermute(value, 'clus', [(c, c ^ d) for c in range(servers)])  6.85 us
    ppermute x3, starting transfers between devices, across(): return lax.ppermute(value, 'rep', beyond)  3.26 us
    ppermute x2, starting transfers between devices, shift(): lax.ppermute(value, 'rep', [(g, (g + by) % groups) for g in range(groups)])  2.64 us
    ppermute x2, waiting for transfers between devices, shift(): lax.ppermute(value, 'rep', [(g, (g + by) % groups) for g in range(groups)])  1.33 us
    ppermute x3, waiting for transfers between devices, inside(): return lax.ppermute(value, 'rep', within)  1.17 us
  transfers between devices with their start and end apart: 17, of which 10 were waited for; matrix products, arithmetic and copies ran while one was open for 1% of the time, Pallas kernels for 15%

profile of v17, /device:TPU:0, one launch (start us, length us, event | category | flops | bytes accessed | tf_op | source)
XLA Modules:
  0.0 51.9 jit_solution(494074831199632984)
XLA Ops:
  0.0 2.9 %collective-permute-start.12 = (s32[4,32]{1,0:T(4,128)}, s32[4,32]{1,0:T(4,128)S(1)}, u32[]{:S(2)}, u32[]{:S(2)}) collective-permute-start(s32[4,32]{1,0:T(4,128)} %bitcast.12), channel_id=1, source_target_pairs={{0,8},{8,0},{16,24},{24,16},{1,9},{9,1},{17,25},{25,17},{2,10},{10... | collective-permute-start | bytes 1544 | tf_op jit(solution)/shard_map/ppermute | solution.py:504
  2.9 1.5 %collective-permute-start.11 = (s32[4,32]{1,0:T(4,128)}, s32[4,32]{1,0:T(4,128)S(1)}, u32[]{:S(2)}, u32[]{:S(2)}) collective-permute-start(s32[4,32]{1,0:T(4,128)} %bitcast.13), channel_id=1, source_target_pairs={{0,16},{8,24},{16,0},{24,8},{1,17},{9,25},{17,1},{25,9},{2,18},{10... | collective-permute-start | bytes 1544 | tf_op jit(solution)/shard_map/ppermute | solution.py:504
  4.5 0.0 collective-permute-start.10
  4.5 1.0 %mask.1 = (bf16[512,128]{1,0:T(8,128)(2,1)S(1)}, s32[4,32]{1,0:T(4,128)S(1)}) custom-call(s32[10,1,512]{2,1,0:T(1,128)} %bitcast.11, s32[4,32]{1,0:T(4,128)} %bitcast.15), custom_call_target="tpu_custom_call" | custom-call | flops 1310720 | bytes 131072 | tf_op jit(solution)/shard_map/mask/pallas_call | solution.py:26
  5.5 0.0 collective-permute-done.12.refs_2_
  5.5 1.3 %collective-permute-done.11.refs_1_ = s32[4,32]{1,0:T(4,128)S(1)} collective-permute-done((s32[4,32]{1,0:T(4,128)}, s32[4,32]{1,0:T(4,128)S(1)}, u32[]{:S(2)}, u32[]{:S(2)}) %collective-permute-start.11) | collective-permute-done | bytes 544 | tf_op jit(solution)/shard_map/ppermute | solution.py:504
  6.7 2.4 %collective-permute-done.10.refs_0_ = s32[4,32]{1,0:T(4,128)S(1)} collective-permute-done((s32[4,32]{1,0:T(4,128)}, s32[4,32]{1,0:T(4,128)S(1)}, u32[]{:S(2)}, u32[]{:S(2)}) %collective-permute-start.10) | collective-permute-done | bytes 544 | tf_op jit(solution)/shard_map/ppermute | solution.py:504
  9.2 0.5 list.1
  9.6 1.4 %collective-permute-start.13 = (s32[8,128]{1,0:T(8,128)S(1)}, s32[8,128]{1,0:T(8,128)S(1)}, u32[]{:S(2)}, u32[]{:S(2)}) collective-permute-start(s32[8,128]{1,0:T(8,128)S(1)} %get-tuple-element.114.refs_0_), channel_id=1, source_target_pairs={{0,7},{1,2},{2,1},{3,4},{4,3},{5,6},{6,5},{7,0},{8,15},{9,10},{10,... | collective-permute-start | bytes 12296 | tf_op jit(solution)/shard_map/ppermute | solution.py:510
  11.0 1.9 %normalize.1.x_ref = bf16[512,2048]{1,0:T(8,128)(2,1)S(1)} custom-call(bf16[512,2048]{1,0:T(8,128)(2,1)} %bitcast.10), custom_call_target="tpu_custom_call" | custom-call | flops 6291456 | bytes 4194304 | tf_op jit(solution)/shard_map/normalize/pallas_call | solution.py:26
  12.9 1.6 %collective-permute-done.13.beyond_ref.refs_1_ = s32[8,128]{1,0:T(8,128)S(1)} collective-permute-done((s32[8,128]{1,0:T(8,128)S(1)}, s32[8,128]{1,0:T(8,128)S(1)}, u32[]{:S(2)}, u32[]{:S(2)}) %collective-permute-start.13) | collective-permute-done | bytes 4128 | tf_op jit(solution)/shard_map/ppermute | solution.py:510
  14.5 0.5 pack_far.1
  15.0 1.4 %collective-permute-start.16 = (bf16[48,2048]{1,0:T(8,128)(2,1)S(1)}, bf16[48,2048]{1,0:T(8,128)(2,1)S(1)}, u32[]{:S(2)}, u32[]{:S(2)}) collective-permute-start(bf16[48,2048]{1,0:T(8,128)(2,1)S(1)} %get-tuple-element.115.x_ref), channel_id=1, source_target_pairs={{0,7},{1,2},{2,1},{3,4},{4,3},{5,6},{6,5},{7,0},{8,15},{9,10},{10,... | collective-permute-start | bytes 589832 | tf_op jit(solution)/shard_map/ppermute | solution.py:510
  16.4 0.0 collective-permute-start.14
  16.4 1.2 %collective-permute-done.14.refs_2_ = s32[8,128]{1,0:T(8,128)S(1)} collective-permute-done((s32[8,128]{1,0:T(8,128)S(1)}, s32[8,128]{1,0:T(8,128)S(1)}, u32[]{:S(2)}, u32[]{:S(2)}) %collective-permute-start.14) | collective-permute-done | bytes 4128 | tf_op jit(solution)/shard_map/ppermute | solution.py:513
  17.6 1.2 %serve_near.1 = (bf16[48,2048]{1,0:T(8,128)(2,1)S(1)}, bf16[128,2048]{1,0:T(8,128)(2,1)S(1)}, bf16[176,2048]{1,0:T(8,128)(2,1)S(1)}, bf16[80,2048]{1,0:T(8,128)(...) custom-call(bf16[512,2048]{1,0:T(8,128)(2,1)S(1)} %normalize.1.x_ref, ...), custom_call_target="tpu_custom_call" | custom-call | flops 805306368 | tf_op jit(solution)/shard_map/serve_near/pallas_call | solution.py:26
  18.8 0.2 collective-permute-start.15
  19.1 4.2 %collective-permute-done.16.far_ref = bf16[48,2048]{1,0:T(8,128)(2,1)S(1)} collective-permute-done((bf16[48,2048]{1,0:T(8,128)(2,1)S(1)}, bf16[48,2048]{1,0:T(8,128)(2,1)S(1)}, u32[]{:S(2)}, u32[]{:S(2)}) %collective-permute-start.16) | collective-permute-done | bytes 196640 | tf_op jit(solution)/shard_map/ppermute | solution.py:510
  23.3 0.3 unpack.5.base_ref
  23.5 0.0 collective-permute-done.15.core_ref
  23.6 0.3 combine.1
  23.8 0.5 %collective-permute-start.17 = (bf16[32,2048]{1,0:T(8,128)(2,1)S(1)}, bf16[32,2048]{1,0:T(8,128)(2,1)S(1)}, u32[]{:S(2)}, u32[]{:S(2)}) collective-permute-start(bf16[32,2048]{1,0:T(8,128)(2,1)S(1)} %get-tuple-element.126), channel_id=1, source_target_pairs={{0,24},{8,16},{16,8},{24,0},{1,25},{9,17},{17,9},{25,1},{2,26},{10... | collective-permute-start | bytes 393224 | tf_op jit(solution)/shard_map/ppermute | solution.py:504
  24.4 1.5 %collective-permute-start.18 = (bf16[32,2048]{1,0:T(8,128)(2,1)S(1)}, bf16[32,2048]{1,0:T(8,128)(2,1)S(1)}, u32[]{:S(2)}, u32[]{:S(2)}) collective-permute-start(bf16[32,2048]{1,0:T(8,128)(2,1)S(1)} %get-tuple-element.127), channel_id=1, source_target_pairs={{0,16},{8,24},{16,0},{24,8},{1,17},{9,25},{17,1},{25,9},{2,18},{10... | collective-permute-start | bytes 393224 | tf_op jit(solution)/shard_map/ppermute | solution.py:504
  25.9 1.5 %collective-permute-start.19 = (bf16[32,2048]{1,0:T(8,128)(2,1)S(1)}, bf16[32,2048]{1,0:T(8,128)(2,1)S(1)}, u32[]{:S(2)}, u32[]{:S(2)}) collective-permute-start(bf16[32,2048]{1,0:T(8,128)(2,1)S(1)} %get-tuple-element.128), channel_id=1, source_target_pairs={{0,8},{8,0},{16,24},{24,16},{1,9},{9,1},{17,25},{25,17},{2,10},{10... | collective-permute-start | bytes 393224 | tf_op jit(solution)/shard_map/ppermute | solution.py:504
  27.4 2.6 %collective-permute-start.20 = (s32[8,128]{1,0:T(8,128)S(1)}, s32[8,128]{1,0:T(8,128)S(1)}, u32[]{:S(2)}, u32[]{:S(2)}) collective-permute-start(s32[8,128]{1,0:T(8,128)S(1)} %get-tuple-element.130.rest_4_), channel_id=1, source_target_pairs={{0,5},{1,6},{2,7},{3,0},{4,1},{5,2},{6,3},{7,4},{8,13},{9,14},{10,... | collective-permute-start | bytes 12296 | tf_op jit(solution)/shard_map/ppermute | solution.py:507
  30.0 1.3 %collective-permute-done.21.rest_6_ = s32[8,128]{1,0:T(8,128)S(1)} collective-permute-done((s32[8,128]{1,0:T(8,128)S(1)}, s32[8,128]{1,0:T(8,128)S(1)}, u32[]{:S(2)}, u32[]{:S(2)}) %collective-permute-start.21) | collective-permute-done | bytes 4128 | tf_op jit(solution)/shard_map/ppermute | solution.py:507
  31.3 0.0 collective-permute-done.20.rest_5_
  31.4 0.0 collective-permute-done.17.rest_0_
  31.4 0.0 collective-permute-done.18.rest_1_
  31.4 0.0 collective-permute-done.19.rest_2_
  31.4 0.7 %mix_far.3 = (bf16[48,2048]{1,0:T(8,128)(2,1)S(1)}, s32[8,128]{1,0:T(8,128)S(1)}) custom-call(bf16[48,2048]{1,0:T(8,128)(2,1)S(1)} %get-tuple-element.115.x_ref, bf16[128,128]{1,0:T(8,128)(2,1)S(1)} %get-tuple-element.120.mask_ref, bf16[32,2048]{1,0:T(8,128)(2,1)S(1)} %collective-permute-done.17.rest_0_, ...), custom_call_target="tpu_custom_call" | custom-call | flops 50331648 | tf_op jit(solution)/shard_map/mix_far/pallas_call | solution.py:26
  32.1 0.5 collective-permute-start.23
  32.5 1.1 %mix_near.3 = (bf16[48,2048]{1,0:T(8,128)(2,1)S(1)}, bf16[128,2048]{1,0:T(8,128)(2,1)S(1)}) custom-call(bf16[176,2048]{1,0:T(8,128)(2,1)S(1)} %get-tuple-element.132.x_ref, bf16[176,128]{1,0:T(8,128)(2,1)S(1)} %get-tuple-element.133.mask_ref, bf16[32,2048]{1,0:T(8,128)(2,1)S(1)} %collective-permute-done.17.rest_0_, ...), custom_call_target="tpu_custom_call" | custom-call | flops 184549376 | tf_op jit(solution)/shard_map/mix_near/pallas_call | solution.py:26
  33.7 0.3 collective-permute-start.22
  34.0 2.5 %mix_whole_late.3.rest_4_.refs_0_ = bf16[512,2048]{1,0:T(8,128)(2,1)S(1)} custom-call(bf16[512,2048]{1,0:T(8,128)(2,1)S(1)} %normalize.1.x_ref, bf16[512,128]{1,0:T(8,128)(2,1)S(1)} %get-tuple-element.116.mask_ref, bf16[32,2048]{1,0:T(8,128)(2,1)S(1)} %collective-permute-done.17.rest_0_, bf16[32,2048]{1,0:T(8,128)(2,1)S(1)} %collective-permute-done.18.rest_1_, ...), custom_call_target="tpu_custom_call" | custom-call | flops 536870912 | tf_op jit(solution)/shard_map/mix_whole_late/pallas_call | solution.py:26
  36.5 3.8 %collective-permute-done.23.far_ref = bf16[48,2048]{1,0:T(8,128)(2,1)S(1)} collective-permute-done((bf16[48,2048]{1,0:T(8,128)(2,1)S(1)}, bf16[48,2048]{1,0:T(8,128)(2,1)S(1)}, u32[]{:S(2)}, u32[]{:S(2)}) %collective-permute-start.23) | collective-permute-done | bytes 196640 | tf_op jit(solution)/shard_map/ppermute | solution.py:510
  40.3 0.0 collective-permute-done.22.core_ref
  40.4 0.4 unpack_both.3
  40.8 1.5 %collective-permute-start.24 = (bf16[32,2048]{1,0:T(8,128)(2,1)S(1)}, bf16[32,2048]{1,0:T(8,128)(2,1)S(1)}, u32[]{:S(2)}, u32[]{:S(2)}) collective-permute-start(bf16[32,2048]{1,0:T(8,128)(2,1)S(1)} %get-tuple-element.137), channel_id=1, source_target_pairs={{0,24},{8,16},{16,8},{24,0},{1,25},{9,17},{17,9},{25,1},{2,26},{10... | collective-permute-start | bytes 393224 | tf_op jit(solution)/shard_map/ppermute | solution.py:504
  42.3 1.5 %collective-permute-start.25 = (bf16[32,2048]{1,0:T(8,128)(2,1)S(1)}, bf16[32,2048]{1,0:T(8,128)(2,1)S(1)}, u32[]{:S(2)}, u32[]{:S(2)}) collective-permute-start(bf16[32,2048]{1,0:T(8,128)(2,1)S(1)} %get-tuple-element.138), channel_id=1, source_target_pairs={{0,16},{8,24},{16,0},{24,8},{1,17},{9,25},{17,1},{25,9},{2,18},{10... | collective-permute-start | bytes 393224 | tf_op jit(solution)/shard_map/ppermute | solution.py:504
  43.8 0.5 %collective-permute-start.26 = (bf16[32,2048]{1,0:T(8,128)(2,1)S(1)}, bf16[32,2048]{1,0:T(8,128)(2,1)S(1)}, u32[]{:S(2)}, u32[]{:S(2)}) collective-permute-start(bf16[32,2048]{1,0:T(8,128)(2,1)S(1)} %get-tuple-element.139), channel_id=1, source_target_pairs={{0,8},{8,0},{16,24},{24,16},{1,9},{9,1},{17,25},{25,17},{2,10},{10... | collective-permute-start | bytes 393224 | tf_op jit(solution)/shard_map/ppermute | solution.py:504
  44.3 0.5 slice.16
  45.5 0.1 mix_whole_early.3
  45.6 1.2 %collective-permute-done.24 = bf16[32,2048]{1,0:T(8,128)(2,1)S(1)} collective-permute-done((bf16[32,2048]{1,0:T(8,128)(2,1)S(1)}, bf16[32,2048]{1,0:T(8,128)(2,1)S(1)}, u32[]{:S(2)}, u32[]{:S(2)}) %collective-permute-start.24) | collective-permute-done | bytes 131104 | tf_op jit(solution)/shard_map/ppermute | solution.py:504
  46.8 1.3 %collective-permute-done.25 = bf16[32,2048]{1,0:T(8,128)(2,1)S(1)} collective-permute-done((bf16[32,2048]{1,0:T(8,128)(2,1)S(1)}, bf16[32,2048]{1,0:T(8,128)(2,1)S(1)}, u32[]{:S(2)}, u32[]{:S(2)}) %collective-permute-start.25) | collective-permute-done | bytes 131104 | tf_op jit(solution)/shard_map/ppermute | solution.py:504
  48.1 0.6 %collective-permute-done.26 = bf16[32,2048]{1,0:T(8,128)(2,1)S(1)} collective-permute-done((bf16[32,2048]{1,0:T(8,128)(2,1)S(1)}, bf16[32,2048]{1,0:T(8,128)(2,1)S(1)}, u32[]{:S(2)}, u32[]{:S(2)}) %collective-permute-start.26) | collective-permute-done | bytes 131104 | tf_op jit(solution)/shard_map/ppermute | solution.py:504
  48.7 3.0 %conditional.1 = (bf16[1,1,512,2048]{3,2,1,0:T(8,128)(2,1)}) conditional(s32[]{:T(128)} %bitcast.6, (bf16[512,2048]{1,0:T(8,128)(2,1)S(1)}, bf16[512,128]{1,0:T(8,128)(2,1)S(1)}, bf16[32,2048]{1,0:T(8,128)(2,1)S(1)}, bf16[32,2048]{1,0:T(8,128)(2,1)S(1)}, bf16[32,2048]{1,0:T(8,128)(2,1)S(1)}, /*index=5*/bf16[32,2048]{1,0:T(8,128)(2,1)S(1)}) %tuple.13, ...), branch_computations={%region_0.0_spmd, %region_1.0_spmd} | conditional | flops 36511809536 | bytes 88408472 | solution.py:571
  48.7 3.0 %mix.2 = bf16[512,2048]{1,0:T(8,128)(2,1)} custom-call(bf16[512,2048]{1,0:T(8,128)(2,1)S(1)} %get-tuple-element.53.x_ref, bf16[512,128]{1,0:T(8,128)(2,1)S(1)} %get-tuple-element.54.mask_ref, bf16[32,2048]{1,0:T(8,128)(2,1)S(1)} %get-tuple-element.55.rest_0_, bf16[32,2048]{1,0:T(8,128)(2,1)S(1)} %get-tuple-element.56.rest_1_, ...), custom_call_target="tpu_custom_call" | custom-call | flops 536870912 | bytes 4194304 | tf_op jit(solution)/shard_map/cond/branch_0_fun/mix/pallas_call | solution.py:26
  (1 shorter events, 0.0 us)
Async XLA Ops:
  0.0 5.5 %collective-permute-start.12 = (s32[4,32]{1,0:T(4,128)}, s32[4,32]{1,0:T(4,128)S(1)}, u32[]{:S(2)}, u32[]{:S(2)}) collective-permute-start(s32[4,32]{1,0:T(4,128)} %bitcast.12), channel_id=1, source_target_pairs={{0,8},{8,0},{16,24},{24,16},{1,9},{9,1},{17,25},{25,17},{2,10},{10... | collective-permute-start | bytes 1544 | tf_op jit(solution)/shard_map/ppermute | solution.py:504
  2.9 3.8 %collective-permute-start.11 = (s32[4,32]{1,0:T(4,128)}, s32[4,32]{1,0:T(4,128)S(1)}, u32[]{:S(2)}, u32[]{:S(2)}) collective-permute-start(s32[4,32]{1,0:T(4,128)} %bitcast.13), channel_id=1, source_target_pairs={{0,16},{8,24},{16,0},{24,8},{1,17},{9,25},{17,1},{25,9},{2,18},{10... | collective-permute-start | bytes 1544 | tf_op jit(solution)/shard_map/ppermute | solution.py:504
  4.5 4.7 %collective-permute-start.10 = (s32[4,32]{1,0:T(4,128)}, s32[4,32]{1,0:T(4,128)S(1)}, u32[]{:S(2)}, u32[]{:S(2)}) collective-permute-start(s32[4,32]{1,0:T(4,128)} %bitcast.14), channel_id=1, source_target_pairs={{0,24},{8,16},{16,8},{24,0},{1,25},{9,17},{17,9},{25,1},{2,26},{10... | collective-permute-start | bytes 1544 | tf_op jit(solution)/shard_map/ppermute | solution.py:504
  9.6 4.9 %collective-permute-start.13 = (s32[8,128]{1,0:T(8,128)S(1)}, s32[8,128]{1,0:T(8,128)S(1)}, u32[]{:S(2)}, u32[]{:S(2)}) collective-permute-start(s32[8,128]{1,0:T(8,128)S(1)} %get-tuple-element.114.refs_0_), channel_id=1, source_target_pairs={{0,7},{1,2},{2,1},{3,4},{4,3},{5,6},{6,5},{7,0},{8,15},{9,10},{10,... | collective-permute-start | bytes 12296 | tf_op jit(solution)/shard_map/ppermute | solution.py:510
  15.0 8.2 %collective-permute-start.16 = (bf16[48,2048]{1,0:T(8,128)(2,1)S(1)}, bf16[48,2048]{1,0:T(8,128)(2,1)S(1)}, u32[]{:S(2)}, u32[]{:S(2)}) collective-permute-start(bf16[48,2048]{1,0:T(8,128)(2,1)S(1)} %get-tuple-element.115.x_ref), channel_id=1, source_target_pairs={{0,7},{1,2},{2,1},{3,4},{4,3},{5,6},{6,5},{7,0},{8,15},{9,10},{10,... | collective-permute-start | bytes 589832 | tf_op jit(solution)/shard_map/ppermute | solution.py:510
  16.4 1.2 %collective-permute-start.14 = (s32[8,128]{1,0:T(8,128)S(1)}, s32[8,128]{1,0:T(8,128)S(1)}, u32[]{:S(2)}, u32[]{:S(2)}) collective-permute-start(s32[8,128]{1,0:T(8,128)S(1)} %get-tuple-element.119), channel_id=1, source_target_pairs={{0,1},{1,0},{2,3},{3,2},{4,5},{5,4},{6,7},{7,6},{8,9},{9,8},{10,11... | collective-permute-start | bytes 12296 | tf_op jit(solution)/shard_map/ppermute | solution.py:513
  18.8 4.7 %collective-permute-start.15 = (bf16[48,2048]{1,0:T(8,128)(2,1)S(1)}, bf16[48,2048]{1,0:T(8,128)(2,1)S(1)}, u32[]{:S(2)}, u32[]{:S(2)}) collective-permute-start(bf16[48,2048]{1,0:T(8,128)(2,1)S(1)} %get-tuple-element.122), channel_id=1, source_target_pairs={{0,1},{1,0},{2,3},{3,2},{4,5},{5,4},{6,7},{7,6},{8,9},{9,8},{10,11... | collective-permute-start | bytes 589832 | tf_op jit(solution)/shard_map/ppermute | solution.py:513
  23.8 7.5 %collective-permute-start.17 = (bf16[32,2048]{1,0:T(8,128)(2,1)S(1)}, bf16[32,2048]{1,0:T(8,128)(2,1)S(1)}, u32[]{:S(2)}, u32[]{:S(2)}) collective-permute-start(bf16[32,2048]{1,0:T(8,128)(2,1)S(1)} %get-tuple-element.126), channel_id=1, source_target_pairs={{0,24},{8,16},{16,8},{24,0},{1,25},{9,17},{17,9},{25,1},{2,26},{10... | collective-permute-start | bytes 393224 | tf_op jit(solution)/shard_map/ppermute | solution.py:504
  24.4 7.0 %collective-permute-start.18 = (bf16[32,2048]{1,0:T(8,128)(2,1)S(1)}, bf16[32,2048]{1,0:T(8,128)(2,1)S(1)}, u32[]{:S(2)}, u32[]{:S(2)}) collective-permute-start(bf16[32,2048]{1,0:T(8,128)(2,1)S(1)} %get-tuple-element.127), channel_id=1, source_target_pairs={{0,16},{8,24},{16,0},{24,8},{1,17},{9,25},{17,1},{25,9},{2,18},{10... | collective-permute-start | bytes 393224 | tf_op jit(solution)/shard_map/ppermute | solution.py:504
  25.9 5.5 %collective-permute-start.19 = (bf16[32,2048]{1,0:T(8,128)(2,1)S(1)}, bf16[32,2048]{1,0:T(8,128)(2,1)S(1)}, u32[]{:S(2)}, u32[]{:S(2)}) collective-permute-start(bf16[32,2048]{1,0:T(8,128)(2,1)S(1)} %get-tuple-element.128), channel_id=1, source_target_pairs={{0,8},{8,0},{16,24},{24,16},{1,9},{9,1},{17,25},{25,17},{2,10},{10... | collective-permute-start | bytes 393224 | tf_op jit(solution)/shard_map/ppermute | solution.py:504
  27.4 3.9 %collective-permute-start.21 = (s32[8,128]{1,0:T(8,128)S(1)}, s32[8,128]{1,0:T(8,128)S(1)}, u32[]{:S(2)}, u32[]{:S(2)}) collective-permute-start(s32[8,128]{1,0:T(8,128)S(1)} %get-tuple-element.130.rest_4_), channel_id=1, source_target_pairs={{0,3},{1,4},{2,5},{3,6},{4,7},{5,0},{6,1},{7,2},{8,11},{9,12},{10,... | collective-permute-start | bytes 12296 | tf_op jit(solution)/shard_map/ppermute | solution.py:507
  27.4 4.0 %collective-permute-start.20 = (s32[8,128]{1,0:T(8,128)S(1)}, s32[8,128]{1,0:T(8,128)S(1)}, u32[]{:S(2)}, u32[]{:S(2)}) collective-permute-start(s32[8,128]{1,0:T(8,128)S(1)} %get-tuple-element.130.rest_4_), channel_id=1, source_target_pairs={{0,5},{1,6},{2,7},{3,0},{4,1},{5,2},{6,3},{7,4},{8,13},{9,14},{10,... | collective-permute-start | bytes 12296 | tf_op jit(solution)/shard_map/ppermute | solution.py:507
  32.1 8.3 %collective-permute-start.23 = (bf16[48,2048]{1,0:T(8,128)(2,1)S(1)}, bf16[48,2048]{1,0:T(8,128)(2,1)S(1)}, u32[]{:S(2)}, u32[]{:S(2)}) collective-permute-start(bf16[48,2048]{1,0:T(8,128)(2,1)S(1)} %get-tuple-element.136), channel_id=1, source_target_pairs={{0,7},{1,2},{2,1},{3,4},{4,3},{5,6},{6,5},{7,0},{8,15},{9,10},{10,... | collective-permute-start | bytes 589832 | tf_op jit(solution)/shard_map/ppermute | solution.py:510
  33.7 6.7 %collective-permute-start.22 = (bf16[48,2048]{1,0:T(8,128)(2,1)S(1)}, bf16[48,2048]{1,0:T(8,128)(2,1)S(1)}, u32[]{:S(2)}, u32[]{:S(2)}) collective-permute-start(bf16[48,2048]{1,0:T(8,128)(2,1)S(1)} %get-tuple-element.135), channel_id=1, source_target_pairs={{0,1},{1,0},{2,3},{3,2},{4,5},{5,4},{6,7},{7,6},{8,9},{9,8},{10,11... | collective-permute-start | bytes 589832 | tf_op jit(solution)/shard_map/ppermute | solution.py:513
  40.8 6.0 %collective-permute-start.24 = (bf16[32,2048]{1,0:T(8,128)(2,1)S(1)}, bf16[32,2048]{1,0:T(8,128)(2,1)S(1)}, u32[]{:S(2)}, u32[]{:S(2)}) collective-permute-start(bf16[32,2048]{1,0:T(8,128)(2,1)S(1)} %get-tuple-element.137), channel_id=1, source_target_pairs={{0,24},{8,16},{16,8},{24,0},{1,25},{9,17},{17,9},{25,1},{2,26},{10... | collective-permute-start | bytes 393224 | tf_op jit(solution)/shard_map/ppermute | solution.py:504
  42.3 5.8 %collective-permute-start.25 = (bf16[32,2048]{1,0:T(8,128)(2,1)S(1)}, bf16[32,2048]{1,0:T(8,128)(2,1)S(1)}, u32[]{:S(2)}, u32[]{:S(2)}) collective-permute-start(bf16[32,2048]{1,0:T(8,128)(2,1)S(1)} %get-tuple-element.138), channel_id=1, source_target_pairs={{0,16},{8,24},{16,0},{24,8},{1,17},{9,25},{17,1},{25,9},{2,18},{10... | collective-permute-start | bytes 393224 | tf_op jit(solution)/shard_map/ppermute | solution.py:504
  43.8 5.0 %collective-permute-start.26 = (bf16[32,2048]{1,0:T(8,128)(2,1)S(1)}, bf16[32,2048]{1,0:T(8,128)(2,1)S(1)}, u32[]{:S(2)}, u32[]{:S(2)}) collective-permute-start(bf16[32,2048]{1,0:T(8,128)(2,1)S(1)} %get-tuple-element.139), channel_id=1, source_target_pairs={{0,8},{8,0},{16,24},{24,16},{1,9},{9,1},{17,25},{25,17},{2,10},{10... | collective-permute-start | bytes 393224 | tf_op jit(solution)/shard_map/ppermute | solution.py:504

commit v18 on v17

--- a/solution.py
+++ b/solution.py
@@ -105,7 +105,7 @@
 
 
 def list_kernel(rows, *refs):
-    parts, refs = refs[-6::-1], refs[-5:]
+    parts, refs = refs[:-5], refs[-5:]
     own_ref, far_ref, core_ref, expand_far_ref, expand_core_ref = refs
     total = own_ref.shape[1]
     lane = lax.broadcasted_iota(jnp.int32, (total, total), 1)
@@ -146,7 +146,7 @@
         "list",
         functools.partial(list_kernel, rows),
         [int32(8, total)] * 3 + [bf16(total, total)] * 2,
-        *reversed(parts),
+        *parts,
         flops=40 * total * total,
     )
 

time: 52.1 us -> 51.1 us (0.981)
  waiting for transfers between devices: 19 us -> 16.8 us
  starting transfers between devices: 18.1 us -> 19.2 us
    ppermute x3, starting transfers between devices: 3.26 us -> 4.72 us  [across(): return lax.ppermute(value, 'rep', beyond)]
    ppermute x3, waiting for transfers between devices: 9.67 us -> 8.47 us  [across(): return lax.ppermute(value, 'rep', beyond)]
    ppermute x9, waiting for transfers between devices: 6.85 us -> 5.88 us  [turn(): return lax.ppermute(value, 'clus', [(c, c ^ d) for c in range(servers)])]
  transfers between devices with their start and end apart: 17 -> 17, of which waited for: 10 -> 11; matrix products, arithmetic and copies ran while one was open for 1% -> 1% of each run, Pallas kernels for 15% -> 16%
where the time goes in v18:
time: 51.1 us; the launch traced here: 50.9 us
  starting transfers between devices  19.2 us (38%)
  waiting for transfers between devices  16.8 us (33%)
  Pallas kernels  13.4 us (26%)
  between operations  0.94 us (2%)
    pallas_call x13, Pallas kernels, kernel_call(): pl.pallas_call(kernel, out_shape=outs, scratch_shapes=scratch, compiler_p...  13.4 us
    ppermute x9, starting transfers between devices, turn(): return lax.ppermute(value, 'clus', [(c, c ^ d) for c in range(servers)])  11.6 us
    ppermute x3, waiting for transfers between devices, across(): return lax.ppermute(value, 'rep', beyond)  8.47 us
    ppermute x9, waiting for transfers between devices, turn(): return lax.ppermute(value, 'clus', [(c, c ^ d) for c in range(servers)])  5.88 us
    ppermute x3, starting transfers between devices, across(): return lax.ppermute(value, 'rep', beyond)  4.72 us
    ppermute x2, starting transfers between devices, shift(): lax.ppermute(value, 'rep', [(g, (g + by) % groups) for g in range(groups)])  2.64 us
    ppermute x2, waiting for transfers between devices, shift(): lax.ppermute(value, 'rep', [(g, (g + by) % groups) for g in range(groups)])  1.33 us
    ppermute x3, waiting for transfers between devices, inside(): return lax.ppermute(value, 'rep', within)  1.17 us
  transfers between devices with their start and end apart: 17, of which 11 were waited for; matrix products, arithmetic and copies ran while one was open for 1% of the time, Pallas kernels for 16%

profile of v18, /device:TPU:0, one launch (start us, length us, event | category | flops | bytes accessed | tf_op | source)
XLA Modules:
  0.0 50.9 jit_solution(13022664389169679900)
XLA Ops:
  0.0 3.9 %collective-permute-start.12 = (s32[4,32]{1,0:T(4,128)}, s32[4,32]{1,0:T(4,128)S(1)}, u32[]{:S(2)}, u32[]{:S(2)}) collective-permute-start(s32[4,32]{1,0:T(4,128)} %bitcast.12), channel_id=1, source_target_pairs={{0,24},{8,16},{16,8},{24,0},{1,25},{9,17},{17,9},{25,1},{2,26},{10... | collective-permute-start | bytes 1544 | tf_op jit(solution)/shard_map/ppermute | solution.py:504
  3.9 0.5 collective-permute-start.11
  4.4 0.1 collective-permute-start.10
  4.5 1.0 %mask.1 = (bf16[512,128]{1,0:T(8,128)(2,1)S(1)}, s32[4,32]{1,0:T(4,128)S(1)}) custom-call(s32[10,1,512]{2,1,0:T(1,128)} %bitcast.11, s32[4,32]{1,0:T(4,128)} %bitcast.15), custom_call_target="tpu_custom_call" | custom-call | flops 1310720 | bytes 131072 | tf_op jit(solution)/shard_map/mask/pallas_call | solution.py:26
  5.5 0.2 collective-permute-done.12.refs_3_
  5.7 2.0 %collective-permute-done.11.refs_2_ = s32[4,32]{1,0:T(4,128)S(1)} collective-permute-done((s32[4,32]{1,0:T(4,128)}, s32[4,32]{1,0:T(4,128)S(1)}, u32[]{:S(2)}, u32[]{:S(2)}) %collective-permute-start.11) | collective-permute-done | bytes 544 | tf_op jit(solution)/shard_map/ppermute | solution.py:504
  7.7 0.5 collective-permute-done.10.refs_1_
  8.2 0.5 list.1
  8.7 1.4 %collective-permute-start.13 = (s32[8,128]{1,0:T(8,128)S(1)}, s32[8,128]{1,0:T(8,128)S(1)}, u32[]{:S(2)}, u32[]{:S(2)}) collective-permute-start(s32[8,128]{1,0:T(8,128)S(1)} %get-tuple-element.114.refs_0_), channel_id=1, source_target_pairs={{0,7},{1,2},{2,1},{3,4},{4,3},{5,6},{6,5},{7,0},{8,15},{9,10},{10,... | collective-permute-start | bytes 12296 | tf_op jit(solution)/shard_map/ppermute | solution.py:510
  10.1 1.9 %normalize.1.x_ref = bf16[512,2048]{1,0:T(8,128)(2,1)S(1)} custom-call(bf16[512,2048]{1,0:T(8,128)(2,1)} %bitcast.10), custom_call_target="tpu_custom_call" | custom-call | flops 6291456 | bytes 4194304 | tf_op jit(solution)/shard_map/normalize/pallas_call | solution.py:26
  11.9 1.6 %collective-permute-done.13.beyond_ref.refs_1_ = s32[8,128]{1,0:T(8,128)S(1)} collective-permute-done((s32[8,128]{1,0:T(8,128)S(1)}, s32[8,128]{1,0:T(8,128)S(1)}, u32[]{:S(2)}, u32[]{:S(2)}) %collective-permute-start.13) | collective-permute-done | bytes 4128 | tf_op jit(solution)/shard_map/ppermute | solution.py:510
  13.6 0.5 %pack_far.1 = (bf16[128,512]{1,0:T(8,128)(2,1)S(1)}, bf16[48,2048]{1,0:T(8,128)(2,1)S(1)}) custom-call(bf16[512,2048]{1,0:T(8,128)(2,1)S(1)} %normalize.1.x_ref, s32[8,128]{1,0:T(8,128)S(1)} %collective-permute-done.13.beyond_ref.refs_1_), custom_call_target="tpu_custom_call" | custom-call | flops 100663296 | tf_op jit(solution)/shard_map/pack_far/pallas_call | solution.py:26
  14.1 1.4 %collective-permute-start.16 = (bf16[48,2048]{1,0:T(8,128)(2,1)S(1)}, bf16[48,2048]{1,0:T(8,128)(2,1)S(1)}, u32[]{:S(2)}, u32[]{:S(2)}) collective-permute-start(bf16[48,2048]{1,0:T(8,128)(2,1)S(1)} %get-tuple-element.115.x_ref), channel_id=1, source_target_pairs={{0,7},{1,2},{2,1},{3,4},{4,3},{5,6},{6,5},{7,0},{8,15},{9,10},{10,... | collective-permute-start | bytes 589832 | tf_op jit(solution)/shard_map/ppermute | solution.py:510
  15.5 0.0 collective-permute-start.14
  15.5 1.2 %collective-permute-done.14.refs_2_ = s32[8,128]{1,0:T(8,128)S(1)} collective-permute-done((s32[8,128]{1,0:T(8,128)S(1)}, s32[8,128]{1,0:T(8,128)S(1)}, u32[]{:S(2)}, u32[]{:S(2)}) %collective-permute-start.14) | collective-permute-done | bytes 4128 | tf_op jit(solution)/shard_map/ppermute | solution.py:513
  16.7 1.2 %serve_near.1 = (bf16[48,2048]{1,0:T(8,128)(2,1)S(1)}, bf16[128,2048]{1,0:T(8,128)(2,1)S(1)}, bf16[176,2048]{1,0:T(8,128)(2,1)S(1)}, bf16[80,2048]{1,0:T(8,128)(...) custom-call(bf16[512,2048]{1,0:T(8,128)(2,1)S(1)} %normalize.1.x_ref, ...), custom_call_target="tpu_custom_call" | custom-call | flops 805306368 | tf_op jit(solution)/shard_map/serve_near/pallas_call | solution.py:26
  17.9 0.2 collective-permute-start.15
  18.1 4.2 %collective-permute-done.16.far_ref = bf16[48,2048]{1,0:T(8,128)(2,1)S(1)} collective-permute-done((bf16[48,2048]{1,0:T(8,128)(2,1)S(1)}, bf16[48,2048]{1,0:T(8,128)(2,1)S(1)}, u32[]{:S(2)}, u32[]{:S(2)}) %collective-permute-start.16) | collective-permute-done | bytes 196640 | tf_op jit(solution)/shard_map/ppermute | solution.py:510
  22.3 0.3 unpack.5.base_ref
  22.6 0.0 collective-permute-done.15.core_ref
  22.6 0.3 combine.1
  22.9 1.5 %collective-permute-start.17 = (bf16[32,2048]{1,0:T(8,128)(2,1)S(1)}, bf16[32,2048]{1,0:T(8,128)(2,1)S(1)}, u32[]{:S(2)}, u32[]{:S(2)}) collective-permute-start(bf16[32,2048]{1,0:T(8,128)(2,1)S(1)} %get-tuple-element.126), channel_id=1, source_target_pairs={{0,24},{8,16},{16,8},{24,0},{1,25},{9,17},{17,9},{25,1},{2,26},{10... | collective-permute-start | bytes 393224 | tf_op jit(solution)/shard_map/ppermute | solution.py:504
  24.4 0.5 %collective-permute-start.18 = (bf16[32,2048]{1,0:T(8,128)(2,1)S(1)}, bf16[32,2048]{1,0:T(8,128)(2,1)S(1)}, u32[]{:S(2)}, u32[]{:S(2)}) collective-permute-start(bf16[32,2048]{1,0:T(8,128)(2,1)S(1)} %get-tuple-element.127), channel_id=1, source_target_pairs={{0,16},{8,24},{16,0},{24,8},{1,17},{9,25},{17,1},{25,9},{2,18},{10... | collective-permute-start | bytes 393224 | tf_op jit(solution)/shard_map/ppermute | solution.py:504
  25.0 1.5 %collective-permute-start.19 = (bf16[32,2048]{1,0:T(8,128)(2,1)S(1)}, bf16[32,2048]{1,0:T(8,128)(2,1)S(1)}, u32[]{:S(2)}, u32[]{:S(2)}) collective-permute-start(bf16[32,2048]{1,0:T(8,128)(2,1)S(1)} %get-tuple-element.128), channel_id=1, source_target_pairs={{0,8},{8,0},{16,24},{24,16},{1,9},{9,1},{17,25},{25,17},{2,10},{10... | collective-permute-start | bytes 393224 | tf_op jit(solution)/shard_map/ppermute | solution.py:504
  26.4 0.0 collective-permute-start.21
  26.4 2.6 %collective-permute-start.20 = (s32[8,128]{1,0:T(8,128)S(1)}, s32[8,128]{1,0:T(8,128)S(1)}, u32[]{:S(2)}, u32[]{:S(2)}) collective-permute-start(s32[8,128]{1,0:T(8,128)S(1)} %get-tuple-element.130.rest_4_), channel_id=1, source_target_pairs={{0,5},{1,6},{2,7},{3,0},{4,1},{5,2},{6,3},{7,4},{8,13},{9,14},{10,... | collective-permute-start | bytes 12296 | tf_op jit(solution)/shard_map/ppermute | solution.py:507
  29.1 1.3 %collective-permute-done.21.rest_6_ = s32[8,128]{1,0:T(8,128)S(1)} collective-permute-done((s32[8,128]{1,0:T(8,128)S(1)}, s32[8,128]{1,0:T(8,128)S(1)}, u32[]{:S(2)}, u32[]{:S(2)}) %collective-permute-start.21) | collective-permute-done | bytes 4128 | tf_op jit(solution)/shard_map/ppermute | solution.py:507
  30.4 0.0 collective-permute-done.20.rest_5_
  30.4 0.0 collective-permute-done.17.rest_0_
  30.4 0.0 collective-permute-done.18.rest_1_
  30.4 0.0 collective-permute-done.19.rest_2_
  30.4 0.7 %mix_far.3 = (bf16[48,2048]{1,0:T(8,128)(2,1)S(1)}, s32[8,128]{1,0:T(8,128)S(1)}) custom-call(bf16[48,2048]{1,0:T(8,128)(2,1)S(1)} %get-tuple-element.115.x_ref, bf16[128,128]{1,0:T(8,128)(2,1)S(1)} %get-tuple-element.120.mask_ref, bf16[32,2048]{1,0:T(8,128)(2,1)S(1)} %collective-permute-done.17.rest_0_, ...), custom_call_target="tpu_custom_call" | custom-call | flops 50331648 | tf_op jit(solution)/shard_map/mix_far/pallas_call | solution.py:26
  31.1 1.9 %collective-permute-start.23 = (bf16[48,2048]{1,0:T(8,128)(2,1)S(1)}, bf16[48,2048]{1,0:T(8,128)(2,1)S(1)}, u32[]{:S(2)}, u32[]{:S(2)}) collective-permute-start(bf16[48,2048]{1,0:T(8,128)(2,1)S(1)} %get-tuple-element.136), channel_id=1, source_target_pairs={{0,7},{1,2},{2,1},{3,4},{4,3},{5,6},{6,5},{7,0},{8,15},{9,10},{10,... | collective-permute-start | bytes 589832 | tf_op jit(solution)/shard_map/ppermute | solution.py:510
  33.0 1.1 %mix_near.3 = (bf16[48,2048]{1,0:T(8,128)(2,1)S(1)}, bf16[128,2048]{1,0:T(8,128)(2,1)S(1)}) custom-call(bf16[176,2048]{1,0:T(8,128)(2,1)S(1)} %get-tuple-element.132.x_ref, bf16[176,128]{1,0:T(8,128)(2,1)S(1)} %get-tuple-element.133.mask_ref, bf16[32,2048]{1,0:T(8,128)(2,1)S(1)} %collective-permute-done.17.rest_0_, ...), custom_call_target="tpu_custom_call" | custom-call | flops 184549376 | tf_op jit(solution)/shard_map/mix_near/pallas_call | solution.py:26
  34.2 0.1 collective-permute-start.22
  34.2 2.5 %mix_whole_late.3.rest_4_.refs_0_ = bf16[512,2048]{1,0:T(8,128)(2,1)S(1)} custom-call(bf16[512,2048]{1,0:T(8,128)(2,1)S(1)} %normalize.1.x_ref, bf16[512,128]{1,0:T(8,128)(2,1)S(1)} %get-tuple-element.116.mask_ref, bf16[32,2048]{1,0:T(8,128)(2,1)S(1)} %collective-permute-done.17.rest_0_, bf16[32,2048]{1,0:T(8,128)(2,1)S(1)} %collective-permute-done.18.rest_1_, ...), custom_call_target="tpu_custom_call" | custom-call | flops 536870912 | tf_op jit(solution)/shard_map/mix_whole_late/pallas_call | solution.py:26
  36.8 2.6 %collective-permute-done.23.far_ref = bf16[48,2048]{1,0:T(8,128)(2,1)S(1)} collective-permute-done((bf16[48,2048]{1,0:T(8,128)(2,1)S(1)}, bf16[48,2048]{1,0:T(8,128)(2,1)S(1)}, u32[]{:S(2)}, u32[]{:S(2)}) %collective-permute-start.23) | collective-permute-done | bytes 196640 | tf_op jit(solution)/shard_map/ppermute | solution.py:510
  39.4 0.4 unpack_both.3
  39.8 2.5 %collective-permute-start.24 = (bf16[32,2048]{1,0:T(8,128)(2,1)S(1)}, bf16[32,2048]{1,0:T(8,128)(2,1)S(1)}, u32[]{:S(2)}, u32[]{:S(2)}) collective-permute-start(bf16[32,2048]{1,0:T(8,128)(2,1)S(1)} %get-tuple-element.137), channel_id=1, source_target_pairs={{0,24},{8,16},{16,8},{24,0},{1,25},{9,17},{17,9},{25,1},{2,26},{10... | collective-permute-start | bytes 393224 | tf_op jit(solution)/shard_map/ppermute | solution.py:504
  42.3 0.5 collective-permute-start.25
  42.8 0.6 %collective-permute-start.26 = (bf16[32,2048]{1,0:T(8,128)(2,1)S(1)}, bf16[32,2048]{1,0:T(8,128)(2,1)S(1)}, u32[]{:S(2)}, u32[]{:S(2)}) collective-permute-start(bf16[32,2048]{1,0:T(8,128)(2,1)S(1)} %get-tuple-element.139), channel_id=1, source_target_pairs={{0,8},{8,0},{16,24},{24,16},{1,9},{9,1},{17,25},{25,17},{2,10},{10... | collective-permute-start | bytes 393224 | tf_op jit(solution)/shard_map/ppermute | solution.py:504
  43.4 0.5 %slice.16 = s32[1,1]{1,0:T(1,128)} slice(s32[8,128]{1,0:T(8,128)S(1)} %get-tuple-element.131), slice={[0:1], [0:1]} | slice | bytes 8 | tf_op jit(solution)/shard_map/slice | solution.py:571
  44.5 0.1 mix_whole_early.3
  44.6 1.1 %collective-permute-done.24 = bf16[32,2048]{1,0:T(8,128)(2,1)S(1)} collective-permute-done((bf16[32,2048]{1,0:T(8,128)(2,1)S(1)}, bf16[32,2048]{1,0:T(8,128)(2,1)S(1)}, u32[]{:S(2)}, u32[]{:S(2)}) %collective-permute-start.24) | collective-permute-done | bytes 131104 | tf_op jit(solution)/shard_map/ppermute | solution.py:504
  45.7 1.5 %collective-permute-done.25 = bf16[32,2048]{1,0:T(8,128)(2,1)S(1)} collective-permute-done((bf16[32,2048]{1,0:T(8,128)(2,1)S(1)}, bf16[32,2048]{1,0:T(8,128)(2,1)S(1)}, u32[]{:S(2)}, u32[]{:S(2)}) %collective-permute-start.25) | collective-permute-done | bytes 131104 | tf_op jit(solution)/shard_map/ppermute | solution.py:504
  47.3 0.5 collective-permute-done.26
  47.8 3.0 %conditional.1 = (bf16[1,1,512,2048]{3,2,1,0:T(8,128)(2,1)}) conditional(s32[]{:T(128)} %bitcast.6, (bf16[512,2048]{1,0:T(8,128)(2,1)S(1)}, bf16[512,128]{1,0:T(8,128)(2,1)S(1)}, bf16[32,2048]{1,0:T(8,128)(2,1)S(1)}, bf16[32,2048]{1,0:T(8,128)(2,1)S(1)}, bf16[32,2048]{1,0:T(8,128)(2,1)S(1)}, /*index=5*/bf16[32,2048]{1,0:T(8,128)(2,1)S(1)}) %tuple.13, ...), branch_computations={%region_0.0_spmd, %region_1.0_spmd} | conditional | flops 36511809536 | bytes 88408472 | solution.py:571
  47.8 3.0 %mix.2 = bf16[512,2048]{1,0:T(8,128)(2,1)} custom-call(bf16[512,2048]{1,0:T(8,128)(2,1)S(1)} %get-tuple-element.53.x_ref, bf16[512,128]{1,0:T(8,128)(2,1)S(1)} %get-tuple-element.54.mask_ref, bf16[32,2048]{1,0:T(8,128)(2,1)S(1)} %get-tuple-element.55.rest_0_, bf16[32,2048]{1,0:T(8,128)(2,1)S(1)} %get-tuple-element.56.rest_1_, ...), custom_call_target="tpu_custom_call" | custom-call | flops 536870912 | bytes 4194304 | tf_op jit(solution)/shard_map/cond/branch_0_fun/mix/pallas_call | solution.py:26
  (1 shorter events, 0.0 us)
Async XLA Ops:
  0.0 5.7 %collective-permute-start.12 = (s32[4,32]{1,0:T(4,128)}, s32[4,32]{1,0:T(4,128)S(1)}, u32[]{:S(2)}, u32[]{:S(2)}) collective-permute-start(s32[4,32]{1,0:T(4,128)} %bitcast.12), channel_id=1, source_target_pairs={{0,24},{8,16},{16,8},{24,0},{1,25},{9,17},{17,9},{25,1},{2,26},{10... | collective-permute-start | bytes 1544 | tf_op jit(solution)/shard_map/ppermute | solution.py:504
  3.9 3.8 %collective-permute-start.11 = (s32[4,32]{1,0:T(4,128)}, s32[4,32]{1,0:T(4,128)S(1)}, u32[]{:S(2)}, u32[]{:S(2)}) collective-permute-start(s32[4,32]{1,0:T(4,128)} %bitcast.13), channel_id=1, source_target_pairs={{0,16},{8,24},{16,0},{24,8},{1,17},{9,25},{17,1},{25,9},{2,18},{10... | collective-permute-start | bytes 1544 | tf_op jit(solution)/shard_map/ppermute | solution.py:504
  4.4 3.8 %collective-permute-start.10 = (s32[4,32]{1,0:T(4,128)}, s32[4,32]{1,0:T(4,128)S(1)}, u32[]{:S(2)}, u32[]{:S(2)}) collective-permute-start(s32[4,32]{1,0:T(4,128)} %bitcast.14), channel_id=1, source_target_pairs={{0,8},{8,0},{16,24},{24,16},{1,9},{9,1},{17,25},{25,17},{2,10},{10... | collective-permute-start | bytes 1544 | tf_op jit(solution)/shard_map/ppermute | solution.py:504
  8.7 4.9 %collective-permute-start.13 = (s32[8,128]{1,0:T(8,128)S(1)}, s32[8,128]{1,0:T(8,128)S(1)}, u32[]{:S(2)}, u32[]{:S(2)}) collective-permute-start(s32[8,128]{1,0:T(8,128)S(1)} %get-tuple-element.114.refs_0_), channel_id=1, source_target_pairs={{0,7},{1,2},{2,1},{3,4},{4,3},{5,6},{6,5},{7,0},{8,15},{9,10},{10,... | collective-permute-start | bytes 12296 | tf_op jit(solution)/shard_map/ppermute | solution.py:510
  14.1 8.2 %collective-permute-start.16 = (bf16[48,2048]{1,0:T(8,128)(2,1)S(1)}, bf16[48,2048]{1,0:T(8,128)(2,1)S(1)}, u32[]{:S(2)}, u32[]{:S(2)}) collective-permute-start(bf16[48,2048]{1,0:T(8,128)(2,1)S(1)} %get-tuple-element.115.x_ref), channel_id=1, source_target_pairs={{0,7},{1,2},{2,1},{3,4},{4,3},{5,6},{6,5},{7,0},{8,15},{9,10},{10,... | collective-permute-start | bytes 589832 | tf_op jit(solution)/shard_map/ppermute | solution.py:510
  15.5 1.2 %collective-permute-start.14 = (s32[8,128]{1,0:T(8,128)S(1)}, s32[8,128]{1,0:T(8,128)S(1)}, u32[]{:S(2)}, u32[]{:S(2)}) collective-permute-start(s32[8,128]{1,0:T(8,128)S(1)} %get-tuple-element.119), channel_id=1, source_target_pairs={{0,1},{1,0},{2,3},{3,2},{4,5},{5,4},{6,7},{7,6},{8,9},{9,8},{10,11... | collective-permute-start | bytes 12296 | tf_op jit(solution)/shard_map/ppermute | solution.py:513
  17.9 4.7 %collective-permute-start.15 = (bf16[48,2048]{1,0:T(8,128)(2,1)S(1)}, bf16[48,2048]{1,0:T(8,128)(2,1)S(1)}, u32[]{:S(2)}, u32[]{:S(2)}) collective-permute-start(bf16[48,2048]{1,0:T(8,128)(2,1)S(1)} %get-tuple-element.122), channel_id=1, source_target_pairs={{0,1},{1,0},{2,3},{3,2},{4,5},{5,4},{6,7},{7,6},{8,9},{9,8},{10,11... | collective-permute-start | bytes 589832 | tf_op jit(solution)/shard_map/ppermute | solution.py:513
  22.9 7.5 %collective-permute-start.17 = (bf16[32,2048]{1,0:T(8,128)(2,1)S(1)}, bf16[32,2048]{1,0:T(8,128)(2,1)S(1)}, u32[]{:S(2)}, u32[]{:S(2)}) collective-permute-start(bf16[32,2048]{1,0:T(8,128)(2,1)S(1)} %get-tuple-element.126), channel_id=1, source_target_pairs={{0,24},{8,16},{16,8},{24,0},{1,25},{9,17},{17,9},{25,1},{2,26},{10... | collective-permute-start | bytes 393224 | tf_op jit(solution)/shard_map/ppermute | solution.py:504
  24.4 6.0 %collective-permute-start.18 = (bf16[32,2048]{1,0:T(8,128)(2,1)S(1)}, bf16[32,2048]{1,0:T(8,128)(2,1)S(1)}, u32[]{:S(2)}, u32[]{:S(2)}) collective-permute-start(bf16[32,2048]{1,0:T(8,128)(2,1)S(1)} %get-tuple-element.127), channel_id=1, source_target_pairs={{0,16},{8,24},{16,0},{24,8},{1,17},{9,25},{17,1},{25,9},{2,18},{10... | collective-permute-start | bytes 393224 | tf_op jit(solution)/shard_map/ppermute | solution.py:504
  25.0 5.5 %collective-permute-start.19 = (bf16[32,2048]{1,0:T(8,128)(2,1)S(1)}, bf16[32,2048]{1,0:T(8,128)(2,1)S(1)}, u32[]{:S(2)}, u32[]{:S(2)}) collective-permute-start(bf16[32,2048]{1,0:T(8,128)(2,1)S(1)} %get-tuple-element.128), channel_id=1, source_target_pairs={{0,8},{8,0},{16,24},{24,16},{1,9},{9,1},{17,25},{25,17},{2,10},{10... | collective-permute-start | bytes 393224 | tf_op jit(solution)/shard_map/ppermute | solution.py:504
  26.4 3.9 %collective-permute-start.21 = (s32[8,128]{1,0:T(8,128)S(1)}, s32[8,128]{1,0:T(8,128)S(1)}, u32[]{:S(2)}, u32[]{:S(2)}) collective-permute-start(s32[8,128]{1,0:T(8,128)S(1)} %get-tuple-element.130.rest_4_), channel_id=1, source_target_pairs={{0,3},{1,4},{2,5},{3,6},{4,7},{5,0},{6,1},{7,2},{8,11},{9,12},{10,... | collective-permute-start | bytes 12296 | tf_op jit(solution)/shard_map/ppermute | solution.py:507
  26.4 4.0 %collective-permute-start.20 = (s32[8,128]{1,0:T(8,128)S(1)}, s32[8,128]{1,0:T(8,128)S(1)}, u32[]{:S(2)}, u32[]{:S(2)}) collective-permute-start(s32[8,128]{1,0:T(8,128)S(1)} %get-tuple-element.130.rest_4_), channel_id=1, source_target_pairs={{0,5},{1,6},{2,7},{3,0},{4,1},{5,2},{6,3},{7,4},{8,13},{9,14},{10,... | collective-permute-start | bytes 12296 | tf_op jit(solution)/shard_map/ppermute | solution.py:507
  31.1 8.3 %collective-permute-start.23 = (bf16[48,2048]{1,0:T(8,128)(2,1)S(1)}, bf16[48,2048]{1,0:T(8,128)(2,1)S(1)}, u32[]{:S(2)}, u32[]{:S(2)}) collective-permute-start(bf16[48,2048]{1,0:T(8,128)(2,1)S(1)} %get-tuple-element.136), channel_id=1, source_target_pairs={{0,7},{1,2},{2,1},{3,4},{4,3},{5,6},{6,5},{7,0},{8,15},{9,10},{10,... | collective-permute-start | bytes 589832 | tf_op jit(solution)/shard_map/ppermute | solution.py:510
  34.2 5.2 %collective-permute-start.22 = (bf16[48,2048]{1,0:T(8,128)(2,1)S(1)}, bf16[48,2048]{1,0:T(8,128)(2,1)S(1)}, u32[]{:S(2)}, u32[]{:S(2)}) collective-permute-start(bf16[48,2048]{1,0:T(8,128)(2,1)S(1)} %get-tuple-element.135), channel_id=1, source_target_pairs={{0,1},{1,0},{2,3},{3,2},{4,5},{5,4},{6,7},{7,6},{8,9},{9,8},{10,11... | collective-permute-start | bytes 589832 | tf_op jit(solution)/shard_map/ppermute | solution.py:513
  39.8 5.9 %collective-permute-start.24 = (bf16[32,2048]{1,0:T(8,128)(2,1)S(1)}, bf16[32,2048]{1,0:T(8,128)(2,1)S(1)}, u32[]{:S(2)}, u32[]{:S(2)}) collective-permute-start(bf16[32,2048]{1,0:T(8,128)(2,1)S(1)} %get-tuple-element.137), channel_id=1, source_target_pairs={{0,24},{8,16},{16,8},{24,0},{1,25},{9,17},{17,9},{25,1},{2,26},{10... | collective-permute-start | bytes 393224 | tf_op jit(solution)/shard_map/ppermute | solution.py:504
  42.3 5.0 %collective-permute-start.25 = (bf16[32,2048]{1,0:T(8,128)(2,1)S(1)}, bf16[32,2048]{1,0:T(8,128)(2,1)S(1)}, u32[]{:S(2)}, u32[]{:S(2)}) collective-permute-start(bf16[32,2048]{1,0:T(8,128)(2,1)S(1)} %get-tuple-element.138), channel_id=1, source_target_pairs={{0,16},{8,24},{16,0},{24,8},{1,17},{9,25},{17,1},{25,9},{2,18},{10... | collective-permute-start | bytes 393224 | tf_op jit(solution)/shard_map/ppermute | solution.py:504
  42.8 5.0 %collective-permute-start.26 = (bf16[32,2048]{1,0:T(8,128)(2,1)S(1)}, bf16[32,2048]{1,0:T(8,128)(2,1)S(1)}, u32[]{:S(2)}, u32[]{:S(2)}) collective-permute-start(bf16[32,2048]{1,0:T(8,128)(2,1)S(1)} %get-tuple-element.139), channel_id=1, source_target_pairs={{0,8},{8,0},{16,24},{24,16},{1,9},{9,1},{17,25},{25,17},{2,10},{10... | collective-permute-start | bytes 393224 | tf_op jit(solution)/shard_map/ppermute | solution.py:504

commit v19 on v18

--- a/solution.py
+++ b/solution.py
@@ -165,26 +165,30 @@
     return jnp.dot(select, x, preferred_element_type=jnp.float32).astype(jnp.bfloat16)
 
 
-def far_kernel(x_ref, beyond_ref, pack_ref, far_ref):
+def far_kernel(x_ref, beyond_ref, core_list_ref, pack_ref, told_ref, far_ref):
+    place = lax.broadcasted_iota(jnp.int32, told_ref.shape, 0)
+    most = jnp.maximum(core_list_ref[...], beyond_ref[...])
+    told_ref[...] = jnp.where(place == 1, most, core_list_ref[...])
     pack_ref[...] = one_hot(beyond_ref[0:1], x_ref.shape[0])
     far_ref[...] = take(pack_ref[: far_ref.shape[0]], x_ref[...])
 
 
-def far_call(x, beyond, sent):
+def far_call(x, beyond, core_list, sent):
     rows, width = x.shape
     total = beyond.shape[1]
     return kernel_call(
         "pack_far",
         far_kernel,
-        [bf16(total, rows), bf16(sent, width)],
+        [bf16(total, rows), int32(*core_list.shape), bf16(sent, width)],
         x,
         beyond,
+        core_list,
         flops=2 * rows * sent * width,
     )
 
 
 def near_kernel(x_ref, mask_ref, pack_ref, own_list_ref, *refs):
-    far_list_ref, beyond_ref, within_ref, *refs = refs
+    told_ref, within_ref, *refs = refs
     core_ref, own_ref, near_ref, rest_far_ref, rest_core_ref, *refs = refs
     far_mask_ref, core_mask_ref, near_mask_ref, most_ref, select = refs
     total, sent = own_ref.shape[0], core_ref.shape[0]
@@ -203,11 +207,11 @@
     near_mask_ref[:sent] = masks[:sent]
     near_mask_ref[sent:] = masks[total:]
     far_mask_ref[...] = take(pack_ref[...], mask_ref[...])
-    most = jnp.maximum(far_list_ref[...], jnp.maximum(beyond_ref[...], within_ref[...]))
+    most = jnp.maximum(told_ref[...], within_ref[...])
     most_ref[...] = jnp.broadcast_to(most[1:2, :LANES], most_ref.shape)
 
 
-def near_call(x, mask, pack, own_list, far_list, beyond, within, sent):
+def near_call(x, mask, pack, own_list, told, within, sent):
     rows, width = x.shape
     total = mask.shape[1]
     return kernel_call(
@@ -228,8 +232,7 @@
         mask,
         pack,
         own_list,
-        far_list,
-        beyond,
+        told,
         within,
         flops=6 * total * rows * width,
         scratch=[pltpu.VMEM((2 * total, rows), jnp.bfloat16)],
@@ -549,21 +552,19 @@
     own_list, far_list, core_list, *expands = list_call(
         [held] + [asked[d] for d in range(1, servers)], rows
     )
-    beyond_list, within_list = across(far_list), inside(core_list)
+    beyond_list = across(far_list)
     x = normalize_call(descriptors[0, 0])
-    pack, far = far_call(x, beyond_list, sent)
+    pack, told, far = far_call(x, beyond_list, core_list, sent)
     core, own, near, *others, most = near_call(
-        x, mask, pack, own_list, far_list, beyond_list, within_list, sent
+        x, mask, pack, own_list, told, inside(told), sent
     )
     rest, masks = others[:2], others[2:]
     most, first = exchange(expands, far, core, own, most)
-    mosts = [most]
-    reach = 1
-    while 2 * reach + 1 < groups:
-        by = 2 * reach + 1
+    mosts, known = [most], 4
+    while known < groups:
         most = functools.reduce(jnp.maximum, mosts)
-        mosts = [most, shift(most, -by), shift(most, by)]
-        reach += by
+        mosts = [most, shift(most, known)]
+        known *= 2
     y, most, last = next_round(
         x, mask, far, near, masks[0], masks[2], expands, first, mosts
     )

time: 51.1 us -> 50.4 us (0.986)
  starting transfers between devices: 19.2 us -> 16.1 us
  waiting for transfers between devices: 16.8 us -> 19.3 us
    ppermute x2 -> x1, waiting for transfers between devices: 1.33 us -> 4.5 us  [shift(): lax.ppermute(value, 'rep', [(g, (g + by) % groups) for g in range(groups)])]
    ppermute x2 -> x1, starting transfers between devices: 2.64 us -> 0.01 us  [shift(): lax.ppermute(value, 'rep', [(g, (g + by) % groups) for g in range(groups)])]
    ppermute x9, waiting for transfers between devices: 5.88 us -> 5.26 us  [turn(): return lax.ppermute(value, 'clus', [(c, c ^ d) for c in range(servers)])]
    ppermute x3, starting transfers between devices: 4.72 us -> 4.17 us  [across(): return lax.ppermute(value, 'rep', beyond)]
  transfers between devices with their start and end apart: 17 -> 16, of which waited for: 11 -> 10; matrix products, arithmetic and copies ran while one was open for 1% -> 1% of each run, Pallas kernels for 16% -> 16%
where the time goes in v19:
time: 50.4 us; the launch traced here: 50.2 us
  waiting for transfers between devices  19.3 us (38%)
  starting transfers between devices  16.1 us (32%)
  Pallas kernels  13.4 us (27%)
  between operations  0.94 us (2%)
  local copies, waits for them, and re-layouts  0.51 us (1%)
    pallas_call x13, Pallas kernels, kernel_call(): pl.pallas_call(kernel, out_shape=outs, scratch_shapes=scratch, compiler_p...  13.4 us
    ppermute x9, starting transfers between devices, turn(): return lax.ppermute(value, 'clus', [(c, c ^ d) for c in range(servers)])  11.6 us
    ppermute x3, waiting for transfers between devices, across(): return lax.ppermute(value, 'rep', beyond)  8.35 us
    ppermute x9, waiting for transfers between devices, turn(): return lax.ppermute(value, 'clus', [(c, c ^ d) for c in range(servers)])  5.26 us
    ppermute x1, waiting for transfers between devices, shift(): lax.ppermute(value, 'rep', [(g, (g + by) % groups) for g in range(groups)])  4.5 us
    ppermute x3, starting transfers between devices, across(): return lax.ppermute(value, 'rep', beyond)  4.17 us
    ppermute x3, waiting for transfers between devices, inside(): return lax.ppermute(value, 'rep', within)  1.17 us
  transfers between devices with their start and end apart: 16, of which 10 were waited for; matrix products, arithmetic and copies ran while one was open for 1% of the time, Pallas kernels for 16%

profile of v19, /device:TPU:0, one launch (start us, length us, event | category | flops | bytes accessed | tf_op | source)
XLA Modules:
  0.0 50.2 jit_solution(15007499134797924694)
XLA Ops:
  0.0 3.9 %collective-permute-start.12 = (s32[4,32]{1,0:T(4,128)}, s32[4,32]{1,0:T(4,128)S(1)}, u32[]{:S(2)}, u32[]{:S(2)}) collective-permute-start(s32[4,32]{1,0:T(4,128)} %bitcast.12), channel_id=1, source_target_pairs={{0,24},{8,16},{16,8},{24,0},{1,25},{9,17},{17,9},{25,1},{2,26},{10... | collective-permute-start | bytes 1544 | tf_op jit(solution)/shard_map/ppermute | solution.py:507
  3.9 0.5 %collective-permute-start.11 = (s32[4,32]{1,0:T(4,128)}, s32[4,32]{1,0:T(4,128)S(1)}, u32[]{:S(2)}, u32[]{:S(2)}) collective-permute-start(s32[4,32]{1,0:T(4,128)} %bitcast.13), channel_id=1, source_target_pairs={{0,16},{8,24},{16,0},{24,8},{1,17},{9,25},{17,1},{25,9},{2,18},{10... | collective-permute-start | bytes 1544 | tf_op jit(solution)/shard_map/ppermute | solution.py:507
  4.4 0.1 collective-permute-start.10
  4.5 1.0 %mask.1 = (bf16[512,128]{1,0:T(8,128)(2,1)S(1)}, s32[4,32]{1,0:T(4,128)S(1)}) custom-call(s32[10,1,512]{2,1,0:T(1,128)} %bitcast.11, s32[4,32]{1,0:T(4,128)} %bitcast.15), custom_call_target="tpu_custom_call" | custom-call | flops 1310720 | bytes 131072 | tf_op jit(solution)/shard_map/mask/pallas_call | solution.py:26
  5.5 0.2 collective-permute-done.12.refs_3_
  5.7 2.0 %collective-permute-done.11.refs_2_ = s32[4,32]{1,0:T(4,128)S(1)} collective-permute-done((s32[4,32]{1,0:T(4,128)}, s32[4,32]{1,0:T(4,128)S(1)}, u32[]{:S(2)}, u32[]{:S(2)}) %collective-permute-start.11) | collective-permute-done | bytes 544 | tf_op jit(solution)/shard_map/ppermute | solution.py:507
  7.7 0.5 %collective-permute-done.10.refs_1_ = s32[4,32]{1,0:T(4,128)S(1)} collective-permute-done((s32[4,32]{1,0:T(4,128)}, s32[4,32]{1,0:T(4,128)S(1)}, u32[]{:S(2)}, u32[]{:S(2)}) %collective-permute-start.10) | collective-permute-done | bytes 544 | tf_op jit(solution)/shard_map/ppermute | solution.py:507
  8.2 0.5 list.1
  8.7 1.4 %collective-permute-start.13 = (s32[8,128]{1,0:T(8,128)S(1)}, s32[8,128]{1,0:T(8,128)S(1)}, u32[]{:S(2)}, u32[]{:S(2)}) collective-permute-start(s32[8,128]{1,0:T(8,128)S(1)} %get-tuple-element.115), channel_id=1, source_target_pairs={{0,7},{1,2},{2,1},{3,4},{4,3},{5,6},{6,5},{7,0},{8,15},{9,10},{10,... | collective-permute-start | bytes 12296 | tf_op jit(solution)/shard_map/ppermute | solution.py:513
  10.1 1.9 %normalize.1.x_ref = bf16[512,2048]{1,0:T(8,128)(2,1)S(1)} custom-call(bf16[512,2048]{1,0:T(8,128)(2,1)} %bitcast.10), custom_call_target="tpu_custom_call" | custom-call | flops 6291456 | bytes 4194304 | tf_op jit(solution)/shard_map/normalize/pallas_call | solution.py:26
  11.9 1.6 %collective-permute-done.13.beyond_ref = s32[8,128]{1,0:T(8,128)S(1)} collective-permute-done((s32[8,128]{1,0:T(8,128)S(1)}, s32[8,128]{1,0:T(8,128)S(1)}, u32[]{:S(2)}, u32[]{:S(2)}) %collective-permute-start.13) | collective-permute-done | bytes 4128 | tf_op jit(solution)/shard_map/ppermute | solution.py:513
  13.6 0.5 %pack_far.1 = (bf16[128,512]{1,0:T(8,128)(2,1)S(1)}, s32[8,128]{1,0:T(8,128)S(1)}, bf16[48,2048]{1,0:T(8,128)(2,1)S(1)}) custom-call(bf16[512,2048]{1,0:T(8,128)(2,1)S(1)} %normalize.1.x_ref, s32[8,128]{1,0:T(8,128)S(1)} %collective-permute-done.13.beyond_ref, s32[8,128]{1,0:T(8,128)S(1)} %get-tuple-element.116.core_list_ref), custom_call_target="tpu_custom_call" | custom-call | flops 100663296 | tf_op jit(solution)/shard_map/pack_far/pallas_call | solution.py:26
  14.1 1.4 %collective-permute-start.16 = (bf16[48,2048]{1,0:T(8,128)(2,1)S(1)}, bf16[48,2048]{1,0:T(8,128)(2,1)S(1)}, u32[]{:S(2)}, u32[]{:S(2)}) collective-permute-start(bf16[48,2048]{1,0:T(8,128)(2,1)S(1)} %get-tuple-element.117.x_ref), channel_id=1, source_target_pairs={{0,7},{1,2},{2,1},{3,4},{4,3},{5,6},{6,5},{7,0},{8,15},{9,10},{10,... | collective-permute-start | bytes 589832 | tf_op jit(solution)/shard_map/ppermute | solution.py:513
  15.5 0.0 collective-permute-start.14
  15.5 1.2 %collective-permute-done.14.refs_1_ = s32[8,128]{1,0:T(8,128)S(1)} collective-permute-done((s32[8,128]{1,0:T(8,128)S(1)}, s32[8,128]{1,0:T(8,128)S(1)}, u32[]{:S(2)}, u32[]{:S(2)}) %collective-permute-start.14) | collective-permute-done | bytes 4128 | tf_op jit(solution)/shard_map/ppermute | solution.py:516
  16.7 1.2 %serve_near.1 = (bf16[48,2048]{1,0:T(8,128)(2,1)S(1)}, bf16[128,2048]{1,0:T(8,128)(2,1)S(1)}, bf16[176,2048]{1,0:T(8,128)(2,1)S(1)}, bf16[80,2048]{1,0:T(8,128)(...) custom-call(bf16[512,2048]{1,0:T(8,128)(2,1)S(1)} %normalize.1.x_ref, ...), custom_call_target="tpu_custom_call" | custom-call | flops 805306368 | tf_op jit(solution)/shard_map/serve_near/pallas_call | solution.py:26
  17.9 0.2 collective-permute-start.15
  18.1 4.2 %collective-permute-done.16.far_ref = bf16[48,2048]{1,0:T(8,128)(2,1)S(1)} collective-permute-done((bf16[48,2048]{1,0:T(8,128)(2,1)S(1)}, bf16[48,2048]{1,0:T(8,128)(2,1)S(1)}, u32[]{:S(2)}, u32[]{:S(2)}) %collective-permute-start.16) | collective-permute-done | bytes 196640 | tf_op jit(solution)/shard_map/ppermute | solution.py:513
  22.3 0.3 unpack.5.base_ref
  22.6 0.0 collective-permute-done.15.core_ref
  22.6 0.3 combine.1
  22.9 1.6 %collective-permute-start.17 = (bf16[32,2048]{1,0:T(8,128)(2,1)S(1)}, bf16[32,2048]{1,0:T(8,128)(2,1)S(1)}, u32[]{:S(2)}, u32[]{:S(2)}) collective-permute-start(bf16[32,2048]{1,0:T(8,128)(2,1)S(1)} %get-tuple-element.128), channel_id=1, source_target_pairs={{0,24},{8,16},{16,8},{24,0},{1,25},{9,17},{17,9},{25,1},{2,26},{10... | collective-permute-start | bytes 393224 | tf_op jit(solution)/shard_map/ppermute | solution.py:507
  24.4 0.5 %collective-permute-start.18 = (bf16[32,2048]{1,0:T(8,128)(2,1)S(1)}, bf16[32,2048]{1,0:T(8,128)(2,1)S(1)}, u32[]{:S(2)}, u32[]{:S(2)}) collective-permute-start(bf16[32,2048]{1,0:T(8,128)(2,1)S(1)} %get-tuple-element.129), channel_id=1, source_target_pairs={{0,16},{8,24},{16,0},{24,8},{1,17},{9,25},{17,1},{25,9},{2,18},{10... | collective-permute-start | bytes 393224 | tf_op jit(solution)/shard_map/ppermute | solution.py:507
  25.0 1.5 %collective-permute-start.19 = (bf16[32,2048]{1,0:T(8,128)(2,1)S(1)}, bf16[32,2048]{1,0:T(8,128)(2,1)S(1)}, u32[]{:S(2)}, u32[]{:S(2)}) collective-permute-start(bf16[32,2048]{1,0:T(8,128)(2,1)S(1)} %get-tuple-element.130), channel_id=1, source_target_pairs={{0,8},{8,0},{16,24},{24,16},{1,9},{9,1},{17,25},{25,17},{2,10},{10... | collective-permute-start | bytes 393224 | tf_op jit(solution)/shard_map/ppermute | solution.py:507
  26.4 0.0 collective-permute-start.20
  26.4 4.5 %collective-permute-done.20.rest_5_ = s32[8,128]{1,0:T(8,128)S(1)} collective-permute-done((s32[8,128]{1,0:T(8,128)S(1)}, s32[8,128]{1,0:T(8,128)S(1)}, u32[]{:S(2)}, u32[]{:S(2)}) %collective-permute-start.20) | collective-permute-done | bytes 4128 | tf_op jit(solution)/shard_map/ppermute | solution.py:510
  31.0 0.0 collective-permute-done.17.rest_0_
  31.0 0.0 collective-permute-done.18.rest_1_
  31.0 0.0 collective-permute-done.19.rest_2_
  31.0 0.7 %mix_far.3 = (bf16[48,2048]{1,0:T(8,128)(2,1)S(1)}, s32[8,128]{1,0:T(8,128)S(1)}) custom-call(bf16[48,2048]{1,0:T(8,128)(2,1)S(1)} %get-tuple-element.117.x_ref, bf16[128,128]{1,0:T(8,128)(2,1)S(1)} %get-tuple-element.122.mask_ref, bf16[32,2048]{1,0:T(8,128)(2,1)S(1)} %collective-permute-done.17.rest_0_, ...), custom_call_target="tpu_custom_call" | custom-call | flops 50331648 | tf_op jit(solution)/shard_map/mix_far/pallas_call | solution.py:26
  31.6 1.4 %collective-permute-start.22 = (bf16[48,2048]{1,0:T(8,128)(2,1)S(1)}, bf16[48,2048]{1,0:T(8,128)(2,1)S(1)}, u32[]{:S(2)}, u32[]{:S(2)}) collective-permute-start(bf16[48,2048]{1,0:T(8,128)(2,1)S(1)} %get-tuple-element.138), channel_id=1, source_target_pairs={{0,7},{1,2},{2,1},{3,4},{4,3},{5,6},{6,5},{7,0},{8,15},{9,10},{10,... | collective-permute-start | bytes 589832 | tf_op jit(solution)/shard_map/ppermute | solution.py:513
  33.0 1.1 %mix_near.3 = (bf16[48,2048]{1,0:T(8,128)(2,1)S(1)}, bf16[128,2048]{1,0:T(8,128)(2,1)S(1)}) custom-call(bf16[176,2048]{1,0:T(8,128)(2,1)S(1)} %get-tuple-element.134.x_ref, bf16[176,128]{1,0:T(8,128)(2,1)S(1)} %get-tuple-element.135.mask_ref, bf16[32,2048]{1,0:T(8,128)(2,1)S(1)} %collective-permute-done.17.rest_0_, ...), custom_call_target="tpu_custom_call" | custom-call | flops 184549376 | tf_op jit(solution)/shard_map/mix_near/pallas_call | solution.py:26
  34.1 0.1 collective-permute-start.21
  34.2 2.5 %mix_whole_late.3.rest_4_.refs_0_ = bf16[512,2048]{1,0:T(8,128)(2,1)S(1)} custom-call(bf16[512,2048]{1,0:T(8,128)(2,1)S(1)} %normalize.1.x_ref, bf16[512,128]{1,0:T(8,128)(2,1)S(1)} %get-tuple-element.118.mask_ref, bf16[32,2048]{1,0:T(8,128)(2,1)S(1)} %collective-permute-done.17.rest_0_, bf16[32,2048]{1,0:T(8,128)(2,1)S(1)} %collective-permute-done.18.rest_1_, ...), custom_call_target="tpu_custom_call" | custom-call | flops 536870912 | tf_op jit(solution)/shard_map/mix_whole_late/pallas_call | solution.py:26
  36.7 2.5 %collective-permute-done.22.far_ref = bf16[48,2048]{1,0:T(8,128)(2,1)S(1)} collective-permute-done((bf16[48,2048]{1,0:T(8,128)(2,1)S(1)}, bf16[48,2048]{1,0:T(8,128)(2,1)S(1)}, u32[]{:S(2)}, u32[]{:S(2)}) %collective-permute-start.22) | collective-permute-done | bytes 196640 | tf_op jit(solution)/shard_map/ppermute | solution.py:513
  39.3 0.0 collective-permute-done.21.core_ref
  39.3 0.4 unpack_both.3
  39.7 1.4 %collective-permute-start.23 = (bf16[32,2048]{1,0:T(8,128)(2,1)S(1)}, bf16[32,2048]{1,0:T(8,128)(2,1)S(1)}, u32[]{:S(2)}, u32[]{:S(2)}) collective-permute-start(bf16[32,2048]{1,0:T(8,128)(2,1)S(1)} %get-tuple-element.139), channel_id=1, source_target_pairs={{0,24},{8,16},{16,8},{24,0},{1,25},{9,17},{17,9},{25,1},{2,26},{10... | collective-permute-start | bytes 393224 | tf_op jit(solution)/shard_map/ppermute | solution.py:507
  41.1 0.6 %collective-permute-start.24 = (bf16[32,2048]{1,0:T(8,128)(2,1)S(1)}, bf16[32,2048]{1,0:T(8,128)(2,1)S(1)}, u32[]{:S(2)}, u32[]{:S(2)}) collective-permute-start(bf16[32,2048]{1,0:T(8,128)(2,1)S(1)} %get-tuple-element.140), channel_id=1, source_target_pairs={{0,16},{8,24},{16,0},{24,8},{1,17},{9,25},{17,1},{25,9},{2,18},{10... | collective-permute-start | bytes 393224 | tf_op jit(solution)/shard_map/ppermute | solution.py:507
  41.7 1.6 %collective-permute-start.25 = (bf16[32,2048]{1,0:T(8,128)(2,1)S(1)}, bf16[32,2048]{1,0:T(8,128)(2,1)S(1)}, u32[]{:S(2)}, u32[]{:S(2)}) collective-permute-start(bf16[32,2048]{1,0:T(8,128)(2,1)S(1)} %get-tuple-element.141), channel_id=1, source_target_pairs={{0,8},{8,0},{16,24},{24,16},{1,9},{9,1},{17,25},{25,17},{2,10},{10... | collective-permute-start | bytes 393224 | tf_op jit(solution)/shard_map/ppermute | solution.py:507
  43.3 0.5 %slice.16 = s32[1,1]{1,0:T(1,128)} slice(s32[8,128]{1,0:T(8,128)S(1)} %get-tuple-element.133), slice={[0:1], [0:1]} | slice | bytes 8 | tf_op jit(solution)/shard_map/slice | solution.py:572
  44.4 0.1 mix_whole_early.3
  44.5 1.2 %collective-permute-done.23 = bf16[32,2048]{1,0:T(8,128)(2,1)S(1)} collective-permute-done((bf16[32,2048]{1,0:T(8,128)(2,1)S(1)}, bf16[32,2048]{1,0:T(8,128)(2,1)S(1)}, u32[]{:S(2)}, u32[]{:S(2)}) %collective-permute-start.23) | collective-permute-done | bytes 131104 | tf_op jit(solution)/shard_map/ppermute | solution.py:507
  45.7 1.3 %collective-permute-done.24 = bf16[32,2048]{1,0:T(8,128)(2,1)S(1)} collective-permute-done((bf16[32,2048]{1,0:T(8,128)(2,1)S(1)}, bf16[32,2048]{1,0:T(8,128)(2,1)S(1)}, u32[]{:S(2)}, u32[]{:S(2)}) %collective-permute-start.24) | collective-permute-done | bytes 131104 | tf_op jit(solution)/shard_map/ppermute | solution.py:507
  47.0 0.0 collective-permute-done.25
  47.0 3.0 %conditional.1 = (bf16[1,1,512,2048]{3,2,1,0:T(8,128)(2,1)}) conditional(s32[]{:T(128)} %bitcast.6, (bf16[512,2048]{1,0:T(8,128)(2,1)S(1)}, bf16[512,128]{1,0:T(8,128)(2,1)S(1)}, bf16[32,2048]{1,0:T(8,128)(2,1)S(1)}, bf16[32,2048]{1,0:T(8,128)(2,1)S(1)}, bf16[32,2048]{1,0:T(8,128)(2,1)S(1)}, /*index=5*/bf16[32,2048]{1,0:T(8,128)(2,1)S(1)}) %tuple.13, ...), branch_computations={%region_0.0_spmd, %region_1.0_spmd} | conditional | flops 36511809536 | bytes 88408472 | solution.py:572
  47.0 3.0 %mix.2 = bf16[512,2048]{1,0:T(8,128)(2,1)} custom-call(bf16[512,2048]{1,0:T(8,128)(2,1)S(1)} %get-tuple-element.53.x_ref, bf16[512,128]{1,0:T(8,128)(2,1)S(1)} %get-tuple-element.54.mask_ref, bf16[32,2048]{1,0:T(8,128)(2,1)S(1)} %get-tuple-element.55.rest_0_, bf16[32,2048]{1,0:T(8,128)(2,1)S(1)} %get-tuple-element.56.rest_1_, ...), custom_call_target="tpu_custom_call" | custom-call | flops 536870912 | bytes 4194304 | tf_op jit(solution)/shard_map/cond/branch_0_fun/mix/pallas_call | solution.py:26
Async XLA Ops:
  0.0 5.7 %collective-permute-start.12 = (s32[4,32]{1,0:T(4,128)}, s32[4,32]{1,0:T(4,128)S(1)}, u32[]{:S(2)}, u32[]{:S(2)}) collective-permute-start(s32[4,32]{1,0:T(4,128)} %bitcast.12), channel_id=1, source_target_pairs={{0,24},{8,16},{16,8},{24,0},{1,25},{9,17},{17,9},{25,1},{2,26},{10... | collective-permute-start | bytes 1544 | tf_op jit(solution)/shard_map/ppermute | solution.py:507
  3.9 3.8 %collective-permute-start.11 = (s32[4,32]{1,0:T(4,128)}, s32[4,32]{1,0:T(4,128)S(1)}, u32[]{:S(2)}, u32[]{:S(2)}) collective-permute-start(s32[4,32]{1,0:T(4,128)} %bitcast.13), channel_id=1, source_target_pairs={{0,16},{8,24},{16,0},{24,8},{1,17},{9,25},{17,1},{25,9},{2,18},{10... | collective-permute-start | bytes 1544 | tf_op jit(solution)/shard_map/ppermute | solution.py:507
  4.4 3.8 %collective-permute-start.10 = (s32[4,32]{1,0:T(4,128)}, s32[4,32]{1,0:T(4,128)S(1)}, u32[]{:S(2)}, u32[]{:S(2)}) collective-permute-start(s32[4,32]{1,0:T(4,128)} %bitcast.14), channel_id=1, source_target_pairs={{0,8},{8,0},{16,24},{24,16},{1,9},{9,1},{17,25},{25,17},{2,10},{10... | collective-permute-start | bytes 1544 | tf_op jit(solution)/shard_map/ppermute | solution.py:507
  8.7 4.9 %collective-permute-start.13 = (s32[8,128]{1,0:T(8,128)S(1)}, s32[8,128]{1,0:T(8,128)S(1)}, u32[]{:S(2)}, u32[]{:S(2)}) collective-permute-start(s32[8,128]{1,0:T(8,128)S(1)} %get-tuple-element.115), channel_id=1, source_target_pairs={{0,7},{1,2},{2,1},{3,4},{4,3},{5,6},{6,5},{7,0},{8,15},{9,10},{10,... | collective-permute-start | bytes 12296 | tf_op jit(solution)/shard_map/ppermute | solution.py:513
  14.1 8.2 %collective-permute-start.16 = (bf16[48,2048]{1,0:T(8,128)(2,1)S(1)}, bf16[48,2048]{1,0:T(8,128)(2,1)S(1)}, u32[]{:S(2)}, u32[]{:S(2)}) collective-permute-start(bf16[48,2048]{1,0:T(8,128)(2,1)S(1)} %get-tuple-element.117.x_ref), channel_id=1, source_target_pairs={{0,7},{1,2},{2,1},{3,4},{4,3},{5,6},{6,5},{7,0},{8,15},{9,10},{10,... | collective-permute-start | bytes 589832 | tf_op jit(solution)/shard_map/ppermute | solution.py:513
  15.5 1.2 %collective-permute-start.14 = (s32[8,128]{1,0:T(8,128)S(1)}, s32[8,128]{1,0:T(8,128)S(1)}, u32[]{:S(2)}, u32[]{:S(2)}) collective-permute-start(s32[8,128]{1,0:T(8,128)S(1)} %get-tuple-element.121.refs_0_), channel_id=1, source_target_pairs={{0,1},{1,0},{2,3},{3,2},{4,5},{5,4},{6,7},{7,6},{8,9},{9,8},{10,11... | collective-permute-start | bytes 12296 | tf_op jit(solution)/shard_map/ppermute | solution.py:516
  17.9 4.7 %collective-permute-start.15 = (bf16[48,2048]{1,0:T(8,128)(2,1)S(1)}, bf16[48,2048]{1,0:T(8,128)(2,1)S(1)}, u32[]{:S(2)}, u32[]{:S(2)}) collective-permute-start(bf16[48,2048]{1,0:T(8,128)(2,1)S(1)} %get-tuple-element.124), channel_id=1, source_target_pairs={{0,1},{1,0},{2,3},{3,2},{4,5},{5,4},{6,7},{7,6},{8,9},{9,8},{10,11... | collective-permute-start | bytes 589832 | tf_op jit(solution)/shard_map/ppermute | solution.py:516
  22.9 8.1 %collective-permute-start.17 = (bf16[32,2048]{1,0:T(8,128)(2,1)S(1)}, bf16[32,2048]{1,0:T(8,128)(2,1)S(1)}, u32[]{:S(2)}, u32[]{:S(2)}) collective-permute-start(bf16[32,2048]{1,0:T(8,128)(2,1)S(1)} %get-tuple-element.128), channel_id=1, source_target_pairs={{0,24},{8,16},{16,8},{24,0},{1,25},{9,17},{17,9},{25,1},{2,26},{10... | collective-permute-start | bytes 393224 | tf_op jit(solution)/shard_map/ppermute | solution.py:507
  24.4 6.5 %collective-permute-start.18 = (bf16[32,2048]{1,0:T(8,128)(2,1)S(1)}, bf16[32,2048]{1,0:T(8,128)(2,1)S(1)}, u32[]{:S(2)}, u32[]{:S(2)}) collective-permute-start(bf16[32,2048]{1,0:T(8,128)(2,1)S(1)} %get-tuple-element.129), channel_id=1, source_target_pairs={{0,16},{8,24},{16,0},{24,8},{1,17},{9,25},{17,1},{25,9},{2,18},{10... | collective-permute-start | bytes 393224 | tf_op jit(solution)/shard_map/ppermute | solution.py:507
  25.0 6.0 %collective-permute-start.19 = (bf16[32,2048]{1,0:T(8,128)(2,1)S(1)}, bf16[32,2048]{1,0:T(8,128)(2,1)S(1)}, u32[]{:S(2)}, u32[]{:S(2)}) collective-permute-start(bf16[32,2048]{1,0:T(8,128)(2,1)S(1)} %get-tuple-element.130), channel_id=1, source_target_pairs={{0,8},{8,0},{16,24},{24,16},{1,9},{9,1},{17,25},{25,17},{2,10},{10... | collective-permute-start | bytes 393224 | tf_op jit(solution)/shard_map/ppermute | solution.py:507
  26.4 4.5 %collective-permute-start.20 = (s32[8,128]{1,0:T(8,128)S(1)}, s32[8,128]{1,0:T(8,128)S(1)}, u32[]{:S(2)}, u32[]{:S(2)}) collective-permute-start(s32[8,128]{1,0:T(8,128)S(1)} %get-tuple-element.132.rest_4_), channel_id=1, source_target_pairs={{0,4},{1,5},{2,6},{3,7},{4,0},{5,1},{6,2},{7,3},{8,12},{9,13},{10,... | collective-permute-start | bytes 12296 | tf_op jit(solution)/shard_map/ppermute | solution.py:510
  31.6 7.6 %collective-permute-start.22 = (bf16[48,2048]{1,0:T(8,128)(2,1)S(1)}, bf16[48,2048]{1,0:T(8,128)(2,1)S(1)}, u32[]{:S(2)}, u32[]{:S(2)}) collective-permute-start(bf16[48,2048]{1,0:T(8,128)(2,1)S(1)} %get-tuple-element.138), channel_id=1, source_target_pairs={{0,7},{1,2},{2,1},{3,4},{4,3},{5,6},{6,5},{7,0},{8,15},{9,10},{10,... | collective-permute-start | bytes 589832 | tf_op jit(solution)/shard_map/ppermute | solution.py:513
  34.1 5.1 %collective-permute-start.21 = (bf16[48,2048]{1,0:T(8,128)(2,1)S(1)}, bf16[48,2048]{1,0:T(8,128)(2,1)S(1)}, u32[]{:S(2)}, u32[]{:S(2)}) collective-permute-start(bf16[48,2048]{1,0:T(8,128)(2,1)S(1)} %get-tuple-element.137), channel_id=1, source_target_pairs={{0,1},{1,0},{2,3},{3,2},{4,5},{5,4},{6,7},{7,6},{8,9},{9,8},{10,11... | collective-permute-start | bytes 589832 | tf_op jit(solution)/shard_map/ppermute | solution.py:516
  39.7 6.0 %collective-permute-start.23 = (bf16[32,2048]{1,0:T(8,128)(2,1)S(1)}, bf16[32,2048]{1,0:T(8,128)(2,1)S(1)}, u32[]{:S(2)}, u32[]{:S(2)}) collective-permute-start(bf16[32,2048]{1,0:T(8,128)(2,1)S(1)} %get-tuple-element.139), channel_id=1, source_target_pairs={{0,24},{8,16},{16,8},{24,0},{1,25},{9,17},{17,9},{25,1},{2,26},{10... | collective-permute-start | bytes 393224 | tf_op jit(solution)/shard_map/ppermute | solution.py:507
  41.1 5.9 %collective-permute-start.24 = (bf16[32,2048]{1,0:T(8,128)(2,1)S(1)}, bf16[32,2048]{1,0:T(8,128)(2,1)S(1)}, u32[]{:S(2)}, u32[]{:S(2)}) collective-permute-start(bf16[32,2048]{1,0:T(8,128)(2,1)S(1)} %get-tuple-element.140), channel_id=1, source_target_pairs={{0,16},{8,24},{16,0},{24,8},{1,17},{9,25},{17,1},{25,9},{2,18},{10... | collective-permute-start | bytes 393224 | tf_op jit(solution)/shard_map/ppermute | solution.py:507
  41.7 5.3 %collective-permute-start.25 = (bf16[32,2048]{1,0:T(8,128)(2,1)S(1)}, bf16[32,2048]{1,0:T(8,128)(2,1)S(1)}, u32[]{:S(2)}, u32[]{:S(2)}) collective-permute-start(bf16[32,2048]{1,0:T(8,128)(2,1)S(1)} %get-tuple-element.141), channel_id=1, source_target_pairs={{0,8},{8,0},{16,24},{24,16},{1,9},{9,1},{17,25},{25,17},{2,10},{10... | collective-permute-start | bytes 393224 | tf_op jit(solution)/shard_map/ppermute | solution.py:507

commit v20 on v19

--- a/solution.py
+++ b/solution.py
@@ -151,12 +151,13 @@
     )
 
 
-def one_hot(numbers, rows):
+def one_hot(numbers, rows, count=None):
     total = numbers.shape[1]
     column = jnp.broadcast_to(numbers.astype(jnp.float32), (LANES, total)).T.astype(jnp.int32)
+    column = column[:count]
     tiles = []
     for start in range(0, rows, LANES):
-        lane = lax.broadcasted_iota(jnp.int32, (total, LANES), 1) + start
+        lane = lax.broadcasted_iota(jnp.int32, column.shape, 1) + start
         tiles.append(jnp.where(column == lane, 1.0, 0.0).astype(jnp.bfloat16))
     return jnp.concatenate(tiles, axis=1)
 
@@ -165,21 +166,19 @@
     return jnp.dot(select, x, preferred_element_type=jnp.float32).astype(jnp.bfloat16)
 
 
-def far_kernel(x_ref, beyond_ref, core_list_ref, pack_ref, told_ref, far_ref):
+def far_kernel(x_ref, beyond_ref, core_list_ref, told_ref, far_ref):
+    far_ref[...] = take(one_hot(beyond_ref[0:1], *x_ref.shape[:1], far_ref.shape[0]), x_ref[...])
     place = lax.broadcasted_iota(jnp.int32, told_ref.shape, 0)
     most = jnp.maximum(core_list_ref[...], beyond_ref[...])
     told_ref[...] = jnp.where(place == 1, most, core_list_ref[...])
-    pack_ref[...] = one_hot(beyond_ref[0:1], x_ref.shape[0])
-    far_ref[...] = take(pack_ref[: far_ref.shape[0]], x_ref[...])
 
 
 def far_call(x, beyond, core_list, sent):
     rows, width = x.shape
-    total = beyond.shape[1]
     return kernel_call(
         "pack_far",
         far_kernel,
-        [bf16(total, rows), int32(*core_list.shape), bf16(sent, width)],
+        [int32(*core_list.shape), bf16(sent, width)],
         x,
         beyond,
         core_list,
@@ -187,7 +186,7 @@
     )
 
 
-def near_kernel(x_ref, mask_ref, pack_ref, own_list_ref, *refs):
+def near_kernel(x_ref, mask_ref, beyond_ref, own_list_ref, *refs):
     told_ref, within_ref, *refs = refs
     core_ref, own_ref, near_ref, rest_far_ref, rest_core_ref, *refs = refs
     far_mask_ref, core_mask_ref, near_mask_ref, most_ref, select = refs
@@ -201,17 +200,18 @@
     rest_core_ref[...] = fetched[sent:total]
     own_ref[...] = fetched[total:]
     near_ref[sent:] = fetched[total:]
-    rest_far_ref[...] = take(pack_ref[sent:], x_ref[...])
+    pack = one_hot(beyond_ref[0:1], rows)
+    rest_far_ref[...] = take(pack[sent:], x_ref[...])
     masks = take(select[...], mask_ref[...])
     core_mask_ref[...] = masks[:total]
     near_mask_ref[:sent] = masks[:sent]
     near_mask_ref[sent:] = masks[total:]
-    far_mask_ref[...] = take(pack_ref[...], mask_ref[...])
+    far_mask_ref[...] = take(pack, mask_ref[...])
     most = jnp.maximum(told_ref[...], within_ref[...])
     most_ref[...] = jnp.broadcast_to(most[1:2, :LANES], most_ref.shape)
 
 
-def near_call(x, mask, pack, own_list, told, within, sent):
+def near_call(x, mask, beyond, own_list, told, within, sent):
     rows, width = x.shape
     total = mask.shape[1]
     return kernel_call(
@@ -230,7 +230,7 @@
         ],
         x,
         mask,
-        pack,
+        beyond,
         own_list,
         told,
         within,
@@ -322,10 +322,14 @@
         buffer[d * cap : (d + 1) * cap] = ref[...]
 
 
+def cube(dots, width):
+    positive = jnp.maximum(dots * (1.0 / width), 0.0)
+    return (positive * positive * positive).astype(jnp.bfloat16)
+
+
 def weigh(x, buffer, mask):
     dots = lax.dot_general(x, buffer, BOTH_LAST, preferred_element_type=jnp.float32)
-    positive = jnp.maximum(dots * (1.0 / x.shape[1]), 0.0)
-    return (positive * positive * positive).astype(jnp.bfloat16) * mask
+    return cube(dots, x.shape[1]) * mask
 
 
 def mix(x, weights, buffer):
@@ -416,11 +420,13 @@
     )
 
 
-def mix_blocks(x_ref, mask_ref, buffer, whole, out_ref, sems):
+def mix_blocks(x_ref, mask_ref, buffer, turned, whole, out_ref, sems):
     copies = []
+    turned[...] = buffer[...].T
     for start in range(0, x_ref.shape[0], BLOCK):
         here = pl.ds(start, BLOCK)
-        weights = weigh(x_ref[here], buffer[...], mask_ref[here])
+        dots = jnp.dot(x_ref[here], turned[...], preferred_element_type=jnp.float32)
+        weights = cube(dots, x_ref.shape[1]) * mask_ref[here]
         whole[here] = mix(x_ref[here], weights, buffer[...])
         for half in range(start, start + BLOCK, COPY):
             rows = pl.ds(half, COPY)
@@ -434,12 +440,12 @@
 
 
 def early_kernel(servers, x_ref, mask_ref, *rest):
-    parts, (_, out_ref, buffer, whole, sems) = rest[:servers], rest[servers:]
+    parts, (_, out_ref, buffer, turned, whole, sems) = rest[:servers], rest[servers:]
 
     @pl.when(jnp.logical_not(is_late()))
     def _():
         fill(buffer, parts)
-        mix_blocks(x_ref, mask_ref, buffer, whole, out_ref, sems)
+        mix_blocks(x_ref, mask_ref, buffer, turned, whole, out_ref, sems)
 
 
 def early_call(x, mask, parts, out):
@@ -456,6 +462,7 @@
         flops=4 * total * rows * width,
         scratch=[
             pltpu.VMEM((total, width), jnp.bfloat16),
+            pltpu.VMEM((width, total), jnp.bfloat16),
             pltpu.VMEM((rows, width), jnp.bfloat16),
             pltpu.SemaphoreType.DMA((rows // COPY,)),
         ],
@@ -467,9 +474,9 @@
 
 
 def last_kernel(servers, x_ref, mask_ref, *rest):
-    parts, (out_ref, buffer, whole, sems) = rest[:servers], rest[servers:]
+    parts, (out_ref, buffer, turned, whole, sems) = rest[:servers], rest[servers:]
     fill(buffer, parts)
-    mix_blocks(x_ref, mask_ref, buffer, whole, out_ref, sems)
+    mix_blocks(x_ref, mask_ref, buffer, turned, whole, out_ref, sems)
 
 
 def last_call(x, mask, parts):
@@ -486,6 +493,7 @@
         moved=4 * rows * width,
         scratch=[
             pltpu.VMEM((total, width), jnp.bfloat16),
+            pltpu.VMEM((width, total), jnp.bfloat16),
             pltpu.VMEM((rows, width), jnp.bfloat16),
             pltpu.SemaphoreType.DMA((rows // COPY,)),
         ],
@@ -554,9 +562,9 @@
     )
     beyond_list = across(far_list)
     x = normalize_call(descriptors[0, 0])
-    pack, told, far = far_call(x, beyond_list, core_list, sent)
+    told, far = far_call(x, beyond_list, core_list, sent)
     core, own, near, *others, most = near_call(
-        x, mask, pack, own_list, told, inside(told), sent
+        x, mask, beyond_list, own_list, told, inside(told), sent
     )
     rest, masks = others[:2], others[2:]
     most, first = exchange(expands, far, core, own, most)

time: 50.4 us -> 50.6 us (level)
  no operation moved by 1% of the time
where the time goes in v20:
time: 50.6 us; the launch traced here: 50.4 us
  waiting for transfers between devices  19.3 us (38%)
  starting transfers between devices  16.1 us (32%)
  Pallas kernels  13.3 us (26%)
  between operations  0.96 us (2%)
  local copies, waits for them, and re-layouts  0.51 us (1%)
    pallas_call x13, Pallas kernels, kernel_call(): pl.pallas_call(kernel, out_shape=outs, scratch_shapes=scratch, compiler_p...  13.3 us
    ppermute x9, starting transfers between devices, turn(): return lax.ppermute(value, 'clus', [(c, c ^ d) for c in range(servers)])  11.6 us
    ppermute x3, waiting for transfers between devices, across(): return lax.ppermute(value, 'rep', beyond)  8.36 us
    ppermute x9, waiting for transfers between devices, turn(): return lax.ppermute(value, 'clus', [(c, c ^ d) for c in range(servers)])  5.26 us
    ppermute x1, waiting for transfers between devices, shift(): lax.ppermute(value, 'rep', [(g, (g + by) % groups) for g in range(groups)])  4.5 us
    ppermute x3, starting transfers between devices, across(): return lax.ppermute(value, 'rep', beyond)  4.21 us
    ppermute x3, waiting for transfers between devices, inside(): return lax.ppermute(value, 'rep', within)  1.17 us
  transfers between devices with their start and end apart: 16, of which 10 were waited for; matrix products, arithmetic and copies ran while one was open for 1% of the time, Pallas kernels for 16%

profile of v20, /device:TPU:0, one launch (start us, length us, event | category | flops | bytes accessed | tf_op | source)
XLA Modules:
  0.0 50.4 jit_solution(5188086094058209236)
XLA Ops:
  0.0 3.9 %collective-permute-start.12 = (s32[4,32]{1,0:T(4,128)}, s32[4,32]{1,0:T(4,128)S(1)}, u32[]{:S(2)}, u32[]{:S(2)}) collective-permute-start(s32[4,32]{1,0:T(4,128)} %bitcast.12), channel_id=1, source_target_pairs={{0,24},{8,16},{16,8},{24,0},{1,25},{9,17},{17,9},{25,1},{2,26},{10... | collective-permute-start | bytes 1544 | tf_op jit(solution)/shard_map/ppermute | solution.py:515
  3.9 0.5 %collective-permute-start.11 = (s32[4,32]{1,0:T(4,128)}, s32[4,32]{1,0:T(4,128)S(1)}, u32[]{:S(2)}, u32[]{:S(2)}) collective-permute-start(s32[4,32]{1,0:T(4,128)} %bitcast.13), channel_id=1, source_target_pairs={{0,16},{8,24},{16,0},{24,8},{1,17},{9,25},{17,1},{25,9},{2,18},{10... | collective-permute-start | bytes 1544 | tf_op jit(solution)/shard_map/ppermute | solution.py:515
  4.4 0.1 collective-permute-start.10
  4.5 1.0 %mask.1 = (bf16[512,128]{1,0:T(8,128)(2,1)S(1)}, s32[4,32]{1,0:T(4,128)S(1)}) custom-call(s32[10,1,512]{2,1,0:T(1,128)} %bitcast.11, s32[4,32]{1,0:T(4,128)} %bitcast.15), custom_call_target="tpu_custom_call" | custom-call | flops 1310720 | bytes 131072 | tf_op jit(solution)/shard_map/mask/pallas_call | solution.py:26
  5.5 0.2 collective-permute-done.12.refs_3_
  5.7 2.0 %collective-permute-done.11.refs_2_ = s32[4,32]{1,0:T(4,128)S(1)} collective-permute-done((s32[4,32]{1,0:T(4,128)}, s32[4,32]{1,0:T(4,128)S(1)}, u32[]{:S(2)}, u32[]{:S(2)}) %collective-permute-start.11) | collective-permute-done | bytes 544 | tf_op jit(solution)/shard_map/ppermute | solution.py:515
  7.7 0.5 %collective-permute-done.10.refs_1_ = s32[4,32]{1,0:T(4,128)S(1)} collective-permute-done((s32[4,32]{1,0:T(4,128)}, s32[4,32]{1,0:T(4,128)S(1)}, u32[]{:S(2)}, u32[]{:S(2)}) %collective-permute-start.10) | collective-permute-done | bytes 544 | tf_op jit(solution)/shard_map/ppermute | solution.py:515
  8.2 0.5 list.1
  8.7 1.4 %collective-permute-start.13 = (s32[8,128]{1,0:T(8,128)S(1)}, s32[8,128]{1,0:T(8,128)S(1)}, u32[]{:S(2)}, u32[]{:S(2)}) collective-permute-start(s32[8,128]{1,0:T(8,128)S(1)} %get-tuple-element.114), channel_id=1, source_target_pairs={{0,7},{1,2},{2,1},{3,4},{4,3},{5,6},{6,5},{7,0},{8,15},{9,10},{10,... | collective-permute-start | bytes 12296 | tf_op jit(solution)/shard_map/ppermute | solution.py:521
  10.1 1.9 %normalize.1.x_ref = bf16[512,2048]{1,0:T(8,128)(2,1)S(1)} custom-call(bf16[512,2048]{1,0:T(8,128)(2,1)} %bitcast.10), custom_call_target="tpu_custom_call" | custom-call | flops 6291456 | bytes 4194304 | tf_op jit(solution)/shard_map/normalize/pallas_call | solution.py:26
  11.9 1.6 %collective-permute-done.13.beyond_ref = s32[8,128]{1,0:T(8,128)S(1)} collective-permute-done((s32[8,128]{1,0:T(8,128)S(1)}, s32[8,128]{1,0:T(8,128)S(1)}, u32[]{:S(2)}, u32[]{:S(2)}) %collective-permute-start.13) | collective-permute-done | bytes 4128 | tf_op jit(solution)/shard_map/ppermute | solution.py:521
  13.6 0.5 %pack_far.1 = (s32[8,128]{1,0:T(8,128)S(1)}, bf16[48,2048]{1,0:T(8,128)(2,1)S(1)}) custom-call(bf16[512,2048]{1,0:T(8,128)(2,1)S(1)} %normalize.1.x_ref, s32[8,128]{1,0:T(8,128)S(1)} %collective-permute-done.13.beyond_ref, s32[8,128]{1,0:T(8,128)S(1)} %get-tuple-element.115.core_list_ref), custom_call_target="tpu_custom_call" | custom-call | flops 100663296 | tf_op jit(solution)/shard_map/pack_far/pallas_call | solution.py:26
  14.1 1.4 %collective-permute-start.16 = (bf16[48,2048]{1,0:T(8,128)(2,1)S(1)}, bf16[48,2048]{1,0:T(8,128)(2,1)S(1)}, u32[]{:S(2)}, u32[]{:S(2)}) collective-permute-start(bf16[48,2048]{1,0:T(8,128)(2,1)S(1)} %get-tuple-element.116.x_ref), channel_id=1, source_target_pairs={{0,7},{1,2},{2,1},{3,4},{4,3},{5,6},{6,5},{7,0},{8,15},{9,10},{10,... | collective-permute-start | bytes 589832 | tf_op jit(solution)/shard_map/ppermute | solution.py:521
  15.5 0.0 collective-permute-start.14
  15.5 1.2 %collective-permute-done.14.refs_1_ = s32[8,128]{1,0:T(8,128)S(1)} collective-permute-done((s32[8,128]{1,0:T(8,128)S(1)}, s32[8,128]{1,0:T(8,128)S(1)}, u32[]{:S(2)}, u32[]{:S(2)}) %collective-permute-start.14) | collective-permute-done | bytes 4128 | tf_op jit(solution)/shard_map/ppermute | solution.py:524
  16.7 1.2 %serve_near.1 = (bf16[48,2048]{1,0:T(8,128)(2,1)S(1)}, bf16[128,2048]{1,0:T(8,128)(2,1)S(1)}, bf16[176,2048]{1,0:T(8,128)(2,1)S(1)}, bf16[80,2048]{1,0:T(8,128)(...) custom-call(bf16[512,2048]{1,0:T(8,128)(2,1)S(1)} %normalize.1.x_ref, ...), custom_call_target="tpu_custom_call" | custom-call | flops 805306368 | tf_op jit(solution)/shard_map/serve_near/pallas_call | solution.py:26
  17.9 0.2 collective-permute-start.15
  18.1 4.2 %collective-permute-done.16.far_ref = bf16[48,2048]{1,0:T(8,128)(2,1)S(1)} collective-permute-done((bf16[48,2048]{1,0:T(8,128)(2,1)S(1)}, bf16[48,2048]{1,0:T(8,128)(2,1)S(1)}, u32[]{:S(2)}, u32[]{:S(2)}) %collective-permute-start.16) | collective-permute-done | bytes 196640 | tf_op jit(solution)/shard_map/ppermute | solution.py:521
  22.3 0.3 unpack.5.base_ref
  22.6 0.0 collective-permute-done.15.core_ref
  22.6 0.3 combine.1
  22.9 1.6 %collective-permute-start.17 = (bf16[32,2048]{1,0:T(8,128)(2,1)S(1)}, bf16[32,2048]{1,0:T(8,128)(2,1)S(1)}, u32[]{:S(2)}, u32[]{:S(2)}) collective-permute-start(bf16[32,2048]{1,0:T(8,128)(2,1)S(1)} %get-tuple-element.126), channel_id=1, source_target_pairs={{0,24},{8,16},{16,8},{24,0},{1,25},{9,17},{17,9},{25,1},{2,26},{10... | collective-permute-start | bytes 393224 | tf_op jit(solution)/shard_map/ppermute | solution.py:515
  24.4 0.5 %collective-permute-start.18 = (bf16[32,2048]{1,0:T(8,128)(2,1)S(1)}, bf16[32,2048]{1,0:T(8,128)(2,1)S(1)}, u32[]{:S(2)}, u32[]{:S(2)}) collective-permute-start(bf16[32,2048]{1,0:T(8,128)(2,1)S(1)} %get-tuple-element.127), channel_id=1, source_target_pairs={{0,16},{8,24},{16,0},{24,8},{1,17},{9,25},{17,1},{25,9},{2,18},{10... | collective-permute-start | bytes 393224 | tf_op jit(solution)/shard_map/ppermute | solution.py:515
  25.0 1.5 %collective-permute-start.19 = (bf16[32,2048]{1,0:T(8,128)(2,1)S(1)}, bf16[32,2048]{1,0:T(8,128)(2,1)S(1)}, u32[]{:S(2)}, u32[]{:S(2)}) collective-permute-start(bf16[32,2048]{1,0:T(8,128)(2,1)S(1)} %get-tuple-element.128), channel_id=1, source_target_pairs={{0,8},{8,0},{16,24},{24,16},{1,9},{9,1},{17,25},{25,17},{2,10},{10... | collective-permute-start | bytes 393224 | tf_op jit(solution)/shard_map/ppermute | solution.py:515
  26.4 0.0 collective-permute-start.20
  26.4 4.5 %collective-permute-done.20.rest_5_ = s32[8,128]{1,0:T(8,128)S(1)} collective-permute-done((s32[8,128]{1,0:T(8,128)S(1)}, s32[8,128]{1,0:T(8,128)S(1)}, u32[]{:S(2)}, u32[]{:S(2)}) %collective-permute-start.20) | collective-permute-done | bytes 4128 | tf_op jit(solution)/shard_map/ppermute | solution.py:518
  30.9 0.0 collective-permute-done.17.rest_0_
  30.9 0.0 collective-permute-done.18.rest_1_
  30.9 0.0 collective-permute-done.19.rest_2_
  30.9 0.7 %mix_far.3 = (bf16[48,2048]{1,0:T(8,128)(2,1)S(1)}, s32[8,128]{1,0:T(8,128)S(1)}) custom-call(bf16[48,2048]{1,0:T(8,128)(2,1)S(1)} %get-tuple-element.116.x_ref, bf16[128,128]{1,0:T(8,128)(2,1)S(1)} %get-tuple-element.120.mask_ref, bf16[32,2048]{1,0:T(8,128)(2,1)S(1)} %collective-permute-done.17.rest_0_, ...), custom_call_target="tpu_custom_call" | custom-call | flops 50331648 | tf_op jit(solution)/shard_map/mix_far/pallas_call | solution.py:26
  31.6 1.4 %collective-permute-start.22 = (bf16[48,2048]{1,0:T(8,128)(2,1)S(1)}, bf16[48,2048]{1,0:T(8,128)(2,1)S(1)}, u32[]{:S(2)}, u32[]{:S(2)}) collective-permute-start(bf16[48,2048]{1,0:T(8,128)(2,1)S(1)} %get-tuple-element.136), channel_id=1, source_target_pairs={{0,7},{1,2},{2,1},{3,4},{4,3},{5,6},{6,5},{7,0},{8,15},{9,10},{10,... | collective-permute-start | bytes 589832 | tf_op jit(solution)/shard_map/ppermute | solution.py:521
  33.0 1.1 %mix_near.3 = (bf16[48,2048]{1,0:T(8,128)(2,1)S(1)}, bf16[128,2048]{1,0:T(8,128)(2,1)S(1)}) custom-call(bf16[176,2048]{1,0:T(8,128)(2,1)S(1)} %get-tuple-element.132.x_ref, bf16[176,128]{1,0:T(8,128)(2,1)S(1)} %get-tuple-element.133.mask_ref, bf16[32,2048]{1,0:T(8,128)(2,1)S(1)} %collective-permute-done.17.rest_0_, ...), custom_call_target="tpu_custom_call" | custom-call | flops 184549376 | tf_op jit(solution)/shard_map/mix_near/pallas_call | solution.py:26
  34.2 0.1 collective-permute-start.21
  34.2 2.5 %mix_whole_late.3.rest_4_.refs_0_ = bf16[512,2048]{1,0:T(8,128)(2,1)S(1)} custom-call(bf16[512,2048]{1,0:T(8,128)(2,1)S(1)} %normalize.1.x_ref, bf16[512,128]{1,0:T(8,128)(2,1)S(1)} %get-tuple-element.117.mask_ref, bf16[32,2048]{1,0:T(8,128)(2,1)S(1)} %collective-permute-done.17.rest_0_, bf16[32,2048]{1,0:T(8,128)(2,1)S(1)} %collective-permute-done.18.rest_1_, ...), custom_call_target="tpu_custom_call" | custom-call | flops 536870912 | tf_op jit(solution)/shard_map/mix_whole_late/pallas_call | solution.py:26
  36.8 2.5 %collective-permute-done.22.far_ref = bf16[48,2048]{1,0:T(8,128)(2,1)S(1)} collective-permute-done((bf16[48,2048]{1,0:T(8,128)(2,1)S(1)}, bf16[48,2048]{1,0:T(8,128)(2,1)S(1)}, u32[]{:S(2)}, u32[]{:S(2)}) %collective-permute-start.22) | collective-permute-done | bytes 196640 | tf_op jit(solution)/shard_map/ppermute | solution.py:521
  39.3 0.0 collective-permute-done.21.core_ref
  39.3 0.4 unpack_both.3
  39.7 1.5 %collective-permute-start.23 = (bf16[32,2048]{1,0:T(8,128)(2,1)S(1)}, bf16[32,2048]{1,0:T(8,128)(2,1)S(1)}, u32[]{:S(2)}, u32[]{:S(2)}) collective-permute-start(bf16[32,2048]{1,0:T(8,128)(2,1)S(1)} %get-tuple-element.137), channel_id=1, source_target_pairs={{0,24},{8,16},{16,8},{24,0},{1,25},{9,17},{17,9},{25,1},{2,26},{10... | collective-permute-start | bytes 393224 | tf_op jit(solution)/shard_map/ppermute | solution.py:515
  41.2 0.6 %collective-permute-start.24 = (bf16[32,2048]{1,0:T(8,128)(2,1)S(1)}, bf16[32,2048]{1,0:T(8,128)(2,1)S(1)}, u32[]{:S(2)}, u32[]{:S(2)}) collective-permute-start(bf16[32,2048]{1,0:T(8,128)(2,1)S(1)} %get-tuple-element.138), channel_id=1, source_target_pairs={{0,16},{8,24},{16,0},{24,8},{1,17},{9,25},{17,1},{25,9},{2,18},{10... | collective-permute-start | bytes 393224 | tf_op jit(solution)/shard_map/ppermute | solution.py:515
  41.7 1.5 %collective-permute-start.25 = (bf16[32,2048]{1,0:T(8,128)(2,1)S(1)}, bf16[32,2048]{1,0:T(8,128)(2,1)S(1)}, u32[]{:S(2)}, u32[]{:S(2)}) collective-permute-start(bf16[32,2048]{1,0:T(8,128)(2,1)S(1)} %get-tuple-element.139), channel_id=1, source_target_pairs={{0,8},{8,0},{16,24},{24,16},{1,9},{9,1},{17,25},{25,17},{2,10},{10... | collective-permute-start | bytes 393224 | tf_op jit(solution)/shard_map/ppermute | solution.py:515
  43.3 0.5 %slice.16 = s32[1,1]{1,0:T(1,128)} slice(s32[8,128]{1,0:T(8,128)S(1)} %get-tuple-element.131), slice={[0:1], [0:1]} | slice | bytes 8 | tf_op jit(solution)/shard_map/slice | solution.py:580
  44.4 0.1 mix_whole_early.3
  44.5 1.2 %collective-permute-done.23 = bf16[32,2048]{1,0:T(8,128)(2,1)S(1)} collective-permute-done((bf16[32,2048]{1,0:T(8,128)(2,1)S(1)}, bf16[32,2048]{1,0:T(8,128)(2,1)S(1)}, u32[]{:S(2)}, u32[]{:S(2)}) %collective-permute-start.23) | collective-permute-done | bytes 131104 | tf_op jit(solution)/shard_map/ppermute | solution.py:515
  45.7 1.3 %collective-permute-done.24 = bf16[32,2048]{1,0:T(8,128)(2,1)S(1)} collective-permute-done((bf16[32,2048]{1,0:T(8,128)(2,1)S(1)}, bf16[32,2048]{1,0:T(8,128)(2,1)S(1)}, u32[]{:S(2)}, u32[]{:S(2)}) %collective-permute-start.24) | collective-permute-done | bytes 131104 | tf_op jit(solution)/shard_map/ppermute | solution.py:515
  47.0 0.0 collective-permute-done.25
  47.0 3.2 %conditional.1 = (bf16[1,1,512,2048]{3,2,1,0:T(8,128)(2,1)}) conditional(s32[]{:T(128)} %bitcast.6, (bf16[512,2048]{1,0:T(8,128)(2,1)S(1)}, bf16[512,128]{1,0:T(8,128)(2,1)S(1)}, bf16[32,2048]{1,0:T(8,128)(2,1)S(1)}, bf16[32,2048]{1,0:T(8,128)(2,1)S(1)}, bf16[32,2048]{1,0:T(8,128)(2,1)S(1)}, /*index=5*/bf16[32,2048]{1,0:T(8,128)(2,1)S(1)}) %tuple.13, ...), branch_computations={%region_0.0_spmd, %region_1.0_spmd} | conditional | flops 36511809536 | bytes 88408472 | solution.py:580
  47.1 3.0 %mix.2 = bf16[512,2048]{1,0:T(8,128)(2,1)} custom-call(bf16[512,2048]{1,0:T(8,128)(2,1)S(1)} %get-tuple-element.53.x_ref, bf16[512,128]{1,0:T(8,128)(2,1)S(1)} %get-tuple-element.54.mask_ref, bf16[32,2048]{1,0:T(8,128)(2,1)S(1)} %get-tuple-element.55.rest_0_, bf16[32,2048]{1,0:T(8,128)(2,1)S(1)} %get-tuple-element.56.rest_1_, ...), custom_call_target="tpu_custom_call" | custom-call | flops 536870912 | bytes 4194304 | tf_op jit(solution)/shard_map/cond/branch_0_fun/mix/pallas_call | solution.py:26
Async XLA Ops:
  0.0 5.7 %collective-permute-start.12 = (s32[4,32]{1,0:T(4,128)}, s32[4,32]{1,0:T(4,128)S(1)}, u32[]{:S(2)}, u32[]{:S(2)}) collective-permute-start(s32[4,32]{1,0:T(4,128)} %bitcast.12), channel_id=1, source_target_pairs={{0,24},{8,16},{16,8},{24,0},{1,25},{9,17},{17,9},{25,1},{2,26},{10... | collective-permute-start | bytes 1544 | tf_op jit(solution)/shard_map/ppermute | solution.py:515
  3.9 3.8 %collective-permute-start.11 = (s32[4,32]{1,0:T(4,128)}, s32[4,32]{1,0:T(4,128)S(1)}, u32[]{:S(2)}, u32[]{:S(2)}) collective-permute-start(s32[4,32]{1,0:T(4,128)} %bitcast.13), channel_id=1, source_target_pairs={{0,16},{8,24},{16,0},{24,8},{1,17},{9,25},{17,1},{25,9},{2,18},{10... | collective-permute-start | bytes 1544 | tf_op jit(solution)/shard_map/ppermute | solution.py:515
  4.4 3.8 %collective-permute-start.10 = (s32[4,32]{1,0:T(4,128)}, s32[4,32]{1,0:T(4,128)S(1)}, u32[]{:S(2)}, u32[]{:S(2)}) collective-permute-start(s32[4,32]{1,0:T(4,128)} %bitcast.14), channel_id=1, source_target_pairs={{0,8},{8,0},{16,24},{24,16},{1,9},{9,1},{17,25},{25,17},{2,10},{10... | collective-permute-start | bytes 1544 | tf_op jit(solution)/shard_map/ppermute | solution.py:515
  8.7 4.9 %collective-permute-start.13 = (s32[8,128]{1,0:T(8,128)S(1)}, s32[8,128]{1,0:T(8,128)S(1)}, u32[]{:S(2)}, u32[]{:S(2)}) collective-permute-start(s32[8,128]{1,0:T(8,128)S(1)} %get-tuple-element.114), channel_id=1, source_target_pairs={{0,7},{1,2},{2,1},{3,4},{4,3},{5,6},{6,5},{7,0},{8,15},{9,10},{10,... | collective-permute-start | bytes 12296 | tf_op jit(solution)/shard_map/ppermute | solution.py:521
  14.1 8.2 %collective-permute-start.16 = (bf16[48,2048]{1,0:T(8,128)(2,1)S(1)}, bf16[48,2048]{1,0:T(8,128)(2,1)S(1)}, u32[]{:S(2)}, u32[]{:S(2)}) collective-permute-start(bf16[48,2048]{1,0:T(8,128)(2,1)S(1)} %get-tuple-element.116.x_ref), channel_id=1, source_target_pairs={{0,7},{1,2},{2,1},{3,4},{4,3},{5,6},{6,5},{7,0},{8,15},{9,10},{10,... | collective-permute-start | bytes 589832 | tf_op jit(solution)/shard_map/ppermute | solution.py:521
  15.5 1.2 %collective-permute-start.14 = (s32[8,128]{1,0:T(8,128)S(1)}, s32[8,128]{1,0:T(8,128)S(1)}, u32[]{:S(2)}, u32[]{:S(2)}) collective-permute-start(s32[8,128]{1,0:T(8,128)S(1)} %get-tuple-element.119.refs_0_), channel_id=1, source_target_pairs={{0,1},{1,0},{2,3},{3,2},{4,5},{5,4},{6,7},{7,6},{8,9},{9,8},{10,11... | collective-permute-start | bytes 12296 | tf_op jit(solution)/shard_map/ppermute | solution.py:524
  17.9 4.7 %collective-permute-start.15 = (bf16[48,2048]{1,0:T(8,128)(2,1)S(1)}, bf16[48,2048]{1,0:T(8,128)(2,1)S(1)}, u32[]{:S(2)}, u32[]{:S(2)}) collective-permute-start(bf16[48,2048]{1,0:T(8,128)(2,1)S(1)} %get-tuple-element.122), channel_id=1, source_target_pairs={{0,1},{1,0},{2,3},{3,2},{4,5},{5,4},{6,7},{7,6},{8,9},{9,8},{10,11... | collective-permute-start | bytes 589832 | tf_op jit(solution)/shard_map/ppermute | solution.py:524
  22.9 8.1 %collective-permute-start.17 = (bf16[32,2048]{1,0:T(8,128)(2,1)S(1)}, bf16[32,2048]{1,0:T(8,128)(2,1)S(1)}, u32[]{:S(2)}, u32[]{:S(2)}) collective-permute-start(bf16[32,2048]{1,0:T(8,128)(2,1)S(1)} %get-tuple-element.126), channel_id=1, source_target_pairs={{0,24},{8,16},{16,8},{24,0},{1,25},{9,17},{17,9},{25,1},{2,26},{10... | collective-permute-start | bytes 393224 | tf_op jit(solution)/shard_map/ppermute | solution.py:515
  24.4 6.5 %collective-permute-start.18 = (bf16[32,2048]{1,0:T(8,128)(2,1)S(1)}, bf16[32,2048]{1,0:T(8,128)(2,1)S(1)}, u32[]{:S(2)}, u32[]{:S(2)}) collective-permute-start(bf16[32,2048]{1,0:T(8,128)(2,1)S(1)} %get-tuple-element.127), channel_id=1, source_target_pairs={{0,16},{8,24},{16,0},{24,8},{1,17},{9,25},{17,1},{25,9},{2,18},{10... | collective-permute-start | bytes 393224 | tf_op jit(solution)/shard_map/ppermute | solution.py:515
  25.0 6.0 %collective-permute-start.19 = (bf16[32,2048]{1,0:T(8,128)(2,1)S(1)}, bf16[32,2048]{1,0:T(8,128)(2,1)S(1)}, u32[]{:S(2)}, u32[]{:S(2)}) collective-permute-start(bf16[32,2048]{1,0:T(8,128)(2,1)S(1)} %get-tuple-element.128), channel_id=1, source_target_pairs={{0,8},{8,0},{16,24},{24,16},{1,9},{9,1},{17,25},{25,17},{2,10},{10... | collective-permute-start | bytes 393224 | tf_op jit(solution)/shard_map/ppermute | solution.py:515
  26.4 4.5 %collective-permute-start.20 = (s32[8,128]{1,0:T(8,128)S(1)}, s32[8,128]{1,0:T(8,128)S(1)}, u32[]{:S(2)}, u32[]{:S(2)}) collective-permute-start(s32[8,128]{1,0:T(8,128)S(1)} %get-tuple-element.130.rest_4_), channel_id=1, source_target_pairs={{0,4},{1,5},{2,6},{3,7},{4,0},{5,1},{6,2},{7,3},{8,12},{9,13},{10,... | collective-permute-start | bytes 12296 | tf_op jit(solution)/shard_map/ppermute | solution.py:518
  31.6 7.7 %collective-permute-start.22 = (bf16[48,2048]{1,0:T(8,128)(2,1)S(1)}, bf16[48,2048]{1,0:T(8,128)(2,1)S(1)}, u32[]{:S(2)}, u32[]{:S(2)}) collective-permute-start(bf16[48,2048]{1,0:T(8,128)(2,1)S(1)} %get-tuple-element.136), channel_id=1, source_target_pairs={{0,7},{1,2},{2,1},{3,4},{4,3},{5,6},{6,5},{7,0},{8,15},{9,10},{10,... | collective-permute-start | bytes 589832 | tf_op jit(solution)/shard_map/ppermute | solution.py:521
  34.2 5.1 %collective-permute-start.21 = (bf16[48,2048]{1,0:T(8,128)(2,1)S(1)}, bf16[48,2048]{1,0:T(8,128)(2,1)S(1)}, u32[]{:S(2)}, u32[]{:S(2)}) collective-permute-start(bf16[48,2048]{1,0:T(8,128)(2,1)S(1)} %get-tuple-element.135), channel_id=1, source_target_pairs={{0,1},{1,0},{2,3},{3,2},{4,5},{5,4},{6,7},{7,6},{8,9},{9,8},{10,11... | collective-permute-start | bytes 589832 | tf_op jit(solution)/shard_map/ppermute | solution.py:524
  39.7 6.0 %collective-permute-start.23 = (bf16[32,2048]{1,0:T(8,128)(2,1)S(1)}, bf16[32,2048]{1,0:T(8,128)(2,1)S(1)}, u32[]{:S(2)}, u32[]{:S(2)}) collective-permute-start(bf16[32,2048]{1,0:T(8,128)(2,1)S(1)} %get-tuple-element.137), channel_id=1, source_target_pairs={{0,24},{8,16},{16,8},{24,0},{1,25},{9,17},{17,9},{25,1},{2,26},{10... | collective-permute-start | bytes 393224 | tf_op jit(solution)/shard_map/ppermute | solution.py:515
  41.2 5.9 %collective-permute-start.24 = (bf16[32,2048]{1,0:T(8,128)(2,1)S(1)}, bf16[32,2048]{1,0:T(8,128)(2,1)S(1)}, u32[]{:S(2)}, u32[]{:S(2)}) collective-permute-start(bf16[32,2048]{1,0:T(8,128)(2,1)S(1)} %get-tuple-element.138), channel_id=1, source_target_pairs={{0,16},{8,24},{16,0},{24,8},{1,17},{9,25},{17,1},{25,9},{2,18},{10... | collective-permute-start | bytes 393224 | tf_op jit(solution)/shard_map/ppermute | solution.py:515
  41.7 5.3 %collective-permute-start.25 = (bf16[32,2048]{1,0:T(8,128)(2,1)S(1)}, bf16[32,2048]{1,0:T(8,128)(2,1)S(1)}, u32[]{:S(2)}, u32[]{:S(2)}) collective-permute-start(bf16[32,2048]{1,0:T(8,128)(2,1)S(1)} %get-tuple-element.139), channel_id=1, source_target_pairs={{0,8},{8,0},{16,24},{24,16},{1,9},{9,1},{17,25},{25,17},{2,10},{10... | collective-permute-start | bytes 393224 | tf_op jit(solution)/shard_map/ppermute | solution.py:515

commit v21 on v20

--- a/solution.py
+++ b/solution.py
@@ -189,7 +189,7 @@
 def near_kernel(x_ref, mask_ref, beyond_ref, own_list_ref, *refs):
     told_ref, within_ref, *refs = refs
     core_ref, own_ref, near_ref, rest_far_ref, rest_core_ref, *refs = refs
-    far_mask_ref, core_mask_ref, near_mask_ref, most_ref, select = refs
+    far_mask_ref, core_mask_ref, near_mask_ref, far_turned_ref, most_ref, select = refs
     total, sent = own_ref.shape[0], core_ref.shape[0]
     rows = x_ref.shape[0]
     select[:total] = one_hot(within_ref[0:1], rows)
@@ -201,7 +201,9 @@
     own_ref[...] = fetched[total:]
     near_ref[sent:] = fetched[total:]
     pack = one_hot(beyond_ref[0:1], rows)
-    rest_far_ref[...] = take(pack[sent:], x_ref[...])
+    far = jnp.dot(pack, x_ref[...], preferred_element_type=jnp.float32)
+    rest_far_ref[...] = far[sent:].astype(jnp.bfloat16)
+    far_turned_ref[...] = far.T.astype(jnp.bfloat16)
     masks = take(select[...], mask_ref[...])
     core_mask_ref[...] = masks[:total]
     near_mask_ref[:sent] = masks[:sent]
@@ -226,6 +228,7 @@
             bf16(total, total),
             bf16(total, total),
             bf16(sent + total, total),
+            bf16(width, total),
             int32(8, LANES),
         ],
         x,
@@ -337,16 +340,18 @@
     return normalize(mixed).astype(jnp.bfloat16)
 
 
-def far_mix_kernel(servers, x_ref, mask_ref, *rest):
+def far_mix_kernel(servers, x_ref, turned_ref, mask_ref, *rest):
     parts, rest = rest[:servers], rest[servers:]
     *most_refs, out_ref, most_ref, buffer = rest
     most_ref[...] = functools.reduce(jnp.maximum, [ref[...] for ref in most_refs])
     fill(buffer, parts)
-    weights = weigh(x_ref[...], buffer[...], mask_ref[: x_ref.shape[0]])
+    rows, width = x_ref.shape
+    dots = jnp.dot(buffer[...], turned_ref[...], preferred_element_type=jnp.float32).T[:rows]
+    weights = cube(dots, width) * mask_ref[:rows]
     out_ref[...] = mix(x_ref[...], weights, buffer[...])
 
 
-def far_mix_call(x, mask, parts, mosts):
+def far_mix_call(x, turned, mask, parts, mosts):
     rows, width = x.shape
     total, servers = mask.shape[1], len(parts)
     return kernel_call(
@@ -354,6 +359,7 @@
         functools.partial(far_mix_kernel, servers),
         [bf16(rows, width), int32(*mosts[0].shape)],
         x,
+        turned,
         mask,
         *reversed(parts),
         *mosts,
@@ -425,13 +431,16 @@
     turned[...] = buffer[...].T
     for start in range(0, x_ref.shape[0], BLOCK):
         here = pl.ds(start, BLOCK)
-        dots = jnp.dot(x_ref[here], turned[...], preferred_element_type=jnp.float32)
-        weights = cube(dots, x_ref.shape[1]) * mask_ref[here]
-        whole[here] = mix(x_ref[here], weights, buffer[...])
-        for half in range(start, start + BLOCK, COPY):
-            rows = pl.ds(half, COPY)
+        if start % (2 * BLOCK) == 0:
+            two = pl.ds(start, 2 * BLOCK)
+            dots = jnp.dot(x_ref[two], turned[...], preferred_element_type=jnp.float32)
+            weights = cube(dots, x_ref.shape[1]) * mask_ref[two]
+        half = start % (2 * BLOCK)
+        whole[here] = mix(x_ref[here], weights[half : half + BLOCK], buffer[...])
+        for first in range(start, start + BLOCK, COPY):
+            rows = pl.ds(first, COPY)
             copy = pltpu.make_async_copy(
-                whole.at[rows], out_ref.at[rows], sems.at[half // COPY]
+                whole.at[rows], out_ref.at[rows], sems.at[first // COPY]
             )
             copy.start()
             copies.append(copy)
@@ -532,8 +541,8 @@
         most, parts = combine_call(expands[1], inside(core), base, most, servers)
         return most, turned(parts)
 
-    def next_round(x, mask, far, near, far_mask, near_mask, expands, parts, mosts):
-        far, most = far_mix_call(far, far_mask, parts, mosts)
+    def next_round(x, mask, far, near, far_turned, far_mask, near_mask, expands, parts, mosts):
+        far, most = far_mix_call(far, far_turned, far_mask, parts, mosts)
         core, own = near_mix_call(near, near_mask, parts)
         y = late_call(x, mask, parts)
         last = unpack_both_call(expands, across(far), inside(core), own, y, servers)
@@ -548,7 +557,7 @@
         near = jnp.concatenate([near[:sent], rest[1], near[sent:]], axis=0)
         near_mask = jnp.concatenate([masks[1], masks[2][sent:]], axis=0)
         y, _, last = next_round(
-            x, mask, far, near, masks[0], near_mask, expands, first, [most]
+            x, mask, far, near, masks[3], masks[0], near_mask, expands, first, [most]
         )
         return last_call(y, mask, last)
 
@@ -574,7 +583,7 @@
         mosts = [most, shift(most, known)]
         known *= 2
     y, most, last = next_round(
-        x, mask, far, near, masks[0], masks[2], expands, first, mosts
+        x, mask, far, near, masks[3], masks[0], masks[2], expands, first, mosts
     )
     state = x, y, mask, far, near, rest, masks, expands, most, first, last
     return lax.cond(most[0, 0] > sent, in_full, as_sent, *state)[None, None]

time: 50.6 us -> 50.4 us (level)
  no operation moved by 1% of the time
where the time goes in v21:
time: 50.4 us; the launch traced here: 50.2 us
  waiting for transfers between devices  19.4 us (38%)
  starting transfers between devices  16.1 us (32%)
  Pallas kernels  13 us (26%)
  between operations  0.96 us (2%)
  local copies, waits for them, and re-layouts  0.51 us (1%)
    pallas_call x13, Pallas kernels, kernel_call(): pl.pallas_call(kernel, out_shape=outs, scratch_shapes=scratch, compiler_p...  13 us
    ppermute x9, starting transfers between devices, turn(): return lax.ppermute(value, 'clus', [(c, c ^ d) for c in range(servers)])  11.6 us
    ppermute x3, waiting for transfers between devices, across(): return lax.ppermute(value, 'rep', beyond)  8.44 us
    ppermute x9, waiting for transfers between devices, turn(): return lax.ppermute(value, 'clus', [(c, c ^ d) for c in range(servers)])  5.26 us
    ppermute x1, waiting for transfers between devices, shift(): lax.ppermute(value, 'rep', [(g, (g + by) % groups) for g in range(groups)])  4.5 us
    ppermute x3, starting transfers between devices, across(): return lax.ppermute(value, 'rep', beyond)  4.2 us
    ppermute x3, waiting for transfers between devices, inside(): return lax.ppermute(value, 'rep', within)  1.17 us
  transfers between devices with their start and end apart: 16, of which 10 were waited for; matrix products, arithmetic and copies ran while one was open for 1% of the time, Pallas kernels for 16%

profile of v21, /device:TPU:0, one launch (start us, length us, event | category | flops | bytes accessed | tf_op | source)
XLA Modules:
  0.0 50.2 jit_solution(15088351663582619852)
XLA Ops:
  0.0 3.9 %collective-permute-start.12 = (s32[4,32]{1,0:T(4,128)}, s32[4,32]{1,0:T(4,128)S(1)}, u32[]{:S(2)}, u32[]{:S(2)}) collective-permute-start(s32[4,32]{1,0:T(4,128)} %bitcast.12), channel_id=1, source_target_pairs={{0,24},{8,16},{16,8},{24,0},{1,25},{9,17},{17,9},{25,1},{2,26},{10... | collective-permute-start | bytes 1544 | tf_op jit(solution)/shard_map/ppermute | solution.py:524
  3.9 0.5 %collective-permute-start.11 = (s32[4,32]{1,0:T(4,128)}, s32[4,32]{1,0:T(4,128)S(1)}, u32[]{:S(2)}, u32[]{:S(2)}) collective-permute-start(s32[4,32]{1,0:T(4,128)} %bitcast.13), channel_id=1, source_target_pairs={{0,16},{8,24},{16,0},{24,8},{1,17},{9,25},{17,1},{25,9},{2,18},{10... | collective-permute-start | bytes 1544 | tf_op jit(solution)/shard_map/ppermute | solution.py:524
  4.4 0.1 collective-permute-start.10
  4.5 1.0 %mask.1 = (bf16[512,128]{1,0:T(8,128)(2,1)S(1)}, s32[4,32]{1,0:T(4,128)S(1)}) custom-call(s32[10,1,512]{2,1,0:T(1,128)} %bitcast.11, s32[4,32]{1,0:T(4,128)} %bitcast.15), custom_call_target="tpu_custom_call" | custom-call | flops 1310720 | bytes 131072 | tf_op jit(solution)/shard_map/mask/pallas_call | solution.py:26
  5.5 0.2 collective-permute-done.12.refs_3_
  5.7 2.0 %collective-permute-done.11.refs_2_ = s32[4,32]{1,0:T(4,128)S(1)} collective-permute-done((s32[4,32]{1,0:T(4,128)}, s32[4,32]{1,0:T(4,128)S(1)}, u32[]{:S(2)}, u32[]{:S(2)}) %collective-permute-start.11) | collective-permute-done | bytes 544 | tf_op jit(solution)/shard_map/ppermute | solution.py:524
  7.7 0.5 %collective-permute-done.10.refs_1_ = s32[4,32]{1,0:T(4,128)S(1)} collective-permute-done((s32[4,32]{1,0:T(4,128)}, s32[4,32]{1,0:T(4,128)S(1)}, u32[]{:S(2)}, u32[]{:S(2)}) %collective-permute-start.10) | collective-permute-done | bytes 544 | tf_op jit(solution)/shard_map/ppermute | solution.py:524
  8.2 0.5 list.1
  8.7 1.4 %collective-permute-start.13 = (s32[8,128]{1,0:T(8,128)S(1)}, s32[8,128]{1,0:T(8,128)S(1)}, u32[]{:S(2)}, u32[]{:S(2)}) collective-permute-start(s32[8,128]{1,0:T(8,128)S(1)} %get-tuple-element.118), channel_id=1, source_target_pairs={{0,7},{1,2},{2,1},{3,4},{4,3},{5,6},{6,5},{7,0},{8,15},{9,10},{10,... | collective-permute-start | bytes 12296 | tf_op jit(solution)/shard_map/ppermute | solution.py:530
  10.1 1.9 %normalize.1.x_ref = bf16[512,2048]{1,0:T(8,128)(2,1)S(1)} custom-call(bf16[512,2048]{1,0:T(8,128)(2,1)} %bitcast.10), custom_call_target="tpu_custom_call" | custom-call | flops 6291456 | bytes 4194304 | tf_op jit(solution)/shard_map/normalize/pallas_call | solution.py:26
  11.9 1.6 %collective-permute-done.13.beyond_ref = s32[8,128]{1,0:T(8,128)S(1)} collective-permute-done((s32[8,128]{1,0:T(8,128)S(1)}, s32[8,128]{1,0:T(8,128)S(1)}, u32[]{:S(2)}, u32[]{:S(2)}) %collective-permute-start.13) | collective-permute-done | bytes 4128 | tf_op jit(solution)/shard_map/ppermute | solution.py:530
  13.6 0.5 %pack_far.1 = (s32[8,128]{1,0:T(8,128)S(1)}, bf16[48,2048]{1,0:T(8,128)(2,1)S(1)}) custom-call(bf16[512,2048]{1,0:T(8,128)(2,1)S(1)} %normalize.1.x_ref, s32[8,128]{1,0:T(8,128)S(1)} %collective-permute-done.13.beyond_ref, s32[8,128]{1,0:T(8,128)S(1)} %get-tuple-element.119.core_list_ref), custom_call_target="tpu_custom_call" | custom-call | flops 100663296 | tf_op jit(solution)/shard_map/pack_far/pallas_call | solution.py:26
  14.1 1.4 %collective-permute-start.16 = (bf16[48,2048]{1,0:T(8,128)(2,1)S(1)}, bf16[48,2048]{1,0:T(8,128)(2,1)S(1)}, u32[]{:S(2)}, u32[]{:S(2)}) collective-permute-start(bf16[48,2048]{1,0:T(8,128)(2,1)S(1)} %get-tuple-element.120.x_ref), channel_id=1, source_target_pairs={{0,7},{1,2},{2,1},{3,4},{4,3},{5,6},{6,5},{7,0},{8,15},{9,10},{10,... | collective-permute-start | bytes 589832 | tf_op jit(solution)/shard_map/ppermute | solution.py:530
  15.5 0.0 collective-permute-start.14
  15.5 1.2 %collective-permute-done.14.refs_1_ = s32[8,128]{1,0:T(8,128)S(1)} collective-permute-done((s32[8,128]{1,0:T(8,128)S(1)}, s32[8,128]{1,0:T(8,128)S(1)}, u32[]{:S(2)}, u32[]{:S(2)}) %collective-permute-start.14) | collective-permute-done | bytes 4128 | tf_op jit(solution)/shard_map/ppermute | solution.py:533
  16.7 1.1 %serve_near.1 = (bf16[48,2048]{1,0:T(8,128)(2,1)S(1)}, bf16[128,2048]{1,0:T(8,128)(2,1)S(1)}, bf16[176,2048]{1,0:T(8,128)(2,1)S(1)}, bf16[80,2048]{1,0:T(8,128)(...) custom-call(bf16[512,2048]{1,0:T(8,128)(2,1)S(1)} %normalize.1.x_ref, ...), custom_call_target="tpu_custom_call" | custom-call | flops 805306368 | tf_op jit(solution)/shard_map/serve_near/pallas_call | solution.py:26
  17.8 0.2 collective-permute-start.15
  18.0 4.3 %collective-permute-done.16.far_ref = bf16[48,2048]{1,0:T(8,128)(2,1)S(1)} collective-permute-done((bf16[48,2048]{1,0:T(8,128)(2,1)S(1)}, bf16[48,2048]{1,0:T(8,128)(2,1)S(1)}, u32[]{:S(2)}, u32[]{:S(2)}) %collective-permute-start.16) | collective-permute-done | bytes 196640 | tf_op jit(solution)/shard_map/ppermute | solution.py:530
  22.3 0.3 unpack.5.base_ref
  22.6 0.0 collective-permute-done.15.core_ref
  22.6 0.3 combine.1
  22.9 1.6 %collective-permute-start.17 = (bf16[32,2048]{1,0:T(8,128)(2,1)S(1)}, bf16[32,2048]{1,0:T(8,128)(2,1)S(1)}, u32[]{:S(2)}, u32[]{:S(2)}) collective-permute-start(bf16[32,2048]{1,0:T(8,128)(2,1)S(1)} %get-tuple-element.131), channel_id=1, source_target_pairs={{0,24},{8,16},{16,8},{24,0},{1,25},{9,17},{17,9},{25,1},{2,26},{10... | collective-permute-start | bytes 393224 | tf_op jit(solution)/shard_map/ppermute | solution.py:524
  24.4 0.5 %collective-permute-start.18 = (bf16[32,2048]{1,0:T(8,128)(2,1)S(1)}, bf16[32,2048]{1,0:T(8,128)(2,1)S(1)}, u32[]{:S(2)}, u32[]{:S(2)}) collective-permute-start(bf16[32,2048]{1,0:T(8,128)(2,1)S(1)} %get-tuple-element.132), channel_id=1, source_target_pairs={{0,16},{8,24},{16,0},{24,8},{1,17},{9,25},{17,1},{25,9},{2,18},{10... | collective-permute-start | bytes 393224 | tf_op jit(solution)/shard_map/ppermute | solution.py:524
  25.0 1.5 %collective-permute-start.19 = (bf16[32,2048]{1,0:T(8,128)(2,1)S(1)}, bf16[32,2048]{1,0:T(8,128)(2,1)S(1)}, u32[]{:S(2)}, u32[]{:S(2)}) collective-permute-start(bf16[32,2048]{1,0:T(8,128)(2,1)S(1)} %get-tuple-element.133), channel_id=1, source_target_pairs={{0,8},{8,0},{16,24},{24,16},{1,9},{9,1},{17,25},{25,17},{2,10},{10... | collective-permute-start | bytes 393224 | tf_op jit(solution)/shard_map/ppermute | solution.py:524
  26.4 0.0 collective-permute-start.20
  26.4 4.5 %collective-permute-done.20.rest_5_ = s32[8,128]{1,0:T(8,128)S(1)} collective-permute-done((s32[8,128]{1,0:T(8,128)S(1)}, s32[8,128]{1,0:T(8,128)S(1)}, u32[]{:S(2)}, u32[]{:S(2)}) %collective-permute-start.20) | collective-permute-done | bytes 4128 | tf_op jit(solution)/shard_map/ppermute | solution.py:527
  30.9 0.0 collective-permute-done.17.rest_0_
  30.9 0.0 collective-permute-done.18.rest_1_
  30.9 0.0 collective-permute-done.19.rest_2_
  30.9 0.6 %mix_far.3 = (bf16[48,2048]{1,0:T(8,128)(2,1)S(1)}, s32[8,128]{1,0:T(8,128)S(1)}) custom-call(bf16[48,2048]{1,0:T(8,128)(2,1)S(1)} %get-tuple-element.120.x_ref, bf16[2048,128]{1,0:T(8,128)(2,1)S(1)} %get-tuple-element.124.turned_ref, bf16[128,128]{1,0:T(8,128)(2,1)S(1)} %get-tuple-element.125.mask_ref, ...), custom_call_target="tpu_custom_call" | custom-call | flops 50331648 | tf_op jit(solution)/shard_map/mix_far/pallas_call | solution.py:26
  31.6 1.4 %collective-permute-start.22 = (bf16[48,2048]{1,0:T(8,128)(2,1)S(1)}, bf16[48,2048]{1,0:T(8,128)(2,1)S(1)}, u32[]{:S(2)}, u32[]{:S(2)}) collective-permute-start(bf16[48,2048]{1,0:T(8,128)(2,1)S(1)} %get-tuple-element.141), channel_id=1, source_target_pairs={{0,7},{1,2},{2,1},{3,4},{4,3},{5,6},{6,5},{7,0},{8,15},{9,10},{10,... | collective-permute-start | bytes 589832 | tf_op jit(solution)/shard_map/ppermute | solution.py:530
  33.0 1.1 %mix_near.3 = (bf16[48,2048]{1,0:T(8,128)(2,1)S(1)}, bf16[128,2048]{1,0:T(8,128)(2,1)S(1)}) custom-call(bf16[176,2048]{1,0:T(8,128)(2,1)S(1)} %get-tuple-element.137.x_ref, bf16[176,128]{1,0:T(8,128)(2,1)S(1)} %get-tuple-element.138.mask_ref, bf16[32,2048]{1,0:T(8,128)(2,1)S(1)} %collective-permute-done.17.rest_0_, ...), custom_call_target="tpu_custom_call" | custom-call | flops 184549376 | tf_op jit(solution)/shard_map/mix_near/pallas_call | solution.py:26
  34.1 0.1 collective-permute-start.21
  34.2 2.5 %mix_whole_late.3.rest_4_.refs_0_ = bf16[512,2048]{1,0:T(8,128)(2,1)S(1)} custom-call(bf16[512,2048]{1,0:T(8,128)(2,1)S(1)} %normalize.1.x_ref, bf16[512,128]{1,0:T(8,128)(2,1)S(1)} %get-tuple-element.121.mask_ref, bf16[32,2048]{1,0:T(8,128)(2,1)S(1)} %collective-permute-done.17.rest_0_, bf16[32,2048]{1,0:T(8,128)(2,1)S(1)} %collective-permute-done.18.rest_1_, ...), custom_call_target="tpu_custom_call" | custom-call | flops 536870912 | tf_op jit(solution)/shard_map/mix_whole_late/pallas_call | solution.py:26
  36.7 2.5 %collective-permute-done.22.far_ref = bf16[48,2048]{1,0:T(8,128)(2,1)S(1)} collective-permute-done((bf16[48,2048]{1,0:T(8,128)(2,1)S(1)}, bf16[48,2048]{1,0:T(8,128)(2,1)S(1)}, u32[]{:S(2)}, u32[]{:S(2)}) %collective-permute-start.22) | collective-permute-done | bytes 196640 | tf_op jit(solution)/shard_map/ppermute | solution.py:530
  39.3 0.0 collective-permute-done.21.core_ref
  39.3 0.4 unpack_both.3
  39.7 1.5 %collective-permute-start.23 = (bf16[32,2048]{1,0:T(8,128)(2,1)S(1)}, bf16[32,2048]{1,0:T(8,128)(2,1)S(1)}, u32[]{:S(2)}, u32[]{:S(2)}) collective-permute-start(bf16[32,2048]{1,0:T(8,128)(2,1)S(1)} %get-tuple-element.142), channel_id=1, source_target_pairs={{0,24},{8,16},{16,8},{24,0},{1,25},{9,17},{17,9},{25,1},{2,26},{10... | collective-permute-start | bytes 393224 | tf_op jit(solution)/shard_map/ppermute | solution.py:524
  41.1 0.6 %collective-permute-start.24 = (bf16[32,2048]{1,0:T(8,128)(2,1)S(1)}, bf16[32,2048]{1,0:T(8,128)(2,1)S(1)}, u32[]{:S(2)}, u32[]{:S(2)}) collective-permute-start(bf16[32,2048]{1,0:T(8,128)(2,1)S(1)} %get-tuple-element.143), channel_id=1, source_target_pairs={{0,16},{8,24},{16,0},{24,8},{1,17},{9,25},{17,1},{25,9},{2,18},{10... | collective-permute-start | bytes 393224 | tf_op jit(solution)/shard_map/ppermute | solution.py:524
  41.7 1.5 %collective-permute-start.25 = (bf16[32,2048]{1,0:T(8,128)(2,1)S(1)}, bf16[32,2048]{1,0:T(8,128)(2,1)S(1)}, u32[]{:S(2)}, u32[]{:S(2)}) collective-permute-start(bf16[32,2048]{1,0:T(8,128)(2,1)S(1)} %get-tuple-element.144), channel_id=1, source_target_pairs={{0,8},{8,0},{16,24},{24,16},{1,9},{9,1},{17,25},{25,17},{2,10},{10... | collective-permute-start | bytes 393224 | tf_op jit(solution)/shard_map/ppermute | solution.py:524
  43.2 0.5 %slice.16 = s32[1,1]{1,0:T(1,128)} slice(s32[8,128]{1,0:T(8,128)S(1)} %get-tuple-element.136), slice={[0:1], [0:1]} | slice | bytes 8 | tf_op jit(solution)/shard_map/slice | solution.py:589
  44.4 0.1 mix_whole_early.3
  44.5 1.2 %collective-permute-done.23 = bf16[32,2048]{1,0:T(8,128)(2,1)S(1)} collective-permute-done((bf16[32,2048]{1,0:T(8,128)(2,1)S(1)}, bf16[32,2048]{1,0:T(8,128)(2,1)S(1)}, u32[]{:S(2)}, u32[]{:S(2)}) %collective-permute-start.23) | collective-permute-done | bytes 131104 | tf_op jit(solution)/shard_map/ppermute | solution.py:524
  45.7 1.3 %collective-permute-done.24 = bf16[32,2048]{1,0:T(8,128)(2,1)S(1)} collective-permute-done((bf16[32,2048]{1,0:T(8,128)(2,1)S(1)}, bf16[32,2048]{1,0:T(8,128)(2,1)S(1)}, u32[]{:S(2)}, u32[]{:S(2)}) %collective-permute-start.24) | collective-permute-done | bytes 131104 | tf_op jit(solution)/shard_map/ppermute | solution.py:524
  47.0 0.0 collective-permute-done.25
  47.0 3.0 %conditional.1 = (bf16[1,1,512,2048]{3,2,1,0:T(8,128)(2,1)}) conditional(s32[]{:T(128)} %bitcast.6, (bf16[512,2048]{1,0:T(8,128)(2,1)S(1)}, bf16[512,128]{1,0:T(8,128)(2,1)S(1)}, bf16[32,2048]{1,0:T(8,128)(2,1)S(1)}, bf16[32,2048]{1,0:T(8,128)(2,1)S(1)}, bf16[32,2048]{1,0:T(8,128)(2,1)S(1)}, /*index=5*/bf16[32,2048]{1,0:T(8,128)(2,1)S(1)}) %tuple.13, ...), branch_computations={%region_0.0_spmd, %region_1.0_spmd} | conditional | flops 36511809536 | bytes 88408472 | solution.py:589
  47.0 2.7 %mix.2 = bf16[512,2048]{1,0:T(8,128)(2,1)} custom-call(bf16[512,2048]{1,0:T(8,128)(2,1)S(1)} %get-tuple-element.55.x_ref, bf16[512,128]{1,0:T(8,128)(2,1)S(1)} %get-tuple-element.56.mask_ref, bf16[32,2048]{1,0:T(8,128)(2,1)S(1)} %get-tuple-element.57.rest_0_, bf16[32,2048]{1,0:T(8,128)(2,1)S(1)} %get-tuple-element.58.rest_1_, ...), custom_call_target="tpu_custom_call" | custom-call | flops 536870912 | bytes 4194304 | tf_op jit(solution)/shard_map/cond/branch_0_fun/mix/pallas_call | solution.py:26
Async XLA Ops:
  0.0 5.7 %collective-permute-start.12 = (s32[4,32]{1,0:T(4,128)}, s32[4,32]{1,0:T(4,128)S(1)}, u32[]{:S(2)}, u32[]{:S(2)}) collective-permute-start(s32[4,32]{1,0:T(4,128)} %bitcast.12), channel_id=1, source_target_pairs={{0,24},{8,16},{16,8},{24,0},{1,25},{9,17},{17,9},{25,1},{2,26},{10... | collective-permute-start | bytes 1544 | tf_op jit(solution)/shard_map/ppermute | solution.py:524
  3.9 3.8 %collective-permute-start.11 = (s32[4,32]{1,0:T(4,128)}, s32[4,32]{1,0:T(4,128)S(1)}, u32[]{:S(2)}, u32[]{:S(2)}) collective-permute-start(s32[4,32]{1,0:T(4,128)} %bitcast.13), channel_id=1, source_target_pairs={{0,16},{8,24},{16,0},{24,8},{1,17},{9,25},{17,1},{25,9},{2,18},{10... | collective-permute-start | bytes 1544 | tf_op jit(solution)/shard_map/ppermute | solution.py:524
  4.4 3.8 %collective-permute-start.10 = (s32[4,32]{1,0:T(4,128)}, s32[4,32]{1,0:T(4,128)S(1)}, u32[]{:S(2)}, u32[]{:S(2)}) collective-permute-start(s32[4,32]{1,0:T(4,128)} %bitcast.14), channel_id=1, source_target_pairs={{0,8},{8,0},{16,24},{24,16},{1,9},{9,1},{17,25},{25,17},{2,10},{10... | collective-permute-start | bytes 1544 | tf_op jit(solution)/shard_map/ppermute | solution.py:524
  8.7 4.9 %collective-permute-start.13 = (s32[8,128]{1,0:T(8,128)S(1)}, s32[8,128]{1,0:T(8,128)S(1)}, u32[]{:S(2)}, u32[]{:S(2)}) collective-permute-start(s32[8,128]{1,0:T(8,128)S(1)} %get-tuple-element.118), channel_id=1, source_target_pairs={{0,7},{1,2},{2,1},{3,4},{4,3},{5,6},{6,5},{7,0},{8,15},{9,10},{10,... | collective-permute-start | bytes 12296 | tf_op jit(solution)/shard_map/ppermute | solution.py:530
  14.1 8.2 %collective-permute-start.16 = (bf16[48,2048]{1,0:T(8,128)(2,1)S(1)}, bf16[48,2048]{1,0:T(8,128)(2,1)S(1)}, u32[]{:S(2)}, u32[]{:S(2)}) collective-permute-start(bf16[48,2048]{1,0:T(8,128)(2,1)S(1)} %get-tuple-element.120.x_ref), channel_id=1, source_target_pairs={{0,7},{1,2},{2,1},{3,4},{4,3},{5,6},{6,5},{7,0},{8,15},{9,10},{10,... | collective-permute-start | bytes 589832 | tf_op jit(solution)/shard_map/ppermute | solution.py:530
  15.5 1.2 %collective-permute-start.14 = (s32[8,128]{1,0:T(8,128)S(1)}, s32[8,128]{1,0:T(8,128)S(1)}, u32[]{:S(2)}, u32[]{:S(2)}) collective-permute-start(s32[8,128]{1,0:T(8,128)S(1)} %get-tuple-element.123.refs_0_), channel_id=1, source_target_pairs={{0,1},{1,0},{2,3},{3,2},{4,5},{5,4},{6,7},{7,6},{8,9},{9,8},{10,11... | collective-permute-start | bytes 12296 | tf_op jit(solution)/shard_map/ppermute | solution.py:533
  17.8 4.8 %collective-permute-start.15 = (bf16[48,2048]{1,0:T(8,128)(2,1)S(1)}, bf16[48,2048]{1,0:T(8,128)(2,1)S(1)}, u32[]{:S(2)}, u32[]{:S(2)}) collective-permute-start(bf16[48,2048]{1,0:T(8,128)(2,1)S(1)} %get-tuple-element.127), channel_id=1, source_target_pairs={{0,1},{1,0},{2,3},{3,2},{4,5},{5,4},{6,7},{7,6},{8,9},{9,8},{10,11... | collective-permute-start | bytes 589832 | tf_op jit(solution)/shard_map/ppermute | solution.py:533
  22.9 8.1 %collective-permute-start.17 = (bf16[32,2048]{1,0:T(8,128)(2,1)S(1)}, bf16[32,2048]{1,0:T(8,128)(2,1)S(1)}, u32[]{:S(2)}, u32[]{:S(2)}) collective-permute-start(bf16[32,2048]{1,0:T(8,128)(2,1)S(1)} %get-tuple-element.131), channel_id=1, source_target_pairs={{0,24},{8,16},{16,8},{24,0},{1,25},{9,17},{17,9},{25,1},{2,26},{10... | collective-permute-start | bytes 393224 | tf_op jit(solution)/shard_map/ppermute | solution.py:524
  24.4 6.5 %collective-permute-start.18 = (bf16[32,2048]{1,0:T(8,128)(2,1)S(1)}, bf16[32,2048]{1,0:T(8,128)(2,1)S(1)}, u32[]{:S(2)}, u32[]{:S(2)}) collective-permute-start(bf16[32,2048]{1,0:T(8,128)(2,1)S(1)} %get-tuple-element.132), channel_id=1, source_target_pairs={{0,16},{8,24},{16,0},{24,8},{1,17},{9,25},{17,1},{25,9},{2,18},{10... | collective-permute-start | bytes 393224 | tf_op jit(solution)/shard_map/ppermute | solution.py:524
  25.0 6.0 %collective-permute-start.19 = (bf16[32,2048]{1,0:T(8,128)(2,1)S(1)}, bf16[32,2048]{1,0:T(8,128)(2,1)S(1)}, u32[]{:S(2)}, u32[]{:S(2)}) collective-permute-start(bf16[32,2048]{1,0:T(8,128)(2,1)S(1)} %get-tuple-element.133), channel_id=1, source_target_pairs={{0,8},{8,0},{16,24},{24,16},{1,9},{9,1},{17,25},{25,17},{2,10},{10... | collective-permute-start | bytes 393224 | tf_op jit(solution)/shard_map/ppermute | solution.py:524
  26.4 4.5 %collective-permute-start.20 = (s32[8,128]{1,0:T(8,128)S(1)}, s32[8,128]{1,0:T(8,128)S(1)}, u32[]{:S(2)}, u32[]{:S(2)}) collective-permute-start(s32[8,128]{1,0:T(8,128)S(1)} %get-tuple-element.135.rest_4_), channel_id=1, source_target_pairs={{0,4},{1,5},{2,6},{3,7},{4,0},{5,1},{6,2},{7,3},{8,12},{9,13},{10,... | collective-permute-start | bytes 12296 | tf_op jit(solution)/shard_map/ppermute | solution.py:527
  31.6 7.7 %collective-permute-start.22 = (bf16[48,2048]{1,0:T(8,128)(2,1)S(1)}, bf16[48,2048]{1,0:T(8,128)(2,1)S(1)}, u32[]{:S(2)}, u32[]{:S(2)}) collective-permute-start(bf16[48,2048]{1,0:T(8,128)(2,1)S(1)} %get-tuple-element.141), channel_id=1, source_target_pairs={{0,7},{1,2},{2,1},{3,4},{4,3},{5,6},{6,5},{7,0},{8,15},{9,10},{10,... | collective-permute-start | bytes 589832 | tf_op jit(solution)/shard_map/ppermute | solution.py:530
  34.1 5.1 %collective-permute-start.21 = (bf16[48,2048]{1,0:T(8,128)(2,1)S(1)}, bf16[48,2048]{1,0:T(8,128)(2,1)S(1)}, u32[]{:S(2)}, u32[]{:S(2)}) collective-permute-start(bf16[48,2048]{1,0:T(8,128)(2,1)S(1)} %get-tuple-element.140), channel_id=1, source_target_pairs={{0,1},{1,0},{2,3},{3,2},{4,5},{5,4},{6,7},{7,6},{8,9},{9,8},{10,11... | collective-permute-start | bytes 589832 | tf_op jit(solution)/shard_map/ppermute | solution.py:533
  39.7 6.0 %collective-permute-start.23 = (bf16[32,2048]{1,0:T(8,128)(2,1)S(1)}, bf16[32,2048]{1,0:T(8,128)(2,1)S(1)}, u32[]{:S(2)}, u32[]{:S(2)}) collective-permute-start(bf16[32,2048]{1,0:T(8,128)(2,1)S(1)} %get-tuple-element.142), channel_id=1, source_target_pairs={{0,24},{8,16},{16,8},{24,0},{1,25},{9,17},{17,9},{25,1},{2,26},{10... | collective-permute-start | bytes 393224 | tf_op jit(solution)/shard_map/ppermute | solution.py:524
  41.1 5.9 %collective-permute-start.24 = (bf16[32,2048]{1,0:T(8,128)(2,1)S(1)}, bf16[32,2048]{1,0:T(8,128)(2,1)S(1)}, u32[]{:S(2)}, u32[]{:S(2)}) collective-permute-start(bf16[32,2048]{1,0:T(8,128)(2,1)S(1)} %get-tuple-element.143), channel_id=1, source_target_pairs={{0,16},{8,24},{16,0},{24,8},{1,17},{9,25},{17,1},{25,9},{2,18},{10... | collective-permute-start | bytes 393224 | tf_op jit(solution)/shard_map/ppermute | solution.py:524
  41.7 5.3 %collective-permute-start.25 = (bf16[32,2048]{1,0:T(8,128)(2,1)S(1)}, bf16[32,2048]{1,0:T(8,128)(2,1)S(1)}, u32[]{:S(2)}, u32[]{:S(2)}) collective-permute-start(bf16[32,2048]{1,0:T(8,128)(2,1)S(1)} %get-tuple-element.144), channel_id=1, source_target_pairs={{0,8},{8,0},{16,24},{24,16},{1,9},{9,1},{17,25},{25,17},{2,10},{10... | collective-permute-start | bytes 393224 | tf_op jit(solution)/shard_map/ppermute | solution.py:524

commit v22 on v21

--- a/solution.py
+++ b/solution.py
@@ -341,9 +341,7 @@
 
 
 def far_mix_kernel(servers, x_ref, turned_ref, mask_ref, *rest):
-    parts, rest = rest[:servers], rest[servers:]
-    *most_refs, out_ref, most_ref, buffer = rest
-    most_ref[...] = functools.reduce(jnp.maximum, [ref[...] for ref in most_refs])
+    parts, (out_ref, buffer) = rest[:servers], rest[servers:]
     fill(buffer, parts)
     rows, width = x_ref.shape
     dots = jnp.dot(buffer[...], turned_ref[...], preferred_element_type=jnp.float32).T[:rows]
@@ -351,25 +349,26 @@
     out_ref[...] = mix(x_ref[...], weights, buffer[...])
 
 
-def far_mix_call(x, turned, mask, parts, mosts):
+def far_mix_call(x, turned, mask, parts):
     rows, width = x.shape
     total, servers = mask.shape[1], len(parts)
     return kernel_call(
         "mix_far",
         functools.partial(far_mix_kernel, servers),
-        [bf16(rows, width), int32(*mosts[0].shape)],
+        bf16(rows, width),
         x,
         turned,
         mask,
         *reversed(parts),
-        *mosts,
         flops=4 * total * rows * width,
         scratch=[pltpu.VMEM((total, width), jnp.bfloat16)],
     )
 
 
 def near_mix_kernel(servers, x_ref, mask_ref, *rest):
-    parts, (core_ref, own_ref, buffer) = rest[:servers], rest[servers:]
+    parts, rest = rest[:servers], rest[servers:]
+    *most_refs, core_ref, own_ref, most_ref, buffer = rest
+    most_ref[...] = functools.reduce(jnp.maximum, [ref[...] for ref in most_refs])
     fill(buffer, parts)
     weights = weigh(x_ref[...], buffer[...], mask_ref[...])
     mixed = mix(x_ref[...], weights, buffer[...])
@@ -377,16 +376,17 @@
     own_ref[...] = mixed[core_ref.shape[0] :]
 
 
-def near_mix_call(x, mask, parts):
+def near_mix_call(x, mask, parts, mosts):
     rows, width = x.shape
     total, servers = mask.shape[1], len(parts)
     return kernel_call(
         "mix_near",
         functools.partial(near_mix_kernel, servers),
-        [bf16(rows - total, width), bf16(total, width)],
+        [bf16(rows - total, width), bf16(total, width), int32(*mosts[0].shape)],
         x,
         mask,
         *reversed(parts),
+        *mosts,
         flops=4 * total * rows * width,
         scratch=[pltpu.VMEM((total, width), jnp.bfloat16)],
     )
@@ -542,8 +542,8 @@
         return most, turned(parts)
 
     def next_round(x, mask, far, near, far_turned, far_mask, near_mask, expands, parts, mosts):
-        far, most = far_mix_call(far, far_turned, far_mask, parts, mosts)
-        core, own = near_mix_call(near, near_mask, parts)
+        far = far_mix_call(far, far_turned, far_mask, parts)
+        core, own, most = near_mix_call(near, near_mask, parts, mosts)
         y = late_call(x, mask, parts)
         last = unpack_both_call(expands, across(far), inside(core), own, y, servers)
         return early_call(x, mask, parts, y), most, turned(last)

time: 50.4 us -> 50.4 us (level)
  waiting for transfers between devices: 19.4 us -> 18.7 us
  starting transfers between devices: 16.1 us -> 16.7 us
    ppermute x1, waiting for transfers between devices: 4.5 us -> 0.01 us  [shift(): lax.ppermute(value, 'rep', [(g, (g + by) % groups) for g in range(groups)])]
    ppermute x9, waiting for transfers between devices: 5.26 us -> 9.14 us  [turn(): return lax.ppermute(value, 'clus', [(c, c ^ d) for c in range(servers)])]
    ppermute x3, starting transfers between devices: 4.2 us -> 4.84 us  [across(): return lax.ppermute(value, 'rep', beyond)]
  transfers between devices with their start and end apart: 16 -> 16, of which waited for: 10 -> 12; matrix products, arithmetic and copies ran while one was open for 1% -> 1% of each run, Pallas kernels for 16% -> 17%
where the time goes in v22:
time: 50.4 us; the launch traced here: 50.2 us
  waiting for transfers between devices  18.7 us (37%)
  starting transfers between devices  16.7 us (33%)
  Pallas kernels  13 us (26%)
  between operations  0.95 us (2%)
  local copies, waits for them, and re-layouts  0.51 us (1%)
    pallas_call x13, Pallas kernels, kernel_call(): pl.pallas_call(kernel, out_shape=outs, scratch_shapes=scratch, compiler_p...  13 us
    ppermute x9, starting transfers between devices, turn(): return lax.ppermute(value, 'clus', [(c, c ^ d) for c in range(servers)])  11.6 us
    ppermute x9, waiting for transfers between devices, turn(): return lax.ppermute(value, 'clus', [(c, c ^ d) for c in range(servers)])  9.14 us
    ppermute x3, waiting for transfers between devices, across(): return lax.ppermute(value, 'rep', beyond)  8.43 us
    ppermute x3, starting transfers between devices, across(): return lax.ppermute(value, 'rep', beyond)  4.84 us
    ppermute x3, waiting for transfers between devices, inside(): return lax.ppermute(value, 'rep', within)  1.17 us
  transfers between devices with their start and end apart: 16, of which 12 were waited for; matrix products, arithmetic and copies ran while one was open for 1% of the time, Pallas kernels for 17%

profile of v22, /device:TPU:0, one launch (start us, length us, event | category | flops | bytes accessed | tf_op | source)
XLA Modules:
  0.0 50.2 jit_solution(3024594207902631048)
XLA Ops:
  0.0 3.9 %collective-permute-start.12 = (s32[4,32]{1,0:T(4,128)}, s32[4,32]{1,0:T(4,128)S(1)}, u32[]{:S(2)}, u32[]{:S(2)}) collective-permute-start(s32[4,32]{1,0:T(4,128)} %bitcast.12), channel_id=1, source_target_pairs={{0,24},{8,16},{16,8},{24,0},{1,25},{9,17},{17,9},{25,1},{2,26},{10... | collective-permute-start | bytes 1544 | tf_op jit(solution)/shard_map/ppermute | solution.py:524
  3.9 0.5 %collective-permute-start.11 = (s32[4,32]{1,0:T(4,128)}, s32[4,32]{1,0:T(4,128)S(1)}, u32[]{:S(2)}, u32[]{:S(2)}) collective-permute-start(s32[4,32]{1,0:T(4,128)} %bitcast.13), channel_id=1, source_target_pairs={{0,16},{8,24},{16,0},{24,8},{1,17},{9,25},{17,1},{25,9},{2,18},{10... | collective-permute-start | bytes 1544 | tf_op jit(solution)/shard_map/ppermute | solution.py:524
  4.4 0.1 collective-permute-start.10
  4.5 1.0 %mask.1 = (bf16[512,128]{1,0:T(8,128)(2,1)S(1)}, s32[4,32]{1,0:T(4,128)S(1)}) custom-call(s32[10,1,512]{2,1,0:T(1,128)} %bitcast.11, s32[4,32]{1,0:T(4,128)} %bitcast.15), custom_call_target="tpu_custom_call" | custom-call | flops 1310720 | bytes 131072 | tf_op jit(solution)/shard_map/mask/pallas_call | solution.py:26
  5.5 0.2 collective-permute-done.12.refs_3_
  5.7 2.0 %collective-permute-done.11.refs_2_ = s32[4,32]{1,0:T(4,128)S(1)} collective-permute-done((s32[4,32]{1,0:T(4,128)}, s32[4,32]{1,0:T(4,128)S(1)}, u32[]{:S(2)}, u32[]{:S(2)}) %collective-permute-start.11) | collective-permute-done | bytes 544 | tf_op jit(solution)/shard_map/ppermute | solution.py:524
  7.7 0.5 %collective-permute-done.10.refs_1_ = s32[4,32]{1,0:T(4,128)S(1)} collective-permute-done((s32[4,32]{1,0:T(4,128)}, s32[4,32]{1,0:T(4,128)S(1)}, u32[]{:S(2)}, u32[]{:S(2)}) %collective-permute-start.10) | collective-permute-done | bytes 544 | tf_op jit(solution)/shard_map/ppermute | solution.py:524
  8.2 0.5 list.1
  8.7 1.4 %collective-permute-start.13 = (s32[8,128]{1,0:T(8,128)S(1)}, s32[8,128]{1,0:T(8,128)S(1)}, u32[]{:S(2)}, u32[]{:S(2)}) collective-permute-start(s32[8,128]{1,0:T(8,128)S(1)} %get-tuple-element.117), channel_id=1, source_target_pairs={{0,7},{1,2},{2,1},{3,4},{4,3},{5,6},{6,5},{7,0},{8,15},{9,10},{10,... | collective-permute-start | bytes 12296 | tf_op jit(solution)/shard_map/ppermute | solution.py:530
  10.1 1.9 %normalize.1.x_ref = bf16[512,2048]{1,0:T(8,128)(2,1)S(1)} custom-call(bf16[512,2048]{1,0:T(8,128)(2,1)} %bitcast.10), custom_call_target="tpu_custom_call" | custom-call | flops 6291456 | bytes 4194304 | tf_op jit(solution)/shard_map/normalize/pallas_call | solution.py:26
  11.9 1.6 %collective-permute-done.13.beyond_ref = s32[8,128]{1,0:T(8,128)S(1)} collective-permute-done((s32[8,128]{1,0:T(8,128)S(1)}, s32[8,128]{1,0:T(8,128)S(1)}, u32[]{:S(2)}, u32[]{:S(2)}) %collective-permute-start.13) | collective-permute-done | bytes 4128 | tf_op jit(solution)/shard_map/ppermute | solution.py:530
  13.6 0.5 %pack_far.1 = (s32[8,128]{1,0:T(8,128)S(1)}, bf16[48,2048]{1,0:T(8,128)(2,1)S(1)}) custom-call(bf16[512,2048]{1,0:T(8,128)(2,1)S(1)} %normalize.1.x_ref, s32[8,128]{1,0:T(8,128)S(1)} %collective-permute-done.13.beyond_ref, s32[8,128]{1,0:T(8,128)S(1)} %get-tuple-element.119.core_list_ref), custom_call_target="tpu_custom_call" | custom-call | flops 100663296 | tf_op jit(solution)/shard_map/pack_far/pallas_call | solution.py:26
  14.1 1.4 %collective-permute-start.16 = (bf16[48,2048]{1,0:T(8,128)(2,1)S(1)}, bf16[48,2048]{1,0:T(8,128)(2,1)S(1)}, u32[]{:S(2)}, u32[]{:S(2)}) collective-permute-start(bf16[48,2048]{1,0:T(8,128)(2,1)S(1)} %get-tuple-element.126.x_ref), channel_id=1, source_target_pairs={{0,7},{1,2},{2,1},{3,4},{4,3},{5,6},{6,5},{7,0},{8,15},{9,10},{10,... | collective-permute-start | bytes 589832 | tf_op jit(solution)/shard_map/ppermute | solution.py:530
  15.5 0.0 collective-permute-start.14
  15.5 1.2 %collective-permute-done.14.refs_1_ = s32[8,128]{1,0:T(8,128)S(1)} collective-permute-done((s32[8,128]{1,0:T(8,128)S(1)}, s32[8,128]{1,0:T(8,128)S(1)}, u32[]{:S(2)}, u32[]{:S(2)}) %collective-permute-start.14) | collective-permute-done | bytes 4128 | tf_op jit(solution)/shard_map/ppermute | solution.py:533
  16.7 1.1 %serve_near.1 = (bf16[48,2048]{1,0:T(8,128)(2,1)S(1)}, bf16[128,2048]{1,0:T(8,128)(2,1)S(1)}, bf16[176,2048]{1,0:T(8,128)(2,1)S(1)}, bf16[80,2048]{1,0:T(8,128)(...) custom-call(bf16[512,2048]{1,0:T(8,128)(2,1)S(1)} %normalize.1.x_ref, ...), custom_call_target="tpu_custom_call" | custom-call | flops 805306368 | tf_op jit(solution)/shard_map/serve_near/pallas_call | solution.py:26
  17.8 0.2 collective-permute-start.15
  18.0 4.3 %collective-permute-done.16.far_ref = bf16[48,2048]{1,0:T(8,128)(2,1)S(1)} collective-permute-done((bf16[48,2048]{1,0:T(8,128)(2,1)S(1)}, bf16[48,2048]{1,0:T(8,128)(2,1)S(1)}, u32[]{:S(2)}, u32[]{:S(2)}) %collective-permute-start.16) | collective-permute-done | bytes 196640 | tf_op jit(solution)/shard_map/ppermute | solution.py:530
  22.3 0.3 unpack.5.base_ref
  22.6 0.0 collective-permute-done.15.core_ref
  22.6 0.3 combine.1
  22.9 1.6 %collective-permute-start.17 = (bf16[32,2048]{1,0:T(8,128)(2,1)S(1)}, bf16[32,2048]{1,0:T(8,128)(2,1)S(1)}, u32[]{:S(2)}, u32[]{:S(2)}) collective-permute-start(bf16[32,2048]{1,0:T(8,128)(2,1)S(1)} %get-tuple-element.129), channel_id=1, source_target_pairs={{0,24},{8,16},{16,8},{24,0},{1,25},{9,17},{17,9},{25,1},{2,26},{10... | collective-permute-start | bytes 393224 | tf_op jit(solution)/shard_map/ppermute | solution.py:524
  24.4 0.5 %collective-permute-start.18 = (bf16[32,2048]{1,0:T(8,128)(2,1)S(1)}, bf16[32,2048]{1,0:T(8,128)(2,1)S(1)}, u32[]{:S(2)}, u32[]{:S(2)}) collective-permute-start(bf16[32,2048]{1,0:T(8,128)(2,1)S(1)} %get-tuple-element.130), channel_id=1, source_target_pairs={{0,16},{8,24},{16,0},{24,8},{1,17},{9,25},{17,1},{25,9},{2,18},{10... | collective-permute-start | bytes 393224 | tf_op jit(solution)/shard_map/ppermute | solution.py:524
  25.0 1.5 %collective-permute-start.19 = (bf16[32,2048]{1,0:T(8,128)(2,1)S(1)}, bf16[32,2048]{1,0:T(8,128)(2,1)S(1)}, u32[]{:S(2)}, u32[]{:S(2)}) collective-permute-start(bf16[32,2048]{1,0:T(8,128)(2,1)S(1)} %get-tuple-element.131), channel_id=1, source_target_pairs={{0,8},{8,0},{16,24},{24,16},{1,9},{9,1},{17,25},{25,17},{2,10},{10... | collective-permute-start | bytes 393224 | tf_op jit(solution)/shard_map/ppermute | solution.py:524
  26.4 0.0 collective-permute-start.20
  26.4 2.5 %collective-permute-done.17.rest_0_ = bf16[32,2048]{1,0:T(8,128)(2,1)S(1)} collective-permute-done((bf16[32,2048]{1,0:T(8,128)(2,1)S(1)}, bf16[32,2048]{1,0:T(8,128)(2,1)S(1)}, u32[]{:S(2)}, u32[]{:S(2)}) %collective-permute-start.17) | collective-permute-done | bytes 131104 | tf_op jit(solution)/shard_map/ppermute | solution.py:524
  28.9 1.3 %collective-permute-done.18.rest_1_ = bf16[32,2048]{1,0:T(8,128)(2,1)S(1)} collective-permute-done((bf16[32,2048]{1,0:T(8,128)(2,1)S(1)}, bf16[32,2048]{1,0:T(8,128)(2,1)S(1)}, u32[]{:S(2)}, u32[]{:S(2)}) %collective-permute-start.18) | collective-permute-done | bytes 131104 | tf_op jit(solution)/shard_map/ppermute | solution.py:524
  30.2 0.1 collective-permute-done.19.rest_2_
  30.3 0.6 %mix_far.3 = bf16[48,2048]{1,0:T(8,128)(2,1)S(1)} custom-call(bf16[48,2048]{1,0:T(8,128)(2,1)S(1)} %get-tuple-element.126.x_ref, bf16[2048,128]{1,0:T(8,128)(2,1)S(1)} %get-tuple-element.137.turned_ref, bf16[128,128]{1,0:T(8,128)(2,1)S(1)} %get-tuple-element.138.mask_ref, bf16[32,2048]{1,0:T(8,128)(2,1)S(1)} %collective-permute-done.17.rest_0_, ...), custom_call_target="tpu_custom_call" | custom-call | flops 50331648 | tf_op jit(solution)/shard_map/mix_far/pallas_call | solution.py:26
  31.0 2.0 %collective-permute-start.22 = (bf16[48,2048]{1,0:T(8,128)(2,1)S(1)}, bf16[48,2048]{1,0:T(8,128)(2,1)S(1)}, u32[]{:S(2)}, u32[]{:S(2)}) collective-permute-start(bf16[48,2048]{1,0:T(8,128)(2,1)S(1)} %mix_far.3), channel_id=1, source_target_pairs={{0,7},{1,2},{2,1},{3,4},{4,3},{5,6},{6,5},{7,0},{8,15},{9,10},{10,... | collective-permute-start | bytes 589832 | tf_op jit(solution)/shard_map/ppermute | solution.py:530
  33.0 0.0 collective-permute-done.20.rest_5_
  33.0 1.1 %mix_near.3 = (bf16[48,2048]{1,0:T(8,128)(2,1)S(1)}, bf16[128,2048]{1,0:T(8,128)(2,1)S(1)}, s32[8,128]{1,0:T(8,128)S(1)}) custom-call(bf16[176,2048]{1,0:T(8,128)(2,1)S(1)} %get-tuple-element.121.x_ref, bf16[176,128]{1,0:T(8,128)(2,1)S(1)} %get-tuple-element.122.mask_ref, bf16[32,2048]{1,0:T(8,128)(2,1)S(1)} %collective-permute-done.17.rest_0_, ...), custom_call_target="tpu_custom_call" | custom-call | flops 184549376 | tf_op jit(solution)/shard_map/mix_near/pallas_call | solution.py:26
  34.1 0.1 collective-permute-start.21
  34.2 2.5 %mix_whole_late.3.rest_4_.refs_0_ = bf16[512,2048]{1,0:T(8,128)(2,1)S(1)} custom-call(bf16[512,2048]{1,0:T(8,128)(2,1)S(1)} %normalize.1.x_ref, bf16[512,128]{1,0:T(8,128)(2,1)S(1)} %get-tuple-element.115.mask_ref, bf16[32,2048]{1,0:T(8,128)(2,1)S(1)} %collective-permute-done.17.rest_0_, bf16[32,2048]{1,0:T(8,128)(2,1)S(1)} %collective-permute-done.18.rest_1_, ...), custom_call_target="tpu_custom_call" | custom-call | flops 536870912 | tf_op jit(solution)/shard_map/mix_whole_late/pallas_call | solution.py:26
  36.7 2.5 %collective-permute-done.22.far_ref = bf16[48,2048]{1,0:T(8,128)(2,1)S(1)} collective-permute-done((bf16[48,2048]{1,0:T(8,128)(2,1)S(1)}, bf16[48,2048]{1,0:T(8,128)(2,1)S(1)}, u32[]{:S(2)}, u32[]{:S(2)}) %collective-permute-start.22) | collective-permute-done | bytes 196640 | tf_op jit(solution)/shard_map/ppermute | solution.py:530
  39.2 0.0 collective-permute-done.21.core_ref
  39.3 0.4 unpack_both.3
  39.7 1.5 %collective-permute-start.23 = (bf16[32,2048]{1,0:T(8,128)(2,1)S(1)}, bf16[32,2048]{1,0:T(8,128)(2,1)S(1)}, u32[]{:S(2)}, u32[]{:S(2)}) collective-permute-start(bf16[32,2048]{1,0:T(8,128)(2,1)S(1)} %get-tuple-element.139), channel_id=1, source_target_pairs={{0,24},{8,16},{16,8},{24,0},{1,25},{9,17},{17,9},{25,1},{2,26},{10... | collective-permute-start | bytes 393224 | tf_op jit(solution)/shard_map/ppermute | solution.py:524
  41.1 0.6 %collective-permute-start.24 = (bf16[32,2048]{1,0:T(8,128)(2,1)S(1)}, bf16[32,2048]{1,0:T(8,128)(2,1)S(1)}, u32[]{:S(2)}, u32[]{:S(2)}) collective-permute-start(bf16[32,2048]{1,0:T(8,128)(2,1)S(1)} %get-tuple-element.140), channel_id=1, source_target_pairs={{0,16},{8,24},{16,0},{24,8},{1,17},{9,25},{17,1},{25,9},{2,18},{10... | collective-permute-start | bytes 393224 | tf_op jit(solution)/shard_map/ppermute | solution.py:524
  41.7 1.5 %collective-permute-start.25 = (bf16[32,2048]{1,0:T(8,128)(2,1)S(1)}, bf16[32,2048]{1,0:T(8,128)(2,1)S(1)}, u32[]{:S(2)}, u32[]{:S(2)}) collective-permute-start(bf16[32,2048]{1,0:T(8,128)(2,1)S(1)} %get-tuple-element.141), channel_id=1, source_target_pairs={{0,8},{8,0},{16,24},{24,16},{1,9},{9,1},{17,25},{25,17},{2,10},{10... | collective-permute-start | bytes 393224 | tf_op jit(solution)/shard_map/ppermute | solution.py:524
  43.2 0.5 %slice.16 = s32[1,1]{1,0:T(1,128)} slice(s32[8,128]{1,0:T(8,128)S(1)} %get-tuple-element.134), slice={[0:1], [0:1]} | slice | bytes 8 | tf_op jit(solution)/shard_map/slice | solution.py:589
  44.4 0.1 mix_whole_early.3
  44.5 1.2 %collective-permute-done.23 = bf16[32,2048]{1,0:T(8,128)(2,1)S(1)} collective-permute-done((bf16[32,2048]{1,0:T(8,128)(2,1)S(1)}, bf16[32,2048]{1,0:T(8,128)(2,1)S(1)}, u32[]{:S(2)}, u32[]{:S(2)}) %collective-permute-start.23) | collective-permute-done | bytes 131104 | tf_op jit(solution)/shard_map/ppermute | solution.py:524
  45.7 1.3 %collective-permute-done.24 = bf16[32,2048]{1,0:T(8,128)(2,1)S(1)} collective-permute-done((bf16[32,2048]{1,0:T(8,128)(2,1)S(1)}, bf16[32,2048]{1,0:T(8,128)(2,1)S(1)}, u32[]{:S(2)}, u32[]{:S(2)}) %collective-permute-start.24) | collective-permute-done | bytes 131104 | tf_op jit(solution)/shard_map/ppermute | solution.py:524
  47.0 0.0 collective-permute-done.25
  47.0 3.0 %conditional.1 = (bf16[1,1,512,2048]{3,2,1,0:T(8,128)(2,1)}) conditional(s32[]{:T(128)} %bitcast.6, (bf16[512,2048]{1,0:T(8,128)(2,1)S(1)}, bf16[512,128]{1,0:T(8,128)(2,1)S(1)}, bf16[32,2048]{1,0:T(8,128)(2,1)S(1)}, bf16[32,2048]{1,0:T(8,128)(2,1)S(1)}, bf16[32,2048]{1,0:T(8,128)(2,1)S(1)}, /*index=5*/bf16[32,2048]{1,0:T(8,128)(2,1)S(1)}) %tuple.13, ...), branch_computations={%region_0.0_spmd, %region_1.0_spmd} | conditional | flops 36511809536 | bytes 88408472 | solution.py:589
  47.0 2.8 %mix.2 = bf16[512,2048]{1,0:T(8,128)(2,1)} custom-call(bf16[512,2048]{1,0:T(8,128)(2,1)S(1)} %get-tuple-element.55.x_ref, bf16[512,128]{1,0:T(8,128)(2,1)S(1)} %get-tuple-element.56.mask_ref, bf16[32,2048]{1,0:T(8,128)(2,1)S(1)} %get-tuple-element.57.rest_0_, bf16[32,2048]{1,0:T(8,128)(2,1)S(1)} %get-tuple-element.58.rest_1_, ...), custom_call_target="tpu_custom_call" | custom-call | flops 536870912 | bytes 4194304 | tf_op jit(solution)/shard_map/cond/branch_0_fun/mix/pallas_call | solution.py:26
Async XLA Ops:
  0.0 5.7 %collective-permute-start.12 = (s32[4,32]{1,0:T(4,128)}, s32[4,32]{1,0:T(4,128)S(1)}, u32[]{:S(2)}, u32[]{:S(2)}) collective-permute-start(s32[4,32]{1,0:T(4,128)} %bitcast.12), channel_id=1, source_target_pairs={{0,24},{8,16},{16,8},{24,0},{1,25},{9,17},{17,9},{25,1},{2,26},{10... | collective-permute-start | bytes 1544 | tf_op jit(solution)/shard_map/ppermute | solution.py:524
  3.9 3.8 %collective-permute-start.11 = (s32[4,32]{1,0:T(4,128)}, s32[4,32]{1,0:T(4,128)S(1)}, u32[]{:S(2)}, u32[]{:S(2)}) collective-permute-start(s32[4,32]{1,0:T(4,128)} %bitcast.13), channel_id=1, source_target_pairs={{0,16},{8,24},{16,0},{24,8},{1,17},{9,25},{17,1},{25,9},{2,18},{10... | collective-permute-start | bytes 1544 | tf_op jit(solution)/shard_map/ppermute | solution.py:524
  4.4 3.8 %collective-permute-start.10 = (s32[4,32]{1,0:T(4,128)}, s32[4,32]{1,0:T(4,128)S(1)}, u32[]{:S(2)}, u32[]{:S(2)}) collective-permute-start(s32[4,32]{1,0:T(4,128)} %bitcast.14), channel_id=1, source_target_pairs={{0,8},{8,0},{16,24},{24,16},{1,9},{9,1},{17,25},{25,17},{2,10},{10... | collective-permute-start | bytes 1544 | tf_op jit(solution)/shard_map/ppermute | solution.py:524
  8.7 4.9 %collective-permute-start.13 = (s32[8,128]{1,0:T(8,128)S(1)}, s32[8,128]{1,0:T(8,128)S(1)}, u32[]{:S(2)}, u32[]{:S(2)}) collective-permute-start(s32[8,128]{1,0:T(8,128)S(1)} %get-tuple-element.117), channel_id=1, source_target_pairs={{0,7},{1,2},{2,1},{3,4},{4,3},{5,6},{6,5},{7,0},{8,15},{9,10},{10,... | collective-permute-start | bytes 12296 | tf_op jit(solution)/shard_map/ppermute | solution.py:530
  14.1 8.2 %collective-permute-start.16 = (bf16[48,2048]{1,0:T(8,128)(2,1)S(1)}, bf16[48,2048]{1,0:T(8,128)(2,1)S(1)}, u32[]{:S(2)}, u32[]{:S(2)}) collective-permute-start(bf16[48,2048]{1,0:T(8,128)(2,1)S(1)} %get-tuple-element.126.x_ref), channel_id=1, source_target_pairs={{0,7},{1,2},{2,1},{3,4},{4,3},{5,6},{6,5},{7,0},{8,15},{9,10},{10,... | collective-permute-start | bytes 589832 | tf_op jit(solution)/shard_map/ppermute | solution.py:530
  15.5 1.2 %collective-permute-start.14 = (s32[8,128]{1,0:T(8,128)S(1)}, s32[8,128]{1,0:T(8,128)S(1)}, u32[]{:S(2)}, u32[]{:S(2)}) collective-permute-start(s32[8,128]{1,0:T(8,128)S(1)} %get-tuple-element.120.refs_0_), channel_id=1, source_target_pairs={{0,1},{1,0},{2,3},{3,2},{4,5},{5,4},{6,7},{7,6},{8,9},{9,8},{10,11... | collective-permute-start | bytes 12296 | tf_op jit(solution)/shard_map/ppermute | solution.py:533
  17.8 4.8 %collective-permute-start.15 = (bf16[48,2048]{1,0:T(8,128)(2,1)S(1)}, bf16[48,2048]{1,0:T(8,128)(2,1)S(1)}, u32[]{:S(2)}, u32[]{:S(2)}) collective-permute-start(bf16[48,2048]{1,0:T(8,128)(2,1)S(1)} %get-tuple-element.124), channel_id=1, source_target_pairs={{0,1},{1,0},{2,3},{3,2},{4,5},{5,4},{6,7},{7,6},{8,9},{9,8},{10,11... | collective-permute-start | bytes 589832 | tf_op jit(solution)/shard_map/ppermute | solution.py:533
  22.9 6.0 %collective-permute-start.17 = (bf16[32,2048]{1,0:T(8,128)(2,1)S(1)}, bf16[32,2048]{1,0:T(8,128)(2,1)S(1)}, u32[]{:S(2)}, u32[]{:S(2)}) collective-permute-start(bf16[32,2048]{1,0:T(8,128)(2,1)S(1)} %get-tuple-element.129), channel_id=1, source_target_pairs={{0,24},{8,16},{16,8},{24,0},{1,25},{9,17},{17,9},{25,1},{2,26},{10... | collective-permute-start | bytes 393224 | tf_op jit(solution)/shard_map/ppermute | solution.py:524
  24.4 5.8 %collective-permute-start.18 = (bf16[32,2048]{1,0:T(8,128)(2,1)S(1)}, bf16[32,2048]{1,0:T(8,128)(2,1)S(1)}, u32[]{:S(2)}, u32[]{:S(2)}) collective-permute-start(bf16[32,2048]{1,0:T(8,128)(2,1)S(1)} %get-tuple-element.130), channel_id=1, source_target_pairs={{0,16},{8,24},{16,0},{24,8},{1,17},{9,25},{17,1},{25,9},{2,18},{10... | collective-permute-start | bytes 393224 | tf_op jit(solution)/shard_map/ppermute | solution.py:524
  25.0 5.4 %collective-permute-start.19 = (bf16[32,2048]{1,0:T(8,128)(2,1)S(1)}, bf16[32,2048]{1,0:T(8,128)(2,1)S(1)}, u32[]{:S(2)}, u32[]{:S(2)}) collective-permute-start(bf16[32,2048]{1,0:T(8,128)(2,1)S(1)} %get-tuple-element.131), channel_id=1, source_target_pairs={{0,8},{8,0},{16,24},{24,16},{1,9},{9,1},{17,25},{25,17},{2,10},{10... | collective-permute-start | bytes 393224 | tf_op jit(solution)/shard_map/ppermute | solution.py:524
  26.4 6.6 %collective-permute-start.20 = (s32[8,128]{1,0:T(8,128)S(1)}, s32[8,128]{1,0:T(8,128)S(1)}, u32[]{:S(2)}, u32[]{:S(2)}) collective-permute-start(s32[8,128]{1,0:T(8,128)S(1)} %get-tuple-element.133.rest_4_), channel_id=1, source_target_pairs={{0,4},{1,5},{2,6},{3,7},{4,0},{5,1},{6,2},{7,3},{8,12},{9,13},{10,... | collective-permute-start | bytes 12296 | tf_op jit(solution)/shard_map/ppermute | solution.py:527
  31.0 8.3 %collective-permute-start.22 = (bf16[48,2048]{1,0:T(8,128)(2,1)S(1)}, bf16[48,2048]{1,0:T(8,128)(2,1)S(1)}, u32[]{:S(2)}, u32[]{:S(2)}) collective-permute-start(bf16[48,2048]{1,0:T(8,128)(2,1)S(1)} %mix_far.3), channel_id=1, source_target_pairs={{0,7},{1,2},{2,1},{3,4},{4,3},{5,6},{6,5},{7,0},{8,15},{9,10},{10,... | collective-permute-start | bytes 589832 | tf_op jit(solution)/shard_map/ppermute | solution.py:530
  34.1 5.1 %collective-permute-start.21 = (bf16[48,2048]{1,0:T(8,128)(2,1)S(1)}, bf16[48,2048]{1,0:T(8,128)(2,1)S(1)}, u32[]{:S(2)}, u32[]{:S(2)}) collective-permute-start(bf16[48,2048]{1,0:T(8,128)(2,1)S(1)} %get-tuple-element.136), channel_id=1, source_target_pairs={{0,1},{1,0},{2,3},{3,2},{4,5},{5,4},{6,7},{7,6},{8,9},{9,8},{10,11... | collective-permute-start | bytes 589832 | tf_op jit(solution)/shard_map/ppermute | solution.py:533
  39.7 6.0 %collective-permute-start.23 = (bf16[32,2048]{1,0:T(8,128)(2,1)S(1)}, bf16[32,2048]{1,0:T(8,128)(2,1)S(1)}, u32[]{:S(2)}, u32[]{:S(2)}) collective-permute-start(bf16[32,2048]{1,0:T(8,128)(2,1)S(1)} %get-tuple-element.139), channel_id=1, source_target_pairs={{0,24},{8,16},{16,8},{24,0},{1,25},{9,17},{17,9},{25,1},{2,26},{10... | collective-permute-start | bytes 393224 | tf_op jit(solution)/shard_map/ppermute | solution.py:524
  41.1 5.9 %collective-permute-start.24 = (bf16[32,2048]{1,0:T(8,128)(2,1)S(1)}, bf16[32,2048]{1,0:T(8,128)(2,1)S(1)}, u32[]{:S(2)}, u32[]{:S(2)}) collective-permute-start(bf16[32,2048]{1,0:T(8,128)(2,1)S(1)} %get-tuple-element.140), channel_id=1, source_target_pairs={{0,16},{8,24},{16,0},{24,8},{1,17},{9,25},{17,1},{25,9},{2,18},{10... | collective-permute-start | bytes 393224 | tf_op jit(solution)/shard_map/ppermute | solution.py:524
  41.7 5.3 %collective-permute-start.25 = (bf16[32,2048]{1,0:T(8,128)(2,1)S(1)}, bf16[32,2048]{1,0:T(8,128)(2,1)S(1)}, u32[]{:S(2)}, u32[]{:S(2)}) collective-permute-start(bf16[32,2048]{1,0:T(8,128)(2,1)S(1)} %get-tuple-element.141), channel_id=1, source_target_pairs={{0,8},{8,0},{16,24},{24,16},{1,9},{9,1},{17,25},{25,17},{2,10},{10... | collective-permute-start | bytes 393224 | tf_op jit(solution)/shard_map/ppermute | solution.py:524

commit v23 on v22

--- a/solution.py
+++ b/solution.py
@@ -69,30 +69,43 @@
     )
 
 
-def mask_kernel(slot_cap, pick_hbm, wanted_hbm, mask_ref, wanted_ref, pick, sems):
+def keeps_back(groups):
+    return lax.axis_index("rep") == groups - 2
+
+
+def make_mask(slot_cap, pick):
+    total = lax.axis_size("clus") * slot_cap
+    shape = total, pick.shape[2]
+    slot = lax.broadcasted_iota(jnp.int32, shape, 0)
+    slot = slot ^ (lax.axis_index("clus") * slot_cap)
+    chosen = jnp.zeros(shape, jnp.float32)
+    for k in range(pick.shape[0]):
+        chosen = jnp.where(pick[k] == slot, 1.0, chosen)
+    return chosen.T.astype(jnp.bfloat16)
+
+
+def mask_kernel(groups, slot_cap, pick_hbm, wanted_hbm, mask_ref, wanted_ref, pick, sems):
     copies = [
         pltpu.make_async_copy(pick_hbm, pick, sems.at[0]),
         pltpu.make_async_copy(wanted_hbm, wanted_ref, sems.at[1]),
     ]
     for copy in copies:
         copy.start()
-    shape = mask_ref.shape[1], mask_ref.shape[0]
-    slot = lax.broadcasted_iota(jnp.int32, shape, 0)
-    slot = slot ^ (lax.axis_index("clus") * slot_cap)
-    chosen = jnp.zeros(shape, jnp.float32)
     copies[0].wait()
-    for k in range(pick.shape[0]):
-        chosen = jnp.where(pick[k] == slot, 1.0, chosen)
-    mask_ref[...] = chosen.T.astype(jnp.bfloat16)
+
+    @pl.when(jnp.logical_not(keeps_back(groups)))
+    def _():
+        mask_ref[...] = make_mask(slot_cap, pick)
+
     copies[1].wait()
 
 
-def mask_call(slots, wanted):
+def mask_call(groups, slots, wanted):
     count, _, rows = slots.shape
     total = wanted.size
     return kernel_call(
         "mask",
-        functools.partial(mask_kernel, wanted.shape[1]),
+        functools.partial(mask_kernel, groups, wanted.shape[1]),
         [bf16(rows, total), pltpu.VMEM(wanted.shape, jnp.int32)],
         slots,
         wanted,
@@ -101,6 +114,65 @@
         scratch=[pltpu.VMEM(slots.shape, jnp.int32), pltpu.SemaphoreType.DMA((2,))],
         mib=56,
         in_specs=[pl.BlockSpec(memory_space=pl.ANY)] * 2,
+    )
+
+
+def late_mask_kernel(groups, slot_cap, pick_hbm, _, base_ref, out_ref, pick, mask, sem):
+    @pl.when(keeps_back(groups))
+    def _():
+        copy = pltpu.make_async_copy(pick_hbm, pick, sem)
+        copy.start()
+        copy.wait()
+        mask[...] = make_mask(slot_cap, pick)
+        copy = pltpu.make_async_copy(mask, out_ref, sem)
+        copy.start()
+        copy.wait()
+
+
+def late_mask_call(groups, slot_cap, slots, mask, base):
+    any_space = pl.BlockSpec(memory_space=pl.ANY)
+    return kernel_call(
+        "mask_late",
+        functools.partial(late_mask_kernel, groups, slot_cap),
+        bf16(*mask.shape),
+        slots,
+        mask,
+        base,
+        flops=2 * mask.size,
+        scratch=[
+            pltpu.VMEM(slots.shape, jnp.int32),
+            pltpu.VMEM(mask.shape, jnp.bfloat16),
+            pltpu.SemaphoreType.DMA,
+        ],
+        in_specs=[any_space] * 3,
+        out_specs=any_space,
+        input_output_aliases={1: 0},
+    )
+
+
+def served_masks_kernel(mask_ref, beyond_ref, own_list_ref, within_ref, *out_refs):
+    far_ref, core_ref, near_ref = out_refs
+    rows, total = mask_ref.shape
+    sent = near_ref.shape[0] - total
+    mask = mask_ref[...]
+    far_ref[...] = take(one_hot(beyond_ref[0:1], rows), mask)
+    core = take(one_hot(within_ref[0:1], rows), mask)
+    core_ref[...] = core
+    near_ref[:sent] = core[:sent]
+    near_ref[sent:] = take(one_hot(own_list_ref[0:1], rows), mask)
+
+
+def served_masks_call(mask, beyond, own_list, within, sent):
+    rows, total = mask.shape
+    return kernel_call(
+        "served_masks",
+        served_masks_kernel,
+        [bf16(total, total), bf16(total, total), bf16(sent + total, total)],
+        mask,
+        beyond,
+        own_list,
+        within,
+        flops=6 * total * rows * total,
     )
 
 
@@ -186,10 +258,10 @@
     )
 
 
-def near_kernel(x_ref, mask_ref, beyond_ref, own_list_ref, *refs):
+def near_kernel(x_ref, beyond_ref, own_list_ref, *refs):
     told_ref, within_ref, *refs = refs
     core_ref, own_ref, near_ref, rest_far_ref, rest_core_ref, *refs = refs
-    far_mask_ref, core_mask_ref, near_mask_ref, far_turned_ref, most_ref, select = refs
+    far_turned_ref, most_ref, select = refs
     total, sent = own_ref.shape[0], core_ref.shape[0]
     rows = x_ref.shape[0]
     select[:total] = one_hot(within_ref[0:1], rows)
@@ -204,18 +276,13 @@
     far = jnp.dot(pack, x_ref[...], preferred_element_type=jnp.float32)
     rest_far_ref[...] = far[sent:].astype(jnp.bfloat16)
     far_turned_ref[...] = far.T.astype(jnp.bfloat16)
-    masks = take(select[...], mask_ref[...])
-    core_mask_ref[...] = masks[:total]
-    near_mask_ref[:sent] = masks[:sent]
-    near_mask_ref[sent:] = masks[total:]
-    far_mask_ref[...] = take(pack, mask_ref[...])
     most = jnp.maximum(told_ref[...], within_ref[...])
     most_ref[...] = jnp.broadcast_to(most[1:2, :LANES], most_ref.shape)
 
 
-def near_call(x, mask, beyond, own_list, told, within, sent):
+def near_call(x, beyond, own_list, told, within, sent):
     rows, width = x.shape
-    total = mask.shape[1]
+    total = beyond.shape[1]
     return kernel_call(
         "serve_near",
         near_kernel,
@@ -225,14 +292,10 @@
             bf16(sent + total, width),
             bf16(total - sent, width),
             bf16(total - sent, width),
-            bf16(total, total),
-            bf16(total, total),
-            bf16(sent + total, total),
             bf16(width, total),
             int32(8, LANES),
         ],
         x,
-        mask,
         beyond,
         own_list,
         told,
@@ -268,7 +331,7 @@
     )
 
 
-def combine_kernel(expand_ref, core_ref, base_ref, most_ref, out_most_ref, *out_refs):
+def combine_kernel(expand_ref, core_ref, base_ref, most_ref, _, out_most_ref, *out_refs):
     out_most_ref[...] = most_ref[...]
     cap, sent = out_refs[0].shape[0], core_ref.shape[0]
     rows = jnp.dot(expand_ref[:, :sent], core_ref[...], preferred_element_type=jnp.float32)
@@ -277,7 +340,7 @@
         out[...] = rows[d * cap : (d + 1) * cap]
 
 
-def combine_call(expand, core, base, most, servers):
+def combine_call(expand, core, base, most, after, servers):
     total, width = base.shape
     most, *parts = kernel_call(
         "combine",
@@ -287,7 +350,10 @@
         core,
         base,
         most,
+        after,
         flops=2 * total * core.shape[0] * width,
+        in_specs=[pl.BlockSpec(memory_space=pltpu.VMEM)] * 4
+        + [pl.BlockSpec(memory_space=pl.ANY)],
     )
     return most, parts
 
@@ -536,11 +602,6 @@
         got = {d: turn(parts[d], d) for d in reversed(range(1, servers))}
         return [parts[0]] + [got[d] for d in range(1, servers)]
 
-    def exchange(expands, far, core, own, most):
-        base = unpack_call(expands[0], across(far), own)
-        most, parts = combine_call(expands[1], inside(core), base, most, servers)
-        return most, turned(parts)
-
     def next_round(x, mask, far, near, far_turned, far_mask, near_mask, expands, parts, mosts):
         far = far_mix_call(far, far_turned, far_mask, parts)
         core, own, most = near_mix_call(near, near_mask, parts, mosts)
@@ -565,18 +626,23 @@
         return last_call(y, mask, last)
 
     asked = {d: turn(wanted, d) for d in reversed(range(1, servers))}
-    mask, held = mask_call(pick.transpose(0, 3, 1, 2)[0], wanted)
+    slots = pick.transpose(0, 3, 1, 2)[0]
+    mask, held = mask_call(groups, slots, wanted)
     own_list, far_list, core_list, *expands = list_call(
         [held] + [asked[d] for d in range(1, servers)], rows
     )
     beyond_list = across(far_list)
     x = normalize_call(descriptors[0, 0])
     told, far = far_call(x, beyond_list, core_list, sent)
-    core, own, near, *others, most = near_call(
-        x, mask, beyond_list, own_list, told, inside(told), sent
-    )
-    rest, masks = others[:2], others[2:]
-    most, first = exchange(expands, far, core, own, most)
+    within_list = inside(told)
+    core, own, near, *rest, far_turned, most = near_call(
+        x, beyond_list, own_list, told, within_list, sent
+    )
+    base = unpack_call(expands[0], across(far), own)
+    mask = late_mask_call(groups, cap, slots, mask, base)
+    most, first = combine_call(expands[1], inside(core), base, most, mask, servers)
+    first = turned(first)
+    masks = *served_masks_call(mask, beyond_list, own_list, within_list, sent), far_turned
     mosts, known = [most], 4
     while known < groups:
         most = functools.reduce(jnp.maximum, mosts)

time: 50.4 us -> 50.6 us (level)
    ppermute x3, waiting for transfers between devices: 8.43 us -> 8.94 us  [across(): return lax.ppermute(value, 'rep', beyond)]
    pallas_call x13 -> x15, Pallas kernels: 13 us -> 13.3 us  [kernel_call(): pl.pallas_call(kernel, out_shape=outs, scratch_shapes=scratch, compiler_p...]
  transfers between devices with their start and end apart: 16 -> 16, of which waited for: 12 -> 12; matrix products, arithmetic and copies ran while one was open for 1% -> 1% of each run, Pallas kernels for 17% -> 18%
where the time goes in v23:
time: 50.6 us; the launch traced here: 50.4 us
  waiting for transfers between devices  18.8 us (37%)
  starting transfers between devices  16.3 us (32%)
  Pallas kernels  13.3 us (26%)
  local copies, waits for them, and re-layouts  0.96 us (2%)
  between operations  0.96 us (2%)
    pallas_call x15, Pallas kernels, kernel_call(): pl.pallas_call(kernel, out_shape=outs, scratch_shapes=scratch, compiler_p...  13.3 us
    ppermute x9, starting transfers between devices, turn(): return lax.ppermute(value, 'clus', [(c, c ^ d) for c in range(servers)])  11.6 us
    ppermute x3, waiting for transfers between devices, across(): return lax.ppermute(value, 'rep', beyond)  8.94 us
    ppermute x9, waiting for transfers between devices, turn(): return lax.ppermute(value, 'clus', [(c, c ^ d) for c in range(servers)])  8.73 us
    ppermute x3, starting transfers between devices, across(): return lax.ppermute(value, 'rep', beyond)  4.35 us
    ppermute x3, waiting for transfers between devices, inside(): return lax.ppermute(value, 'rep', within)  1.17 us
  transfers between devices with their start and end apart: 16, of which 12 were waited for; matrix products, arithmetic and copies ran while one was open for 1% of the time, Pallas kernels for 18%

profile of v23, /device:TPU:0, one launch (start us, length us, event | category | flops | bytes accessed | tf_op | source)
XLA Modules:
  0.0 50.4 jit_solution(8055702944631506778)
XLA Ops:
  0.0 3.9 %collective-permute-start.12 = (s32[4,32]{1,0:T(4,128)}, s32[4,32]{1,0:T(4,128)S(1)}, u32[]{:S(2)}, u32[]{:S(2)}) collective-permute-start(s32[4,32]{1,0:T(4,128)} %bitcast.13), channel_id=1, source_target_pairs={{0,24},{8,16},{16,8},{24,0},{1,25},{9,17},{17,9},{25,1},{2,26},{10... | collective-permute-start | bytes 1544 | tf_op jit(solution)/shard_map/ppermute | solution.py:590
  3.9 0.5 %collective-permute-start.11 = (s32[4,32]{1,0:T(4,128)}, s32[4,32]{1,0:T(4,128)S(1)}, u32[]{:S(2)}, u32[]{:S(2)}) collective-permute-start(s32[4,32]{1,0:T(4,128)} %bitcast.14), channel_id=1, source_target_pairs={{0,16},{8,24},{16,0},{24,8},{1,17},{9,25},{17,1},{25,9},{2,18},{10... | collective-permute-start | bytes 1544 | tf_op jit(solution)/shard_map/ppermute | solution.py:590
  4.4 0.1 collective-permute-start.10
  4.5 1.0 %mask.1 = (bf16[512,128]{1,0:T(8,128)(2,1)S(1)}, s32[4,32]{1,0:T(4,128)S(1)}) custom-call(s32[10,1,512]{2,1,0:T(1,128)} %bitcast.8, s32[4,32]{1,0:T(4,128)} %bitcast.16), custom_call_target="tpu_custom_call" | custom-call | flops 1310720 | bytes 131072 | tf_op jit(solution)/shard_map/mask/pallas_call | solution.py:26
  5.5 0.2 collective-permute-done.12.refs_3_
  5.7 2.0 %collective-permute-done.11.refs_2_ = s32[4,32]{1,0:T(4,128)S(1)} collective-permute-done((s32[4,32]{1,0:T(4,128)}, s32[4,32]{1,0:T(4,128)S(1)}, u32[]{:S(2)}, u32[]{:S(2)}) %collective-permute-start.11) | collective-permute-done | bytes 544 | tf_op jit(solution)/shard_map/ppermute | solution.py:590
  7.7 0.5 %collective-permute-done.10.refs_1_ = s32[4,32]{1,0:T(4,128)S(1)} collective-permute-done((s32[4,32]{1,0:T(4,128)}, s32[4,32]{1,0:T(4,128)S(1)}, u32[]{:S(2)}, u32[]{:S(2)}) %collective-permute-start.10) | collective-permute-done | bytes 544 | tf_op jit(solution)/shard_map/ppermute | solution.py:590
  8.2 0.5 list.1
  8.7 1.4 %collective-permute-start.13 = (s32[8,128]{1,0:T(8,128)S(1)}, s32[8,128]{1,0:T(8,128)S(1)}, u32[]{:S(2)}, u32[]{:S(2)}) collective-permute-start(s32[8,128]{1,0:T(8,128)S(1)} %get-tuple-element.116), channel_id=1, source_target_pairs={{0,7},{1,2},{2,1},{3,4},{4,3},{5,6},{6,5},{7,0},{8,15},{9,10},{10,... | collective-permute-start | bytes 12296 | tf_op jit(solution)/shard_map/ppermute | solution.py:596
  10.1 1.9 %normalize.1.x_ref = bf16[512,2048]{1,0:T(8,128)(2,1)S(1)} custom-call(bf16[512,2048]{1,0:T(8,128)(2,1)} %bitcast.12), custom_call_target="tpu_custom_call" | custom-call | flops 6291456 | bytes 4194304 | tf_op jit(solution)/shard_map/normalize/pallas_call | solution.py:26
  11.9 1.6 %collective-permute-done.13.beyond_ref = s32[8,128]{1,0:T(8,128)S(1)} collective-permute-done((s32[8,128]{1,0:T(8,128)S(1)}, s32[8,128]{1,0:T(8,128)S(1)}, u32[]{:S(2)}, u32[]{:S(2)}) %collective-permute-start.13) | collective-permute-done | bytes 4128 | tf_op jit(solution)/shard_map/ppermute | solution.py:596
  13.6 0.5 %pack_far.1 = (s32[8,128]{1,0:T(8,128)S(1)}, bf16[48,2048]{1,0:T(8,128)(2,1)S(1)}) custom-call(bf16[512,2048]{1,0:T(8,128)(2,1)S(1)} %normalize.1.x_ref, s32[8,128]{1,0:T(8,128)S(1)} %collective-permute-done.13.beyond_ref, s32[8,128]{1,0:T(8,128)S(1)} %get-tuple-element.118.core_list_ref), custom_call_target="tpu_custom_call" | custom-call | flops 100663296 | tf_op jit(solution)/shard_map/pack_far/pallas_call | solution.py:26
  14.1 1.4 %collective-permute-start.15 = (bf16[48,2048]{1,0:T(8,128)(2,1)S(1)}, bf16[48,2048]{1,0:T(8,128)(2,1)S(1)}, u32[]{:S(2)}, u32[]{:S(2)}) collective-permute-start(bf16[48,2048]{1,0:T(8,128)(2,1)S(1)} %get-tuple-element.123.x_ref), channel_id=1, source_target_pairs={{0,7},{1,2},{2,1},{3,4},{4,3},{5,6},{6,5},{7,0},{8,15},{9,10},{10,... | collective-permute-start | bytes 589832 | tf_op jit(solution)/shard_map/ppermute | solution.py:596
  15.5 0.0 collective-permute-start.14
  15.5 1.2 %collective-permute-done.14.refs_1_.within_ref = s32[8,128]{1,0:T(8,128)S(1)} collective-permute-done((s32[8,128]{1,0:T(8,128)S(1)}, s32[8,128]{1,0:T(8,128)S(1)}, u32[]{:S(2)}, u32[]{:S(2)}) %collective-permute-start.14) | collective-permute-done | bytes 4128 | tf_op jit(solution)/shard_map/ppermute | solution.py:599
  16.7 1.1 %serve_near.1 = (bf16[48,2048]{1,0:T(8,128)(2,1)S(1)}, bf16[128,2048]{1,0:T(8,128)(2,1)S(1)}, bf16[176,2048]{1,0:T(8,128)(2,1)S(1)}, bf16[80,2048]{1,0:T(8,128)(...) custom-call(bf16[512,2048]{1,0:T(8,128)(2,1)S(1)} %normalize.1.x_ref, ...), custom_call_target="tpu_custom_call" | custom-call | flops 805306368 | tf_op jit(solution)/shard_map/serve_near/pallas_call | solution.py:26
  17.8 0.2 collective-permute-start.16
  18.0 4.3 %collective-permute-done.15.far_ref = bf16[48,2048]{1,0:T(8,128)(2,1)S(1)} collective-permute-done((bf16[48,2048]{1,0:T(8,128)(2,1)S(1)}, bf16[48,2048]{1,0:T(8,128)(2,1)S(1)}, u32[]{:S(2)}, u32[]{:S(2)}) %collective-permute-start.15) | collective-permute-done | bytes 196640 | tf_op jit(solution)/shard_map/ppermute | solution.py:596
  22.3 0.3 unpack.5.base_ref
  22.6 0.4 copy-done
  23.1 0.0 collective-permute-done.16.core_ref
  23.1 0.3 combine.1
  23.4 1.5 %collective-permute-start.17 = (bf16[32,2048]{1,0:T(8,128)(2,1)S(1)}, bf16[32,2048]{1,0:T(8,128)(2,1)S(1)}, u32[]{:S(2)}, u32[]{:S(2)}) collective-permute-start(bf16[32,2048]{1,0:T(8,128)(2,1)S(1)} %get-tuple-element.129), channel_id=1, source_target_pairs={{0,24},{8,16},{16,8},{24,0},{1,25},{9,17},{17,9},{25,1},{2,26},{10... | collective-permute-start | bytes 393224 | tf_op jit(solution)/shard_map/ppermute | solution.py:590
  24.9 0.5 %collective-permute-start.18 = (bf16[32,2048]{1,0:T(8,128)(2,1)S(1)}, bf16[32,2048]{1,0:T(8,128)(2,1)S(1)}, u32[]{:S(2)}, u32[]{:S(2)}) collective-permute-start(bf16[32,2048]{1,0:T(8,128)(2,1)S(1)} %get-tuple-element.130), channel_id=1, source_target_pairs={{0,16},{8,24},{16,0},{24,8},{1,17},{9,25},{17,1},{25,9},{2,18},{10... | collective-permute-start | bytes 393224 | tf_op jit(solution)/shard_map/ppermute | solution.py:590
  25.4 1.5 %collective-permute-start.19 = (bf16[32,2048]{1,0:T(8,128)(2,1)S(1)}, bf16[32,2048]{1,0:T(8,128)(2,1)S(1)}, u32[]{:S(2)}, u32[]{:S(2)}) collective-permute-start(bf16[32,2048]{1,0:T(8,128)(2,1)S(1)} %get-tuple-element.131), channel_id=1, source_target_pairs={{0,8},{8,0},{16,24},{24,16},{1,9},{9,1},{17,25},{25,17},{2,10},{10... | collective-permute-start | bytes 393224 | tf_op jit(solution)/shard_map/ppermute | solution.py:590
  26.9 0.3 served_masks.1
  27.2 0.1 collective-permute-start.20
  27.3 2.1 %collective-permute-done.17.rest_0_ = bf16[32,2048]{1,0:T(8,128)(2,1)S(1)} collective-permute-done((bf16[32,2048]{1,0:T(8,128)(2,1)S(1)}, bf16[32,2048]{1,0:T(8,128)(2,1)S(1)}, u32[]{:S(2)}, u32[]{:S(2)}) %collective-permute-start.17) | collective-permute-done | bytes 131104 | tf_op jit(solution)/shard_map/ppermute | solution.py:590
  29.4 1.3 %collective-permute-done.18.rest_1_ = bf16[32,2048]{1,0:T(8,128)(2,1)S(1)} collective-permute-done((bf16[32,2048]{1,0:T(8,128)(2,1)S(1)}, bf16[32,2048]{1,0:T(8,128)(2,1)S(1)}, u32[]{:S(2)}, u32[]{:S(2)}) %collective-permute-start.18) | collective-permute-done | bytes 131104 | tf_op jit(solution)/shard_map/ppermute | solution.py:590
  30.7 0.1 collective-permute-done.19.rest_2_
  30.8 0.6 %mix_far.3 = bf16[48,2048]{1,0:T(8,128)(2,1)S(1)} custom-call(bf16[48,2048]{1,0:T(8,128)(2,1)S(1)} %get-tuple-element.123.x_ref, bf16[2048,128]{1,0:T(8,128)(2,1)S(1)} %get-tuple-element.137.turned_ref, bf16[128,128]{1,0:T(8,128)(2,1)S(1)} %get-tuple-element.138.mask_ref, bf16[32,2048]{1,0:T(8,128)(2,1)S(1)} %collective-permute-done.17.rest_0_, ...), custom_call_target="tpu_custom_call" | custom-call | flops 50331648 | tf_op jit(solution)/shard_map/mix_far/pallas_call | solution.py:26
  31.4 1.6 %collective-permute-start.22 = (bf16[48,2048]{1,0:T(8,128)(2,1)S(1)}, bf16[48,2048]{1,0:T(8,128)(2,1)S(1)}, u32[]{:S(2)}, u32[]{:S(2)}) collective-permute-start(bf16[48,2048]{1,0:T(8,128)(2,1)S(1)} %mix_far.3), channel_id=1, source_target_pairs={{0,7},{1,2},{2,1},{3,4},{4,3},{5,6},{6,5},{7,0},{8,15},{9,10},{10,... | collective-permute-start | bytes 589832 | tf_op jit(solution)/shard_map/ppermute | solution.py:596
  33.0 1.1 %mix_near.3 = (bf16[48,2048]{1,0:T(8,128)(2,1)S(1)}, bf16[128,2048]{1,0:T(8,128)(2,1)S(1)}, s32[8,128]{1,0:T(8,128)S(1)}) custom-call(bf16[176,2048]{1,0:T(8,128)(2,1)S(1)} %get-tuple-element.120.x_ref, bf16[176,128]{1,0:T(8,128)(2,1)S(1)} %get-tuple-element.125.mask_ref, bf16[32,2048]{1,0:T(8,128)(2,1)S(1)} %collective-permute-done.17.rest_0_, ...), custom_call_target="tpu_custom_call" | custom-call | flops 184549376 | tf_op jit(solution)/shard_map/mix_near/pallas_call | solution.py:26
  34.1 0.1 collective-permute-start.21
  34.2 2.5 %mix_whole_late.3.rest_4_.refs_0_ = bf16[512,2048]{1,0:T(8,128)(2,1)S(1)} custom-call(bf16[512,2048]{1,0:T(8,128)(2,1)S(1)} %normalize.1.x_ref, bf16[512,128]{1,0:T(8,128)(2,1)S(1)} %mask_late.1.mask_ref._, bf16[32,2048]{1,0:T(8,128)(2,1)S(1)} %collective-permute-done.17.rest_0_, bf16[32,2048]{1,0:T(8,128)(2,1)S(1)} %collective-permute-done.18.rest_1_, ...), custom_call_target="tpu_custom_call" | custom-call | flops 536870912 | tf_op jit(solution)/shard_map/mix_whole_late/pallas_call | solution.py:26
  36.7 3.0 %collective-permute-done.22.far_ref = bf16[48,2048]{1,0:T(8,128)(2,1)S(1)} collective-permute-done((bf16[48,2048]{1,0:T(8,128)(2,1)S(1)}, bf16[48,2048]{1,0:T(8,128)(2,1)S(1)}, u32[]{:S(2)}, u32[]{:S(2)}) %collective-permute-start.22) | collective-permute-done | bytes 196640 | tf_op jit(solution)/shard_map/ppermute | solution.py:596
  39.7 0.0 collective-permute-done.21.core_ref
  39.7 0.4 unpack_both.3
  40.1 1.4 %collective-permute-start.23 = (bf16[32,2048]{1,0:T(8,128)(2,1)S(1)}, bf16[32,2048]{1,0:T(8,128)(2,1)S(1)}, u32[]{:S(2)}, u32[]{:S(2)}) collective-permute-start(bf16[32,2048]{1,0:T(8,128)(2,1)S(1)} %get-tuple-element.139), channel_id=1, source_target_pairs={{0,24},{8,16},{16,8},{24,0},{1,25},{9,17},{17,9},{25,1},{2,26},{10... | collective-permute-start | bytes 393224 | tf_op jit(solution)/shard_map/ppermute | solution.py:590
  41.6 0.6 %collective-permute-start.24 = (bf16[32,2048]{1,0:T(8,128)(2,1)S(1)}, bf16[32,2048]{1,0:T(8,128)(2,1)S(1)}, u32[]{:S(2)}, u32[]{:S(2)}) collective-permute-start(bf16[32,2048]{1,0:T(8,128)(2,1)S(1)} %get-tuple-element.140), channel_id=1, source_target_pairs={{0,16},{8,24},{16,0},{24,8},{1,17},{9,25},{17,1},{25,9},{2,18},{10... | collective-permute-start | bytes 393224 | tf_op jit(solution)/shard_map/ppermute | solution.py:590
  42.2 1.5 %collective-permute-start.25 = (bf16[32,2048]{1,0:T(8,128)(2,1)S(1)}, bf16[32,2048]{1,0:T(8,128)(2,1)S(1)}, u32[]{:S(2)}, u32[]{:S(2)}) collective-permute-start(bf16[32,2048]{1,0:T(8,128)(2,1)S(1)} %get-tuple-element.141), channel_id=1, source_target_pairs={{0,8},{8,0},{16,24},{24,16},{1,9},{9,1},{17,25},{25,17},{2,10},{10... | collective-permute-start | bytes 393224 | tf_op jit(solution)/shard_map/ppermute | solution.py:590
  43.7 0.5 %slice.16 = s32[1,1]{1,0:T(1,128)} slice(s32[8,128]{1,0:T(8,128)S(1)} %get-tuple-element.134), slice={[0:1], [0:1]} | slice | bytes 8 | tf_op jit(solution)/shard_map/slice | solution.py:655
  44.9 0.1 mix_whole_early.3
  45.0 1.2 %collective-permute-done.23 = bf16[32,2048]{1,0:T(8,128)(2,1)S(1)} collective-permute-done((bf16[32,2048]{1,0:T(8,128)(2,1)S(1)}, bf16[32,2048]{1,0:T(8,128)(2,1)S(1)}, u32[]{:S(2)}, u32[]{:S(2)}) %collective-permute-start.23) | collective-permute-done | bytes 131104 | tf_op jit(solution)/shard_map/ppermute | solution.py:590
  46.2 1.3 %collective-permute-done.24 = bf16[32,2048]{1,0:T(8,128)(2,1)S(1)} collective-permute-done((bf16[32,2048]{1,0:T(8,128)(2,1)S(1)}, bf16[32,2048]{1,0:T(8,128)(2,1)S(1)}, u32[]{:S(2)}, u32[]{:S(2)}) %collective-permute-start.24) | collective-permute-done | bytes 131104 | tf_op jit(solution)/shard_map/ppermute | solution.py:590
  47.5 0.0 collective-permute-done.25
  47.5 2.8 %conditional.1 = (bf16[1,1,512,2048]{3,2,1,0:T(8,128)(2,1)}) conditional(s32[]{:T(128)} %bitcast.7, (bf16[512,2048]{1,0:T(8,128)(2,1)S(1)}, bf16[512,128]{1,0:T(8,128)(2,1)S(1)}, bf16[32,2048]{1,0:T(8,128)(2,1)S(1)}, bf16[32,2048]{1,0:T(8,128)(2,1)S(1)}, bf16[32,2048]{1,0:T(8,128)(2,1)S(1)}, /*index=5*/bf16[32,2048]{1,0:T(8,128)(2,1)S(1)}) %tuple.13, ...), branch_computations={%region_0.0_spmd, %region_1.0_spmd} | conditional | flops 36511809536 | bytes 88408472 | solution.py:655
  47.5 2.7 %mix.2 = bf16[512,2048]{1,0:T(8,128)(2,1)} custom-call(bf16[512,2048]{1,0:T(8,128)(2,1)S(1)} %get-tuple-element.55.x_ref, bf16[512,128]{1,0:T(8,128)(2,1)S(1)} %get-tuple-element.56.mask_ref, bf16[32,2048]{1,0:T(8,128)(2,1)S(1)} %get-tuple-element.57.rest_0_, bf16[32,2048]{1,0:T(8,128)(2,1)S(1)} %get-tuple-element.58.rest_1_, ...), custom_call_target="tpu_custom_call" | custom-call | flops 536870912 | bytes 4194304 | tf_op jit(solution)/shard_map/cond/branch_0_fun/mix/pallas_call | solution.py:26
  (3 shorter events, 0.0 us)
Async XLA Ops:
  0.0 5.7 %collective-permute-start.12 = (s32[4,32]{1,0:T(4,128)}, s32[4,32]{1,0:T(4,128)S(1)}, u32[]{:S(2)}, u32[]{:S(2)}) collective-permute-start(s32[4,32]{1,0:T(4,128)} %bitcast.13), channel_id=1, source_target_pairs={{0,24},{8,16},{16,8},{24,0},{1,25},{9,17},{17,9},{25,1},{2,26},{10... | collective-permute-start | bytes 1544 | tf_op jit(solution)/shard_map/ppermute | solution.py:590
  3.9 3.8 %collective-permute-start.11 = (s32[4,32]{1,0:T(4,128)}, s32[4,32]{1,0:T(4,128)S(1)}, u32[]{:S(2)}, u32[]{:S(2)}) collective-permute-start(s32[4,32]{1,0:T(4,128)} %bitcast.14), channel_id=1, source_target_pairs={{0,16},{8,24},{16,0},{24,8},{1,17},{9,25},{17,1},{25,9},{2,18},{10... | collective-permute-start | bytes 1544 | tf_op jit(solution)/shard_map/ppermute | solution.py:590
  4.4 3.8 %collective-permute-start.10 = (s32[4,32]{1,0:T(4,128)}, s32[4,32]{1,0:T(4,128)S(1)}, u32[]{:S(2)}, u32[]{:S(2)}) collective-permute-start(s32[4,32]{1,0:T(4,128)} %bitcast.15), channel_id=1, source_target_pairs={{0,8},{8,0},{16,24},{24,16},{1,9},{9,1},{17,25},{25,17},{2,10},{10... | collective-permute-start | bytes 1544 | tf_op jit(solution)/shard_map/ppermute | solution.py:590
  8.7 4.9 %collective-permute-start.13 = (s32[8,128]{1,0:T(8,128)S(1)}, s32[8,128]{1,0:T(8,128)S(1)}, u32[]{:S(2)}, u32[]{:S(2)}) collective-permute-start(s32[8,128]{1,0:T(8,128)S(1)} %get-tuple-element.116), channel_id=1, source_target_pairs={{0,7},{1,2},{2,1},{3,4},{4,3},{5,6},{6,5},{7,0},{8,15},{9,10},{10,... | collective-permute-start | bytes 12296 | tf_op jit(solution)/shard_map/ppermute | solution.py:596
  14.1 8.2 %collective-permute-start.15 = (bf16[48,2048]{1,0:T(8,128)(2,1)S(1)}, bf16[48,2048]{1,0:T(8,128)(2,1)S(1)}, u32[]{:S(2)}, u32[]{:S(2)}) collective-permute-start(bf16[48,2048]{1,0:T(8,128)(2,1)S(1)} %get-tuple-element.123.x_ref), channel_id=1, source_target_pairs={{0,7},{1,2},{2,1},{3,4},{4,3},{5,6},{6,5},{7,0},{8,15},{9,10},{10,... | collective-permute-start | bytes 589832 | tf_op jit(solution)/shard_map/ppermute | solution.py:596
  15.5 1.2 %collective-permute-start.14 = (s32[8,128]{1,0:T(8,128)S(1)}, s32[8,128]{1,0:T(8,128)S(1)}, u32[]{:S(2)}, u32[]{:S(2)}) collective-permute-start(s32[8,128]{1,0:T(8,128)S(1)} %get-tuple-element.119.refs_0_), channel_id=1, source_target_pairs={{0,1},{1,0},{2,3},{3,2},{4,5},{5,4},{6,7},{7,6},{8,9},{9,8},{10,11... | collective-permute-start | bytes 12296 | tf_op jit(solution)/shard_map/ppermute | solution.py:599
  17.8 5.3 %collective-permute-start.16 = (bf16[48,2048]{1,0:T(8,128)(2,1)S(1)}, bf16[48,2048]{1,0:T(8,128)(2,1)S(1)}, u32[]{:S(2)}, u32[]{:S(2)}) collective-permute-start(bf16[48,2048]{1,0:T(8,128)(2,1)S(1)} %get-tuple-element.127), channel_id=1, source_target_pairs={{0,1},{1,0},{2,3},{3,2},{4,5},{5,4},{6,7},{7,6},{8,9},{9,8},{10,11... | collective-permute-start | bytes 589832 | tf_op jit(solution)/shard_map/ppermute | solution.py:599
  22.3 0.7 %copy-start = (s32[1,1,512,10]{2,1,3,0:T(1,128)S(1)}, s32[1,1,512,10]{2,1,3,0:T(1,128)}, u32[]{:S(2)}) copy-start(s32[1,1,512,10]{2,1,3,0:T(1,128)} %param.7) | copy-start | bytes 61444
  23.4 6.0 %collective-permute-start.17 = (bf16[32,2048]{1,0:T(8,128)(2,1)S(1)}, bf16[32,2048]{1,0:T(8,128)(2,1)S(1)}, u32[]{:S(2)}, u32[]{:S(2)}) collective-permute-start(bf16[32,2048]{1,0:T(8,128)(2,1)S(1)} %get-tuple-element.129), channel_id=1, source_target_pairs={{0,24},{8,16},{16,8},{24,0},{1,25},{9,17},{17,9},{25,1},{2,26},{10... | collective-permute-start | bytes 393224 | tf_op jit(solution)/shard_map/ppermute | solution.py:590
  24.9 5.8 %collective-permute-start.18 = (bf16[32,2048]{1,0:T(8,128)(2,1)S(1)}, bf16[32,2048]{1,0:T(8,128)(2,1)S(1)}, u32[]{:S(2)}, u32[]{:S(2)}) collective-permute-start(bf16[32,2048]{1,0:T(8,128)(2,1)S(1)} %get-tuple-element.130), channel_id=1, source_target_pairs={{0,16},{8,24},{16,0},{24,8},{1,17},{9,25},{17,1},{25,9},{2,18},{10... | collective-permute-start | bytes 393224 | tf_op jit(solution)/shard_map/ppermute | solution.py:590
  25.4 5.4 %collective-permute-start.19 = (bf16[32,2048]{1,0:T(8,128)(2,1)S(1)}, bf16[32,2048]{1,0:T(8,128)(2,1)S(1)}, u32[]{:S(2)}, u32[]{:S(2)}) collective-permute-start(bf16[32,2048]{1,0:T(8,128)(2,1)S(1)} %get-tuple-element.131), channel_id=1, source_target_pairs={{0,8},{8,0},{16,24},{24,16},{1,9},{9,1},{17,25},{25,17},{2,10},{10... | collective-permute-start | bytes 393224 | tf_op jit(solution)/shard_map/ppermute | solution.py:590
  27.2 5.8 %collective-permute-start.20 = (s32[8,128]{1,0:T(8,128)S(1)}, s32[8,128]{1,0:T(8,128)S(1)}, u32[]{:S(2)}, u32[]{:S(2)}) collective-permute-start(s32[8,128]{1,0:T(8,128)S(1)} %get-tuple-element.133.rest_4_), channel_id=1, source_target_pairs={{0,4},{1,5},{2,6},{3,7},{4,0},{5,1},{6,2},{7,3},{8,12},{9,13},{10,... | collective-permute-start | bytes 12296 | tf_op jit(solution)/shard_map/ppermute | solution.py:593
  31.4 8.3 %collective-permute-start.22 = (bf16[48,2048]{1,0:T(8,128)(2,1)S(1)}, bf16[48,2048]{1,0:T(8,128)(2,1)S(1)}, u32[]{:S(2)}, u32[]{:S(2)}) collective-permute-start(bf16[48,2048]{1,0:T(8,128)(2,1)S(1)} %mix_far.3), channel_id=1, source_target_pairs={{0,7},{1,2},{2,1},{3,4},{4,3},{5,6},{6,5},{7,0},{8,15},{9,10},{10,... | collective-permute-start | bytes 589832 | tf_op jit(solution)/shard_map/ppermute | solution.py:596
  34.1 5.6 %collective-permute-start.21 = (bf16[48,2048]{1,0:T(8,128)(2,1)S(1)}, bf16[48,2048]{1,0:T(8,128)(2,1)S(1)}, u32[]{:S(2)}, u32[]{:S(2)}) collective-permute-start(bf16[48,2048]{1,0:T(8,128)(2,1)S(1)} %get-tuple-element.136), channel_id=1, source_target_pairs={{0,1},{1,0},{2,3},{3,2},{4,5},{5,4},{6,7},{7,6},{8,9},{9,8},{10,11... | collective-permute-start | bytes 589832 | tf_op jit(solution)/shard_map/ppermute | solution.py:599
  40.1 6.0 %collective-permute-start.23 = (bf16[32,2048]{1,0:T(8,128)(2,1)S(1)}, bf16[32,2048]{1,0:T(8,128)(2,1)S(1)}, u32[]{:S(2)}, u32[]{:S(2)}) collective-permute-start(bf16[32,2048]{1,0:T(8,128)(2,1)S(1)} %get-tuple-element.139), channel_id=1, source_target_pairs={{0,24},{8,16},{16,8},{24,0},{1,25},{9,17},{17,9},{25,1},{2,26},{10... | collective-permute-start | bytes 393224 | tf_op jit(solution)/shard_map/ppermute | solution.py:590
  41.6 5.9 %collective-permute-start.24 = (bf16[32,2048]{1,0:T(8,128)(2,1)S(1)}, bf16[32,2048]{1,0:T(8,128)(2,1)S(1)}, u32[]{:S(2)}, u32[]{:S(2)}) collective-permute-start(bf16[32,2048]{1,0:T(8,128)(2,1)S(1)} %get-tuple-element.140), channel_id=1, source_target_pairs={{0,16},{8,24},{16,0},{24,8},{1,17},{9,25},{17,1},{25,9},{2,18},{10... | collective-permute-start | bytes 393224 | tf_op jit(solution)/shard_map/ppermute | solution.py:590
  42.2 5.3 %collective-permute-start.25 = (bf16[32,2048]{1,0:T(8,128)(2,1)S(1)}, bf16[32,2048]{1,0:T(8,128)(2,1)S(1)}, u32[]{:S(2)}, u32[]{:S(2)}) collective-permute-start(bf16[32,2048]{1,0:T(8,128)(2,1)S(1)} %get-tuple-element.141), channel_id=1, source_target_pairs={{0,8},{8,0},{16,24},{24,16},{1,9},{9,1},{17,25},{25,17},{2,10},{10... | collective-permute-start | bytes 393224 | tf_op jit(solution)/shard_map/ppermute | solution.py:590

commit v24 on v22

--- a/solution.py
+++ b/solution.py
@@ -268,32 +268,8 @@
     )
 
 
-def combine_kernel(expand_ref, core_ref, base_ref, most_ref, out_most_ref, *out_refs):
-    out_most_ref[...] = most_ref[...]
-    cap, sent = out_refs[0].shape[0], core_ref.shape[0]
-    rows = jnp.dot(expand_ref[:, :sent], core_ref[...], preferred_element_type=jnp.float32)
-    rows = (rows + base_ref[...].astype(jnp.float32)).astype(jnp.bfloat16)
-    for d, out in enumerate(out_refs):
-        out[...] = rows[d * cap : (d + 1) * cap]
-
-
-def combine_call(expand, core, base, most, servers):
-    total, width = base.shape
-    most, *parts = kernel_call(
-        "combine",
-        combine_kernel,
-        [int32(*most.shape)] + [bf16(total // servers, width)] * servers,
-        expand,
-        core,
-        base,
-        most,
-        flops=2 * total * core.shape[0] * width,
-    )
-    return most, parts
-
-
-def unpack_both_kernel(far_expand, core_expand, own_ref, core_ref, far_ref, *refs):
-    out_refs = refs[1:]
+def unpack_both_kernel(far_first, far_expand, core_expand, own_ref, a_ref, b_ref, _, *out_refs):
+    far_ref, core_ref = (a_ref, b_ref) if far_first else (b_ref, a_ref)
     cap, sent = out_refs[0].shape[0], far_ref.shape[0]
     rows = jnp.dot(core_expand[:, :sent], core_ref[...], preferred_element_type=jnp.float32)
     rows += jnp.dot(far_expand[:, :sent], far_ref[...], preferred_element_type=jnp.float32)
@@ -302,16 +278,15 @@
         out[...] = rows[d * cap : (d + 1) * cap]
 
 
-def unpack_both_call(expands, far, core, own, after, servers):
+def unpack_both_call(expands, far, core, own, after, servers, far_first=False):
     total, width = own.shape
     return kernel_call(
         "unpack_both",
-        unpack_both_kernel,
+        functools.partial(unpack_both_kernel, far_first),
         [bf16(total // servers, width)] * servers,
         *expands,
         own,
-        core,
-        far,
+        *((far, core) if far_first else (core, far)),
         after,
         flops=4 * total * far.shape[0] * width,
         in_specs=[pl.BlockSpec(memory_space=pltpu.VMEM)] * 5
@@ -536,11 +511,6 @@
         got = {d: turn(parts[d], d) for d in reversed(range(1, servers))}
         return [parts[0]] + [got[d] for d in range(1, servers)]
 
-    def exchange(expands, far, core, own, most):
-        base = unpack_call(expands[0], across(far), own)
-        most, parts = combine_call(expands[1], inside(core), base, most, servers)
-        return most, turned(parts)
-
     def next_round(x, mask, far, near, far_turned, far_mask, near_mask, expands, parts, mosts):
         far = far_mix_call(far, far_turned, far_mask, parts)
         core, own, most = near_mix_call(near, near_mask, parts, mosts)
@@ -576,7 +546,9 @@
         x, mask, beyond_list, own_list, told, inside(told), sent
     )
     rest, masks = others[:2], others[2:]
-    most, first = exchange(expands, far, core, own, most)
+    first = turned(
+        unpack_both_call(expands, across(far), inside(core), own, most, servers, far_first=False)
+    )
     mosts, known = [most], 4
     while known < groups:
         most = functools.reduce(jnp.maximum, mosts)

time: 50.4 us -> 49.9 us (0.990)
  starting transfers between devices: 16.7 us -> 15.8 us
  waiting for transfers between devices: 18.7 us -> 19.4 us
    ppermute x3, waiting for transfers between devices: 8.43 us -> 9.77 us  [across(): return lax.ppermute(value, 'rep', beyond)]
    ppermute x3, waiting for transfers between devices: 1.17 us -> 0.01 us  [inside(): return lax.ppermute(value, 'rep', within)]
    ppermute x3, starting transfers between devices: 4.84 us -> 3.97 us  [across(): return lax.ppermute(value, 'rep', beyond)]
    pallas_call x13 -> x12, Pallas kernels: 13 us -> 12.9 us  [kernel_call(): pl.pallas_call(kernel, out_shape=outs, scratch_shapes=scratch, compiler_p...]
  transfers between devices with their start and end apart: 16 -> 16, of which waited for: 12 -> 11; matrix products, arithmetic and copies ran while one was open for 1% -> 1% of each run, Pallas kernels for 17% -> 17%
where the time goes in v24:
time: 49.9 us; the launch traced here: 49.7 us
  waiting for transfers between devices  19.4 us (39%)
  starting transfers between devices  15.8 us (32%)
  Pallas kernels  12.9 us (26%)
  between operations  0.95 us (2%)
  local copies, waits for them, and re-layouts  0.51 us (1%)
    pallas_call x12, Pallas kernels, kernel_call(): pl.pallas_call(kernel, out_shape=outs, scratch_shapes=scratch, compiler_p...  12.9 us
    ppermute x9, starting transfers between devices, turn(): return lax.ppermute(value, 'clus', [(c, c ^ d) for c in range(servers)])  11.6 us
    ppermute x3, waiting for transfers between devices, across(): return lax.ppermute(value, 'rep', beyond)  9.77 us
    ppermute x9, waiting for transfers between devices, turn(): return lax.ppermute(value, 'clus', [(c, c ^ d) for c in range(servers)])  9.61 us
    ppermute x3, starting transfers between devices, across(): return lax.ppermute(value, 'rep', beyond)  3.97 us
  transfers between devices with their start and end apart: 16, of which 11 were waited for; matrix products, arithmetic and copies ran while one was open for 1% of the time, Pallas kernels for 17%

profile of v24, /device:TPU:0, one launch (start us, length us, event | category | flops | bytes accessed | tf_op | source)
XLA Modules:
  0.0 49.7 jit_solution(1961467756124804088)
XLA Ops:
  0.0 3.9 %collective-permute-start.12 = (s32[4,32]{1,0:T(4,128)}, s32[4,32]{1,0:T(4,128)S(1)}, u32[]{:S(2)}, u32[]{:S(2)}) collective-permute-start(s32[4,32]{1,0:T(4,128)} %bitcast.12), channel_id=1, source_target_pairs={{0,24},{8,16},{16,8},{24,0},{1,25},{9,17},{17,9},{25,1},{2,26},{10... | collective-permute-start | bytes 1544 | tf_op jit(solution)/shard_map/ppermute | solution.py:499
  3.9 0.5 %collective-permute-start.11 = (s32[4,32]{1,0:T(4,128)}, s32[4,32]{1,0:T(4,128)S(1)}, u32[]{:S(2)}, u32[]{:S(2)}) collective-permute-start(s32[4,32]{1,0:T(4,128)} %bitcast.13), channel_id=1, source_target_pairs={{0,16},{8,24},{16,0},{24,8},{1,17},{9,25},{17,1},{25,9},{2,18},{10... | collective-permute-start | bytes 1544 | tf_op jit(solution)/shard_map/ppermute | solution.py:499
  4.4 0.1 collective-permute-start.10
  4.5 1.0 %mask.1 = (bf16[512,128]{1,0:T(8,128)(2,1)S(1)}, s32[4,32]{1,0:T(4,128)S(1)}) custom-call(s32[10,1,512]{2,1,0:T(1,128)} %bitcast.11, s32[4,32]{1,0:T(4,128)} %bitcast.15), custom_call_target="tpu_custom_call" | custom-call | flops 1310720 | bytes 131072 | tf_op jit(solution)/shard_map/mask/pallas_call | solution.py:26
  5.5 0.2 collective-permute-done.12.refs_3_
  5.7 2.0 %collective-permute-done.11.refs_2_ = s32[4,32]{1,0:T(4,128)S(1)} collective-permute-done((s32[4,32]{1,0:T(4,128)}, s32[4,32]{1,0:T(4,128)S(1)}, u32[]{:S(2)}, u32[]{:S(2)}) %collective-permute-start.11) | collective-permute-done | bytes 544 | tf_op jit(solution)/shard_map/ppermute | solution.py:499
  7.7 0.5 %collective-permute-done.10.refs_1_ = s32[4,32]{1,0:T(4,128)S(1)} collective-permute-done((s32[4,32]{1,0:T(4,128)}, s32[4,32]{1,0:T(4,128)S(1)}, u32[]{:S(2)}, u32[]{:S(2)}) %collective-permute-start.10) | collective-permute-done | bytes 544 | tf_op jit(solution)/shard_map/ppermute | solution.py:499
  8.2 0.5 list.1
  8.7 1.4 %collective-permute-start.13 = (s32[8,128]{1,0:T(8,128)S(1)}, s32[8,128]{1,0:T(8,128)S(1)}, u32[]{:S(2)}, u32[]{:S(2)}) collective-permute-start(s32[8,128]{1,0:T(8,128)S(1)} %get-tuple-element.116), channel_id=1, source_target_pairs={{0,7},{1,2},{2,1},{3,4},{4,3},{5,6},{6,5},{7,0},{8,15},{9,10},{10,... | collective-permute-start | bytes 12296 | tf_op jit(solution)/shard_map/ppermute | solution.py:505
  10.1 1.9 %normalize.1.x_ref = bf16[512,2048]{1,0:T(8,128)(2,1)S(1)} custom-call(bf16[512,2048]{1,0:T(8,128)(2,1)} %bitcast.10), custom_call_target="tpu_custom_call" | custom-call | flops 6291456 | bytes 4194304 | tf_op jit(solution)/shard_map/normalize/pallas_call | solution.py:26
  11.9 1.6 %collective-permute-done.13.beyond_ref = s32[8,128]{1,0:T(8,128)S(1)} collective-permute-done((s32[8,128]{1,0:T(8,128)S(1)}, s32[8,128]{1,0:T(8,128)S(1)}, u32[]{:S(2)}, u32[]{:S(2)}) %collective-permute-start.13) | collective-permute-done | bytes 4128 | tf_op jit(solution)/shard_map/ppermute | solution.py:505
  13.6 0.5 %pack_far.1 = (s32[8,128]{1,0:T(8,128)S(1)}, bf16[48,2048]{1,0:T(8,128)(2,1)S(1)}) custom-call(bf16[512,2048]{1,0:T(8,128)(2,1)S(1)} %normalize.1.x_ref, s32[8,128]{1,0:T(8,128)S(1)} %collective-permute-done.13.beyond_ref, s32[8,128]{1,0:T(8,128)S(1)} %get-tuple-element.118.core_list_ref), custom_call_target="tpu_custom_call" | custom-call | flops 100663296 | tf_op jit(solution)/shard_map/pack_far/pallas_call | solution.py:26
  14.1 0.1 collective-permute-start.14
  14.2 1.9 %collective-permute-start.16 = (bf16[48,2048]{1,0:T(8,128)(2,1)S(1)}, bf16[48,2048]{1,0:T(8,128)(2,1)S(1)}, u32[]{:S(2)}, u32[]{:S(2)}) collective-permute-start(bf16[48,2048]{1,0:T(8,128)(2,1)S(1)} %get-tuple-element.126.x_ref), channel_id=1, source_target_pairs={{0,7},{1,2},{2,1},{3,4},{4,3},{5,6},{6,5},{7,0},{8,15},{9,10},{10,... | collective-permute-start | bytes 589832 | tf_op jit(solution)/shard_map/ppermute | solution.py:505
  16.1 0.0 collective-permute-done.14.refs_1_
  16.1 1.1 %serve_near.1 = (bf16[48,2048]{1,0:T(8,128)(2,1)S(1)}, bf16[128,2048]{1,0:T(8,128)(2,1)S(1)}, bf16[176,2048]{1,0:T(8,128)(2,1)S(1)}, bf16[80,2048]{1,0:T(8,128)(...) custom-call(bf16[512,2048]{1,0:T(8,128)(2,1)S(1)} %normalize.1.x_ref, ...), custom_call_target="tpu_custom_call" | custom-call | flops 805306368 | tf_op jit(solution)/shard_map/serve_near/pallas_call | solution.py:26
  17.2 0.1 collective-permute-start.15
  17.3 5.1 %collective-permute-done.16.b_ref = bf16[48,2048]{1,0:T(8,128)(2,1)S(1)} collective-permute-done((bf16[48,2048]{1,0:T(8,128)(2,1)S(1)}, bf16[48,2048]{1,0:T(8,128)(2,1)S(1)}, u32[]{:S(2)}, u32[]{:S(2)}) %collective-permute-start.16) | collective-permute-done | bytes 196640 | tf_op jit(solution)/shard_map/ppermute | solution.py:505
  22.4 0.0 collective-permute-done.15.a_ref
  22.4 0.4 unpack_both.4
  22.8 1.6 %collective-permute-start.17 = (bf16[32,2048]{1,0:T(8,128)(2,1)S(1)}, bf16[32,2048]{1,0:T(8,128)(2,1)S(1)}, u32[]{:S(2)}, u32[]{:S(2)}) collective-permute-start(bf16[32,2048]{1,0:T(8,128)(2,1)S(1)} %get-tuple-element.128), channel_id=1, source_target_pairs={{0,24},{8,16},{16,8},{24,0},{1,25},{9,17},{17,9},{25,1},{2,26},{10... | collective-permute-start | bytes 393224 | tf_op jit(solution)/shard_map/ppermute | solution.py:499
  24.4 0.5 %collective-permute-start.18 = (bf16[32,2048]{1,0:T(8,128)(2,1)S(1)}, bf16[32,2048]{1,0:T(8,128)(2,1)S(1)}, u32[]{:S(2)}, u32[]{:S(2)}) collective-permute-start(bf16[32,2048]{1,0:T(8,128)(2,1)S(1)} %get-tuple-element.129), channel_id=1, source_target_pairs={{0,16},{8,24},{16,0},{24,8},{1,17},{9,25},{17,1},{25,9},{2,18},{10... | collective-permute-start | bytes 393224 | tf_op jit(solution)/shard_map/ppermute | solution.py:499
  24.9 1.5 %collective-permute-start.19 = (bf16[32,2048]{1,0:T(8,128)(2,1)S(1)}, bf16[32,2048]{1,0:T(8,128)(2,1)S(1)}, u32[]{:S(2)}, u32[]{:S(2)}) collective-permute-start(bf16[32,2048]{1,0:T(8,128)(2,1)S(1)} %get-tuple-element.130), channel_id=1, source_target_pairs={{0,8},{8,0},{16,24},{24,16},{1,9},{9,1},{17,25},{25,17},{2,10},{10... | collective-permute-start | bytes 393224 | tf_op jit(solution)/shard_map/ppermute | solution.py:499
  26.4 0.0 collective-permute-start.20
  26.4 3.0 %collective-permute-done.17.rest_0_ = bf16[32,2048]{1,0:T(8,128)(2,1)S(1)} collective-permute-done((bf16[32,2048]{1,0:T(8,128)(2,1)S(1)}, bf16[32,2048]{1,0:T(8,128)(2,1)S(1)}, u32[]{:S(2)}, u32[]{:S(2)}) %collective-permute-start.17) | collective-permute-done | bytes 131104 | tf_op jit(solution)/shard_map/ppermute | solution.py:499
  29.3 1.2 %collective-permute-done.18.rest_1_ = bf16[32,2048]{1,0:T(8,128)(2,1)S(1)} collective-permute-done((bf16[32,2048]{1,0:T(8,128)(2,1)S(1)}, bf16[32,2048]{1,0:T(8,128)(2,1)S(1)}, u32[]{:S(2)}, u32[]{:S(2)}) %collective-permute-start.18) | collective-permute-done | bytes 131104 | tf_op jit(solution)/shard_map/ppermute | solution.py:499
  30.6 0.1 collective-permute-done.19.rest_2_
  30.7 0.6 %mix_far.3 = bf16[48,2048]{1,0:T(8,128)(2,1)S(1)} custom-call(bf16[48,2048]{1,0:T(8,128)(2,1)S(1)} %get-tuple-element.126.x_ref, bf16[2048,128]{1,0:T(8,128)(2,1)S(1)} %get-tuple-element.135.turned_ref, bf16[128,128]{1,0:T(8,128)(2,1)S(1)} %get-tuple-element.136.mask_ref, bf16[32,2048]{1,0:T(8,128)(2,1)S(1)} %collective-permute-done.17.rest_0_, ...), custom_call_target="tpu_custom_call" | custom-call | flops 50331648 | tf_op jit(solution)/shard_map/mix_far/pallas_call | solution.py:26
  31.4 0.7 %collective-permute-start.22 = (bf16[48,2048]{1,0:T(8,128)(2,1)S(1)}, bf16[48,2048]{1,0:T(8,128)(2,1)S(1)}, u32[]{:S(2)}, u32[]{:S(2)}) collective-permute-start(bf16[48,2048]{1,0:T(8,128)(2,1)S(1)} %mix_far.3), channel_id=1, source_target_pairs={{0,7},{1,2},{2,1},{3,4},{4,3},{5,6},{6,5},{7,0},{8,15},{9,10},{10,... | collective-permute-start | bytes 589832 | tf_op jit(solution)/shard_map/ppermute | solution.py:505
  32.0 0.0 collective-permute-done.20.rest_5_
  32.0 1.1 %mix_near.3 = (bf16[48,2048]{1,0:T(8,128)(2,1)S(1)}, bf16[128,2048]{1,0:T(8,128)(2,1)S(1)}, s32[8,128]{1,0:T(8,128)S(1)}) custom-call(bf16[176,2048]{1,0:T(8,128)(2,1)S(1)} %get-tuple-element.120.x_ref, bf16[176,128]{1,0:T(8,128)(2,1)S(1)} %get-tuple-element.121.mask_ref, bf16[32,2048]{1,0:T(8,128)(2,1)S(1)} %collective-permute-done.17.rest_0_, ...), custom_call_target="tpu_custom_call" | custom-call | flops 184549376 | tf_op jit(solution)/shard_map/mix_near/pallas_call | solution.py:26
  33.2 0.1 collective-permute-start.21
  33.2 2.5 %mix_whole_late.3.rest_4_._ = bf16[512,2048]{1,0:T(8,128)(2,1)S(1)} custom-call(bf16[512,2048]{1,0:T(8,128)(2,1)S(1)} %normalize.1.x_ref, bf16[512,128]{1,0:T(8,128)(2,1)S(1)} %get-tuple-element.114.mask_ref, bf16[32,2048]{1,0:T(8,128)(2,1)S(1)} %collective-permute-done.17.rest_0_, bf16[32,2048]{1,0:T(8,128)(2,1)S(1)} %collective-permute-done.18.rest_1_, ...), custom_call_target="tpu_custom_call" | custom-call | flops 536870912 | tf_op jit(solution)/shard_map/mix_whole_late/pallas_call | solution.py:26
  35.7 3.1 %collective-permute-done.22.b_ref = bf16[48,2048]{1,0:T(8,128)(2,1)S(1)} collective-permute-done((bf16[48,2048]{1,0:T(8,128)(2,1)S(1)}, bf16[48,2048]{1,0:T(8,128)(2,1)S(1)}, u32[]{:S(2)}, u32[]{:S(2)}) %collective-permute-start.22) | collective-permute-done | bytes 196640 | tf_op jit(solution)/shard_map/ppermute | solution.py:505
  38.8 0.0 collective-permute-done.21.a_ref
  38.8 0.4 unpack_both.5
  39.2 1.5 %collective-permute-start.23 = (bf16[32,2048]{1,0:T(8,128)(2,1)S(1)}, bf16[32,2048]{1,0:T(8,128)(2,1)S(1)}, u32[]{:S(2)}, u32[]{:S(2)}) collective-permute-start(bf16[32,2048]{1,0:T(8,128)(2,1)S(1)} %get-tuple-element.137), channel_id=1, source_target_pairs={{0,24},{8,16},{16,8},{24,0},{1,25},{9,17},{17,9},{25,1},{2,26},{10... | collective-permute-start | bytes 393224 | tf_op jit(solution)/shard_map/ppermute | solution.py:499
  40.8 0.5 %collective-permute-start.24 = (bf16[32,2048]{1,0:T(8,128)(2,1)S(1)}, bf16[32,2048]{1,0:T(8,128)(2,1)S(1)}, u32[]{:S(2)}, u32[]{:S(2)}) collective-permute-start(bf16[32,2048]{1,0:T(8,128)(2,1)S(1)} %get-tuple-element.138), channel_id=1, source_target_pairs={{0,16},{8,24},{16,0},{24,8},{1,17},{9,25},{17,1},{25,9},{2,18},{10... | collective-permute-start | bytes 393224 | tf_op jit(solution)/shard_map/ppermute | solution.py:499
  41.3 1.5 %collective-permute-start.25 = (bf16[32,2048]{1,0:T(8,128)(2,1)S(1)}, bf16[32,2048]{1,0:T(8,128)(2,1)S(1)}, u32[]{:S(2)}, u32[]{:S(2)}) collective-permute-start(bf16[32,2048]{1,0:T(8,128)(2,1)S(1)} %get-tuple-element.139), channel_id=1, source_target_pairs={{0,8},{8,0},{16,24},{24,16},{1,9},{9,1},{17,25},{25,17},{2,10},{10... | collective-permute-start | bytes 393224 | tf_op jit(solution)/shard_map/ppermute | solution.py:499
  42.8 0.5 %slice.16 = s32[1,1]{1,0:T(1,128)} slice(s32[8,128]{1,0:T(8,128)S(1)} %get-tuple-element.132), slice={[0:1], [0:1]} | slice | bytes 8 | tf_op jit(solution)/shard_map/slice | solution.py:561
  43.9 0.1 mix_whole_early.3
  44.0 1.2 %collective-permute-done.23 = bf16[32,2048]{1,0:T(8,128)(2,1)S(1)} collective-permute-done((bf16[32,2048]{1,0:T(8,128)(2,1)S(1)}, bf16[32,2048]{1,0:T(8,128)(2,1)S(1)}, u32[]{:S(2)}, u32[]{:S(2)}) %collective-permute-start.23) | collective-permute-done | bytes 131104 | tf_op jit(solution)/shard_map/ppermute | solution.py:499
  45.2 1.3 %collective-permute-done.24 = bf16[32,2048]{1,0:T(8,128)(2,1)S(1)} collective-permute-done((bf16[32,2048]{1,0:T(8,128)(2,1)S(1)}, bf16[32,2048]{1,0:T(8,128)(2,1)S(1)}, u32[]{:S(2)}, u32[]{:S(2)}) %collective-permute-start.24) | collective-permute-done | bytes 131104 | tf_op jit(solution)/shard_map/ppermute | solution.py:499
  46.6 0.0 collective-permute-done.25
  46.6 3.0 %conditional.1 = (bf16[1,1,512,2048]{3,2,1,0:T(8,128)(2,1)}) conditional(s32[]{:T(128)} %bitcast.6, (bf16[512,2048]{1,0:T(8,128)(2,1)S(1)}, bf16[512,128]{1,0:T(8,128)(2,1)S(1)}, bf16[32,2048]{1,0:T(8,128)(2,1)S(1)}, bf16[32,2048]{1,0:T(8,128)(2,1)S(1)}, bf16[32,2048]{1,0:T(8,128)(2,1)S(1)}, /*index=5*/bf16[32,2048]{1,0:T(8,128)(2,1)S(1)}) %tuple.13, ...), branch_computations={%region_0.0_spmd, %region_1.0_spmd} | conditional | flops 36511809536 | bytes 88408472 | solution.py:561
  46.6 2.7 %mix.2 = bf16[512,2048]{1,0:T(8,128)(2,1)} custom-call(bf16[512,2048]{1,0:T(8,128)(2,1)S(1)} %get-tuple-element.55.x_ref, bf16[512,128]{1,0:T(8,128)(2,1)S(1)} %get-tuple-element.56.mask_ref, bf16[32,2048]{1,0:T(8,128)(2,1)S(1)} %get-tuple-element.57.rest_0_, bf16[32,2048]{1,0:T(8,128)(2,1)S(1)} %get-tuple-element.58.rest_1_, ...), custom_call_target="tpu_custom_call" | custom-call | flops 536870912 | bytes 4194304 | tf_op jit(solution)/shard_map/cond/branch_0_fun/mix/pallas_call | solution.py:26
Async XLA Ops:
  0.0 5.7 %collective-permute-start.12 = (s32[4,32]{1,0:T(4,128)}, s32[4,32]{1,0:T(4,128)S(1)}, u32[]{:S(2)}, u32[]{:S(2)}) collective-permute-start(s32[4,32]{1,0:T(4,128)} %bitcast.12), channel_id=1, source_target_pairs={{0,24},{8,16},{16,8},{24,0},{1,25},{9,17},{17,9},{25,1},{2,26},{10... | collective-permute-start | bytes 1544 | tf_op jit(solution)/shard_map/ppermute | solution.py:499
  3.9 3.8 %collective-permute-start.11 = (s32[4,32]{1,0:T(4,128)}, s32[4,32]{1,0:T(4,128)S(1)}, u32[]{:S(2)}, u32[]{:S(2)}) collective-permute-start(s32[4,32]{1,0:T(4,128)} %bitcast.13), channel_id=1, source_target_pairs={{0,16},{8,24},{16,0},{24,8},{1,17},{9,25},{17,1},{25,9},{2,18},{10... | collective-permute-start | bytes 1544 | tf_op jit(solution)/shard_map/ppermute | solution.py:499
  4.4 3.8 %collective-permute-start.10 = (s32[4,32]{1,0:T(4,128)}, s32[4,32]{1,0:T(4,128)S(1)}, u32[]{:S(2)}, u32[]{:S(2)}) collective-permute-start(s32[4,32]{1,0:T(4,128)} %bitcast.14), channel_id=1, source_target_pairs={{0,8},{8,0},{16,24},{24,16},{1,9},{9,1},{17,25},{25,17},{2,10},{10... | collective-permute-start | bytes 1544 | tf_op jit(solution)/shard_map/ppermute | solution.py:499
  8.7 4.9 %collective-permute-start.13 = (s32[8,128]{1,0:T(8,128)S(1)}, s32[8,128]{1,0:T(8,128)S(1)}, u32[]{:S(2)}, u32[]{:S(2)}) collective-permute-start(s32[8,128]{1,0:T(8,128)S(1)} %get-tuple-element.116), channel_id=1, source_target_pairs={{0,7},{1,2},{2,1},{3,4},{4,3},{5,6},{6,5},{7,0},{8,15},{9,10},{10,... | collective-permute-start | bytes 12296 | tf_op jit(solution)/shard_map/ppermute | solution.py:505
  14.1 2.0 %collective-permute-start.14 = (s32[8,128]{1,0:T(8,128)S(1)}, s32[8,128]{1,0:T(8,128)S(1)}, u32[]{:S(2)}, u32[]{:S(2)}) collective-permute-start(s32[8,128]{1,0:T(8,128)S(1)} %get-tuple-element.119.refs_0_), channel_id=1, source_target_pairs={{0,1},{1,0},{2,3},{3,2},{4,5},{5,4},{6,7},{7,6},{8,9},{9,8},{10,11... | collective-permute-start | bytes 12296 | tf_op jit(solution)/shard_map/ppermute | solution.py:508
  14.2 8.2 %collective-permute-start.16 = (bf16[48,2048]{1,0:T(8,128)(2,1)S(1)}, bf16[48,2048]{1,0:T(8,128)(2,1)S(1)}, u32[]{:S(2)}, u32[]{:S(2)}) collective-permute-start(bf16[48,2048]{1,0:T(8,128)(2,1)S(1)} %get-tuple-element.126.x_ref), channel_id=1, source_target_pairs={{0,7},{1,2},{2,1},{3,4},{4,3},{5,6},{6,5},{7,0},{8,15},{9,10},{10,... | collective-permute-start | bytes 589832 | tf_op jit(solution)/shard_map/ppermute | solution.py:505
  17.2 5.2 %collective-permute-start.15 = (bf16[48,2048]{1,0:T(8,128)(2,1)S(1)}, bf16[48,2048]{1,0:T(8,128)(2,1)S(1)}, u32[]{:S(2)}, u32[]{:S(2)}) collective-permute-start(bf16[48,2048]{1,0:T(8,128)(2,1)S(1)} %get-tuple-element.125), channel_id=1, source_target_pairs={{0,1},{1,0},{2,3},{3,2},{4,5},{5,4},{6,7},{7,6},{8,9},{9,8},{10,11... | collective-permute-start | bytes 589832 | tf_op jit(solution)/shard_map/ppermute | solution.py:508
  22.8 6.5 %collective-permute-start.17 = (bf16[32,2048]{1,0:T(8,128)(2,1)S(1)}, bf16[32,2048]{1,0:T(8,128)(2,1)S(1)}, u32[]{:S(2)}, u32[]{:S(2)}) collective-permute-start(bf16[32,2048]{1,0:T(8,128)(2,1)S(1)} %get-tuple-element.128), channel_id=1, source_target_pairs={{0,24},{8,16},{16,8},{24,0},{1,25},{9,17},{17,9},{25,1},{2,26},{10... | collective-permute-start | bytes 393224 | tf_op jit(solution)/shard_map/ppermute | solution.py:499
  24.4 6.2 %collective-permute-start.18 = (bf16[32,2048]{1,0:T(8,128)(2,1)S(1)}, bf16[32,2048]{1,0:T(8,128)(2,1)S(1)}, u32[]{:S(2)}, u32[]{:S(2)}) collective-permute-start(bf16[32,2048]{1,0:T(8,128)(2,1)S(1)} %get-tuple-element.129), channel_id=1, source_target_pairs={{0,16},{8,24},{16,0},{24,8},{1,17},{9,25},{17,1},{25,9},{2,18},{10... | collective-permute-start | bytes 393224 | tf_op jit(solution)/shard_map/ppermute | solution.py:499
  24.9 5.8 %collective-permute-start.19 = (bf16[32,2048]{1,0:T(8,128)(2,1)S(1)}, bf16[32,2048]{1,0:T(8,128)(2,1)S(1)}, u32[]{:S(2)}, u32[]{:S(2)}) collective-permute-start(bf16[32,2048]{1,0:T(8,128)(2,1)S(1)} %get-tuple-element.130), channel_id=1, source_target_pairs={{0,8},{8,0},{16,24},{24,16},{1,9},{9,1},{17,25},{25,17},{2,10},{10... | collective-permute-start | bytes 393224 | tf_op jit(solution)/shard_map/ppermute | solution.py:499
  26.4 5.7 %collective-permute-start.20 = (s32[8,128]{1,0:T(8,128)S(1)}, s32[8,128]{1,0:T(8,128)S(1)}, u32[]{:S(2)}, u32[]{:S(2)}) collective-permute-start(s32[8,128]{1,0:T(8,128)S(1)} %get-tuple-element.127._.rest_4_), channel_id=1, source_target_pairs={{0,4},{1,5},{2,6},{3,7},{4,0},{5,1},{6,2},{7,3},{8,12},{9,13},{10,... | collective-permute-start | bytes 12296 | tf_op jit(solution)/shard_map/ppermute | solution.py:502
  31.4 7.4 %collective-permute-start.22 = (bf16[48,2048]{1,0:T(8,128)(2,1)S(1)}, bf16[48,2048]{1,0:T(8,128)(2,1)S(1)}, u32[]{:S(2)}, u32[]{:S(2)}) collective-permute-start(bf16[48,2048]{1,0:T(8,128)(2,1)S(1)} %mix_far.3), channel_id=1, source_target_pairs={{0,7},{1,2},{2,1},{3,4},{4,3},{5,6},{6,5},{7,0},{8,15},{9,10},{10,... | collective-permute-start | bytes 589832 | tf_op jit(solution)/shard_map/ppermute | solution.py:505
  33.2 5.7 %collective-permute-start.21 = (bf16[48,2048]{1,0:T(8,128)(2,1)S(1)}, bf16[48,2048]{1,0:T(8,128)(2,1)S(1)}, u32[]{:S(2)}, u32[]{:S(2)}) collective-permute-start(bf16[48,2048]{1,0:T(8,128)(2,1)S(1)} %get-tuple-element.134), channel_id=1, source_target_pairs={{0,1},{1,0},{2,3},{3,2},{4,5},{5,4},{6,7},{7,6},{8,9},{9,8},{10,11... | collective-permute-start | bytes 589832 | tf_op jit(solution)/shard_map/ppermute | solution.py:508
  39.2 6.0 %collective-permute-start.23 = (bf16[32,2048]{1,0:T(8,128)(2,1)S(1)}, bf16[32,2048]{1,0:T(8,128)(2,1)S(1)}, u32[]{:S(2)}, u32[]{:S(2)}) collective-permute-start(bf16[32,2048]{1,0:T(8,128)(2,1)S(1)} %get-tuple-element.137), channel_id=1, source_target_pairs={{0,24},{8,16},{16,8},{24,0},{1,25},{9,17},{17,9},{25,1},{2,26},{10... | collective-permute-start | bytes 393224 | tf_op jit(solution)/shard_map/ppermute | solution.py:499
  40.8 5.8 %collective-permute-start.24 = (bf16[32,2048]{1,0:T(8,128)(2,1)S(1)}, bf16[32,2048]{1,0:T(8,128)(2,1)S(1)}, u32[]{:S(2)}, u32[]{:S(2)}) collective-permute-start(bf16[32,2048]{1,0:T(8,128)(2,1)S(1)} %get-tuple-element.138), channel_id=1, source_target_pairs={{0,16},{8,24},{16,0},{24,8},{1,17},{9,25},{17,1},{25,9},{2,18},{10... | collective-permute-start | bytes 393224 | tf_op jit(solution)/shard_map/ppermute | solution.py:499
  41.3 5.3 %collective-permute-start.25 = (bf16[32,2048]{1,0:T(8,128)(2,1)S(1)}, bf16[32,2048]{1,0:T(8,128)(2,1)S(1)}, u32[]{:S(2)}, u32[]{:S(2)}) collective-permute-start(bf16[32,2048]{1,0:T(8,128)(2,1)S(1)} %get-tuple-element.139), channel_id=1, source_target_pairs={{0,8},{8,0},{16,24},{24,16},{1,9},{9,1},{17,25},{25,17},{2,10},{10... | collective-permute-start | bytes 393224 | tf_op jit(solution)/shard_map/ppermute | solution.py:499

commit v25 on v24

--- a/solution.py
+++ b/solution.py
@@ -9,7 +9,7 @@
 
 LANES = 128
 BLOCK = 128
-COPY = 64
+COPY = 128
 FIRST_SHARE = 3, 8
 BOTH_LAST = (((1,), (1,)), ((), ()))
 

time: 49.9 us -> 49.9 us (level)
  no operation moved by 1% of the time
where the time goes in v25:
time: 49.9 us; the launch traced here: 49.7 us
  waiting for transfers between devices  19.4 us (39%)
  starting transfers between devices  15.8 us (32%)
  Pallas kernels  12.8 us (26%)
  between operations  0.95 us (2%)
  local copies, waits for them, and re-layouts  0.51 us (1%)
    pallas_call x12, Pallas kernels, kernel_call(): pl.pallas_call(kernel, out_shape=outs, scratch_shapes=scratch, compiler_p...  12.8 us
    ppermute x9, starting transfers between devices, turn(): return lax.ppermute(value, 'clus', [(c, c ^ d) for c in range(servers)])  11.6 us
    ppermute x3, waiting for transfers between devices, across(): return lax.ppermute(value, 'rep', beyond)  9.77 us
    ppermute x9, waiting for transfers between devices, turn(): return lax.ppermute(value, 'clus', [(c, c ^ d) for c in range(servers)])  9.64 us
    ppermute x3, starting transfers between devices, across(): return lax.ppermute(value, 'rep', beyond)  3.97 us
  transfers between devices with their start and end apart: 16, of which 11 were waited for; matrix products, arithmetic and copies ran while one was open for 1% of the time, Pallas kernels for 17%

profile of v25, /device:TPU:0, one launch (start us, length us, event | category | flops | bytes accessed | tf_op | source)
XLA Modules:
  0.0 49.7 jit_solution(1873412051886439094)
XLA Ops:
  0.0 3.9 %collective-permute-start.12 = (s32[4,32]{1,0:T(4,128)}, s32[4,32]{1,0:T(4,128)S(1)}, u32[]{:S(2)}, u32[]{:S(2)}) collective-permute-start(s32[4,32]{1,0:T(4,128)} %bitcast.12), channel_id=1, source_target_pairs={{0,24},{8,16},{16,8},{24,0},{1,25},{9,17},{17,9},{25,1},{2,26},{10... | collective-permute-start | bytes 1544 | tf_op jit(solution)/shard_map/ppermute | solution.py:499
  3.9 0.5 %collective-permute-start.11 = (s32[4,32]{1,0:T(4,128)}, s32[4,32]{1,0:T(4,128)S(1)}, u32[]{:S(2)}, u32[]{:S(2)}) collective-permute-start(s32[4,32]{1,0:T(4,128)} %bitcast.13), channel_id=1, source_target_pairs={{0,16},{8,24},{16,0},{24,8},{1,17},{9,25},{17,1},{25,9},{2,18},{10... | collective-permute-start | bytes 1544 | tf_op jit(solution)/shard_map/ppermute | solution.py:499
  4.4 0.1 collective-permute-start.10
  4.5 1.0 %mask.1 = (bf16[512,128]{1,0:T(8,128)(2,1)S(1)}, s32[4,32]{1,0:T(4,128)S(1)}) custom-call(s32[10,1,512]{2,1,0:T(1,128)} %bitcast.11, s32[4,32]{1,0:T(4,128)} %bitcast.15), custom_call_target="tpu_custom_call" | custom-call | flops 1310720 | bytes 131072 | tf_op jit(solution)/shard_map/mask/pallas_call | solution.py:26
  5.5 0.2 collective-permute-done.12.refs_3_
  5.7 2.0 %collective-permute-done.11.refs_2_ = s32[4,32]{1,0:T(4,128)S(1)} collective-permute-done((s32[4,32]{1,0:T(4,128)}, s32[4,32]{1,0:T(4,128)S(1)}, u32[]{:S(2)}, u32[]{:S(2)}) %collective-permute-start.11) | collective-permute-done | bytes 544 | tf_op jit(solution)/shard_map/ppermute | solution.py:499
  7.7 0.5 %collective-permute-done.10.refs_1_ = s32[4,32]{1,0:T(4,128)S(1)} collective-permute-done((s32[4,32]{1,0:T(4,128)}, s32[4,32]{1,0:T(4,128)S(1)}, u32[]{:S(2)}, u32[]{:S(2)}) %collective-permute-start.10) | collective-permute-done | bytes 544 | tf_op jit(solution)/shard_map/ppermute | solution.py:499
  8.2 0.5 list.1
  8.7 1.4 %collective-permute-start.13 = (s32[8,128]{1,0:T(8,128)S(1)}, s32[8,128]{1,0:T(8,128)S(1)}, u32[]{:S(2)}, u32[]{:S(2)}) collective-permute-start(s32[8,128]{1,0:T(8,128)S(1)} %get-tuple-element.116), channel_id=1, source_target_pairs={{0,7},{1,2},{2,1},{3,4},{4,3},{5,6},{6,5},{7,0},{8,15},{9,10},{10,... | collective-permute-start | bytes 12296 | tf_op jit(solution)/shard_map/ppermute | solution.py:505
  10.1 1.9 %normalize.1.x_ref = bf16[512,2048]{1,0:T(8,128)(2,1)S(1)} custom-call(bf16[512,2048]{1,0:T(8,128)(2,1)} %bitcast.10), custom_call_target="tpu_custom_call" | custom-call | flops 6291456 | bytes 4194304 | tf_op jit(solution)/shard_map/normalize/pallas_call | solution.py:26
  11.9 1.6 %collective-permute-done.13.beyond_ref = s32[8,128]{1,0:T(8,128)S(1)} collective-permute-done((s32[8,128]{1,0:T(8,128)S(1)}, s32[8,128]{1,0:T(8,128)S(1)}, u32[]{:S(2)}, u32[]{:S(2)}) %collective-permute-start.13) | collective-permute-done | bytes 4128 | tf_op jit(solution)/shard_map/ppermute | solution.py:505
  13.6 0.5 %pack_far.1 = (s32[8,128]{1,0:T(8,128)S(1)}, bf16[48,2048]{1,0:T(8,128)(2,1)S(1)}) custom-call(bf16[512,2048]{1,0:T(8,128)(2,1)S(1)} %normalize.1.x_ref, s32[8,128]{1,0:T(8,128)S(1)} %collective-permute-done.13.beyond_ref, s32[8,128]{1,0:T(8,128)S(1)} %get-tuple-element.118.core_list_ref), custom_call_target="tpu_custom_call" | custom-call | flops 100663296 | tf_op jit(solution)/shard_map/pack_far/pallas_call | solution.py:26
  14.1 0.1 collective-permute-start.14
  14.2 1.9 %collective-permute-start.16 = (bf16[48,2048]{1,0:T(8,128)(2,1)S(1)}, bf16[48,2048]{1,0:T(8,128)(2,1)S(1)}, u32[]{:S(2)}, u32[]{:S(2)}) collective-permute-start(bf16[48,2048]{1,0:T(8,128)(2,1)S(1)} %get-tuple-element.126.x_ref), channel_id=1, source_target_pairs={{0,7},{1,2},{2,1},{3,4},{4,3},{5,6},{6,5},{7,0},{8,15},{9,10},{10,... | collective-permute-start | bytes 589832 | tf_op jit(solution)/shard_map/ppermute | solution.py:505
  16.1 0.0 collective-permute-done.14.refs_1_
  16.1 1.1 %serve_near.1 = (bf16[48,2048]{1,0:T(8,128)(2,1)S(1)}, bf16[128,2048]{1,0:T(8,128)(2,1)S(1)}, bf16[176,2048]{1,0:T(8,128)(2,1)S(1)}, bf16[80,2048]{1,0:T(8,128)(...) custom-call(bf16[512,2048]{1,0:T(8,128)(2,1)S(1)} %normalize.1.x_ref, ...), custom_call_target="tpu_custom_call" | custom-call | flops 805306368 | tf_op jit(solution)/shard_map/serve_near/pallas_call | solution.py:26
  17.2 0.1 collective-permute-start.15
  17.3 5.1 %collective-permute-done.16.b_ref = bf16[48,2048]{1,0:T(8,128)(2,1)S(1)} collective-permute-done((bf16[48,2048]{1,0:T(8,128)(2,1)S(1)}, bf16[48,2048]{1,0:T(8,128)(2,1)S(1)}, u32[]{:S(2)}, u32[]{:S(2)}) %collective-permute-start.16) | collective-permute-done | bytes 196640 | tf_op jit(solution)/shard_map/ppermute | solution.py:505
  22.4 0.0 collective-permute-done.15.a_ref
  22.4 0.4 unpack_both.4
  22.8 1.6 %collective-permute-start.17 = (bf16[32,2048]{1,0:T(8,128)(2,1)S(1)}, bf16[32,2048]{1,0:T(8,128)(2,1)S(1)}, u32[]{:S(2)}, u32[]{:S(2)}) collective-permute-start(bf16[32,2048]{1,0:T(8,128)(2,1)S(1)} %get-tuple-element.128), channel_id=1, source_target_pairs={{0,24},{8,16},{16,8},{24,0},{1,25},{9,17},{17,9},{25,1},{2,26},{10... | collective-permute-start | bytes 393224 | tf_op jit(solution)/shard_map/ppermute | solution.py:499
  24.4 0.5 %collective-permute-start.18 = (bf16[32,2048]{1,0:T(8,128)(2,1)S(1)}, bf16[32,2048]{1,0:T(8,128)(2,1)S(1)}, u32[]{:S(2)}, u32[]{:S(2)}) collective-permute-start(bf16[32,2048]{1,0:T(8,128)(2,1)S(1)} %get-tuple-element.129), channel_id=1, source_target_pairs={{0,16},{8,24},{16,0},{24,8},{1,17},{9,25},{17,1},{25,9},{2,18},{10... | collective-permute-start | bytes 393224 | tf_op jit(solution)/shard_map/ppermute | solution.py:499
  24.9 1.5 %collective-permute-start.19 = (bf16[32,2048]{1,0:T(8,128)(2,1)S(1)}, bf16[32,2048]{1,0:T(8,128)(2,1)S(1)}, u32[]{:S(2)}, u32[]{:S(2)}) collective-permute-start(bf16[32,2048]{1,0:T(8,128)(2,1)S(1)} %get-tuple-element.130), channel_id=1, source_target_pairs={{0,8},{8,0},{16,24},{24,16},{1,9},{9,1},{17,25},{25,17},{2,10},{10... | collective-permute-start | bytes 393224 | tf_op jit(solution)/shard_map/ppermute | solution.py:499
  26.4 0.0 collective-permute-start.20
  26.4 3.0 %collective-permute-done.17.rest_0_ = bf16[32,2048]{1,0:T(8,128)(2,1)S(1)} collective-permute-done((bf16[32,2048]{1,0:T(8,128)(2,1)S(1)}, bf16[32,2048]{1,0:T(8,128)(2,1)S(1)}, u32[]{:S(2)}, u32[]{:S(2)}) %collective-permute-start.17) | collective-permute-done | bytes 131104 | tf_op jit(solution)/shard_map/ppermute | solution.py:499
  29.3 1.2 %collective-permute-done.18.rest_1_ = bf16[32,2048]{1,0:T(8,128)(2,1)S(1)} collective-permute-done((bf16[32,2048]{1,0:T(8,128)(2,1)S(1)}, bf16[32,2048]{1,0:T(8,128)(2,1)S(1)}, u32[]{:S(2)}, u32[]{:S(2)}) %collective-permute-start.18) | collective-permute-done | bytes 131104 | tf_op jit(solution)/shard_map/ppermute | solution.py:499
  30.6 0.1 collective-permute-done.19.rest_2_
  30.7 0.6 %mix_far.3 = bf16[48,2048]{1,0:T(8,128)(2,1)S(1)} custom-call(bf16[48,2048]{1,0:T(8,128)(2,1)S(1)} %get-tuple-element.126.x_ref, bf16[2048,128]{1,0:T(8,128)(2,1)S(1)} %get-tuple-element.135.turned_ref, bf16[128,128]{1,0:T(8,128)(2,1)S(1)} %get-tuple-element.136.mask_ref, bf16[32,2048]{1,0:T(8,128)(2,1)S(1)} %collective-permute-done.17.rest_0_, ...), custom_call_target="tpu_custom_call" | custom-call | flops 50331648 | tf_op jit(solution)/shard_map/mix_far/pallas_call | solution.py:26
  31.4 0.7 %collective-permute-start.22 = (bf16[48,2048]{1,0:T(8,128)(2,1)S(1)}, bf16[48,2048]{1,0:T(8,128)(2,1)S(1)}, u32[]{:S(2)}, u32[]{:S(2)}) collective-permute-start(bf16[48,2048]{1,0:T(8,128)(2,1)S(1)} %mix_far.3), channel_id=1, source_target_pairs={{0,7},{1,2},{2,1},{3,4},{4,3},{5,6},{6,5},{7,0},{8,15},{9,10},{10,... | collective-permute-start | bytes 589832 | tf_op jit(solution)/shard_map/ppermute | solution.py:505
  32.0 0.0 collective-permute-done.20.rest_5_
  32.0 1.1 %mix_near.3 = (bf16[48,2048]{1,0:T(8,128)(2,1)S(1)}, bf16[128,2048]{1,0:T(8,128)(2,1)S(1)}, s32[8,128]{1,0:T(8,128)S(1)}) custom-call(bf16[176,2048]{1,0:T(8,128)(2,1)S(1)} %get-tuple-element.120.x_ref, bf16[176,128]{1,0:T(8,128)(2,1)S(1)} %get-tuple-element.121.mask_ref, bf16[32,2048]{1,0:T(8,128)(2,1)S(1)} %collective-permute-done.17.rest_0_, ...), custom_call_target="tpu_custom_call" | custom-call | flops 184549376 | tf_op jit(solution)/shard_map/mix_near/pallas_call | solution.py:26
  33.2 0.1 collective-permute-start.21
  33.2 2.5 %mix_whole_late.3.rest_4_._ = bf16[512,2048]{1,0:T(8,128)(2,1)S(1)} custom-call(bf16[512,2048]{1,0:T(8,128)(2,1)S(1)} %normalize.1.x_ref, bf16[512,128]{1,0:T(8,128)(2,1)S(1)} %get-tuple-element.114.mask_ref, bf16[32,2048]{1,0:T(8,128)(2,1)S(1)} %collective-permute-done.17.rest_0_, bf16[32,2048]{1,0:T(8,128)(2,1)S(1)} %collective-permute-done.18.rest_1_, ...), custom_call_target="tpu_custom_call" | custom-call | flops 536870912 | tf_op jit(solution)/shard_map/mix_whole_late/pallas_call | solution.py:26
  35.7 3.1 %collective-permute-done.22.b_ref = bf16[48,2048]{1,0:T(8,128)(2,1)S(1)} collective-permute-done((bf16[48,2048]{1,0:T(8,128)(2,1)S(1)}, bf16[48,2048]{1,0:T(8,128)(2,1)S(1)}, u32[]{:S(2)}, u32[]{:S(2)}) %collective-permute-start.22) | collective-permute-done | bytes 196640 | tf_op jit(solution)/shard_map/ppermute | solution.py:505
  38.8 0.0 collective-permute-done.21.a_ref
  38.8 0.4 unpack_both.5
  39.2 1.5 %collective-permute-start.23 = (bf16[32,2048]{1,0:T(8,128)(2,1)S(1)}, bf16[32,2048]{1,0:T(8,128)(2,1)S(1)}, u32[]{:S(2)}, u32[]{:S(2)}) collective-permute-start(bf16[32,2048]{1,0:T(8,128)(2,1)S(1)} %get-tuple-element.137), channel_id=1, source_target_pairs={{0,24},{8,16},{16,8},{24,0},{1,25},{9,17},{17,9},{25,1},{2,26},{10... | collective-permute-start | bytes 393224 | tf_op jit(solution)/shard_map/ppermute | solution.py:499
  40.8 0.5 %collective-permute-start.24 = (bf16[32,2048]{1,0:T(8,128)(2,1)S(1)}, bf16[32,2048]{1,0:T(8,128)(2,1)S(1)}, u32[]{:S(2)}, u32[]{:S(2)}) collective-permute-start(bf16[32,2048]{1,0:T(8,128)(2,1)S(1)} %get-tuple-element.138), channel_id=1, source_target_pairs={{0,16},{8,24},{16,0},{24,8},{1,17},{9,25},{17,1},{25,9},{2,18},{10... | collective-permute-start | bytes 393224 | tf_op jit(solution)/shard_map/ppermute | solution.py:499
  41.3 1.5 %collective-permute-start.25 = (bf16[32,2048]{1,0:T(8,128)(2,1)S(1)}, bf16[32,2048]{1,0:T(8,128)(2,1)S(1)}, u32[]{:S(2)}, u32[]{:S(2)}) collective-permute-start(bf16[32,2048]{1,0:T(8,128)(2,1)S(1)} %get-tuple-element.139), channel_id=1, source_target_pairs={{0,8},{8,0},{16,24},{24,16},{1,9},{9,1},{17,25},{25,17},{2,10},{10... | collective-permute-start | bytes 393224 | tf_op jit(solution)/shard_map/ppermute | solution.py:499
  42.8 0.5 %slice.16 = s32[1,1]{1,0:T(1,128)} slice(s32[8,128]{1,0:T(8,128)S(1)} %get-tuple-element.132), slice={[0:1], [0:1]} | slice | bytes 8 | tf_op jit(solution)/shard_map/slice | solution.py:561
  43.9 0.1 mix_whole_early.3
  44.0 1.2 %collective-permute-done.23 = bf16[32,2048]{1,0:T(8,128)(2,1)S(1)} collective-permute-done((bf16[32,2048]{1,0:T(8,128)(2,1)S(1)}, bf16[32,2048]{1,0:T(8,128)(2,1)S(1)}, u32[]{:S(2)}, u32[]{:S(2)}) %collective-permute-start.23) | collective-permute-done | bytes 131104 | tf_op jit(solution)/shard_map/ppermute | solution.py:499
  45.2 1.3 %collective-permute-done.24 = bf16[32,2048]{1,0:T(8,128)(2,1)S(1)} collective-permute-done((bf16[32,2048]{1,0:T(8,128)(2,1)S(1)}, bf16[32,2048]{1,0:T(8,128)(2,1)S(1)}, u32[]{:S(2)}, u32[]{:S(2)}) %collective-permute-start.24) | collective-permute-done | bytes 131104 | tf_op jit(solution)/shard_map/ppermute | solution.py:499
  46.6 0.0 collective-permute-done.25
  46.6 2.9 %conditional.1 = (bf16[1,1,512,2048]{3,2,1,0:T(8,128)(2,1)}) conditional(s32[]{:T(128)} %bitcast.6, (bf16[512,2048]{1,0:T(8,128)(2,1)S(1)}, bf16[512,128]{1,0:T(8,128)(2,1)S(1)}, bf16[32,2048]{1,0:T(8,128)(2,1)S(1)}, bf16[32,2048]{1,0:T(8,128)(2,1)S(1)}, bf16[32,2048]{1,0:T(8,128)(2,1)S(1)}, /*index=5*/bf16[32,2048]{1,0:T(8,128)(2,1)S(1)}) %tuple.13, ...), branch_computations={%region_0.0_spmd, %region_1.0_spmd} | conditional | flops 36511809536 | bytes 88408472 | solution.py:561
  46.6 2.7 %mix.2 = bf16[512,2048]{1,0:T(8,128)(2,1)} custom-call(bf16[512,2048]{1,0:T(8,128)(2,1)S(1)} %get-tuple-element.55.x_ref, bf16[512,128]{1,0:T(8,128)(2,1)S(1)} %get-tuple-element.56.mask_ref, bf16[32,2048]{1,0:T(8,128)(2,1)S(1)} %get-tuple-element.57.rest_0_, bf16[32,2048]{1,0:T(8,128)(2,1)S(1)} %get-tuple-element.58.rest_1_, ...), custom_call_target="tpu_custom_call" | custom-call | flops 536870912 | bytes 4194304 | tf_op jit(solution)/shard_map/cond/branch_0_fun/mix/pallas_call | solution.py:26
Async XLA Ops:
  0.0 5.7 %collective-permute-start.12 = (s32[4,32]{1,0:T(4,128)}, s32[4,32]{1,0:T(4,128)S(1)}, u32[]{:S(2)}, u32[]{:S(2)}) collective-permute-start(s32[4,32]{1,0:T(4,128)} %bitcast.12), channel_id=1, source_target_pairs={{0,24},{8,16},{16,8},{24,0},{1,25},{9,17},{17,9},{25,1},{2,26},{10... | collective-permute-start | bytes 1544 | tf_op jit(solution)/shard_map/ppermute | solution.py:499
  3.9 3.8 %collective-permute-start.11 = (s32[4,32]{1,0:T(4,128)}, s32[4,32]{1,0:T(4,128)S(1)}, u32[]{:S(2)}, u32[]{:S(2)}) collective-permute-start(s32[4,32]{1,0:T(4,128)} %bitcast.13), channel_id=1, source_target_pairs={{0,16},{8,24},{16,0},{24,8},{1,17},{9,25},{17,1},{25,9},{2,18},{10... | collective-permute-start | bytes 1544 | tf_op jit(solution)/shard_map/ppermute | solution.py:499
  4.4 3.8 %collective-permute-start.10 = (s32[4,32]{1,0:T(4,128)}, s32[4,32]{1,0:T(4,128)S(1)}, u32[]{:S(2)}, u32[]{:S(2)}) collective-permute-start(s32[4,32]{1,0:T(4,128)} %bitcast.14), channel_id=1, source_target_pairs={{0,8},{8,0},{16,24},{24,16},{1,9},{9,1},{17,25},{25,17},{2,10},{10... | collective-permute-start | bytes 1544 | tf_op jit(solution)/shard_map/ppermute | solution.py:499
  8.7 4.9 %collective-permute-start.13 = (s32[8,128]{1,0:T(8,128)S(1)}, s32[8,128]{1,0:T(8,128)S(1)}, u32[]{:S(2)}, u32[]{:S(2)}) collective-permute-start(s32[8,128]{1,0:T(8,128)S(1)} %get-tuple-element.116), channel_id=1, source_target_pairs={{0,7},{1,2},{2,1},{3,4},{4,3},{5,6},{6,5},{7,0},{8,15},{9,10},{10,... | collective-permute-start | bytes 12296 | tf_op jit(solution)/shard_map/ppermute | solution.py:505
  14.1 2.0 %collective-permute-start.14 = (s32[8,128]{1,0:T(8,128)S(1)}, s32[8,128]{1,0:T(8,128)S(1)}, u32[]{:S(2)}, u32[]{:S(2)}) collective-permute-start(s32[8,128]{1,0:T(8,128)S(1)} %get-tuple-element.119.refs_0_), channel_id=1, source_target_pairs={{0,1},{1,0},{2,3},{3,2},{4,5},{5,4},{6,7},{7,6},{8,9},{9,8},{10,11... | collective-permute-start | bytes 12296 | tf_op jit(solution)/shard_map/ppermute | solution.py:508
  14.2 8.2 %collective-permute-start.16 = (bf16[48,2048]{1,0:T(8,128)(2,1)S(1)}, bf16[48,2048]{1,0:T(8,128)(2,1)S(1)}, u32[]{:S(2)}, u32[]{:S(2)}) collective-permute-start(bf16[48,2048]{1,0:T(8,128)(2,1)S(1)} %get-tuple-element.126.x_ref), channel_id=1, source_target_pairs={{0,7},{1,2},{2,1},{3,4},{4,3},{5,6},{6,5},{7,0},{8,15},{9,10},{10,... | collective-permute-start | bytes 589832 | tf_op jit(solution)/shard_map/ppermute | solution.py:505
  17.2 5.2 %collective-permute-start.15 = (bf16[48,2048]{1,0:T(8,128)(2,1)S(1)}, bf16[48,2048]{1,0:T(8,128)(2,1)S(1)}, u32[]{:S(2)}, u32[]{:S(2)}) collective-permute-start(bf16[48,2048]{1,0:T(8,128)(2,1)S(1)} %get-tuple-element.125), channel_id=1, source_target_pairs={{0,1},{1,0},{2,3},{3,2},{4,5},{5,4},{6,7},{7,6},{8,9},{9,8},{10,11... | collective-permute-start | bytes 589832 | tf_op jit(solution)/shard_map/ppermute | solution.py:508
  22.8 6.5 %collective-permute-start.17 = (bf16[32,2048]{1,0:T(8,128)(2,1)S(1)}, bf16[32,2048]{1,0:T(8,128)(2,1)S(1)}, u32[]{:S(2)}, u32[]{:S(2)}) collective-permute-start(bf16[32,2048]{1,0:T(8,128)(2,1)S(1)} %get-tuple-element.128), channel_id=1, source_target_pairs={{0,24},{8,16},{16,8},{24,0},{1,25},{9,17},{17,9},{25,1},{2,26},{10... | collective-permute-start | bytes 393224 | tf_op jit(solution)/shard_map/ppermute | solution.py:499
  24.4 6.2 %collective-permute-start.18 = (bf16[32,2048]{1,0:T(8,128)(2,1)S(1)}, bf16[32,2048]{1,0:T(8,128)(2,1)S(1)}, u32[]{:S(2)}, u32[]{:S(2)}) collective-permute-start(bf16[32,2048]{1,0:T(8,128)(2,1)S(1)} %get-tuple-element.129), channel_id=1, source_target_pairs={{0,16},{8,24},{16,0},{24,8},{1,17},{9,25},{17,1},{25,9},{2,18},{10... | collective-permute-start | bytes 393224 | tf_op jit(solution)/shard_map/ppermute | solution.py:499
  24.9 5.8 %collective-permute-start.19 = (bf16[32,2048]{1,0:T(8,128)(2,1)S(1)}, bf16[32,2048]{1,0:T(8,128)(2,1)S(1)}, u32[]{:S(2)}, u32[]{:S(2)}) collective-permute-start(bf16[32,2048]{1,0:T(8,128)(2,1)S(1)} %get-tuple-element.130), channel_id=1, source_target_pairs={{0,8},{8,0},{16,24},{24,16},{1,9},{9,1},{17,25},{25,17},{2,10},{10... | collective-permute-start | bytes 393224 | tf_op jit(solution)/shard_map/ppermute | solution.py:499
  26.4 5.7 %collective-permute-start.20 = (s32[8,128]{1,0:T(8,128)S(1)}, s32[8,128]{1,0:T(8,128)S(1)}, u32[]{:S(2)}, u32[]{:S(2)}) collective-permute-start(s32[8,128]{1,0:T(8,128)S(1)} %get-tuple-element.127._.rest_4_), channel_id=1, source_target_pairs={{0,4},{1,5},{2,6},{3,7},{4,0},{5,1},{6,2},{7,3},{8,12},{9,13},{10,... | collective-permute-start | bytes 12296 | tf_op jit(solution)/shard_map/ppermute | solution.py:502
  31.4 7.4 %collective-permute-start.22 = (bf16[48,2048]{1,0:T(8,128)(2,1)S(1)}, bf16[48,2048]{1,0:T(8,128)(2,1)S(1)}, u32[]{:S(2)}, u32[]{:S(2)}) collective-permute-start(bf16[48,2048]{1,0:T(8,128)(2,1)S(1)} %mix_far.3), channel_id=1, source_target_pairs={{0,7},{1,2},{2,1},{3,4},{4,3},{5,6},{6,5},{7,0},{8,15},{9,10},{10,... | collective-permute-start | bytes 589832 | tf_op jit(solution)/shard_map/ppermute | solution.py:505
  33.2 5.7 %collective-permute-start.21 = (bf16[48,2048]{1,0:T(8,128)(2,1)S(1)}, bf16[48,2048]{1,0:T(8,128)(2,1)S(1)}, u32[]{:S(2)}, u32[]{:S(2)}) collective-permute-start(bf16[48,2048]{1,0:T(8,128)(2,1)S(1)} %get-tuple-element.134), channel_id=1, source_target_pairs={{0,1},{1,0},{2,3},{3,2},{4,5},{5,4},{6,7},{7,6},{8,9},{9,8},{10,11... | collective-permute-start | bytes 589832 | tf_op jit(solution)/shard_map/ppermute | solution.py:508
  39.2 6.0 %collective-permute-start.23 = (bf16[32,2048]{1,0:T(8,128)(2,1)S(1)}, bf16[32,2048]{1,0:T(8,128)(2,1)S(1)}, u32[]{:S(2)}, u32[]{:S(2)}) collective-permute-start(bf16[32,2048]{1,0:T(8,128)(2,1)S(1)} %get-tuple-element.137), channel_id=1, source_target_pairs={{0,24},{8,16},{16,8},{24,0},{1,25},{9,17},{17,9},{25,1},{2,26},{10... | collective-permute-start | bytes 393224 | tf_op jit(solution)/shard_map/ppermute | solution.py:499
  40.8 5.8 %collective-permute-start.24 = (bf16[32,2048]{1,0:T(8,128)(2,1)S(1)}, bf16[32,2048]{1,0:T(8,128)(2,1)S(1)}, u32[]{:S(2)}, u32[]{:S(2)}) collective-permute-start(bf16[32,2048]{1,0:T(8,128)(2,1)S(1)} %get-tuple-element.138), channel_id=1, source_target_pairs={{0,16},{8,24},{16,0},{24,8},{1,17},{9,25},{17,1},{25,9},{2,18},{10... | collective-permute-start | bytes 393224 | tf_op jit(solution)/shard_map/ppermute | solution.py:499
  41.3 5.3 %collective-permute-start.25 = (bf16[32,2048]{1,0:T(8,128)(2,1)S(1)}, bf16[32,2048]{1,0:T(8,128)(2,1)S(1)}, u32[]{:S(2)}, u32[]{:S(2)}) collective-permute-start(bf16[32,2048]{1,0:T(8,128)(2,1)S(1)} %get-tuple-element.139), channel_id=1, source_target_pairs={{0,8},{8,0},{16,24},{24,16},{1,9},{9,1},{17,25},{25,17},{2,10},{10... | collective-permute-start | bytes 393224 | tf_op jit(solution)/shard_map/ppermute | solution.py:499
